TPU v7x, 32 devices: a whole 2x2x4 slice. The times are simulated.
32 devices in a mesh: seq: 8 (over y, x, core), dp: 4 (over z).
Axes of the slice: x: 2, y: 2, z: 4, core: 2. Of those that a mesh axis runs over, the one named last changes fastest.
Arguments:
- points: bfloat16 [4, 4096, 512], P('dp', 'seq'), may hold values from -6 to 6
- cotangent: bfloat16 [4, 4096, 512], P('dp', 'seq'), may hold values from -6 to 6
- dest: int32 [4, 4096], P('dp', 'seq'), may hold values from 0 to 4095, as said below
- w_qkv: bfloat16 [512, 1536], replicated
- w_proj: bfloat16 [512, 512], replicated, may hold values from -0.25 to 0.25
- gain: float32 [512], replicated, may hold values from 0.5 to 1.5
Outputs:
- grad_points: bfloat16 [4, 4096, 512], P('dp', 'seq')
- grad_qkv: float32 [512, 1536], replicated
- grad_proj: float32 [512, 512], replicated
- gain_gradient: float32 [512], replicated
Inputs may be any that keep to these rules, and one draw needn't show every extreme that they name: For each scan, dest is a permutation of the 4096 positions, one serialization order of the points. Of the 512 points of one device, at most 128 have positions on any one device's range of 512 positions, and exactly 128 for some device.
All inputs are finite; a program needn't handle non-finite values.
Results may differ from a plain program's by a relative error of at most 0.013.
The roundings to bfloat16 on the way count: a program that leaves them out, or rounds other values in their place, can miss the bound.
Values may be sent and summed in bfloat16 or wider, within the bound.
No kernel may reach another device: no remote copies, remote signals or barrier semaphores. Data moves between devices by JAX's collectives and lax.ppermute only.
A program may use at most 64 MiB of HBM per device.

v0:
```python
import jax
import jax.numpy as jnp
from jax import lax
from jax.sharding import PartitionSpec as P

HEADS = 8
PATCH = 512


def per_device(points, cotangent, dest, w_qkv, w_proj, gain):
    feats_in = points[0]
    grads_in = cotangent[0]
    places = dest[0]
    rows_dev = feats_in.shape[0]
    width = feats_in.shape[1]
    n_seq = lax.axis_size("seq")
    capacity = 2 * (rows_dev // n_seq)
    owner = places // rows_dev
    slot_local = places % rows_dev
    onehot = (owner[:, None] == jnp.arange(n_seq, dtype=jnp.int32)[None, :]).astype(jnp.int32)
    rank = jnp.sum((jnp.cumsum(onehot, axis=0) - 1) * onehot, axis=1)
    send_slot = owner * capacity + rank
    send_pos = jnp.full((n_seq * capacity,), rows_dev, jnp.int32).at[send_slot].set(slot_local)
    send_pos = send_pos.reshape(n_seq, capacity)

    def pack(values):
        filled = jnp.zeros((n_seq * capacity, width), values.dtype).at[send_slot].set(values)
        return filled.reshape(n_seq, capacity, width)

    def unpack(received, recv_flat):
        flat_vals = received.reshape(n_seq * capacity, width)
        return (
            jnp.zeros((rows_dev, width), received.dtype).at[recv_flat].set(flat_vals, mode="drop")
        )

    recv_feats, recv_grads, recv_pos = (
        lax.all_to_all(pack(feats_in), "seq", split_axis=0, concat_axis=0, tiled=True),
        lax.all_to_all(pack(grads_in), "seq", split_axis=0, concat_axis=0, tiled=True),
        lax.all_to_all(send_pos, "seq", split_axis=0, concat_axis=0, tiled=True),
    )
    recv_flat = recv_pos.reshape(-1)
    serial = unpack(recv_feats, recv_flat)
    feats = serial.astype(jnp.float32)
    centered_input = feats - jnp.mean(feats, axis=1, keepdims=True)
    inverse_deviation = lax.rsqrt(
        jnp.mean(centered_input * centered_input, axis=1, keepdims=True) + 1e-05
    )
    standardized_input = centered_input * inverse_deviation
    normalized_input = (standardized_input * gain[None, :]).astype(jnp.bfloat16)
    qkv = jnp.dot(normalized_input, w_qkv, preferred_element_type=jnp.float32).astype(jnp.bfloat16)
    serial_grad = unpack(recv_grads, recv_flat)
    d_attn = jnp.dot(serial_grad, w_proj.T, preferred_element_type=jnp.float32).astype(jnp.bfloat16)
    patches = rows_dev // PATCH
    head_dim = width // HEADS
    group_heads = 2
    group_cols = group_heads * head_dim
    scale = 1.0 / head_dim**0.5
    attn_list, dq_list, dk_list, dv_list = ([], [], [], [])
    for group_idx in range(HEADS // group_heads):
        lo_col = group_idx * group_cols
        shape_four = (patches, PATCH, group_heads, head_dim)
        query = qkv[:, lo_col : lo_col + group_cols].reshape(shape_four)
        keys = qkv[:, width + lo_col : width + lo_col + group_cols].reshape(shape_four)
        values = qkv[:, 2 * width + lo_col : 2 * width + lo_col + group_cols].reshape(shape_four)
        grad_head = d_attn[:, lo_col : lo_col + group_cols].reshape(shape_four)
        scores = (
            jnp.einsum("pqhd,pkhd->phqk", query, keys, preferred_element_type=jnp.float32) * scale
        )
        top = jnp.max(scores, axis=3, keepdims=True)
        expo = jnp.exp(scores - top)
        probs = expo / jnp.sum(expo, axis=3, keepdims=True)
        probs_b = probs.astype(jnp.bfloat16)
        attn_list.append(
            jnp.einsum("phqk,pkhd->pqhd", probs_b, values, preferred_element_type=jnp.float32)
            .astype(jnp.bfloat16)
            .reshape(rows_dev, group_cols)
        )
        d_probs = jnp.einsum(
            "pqhd,pkhd->phqk", grad_head, values, preferred_element_type=jnp.float32
        )
        d_scores = (
            probs * (d_probs - jnp.sum(d_probs * probs, axis=3, keepdims=True)) * scale
        ).astype(jnp.bfloat16)
        dq_list.append(
            jnp.einsum("phqk,pkhd->pqhd", d_scores, keys, preferred_element_type=jnp.float32)
            .astype(jnp.bfloat16)
            .reshape(rows_dev, group_cols)
        )
        dk_list.append(
            jnp.einsum("phqk,pqhd->pkhd", d_scores, query, preferred_element_type=jnp.float32)
            .astype(jnp.bfloat16)
            .reshape(rows_dev, group_cols)
        )
        dv_list.append(
            jnp.einsum("phqk,pqhd->pkhd", probs_b, grad_head, preferred_element_type=jnp.float32)
            .astype(jnp.bfloat16)
            .reshape(rows_dev, group_cols)
        )
    attn = jnp.concatenate(attn_list, axis=1)
    d_qkv = jnp.concatenate(dq_list + dk_list + dv_list, axis=1)
    grad_proj = jnp.einsum("rc,rd->cd", attn, serial_grad, preferred_element_type=jnp.float32)
    grad_qkv = jnp.einsum("rc,rd->cd", normalized_input, d_qkv, preferred_element_type=jnp.float32)
    normalized_gradient = jnp.dot(d_qkv, w_qkv.T, preferred_element_type=jnp.float32)
    gain_gradient = jnp.sum(normalized_gradient * standardized_input, axis=0)
    gain_scaled = normalized_gradient * gain[None, :]
    residual_branch = inverse_deviation * (
        gain_scaled
        - jnp.mean(gain_scaled, axis=1, keepdims=True)
        - standardized_input * jnp.mean(gain_scaled * standardized_input, axis=1, keepdims=True)
    )
    serial_dx = (serial_grad.astype(jnp.float32) + residual_branch).astype(jnp.bfloat16)
    back_rows = serial_dx[jnp.minimum(recv_flat, rows_dev - 1)].reshape(n_seq, capacity, width)
    returned = lax.all_to_all(back_rows, "seq", split_axis=0, concat_axis=0, tiled=True)
    grad_local = returned.reshape(n_seq * capacity, width)[send_slot]
    grad_qkv, grad_proj, gain_gradient = lax.psum(
        (grad_qkv, grad_proj, gain_gradient), ("seq", "dp")
    )
    return (grad_local[None], grad_qkv, grad_proj, gain_gradient)


def solution(mesh):
    return jax.shard_map(
        per_device,
        mesh=mesh,
        in_specs=(P("dp", "seq", None), P("dp", "seq", None), P("dp", "seq"), P(), P(), P()),
        out_specs=(P("dp", "seq", None), P(), P(), P()),
        check_vma=False,
    )
```

profile of v0, /device:TPU:0, one launch (start us, length us, event | category | flops | bytes accessed | tf_op | source)
XLA Modules:
  0.0 338.1 jit_solution(12128334725376511528)
XLA Ops:
  10.9 3.0 scatter_custom_fusion
  13.9 5.2 %all-to-all-start = ((s32[8,1,128]{2,1,0:T(1,128)}), s32[8,1,128]{2,1,0:T(1,128)S(1)}, u32[]{:S(2)}, u32[]{:S(2)}) async-start(s32[8,1,128]{2,1,0:T(1,128)} %bitcast.7), calls=%async_computation | async-start | bytes 8192 | tf_op jit(solution)/shard_map/all_to_all | solution.py:39
  19.1 4.0 %scatter_custom_fusion.3 = bf16[1024,512]{1,0:T(8,128)(2,1)} fusion(s32[512]{0:T(512)S(1)} %bitcast.265, bf16[1,512,512]{2,1,0:T(8,128)(2,1)} %param.6, bf16[]{:T(256)} %constant.46.clone.1), kind=kCustom, calls=%fused_computation.106 | custom fusion | bytes 1572866 | tf_op jit(solution)/shard_map/scatter | solution.py:27
  23.7 3.6 %all-to-all-start.2 = ((bf16[8,128,512]{2,1,0:T(8,128)(2,1)}), bf16[8,128,512]{2,1,0:T(8,128)(2,1)S(1)}, u32[]{:S(2)}, u32[]{:S(2)}) async-start(bf16[8,128,512]{2,1,0:T(8,128)(2,1)} %bitcast.14), calls=%async_computation.2 | async-start | bytes 2097152 | tf_op jit(solution)/shard_map/all_to_all | solution.py:37
  27.3 3.5 %scatter_custom_fusion.1 = bf16[1024,512]{1,0:T(8,128)(2,1)} fusion(s32[512]{0:T(512)S(1)} %bitcast.266, bf16[1,512,512]{2,1,0:T(8,128)(2,1)S(1)} %copy-done.6, bf16[]{:T(256)} %constant.46.clone.1), kind=kCustom, calls=%fused_computation.108 | custom fusion | bytes 1572866 | tf_op jit(solution)/shard_map/scatter | solution.py:27
  30.7 11.9 %all-to-all-done.2 = bf16[8,128,512]{2,1,0:T(8,128)(2,1)S(1)} async-done(((bf16[8,128,512]{2,1,0:T(8,128)(2,1)}), bf16[8,128,512]{2,1,0:T(8,128)(2,1)S(1)}, u32[]{:S(2)}, u32[]{:S(2)}) %all-to-all-start.2) | async-done | bytes 1048608 | tf_op jit(solution)/shard_map/all_to_all | solution.py:37
  42.7 4.2 %all-to-all-start.1 = ((bf16[8,128,512]{2,1,0:T(8,128)(2,1)}), bf16[8,128,512]{2,1,0:T(8,128)(2,1)}, u32[]{:S(2)}, u32[]{:S(2)}) async-start(bf16[8,128,512]{2,1,0:T(8,128)(2,1)} %bitcast.11), calls=%async_computation.1 | async-start | bytes 2097152 | tf_op jit(solution)/shard_map/all_to_all | solution.py:38
  47.0 5.6 %scatter_custom_fusion.4 = bf16[512,512]{1,0:T(8,128)(2,1)S(1)} fusion(s32[1024]{0:T(1024)S(1)} %bitcast.269, bf16[1024,512]{1,0:T(8,128)(2,1)} %bitcast.199, bf16[]{:T(256)} %constant.46.clone.1), kind=kCustom, calls=%fused_computation.120 | custom fusion | bytes 524800 | tf_op jit(solution)/shard_map/scatter | solution.py:33
  53.2 9.1 %all-to-all-done.1 = bf16[8,128,512]{2,1,0:T(8,128)(2,1)} async-done(((bf16[8,128,512]{2,1,0:T(8,128)(2,1)}), bf16[8,128,512]{2,1,0:T(8,128)(2,1)}, u32[]{:S(2)}, u32[]{:S(2)}) %all-to-all-start.1) | async-done | bytes 1048608 | tf_op jit(solution)/shard_map/all_to_all | solution.py:38
  62.3 5.9 %scatter_custom_fusion.2 = bf16[512,512]{1,0:T(8,128)(2,1)S(1)} fusion(s32[1024]{0:T(1024)S(1)} %bitcast.270, bf16[1024,512]{1,0:T(8,128)(2,1)} %bitcast.12, bf16[]{:T(256)} %constant.46.clone.1), kind=kCustom, calls=%fused_computation.122 | custom fusion | bytes 524800 | tf_op jit(solution)/shard_map/scatter | solution.py:33
  71.7 1.7 copy.55
  73.3 1.7 copy.54
  75.0 1.7 copy.53
  76.7 2.8 fusion.201
  79.4 3.8 %fusion.197 = (f32[2,512]{1,0:T(2,128)}, f32[2,512,512]{1,2,0:T(8,128)}) fusion(bf16[512,2,64]{0,2,1:T(8,128)(2,1)} %bitcast.236, bf16[512,2,64]{0,2,1:T(8,128)(2,1)} %bitcast.240), kind=kOutput, calls=%fused_computation.202 | convolution fusion | flops 68682240 | bytes 2363392 | tf_op jit(solution)/shard_map/sub | solution.py:70
  83.2 2.8 convolution_convert_fusion.9
  86.0 2.8 convolution_convert_fusion.5
  88.8 5.0 %fusion.75 = bf16[2,64,512]{2,1,0:T(8,128)(2,1)} fusion(bf16[512,2,64]{0,2,1:T(8,128)(2,1)} %bitcast.239, f32[2,512,512]{1,2,0:T(8,128)} %fusion.201, f32[2,512,512]{1,2,0:T(8,128)} %get-tuple-element.30, f32[2,512]{1,0:T(2,128)} %get-tuple-element.29), kind=kOutput, calls=%fused_computation.64 | convolution fusion | flops 70845952 | bytes 4460544 | tf_op jit(solution)/shard_map/phqk,pqhd->pkhd/dot_general | solution.py:90
  93.8 5.1 %fusion.72 = bf16[2,64,512]{2,1,0:T(8,128)(2,1)} fusion(bf16[512,2,64]{0,2,1:T(8,128)(2,1)} %bitcast.243, f32[2,512,512]{1,2,0:T(8,128)} %fusion.201, f32[2,512,512]{1,2,0:T(8,128)} %get-tuple-element.30, f32[2,512]{1,0:T(2,128)} %get-tuple-element.29), kind=kOutput, calls=%fused_computation.63 | convolution fusion | flops 70845952 | bytes 4460544 | tf_op jit(solution)/shard_map/phqk,pkhd->pqhd/dot_general | solution.py:85
  99.0 1.7 copy.59
  100.6 1.7 copy.58
  103.0 2.8 fusion.202
  105.8 3.7 %fusion.198 = (f32[2,512]{1,0:T(2,128)}, f32[2,512,512]{1,2,0:T(8,128)}) fusion(bf16[512,2,64]{0,2,1:T(8,128)(2,1)S(1)} %bitcast.247, bf16[512,2,64]{0,2,1:T(8,128)(2,1)} %bitcast.248), kind=kOutput, calls=%fused_computation.203 | convolution fusion | flops 68682240 | bytes 2363392 | tf_op jit(solution)/shard_map/sub | solution.py:70
  109.6 2.9 convolution_convert_fusion.8
  112.4 2.7 convolution_convert_fusion.4
  115.2 5.0 %fusion.69 = bf16[2,64,512]{2,1,0:T(8,128)(2,1)} fusion(bf16[512,2,64]{0,2,1:T(8,128)(2,1)} %bitcast.246, f32[2,512,512]{1,2,0:T(8,128)} %fusion.202, f32[2,512,512]{1,2,0:T(8,128)} %get-tuple-element.32, f32[2,512]{1,0:T(2,128)} %get-tuple-element.31), kind=kOutput, calls=%fused_computation.62 | convolution fusion | flops 70845952 | bytes 4460544 | tf_op jit(solution)/shard_map/phqk,pqhd->pkhd/dot_general | solution.py:90
  120.2 5.1 %fusion.66 = bf16[2,64,512]{2,1,0:T(8,128)(2,1)} fusion(bf16[512,2,64]{0,2,1:T(8,128)(2,1)S(1)} %bitcast.251, f32[2,512,512]{1,2,0:T(8,128)} %fusion.202, f32[2,512,512]{1,2,0:T(8,128)} %get-tuple-element.32, f32[2,512]{1,0:T(2,128)} %get-tuple-element.31), kind=kOutput, calls=%fused_computation.61 | convolution fusion | flops 70845952 | bytes 4460544 | tf_op jit(solution)/shard_map/phqk,pkhd->pqhd/dot_general | solution.py:85
  125.7 2.8 fusion.203
  128.4 12.6 %fusion.199 = (f32[2,512]{1,0:T(2,128)}, f32[2,512,512]{1,2,0:T(8,128)}) fusion(bf16[512,2,64]{0,2,1:T(8,128)(2,1)S(1)} %bitcast.252, bf16[512,2,64]{0,2,1:T(8,128)(2,1)S(1)} %bitcast.256), kind=kOutput, calls=%fused_computation.204 | convolution fusion | flops 68682240 | bytes 2363392 | tf_op jit(solution)/shard_map/sub | solution.py:70
  141.1 2.1 convolution_convert_fusion.7
  143.1 2.7 convolution_convert_fusion.3
  145.8 4.4 %fusion.63 = bf16[2,64,512]{2,1,0:T(8,128)(2,1)S(1)} fusion(bf16[512,2,64]{0,2,1:T(8,128)(2,1)} %bitcast.255, f32[2,512,512]{1,2,0:T(8,128)} %fusion.203, f32[2,512,512]{1,2,0:T(8,128)} %get-tuple-element.34, f32[2,512]{1,0:T(2,128)S(1)} %copy-done.30), kind=kOutput, calls=%fused_computation.60 | convolution fusion | flops 70845952 | bytes 4460544 | tf_op jit(solution)/shard_map/phqk,pqhd->pkhd/dot_general | solution.py:90
  150.2 5.1 %fusion.60 = bf16[2,64,512]{2,1,0:T(8,128)(2,1)} fusion(bf16[512,2,64]{0,2,1:T(8,128)(2,1)S(1)} %bitcast.259, f32[2,512,512]{1,2,0:T(8,128)} %fusion.203, f32[2,512,512]{1,2,0:T(8,128)} %get-tuple-element.34, f32[2,512]{1,0:T(2,128)} %get-tuple-element.33), kind=kOutput, calls=%fused_computation.59 | convolution fusion | flops 70845952 | bytes 4460544 | tf_op jit(solution)/shard_map/phqk,pkhd->pqhd/dot_general | solution.py:85
  155.7 1.8 fusion.204
  157.5 2.8 fusion.200
  160.3 2.1 convolution_convert_fusion.6
  162.5 2.5 convolution_convert_fusion.2
  165.0 5.0 %fusion.57 = bf16[2,64,512]{2,1,0:T(8,128)(2,1)} fusion(bf16[512,2,64]{0,2,1:T(8,128)(2,1)S(1)} %bitcast.231, f32[2,512,512]{1,2,0:T(8,128)} %fusion.204, f32[2,512,512]{1,2,0:T(8,128)} %get-tuple-element.36, f32[2,512]{1,0:T(2,128)S(1)} %copy-done.31), kind=kOutput, calls=%fused_computation.58 | convolution fusion | flops 70845952 | bytes 4460544 | tf_op jit(solution)/shard_map/phqk,pqhd->pkhd/dot_general | solution.py:90
  169.9 5.2 %fusion.54 = bf16[2,64,512]{2,1,0:T(8,128)(2,1)} fusion(bf16[512,2,64]{0,2,1:T(8,128)(2,1)} %bitcast.235, f32[2,512,512]{1,2,0:T(8,128)} %fusion.204, f32[2,512,512]{1,2,0:T(8,128)} %get-tuple-element.36, f32[2,512]{1,0:T(2,128)} %get-tuple-element.35), kind=kOutput, calls=%fused_computation.57 | convolution fusion | flops 70845952 | bytes 4460544 | tf_op jit(solution)/shard_map/phqk,pkhd->pqhd/dot_general | solution.py:85
  178.2 2.7 fusion.132
  181.0 1.4 fusion.98
  183.1 2.6 fusion.84
  186.3 5.1 %gather_fusion = bf16[1024,512]{1,0:T(8,128)(2,1)} fusion(bf16[512,512]{1,0:T(8,128)(2,1)S(1)} %copy.77, s32[1024]{0:T(1024)S(1)} %broadcast_clamp_fusion), kind=kCustom, calls=%fused_computation | custom fusion | bytes 2101248 | tf_op jit(solution)/shard_map/gather | solution.py:112
  191.4 3.6 %all-to-all-start.3 = ((bf16[8,128,512]{2,1,0:T(8,128)(2,1)}), bf16[8,128,512]{2,1,0:T(8,128)(2,1)S(1)}, u32[]{:S(2)}, u32[]{:S(2)}) async-start(bf16[8,128,512]{2,1,0:T(8,128)(2,1)} %bitcast.198), calls=%async_computation.3 | async-start | bytes 2097152 | tf_op jit(solution)/shard_map/all_to_all | solution.py:113
  195.0 51.9 %psum.23 = f32[512]{0:T(512)} all-reduce(f32[512]{0:T(512)S(1)} %get-tuple-element.4), channel_id=1, replica_groups=mesh['seq'=8,'dp'=4] {'seq','dp'}, use_global_device_ids=true, to_apply=%region_27.28 | all-reduce | flops 512 | bytes 4096 | tf_op jit(solution)/shard_map/psum | solution.py:115
  246.9 2.6 gather_fusion.1
  249.6 76.7 %all-reduce.3.cloned.1.call-done = (f32[512,1536]{1,0:T(8,128)}, f32[512,512]{1,0:T(8,128)}) async-done(((f32[512,1536]{1,0:T(8,128)}, f32[512,512]{1,0:T(8,128)}), (f32[512,1536]{1,0:T(8,128)}, f32[512,512]{1,0:T(8,128)})) %all-reduce.3.cloned.1.call-update) | async-done | bytes 4194320 | tf_op jit(solution)/shard_map/psum | solution.py:115
  326.2 3.8 %copy.111 = f32[512,1536]{1,0:T(8,128)} copy(f32[512,1536]{1,0:T(8,128)} %get-tuple-element.41) | data formatting | bytes 6291456
  (113 shorter events, 15.1 us)
Async XLA Ops:
  7.2 62.4 %copy-start = (bf16[512,1536]{1,0:T(8,128)(2,1)S(1)}, bf16[512,1536]{1,0:T(8,128)(2,1)}, u32[]{:S(2)}) copy-start(bf16[512,1536]{1,0:T(8,128)(2,1)} %param.9) | copy-start | bytes 4718596
  7.2 20.1 %copy-start.6 = (bf16[1,512,512]{2,1,0:T(8,128)(2,1)S(1)}, bf16[1,512,512]{2,1,0:T(8,128)(2,1)}, u32[]{:S(2)}) copy-start(bf16[1,512,512]{2,1,0:T(8,128)(2,1)} %param.7) | copy-start | bytes 1572868
  13.9 9.8 %all-to-all-start = ((s32[8,1,128]{2,1,0:T(1,128)}), s32[8,1,128]{2,1,0:T(1,128)S(1)}, u32[]{:S(2)}, u32[]{:S(2)}) async-start(s32[8,1,128]{2,1,0:T(1,128)} %bitcast.7), calls=%async_computation | async-start | bytes 8192 | tf_op jit(solution)/shard_map/all_to_all | solution.py:39
  23.7 19.0 %all-to-all-start.2 = ((bf16[8,128,512]{2,1,0:T(8,128)(2,1)}), bf16[8,128,512]{2,1,0:T(8,128)(2,1)S(1)}, u32[]{:S(2)}, u32[]{:S(2)}) async-start(bf16[8,128,512]{2,1,0:T(8,128)(2,1)} %bitcast.14), calls=%async_computation.2 | async-start | bytes 2097152 | tf_op jit(solution)/shard_map/all_to_all | solution.py:37
  42.7 4.3 %copy-start.3 = (bf16[8,128,512]{2,1,0:T(8,128)(2,1)}, bf16[8,128,512]{2,1,0:T(8,128)(2,1)S(1)}, u32[]{:S(2)}) copy-start(bf16[8,128,512]{2,1,0:T(8,128)(2,1)S(1)} %all-to-all-done.2) | copy-start | bytes 3145732
  42.7 19.7 %all-to-all-start.1 = ((bf16[8,128,512]{2,1,0:T(8,128)(2,1)}), bf16[8,128,512]{2,1,0:T(8,128)(2,1)}, u32[]{:S(2)}, u32[]{:S(2)}) async-start(bf16[8,128,512]{2,1,0:T(8,128)(2,1)} %bitcast.11), calls=%async_computation.1 | async-start | bytes 2097152 | tf_op jit(solution)/shard_map/all_to_all | solution.py:38
  46.9 21.3 %copy-start.4 = (bf16[512,512]{1,0:T(8,128)(2,1)S(1)}, bf16[512,512]{1,0:T(8,128)(2,1)}, u32[]{:S(2)}) copy-start(bf16[512,512]{1,0:T(8,128)(2,1)} %param.10) | copy-start | bytes 1572868
  46.9 279.3 %all-reduce.3.cloned.1.call-start = ((), (), s32[]{:S(2)}) async-start(), calls=%async_computation.4 | async-start | bytes 8388608 | tf_op jit(solution)/shard_map/psum | solution.py:115
  52.9 16.7 %copy-start.23 = (f32[512]{0:T(512)S(1)}, f32[512]{0:T(512)}, u32[]{:S(2)}) copy-start(f32[512]{0:T(512)} %param.11) | copy-start | bytes 6148
  103.0 2.8 copy-start.18
  109.6 2.9 copy-start.5
  115.2 5.0 %copy-start.19 = (bf16[512,128]{0,1:T(8,128)(2,1)S(1)}, bf16[512,128]{0,1:T(8,128)(2,1)}, u32[]{:S(2)}) copy-start(bf16[512,128]{0,1:T(8,128)(2,1)} %copy.57) | copy-start | bytes 393220
  125.5 17.6 %copy-start.20 = (bf16[512,128]{0,1:T(8,128)(2,1)}, bf16[512,128]{0,1:T(8,128)(2,1)S(1)}, u32[]{:S(2)}) copy-start(bf16[512,128]{0,1:T(8,128)(2,1)S(1)} %copy.62) | copy-start | bytes 393220
  125.7 15.4 %copy-start.21 = (bf16[512,128]{0,1:T(8,128)(2,1)}, bf16[512,128]{0,1:T(8,128)(2,1)S(1)}, u32[]{:S(2)}) copy-start(bf16[512,128]{0,1:T(8,128)(2,1)S(1)} %copy.61) | copy-start | bytes 393220
  125.7 15.4 %copy-start.8 = (bf16[512,128]{0,1:T(8,128)(2,1)S(1)}, bf16[512,128]{0,1:T(8,128)(2,1)}, u32[]{:S(2)}) copy-start(bf16[512,128]{0,1:T(8,128)(2,1)} %get-tuple-element.22) | copy-start | bytes 393220
  143.1 2.7 copy-start.30
  145.8 4.4 %copy-start.22 = (bf16[512,128]{0,1:T(8,128)(2,1)S(1)}, bf16[512,128]{0,1:T(8,128)(2,1)}, u32[]{:S(2)}) copy-start(bf16[512,128]{0,1:T(8,128)(2,1)} %copy-done.21) | copy-start | bytes 393220
  150.2 5.5 %copy-start.7 = (bf16[512,128]{0,1:T(8,128)(2,1)S(1)}, bf16[512,128]{0,1:T(8,128)(2,1)}, u32[]{:S(2)}) copy-start(bf16[512,128]{0,1:T(8,128)(2,1)} %get-tuple-element.21) | copy-start | bytes 393220
  155.4 4.9 %copy-start.15 = (bf16[512,128]{0,1:T(8,128)(2,1)}, bf16[512,128]{0,1:T(8,128)(2,1)S(1)}, u32[]{:S(2)}) copy-start(bf16[512,128]{0,1:T(8,128)(2,1)S(1)} %copy.66) | copy-start | bytes 393220
  155.7 6.8 %copy-start.17 = (bf16[512,128]{0,1:T(8,128)(2,1)}, bf16[512,128]{0,1:T(8,128)(2,1)S(1)}, u32[]{:S(2)}) copy-start(bf16[512,128]{0,1:T(8,128)(2,1)S(1)} %copy.65) | copy-start | bytes 393220
  160.3 2.2 copy-start.16
  162.5 2.5 copy-start.31
  169.9 5.2 %copy-start.12 = (bf16[2,64,512]{2,1,0:T(8,128)(2,1)S(1)}, bf16[2,64,512]{2,1,0:T(8,128)(2,1)}, u32[]{:S(2)}) copy-start(bf16[2,64,512]{2,1,0:T(8,128)(2,1)} %fusion.72) | copy-start | bytes 393220
  169.9 5.2 %copy-start.14 = (bf16[2,64,512]{2,1,0:T(8,128)(2,1)S(1)}, bf16[2,64,512]{2,1,0:T(8,128)(2,1)}, u32[]{:S(2)}) copy-start(bf16[2,64,512]{2,1,0:T(8,128)(2,1)} %fusion.66) | copy-start | bytes 393220
  169.9 7.2 %copy-start.10 = (bf16[2,64,512]{2,1,0:T(8,128)(2,1)S(1)}, bf16[2,64,512]{2,1,0:T(8,128)(2,1)}, u32[]{:S(2)}) copy-start(bf16[2,64,512]{2,1,0:T(8,128)(2,1)} %fusion.75) | copy-start | bytes 393220
  169.9 7.2 %copy-start.13 = (bf16[2,64,512]{2,1,0:T(8,128)(2,1)S(1)}, bf16[2,64,512]{2,1,0:T(8,128)(2,1)}, u32[]{:S(2)}) copy-start(bf16[2,64,512]{2,1,0:T(8,128)(2,1)} %fusion.69) | copy-start | bytes 393220
  175.1 3.0 copy-start.9
  175.1 3.0 copy-start.11
  175.1 3.1 copy-start.24
  178.2 2.8 copy-start.1
  178.2 2.8 copy-start.26
  178.2 2.8 copy-start.27
  178.2 2.7 copy-start.28
  178.2 2.7 copy-start.29
  182.4 0.7 copy-start.25
  191.4 55.5 %all-to-all-start.3 = ((bf16[8,128,512]{2,1,0:T(8,128)(2,1)}), bf16[8,128,512]{2,1,0:T(8,128)(2,1)S(1)}, u32[]{:S(2)}, u32[]{:S(2)}) async-start(bf16[8,128,512]{2,1,0:T(8,128)(2,1)} %bitcast.198), calls=%async_computation.3 | async-start | bytes 2097152 | tf_op jit(solution)/shard_map/all_to_all | solution.py:113
  326.2 3.8 %copy-start.2 = (f32[512,512]{1,0:T(8,128)S(1)}, f32[512,512]{1,0:T(8,128)}, u32[]{:S(2)}) copy-start(f32[512,512]{1,0:T(8,128)} %get-tuple-element.42) | copy-start | bytes 3145732
Sparse Core Ops, SparseCore 0:
  182.6 143.6 all-reduce.2
where the time goes:
time: 343 us; the launch traced here: 338 us
  matrix products  102 us (30%)
  waiting for transfers between devices  98.4 us (29%)
  blocking collectives  51.9 us (15%)
  local copies, waits for them, and re-layouts  50.4 us (15%)
  starting transfers between devices  16.6 us (5%)
  between operations  14.7 us (4%)
  other arithmetic  4.24 us (1%)
    psum x1, waiting for transfers between devices, per_device(): lax.psum((grad_qkv, grad_proj, gain_gradient), ('seq', 'dp'))  76.7 us
    psum x1, blocking collectives, per_device(): lax.psum((grad_qkv, grad_proj, gain_gradient), ('seq', 'dp'))  51.9 us
    sub x4, matrix products, per_device(): expo = jnp.exp(scores - top)  22.9 us
    dot_general x4, matrix products, per_device(): jnp.einsum('phqk,pkhd->pqhd', d_scores, keys, preferred_element_type=jnp....  20.5 us
    dot_general x4, matrix products, per_device(): jnp.einsum('phqk,pqhd->pkhd', d_scores, query, preferred_element_type=jnp...  19.3 us
    scatter x4, local copies, waits for them, and re-layouts, unpack(): jnp.zeros((rows_dev, width), received.dtype).at[recv_flat]  11.9 us
    all_to_all x1, waiting for transfers between devices, per_device(): lax.all_to_all(pack(feats_in), 'seq', split_axis=0, concat_axis=0, tiled=...  11.9 us
    dot_general x4, matrix products, per_device(): jnp.einsum('phqk,pkhd->pqhd', probs_b, values, preferred_element_type=jnp...  10.7 us
  transfers between devices with their start and end apart: 5, of which 4 were waited for; matrix products, arithmetic and copies ran while one was open for 7% of the time, Pallas kernels for 0%

commit v1 on v0

v1 whole, which is shorter than its diff:
```python
import functools

import jax
import jax.numpy as jnp
from jax import lax
from jax.experimental import pallas as pl
from jax.experimental.pallas import tpu as pltpu
from jax.sharding import PartitionSpec as P

HEADS = 8
PATCH = 512
EXTRA = 16
LANES = 128
VMEM_LIMIT = 48 * 1024 * 1024
F32 = jnp.float32
BF16 = jnp.bfloat16
NN = (((1,), (0,)), ((), ()))
NT = (((1,), (1,)), ((), ()))


def mm(lhs, rhs, dims=NN):
    return lax.dot_general(lhs, rhs, dims, preferred_element_type=F32)


def iota(shape, dim):
    return lax.broadcasted_iota(jnp.int32, shape, dim)


def hot(mask):
    return jnp.where(mask, jnp.float32(1), jnp.float32(0)).astype(BF16)


def column_hot(row, count):
    size = row.shape[1]
    column = jnp.transpose(jnp.broadcast_to(row, (LANES, size)))
    lane = iota((size, LANES), 1)
    return jnp.concatenate([hot(column == lane + j * LANES) for j in range(count // LANES)], axis=1)


def pack_kernel(n_seq, capacity, me_ref, dest_ref, feats_ref, grads_ref, feats_out, grads_out, slot_out):
    rows, width = feats_ref.shape
    slots = n_seq * capacity
    shift = rows.bit_length() - 1
    places = dest_ref[...]
    owner = lax.shift_right_logical(places, shift)
    within = lax.bitwise_and(places, rows - 1) + 1
    member = iota((n_seq, rows), 0) == owner
    upper = hot(iota((rows, rows), 0) <= iota((rows, rows), 1))
    counts = mm(hot(member), upper)
    rank = jnp.sum(jnp.where(member, counts, 0.0), axis=0, keepdims=True).astype(jnp.int32) - 1
    slot = owner * capacity + rank
    slot_out[...] = slot
    select = hot(iota((slots, rows), 0) == slot)
    feats = mm(select, feats_ref[...]).astype(BF16)
    target = rank + me_ref[0] * capacity
    upper_half = target >= width
    high = lax.shift_right_logical(within, 8).astype(F32)
    low = lax.bitwise_and(within, 255).astype(F32)
    line = iota((n_seq * EXTRA, rows), 0)
    kind = lax.bitwise_and(line, EXTRA - 1)
    digit = jnp.where(kind < 2, high, low)
    wanted = (
        (lax.shift_right_logical(line, EXTRA.bit_length() - 1) == owner)
        & (kind < 4)
        & ((lax.bitwise_and(kind, 1) == 1) == upper_half)
    )
    digits = jnp.where(wanted, digit, 0.0).astype(BF16)
    spread = hot(iota((width, rows), 0) == lax.bitwise_and(target, width - 1))
    position = mm(digits, spread, NT).astype(BF16)
    block = capacity + EXTRA
    for d in range(n_seq):
        feats_out[d * block : d * block + capacity, :] = feats[d * capacity : (d + 1) * capacity]
        feats_out[d * block + capacity : (d + 1) * block, :] = position[d * EXTRA : (d + 1) * EXTRA]
    grads_out[...] = mm(select, grads_ref[...]).astype(BF16)


def forward_kernel(
    n_seq,
    capacity,
    recv_ref,
    w_ref,
    gain_ref,
    pos_out,
    xhat_out,
    inv_out,
    normed_out,
    qkv_out,
    attn_out,
    probs_out,
    trans,
):
    width = w_ref.shape[0]
    rows = xhat_out.shape[0]
    head = width // HEADS
    pair = 2 * head
    step = pl.program_id(0)

    @pl.when(step == 0)
    def _():
        block = capacity + EXTRA
        tile = recv_ref[capacity:block, :].astype(F32)
        for s in range(1, n_seq):
            tile = tile + recv_ref[s * block + capacity : (s + 1) * block, :].astype(F32)
        high = jnp.concatenate([tile[0:1], tile[1:2]], axis=1)
        low = jnp.concatenate([tile[2:3], tile[3:4]], axis=1)
        pos = (high * 256.0 + low).astype(jnp.int32) - 1
        pos_out[...] = pos
        place = hot(iota((rows, n_seq * capacity), 0) == pos)
        values = jnp.concatenate(
            [recv_ref[s * block : s * block + capacity, :] for s in range(n_seq)], axis=0
        )
        feats = mm(place, values)
        centered = feats - jnp.mean(feats, axis=1, keepdims=True)
        inv = lax.rsqrt(jnp.mean(centered * centered, axis=1, keepdims=True) + 1e-05)
        xhat = centered * inv
        xhat_out[...] = xhat
        inv_out[...] = jnp.broadcast_to(inv, inv_out.shape)
        normed = (xhat * gain_ref[...]).astype(BF16)
        normed_out[...] = normed
        qkv = mm(normed, w_ref[...])
        qkv_out[...] = qkv.astype(BF16)
        trans[...] = jnp.transpose(qkv).astype(BF16)

    lo = pl.multiple_of(step * pair, pair)
    keys = qkv_out[:, pl.ds(pl.multiple_of(width + step * pair, pair), pair)]
    query_t = trans[pl.ds(lo, pair), :] * BF16(0.125)
    zero = jnp.zeros((head, rows), BF16)
    for j in range(2):
        part = query_t[j * head : (j + 1) * head]
        part = jnp.concatenate([part, zero] if j == 0 else [zero, part], axis=0)
        scores = mm(keys, part)
        expo = jnp.exp(scores - jnp.max(scores, axis=0, keepdims=True))
        probs = expo * (1.0 / jnp.sum(expo, axis=0, keepdims=True))
        probs_out[j] = probs
        values_t = trans[pl.ds(pl.multiple_of(2 * width + step * pair + j * head, head), head), :]
        attn_out[j * head : (j + 1) * head, :] = mm(values_t, probs.astype(BF16)).astype(BF16)


def backward_kernel(
    recv_ref,
    pos_ref,
    w_qkv_ref,
    w_proj_ref,
    gain_ref,
    xhat_ref,
    inv_ref,
    normed_ref,
    qkv_ref,
    attn_ref,
    probs_ref,
    grad_qkv_out,
    grad_proj_out,
    gain_out,
    back_out,
    serial_grad,
    d_attn,
    d_attn_t,
    keys_t,
    d_qkv,
):
    width = w_proj_ref.shape[0]
    rows = xhat_ref.shape[0]
    head = width // HEADS
    pair = 2 * head
    step = pl.program_id(0)

    @pl.when(step == 0)
    def _():
        place = hot(iota((rows, recv_ref.shape[0]), 0) == pos_ref[...])
        grads = mm(place, recv_ref[...]).astype(BF16)
        serial_grad[...] = grads
        d_att = mm(grads, w_proj_ref[...], NT).astype(BF16)
        d_attn[...] = d_att
        d_attn_t[...] = jnp.transpose(d_att.astype(F32)).astype(BF16)
        keys_t[...] = jnp.transpose(qkv_ref[:, width : 2 * width].astype(F32)).astype(BF16)

    lo = pl.multiple_of(step * pair, pair)
    queries = qkv_ref[:, pl.ds(lo, pair)]
    values = qkv_ref[:, pl.ds(pl.multiple_of(2 * width + step * pair, pair), pair)]
    d_att_t = d_attn_t[pl.ds(lo, pair), :] * BF16(0.125)
    d_att = d_attn[:, pl.ds(lo, pair)]
    zero = jnp.zeros((head, rows), BF16)
    d_q, d_k, d_v = [], [], []
    for j in range(2):
        part = d_att_t[j * head : (j + 1) * head]
        part = jnp.concatenate([part, zero] if j == 0 else [zero, part], axis=0)
        probs = probs_ref[j]
        d_probs = mm(values, part)
        total = jnp.sum(d_probs * probs, axis=0, keepdims=True)
        d_scores = (probs * (d_probs - total)).astype(BF16)
        k_t = keys_t[pl.ds(pl.multiple_of(step * pair + j * head, head), head), :]
        d_q.append(mm(k_t, d_scores))
        d_k.append(mm(d_scores, queries))
        d_v.append(mm(probs.astype(BF16), d_att))
    first = iota((rows, pair), 1) < head
    d_qkv[:, pl.ds(lo, pair)] = jnp.transpose(jnp.concatenate(d_q, axis=0)).astype(BF16)
    d_qkv[:, pl.ds(pl.multiple_of(width + step * pair, pair), pair)] = jnp.where(
        first, d_k[0], d_k[1]
    ).astype(BF16)
    d_qkv[:, pl.ds(pl.multiple_of(2 * width + step * pair, pair), pair)] = jnp.where(
        first, d_v[0], d_v[1]
    ).astype(BF16)

    @pl.when(step == pl.num_programs(0) - 1)
    def _():
        normed_t = jnp.transpose(normed_ref[...].astype(F32)).astype(BF16)
        grad_qkv_out[...] = mm(normed_t, d_qkv[...])
        grad_proj_out[...] = mm(attn_ref[...], serial_grad[...])
        d_normed = mm(d_qkv[...], w_qkv_ref[...], NT)
        xhat = xhat_ref[...]
        gain_out[...] = jnp.sum(d_normed * xhat, axis=0, keepdims=True)
        scaled = d_normed * gain_ref[...]
        residual = inv_ref[:, 0:1] * (
            scaled
            - jnp.mean(scaled, axis=1, keepdims=True)
            - xhat * jnp.mean(scaled * xhat, axis=1, keepdims=True)
        )
        serial_dx = (serial_grad[...].astype(F32) + residual).astype(BF16)
        back_out[...] = mm(column_hot(pos_ref[...], rows), serial_dx).astype(BF16)


def unpack_kernel(slot_ref, recv_ref, out_ref):
    out_ref[...] = mm(column_hot(slot_ref[...], recv_ref.shape[0]), recv_ref[...]).astype(BF16)


def whole(shape):
    return pl.BlockSpec(shape, lambda *_: (0,) * len(shape))


def shape_of(shape, dtype):
    return jax.ShapeDtypeStruct(shape, dtype)


def per_device(points, cotangent, dest, w_qkv, w_proj, gain):
    feats = points[0]
    grads = cotangent[0]
    rows, width = feats.shape
    n_seq = lax.axis_size("seq")
    capacity = 2 * (rows // n_seq)
    slots = n_seq * capacity
    block = capacity + EXTRA
    pairs = HEADS // 2
    pair = width // pairs
    me = jnp.reshape(lax.axis_index("seq").astype(jnp.int32), (1,))
    gain_row = gain.reshape(1, width)
    params = pltpu.CompilerParams(vmem_limit_bytes=VMEM_LIMIT)
    in_vmem = pl.BlockSpec(memory_space=pltpu.VMEM)

    feats_sent, grads_sent, slot = pl.pallas_call(
        functools.partial(pack_kernel, n_seq, capacity),
        out_shape=(
            shape_of((n_seq * block, width), BF16),
            shape_of((slots, width), BF16),
            shape_of((1, rows), jnp.int32),
        ),
        in_specs=[pl.BlockSpec(memory_space=pltpu.SMEM), in_vmem, in_vmem, in_vmem],
        out_specs=[in_vmem] * 3,
        compiler_params=params,
        cost_estimate=pl.CostEstimate(flops=2 * slots * rows * width * 2, bytes_accessed=4 << 20, transcendentals=0),
        name="pack",
    )(me, dest, feats, grads)

    def exchange(sent, size):
        sent = sent.reshape(n_seq, size, width)
        got = lax.all_to_all(sent, "seq", split_axis=0, concat_axis=0, tiled=True)
        return got.reshape(n_seq * size, width)

    feats_got = exchange(feats_sent, block)
    grads_got = exchange(grads_sent, capacity)

    pos, xhat, inv, normed, qkv, attn_t, probs = pl.pallas_call(
        functools.partial(forward_kernel, n_seq, capacity),
        grid=(pairs,),
        out_shape=(
            shape_of((1, slots), jnp.int32),
            shape_of((rows, width), F32),
            shape_of((rows, LANES), F32),
            shape_of((rows, width), BF16),
            shape_of((rows, 3 * width), BF16),
            shape_of((width, rows), BF16),
            shape_of((HEADS, rows, rows), F32),
        ),
        in_specs=[whole((n_seq * block, width)), whole((width, 3 * width)), whole((1, width))],
        out_specs=[
            whole((1, slots)),
            whole((rows, width)),
            whole((rows, LANES)),
            whole((rows, width)),
            whole((rows, 3 * width)),
            pl.BlockSpec((pair, rows), lambda i: (i, 0)),
            pl.BlockSpec((2, rows, rows), lambda i: (i, 0, 0)),
        ],
        scratch_shapes=[pltpu.VMEM((3 * width, rows), BF16)],
        compiler_params=params,
        cost_estimate=pl.CostEstimate(
            flops=6 * rows * width * width + 8 * HEADS * rows * rows * pair,
            bytes_accessed=16 << 20,
            transcendentals=HEADS * rows * rows,
        ),
        name="forward",
    )(feats_got, w_qkv, gain_row)

    grad_qkv, grad_proj, gain_grad, back = pl.pallas_call(
        backward_kernel,
        grid=(pairs,),
        out_shape=(
            shape_of((width, 3 * width), F32),
            shape_of((width, width), F32),
            shape_of((1, width), F32),
            shape_of((slots, width), BF16),
        ),
        in_specs=[
            whole((slots, width)),
            whole((1, slots)),
            whole((width, 3 * width)),
            whole((width, width)),
            whole((1, width)),
            whole((rows, width)),
            whole((rows, LANES)),
            whole((rows, width)),
            whole((rows, 3 * width)),
            whole((width, rows)),
            pl.BlockSpec((2, rows, rows), lambda i: (i, 0, 0)),
        ],
        out_specs=[
            whole((width, 3 * width)),
            whole((width, width)),
            whole((1, width)),
            whole((slots, width)),
        ],
        scratch_shapes=[
            pltpu.VMEM((rows, width), BF16),
            pltpu.VMEM((rows, width), BF16),
            pltpu.VMEM((width, rows), BF16),
            pltpu.VMEM((width, rows), BF16),
            pltpu.VMEM((rows, 3 * width), BF16),
        ],
        compiler_params=params,
        cost_estimate=pl.CostEstimate(
            flops=14 * rows * width * width + 8 * HEADS * rows * rows * pair,
            bytes_accessed=24 << 20,
            transcendentals=0,
        ),
        name="backward",
    )(grads_got, pos, w_qkv, w_proj, gain_row, xhat, inv, normed, qkv, attn_t, probs)

    returned = exchange(back, capacity)
    grad_local = pl.pallas_call(
        unpack_kernel,
        out_shape=shape_of((rows, width), BF16),
        in_specs=[in_vmem] * 2,
        out_specs=in_vmem,
        compiler_params=params,
        cost_estimate=pl.CostEstimate(flops=2 * slots * rows * width, bytes_accessed=2 << 20, transcendentals=0),
        name="unpack",
    )(slot, returned)
    grad_qkv, grad_proj, gain_grad = lax.psum((grad_qkv, grad_proj, gain_grad[0]), ("seq", "dp"))
    return (grad_local[None], grad_qkv, grad_proj, gain_grad)


def solution(mesh):
    return jax.shard_map(
        per_device,
        mesh=mesh,
        in_specs=(P("dp", "seq", None), P("dp", "seq", None), P("dp", "seq"), P(), P(), P()),
        out_specs=(P("dp", "seq", None), P(), P(), P()),
        check_vma=False,
    )
```

time: 343 us -> 232 us (0.68); the launches traced: 338 us -> 232 us
  matrix products: 102 us -> 0 us
  local copies, waits for them, and re-layouts: 50.4 us -> 13.5 us
  Pallas kernels: 0 us -> 30.3 us
  blocking collectives: 51.9 us -> 78.5 us
  waiting for transfers between devices: 98.4 us -> 88.1 us
  starting transfers between devices: 16.6 us -> 7.17 us
  other arithmetic: 4.24 us -> 0 us
    dot_general x25 -> x0, matrix products: 78.9 us -> none  [the longest x4 20.5 us: per_device(): jnp.einsum('phqk,pkhd->pqhd', d_scores, keys, preferred_element_type=jnp....]
    pallas_call x0 -> x4, Pallas kernels: none -> 30.3 us  [the longest x1 16.1 us: per_device(): pl.pallas_call(backward_kernel, grid=(pairs,), out_shape=(shape_of((width...]
    sub x4 -> x0, matrix products: 22.9 us -> none  [per_device(): expo = jnp.exp(scores - top)]
    scatter x7 -> x0, local copies, waits for them, and re-layouts: 22.4 us -> none  [the longest x4 11.9 us: unpack(): jnp.zeros((rows_dev, width), received.dtype).at[recv_flat]]
    all_to_all x0 -> x1, blocking collectives: none -> 21.9 us  [exchange(): got = lax.all_to_all(sent, 'seq', split_axis=0, concat_axis=0, tiled=True)]
    all_to_all x4 -> x2, waiting for transfers between devices: 21.7 us -> 2.44 us  [exchange(): got = lax.all_to_all(sent, 'seq', split_axis=0, concat_axis=0, tiled=True)]
    slice x15 -> x0, local copies, waits for them, and re-layouts: 11.8 us -> none  [the longest x5 4.6 us: per_device(): query = qkv[:, lo_col:lo_col + group_cols].reshape(shape_four)]
    all_to_all x4 -> x2, starting transfers between devices: 16.5 us -> 7.13 us  [exchange(): got = lax.all_to_all(sent, 'seq', split_axis=0, concat_axis=0, tiled=True)]
  transfers between devices with their start and end apart: 5 -> 3, of which waited for: 4 -> 2; matrix products, arithmetic and copies ran while one was open for 7% -> 0% of each run, Pallas kernels for 0% -> 5%
where the time goes in v1:
time: 232 us
  waiting for transfers between devices  88.1 us (38%)
  blocking collectives  78.5 us (34%)
  Pallas kernels  30.3 us (13%)
  between operations  14.1 us (6%)
  local copies, waits for them, and re-layouts  13.5 us (6%)
  starting transfers between devices  7.17 us (3%)
    psum x1, waiting for transfers between devices, per_device(): lax.psum((grad_qkv, grad_proj, gain_grad[0]), ('seq', 'dp'))  85.6 us
    psum x1, blocking collectives, per_device(): lax.psum((grad_qkv, grad_proj, gain_grad[0]), ('seq', 'dp'))  56.6 us
    all_to_all x1, blocking collectives, exchange(): got = lax.all_to_all(sent, 'seq', split_axis=0, concat_axis=0, tiled=True)  21.9 us
    pallas_call x1, Pallas kernels, per_device(): pl.pallas_call(backward_kernel, grid=(pairs,), out_shape=(shape_of((width...  16.1 us
    unnamed x24, local copies, waits for them, and re-layouts  13.5 us
    pallas_call x1, Pallas kernels, per_device(): pl.pallas_call(functools.partial(forward_kernel, n_seq, capacity), grid=(...  10 us
    all_to_all x2, starting transfers between devices, exchange(): got = lax.all_to_all(sent, 'seq', split_axis=0, concat_axis=0, tiled=True)  7.13 us
  transfers between devices with their start and end apart: 3, of which 2 were waited for; matrix products, arithmetic and copies ran while one was open for 0% of the time, Pallas kernels for 5%

profile of v1, /device:TPU:0, one launch (start us, length us, event | category | flops | bytes accessed | tf_op | source)
XLA Modules:
  0.0 231.6 jit_solution(16813672404441024101)
XLA Ops:
  7.2 0.0 copy-start.7
  7.2 1.0 copy-done.7
  8.2 0.0 copy-start.8
  8.2 1.0 copy-done.8
  9.3 0.0 copy-start.9
  9.3 0.7 copy-done.9
  9.9 2.5 %pack.1 = (bf16[1152,512]{1,0:T(8,128)(2,1)S(1)}, bf16[1024,512]{1,0:T(8,128)(2,1)}, s32[1,512]{1,0:T(1,128)S(1)}) custom-call(s32[1]{0:T(128)} %bitcast.me_ref, s32[1,512]{1,0:T(1,128)S(1)} %copy-done.9, bf16[512,512]{1,0:T(8,128)(2,1)S(1)} %bitcast.19, bf16[512,512]{1,0:T(8,128)(2,1)S(1)} %bitcast.20), custom_call_target="tpu_custom_call" | custom-call | flops 1073741824 | bytes 4194304 | tf_op jit(solution)/shard_map/pack/pallas_call | solution.py:249
  12.5 0.0 copy-start.6
  12.5 21.9 %all_to_all.15 = bf16[8,144,512]{2,1,0:T(8,128)(2,1)S(1)} all-to-all(bf16[8,144,512]{2,1,0:T(8,128)(2,1)S(1)} %bitcast.14), channel_id=1, replica_groups=mesh['seq'=8,'dp'=4] {'seq'}, dimensions={0} | all-to-all | bytes 2359296 | tf_op jit(solution)/shard_map/all_to_all | solution.py:265
  34.3 3.6 %all-to-all-start = ((bf16[8,128,512]{2,1,0:T(8,128)(2,1)}), bf16[8,128,512]{2,1,0:T(8,128)(2,1)S(1)}, u32[]{:S(2)}, u32[]{:S(2)}) async-start(bf16[8,128,512]{2,1,0:T(8,128)(2,1)} %bitcast.3), calls=%async_computation | async-start | bytes 2097152 | tf_op jit(solution)/shard_map/all_to_all | solution.py:265
  37.9 0.0 all-reduce.3.cloned.1.call-start
  38.0 0.0 copy-done.6
  38.0 10.0 %forward.1 = (s32[1,1024]{1,0:T(1,128)S(1)}, f32[512,512]{1,0:T(8,128)S(1)}, f32[512,128]{1,0:T(8,128)S(1)}, bf16[512,512]{1,0:T(8,128)(2,1)S(1)}, bf16[512,1536...) custom-call(bf16[1152,512]{1,0:T(8,128)(2,1)S(1)} %bitcast.13, ...), custom_call_target="tpu_custom_call" | custom-call | flops 2952790016 | bytes 16777216 | tf_op jit(solution)/shard_map/forward/pallas_call | solution.py:271
  48.0 0.0 copy-start
  48.0 1.2 copy-done
  49.2 0.0 copy-start.2
  49.2 0.8 copy-done.2
  50.0 0.0 copy-start.4
  50.0 0.8 copy-done.4
  50.8 2.4 %all-to-all-done = bf16[8,128,512]{2,1,0:T(8,128)(2,1)S(1)} async-done(((bf16[8,128,512]{2,1,0:T(8,128)(2,1)}), bf16[8,128,512]{2,1,0:T(8,128)(2,1)S(1)}, u32[]{:S(2)}, u32[]{:S(2)}) %all-to-all-start) | async-done | bytes 1048608 | tf_op jit(solution)/shard_map/all_to_all | solution.py:265
  53.2 0.0 copy-start.1
  53.3 1.0 copy-done.1
  54.3 0.0 copy-start.3
  54.3 1.0 copy-done.3
  55.3 0.0 copy-start.5
  55.3 1.0 copy-done.5
  56.4 16.1 %backward.1 = (f32[512,1536]{1,0:T(8,128)}, f32[512,512]{1,0:T(8,128)}, f32[1,512]{1,0:T(1,128)S(1)}, bf16[1024,512]{1,0:T(8,128)(2,1)}) custom-call(bf16[1024,512]{1,0:T(8,128)(2,1)S(1)} %bitcast.12, s32[1,1024]{1,0:T(1,128)S(1)} %get-tuple-element.21.pos_ref, bf16[512,1536]{1,0:T(8,128)(2,1)} %w_qkv_ref.1, bf16[512,512]{1,0:T(8,128)(2,1)S(1)} %copy-done.1, ...), custom_call_target="tpu_custom_call" | custom-call | flops 4026531840 | bytes 25165824 | tf_op jit(solution)/shard_map/backward/pallas_call | solution.py:303
  72.5 0.0 all-reduce.3.cloned.1.call-update
  72.5 3.6 %all-to-all-start.2 = ((bf16[8,128,512]{2,1,0:T(8,128)(2,1)}), bf16[8,128,512]{2,1,0:T(8,128)(2,1)S(1)}, u32[]{:S(2)}, u32[]{:S(2)}) async-start(bf16[8,128,512]{2,1,0:T(8,128)(2,1)} %bitcast.8), calls=%async_computation.2 | async-start | bytes 2097152 | tf_op jit(solution)/shard_map/all_to_all | solution.py:265
  76.1 56.6 %psum.23 = f32[512]{0:T(512)} all-reduce(f32[512]{0:T(512)S(1)} %bitcast.18), channel_id=1, replica_groups=mesh['seq'=8,'dp'=4] {'seq','dp'}, use_global_device_ids=true, to_apply=%region_2.0 | all-reduce | flops 512 | bytes 4096 | tf_op jit(solution)/shard_map/psum | solution.py:357
  132.7 0.0 all-to-all-done.2
  132.7 1.5 unpack.1
  134.3 85.6 %all-reduce.3.cloned.1.call-done = (f32[512,1536]{1,0:T(8,128)}, f32[512,512]{1,0:T(8,128)}) async-done(((f32[512,1536]{1,0:T(8,128)}, f32[512,512]{1,0:T(8,128)}), (f32[512,1536]{1,0:T(8,128)}, f32[512,512]{1,0:T(8,128)})) %all-reduce.3.cloned.1.call-update) | async-done | bytes 4194320 | tf_op jit(solution)/shard_map/psum | solution.py:357
  219.9 0.0 copy-start.10
  219.9 3.8 %copy.12 = f32[512,1536]{1,0:T(8,128)} copy(f32[512,1536]{1,0:T(8,128)} %get-tuple-element.35) | data formatting | bytes 6291456
  223.8 0.0 copy-done.10
  223.8 1.0 copy.13
Async XLA Ops:
  7.2 1.0 copy-start.7
  8.2 1.0 copy-start.8
  9.3 0.7 copy-start.9
  12.5 25.5 %copy-start.6 = (f32[512]{0:T(512)S(1)}, f32[512]{0:T(512)}, u32[]{:S(2)}) copy-start(f32[512]{0:T(512)} %param.11) | copy-start | bytes 6148
  34.3 18.9 %all-to-all-start = ((bf16[8,128,512]{2,1,0:T(8,128)(2,1)}), bf16[8,128,512]{2,1,0:T(8,128)(2,1)S(1)}, u32[]{:S(2)}, u32[]{:S(2)}) async-start(bf16[8,128,512]{2,1,0:T(8,128)(2,1)} %bitcast.3), calls=%async_computation | async-start | bytes 2097152 | tf_op jit(solution)/shard_map/all_to_all | solution.py:265
  37.9 182.0 %all-reduce.3.cloned.1.call-start = ((), (), s32[]{:S(2)}) async-start(), calls=%async_computation.3 | async-start | bytes 8388608 | tf_op jit(solution)/shard_map/psum | solution.py:357
  48.0 1.2 copy-start
  49.2 0.8 copy-start.2
  50.0 0.8 copy-start.4
  53.2 1.0 copy-start.1
  54.3 1.0 copy-start.3
  55.3 1.0 copy-start.5
  72.5 60.2 %all-to-all-start.2 = ((bf16[8,128,512]{2,1,0:T(8,128)(2,1)}), bf16[8,128,512]{2,1,0:T(8,128)(2,1)S(1)}, u32[]{:S(2)}, u32[]{:S(2)}) async-start(bf16[8,128,512]{2,1,0:T(8,128)(2,1)} %bitcast.8), calls=%async_computation.2 | async-start | bytes 2097152 | tf_op jit(solution)/shard_map/all_to_all | solution.py:265
  219.9 3.8 %copy-start.10 = (f32[512,512]{1,0:T(8,128)S(1)}, f32[512,512]{1,0:T(8,128)}, u32[]{:S(2)}) copy-start(f32[512,512]{1,0:T(8,128)} %get-tuple-element.36) | copy-start | bytes 3145732
Sparse Core Ops, SparseCore 0:
  72.6 147.2 all-reduce.2

commit v2 on v1

--- a/solution.py
+++ b/solution.py
@@ -11,7 +11,7 @@
 PATCH = 512
 EXTRA = 16
 LANES = 128
-VMEM_LIMIT = 48 * 1024 * 1024
+MIB = 1024 * 1024
 F32 = jnp.float32
 BF16 = jnp.bfloat16
 NN = (((1,), (0,)), ((), ()))
@@ -137,6 +137,7 @@
 
 
 def backward_kernel(
+    me_ref,
     recv_ref,
     pos_ref,
     w_qkv_ref,
@@ -148,15 +149,16 @@
     qkv_ref,
     attn_ref,
     probs_ref,
-    grad_qkv_out,
-    grad_proj_out,
-    gain_out,
+    send_out,
+    keep_out,
     back_out,
     serial_grad,
     d_attn,
     d_attn_t,
     keys_t,
     d_qkv,
+    normed_t,
+    gain_column,
 ):
     width = w_proj_ref.shape[0]
     rows = xhat_ref.shape[0]
@@ -203,12 +205,18 @@
 
     @pl.when(step == pl.num_programs(0) - 1)
     def _():
-        normed_t = jnp.transpose(normed_ref[...].astype(F32)).astype(BF16)
-        grad_qkv_out[...] = mm(normed_t, d_qkv[...])
-        grad_proj_out[...] = mm(attn_ref[...], serial_grad[...])
+        normed_t[...] = jnp.transpose(normed_ref[...].astype(F32)).astype(BF16)
         d_normed = mm(d_qkv[...], w_qkv_ref[...], NT)
         xhat = xhat_ref[...]
-        gain_out[...] = jnp.sum(d_normed * xhat, axis=0, keepdims=True)
+        gain_row = jnp.sum(d_normed * xhat, axis=0, keepdims=True)
+        gain_column[...] = jnp.transpose(jnp.broadcast_to(gain_row, (LANES, width)))
+        half = width // 2
+        bit = lax.bitwise_and(me_ref[0], 1)
+        for out, start in ((send_out, (1 - bit) * half), (keep_out, bit * half)):
+            part = pl.ds(pl.multiple_of(start, half), half)
+            out[:, : 3 * width] = mm(normed_t[part, :], d_qkv[...])
+            out[:, 3 * width : 4 * width] = mm(attn_ref[part, :], serial_grad[...])
+            out[:, 4 * width :] = gain_column[part, :]
         scaled = d_normed * gain_ref[...]
         residual = inv_ref[:, 0:1] * (
             scaled
@@ -224,11 +232,48 @@
 
 
 def whole(shape):
-    return pl.BlockSpec(shape, lambda *_: (0,) * len(shape))
+    return pl.BlockSpec(shape, lambda *_: (0,) * len(shape), pipeline_mode=pl.Buffered(1))
+
+
+def params(mib):
+    return pltpu.CompilerParams(vmem_limit_bytes=mib * MIB)
 
 
 def shape_of(shape, dtype):
     return jax.ShapeDtypeStruct(shape, dtype)
+
+
+def reduce_and_share(send, keep):
+    n_seq, n_dp = lax.axis_size("seq"), lax.axis_size("dp")
+    me, plane = lax.axis_index("seq"), lax.axis_index("dp")
+    seq_bits = list(range(1, n_seq.bit_length() - 1))
+    middle = len(seq_bits) // 2
+    orders = (seq_bits, seq_bits[middle:] + seq_bits[:middle])
+    odd = lax.bitwise_and(me, 1)
+
+    def bit_of(index, bit):
+        return lax.bitwise_and(lax.shift_right_logical(index, jnp.asarray(bit, index.dtype)), 1)
+
+    steps = [("seq", [(i, i ^ 1) for i in range(n_seq)], odd)]
+    for even_bit, odd_bit in zip(*orders):
+        pairs = [(i, i ^ (1 << (odd_bit if i & 1 else even_bit))) for i in range(n_seq)]
+        steps.append(("seq", pairs, jnp.where(odd == 1, bit_of(me, odd_bit), bit_of(me, even_bit))))
+    for bit in range(n_dp.bit_length() - 1):
+        steps.append(("dp", [(i, i ^ (1 << bit)) for i in range(n_dp)], bit_of(plane, bit)))
+
+    for i, (axis, pairs, bit) in enumerate(steps):
+        if i > 0:
+            half = part.shape[0] // 2
+            send = lax.dynamic_slice_in_dim(part, (1 - bit) * half, half)
+            keep = lax.dynamic_slice_in_dim(part, bit * half, half)
+        part = keep + lax.ppermute(send, axis, pairs)
+    part = part.astype(BF16)
+    for axis, pairs, bit in reversed(steps):
+        other = lax.ppermute(part, axis, pairs)
+        part = jnp.where(
+            bit == 0, jnp.concatenate([part, other], axis=0), jnp.concatenate([other, part], axis=0)
+        )
+    return part
 
 
 def per_device(points, cotangent, dest, w_qkv, w_proj, gain):
@@ -243,7 +288,7 @@
     pair = width // pairs
     me = jnp.reshape(lax.axis_index("seq").astype(jnp.int32), (1,))
     gain_row = gain.reshape(1, width)
-    params = pltpu.CompilerParams(vmem_limit_bytes=VMEM_LIMIT)
+    smem = pl.BlockSpec(memory_space=pltpu.SMEM)
     in_vmem = pl.BlockSpec(memory_space=pltpu.VMEM)
 
     feats_sent, grads_sent, slot = pl.pallas_call(
@@ -253,9 +298,9 @@
             shape_of((slots, width), BF16),
             shape_of((1, rows), jnp.int32),
         ),
-        in_specs=[pl.BlockSpec(memory_space=pltpu.SMEM), in_vmem, in_vmem, in_vmem],
+        in_specs=[smem, in_vmem, in_vmem, in_vmem],
         out_specs=[in_vmem] * 3,
-        compiler_params=params,
+        compiler_params=params(20),
         cost_estimate=pl.CostEstimate(flops=2 * slots * rows * width * 2, bytes_accessed=4 << 20, transcendentals=0),
         name="pack",
     )(me, dest, feats, grads)
@@ -291,7 +336,7 @@
             pl.BlockSpec((2, rows, rows), lambda i: (i, 0, 0)),
         ],
         scratch_shapes=[pltpu.VMEM((3 * width, rows), BF16)],
-        compiler_params=params,
+        compiler_params=params(32),
         cost_estimate=pl.CostEstimate(
             flops=6 * rows * width * width + 8 * HEADS * rows * rows * pair,
             bytes_accessed=16 << 20,
@@ -300,16 +345,16 @@
         name="forward",
     )(feats_got, w_qkv, gain_row)
 
-    grad_qkv, grad_proj, gain_grad, back = pl.pallas_call(
+    send, keep, back = pl.pallas_call(
         backward_kernel,
         grid=(pairs,),
         out_shape=(
-            shape_of((width, 3 * width), F32),
-            shape_of((width, width), F32),
-            shape_of((1, width), F32),
+            shape_of((width // 2, 4 * width + LANES), F32),
+            shape_of((width // 2, 4 * width + LANES), F32),
             shape_of((slots, width), BF16),
         ),
         in_specs=[
+            smem,
             whole((slots, width)),
             whole((1, slots)),
             whole((width, 3 * width)),
@@ -323,9 +368,8 @@
             pl.BlockSpec((2, rows, rows), lambda i: (i, 0, 0)),
         ],
         out_specs=[
-            whole((width, 3 * width)),
-            whole((width, width)),
-            whole((1, width)),
+            whole((width // 2, 4 * width + LANES)),
+            whole((width // 2, 4 * width + LANES)),
             whole((slots, width)),
         ],
         scratch_shapes=[
@@ -334,15 +378,17 @@
             pltpu.VMEM((width, rows), BF16),
             pltpu.VMEM((width, rows), BF16),
             pltpu.VMEM((rows, 3 * width), BF16),
+            pltpu.VMEM((width, rows), BF16),
+            pltpu.VMEM((width, LANES), F32),
         ],
-        compiler_params=params,
+        compiler_params=params(40),
         cost_estimate=pl.CostEstimate(
             flops=14 * rows * width * width + 8 * HEADS * rows * rows * pair,
             bytes_accessed=24 << 20,
             transcendentals=0,
         ),
         name="backward",
-    )(grads_got, pos, w_qkv, w_proj, gain_row, xhat, inv, normed, qkv, attn_t, probs)
+    )(me, grads_got, pos, w_qkv, w_proj, gain_row, xhat, inv, normed, qkv, attn_t, probs)
 
     returned = exchange(back, capacity)
     grad_local = pl.pallas_call(
@@ -350,12 +396,12 @@
         out_shape=shape_of((rows, width), BF16),
         in_specs=[in_vmem] * 2,
         out_specs=in_vmem,
-        compiler_params=params,
+        compiler_params=params(20),
         cost_estimate=pl.CostEstimate(flops=2 * slots * rows * width, bytes_accessed=2 << 20, transcendentals=0),
         name="unpack",
     )(slot, returned)
-    grad_qkv, grad_proj, gain_grad = lax.psum((grad_qkv, grad_proj, gain_grad[0]), ("seq", "dp"))
-    return (grad_local[None], grad_qkv, grad_proj, gain_grad)
+    total = reduce_and_share(send, keep).astype(F32)
+    return (grad_local[None], total[:, : 3 * width], total[:, 3 * width : 4 * width], total[:, 4 * width])
 
 
 def solution(mesh):

time: 232 us -> 176 us (0.76)
  blocking collectives: 78.5 us -> 21.8 us
  starting transfers between devices: 7.17 us -> 24.9 us
  waiting for transfers between devices: 88.1 us -> 73.9 us
  between operations: 14.1 us -> 0.81 us
  local copies, waits for them, and re-layouts: 13.5 us -> 23.7 us
  Pallas kernels: 30.3 us -> 25.2 us
  other arithmetic: 0 us -> 4.64 us
    psum x1 -> x0, waiting for transfers between devices: 85.6 us -> none  [per_device(): lax.psum((grad_qkv, grad_proj, gain_grad[0]), ('seq', 'dp'))]
    ppermute x0 -> x10, waiting for transfers between devices: none -> 58.4 us  [the longest x5 36.1 us: reduce_and_share(): part = keep + lax.ppermute(send, axis, pairs)]
    psum x1 -> x0, blocking collectives: 56.6 us -> none  [per_device(): lax.psum((grad_qkv, grad_proj, gain_grad[0]), ('seq', 'dp'))]
    ppermute x0 -> x10, starting transfers between devices: none -> 16.9 us  [the longest x5 8.62 us: reduce_and_share(): part = keep + lax.ppermute(send, axis, pairs)]
    all_to_all x2, waiting for transfers between devices: 2.44 us -> 15.4 us  [exchange(): got = lax.all_to_all(sent, 'seq', split_axis=0, concat_axis=0, tiled=True)]
    unnamed x24 -> x38, local copies, waits for them, and re-layouts: 13.5 us -> 19.6 us
    slice x0 -> x3, local copies, waits for them, and re-layouts: none -> 3.92 us  [the longest x1 2.09 us: per_device(): total[:, :3 * width]]
    add x0 -> x4, other arithmetic: none -> 3.47 us  [reduce_and_share(): part = keep + lax.ppermute(send, axis, pairs)]
  transfers between devices with their start and end apart: 3 -> 12, of which waited for: 2 -> 10; matrix products, arithmetic and copies ran while one was open for 0% -> 0% of each run, Pallas kernels for 5% -> 5%
where the time goes in v2:
time: 176 us; the launch traced here: 175 us
  waiting for transfers between devices  73.9 us (42%)
  Pallas kernels  25.2 us (14%)
  starting transfers between devices  24.9 us (14%)
  local copies, waits for them, and re-layouts  23.7 us (13%)
  blocking collectives  21.8 us (12%)
  other arithmetic  4.64 us (3%)
    ppermute x5, waiting for transfers between devices, reduce_and_share(): part = keep + lax.ppermute(send, axis, pairs)  36.1 us
    ppermute x5, waiting for transfers between devices, reduce_and_share(): other = lax.ppermute(part, axis, pairs)  22.4 us
    all_to_all x1, blocking collectives, exchange(): got = lax.all_to_all(sent, 'seq', split_axis=0, concat_axis=0, tiled=True)  21.8 us
    unnamed x38, local copies, waits for them, and re-layouts  19.6 us
    all_to_all x2, waiting for transfers between devices, exchange(): got = lax.all_to_all(sent, 'seq', split_axis=0, concat_axis=0, tiled=True)  15.4 us
    pallas_call x1, Pallas kernels, per_device(): pl.pallas_call(backward_kernel, grid=(pairs,), out_shape=(shape_of((width...  14.6 us
    ppermute x5, starting transfers between devices, reduce_and_share(): part = keep + lax.ppermute(send, axis, pairs)  8.62 us
    ppermute x5, starting transfers between devices, reduce_and_share(): other = lax.ppermute(part, axis, pairs)  8.33 us
  transfers between devices with their start and end apart: 12, of which 10 were waited for; matrix products, arithmetic and copies ran while one was open for 0% of the time, Pallas kernels for 5%

profile of v2, /device:TPU:0, one launch (start us, length us, event | category | flops | bytes accessed | tf_op | source)
XLA Modules:
  0.0 174.9 jit_solution(8255857986656204907)
XLA Ops:
  0.6 1.0 copy-done.15
  1.7 1.0 copy-done.16
  2.7 0.7 copy-done.17
  3.4 1.6 pack.1
  5.0 21.8 %all_to_all.15 = bf16[8,144,512]{2,1,0:T(8,128)(2,1)} all-to-all(bf16[8,144,512]{2,1,0:T(8,128)(2,1)S(1)} %bitcast.13), channel_id=1, replica_groups=mesh['seq'=8,'dp'=4] {'seq'}, dimensions={0} | all-to-all | bytes 2359296 | tf_op jit(solution)/shard_map/all_to_all | solution.py:310
  26.9 3.7 %all-to-all-start = ((bf16[8,128,512]{2,1,0:T(8,128)(2,1)}), bf16[8,128,512]{2,1,0:T(8,128)(2,1)S(1)}, u32[]{:S(2)}, u32[]{:S(2)}) async-start(bf16[8,128,512]{2,1,0:T(8,128)(2,1)} %bitcast.14), calls=%async_computation | async-start | bytes 2097152 | tf_op jit(solution)/shard_map/all_to_all | solution.py:310
  30.6 1.3 copy-done.5
  31.9 7.5 %forward.1 = (s32[1,1024]{1,0:T(1,128)S(1)}, f32[512,512]{1,0:T(8,128)S(1)}, f32[512,128]{1,0:T(8,128)S(1)}, bf16[512,512]{1,0:T(8,128)(2,1)S(1)}, bf16[512,1536...) custom-call(bf16[1152,512]{1,0:T(8,128)(2,1)S(1)} %bitcast.12, ...), custom_call_target="tpu_custom_call" | custom-call | flops 2952790016 | bytes 16777216 | tf_op jit(solution)/shard_map/forward/pallas_call | solution.py:316
  39.4 3.3 %copy-done = f32[8,512,512]{2,1,0:T(8,128)} copy-done((f32[8,512,512]{2,1,0:T(8,128)}, f32[8,512,512]{2,1,0:T(8,128)S(1)}, u32[]{:S(2)}) %copy-start) | copy-done | bytes 8388632
  42.6 1.1 copy-done.3
  43.8 1.0 copy-done.7
  44.8 0.8 copy-done.10
  45.6 0.8 copy-done.12
  46.4 1.4 copy-done.2
  47.8 1.4 copy-done.4
  49.2 1.2 copy-done.8
  50.4 1.0 copy-done.9
  51.5 1.0 copy-done.11
  52.5 1.0 copy-done.13
  53.6 14.6 %backward.1 = (f32[256,2176]{1,0:T(8,128)}, f32[256,2176]{1,0:T(8,128)S(1)}, bf16[1024,512]{1,0:T(8,128)(2,1)}) custom-call(s32[1]{0:T(128)} %bitcast.me_ref, bf16[1024,512]{1,0:T(8,128)(2,1)S(1)} %bitcast.11, s32[1,1024]{1,0:T(1,128)S(1)} %get-tuple-element.20.pos_ref, bf16[512,1536]{1,0:T(8,128)(2,1)S(1)} %copy-done.2, bf16[512,512]{1,0:T(8,128)(2,1)S(1)} %copy-done.9, ...), custom_call_target="tpu_custom_call" | custom-call | flops 4026531840 | bytes 25165824 | tf_op jit(solution)/shard_map/backward/pallas_call | solution.py:348
  68.1 0.4 collective-permute-start
  68.5 4.3 %collective-permute-done = f32[256,2176]{1,0:T(8,128)} collective-permute-done((f32[256,2176]{1,0:T(8,128)}, f32[256,2176]{1,0:T(8,128)}, u32[]{:S(2)}, u32[]{:S(2)}) %collective-permute-start) | collective-permute-done | bytes 2228256 | tf_op jit(solution)/shard_map/ppermute | solution.py:269
  72.8 1.9 %add.39 = f32[256,2176]{1,0:T(8,128)S(1)} add(f32[256,2176]{1,0:T(8,128)S(1)} %get-tuple-element.28, f32[256,2176]{1,0:T(8,128)} %collective-permute-done) | non-fusion elementwise | flops 557056 | bytes 6684672 | tf_op jit(solution)/shard_map/add | solution.py:269
  74.8 1.4 copy-done.18
  76.2 2.0 %collective-permute-start.1 = (f32[128,2176]{1,0:T(8,128)S(1)}, f32[128,2176]{1,0:T(8,128)S(1)}, u32[]{:S(2)}, u32[]{:S(2)}) collective-permute-start(f32[128,2176]{1,0:T(8,128)S(1)} %constant_dynamic-slice_fusion.3), channel_id=1, source_target_pairs={{0,8},{4,20},{8,0},{12,28},{16,24},{20,4},{24,16},{28,12},{1,9},{5... | collective-permute-start | bytes 3342344 | tf_op jit(solution)/shard_map/ppermute | solution.py:269
  78.2 13.6 %collective-permute-done.1 = f32[128,2176]{1,0:T(8,128)S(1)} collective-permute-done((f32[128,2176]{1,0:T(8,128)S(1)}, f32[128,2176]{1,0:T(8,128)S(1)}, u32[]{:S(2)}, u32[]{:S(2)}) %collective-permute-start.1) | collective-permute-done | bytes 1114144 | tf_op jit(solution)/shard_map/ppermute | solution.py:269
  91.8 1.5 dynamic-slice_add_fusion
  93.3 2.0 %collective-permute-start.2 = (f32[64,2176]{1,0:T(8,128)S(1)}, f32[64,2176]{1,0:T(8,128)S(1)}, u32[]{:S(2)}, u32[]{:S(2)}) collective-permute-start(f32[64,2176]{1,0:T(8,128)S(1)} %constant_dynamic-slice_fusion.2), channel_id=1, source_target_pairs={{0,16},{4,12},{8,24},{12,4},{16,0},{20,28},{24,8},{28,20},{1,17},{... | collective-permute-start | bytes 1671176 | tf_op jit(solution)/shard_map/ppermute | solution.py:269
  95.2 7.6 %collective-permute-done.2 = f32[64,2176]{1,0:T(8,128)S(1)} collective-permute-done((f32[64,2176]{1,0:T(8,128)S(1)}, f32[64,2176]{1,0:T(8,128)S(1)}, u32[]{:S(2)}, u32[]{:S(2)}) %collective-permute-start.2) | collective-permute-done | bytes 557088 | tf_op jit(solution)/shard_map/ppermute | solution.py:269
  103.0 1.6 collective-permute-start.3
  104.6 5.6 %collective-permute-done.3 = f32[32,2176]{1,0:T(8,128)S(1)} collective-permute-done((f32[32,2176]{1,0:T(8,128)S(1)}, f32[32,2176]{1,0:T(8,128)S(1)}, u32[]{:S(2)}, u32[]{:S(2)}) %collective-permute-start.3) | collective-permute-done | bytes 278560 | tf_op jit(solution)/shard_map/ppermute | solution.py:269
  110.3 2.7 %collective-permute-start.4 = (f32[16,2176]{1,0:T(8,128)S(1)}, f32[16,2176]{1,0:T(8,128)S(1)}, u32[]{:S(2)}, u32[]{:S(2)}) collective-permute-start(f32[16,2176]{1,0:T(8,128)S(1)} %constant_dynamic-slice_fusion), channel_id=1, source_target_pairs={{0,2},{1,3},{2,0},{3,1},{4,6},{5,7},{6,4},{7,5},{8,10},{9,11},{10,... | collective-permute-start | bytes 417800 | tf_op jit(solution)/shard_map/ppermute | solution.py:269
  113.0 4.9 %collective-permute-done.4 = f32[16,2176]{1,0:T(8,128)S(1)} collective-permute-done((f32[16,2176]{1,0:T(8,128)S(1)}, f32[16,2176]{1,0:T(8,128)S(1)}, u32[]{:S(2)}, u32[]{:S(2)}) %collective-permute-start.4) | collective-permute-done | bytes 139296 | tf_op jit(solution)/shard_map/ppermute | solution.py:269
  117.9 1.3 collective-permute-start.5
  119.1 4.1 %collective-permute-done.5 = bf16[16,2176]{1,0:T(8,128)(2,1)S(1)} collective-permute-done((bf16[16,2176]{1,0:T(8,128)(2,1)S(1)}, bf16[16,2176]{1,0:T(8,128)(2,1)S(1)}, u32[]{:S(2)}, u32[]{:S(2)}) %collective-permute-start.5) | collective-permute-done | bytes 69664 | tf_op jit(solution)/shard_map/ppermute | solution.py:272
  123.3 3.0 %collective-permute-start.6 = (bf16[32,2176]{1,0:T(8,128)(2,1)S(1)}, bf16[32,2176]{1,0:T(8,128)(2,1)S(1)}, u32[]{:S(2)}, u32[]{:S(2)}) collective-permute-start(bf16[32,2176]{1,0:T(8,128)(2,1)S(1)} %maximum_select_fusion.4), channel_id=1, source_target_pairs={{0,1},{1,0},{2,3},{3,2},{4,5},{5,4},{6,7},{7,6},{8,9},{9,8},{10,11... | collective-permute-start | bytes 417800 | tf_op jit(solution)/shard_map/ppermute | solution.py:272
  126.3 3.0 %collective-permute-done.6 = bf16[32,2176]{1,0:T(8,128)(2,1)S(1)} collective-permute-done((bf16[32,2176]{1,0:T(8,128)(2,1)S(1)}, bf16[32,2176]{1,0:T(8,128)(2,1)S(1)}, u32[]{:S(2)}, u32[]{:S(2)}) %collective-permute-start.6) | collective-permute-done | bytes 139296 | tf_op jit(solution)/shard_map/ppermute | solution.py:272
  129.4 2.0 %collective-permute-start.7 = (bf16[64,2176]{1,0:T(8,128)(2,1)S(1)}, bf16[64,2176]{1,0:T(8,128)(2,1)S(1)}, u32[]{:S(2)}, u32[]{:S(2)}) collective-permute-start(bf16[64,2176]{1,0:T(8,128)(2,1)S(1)} %maximum_select_fusion.3), channel_id=1, source_target_pairs={{0,16},{4,12},{8,24},{12,4},{16,0},{20,28},{24,8},{28,20},{1,17},{... | collective-permute-start | bytes 835592 | tf_op jit(solution)/shard_map/ppermute | solution.py:272
  131.4 7.6 %collective-permute-done.7 = bf16[64,2176]{1,0:T(8,128)(2,1)S(1)} collective-permute-done((bf16[64,2176]{1,0:T(8,128)(2,1)S(1)}, bf16[64,2176]{1,0:T(8,128)(2,1)S(1)}, u32[]{:S(2)}, u32[]{:S(2)}) %collective-permute-start.7) | collective-permute-done | bytes 278560 | tf_op jit(solution)/shard_map/ppermute | solution.py:272
  139.1 2.0 %collective-permute-start.8 = (bf16[128,2176]{1,0:T(8,128)(2,1)S(1)}, bf16[128,2176]{1,0:T(8,128)(2,1)S(1)}, u32[]{:S(2)}, u32[]{:S(2)}) collective-permute-start(bf16[128,2176]{1,0:T(8,128)(2,1)S(1)} %maximum_select_fusion.2), channel_id=1, source_target_pairs={{0,8},{4,20},{8,0},{12,28},{16,24},{20,4},{24,16},{28,12},{1,9},{5... | collective-permute-start | bytes 1671176 | tf_op jit(solution)/shard_map/ppermute | solution.py:272
  141.1 7.6 %collective-permute-done.8 = bf16[128,2176]{1,0:T(8,128)(2,1)S(1)} collective-permute-done((bf16[128,2176]{1,0:T(8,128)(2,1)S(1)}, bf16[128,2176]{1,0:T(8,128)(2,1)S(1)}, u32[]{:S(2)}, u32[]{:S(2)}) %collective-permute-start.8) | collective-permute-done | bytes 557088 | tf_op jit(solution)/shard_map/ppermute | solution.py:272
  149.0 4.2 %all-to-all-start.2 = ((bf16[8,128,512]{2,1,0:T(8,128)(2,1)}), bf16[8,128,512]{2,1,0:T(8,128)(2,1)S(1)}, u32[]{:S(2)}, u32[]{:S(2)}) async-start(bf16[8,128,512]{2,1,0:T(8,128)(2,1)} %bitcast.8), calls=%async_computation.2 | async-start | bytes 2097152 | tf_op jit(solution)/shard_map/all_to_all | solution.py:310
  153.2 15.4 %all-to-all-done.2 = bf16[8,128,512]{2,1,0:T(8,128)(2,1)S(1)} async-done(((bf16[8,128,512]{2,1,0:T(8,128)(2,1)}), bf16[8,128,512]{2,1,0:T(8,128)(2,1)S(1)}, u32[]{:S(2)}, u32[]{:S(2)}) %all-to-all-start.2) | async-done | bytes 1048608 | tf_op jit(solution)/shard_map/all_to_all | solution.py:310
  168.6 1.5 unpack.1
  170.2 0.8 fusion
  171.0 2.1 %slice.12 = f32[512,1536]{1,0:T(8,128)} slice(f32[512,2176]{1,0:T(8,128)S(1)} %fusion), slice={[0:512], [0:1536]} | slice | bytes 6291456 | tf_op jit(solution)/shard_map/slice | solution.py:404
  173.1 1.1 slice.13
  174.2 0.7 slice_reduce_fusion
  (36 shorter events, 0.8 us)
Async XLA Ops:
  0.6 1.0 copy-start.15
  1.7 1.0 copy-start.16
  2.7 0.7 copy-start.17
  5.0 21.9 %copy-start.6 = (bf16[1024,512]{1,0:T(8,128)(2,1)}, bf16[1024,512]{1,0:T(8,128)(2,1)S(1)}, u32[]{:S(2)}) copy-start(bf16[1024,512]{1,0:T(8,128)(2,1)S(1)} %get-tuple-element.18) | copy-start | bytes 3145732
  26.9 3.7 %copy-start.1 = (bf16[512,1536]{1,0:T(8,128)(2,1)S(1)}, bf16[512,1536]{1,0:T(8,128)(2,1)}, u32[]{:S(2)}) copy-start(bf16[512,1536]{1,0:T(8,128)(2,1)} %w_qkv_ref.1) | copy-start | bytes 4718596
  26.9 3.7 %copy-start.14 = (f32[512]{0:T(512)S(1)}, f32[512]{0:T(512)}, u32[]{:S(2)}) copy-start(f32[512]{0:T(512)} %param.11) | copy-start | bytes 6148
  26.9 19.5 %all-to-all-start = ((bf16[8,128,512]{2,1,0:T(8,128)(2,1)}), bf16[8,128,512]{2,1,0:T(8,128)(2,1)S(1)}, u32[]{:S(2)}, u32[]{:S(2)}) async-start(bf16[8,128,512]{2,1,0:T(8,128)(2,1)} %bitcast.14), calls=%async_computation | async-start | bytes 2097152 | tf_op jit(solution)/shard_map/all_to_all | solution.py:310
  30.6 1.3 copy-start.5
  39.4 3.3 %copy-start = (f32[8,512,512]{2,1,0:T(8,128)}, f32[8,512,512]{2,1,0:T(8,128)S(1)}, u32[]{:S(2)}) copy-start(f32[8,512,512]{2,1,0:T(8,128)S(1)} %get-tuple-element.26.probs_ref) | copy-start | bytes 25165828
  42.6 1.1 copy-start.3
  43.8 1.0 copy-start.7
  44.8 0.8 copy-start.10
  45.6 0.8 copy-start.12
  46.4 1.4 copy-start.2
  47.8 1.4 copy-start.4
  49.2 1.2 copy-start.8
  50.4 1.0 copy-start.9
  51.5 1.0 copy-start.11
  52.5 1.0 copy-start.13
  68.1 4.7 %collective-permute-start = (f32[256,2176]{1,0:T(8,128)}, f32[256,2176]{1,0:T(8,128)}, u32[]{:S(2)}, u32[]{:S(2)}) collective-permute-start(f32[256,2176]{1,0:T(8,128)} %get-tuple-element.29), channel_id=1, source_target_pairs={{0,4},{4,0},{8,12},{12,8},{16,20},{20,16},{24,28},{28,24},{1,5},{5... | collective-permute-start | bytes 6684680 | tf_op jit(solution)/shard_map/ppermute | solution.py:269
  74.8 1.4 copy-start.18
  76.2 15.6 %collective-permute-start.1 = (f32[128,2176]{1,0:T(8,128)S(1)}, f32[128,2176]{1,0:T(8,128)S(1)}, u32[]{:S(2)}, u32[]{:S(2)}) collective-permute-start(f32[128,2176]{1,0:T(8,128)S(1)} %constant_dynamic-slice_fusion.3), channel_id=1, source_target_pairs={{0,8},{4,20},{8,0},{12,28},{16,24},{20,4},{24,16},{28,12},{1,9},{5... | collective-permute-start | bytes 3342344 | tf_op jit(solution)/shard_map/ppermute | solution.py:269
  93.3 9.6 %collective-permute-start.2 = (f32[64,2176]{1,0:T(8,128)S(1)}, f32[64,2176]{1,0:T(8,128)S(1)}, u32[]{:S(2)}, u32[]{:S(2)}) collective-permute-start(f32[64,2176]{1,0:T(8,128)S(1)} %constant_dynamic-slice_fusion.2), channel_id=1, source_target_pairs={{0,16},{4,12},{8,24},{12,4},{16,0},{20,28},{24,8},{28,20},{1,17},{... | collective-permute-start | bytes 1671176 | tf_op jit(solution)/shard_map/ppermute | solution.py:269
  103.0 7.3 %collective-permute-start.3 = (f32[32,2176]{1,0:T(8,128)S(1)}, f32[32,2176]{1,0:T(8,128)S(1)}, u32[]{:S(2)}, u32[]{:S(2)}) collective-permute-start(f32[32,2176]{1,0:T(8,128)S(1)} %constant_dynamic-slice_fusion.1), channel_id=1, source_target_pairs={{0,1},{1,0},{2,3},{3,2},{4,5},{5,4},{6,7},{7,6},{8,9},{9,8},{10,11... | collective-permute-start | bytes 835592 | tf_op jit(solution)/shard_map/ppermute | solution.py:269
  110.3 7.5 %collective-permute-start.4 = (f32[16,2176]{1,0:T(8,128)S(1)}, f32[16,2176]{1,0:T(8,128)S(1)}, u32[]{:S(2)}, u32[]{:S(2)}) collective-permute-start(f32[16,2176]{1,0:T(8,128)S(1)} %constant_dynamic-slice_fusion), channel_id=1, source_target_pairs={{0,2},{1,3},{2,0},{3,1},{4,6},{5,7},{6,4},{7,5},{8,10},{9,11},{10,... | collective-permute-start | bytes 417800 | tf_op jit(solution)/shard_map/ppermute | solution.py:269
  117.9 5.4 %collective-permute-start.5 = (bf16[16,2176]{1,0:T(8,128)(2,1)S(1)}, bf16[16,2176]{1,0:T(8,128)(2,1)S(1)}, u32[]{:S(2)}, u32[]{:S(2)}) collective-permute-start(bf16[16,2176]{1,0:T(8,128)(2,1)S(1)} %add_convert_fusion), channel_id=1, source_target_pairs={{0,2},{1,3},{2,0},{3,1},{4,6},{5,7},{6,4},{7,5},{8,10},{9,11},{10,... | collective-permute-start | bytes 208904 | tf_op jit(solution)/shard_map/ppermute | solution.py:272
  123.3 6.1 %collective-permute-start.6 = (bf16[32,2176]{1,0:T(8,128)(2,1)S(1)}, bf16[32,2176]{1,0:T(8,128)(2,1)S(1)}, u32[]{:S(2)}, u32[]{:S(2)}) collective-permute-start(bf16[32,2176]{1,0:T(8,128)(2,1)S(1)} %maximum_select_fusion.4), channel_id=1, source_target_pairs={{0,1},{1,0},{2,3},{3,2},{4,5},{5,4},{6,7},{7,6},{8,9},{9,8},{10,11... | collective-permute-start | bytes 417800 | tf_op jit(solution)/shard_map/ppermute | solution.py:272
  129.4 9.6 %collective-permute-start.7 = (bf16[64,2176]{1,0:T(8,128)(2,1)S(1)}, bf16[64,2176]{1,0:T(8,128)(2,1)S(1)}, u32[]{:S(2)}, u32[]{:S(2)}) collective-permute-start(bf16[64,2176]{1,0:T(8,128)(2,1)S(1)} %maximum_select_fusion.3), channel_id=1, source_target_pairs={{0,16},{4,12},{8,24},{12,4},{16,0},{20,28},{24,8},{28,20},{1,17},{... | collective-permute-start | bytes 835592 | tf_op jit(solution)/shard_map/ppermute | solution.py:272
  139.1 9.6 %collective-permute-start.8 = (bf16[128,2176]{1,0:T(8,128)(2,1)S(1)}, bf16[128,2176]{1,0:T(8,128)(2,1)S(1)}, u32[]{:S(2)}, u32[]{:S(2)}) collective-permute-start(bf16[128,2176]{1,0:T(8,128)(2,1)S(1)} %maximum_select_fusion.2), channel_id=1, source_target_pairs={{0,8},{4,20},{8,0},{12,28},{16,24},{20,4},{24,16},{28,12},{1,9},{5... | collective-permute-start | bytes 1671176 | tf_op jit(solution)/shard_map/ppermute | solution.py:272
  148.9 21.3 %collective-permute-start.9 = (bf16[256,2176]{1,0:T(8,128)(2,1)S(1)}, bf16[256,2176]{1,0:T(8,128)(2,1)S(1)}, u32[]{:S(2)}, u32[]{:S(2)}) collective-permute-start(bf16[256,2176]{1,0:T(8,128)(2,1)S(1)} %maximum_select_fusion.1), channel_id=1, source_target_pairs={{0,4},{4,0},{8,12},{12,8},{16,20},{20,16},{24,28},{28,24},{1,5},{5... | collective-permute-start | bytes 3342344 | tf_op jit(solution)/shard_map/ppermute | solution.py:272
  149.0 19.7 %all-to-all-start.2 = ((bf16[8,128,512]{2,1,0:T(8,128)(2,1)}), bf16[8,128,512]{2,1,0:T(8,128)(2,1)S(1)}, u32[]{:S(2)}, u32[]{:S(2)}) async-start(bf16[8,128,512]{2,1,0:T(8,128)(2,1)} %bitcast.8), calls=%async_computation.2 | async-start | bytes 2097152 | tf_op jit(solution)/shard_map/all_to_all | solution.py:310

commit v3 on v2

v3 whole, which is shorter than its diff:
```python
import functools

import jax
import jax.numpy as jnp
from jax import lax
from jax.experimental import pallas as pl
from jax.experimental.pallas import tpu as pltpu
from jax.sharding import PartitionSpec as P

HEADS = 8
PATCH = 512
EXTRA = 16
LANES = 128
MIB = 1024 * 1024
F32 = jnp.float32
BF16 = jnp.bfloat16
NN = (((1,), (0,)), ((), ()))
NT = (((1,), (1,)), ((), ()))


def mm(lhs, rhs, dims=NN):
    return lax.dot_general(lhs, rhs, dims, preferred_element_type=F32)


def iota(shape, dim):
    return lax.broadcasted_iota(jnp.int32, shape, dim)


def hot(mask):
    return jnp.where(mask, jnp.float32(1), jnp.float32(0)).astype(BF16)


def column_hot(row, count):
    size = row.shape[1]
    column = jnp.transpose(jnp.broadcast_to(row, (LANES, size)))
    lane = iota((size, LANES), 1)
    return jnp.concatenate([hot(column == lane + j * LANES) for j in range(count // LANES)], axis=1)


def pack_kernel(n_seq, capacity, me_ref, dest_ref, feats_ref, grads_ref, slot_out, *outs):
    rows, width = feats_ref.shape
    slots = n_seq * capacity
    shift = rows.bit_length() - 1
    places = dest_ref[...]
    distance = lax.bitwise_xor(lax.shift_right_logical(places, shift), me_ref[0])
    within = lax.bitwise_and(places, rows - 1) + 1
    member = iota((n_seq, rows), 0) == distance
    upper = hot(iota((rows, rows), 0) <= iota((rows, rows), 1))
    counts = mm(hot(member), upper)
    rank = jnp.sum(jnp.where(member, counts, 0.0), axis=0, keepdims=True).astype(jnp.int32) - 1
    slot = distance * capacity + rank
    slot_out[...] = slot
    select = hot(iota((slots, rows), 0) == slot)
    feats = mm(select, feats_ref[...]).astype(BF16)
    upper_half = slot >= width
    high = lax.shift_right_logical(within, 8).astype(F32)
    low = lax.bitwise_and(within, 255).astype(F32)
    line = iota((n_seq * EXTRA, rows), 0)
    kind = lax.bitwise_and(line, EXTRA - 1)
    digit = jnp.where(kind < 2, high, low)
    wanted = (
        (lax.shift_right_logical(line, EXTRA.bit_length() - 1) == distance)
        & (kind < 4)
        & ((lax.bitwise_and(kind, 1) == 1) == upper_half)
    )
    digits = jnp.where(wanted, digit, 0.0).astype(BF16)
    spread = hot(iota((width, rows), 0) == lax.bitwise_and(slot, width - 1))
    position = mm(digits, spread, NT).astype(BF16)
    for d in range(n_seq):
        outs[d][:capacity, :] = feats[d * capacity : (d + 1) * capacity]
        outs[d][capacity:, :] = position[d * EXTRA : (d + 1) * EXTRA]
    grads = mm(select, grads_ref[...]).astype(BF16)
    for d in range(n_seq):
        outs[n_seq + d][...] = grads[d * capacity : (d + 1) * capacity]


def forward_kernel(n_seq, capacity, w_hbm, gain_ref, *refs):
    recv, refs = refs[:n_seq], refs[n_seq:]
    pos_out, xhat_hbm, inv_hbm, normed_hbm, qkv_hbm, attn_out, probs_out = refs[:7]
    w_ref, xhat_ref, inv_ref, normed_ref, qkv_ref, trans, sems = refs[7:]
    width = w_ref.shape[0]
    rows = xhat_ref.shape[0]
    head = width // HEADS
    pair = 2 * head
    step = pl.program_id(0)
    w_copy = pltpu.make_async_copy(w_hbm, w_ref, sems.at[0])
    saves = [
        pltpu.make_async_copy(source, target, sems.at[1 + i])
        for i, (source, target) in enumerate(
            ((xhat_ref, xhat_hbm), (inv_ref, inv_hbm), (normed_ref, normed_hbm), (qkv_ref, qkv_hbm))
        )
    ]

    @pl.when(step == 0)
    def _():
        w_copy.start()
        tile = recv[0][capacity:, :].astype(F32)
        for s in range(1, n_seq):
            tile = tile + recv[s][capacity:, :].astype(F32)
        high = jnp.concatenate([tile[0:1], tile[1:2]], axis=1)
        low = jnp.concatenate([tile[2:3], tile[3:4]], axis=1)
        pos = (high * 256.0 + low).astype(jnp.int32) - 1
        pos_out[...] = pos
        place = hot(iota((rows, n_seq * capacity), 0) == pos)
        values = jnp.concatenate([recv[s][:capacity, :] for s in range(n_seq)], axis=0)
        feats = mm(place, values)
        centered = feats - jnp.mean(feats, axis=1, keepdims=True)
        inv = lax.rsqrt(jnp.mean(centered * centered, axis=1, keepdims=True) + 1e-05)
        xhat = centered * inv
        xhat_ref[...] = xhat
        inv_ref[...] = jnp.broadcast_to(inv, inv_ref.shape)
        normed = (xhat * gain_ref[...]).astype(BF16)
        normed_ref[...] = normed
        w_copy.wait()
        qkv = mm(normed, w_ref[...])
        qkv_ref[...] = qkv.astype(BF16)
        for save in saves:
            save.start()
        trans[...] = jnp.transpose(qkv).astype(BF16)

    lo = pl.multiple_of(step * pair, pair)
    keys = qkv_ref[:, pl.ds(pl.multiple_of(width + step * pair, pair), pair)]
    query_t = trans[pl.ds(lo, pair), :] * BF16(0.125)
    zero = jnp.zeros((head, rows), BF16)
    for j in range(2):
        part = query_t[j * head : (j + 1) * head]
        part = jnp.concatenate([part, zero] if j == 0 else [zero, part], axis=0)
        scores = mm(keys, part)
        expo = jnp.exp(scores - jnp.max(scores, axis=0, keepdims=True))
        probs = expo * (1.0 / jnp.sum(expo, axis=0, keepdims=True))
        probs_out[j] = probs
        values_t = trans[pl.ds(pl.multiple_of(2 * width + step * pair + j * head, head), head), :]
        attn_out[j * head : (j + 1) * head, :] = mm(values_t, probs.astype(BF16)).astype(BF16)

    @pl.when(step == pl.num_programs(0) - 1)
    def _():
        for save in saves:
            save.wait()


def backward_kernel(n_seq, me_ref, pos_ref, w_proj_ref, gain_ref, qkv_ref, probs_ref, *refs):
    (w_hbm, xhat_hbm, inv_hbm, normed_hbm, attn_hbm), refs = refs[:5], refs[5:]
    recv, refs = refs[:n_seq], refs[n_seq:]
    send_hbm, keep_hbm, refs = refs[0], refs[1], refs[2:]
    back, refs = refs[:n_seq], refs[n_seq:]
    w_ref, xhat_ref, inv_ref, normed_ref, attn_ref, send_ref, keep_ref, refs = *refs[:7], refs[7:]
    serial_grad, d_attn, d_attn_t, keys_t, d_qkv, normed_t, gain_column, sems = refs
    width = w_proj_ref.shape[0]
    rows = xhat_ref.shape[0]
    capacity = recv[0].shape[0]
    head = width // HEADS
    pair = 2 * head
    step = pl.program_id(0)
    loads = [
        pltpu.make_async_copy(source, target, sems.at[i])
        for i, (source, target) in enumerate(
            (
                (normed_hbm, normed_ref),
                (w_hbm, w_ref),
                (xhat_hbm, xhat_ref),
                (inv_hbm, inv_ref),
                (attn_hbm, attn_ref),
            )
        )
    ]
    saves = [
        pltpu.make_async_copy(send_ref, send_hbm, sems.at[5]),
        pltpu.make_async_copy(keep_ref, keep_hbm, sems.at[6]),
    ]

    @pl.when(step == 0)
    def _():
        for load in loads:
            load.start()
        place = hot(iota((rows, n_seq * capacity), 0) == pos_ref[...])
        grads = mm(place, jnp.concatenate([ref[...] for ref in recv], axis=0)).astype(BF16)
        serial_grad[...] = grads
        d_att = mm(grads, w_proj_ref[...], NT).astype(BF16)
        d_attn[...] = d_att
        d_attn_t[...] = jnp.transpose(d_att.astype(F32)).astype(BF16)
        keys_t[...] = jnp.transpose(qkv_ref[:, width : 2 * width].astype(F32)).astype(BF16)

    lo = pl.multiple_of(step * pair, pair)
    queries = qkv_ref[:, pl.ds(lo, pair)]
    values = qkv_ref[:, pl.ds(pl.multiple_of(2 * width + step * pair, pair), pair)]
    d_att_t = d_attn_t[pl.ds(lo, pair), :] * BF16(0.125)
    d_att = d_attn[:, pl.ds(lo, pair)]
    zero = jnp.zeros((head, rows), BF16)
    d_q, d_k, d_v = [], [], []
    for j in range(2):
        part = d_att_t[j * head : (j + 1) * head]
        part = jnp.concatenate([part, zero] if j == 0 else [zero, part], axis=0)
        probs = probs_ref[j]
        d_probs = mm(values, part)
        total = jnp.sum(d_probs * probs, axis=0, keepdims=True)
        d_scores = (probs * (d_probs - total)).astype(BF16)
        k_t = keys_t[pl.ds(pl.multiple_of(step * pair + j * head, head), head), :]
        d_q.append(mm(k_t, d_scores))
        d_k.append(mm(d_scores, queries))
        d_v.append(mm(probs.astype(BF16), d_att))
    first = iota((rows, pair), 1) < head
    d_qkv[:, pl.ds(lo, pair)] = jnp.transpose(jnp.concatenate(d_q, axis=0)).astype(BF16)
    d_qkv[:, pl.ds(pl.multiple_of(width + step * pair, pair), pair)] = jnp.where(
        first, d_k[0], d_k[1]
    ).astype(BF16)
    d_qkv[:, pl.ds(pl.multiple_of(2 * width + step * pair, pair), pair)] = jnp.where(
        first, d_v[0], d_v[1]
    ).astype(BF16)

    @pl.when(step == pl.num_programs(0) - 1)
    def _():
        for load in loads:
            load.wait()
        normed_t[...] = jnp.transpose(normed_ref[...].astype(F32)).astype(BF16)
        d_normed = mm(d_qkv[...], w_ref[...], NT)
        xhat = xhat_ref[...]
        gain_row = jnp.sum(d_normed * xhat, axis=0, keepdims=True)
        gain_column[...] = jnp.transpose(jnp.broadcast_to(gain_row, (LANES, width)))
        half = width // 2
        bit = lax.bitwise_and(me_ref[0], 1)
        for out, start, save in ((send_ref, (1 - bit) * half, saves[0]), (keep_ref, bit * half, saves[1])):
            part = pl.ds(pl.multiple_of(start, half), half)
            out[:, : 3 * width] = mm(normed_t[part, :], d_qkv[...])
            out[:, 3 * width : 4 * width] = mm(attn_ref[part, :], serial_grad[...])
            out[:, 4 * width :] = gain_column[part, :]
            save.start()
        scaled = d_normed * gain_ref[...]
        residual = inv_ref[:, 0:1] * (
            scaled
            - jnp.mean(scaled, axis=1, keepdims=True)
            - xhat * jnp.mean(scaled * xhat, axis=1, keepdims=True)
        )
        serial_dx = (serial_grad[...].astype(F32) + residual).astype(BF16)
        returned = mm(column_hot(pos_ref[...], rows), serial_dx).astype(BF16)
        for d in range(n_seq):
            back[d][...] = returned[d * capacity : (d + 1) * capacity]
        for save in saves:
            save.wait()


def unpack_kernel(slot_ref, *refs):
    values = jnp.concatenate([ref[...] for ref in refs[:-1]], axis=0)
    refs[-1][...] = mm(column_hot(slot_ref[...], values.shape[0]), values).astype(BF16)


def whole(shape):
    return pl.BlockSpec(shape, lambda *_: (0,) * len(shape), pipeline_mode=pl.Buffered(1))


def params(mib):
    return pltpu.CompilerParams(vmem_limit_bytes=mib * MIB)


def shape_of(shape, dtype):
    return jax.ShapeDtypeStruct(shape, dtype)


def by_distance(blocks, axis):
    count = len(blocks)
    return [blocks[0]] + [
        lax.ppermute(blocks[k], axis, [(i, i ^ k) for i in range(count)]) for k in range(1, count)
    ]


def chip_steps():
    n_seq, me = lax.axis_size("seq"), lax.axis_index("seq")
    bits = list(range(1, n_seq.bit_length() - 1))
    middle = len(bits) // 2
    orders = (bits, bits[middle:] + bits[:middle])
    odd = lax.bitwise_and(me, 1) == 1

    def side(bit):
        return lax.bitwise_and(lax.shift_right_logical(me, jnp.asarray(bit, me.dtype)), 1)

    steps = [([(i, i ^ 1) for i in range(n_seq)], side(0))]
    for even_bit, odd_bit in zip(*orders):
        pairs = [(i, i ^ (1 << (odd_bit if i & 1 else even_bit))) for i in range(n_seq)]
        steps.append((pairs, jnp.where(odd, side(odd_bit), side(even_bit))))
    return steps


def reduce_in_plane(send, keep, steps):
    part = keep + lax.ppermute(send, "seq", steps[0][0])
    for pairs, side in steps[1:]:
        half = part.shape[0] // 2
        send = lax.dynamic_slice_in_dim(part, (1 - side) * half, half)
        keep = lax.dynamic_slice_in_dim(part, side * half, half)
        part = keep + lax.ppermute(send, "seq", pairs)
    return part


def sum_over_planes(part):
    n_dp, plane = lax.axis_size("dp"), lax.axis_index("dp")
    size = part.shape[0] // n_dp
    pieces = [
        lax.dynamic_slice_in_dim(part, lax.bitwise_xor(plane, k) * size, size) for k in range(n_dp)
    ]
    total = functools.reduce(jnp.add, by_distance(pieces, "dp")).astype(BF16)
    shares = jnp.stack(by_distance([total] * n_dp, "dp"))
    return jnp.concatenate(
        [lax.dynamic_index_in_dim(shares, lax.bitwise_xor(plane, p), keepdims=False) for p in range(n_dp)],
        axis=0,
    )


def share_in_plane(part, steps):
    for pairs, side in reversed(steps):
        other = lax.ppermute(part, "seq", pairs)
        part = jnp.where(
            side == 0, jnp.concatenate([part, other], axis=0), jnp.concatenate([other, part], axis=0)
        )
    return part


def per_device(points, cotangent, dest, w_qkv, w_proj, gain):
    feats = points[0]
    grads = cotangent[0]
    rows, width = feats.shape
    n_seq = lax.axis_size("seq")
    capacity = 2 * (rows // n_seq)
    slots = n_seq * capacity
    block = capacity + EXTRA
    pairs = HEADS // 2
    pair = width // pairs
    sum_shape = (width // 2, 4 * width + LANES)
    me = jnp.reshape(lax.axis_index("seq").astype(jnp.int32), (1,))
    gain_row = gain.reshape(1, width)
    in_smem = pl.BlockSpec(memory_space=pltpu.SMEM)
    in_vmem = pl.BlockSpec(memory_space=pltpu.VMEM)
    in_hbm = pl.BlockSpec(memory_space=pl.ANY)

    slot, *packed = pl.pallas_call(
        functools.partial(pack_kernel, n_seq, capacity),
        out_shape=[shape_of((1, rows), jnp.int32)]
        + [shape_of((block, width), BF16)] * n_seq
        + [shape_of((capacity, width), BF16)] * n_seq,
        in_specs=[in_smem, in_vmem, in_vmem, in_vmem],
        out_specs=[in_vmem] * (1 + 2 * n_seq),
        compiler_params=params(20),
        cost_estimate=pl.CostEstimate(
            flops=4 * slots * rows * width, bytes_accessed=4 * MIB, transcendentals=0
        ),
        name="pack",
    )(me, dest, feats, grads)
    feats_got = by_distance(packed[:n_seq], "seq")
    feats_got, grads_sent = lax.optimization_barrier((feats_got, packed[n_seq:]))
    grads_got = by_distance(grads_sent, "seq")

    pos, xhat, inv, normed, qkv, attn_t, probs = pl.pallas_call(
        functools.partial(forward_kernel, n_seq, capacity),
        grid=(pairs,),
        out_shape=(
            shape_of((1, slots), jnp.int32),
            shape_of((rows, width), F32),
            shape_of((rows, LANES), F32),
            shape_of((rows, width), BF16),
            shape_of((rows, 3 * width), BF16),
            shape_of((width, rows), BF16),
            shape_of((HEADS, rows, rows), F32),
        ),
        in_specs=[in_hbm, whole((1, width))] + [whole((block, width))] * n_seq,
        out_specs=[whole((1, slots))]
        + [in_hbm] * 4
        + [
            pl.BlockSpec((pair, rows), lambda i: (i, 0)),
            pl.BlockSpec((2, rows, rows), lambda i: (i, 0, 0)),
        ],
        scratch_shapes=[
            pltpu.VMEM((width, 3 * width), BF16),
            pltpu.VMEM((rows, width), F32),
            pltpu.VMEM((rows, LANES), F32),
            pltpu.VMEM((rows, width), BF16),
            pltpu.VMEM((rows, 3 * width), BF16),
            pltpu.VMEM((3 * width, rows), BF16),
            pltpu.SemaphoreType.DMA((5,)),
        ],
        compiler_params=params(26),
        cost_estimate=pl.CostEstimate(
            flops=6 * rows * width * width + 8 * HEADS * rows * rows * pair,
            bytes_accessed=16 * MIB,
            transcendentals=HEADS * rows * rows,
        ),
        name="forward",
    )(w_qkv, gain_row, *feats_got)

    send, keep, *back = pl.pallas_call(
        functools.partial(backward_kernel, n_seq),
        grid=(pairs,),
        out_shape=[shape_of(sum_shape, F32)] * 2 + [shape_of((capacity, width), BF16)] * n_seq,
        in_specs=[
            in_smem,
            whole((1, slots)),
            whole((width, width)),
            whole((1, width)),
            whole((rows, 3 * width)),
            pl.BlockSpec((2, rows, rows), lambda i: (i, 0, 0)),
        ]
        + [in_hbm] * 5
        + [whole((capacity, width))] * n_seq,
        out_specs=[in_hbm] * 2 + [whole((capacity, width))] * n_seq,
        scratch_shapes=[
            pltpu.VMEM((width, 3 * width), BF16),
            pltpu.VMEM((rows, width), F32),
            pltpu.VMEM((rows, LANES), F32),
            pltpu.VMEM((rows, width), BF16),
            pltpu.VMEM((width, rows), BF16),
            pltpu.VMEM(sum_shape, F32),
            pltpu.VMEM(sum_shape, F32),
            pltpu.VMEM((rows, width), BF16),
            pltpu.VMEM((rows, width), BF16),
            pltpu.VMEM((width, rows), BF16),
            pltpu.VMEM((width, rows), BF16),
            pltpu.VMEM((rows, 3 * width), BF16),
            pltpu.VMEM((width, rows), BF16),
            pltpu.VMEM((width, LANES), F32),
            pltpu.SemaphoreType.DMA((7,)),
        ],
        compiler_params=params(34),
        cost_estimate=pl.CostEstimate(
            flops=14 * rows * width * width + 8 * HEADS * rows * rows * pair,
            bytes_accessed=24 * MIB,
            transcendentals=0,
        ),
        name="backward",
    )(me, pos, w_proj, gain_row, qkv, probs, w_qkv, xhat, inv, normed, attn_t, *grads_got)

    steps = chip_steps()
    part = reduce_in_plane(send, keep, steps)
    back, part = lax.optimization_barrier((back, part))
    returned = by_distance(back, "seq")
    part, returned = lax.optimization_barrier((sum_over_planes(part), returned))
    total = share_in_plane(part, steps).astype(F32)
    grad_local = pl.pallas_call(
        unpack_kernel,
        out_shape=shape_of((rows, width), BF16),
        in_specs=[in_vmem] * (1 + n_seq),
        out_specs=in_vmem,
        compiler_params=params(20),
        cost_estimate=pl.CostEstimate(
            flops=2 * slots * rows * width, bytes_accessed=2 * MIB, transcendentals=0
        ),
        name="unpack",
    )(slot, *returned)
    return (grad_local[None], total[:, : 3 * width], total[:, 3 * width : 4 * width], total[:, 4 * width])


def solution(mesh):
    return jax.shard_map(
        per_device,
        mesh=mesh,
        in_specs=(P("dp", "seq", None), P("dp", "seq", None), P("dp", "seq"), P(), P(), P()),
        out_specs=(P("dp", "seq", None), P(), P(), P()),
        check_vma=False,
    )
```

time: 176 us -> 153 us (0.87)
  blocking collectives: 21.8 us -> 0 us
  local copies, waits for them, and re-layouts: 23.7 us -> 11.6 us
  starting transfers between devices: 24.9 us -> 36.5 us
    all_to_all x1 -> x0, blocking collectives: 21.8 us -> none  [exchange(): got = lax.all_to_all(sent, 'seq', split_axis=0, concat_axis=0, tiled=True)]
    ppermute x10 -> x33, starting transfers between devices: 16.9 us -> 36.5 us  [the longest x27 30 us: by_distance(): lax.ppermute(blocks[k], axis, [(i, i ^ k) for i in range(count)])]
    all_to_all x2 -> x0, waiting for transfers between devices: 15.4 us -> none  [exchange(): got = lax.all_to_all(sent, 'seq', split_axis=0, concat_axis=0, tiled=True)]
    ppermute x10 -> x33, waiting for transfers between devices: 58.4 us -> 72.6 us  [the longest x27 29.9 us: by_distance(): lax.ppermute(blocks[k], axis, [(i, i ^ k) for i in range(count)])]
    unnamed x38 -> x18, local copies, waits for them, and re-layouts: 19.6 us -> 7.52 us
    all_to_all x2 -> x0, starting transfers between devices: 7.93 us -> none  [exchange(): got = lax.all_to_all(sent, 'seq', split_axis=0, concat_axis=0, tiled=True)]
  transfers between devices with their start and end apart: 12 -> 33, of which waited for: 10 -> 17; matrix products, arithmetic and copies ran while one was open for 0% -> 0% of each run, Pallas kernels for 5% -> 7%
where the time goes in v3:
time: 153 us
  waiting for transfers between devices  72.6 us (47%)
  starting transfers between devices  36.5 us (24%)
  Pallas kernels  25.5 us (17%)
  local copies, waits for them, and re-layouts  11.6 us (8%)
  other arithmetic  5.87 us (4%)
    ppermute x27, starting transfers between devices, by_distance(): lax.ppermute(blocks[k], axis, [(i, i ^ k) for i in range(count)])  30 us
    ppermute x27, waiting for transfers between devices, by_distance(): lax.ppermute(blocks[k], axis, [(i, i ^ k) for i in range(count)])  29.9 us
    ppermute x2, waiting for transfers between devices, reduce_in_plane(): part = keep + lax.ppermute(send, 'seq', pairs)  24 us
    ppermute x3, waiting for transfers between devices, share_in_plane(): other = lax.ppermute(part, 'seq', pairs)  14.3 us
    pallas_call x1, Pallas kernels, per_device(): pl.pallas_call(functools.partial(backward_kernel, n_seq), grid=(pairs,),...  13.8 us
    pallas_call x1, Pallas kernels, per_device(): pl.pallas_call(functools.partial(forward_kernel, n_seq, capacity), grid=(...  8.56 us
    unnamed x18, local copies, waits for them, and re-layouts  7.52 us
    ppermute x1, waiting for transfers between devices, reduce_in_plane(): part = keep + lax.ppermute(send, 'seq', steps[0][0])  4.32 us
  transfers between devices with their start and end apart: 33, of which 17 were waited for; matrix products, arithmetic and copies ran while one was open for 0% of the time, Pallas kernels for 7%

profile of v3, /device:TPU:0, one launch (start us, length us, event | category | flops | bytes accessed | tf_op | source)
XLA Modules:
  0.0 153.0 jit_solution(14129657361188722461)
XLA Ops:
  0.7 1.1 copy-done.5
  1.8 1.0 copy-done.6
  2.9 0.7 copy-done.7
  3.5 1.6 %pack.1 = (s32[1,512]{1,0:T(1,128)S(1)}, bf16[144,512]{1,0:T(8,128)(2,1)S(1)}, bf16[144,512]{1,0:T(8,128)(2,1)S(1)}, bf16[144,512]{1,0:T(8,128)(2,1)S(1)}, bf16[...) custom-call(s32[1]{0:T(128)} %bitcast.me_ref, ...), custom_call_target="tpu_custom_call" | custom-call | flops 1073741824 | bytes 4194304 | tf_op jit(solution)/shard_map/pack/pallas_call | solution.py:332
  5.7 2.6 %collective-permute-start.1 = (bf16[144,512]{1,0:T(8,128)(2,1)S(1)}, bf16[144,512]{1,0:T(8,128)(2,1)S(1)}, u32[]{:S(2)}, u32[]{:S(2)}) collective-permute-start(bf16[144,512]{1,0:T(8,128)(2,1)S(1)} %get-tuple-element.75), channel_id=1, source_target_pairs={{0,8},{4,12},{8,0},{12,4},{16,24},{20,28},{24,16},{28,20},{1,9},{5... | collective-permute-start | bytes 442376 | tf_op jit(solution)/shard_map/ppermute | solution.py:261
  8.3 1.8 %collective-permute-start.3 = (bf16[144,512]{1,0:T(8,128)(2,1)S(1)}, bf16[144,512]{1,0:T(8,128)(2,1)S(1)}, u32[]{:S(2)}, u32[]{:S(2)}) collective-permute-start(bf16[144,512]{1,0:T(8,128)(2,1)S(1)} %get-tuple-element.77), channel_id=1, source_target_pairs={{0,16},{4,20},{8,24},{12,28},{16,0},{20,4},{24,8},{28,12},{1,17},{... | collective-permute-start | bytes 442376 | tf_op jit(solution)/shard_map/ppermute | solution.py:261
  10.1 2.6 %collective-permute-start.5 = (bf16[144,512]{1,0:T(8,128)(2,1)S(1)}, bf16[144,512]{1,0:T(8,128)(2,1)S(1)}, u32[]{:S(2)}, u32[]{:S(2)}) collective-permute-start(bf16[144,512]{1,0:T(8,128)(2,1)S(1)} %get-tuple-element.79), channel_id=1, source_target_pairs={{0,24},{4,28},{8,16},{12,20},{16,8},{20,12},{24,0},{28,4},{1,25},{... | collective-permute-start | bytes 442376 | tf_op jit(solution)/shard_map/ppermute | solution.py:261
  12.9 1.7 %collective-permute-start.6 = (bf16[144,512]{1,0:T(8,128)(2,1)S(1)}, bf16[144,512]{1,0:T(8,128)(2,1)S(1)}, u32[]{:S(2)}, u32[]{:S(2)}) collective-permute-start(bf16[144,512]{1,0:T(8,128)(2,1)S(1)} %get-tuple-element.80), channel_id=1, source_target_pairs={{0,28},{4,24},{8,20},{12,16},{16,12},{20,8},{24,4},{28,0},{1,29},{... | collective-permute-start | bytes 442376 | tf_op jit(solution)/shard_map/ppermute | solution.py:261
  14.6 0.9 collective-permute-done.2.refs_3_
  15.6 7.6 %collective-permute-done.4.refs_5_ = bf16[144,512]{1,0:T(8,128)(2,1)S(1)} collective-permute-done((bf16[144,512]{1,0:T(8,128)(2,1)S(1)}, bf16[144,512]{1,0:T(8,128)(2,1)S(1)}, u32[]{:S(2)}, u32[]{:S(2)}) %collective-permute-start.4) | collective-permute-done | bytes 147488 | tf_op jit(solution)/shard_map/ppermute | solution.py:261
  23.7 1.7 %collective-permute-start.8 = (bf16[128,512]{1,0:T(8,128)(2,1)S(1)}, bf16[128,512]{1,0:T(8,128)(2,1)S(1)}, u32[]{:S(2)}, u32[]{:S(2)}) collective-permute-start(bf16[128,512]{1,0:T(8,128)(2,1)S(1)} %get-tuple-element.106), channel_id=1, source_target_pairs={{0,8},{4,12},{8,0},{12,4},{16,24},{20,28},{24,16},{28,20},{1,9},{5... | collective-permute-start | bytes 393224 | tf_op jit(solution)/shard_map/ppermute | solution.py:261
  25.4 1.5 %collective-permute-start.10 = (bf16[128,512]{1,0:T(8,128)(2,1)S(1)}, bf16[128,512]{1,0:T(8,128)(2,1)S(1)}, u32[]{:S(2)}, u32[]{:S(2)}) collective-permute-start(bf16[128,512]{1,0:T(8,128)(2,1)S(1)} %get-tuple-element.108), channel_id=1, source_target_pairs={{0,16},{4,20},{8,24},{12,28},{16,0},{20,4},{24,8},{28,12},{1,17},{... | collective-permute-start | bytes 393224 | tf_op jit(solution)/shard_map/ppermute | solution.py:261
  27.2 2.7 %collective-permute-start.12 = (bf16[128,512]{1,0:T(8,128)(2,1)S(1)}, bf16[128,512]{1,0:T(8,128)(2,1)S(1)}, u32[]{:S(2)}, u32[]{:S(2)}) collective-permute-start(bf16[128,512]{1,0:T(8,128)(2,1)S(1)} %get-tuple-element.110), channel_id=1, source_target_pairs={{0,24},{4,28},{8,16},{12,20},{16,8},{20,12},{24,0},{28,4},{1,25},{... | collective-permute-start | bytes 393224 | tf_op jit(solution)/shard_map/ppermute | solution.py:261
  30.0 0.8 collective-permute-start.13
  30.8 8.6 %forward.1 = (s32[1,1024]{1,0:T(1,128)S(1)}, f32[512,512]{1,0:T(8,128)S(1)}, f32[512,128]{1,0:T(8,128)S(1)}, bf16[512,512]{1,0:T(8,128)(2,1)S(1)}, bf16[512,1536...) custom-call(bf16[512,1536]{1,0:T(8,128)(2,1)S(1)} %copy-done.1, f32[1,512]{1,0:T(1,128)S(1)} %bitcast.17, ...), custom_call_target="tpu_custom_call" | custom-call | flops 2952790016 | bytes 16777216 | tf_op jit(solution)/shard_map/forward/pallas_call | solution.py:349
  39.4 3.3 %copy-done = f32[8,512,512]{2,1,0:T(8,128)} copy-done((f32[8,512,512]{2,1,0:T(8,128)}, f32[8,512,512]{2,1,0:T(8,128)S(1)}, u32[]{:S(2)}) %copy-start) | copy-done | bytes 8388632
  42.7 13.8 %backward.1 = (f32[256,2176]{1,0:T(8,128)}, f32[256,2176]{1,0:T(8,128)S(1)}, bf16[128,512]{1,0:T(8,128)(2,1)S(1)}, bf16[128,512]{1,0:T(8,128)(2,1)S(1)}, bf16[12...) custom-call(s32[1]{0:T(128)} %bitcast.me_ref, ...), custom_call_target="tpu_custom_call" | custom-call | flops 4026531840 | bytes 25165824 | tf_op jit(solution)/shard_map/backward/pallas_call | solution.py:386
  56.5 2.2 %collective-permute-start.14 = (f32[256,2176]{1,0:T(8,128)}, f32[256,2176]{1,0:T(8,128)}, u32[]{:S(2)}, u32[]{:S(2)}) collective-permute-start(f32[256,2176]{1,0:T(8,128)} %get-tuple-element.121), channel_id=1, source_target_pairs={{0,4},{4,0},{8,12},{12,8},{16,20},{20,16},{24,28},{28,24},{1,5},{5... | collective-permute-start | bytes 6684680 | tf_op jit(solution)/shard_map/ppermute | solution.py:283
  58.7 4.3 %collective-permute-done.14 = f32[256,2176]{1,0:T(8,128)} collective-permute-done((f32[256,2176]{1,0:T(8,128)}, f32[256,2176]{1,0:T(8,128)}, u32[]{:S(2)}, u32[]{:S(2)}) %collective-permute-start.14) | collective-permute-done | bytes 2228256 | tf_op jit(solution)/shard_map/ppermute | solution.py:283
  63.0 1.9 %add.55 = f32[256,2176]{1,0:T(8,128)S(1)} add(f32[256,2176]{1,0:T(8,128)S(1)} %get-tuple-element.120, f32[256,2176]{1,0:T(8,128)} %collective-permute-done.14) | non-fusion elementwise | flops 557056 | bytes 6684672 | tf_op jit(solution)/shard_map/add | solution.py:283
  64.9 1.4 copy-done.8
  66.3 0.6 collective-permute-start.15
  66.9 15.0 %collective-permute-done.15 = f32[128,2176]{1,0:T(8,128)S(1)} collective-permute-done((f32[128,2176]{1,0:T(8,128)S(1)}, f32[128,2176]{1,0:T(8,128)S(1)}, u32[]{:S(2)}, u32[]{:S(2)}) %collective-permute-start.15) | collective-permute-done | bytes 1114144 | tf_op jit(solution)/shard_map/ppermute | solution.py:288
  81.9 1.5 dynamic-slice_add_fusion
  84.0 9.0 %collective-permute-done.16 = f32[64,2176]{1,0:T(8,128)S(1)} collective-permute-done((f32[64,2176]{1,0:T(8,128)S(1)}, f32[64,2176]{1,0:T(8,128)S(1)}, u32[]{:S(2)}, u32[]{:S(2)}) %collective-permute-start.16) | collective-permute-done | bytes 557088 | tf_op jit(solution)/shard_map/ppermute | solution.py:288
  93.1 3.7 %collective-permute-start.19 = (f32[16,2176]{1,0:T(8,128)S(1)}, f32[16,2176]{1,0:T(8,128)S(1)}, u32[]{:S(2)}, u32[]{:S(2)}) collective-permute-start(f32[16,2176]{1,0:T(8,128)S(1)} %get-tuple-element.141), channel_id=1, source_target_pairs={{0,3},{1,2},{2,1},{3,0},{4,7},{5,6},{6,5},{7,4},{8,11},{9,10},{10,... | collective-permute-start | bytes 417800 | tf_op jit(solution)/shard_map/ppermute | solution.py:261
  96.8 0.8 collective-permute-start.17
  97.6 4.0 %collective-permute-done.19 = f32[16,2176]{1,0:T(8,128)S(1)} collective-permute-done((f32[16,2176]{1,0:T(8,128)S(1)}, f32[16,2176]{1,0:T(8,128)S(1)}, u32[]{:S(2)}, u32[]{:S(2)}) %collective-permute-start.19) | collective-permute-done | bytes 139296 | tf_op jit(solution)/shard_map/ppermute | solution.py:261
  101.6 6.1 %collective-permute-done.18 = f32[16,2176]{1,0:T(8,128)S(1)} collective-permute-done((f32[16,2176]{1,0:T(8,128)S(1)}, f32[16,2176]{1,0:T(8,128)S(1)}, u32[]{:S(2)}, u32[]{:S(2)}) %collective-permute-start.18) | collective-permute-done | bytes 139296 | tf_op jit(solution)/shard_map/ppermute | solution.py:261
  107.7 2.4 %collective-permute-start.22 = (bf16[16,2176]{1,0:T(8,128)(2,1)S(1)}, bf16[16,2176]{1,0:T(8,128)(2,1)S(1)}, u32[]{:S(2)}, u32[]{:S(2)}) collective-permute-start(bf16[16,2176]{1,0:T(8,128)(2,1)S(1)} %add_convert_fusion), channel_id=1, source_target_pairs={{0,3},{1,2},{2,1},{3,0},{4,7},{5,6},{6,5},{7,4},{8,11},{9,10},{10,... | collective-permute-start | bytes 208904 | tf_op jit(solution)/shard_map/ppermute | solution.py:261
  110.1 2.0 %collective-permute-start.20 = (bf16[16,2176]{1,0:T(8,128)(2,1)S(1)}, bf16[16,2176]{1,0:T(8,128)(2,1)S(1)}, u32[]{:S(2)}, u32[]{:S(2)}) collective-permute-start(bf16[16,2176]{1,0:T(8,128)(2,1)S(1)} %add_convert_fusion), channel_id=1, source_target_pairs={{0,1},{1,0},{2,3},{3,2},{4,5},{5,4},{6,7},{7,6},{8,9},{9,8},{10,11... | collective-permute-start | bytes 208904 | tf_op jit(solution)/shard_map/ppermute | solution.py:261
  112.7 1.4 collective-permute-done.22
  114.1 1.5 collective-permute-done.21
  115.5 0.6 collective-permute-start.26
  116.2 1.5 collective-permute-start.28
  117.7 0.7 collective-permute-done.24.refs_2_
  118.5 1.6 %collective-permute-start.29 = (bf16[128,512]{1,0:T(8,128)(2,1)S(1)}, bf16[128,512]{1,0:T(8,128)(2,1)S(1)}, u32[]{:S(2)}, u32[]{:S(2)}) collective-permute-start(bf16[128,512]{1,0:T(8,128)(2,1)S(1)} %get-tuple-element.130), channel_id=1, source_target_pairs={{0,28},{4,24},{8,20},{12,16},{16,12},{20,8},{24,4},{28,0},{1,29},{... | collective-permute-start | bytes 393224 | tf_op jit(solution)/shard_map/ppermute | solution.py:261
  120.5 7.0 %collective-permute-done.26.refs_4_ = bf16[128,512]{1,0:T(8,128)(2,1)S(1)} collective-permute-done((bf16[128,512]{1,0:T(8,128)(2,1)S(1)}, bf16[128,512]{1,0:T(8,128)(2,1)S(1)}, u32[]{:S(2)}, u32[]{:S(2)}) %collective-permute-start.26) | collective-permute-done | bytes 131104 | tf_op jit(solution)/shard_map/ppermute | solution.py:261
  127.5 1.4 collective-permute-start.30
  129.0 5.2 %collective-permute-done.30 = bf16[64,2176]{1,0:T(8,128)(2,1)S(1)} collective-permute-done((bf16[64,2176]{1,0:T(8,128)(2,1)S(1)}, bf16[64,2176]{1,0:T(8,128)(2,1)S(1)}, u32[]{:S(2)}, u32[]{:S(2)}) %collective-permute-start.30) | collective-permute-done | bytes 278560 | tf_op jit(solution)/shard_map/ppermute | solution.py:308
  134.2 1.7 %collective-permute-start.31 = (bf16[128,2176]{1,0:T(8,128)(2,1)S(1)}, bf16[128,2176]{1,0:T(8,128)(2,1)S(1)}, u32[]{:S(2)}, u32[]{:S(2)}) collective-permute-start(bf16[128,2176]{1,0:T(8,128)(2,1)S(1)} %maximum_select_fusion.2), channel_id=1, source_target_pairs={{0,8},{4,20},{8,0},{12,28},{16,24},{20,4},{24,16},{28,12},{1,9},{5... | collective-permute-start | bytes 1671176 | tf_op jit(solution)/shard_map/ppermute | solution.py:308
  136.0 7.9 %collective-permute-done.31 = bf16[128,2176]{1,0:T(8,128)(2,1)S(1)} collective-permute-done((bf16[128,2176]{1,0:T(8,128)(2,1)S(1)}, bf16[128,2176]{1,0:T(8,128)(2,1)S(1)}, u32[]{:S(2)}, u32[]{:S(2)}) %collective-permute-start.31) | collective-permute-done | bytes 557088 | tf_op jit(solution)/shard_map/ppermute | solution.py:308
  144.2 1.6 %unpack.1 = bf16[512,512]{1,0:T(8,128)(2,1)} custom-call(s32[1,512]{1,0:T(1,128)S(1)} %get-tuple-element.72.slot_ref, bf16[128,512]{1,0:T(8,128)(2,1)S(1)} %get-tuple-element.131.refs_0_, bf16[128,512]{1,0:T(8,128)(2,1)S(1)} %collective-permute-done.23.refs_1_, bf16[128,512]{1,0:T(8,128)(2,1)S(1)} %collective-permute-done.24.refs_2_, ...), custom_call_target="tpu_custom_call" | custom-call | flops 536870912 | bytes 2097152 | tf_op jit(solution)/shard_map/unpack/pallas_call | solution.py:433
  145.7 1.3 collective-permute-done.32
  147.0 2.0 %fusion = f32[512,2176]{1,0:T(8,128)S(1)} fusion(bf16[256,2176]{1,0:T(8,128)(2,1)} %collective-permute-done.32, bf16[256,2176]{1,0:T(8,128)(2,1)S(1)} %maximum_select_fusion.1, pred[]{:T(512)S(6)} %eq.13), kind=kLoop, calls=%fused_computation.1 | loop fusion | flops 11141120 | bytes 6684673 | tf_op jit(solution)/shard_map/convert_element_type | solution.py:432
  149.1 2.1 %slice.12 = f32[512,1536]{1,0:T(8,128)} slice(f32[512,2176]{1,0:T(8,128)S(1)} %fusion), slice={[0:512], [0:1536]} | slice | bytes 6291456 | tf_op jit(solution)/shard_map/slice | solution.py:444
  151.1 1.1 slice.13
  152.3 0.7 slice_reduce_fusion
  (56 shorter events, 4.0 us)
Async XLA Ops:
  0.6 30.2 %copy-start.1 = (bf16[512,1536]{1,0:T(8,128)(2,1)S(1)}, bf16[512,1536]{1,0:T(8,128)(2,1)}, u32[]{:S(2)}) copy-start(bf16[512,1536]{1,0:T(8,128)(2,1)} %refs_0_.1) | copy-start | bytes 4718596
  0.6 30.1 %copy-start.4 = (f32[512]{0:T(512)S(1)}, f32[512]{0:T(512)}, u32[]{:S(2)}) copy-start(f32[512]{0:T(512)} %param.11) | copy-start | bytes 6148
  0.7 1.2 copy-start.5
  1.8 1.0 copy-start.6
  2.9 0.7 copy-start.7
  5.1 4.9 %collective-permute-start = (bf16[144,512]{1,0:T(8,128)(2,1)S(1)}, bf16[144,512]{1,0:T(8,128)(2,1)S(1)}, u32[]{:S(2)}, u32[]{:S(2)}) collective-permute-start(bf16[144,512]{1,0:T(8,128)(2,1)S(1)} %get-tuple-element.74), channel_id=1, source_target_pairs={{0,4},{4,0},{8,12},{12,8},{16,20},{20,16},{24,28},{28,24},{1,5},{5... | collective-permute-start | bytes 442376 | tf_op jit(solution)/shard_map/ppermute | solution.py:261
  5.7 7.3 %collective-permute-start.1 = (bf16[144,512]{1,0:T(8,128)(2,1)S(1)}, bf16[144,512]{1,0:T(8,128)(2,1)S(1)}, u32[]{:S(2)}, u32[]{:S(2)}) collective-permute-start(bf16[144,512]{1,0:T(8,128)(2,1)S(1)} %get-tuple-element.75), channel_id=1, source_target_pairs={{0,8},{4,12},{8,0},{12,4},{16,24},{20,28},{24,16},{28,20},{1,9},{5... | collective-permute-start | bytes 442376 | tf_op jit(solution)/shard_map/ppermute | solution.py:261
  8.2 7.3 %collective-permute-start.2 = (bf16[144,512]{1,0:T(8,128)(2,1)S(1)}, bf16[144,512]{1,0:T(8,128)(2,1)S(1)}, u32[]{:S(2)}, u32[]{:S(2)}) collective-permute-start(bf16[144,512]{1,0:T(8,128)(2,1)S(1)} %get-tuple-element.76), channel_id=1, source_target_pairs={{0,12},{4,8},{8,4},{12,0},{16,28},{20,24},{24,20},{28,16},{1,13},{... | collective-permute-start | bytes 442376 | tf_op jit(solution)/shard_map/ppermute | solution.py:261
  8.3 7.3 %collective-permute-start.3 = (bf16[144,512]{1,0:T(8,128)(2,1)S(1)}, bf16[144,512]{1,0:T(8,128)(2,1)S(1)}, u32[]{:S(2)}, u32[]{:S(2)}) collective-permute-start(bf16[144,512]{1,0:T(8,128)(2,1)S(1)} %get-tuple-element.77), channel_id=1, source_target_pairs={{0,16},{4,20},{8,24},{12,28},{16,0},{20,4},{24,8},{28,12},{1,17},{... | collective-permute-start | bytes 442376 | tf_op jit(solution)/shard_map/ppermute | solution.py:261
  10.1 13.1 %collective-permute-start.4 = (bf16[144,512]{1,0:T(8,128)(2,1)S(1)}, bf16[144,512]{1,0:T(8,128)(2,1)S(1)}, u32[]{:S(2)}, u32[]{:S(2)}) collective-permute-start(bf16[144,512]{1,0:T(8,128)(2,1)S(1)} %get-tuple-element.78), channel_id=1, source_target_pairs={{0,20},{4,16},{8,28},{12,24},{16,4},{20,0},{24,12},{28,8},{1,21},{... | collective-permute-start | bytes 442376 | tf_op jit(solution)/shard_map/ppermute | solution.py:261
  10.1 13.1 %collective-permute-start.5 = (bf16[144,512]{1,0:T(8,128)(2,1)S(1)}, bf16[144,512]{1,0:T(8,128)(2,1)S(1)}, u32[]{:S(2)}, u32[]{:S(2)}) collective-permute-start(bf16[144,512]{1,0:T(8,128)(2,1)S(1)} %get-tuple-element.79), channel_id=1, source_target_pairs={{0,24},{4,28},{8,16},{12,20},{16,8},{20,12},{24,0},{28,4},{1,25},{... | collective-permute-start | bytes 442376 | tf_op jit(solution)/shard_map/ppermute | solution.py:261
  12.9 10.2 %collective-permute-start.6 = (bf16[144,512]{1,0:T(8,128)(2,1)S(1)}, bf16[144,512]{1,0:T(8,128)(2,1)S(1)}, u32[]{:S(2)}, u32[]{:S(2)}) collective-permute-start(bf16[144,512]{1,0:T(8,128)(2,1)S(1)} %get-tuple-element.80), channel_id=1, source_target_pairs={{0,28},{4,24},{8,20},{12,16},{16,12},{20,8},{24,4},{28,0},{1,29},{... | collective-permute-start | bytes 442376 | tf_op jit(solution)/shard_map/ppermute | solution.py:261
  23.2 4.1 %collective-permute-start.7 = (bf16[128,512]{1,0:T(8,128)(2,1)S(1)}, bf16[128,512]{1,0:T(8,128)(2,1)S(1)}, u32[]{:S(2)}, u32[]{:S(2)}) collective-permute-start(bf16[128,512]{1,0:T(8,128)(2,1)S(1)} %get-tuple-element.105), channel_id=1, source_target_pairs={{0,4},{4,0},{8,12},{12,8},{16,20},{20,16},{24,28},{28,24},{1,5},{5... | collective-permute-start | bytes 393224 | tf_op jit(solution)/shard_map/ppermute | solution.py:261
  23.7 6.3 %collective-permute-start.8 = (bf16[128,512]{1,0:T(8,128)(2,1)S(1)}, bf16[128,512]{1,0:T(8,128)(2,1)S(1)}, u32[]{:S(2)}, u32[]{:S(2)}) collective-permute-start(bf16[128,512]{1,0:T(8,128)(2,1)S(1)} %get-tuple-element.106), channel_id=1, source_target_pairs={{0,8},{4,12},{8,0},{12,4},{16,24},{20,28},{24,16},{28,20},{1,9},{5... | collective-permute-start | bytes 393224 | tf_op jit(solution)/shard_map/ppermute | solution.py:261
  25.4 17.2 %collective-permute-start.9 = (bf16[128,512]{1,0:T(8,128)(2,1)S(1)}, bf16[128,512]{1,0:T(8,128)(2,1)S(1)}, u32[]{:S(2)}, u32[]{:S(2)}) collective-permute-start(bf16[128,512]{1,0:T(8,128)(2,1)S(1)} %get-tuple-element.107), channel_id=1, source_target_pairs={{0,12},{4,8},{8,4},{12,0},{16,28},{20,24},{24,20},{28,16},{1,13},{... | collective-permute-start | bytes 393224 | tf_op jit(solution)/shard_map/ppermute | solution.py:261
  25.4 17.2 %collective-permute-start.10 = (bf16[128,512]{1,0:T(8,128)(2,1)S(1)}, bf16[128,512]{1,0:T(8,128)(2,1)S(1)}, u32[]{:S(2)}, u32[]{:S(2)}) collective-permute-start(bf16[128,512]{1,0:T(8,128)(2,1)S(1)} %get-tuple-element.108), channel_id=1, source_target_pairs={{0,16},{4,20},{8,24},{12,28},{16,0},{20,4},{24,8},{28,12},{1,17},{... | collective-permute-start | bytes 393224 | tf_op jit(solution)/shard_map/ppermute | solution.py:261
  27.0 15.7 %collective-permute-start.11 = (bf16[128,512]{1,0:T(8,128)(2,1)S(1)}, bf16[128,512]{1,0:T(8,128)(2,1)S(1)}, u32[]{:S(2)}, u32[]{:S(2)}) collective-permute-start(bf16[128,512]{1,0:T(8,128)(2,1)S(1)} %get-tuple-element.109), channel_id=1, source_target_pairs={{0,20},{4,16},{8,28},{12,24},{16,4},{20,0},{24,12},{28,8},{1,21},{... | collective-permute-start | bytes 393224 | tf_op jit(solution)/shard_map/ppermute | solution.py:261
  27.2 15.4 %collective-permute-start.12 = (bf16[128,512]{1,0:T(8,128)(2,1)S(1)}, bf16[128,512]{1,0:T(8,128)(2,1)S(1)}, u32[]{:S(2)}, u32[]{:S(2)}) collective-permute-start(bf16[128,512]{1,0:T(8,128)(2,1)S(1)} %get-tuple-element.110), channel_id=1, source_target_pairs={{0,24},{4,28},{8,16},{12,20},{16,8},{20,12},{24,0},{28,4},{1,25},{... | collective-permute-start | bytes 393224 | tf_op jit(solution)/shard_map/ppermute | solution.py:261
  30.0 12.7 %collective-permute-start.13 = (bf16[128,512]{1,0:T(8,128)(2,1)S(1)}, bf16[128,512]{1,0:T(8,128)(2,1)S(1)}, u32[]{:S(2)}, u32[]{:S(2)}) collective-permute-start(bf16[128,512]{1,0:T(8,128)(2,1)S(1)} %get-tuple-element.111), channel_id=1, source_target_pairs={{0,28},{4,24},{8,20},{12,16},{16,12},{20,8},{24,4},{28,0},{1,29},{... | collective-permute-start | bytes 393224 | tf_op jit(solution)/shard_map/ppermute | solution.py:261
  30.8 11.9 %copy-start.2 = (bf16[512,1536]{1,0:T(8,128)(2,1)S(1)}, bf16[512,1536]{1,0:T(8,128)(2,1)}, u32[]{:S(2)}) copy-start(bf16[512,1536]{1,0:T(8,128)(2,1)} %refs_0_.1) | copy-start | bytes 4718596
  30.8 11.9 %copy-start.3 = (bf16[512,512]{1,0:T(8,128)(2,1)S(1)}, bf16[512,512]{1,0:T(8,128)(2,1)}, u32[]{:S(2)}) copy-start(bf16[512,512]{1,0:T(8,128)(2,1)} %w_proj_ref.1) | copy-start | bytes 1572868
  39.4 3.3 %copy-start = (f32[8,512,512]{2,1,0:T(8,128)}, f32[8,512,512]{2,1,0:T(8,128)S(1)}, u32[]{:S(2)}) copy-start(f32[8,512,512]{2,1,0:T(8,128)S(1)} %get-tuple-element.99.probs_ref) | copy-start | bytes 25165828
  56.5 6.5 %collective-permute-start.14 = (f32[256,2176]{1,0:T(8,128)}, f32[256,2176]{1,0:T(8,128)}, u32[]{:S(2)}, u32[]{:S(2)}) collective-permute-start(f32[256,2176]{1,0:T(8,128)} %get-tuple-element.121), channel_id=1, source_target_pairs={{0,4},{4,0},{8,12},{12,8},{16,20},{20,16},{24,28},{28,24},{1,5},{5... | collective-permute-start | bytes 6684680 | tf_op jit(solution)/shard_map/ppermute | solution.py:283
  64.9 1.4 copy-start.8
  66.3 15.6 %collective-permute-start.15 = (f32[128,2176]{1,0:T(8,128)S(1)}, f32[128,2176]{1,0:T(8,128)S(1)}, u32[]{:S(2)}, u32[]{:S(2)}) collective-permute-start(f32[128,2176]{1,0:T(8,128)S(1)} %constant_dynamic-slice_fusion.4), channel_id=1, source_target_pairs={{0,8},{4,20},{8,0},{12,28},{16,24},{20,4},{24,16},{28,12},{1,9},{5... | collective-permute-start | bytes 3342344 | tf_op jit(solution)/shard_map/ppermute | solution.py:288
  83.4 9.6 %collective-permute-start.16 = (f32[64,2176]{1,0:T(8,128)S(1)}, f32[64,2176]{1,0:T(8,128)S(1)}, u32[]{:S(2)}, u32[]{:S(2)}) collective-permute-start(f32[64,2176]{1,0:T(8,128)S(1)} %constant_dynamic-slice_fusion.3), channel_id=1, source_target_pairs={{0,16},{4,12},{8,24},{12,4},{16,0},{20,28},{24,8},{28,20},{1,17},{... | collective-permute-start | bytes 1671176 | tf_op jit(solution)/shard_map/ppermute | solution.py:288
  93.1 8.5 %collective-permute-start.19 = (f32[16,2176]{1,0:T(8,128)S(1)}, f32[16,2176]{1,0:T(8,128)S(1)}, u32[]{:S(2)}, u32[]{:S(2)}) collective-permute-start(f32[16,2176]{1,0:T(8,128)S(1)} %get-tuple-element.141), channel_id=1, source_target_pairs={{0,3},{1,2},{2,1},{3,0},{4,7},{5,6},{6,5},{7,4},{8,11},{9,10},{10,... | collective-permute-start | bytes 417800 | tf_op jit(solution)/shard_map/ppermute | solution.py:261
  96.8 10.9 %collective-permute-start.18 = (f32[16,2176]{1,0:T(8,128)S(1)}, f32[16,2176]{1,0:T(8,128)S(1)}, u32[]{:S(2)}, u32[]{:S(2)}) collective-permute-start(f32[16,2176]{1,0:T(8,128)S(1)} %get-tuple-element.142), channel_id=1, source_target_pairs={{0,2},{1,3},{2,0},{3,1},{4,6},{5,7},{6,4},{7,5},{8,10},{9,11},{10,... | collective-permute-start | bytes 417800 | tf_op jit(solution)/shard_map/ppermute | solution.py:261
  96.8 10.9 %collective-permute-start.17 = (f32[16,2176]{1,0:T(8,128)S(1)}, f32[16,2176]{1,0:T(8,128)S(1)}, u32[]{:S(2)}, u32[]{:S(2)}) collective-permute-start(f32[16,2176]{1,0:T(8,128)S(1)} %get-tuple-element.140), channel_id=1, source_target_pairs={{0,1},{1,0},{2,3},{3,2},{4,5},{5,4},{6,7},{7,6},{8,9},{9,8},{10,11... | collective-permute-start | bytes 417800 | tf_op jit(solution)/shard_map/ppermute | solution.py:261
  107.7 6.4 %collective-permute-start.22 = (bf16[16,2176]{1,0:T(8,128)(2,1)S(1)}, bf16[16,2176]{1,0:T(8,128)(2,1)S(1)}, u32[]{:S(2)}, u32[]{:S(2)}) collective-permute-start(bf16[16,2176]{1,0:T(8,128)(2,1)S(1)} %add_convert_fusion), channel_id=1, source_target_pairs={{0,3},{1,2},{2,1},{3,0},{4,7},{5,6},{6,5},{7,4},{8,11},{9,10},{10,... | collective-permute-start | bytes 208904 | tf_op jit(solution)/shard_map/ppermute | solution.py:261
  110.1 5.4 %collective-permute-start.21 = (bf16[16,2176]{1,0:T(8,128)(2,1)S(1)}, bf16[16,2176]{1,0:T(8,128)(2,1)S(1)}, u32[]{:S(2)}, u32[]{:S(2)}) collective-permute-start(bf16[16,2176]{1,0:T(8,128)(2,1)S(1)} %add_convert_fusion), channel_id=1, source_target_pairs={{0,2},{1,3},{2,0},{3,1},{4,6},{5,7},{6,4},{7,5},{8,10},{9,11},{10,... | collective-permute-start | bytes 208904 | tf_op jit(solution)/shard_map/ppermute | solution.py:261
  110.1 6.0 %collective-permute-start.20 = (bf16[16,2176]{1,0:T(8,128)(2,1)S(1)}, bf16[16,2176]{1,0:T(8,128)(2,1)S(1)}, u32[]{:S(2)}, u32[]{:S(2)}) collective-permute-start(bf16[16,2176]{1,0:T(8,128)(2,1)S(1)} %add_convert_fusion), channel_id=1, source_target_pairs={{0,1},{1,0},{2,3},{3,2},{4,5},{5,4},{6,7},{7,6},{8,9},{9,8},{10,11... | collective-permute-start | bytes 208904 | tf_op jit(solution)/shard_map/ppermute | solution.py:261
  112.2 4.1 %collective-permute-start.23 = (bf16[128,512]{1,0:T(8,128)(2,1)S(1)}, bf16[128,512]{1,0:T(8,128)(2,1)S(1)}, u32[]{:S(2)}, u32[]{:S(2)}) collective-permute-start(bf16[128,512]{1,0:T(8,128)(2,1)S(1)} %get-tuple-element.124), channel_id=1, source_target_pairs={{0,4},{4,0},{8,12},{12,8},{16,20},{20,16},{24,28},{28,24},{1,5},{5... | collective-permute-start | bytes 393224 | tf_op jit(solution)/shard_map/ppermute | solution.py:261
  112.2 6.3 %collective-permute-start.24 = (bf16[128,512]{1,0:T(8,128)(2,1)S(1)}, bf16[128,512]{1,0:T(8,128)(2,1)S(1)}, u32[]{:S(2)}, u32[]{:S(2)}) collective-permute-start(bf16[128,512]{1,0:T(8,128)(2,1)S(1)} %get-tuple-element.125), channel_id=1, source_target_pairs={{0,8},{4,12},{8,0},{12,4},{16,24},{20,28},{24,16},{28,20},{1,9},{5... | collective-permute-start | bytes 393224 | tf_op jit(solution)/shard_map/ppermute | solution.py:261
  114.1 6.4 %collective-permute-start.25 = (bf16[128,512]{1,0:T(8,128)(2,1)S(1)}, bf16[128,512]{1,0:T(8,128)(2,1)S(1)}, u32[]{:S(2)}, u32[]{:S(2)}) collective-permute-start(bf16[128,512]{1,0:T(8,128)(2,1)S(1)} %get-tuple-element.126), channel_id=1, source_target_pairs={{0,12},{4,8},{8,4},{12,0},{16,28},{20,24},{24,20},{28,16},{1,13},{... | collective-permute-start | bytes 393224 | tf_op jit(solution)/shard_map/ppermute | solution.py:261
  115.5 12.0 %collective-permute-start.26 = (bf16[128,512]{1,0:T(8,128)(2,1)S(1)}, bf16[128,512]{1,0:T(8,128)(2,1)S(1)}, u32[]{:S(2)}, u32[]{:S(2)}) collective-permute-start(bf16[128,512]{1,0:T(8,128)(2,1)S(1)} %get-tuple-element.127), channel_id=1, source_target_pairs={{0,16},{4,20},{8,24},{12,28},{16,0},{20,4},{24,8},{28,12},{1,17},{... | collective-permute-start | bytes 393224 | tf_op jit(solution)/shard_map/ppermute | solution.py:261
  116.1 11.4 %collective-permute-start.27 = (bf16[128,512]{1,0:T(8,128)(2,1)S(1)}, bf16[128,512]{1,0:T(8,128)(2,1)S(1)}, u32[]{:S(2)}, u32[]{:S(2)}) collective-permute-start(bf16[128,512]{1,0:T(8,128)(2,1)S(1)} %get-tuple-element.128), channel_id=1, source_target_pairs={{0,20},{4,16},{8,28},{12,24},{16,4},{20,0},{24,12},{28,8},{1,21},{... | collective-permute-start | bytes 393224 | tf_op jit(solution)/shard_map/ppermute | solution.py:261
  116.2 11.3 %collective-permute-start.28 = (bf16[128,512]{1,0:T(8,128)(2,1)S(1)}, bf16[128,512]{1,0:T(8,128)(2,1)S(1)}, u32[]{:S(2)}, u32[]{:S(2)}) collective-permute-start(bf16[128,512]{1,0:T(8,128)(2,1)S(1)} %get-tuple-element.129), channel_id=1, source_target_pairs={{0,24},{4,28},{8,16},{12,20},{16,8},{20,12},{24,0},{28,4},{1,25},{... | collective-permute-start | bytes 393224 | tf_op jit(solution)/shard_map/ppermute | solution.py:261
  118.5 9.1 %collective-permute-start.29 = (bf16[128,512]{1,0:T(8,128)(2,1)S(1)}, bf16[128,512]{1,0:T(8,128)(2,1)S(1)}, u32[]{:S(2)}, u32[]{:S(2)}) collective-permute-start(bf16[128,512]{1,0:T(8,128)(2,1)S(1)} %get-tuple-element.130), channel_id=1, source_target_pairs={{0,28},{4,24},{8,20},{12,16},{16,12},{20,8},{24,4},{28,0},{1,29},{... | collective-permute-start | bytes 393224 | tf_op jit(solution)/shard_map/ppermute | solution.py:261
  127.5 6.6 %collective-permute-start.30 = (bf16[64,2176]{1,0:T(8,128)(2,1)S(1)}, bf16[64,2176]{1,0:T(8,128)(2,1)S(1)}, u32[]{:S(2)}, u32[]{:S(2)}) collective-permute-start(bf16[64,2176]{1,0:T(8,128)(2,1)S(1)} %pad_maximum_fusion.1), channel_id=1, source_target_pairs={{0,16},{4,12},{8,24},{12,4},{16,0},{20,28},{24,8},{28,20},{1,17},{... | collective-permute-start | bytes 835592 | tf_op jit(solution)/shard_map/ppermute | solution.py:308
  134.2 9.6 %collective-permute-start.31 = (bf16[128,2176]{1,0:T(8,128)(2,1)S(1)}, bf16[128,2176]{1,0:T(8,128)(2,1)S(1)}, u32[]{:S(2)}, u32[]{:S(2)}) collective-permute-start(bf16[128,2176]{1,0:T(8,128)(2,1)S(1)} %maximum_select_fusion.2), channel_id=1, source_target_pairs={{0,8},{4,20},{8,0},{12,28},{16,24},{20,4},{24,16},{28,12},{1,9},{5... | collective-permute-start | bytes 1671176 | tf_op jit(solution)/shard_map/ppermute | solution.py:308
  144.1 3.0 %collective-permute-start.32 = (bf16[256,2176]{1,0:T(8,128)(2,1)S(1)}, bf16[256,2176]{1,0:T(8,128)(2,1)}, u32[]{:S(2)}, u32[]{:S(2)}) collective-permute-start(bf16[256,2176]{1,0:T(8,128)(2,1)S(1)} %maximum_select_fusion.1), channel_id=1, source_target_pairs={{0,4},{4,0},{8,12},{12,8},{16,20},{20,16},{24,28},{28,24},{1,5},{5... | collective-permute-start | bytes 3342344 | tf_op jit(solution)/shard_map/ppermute | solution.py:308

commit v4 on v3

--- a/solution.py
+++ b/solution.py
@@ -37,9 +37,23 @@
     return jnp.concatenate([hot(column == lane + j * LANES) for j in range(count // LANES)], axis=1)
 
 
-def pack_kernel(n_seq, capacity, me_ref, dest_ref, feats_ref, grads_ref, slot_out, *outs):
+def by_receiver(me, distance, capacity):
+    return pl.ds(pl.multiple_of(lax.bitwise_xor(me, distance) * capacity, capacity), capacity)
+
+
+def pack_kernel(n_seq, capacity, me_ref, dest_hbm, feats_hbm, grads_hbm, slot_out, grads_out, *refs):
+    outs, (dest_ref, feats_ref, grads_ref, sems) = refs[:n_seq], refs[n_seq:]
     rows, width = feats_ref.shape
     slots = n_seq * capacity
+    loads = [
+        pltpu.make_async_copy(source, target, sems.at[i])
+        for i, (source, target) in enumerate(
+            ((dest_hbm, dest_ref), (feats_hbm, feats_ref), (grads_hbm, grads_ref))
+        )
+    ]
+    for load in loads:
+        load.start()
+    loads[0].wait()
     shift = rows.bit_length() - 1
     places = dest_ref[...]
     distance = lax.bitwise_xor(lax.shift_right_logical(places, shift), me_ref[0])
@@ -51,6 +65,7 @@
     slot = distance * capacity + rank
     slot_out[...] = slot
     select = hot(iota((slots, rows), 0) == slot)
+    loads[1].wait()
     feats = mm(select, feats_ref[...]).astype(BF16)
     upper_half = slot >= width
     high = lax.shift_right_logical(within, 8).astype(F32)
@@ -69,9 +84,10 @@
     for d in range(n_seq):
         outs[d][:capacity, :] = feats[d * capacity : (d + 1) * capacity]
         outs[d][capacity:, :] = position[d * EXTRA : (d + 1) * EXTRA]
+    loads[2].wait()
     grads = mm(select, grads_ref[...]).astype(BF16)
     for d in range(n_seq):
-        outs[n_seq + d][...] = grads[d * capacity : (d + 1) * capacity]
+        grads_out[by_receiver(me_ref[0], d, capacity), :] = grads[d * capacity : (d + 1) * capacity]
 
 
 def forward_kernel(n_seq, capacity, w_hbm, gain_ref, *refs):
@@ -138,34 +154,37 @@
             save.wait()
 
 
-def backward_kernel(n_seq, me_ref, pos_ref, w_proj_ref, gain_ref, qkv_ref, probs_ref, *refs):
-    (w_hbm, xhat_hbm, inv_hbm, normed_hbm, attn_hbm), refs = refs[:5], refs[5:]
-    recv, refs = refs[:n_seq], refs[n_seq:]
-    send_hbm, keep_hbm, refs = refs[0], refs[1], refs[2:]
-    back, refs = refs[:n_seq], refs[n_seq:]
-    w_ref, xhat_ref, inv_ref, normed_ref, attn_ref, send_ref, keep_ref, refs = *refs[:7], refs[7:]
-    serial_grad, d_attn, d_attn_t, keys_t, d_qkv, normed_t, gain_column, sems = refs
+def backward_kernel(n_seq, first_bits, me_ref, pos_ref, w_proj_ref, probs_ref, *refs):
+    (recv_hbm, qkv_hbm, w_hbm, xhat_hbm, normed_hbm, attn_hbm), refs = refs[:6], refs[6:]
+    outs, serial_grad_hbm, d_normed_hbm, refs = refs[:4], refs[4], refs[5], refs[6:]
+    recv_ref, qkv_ref, w_ref, xhat_ref, normed_ref, attn_ref, refs = *refs[:6], refs[6:]
+    sums, refs = refs[:4], refs[4:]
+    serial_grad, d_normed_ref, d_attn, d_attn_t, keys_t, d_qkv, normed_t, gain_column, sems = refs
     width = w_proj_ref.shape[0]
     rows = xhat_ref.shape[0]
-    capacity = recv[0].shape[0]
+    capacity = recv_ref.shape[0] // n_seq
     head = width // HEADS
     pair = 2 * head
     step = pl.program_id(0)
+    me = me_ref[0]
     loads = [
         pltpu.make_async_copy(source, target, sems.at[i])
         for i, (source, target) in enumerate(
             (
+                (recv_hbm, recv_ref),
+                (qkv_hbm, qkv_ref),
                 (normed_hbm, normed_ref),
                 (w_hbm, w_ref),
                 (xhat_hbm, xhat_ref),
-                (inv_hbm, inv_ref),
                 (attn_hbm, attn_ref),
             )
         )
     ]
     saves = [
-        pltpu.make_async_copy(send_ref, send_hbm, sems.at[5]),
-        pltpu.make_async_copy(keep_ref, keep_hbm, sems.at[6]),
+        pltpu.make_async_copy(source, target, sems.at[6 + i])
+        for i, (source, target) in enumerate(
+            [*zip(sums, outs), (serial_grad, serial_grad_hbm), (d_normed_ref, d_normed_hbm)]
+        )
     ]
 
     @pl.when(step == 0)
@@ -173,11 +192,17 @@
         for load in loads:
             load.start()
         place = hot(iota((rows, n_seq * capacity), 0) == pos_ref[...])
-        grads = mm(place, jnp.concatenate([ref[...] for ref in recv], axis=0)).astype(BF16)
+        loads[0].wait()
+        values = jnp.concatenate(
+            [recv_ref[by_receiver(me, d, capacity), :] for d in range(n_seq)], axis=0
+        )
+        grads = mm(place, values).astype(BF16)
         serial_grad[...] = grads
+        saves[4].start()
         d_att = mm(grads, w_proj_ref[...], NT).astype(BF16)
         d_attn[...] = d_att
         d_attn_t[...] = jnp.transpose(d_att.astype(F32)).astype(BF16)
+        loads[1].wait()
         keys_t[...] = jnp.transpose(qkv_ref[:, width : 2 * width].astype(F32)).astype(BF16)
 
     lo = pl.multiple_of(step * pair, pair)
@@ -209,38 +234,74 @@
 
     @pl.when(step == pl.num_programs(0) - 1)
     def _():
-        for load in loads:
+        for load in loads[2:]:
             load.wait()
         normed_t[...] = jnp.transpose(normed_ref[...].astype(F32)).astype(BF16)
         d_normed = mm(d_qkv[...], w_ref[...], NT)
-        xhat = xhat_ref[...]
-        gain_row = jnp.sum(d_normed * xhat, axis=0, keepdims=True)
+        d_normed_ref[...] = d_normed
+        saves[5].start()
+        gain_row = jnp.sum(d_normed * xhat_ref[...], axis=0, keepdims=True)
         gain_column[...] = jnp.transpose(jnp.broadcast_to(gain_row, (LANES, width)))
-        half = width // 2
-        bit = lax.bitwise_and(me_ref[0], 1)
-        for out, start, save in ((send_ref, (1 - bit) * half, saves[0]), (keep_ref, bit * half, saves[1])):
-            part = pl.ds(pl.multiple_of(start, half), half)
+        quarter = width // 4
+        odd = lax.bitwise_and(me, 1)
+        even_bit, odd_bit = first_bits
+        even_side = lax.bitwise_and(lax.shift_right_logical(me, even_bit), 1)
+        odd_side = lax.bitwise_and(lax.shift_right_logical(me, odd_bit), 1)
+        mine = jnp.where(odd == 1, odd_side, even_side)
+        other = jnp.where(odd == 1, even_side, odd_side)
+        starts = (
+            (1 - odd) * 2 + 1 - other,
+            (1 - odd) * 2 + other,
+            odd * 2 + 1 - mine,
+            odd * 2 + mine,
+        )
+        for out, start, save in zip(sums, starts, saves):
+            part = pl.ds(pl.multiple_of(start * quarter, quarter), quarter)
             out[:, : 3 * width] = mm(normed_t[part, :], d_qkv[...])
             out[:, 3 * width : 4 * width] = mm(attn_ref[part, :], serial_grad[...])
             out[:, 4 * width :] = gain_column[part, :]
             save.start()
-        scaled = d_normed * gain_ref[...]
-        residual = inv_ref[:, 0:1] * (
-            scaled
-            - jnp.mean(scaled, axis=1, keepdims=True)
-            - xhat * jnp.mean(scaled * xhat, axis=1, keepdims=True)
-        )
-        serial_dx = (serial_grad[...].astype(F32) + residual).astype(BF16)
-        returned = mm(column_hot(pos_ref[...], rows), serial_dx).astype(BF16)
-        for d in range(n_seq):
-            back[d][...] = returned[d * capacity : (d + 1) * capacity]
         for save in saves:
             save.wait()
 
 
-def unpack_kernel(slot_ref, *refs):
-    values = jnp.concatenate([ref[...] for ref in refs[:-1]], axis=0)
-    refs[-1][...] = mm(column_hot(slot_ref[...], values.shape[0]), values).astype(BF16)
+def residual_kernel(
+    n_seq, me_ref, pos_ref, gain_ref, inv_ref, xhat_ref, serial_grad_ref, d_normed_ref, back_out
+):
+    xhat = xhat_ref[...]
+    rows = xhat.shape[0]
+    capacity = pos_ref.shape[1] // n_seq
+    scaled = d_normed_ref[...] * gain_ref[...]
+    residual = inv_ref[:, 0:1] * (
+        scaled
+        - jnp.mean(scaled, axis=1, keepdims=True)
+        - xhat * jnp.mean(scaled * xhat, axis=1, keepdims=True)
+    )
+    serial_dx = (serial_grad_ref[...].astype(F32) + residual).astype(BF16)
+    returned = mm(column_hot(pos_ref[...], rows), serial_dx).astype(BF16)
+    for d in range(n_seq):
+        back_out[by_receiver(me_ref[0], d, capacity), :] = returned[d * capacity : (d + 1) * capacity]
+
+
+def unpack_kernel(n_seq, me_ref, slot_ref, recv_ref, out_ref):
+    capacity = recv_ref.shape[0] // n_seq
+    values = jnp.concatenate(
+        [recv_ref[by_receiver(me_ref[0], d, capacity), :] for d in range(n_seq)], axis=0
+    )
+    out_ref[...] = mm(column_hot(slot_ref[...], values.shape[0]), values).astype(BF16)
+
+
+def split_kernel(side_ref, own_ref, other_ref, qkv_out, proj_out, gain_out):
+    width = proj_out.shape[1]
+
+    def write(ref):
+        qkv_out[...] = ref[:, : 3 * width].astype(F32)
+        proj_out[...] = ref[:, 3 * width : 4 * width].astype(F32)
+        gain_out[...] = jnp.transpose(ref[:, 4 * width :].astype(F32))[0:1]
+
+    own = pl.program_id(0) == side_ref[0]
+    pl.when(own)(lambda: write(own_ref))
+    pl.when(jnp.logical_not(own))(lambda: write(other_ref))
 
 
 def whole(shape):
@@ -262,41 +323,55 @@
     ]
 
 
+def chip_orders(n_seq):
+    bits = list(range(1, n_seq.bit_length() - 1))
+    middle = len(bits) // 2
+    return bits, bits[middle:] + bits[:middle]
+
+
 def chip_steps():
     n_seq, me = lax.axis_size("seq"), lax.axis_index("seq")
-    bits = list(range(1, n_seq.bit_length() - 1))
-    middle = len(bits) // 2
-    orders = (bits, bits[middle:] + bits[:middle])
     odd = lax.bitwise_and(me, 1) == 1
 
     def side(bit):
         return lax.bitwise_and(lax.shift_right_logical(me, jnp.asarray(bit, me.dtype)), 1)
 
-    steps = [([(i, i ^ 1) for i in range(n_seq)], side(0))]
-    for even_bit, odd_bit in zip(*orders):
+    steps = []
+    for even_bit, odd_bit in zip(*chip_orders(n_seq)):
         pairs = [(i, i ^ (1 << (odd_bit if i & 1 else even_bit))) for i in range(n_seq)]
         steps.append((pairs, jnp.where(odd, side(odd_bit), side(even_bit))))
     return steps
 
 
-def reduce_in_plane(send, keep, steps):
-    part = keep + lax.ppermute(send, "seq", steps[0][0])
+def piece(terms, index, count):
+    size = terms[0].shape[0] // count
+    return functools.reduce(jnp.add, [lax.dynamic_slice_in_dim(t, index * size, size) for t in terms])
+
+
+def core_pairs():
+    return [(i, i ^ 1) for i in range(lax.axis_size("seq"))]
+
+
+def reduce_in_plane(quarters, steps):
+    pass_on, pass_keep, own_on, own_keep = quarters
+    send = own_on + lax.ppermute(pass_on, "seq", core_pairs())
+    keep = own_keep + lax.ppermute(pass_keep, "seq", core_pairs())
+    terms = [keep, lax.ppermute(send, "seq", steps[0][0])]
     for pairs, side in steps[1:]:
-        half = part.shape[0] // 2
-        send = lax.dynamic_slice_in_dim(part, (1 - side) * half, half)
-        keep = lax.dynamic_slice_in_dim(part, side * half, half)
-        part = keep + lax.ppermute(send, "seq", pairs)
-    return part
-
-
-def sum_over_planes(part):
+        got = lax.ppermute(piece(terms, 1 - side, 2), "seq", pairs)
+        terms = [piece(terms, side, 2), got]
+    return terms
+
+
+def reduce_over_planes(terms):
     n_dp, plane = lax.axis_size("dp"), lax.axis_index("dp")
-    size = part.shape[0] // n_dp
-    pieces = [
-        lax.dynamic_slice_in_dim(part, lax.bitwise_xor(plane, k) * size, size) for k in range(n_dp)
-    ]
-    total = functools.reduce(jnp.add, by_distance(pieces, "dp")).astype(BF16)
-    shares = jnp.stack(by_distance([total] * n_dp, "dp"))
+    pieces = [piece(terms, lax.bitwise_xor(plane, k), n_dp) for k in range(n_dp)]
+    return functools.reduce(jnp.add, by_distance(pieces, "dp")).astype(BF16)
+
+
+def share_over_planes(part):
+    n_dp, plane = lax.axis_size("dp"), lax.axis_index("dp")
+    shares = jnp.stack(by_distance([part] * n_dp, "dp"))
     return jnp.concatenate(
         [lax.dynamic_index_in_dim(shares, lax.bitwise_xor(plane, p), keepdims=False) for p in range(n_dp)],
         axis=0,
@@ -322,29 +397,41 @@
     block = capacity + EXTRA
     pairs = HEADS // 2
     pair = width // pairs
-    sum_shape = (width // 2, 4 * width + LANES)
+    sum_shape = (width // 4, 4 * width + LANES)
     me = jnp.reshape(lax.axis_index("seq").astype(jnp.int32), (1,))
     gain_row = gain.reshape(1, width)
     in_smem = pl.BlockSpec(memory_space=pltpu.SMEM)
     in_vmem = pl.BlockSpec(memory_space=pltpu.VMEM)
     in_hbm = pl.BlockSpec(memory_space=pl.ANY)
-
-    slot, *packed = pl.pallas_call(
+    stay_hbm = pl.BlockSpec(memory_space=pltpu.HBM)
+
+    slot, grads_sent, *feats_sent = pl.pallas_call(
         functools.partial(pack_kernel, n_seq, capacity),
-        out_shape=[shape_of((1, rows), jnp.int32)]
-        + [shape_of((block, width), BF16)] * n_seq
-        + [shape_of((capacity, width), BF16)] * n_seq,
-        in_specs=[in_smem, in_vmem, in_vmem, in_vmem],
-        out_specs=[in_vmem] * (1 + 2 * n_seq),
-        compiler_params=params(20),
+        out_shape=[shape_of((1, rows), jnp.int32), shape_of((slots, width), BF16)]
+        + [shape_of((block, width), BF16)] * n_seq,
+        in_specs=[in_smem] + [stay_hbm] * 3,
+        out_specs=[in_vmem] * (2 + n_seq),
+        scratch_shapes=[
+            pltpu.VMEM((1, rows), jnp.int32),
+            pltpu.VMEM((rows, width), BF16),
+            pltpu.VMEM((rows, width), BF16),
+            pltpu.SemaphoreType.DMA((3,)),
+        ],
+        compiler_params=params(60),
         cost_estimate=pl.CostEstimate(
             flops=4 * slots * rows * width, bytes_accessed=4 * MIB, transcendentals=0
         ),
         name="pack",
     )(me, dest, feats, grads)
-    feats_got = by_distance(packed[:n_seq], "seq")
-    feats_got, grads_sent = lax.optimization_barrier((feats_got, packed[n_seq:]))
-    grads_got = by_distance(grads_sent, "seq")
+
+    def exchange(sent):
+        sent = sent.reshape(n_seq, capacity, width)
+        got = lax.all_to_all(sent, "seq", split_axis=0, concat_axis=0, tiled=True)
+        return got.reshape(slots, width)
+
+    feats_got = by_distance(feats_sent, "seq")
+    feats_got, grads_sent = lax.optimization_barrier((feats_got, grads_sent))
+    grads_got = exchange(grads_sent)
 
     pos, xhat, inv, normed, qkv, attn_t, probs = pl.pallas_call(
         functools.partial(forward_kernel, n_seq, capacity),
@@ -374,7 +461,7 @@
             pltpu.VMEM((3 * width, rows), BF16),
             pltpu.SemaphoreType.DMA((5,)),
         ],
-        compiler_params=params(26),
+        compiler_params=params(24),
         cost_estimate=pl.CostEstimate(
             flops=6 * rows * width * width + 8 * HEADS * rows * rows * pair,
             bytes_accessed=16 * MIB,
@@ -383,65 +470,99 @@
         name="forward",
     )(w_qkv, gain_row, *feats_got)
 
-    send, keep, *back = pl.pallas_call(
-        functools.partial(backward_kernel, n_seq),
+    first_bits = tuple(order[0] for order in chip_orders(n_seq))
+    *quarters, serial_grad, d_normed = pl.pallas_call(
+        functools.partial(backward_kernel, n_seq, first_bits),
         grid=(pairs,),
-        out_shape=[shape_of(sum_shape, F32)] * 2 + [shape_of((capacity, width), BF16)] * n_seq,
+        out_shape=[shape_of(sum_shape, F32)] * 4
+        + [shape_of((rows, width), BF16), shape_of((rows, width), F32)],
         in_specs=[
             in_smem,
             whole((1, slots)),
             whole((width, width)),
-            whole((1, width)),
-            whole((rows, 3 * width)),
             pl.BlockSpec((2, rows, rows), lambda i: (i, 0, 0)),
         ]
-        + [in_hbm] * 5
-        + [whole((capacity, width))] * n_seq,
-        out_specs=[in_hbm] * 2 + [whole((capacity, width))] * n_seq,
+        + [in_hbm] * 6,
+        out_specs=[in_hbm] * 6,
         scratch_shapes=[
+            pltpu.VMEM((slots, width), BF16),
+            pltpu.VMEM((rows, 3 * width), BF16),
             pltpu.VMEM((width, 3 * width), BF16),
             pltpu.VMEM((rows, width), F32),
-            pltpu.VMEM((rows, LANES), F32),
             pltpu.VMEM((rows, width), BF16),
             pltpu.VMEM((width, rows), BF16),
-            pltpu.VMEM(sum_shape, F32),
-            pltpu.VMEM(sum_shape, F32),
+        ]
+        + [pltpu.VMEM(sum_shape, F32)] * 4
+        + [
             pltpu.VMEM((rows, width), BF16),
+            pltpu.VMEM((rows, width), F32),
             pltpu.VMEM((rows, width), BF16),
             pltpu.VMEM((width, rows), BF16),
             pltpu.VMEM((width, rows), BF16),
             pltpu.VMEM((rows, 3 * width), BF16),
             pltpu.VMEM((width, rows), BF16),
             pltpu.VMEM((width, LANES), F32),
-            pltpu.SemaphoreType.DMA((7,)),
+            pltpu.SemaphoreType.DMA((12,)),
         ],
-        compiler_params=params(34),
+        compiler_params=params(32),
         cost_estimate=pl.CostEstimate(
-            flops=14 * rows * width * width + 8 * HEADS * rows * rows * pair,
+            flops=12 * rows * width * width + 8 * HEADS * rows * rows * pair,
             bytes_accessed=24 * MIB,
             transcendentals=0,
         ),
         name="backward",
-    )(me, pos, w_proj, gain_row, qkv, probs, w_qkv, xhat, inv, normed, attn_t, *grads_got)
+    )(me, pos, w_proj, probs, grads_got, qkv, w_qkv, xhat, normed, attn_t)
+
+    back = pl.pallas_call(
+        functools.partial(residual_kernel, n_seq),
+        out_shape=shape_of((slots, width), BF16),
+        in_specs=[in_smem] + [in_vmem] * 6,
+        out_specs=in_vmem,
+        compiler_params=params(20),
+        cost_estimate=pl.CostEstimate(
+            flops=2 * slots * rows * width, bytes_accessed=4 * MIB, transcendentals=0
+        ),
+        name="residual",
+    )(me, pos, gain_row, inv, xhat, serial_grad, d_normed)
 
     steps = chip_steps()
-    part = reduce_in_plane(send, keep, steps)
-    back, part = lax.optimization_barrier((back, part))
-    returned = by_distance(back, "seq")
-    part, returned = lax.optimization_barrier((sum_over_planes(part), returned))
-    total = share_in_plane(part, steps).astype(F32)
+    terms = reduce_in_plane(quarters, steps)
+    back, terms = lax.optimization_barrier((back, terms))
+    returned = exchange(back)
+    part, returned = lax.optimization_barrier((reduce_over_planes(terms), returned))
+    own = share_in_plane(share_over_planes(part), steps)
+    other = lax.ppermute(own, "seq", core_pairs())
     grad_local = pl.pallas_call(
-        unpack_kernel,
+        functools.partial(unpack_kernel, n_seq),
         out_shape=shape_of((rows, width), BF16),
-        in_specs=[in_vmem] * (1 + n_seq),
+        in_specs=[in_smem] + [in_vmem] * 2,
         out_specs=in_vmem,
         compiler_params=params(20),
         cost_estimate=pl.CostEstimate(
             flops=2 * slots * rows * width, bytes_accessed=2 * MIB, transcendentals=0
         ),
         name="unpack",
-    )(slot, *returned)
-    return (grad_local[None], total[:, : 3 * width], total[:, 3 * width : 4 * width], total[:, 4 * width])
+    )(me, slot, returned)
+    half = width // 2
+    grad_qkv, grad_proj, gain_grad = pl.pallas_call(
+        split_kernel,
+        grid=(2,),
+        out_shape=(
+            shape_of((width, 3 * width), F32),
+            shape_of((width, width), F32),
+            shape_of((1, width), F32),
+        ),
+        in_specs=[in_smem] + [whole(own.shape)] * 2,
+        out_specs=[
+            pl.BlockSpec((half, 3 * width), lambda i: (i, 0)),
+            pl.BlockSpec((half, width), lambda i: (i, 0)),
+            pl.BlockSpec((1, half), lambda i: (0, i)),
+        ],
+        compiler_params=params(20),
+        cost_estimate=pl.CostEstimate(flops=0, bytes_accessed=8 * MIB, transcendentals=0),
+        name="split",
+    )(lax.bitwise_and(me, 1), own, other)
+    return (grad_local[None], grad_qkv, grad_proj, gain_grad[0])
 
 
 def solution(mesh):

time: 153 us -> 151 us (0.987)
  waiting for transfers between devices: 72.6 us -> 62.1 us
  local copies, waits for them, and re-layouts: 11.6 us -> 17.9 us
  Pallas kernels: 25.5 us -> 30.6 us
  starting transfers between devices: 36.5 us -> 31.8 us
    ppermute x27 -> x13, starting transfers between devices: 30 us -> 18.2 us  [by_distance(): lax.ppermute(blocks[k], axis, [(i, i ^ k) for i in range(count)])]
    unnamed x18 -> x44, local copies, waits for them, and re-layouts: 7.52 us -> 17.9 us
    all_to_all x0 -> x2, starting transfers between devices: none -> 7.61 us  [exchange(): got = lax.all_to_all(sent, 'seq', split_axis=0, concat_axis=0, tiled=True)]
    ppermute x27 -> x13, waiting for transfers between devices: 29.9 us -> 24.7 us  [by_distance(): lax.ppermute(blocks[k], axis, [(i, i ^ k) for i in range(count)])]
    ppermute x3 -> x5, waiting for transfers between devices: 28.3 us -> 24 us  [the longest x1 13.2 us: reduce_in_plane(): terms = [keep, lax.ppermute(send, 'seq', steps[0][0])]]
    slice x3 -> x0, local copies, waits for them, and re-layouts: 3.92 us -> none  [the longest x1 2.09 us: per_device(): total[:, :3 * width]]
    pallas_call x2 -> x4, Pallas kernels: 15.4 us -> 18.4 us  [the longest x1 12.6 us: per_device(): pl.pallas_call(functools.partial(backward_kernel, n_seq, first_bits), gri...]
    add x3 -> x4, other arithmetic: 3.42 us -> 5.82 us  [the longest x2 3.29 us: piece(): functools.reduce(jnp.add, [lax.dynamic_slice_in_dim(t, index * size, size...]
  transfers between devices with their start and end apart: 33 -> 22, of which waited for: 17 -> 13; matrix products, arithmetic and copies ran while one was open for 0% -> 3% of each run, Pallas kernels for 7% -> 8%
where the time goes in v4:
time: 151 us; the launch traced here: 150 us
  waiting for transfers between devices  62.1 us (41%)
  starting transfers between devices  31.8 us (21%)
  Pallas kernels  30.6 us (20%)
  local copies, waits for them, and re-layouts  17.9 us (12%)
  other arithmetic  7.13 us (5%)
    ppermute x13, waiting for transfers between devices, by_distance(): lax.ppermute(blocks[k], axis, [(i, i ^ k) for i in range(count)])  24.7 us
    ppermute x13, starting transfers between devices, by_distance(): lax.ppermute(blocks[k], axis, [(i, i ^ k) for i in range(count)])  18.2 us
    unnamed x44, local copies, waits for them, and re-layouts  17.9 us
    ppermute x2, waiting for transfers between devices, share_in_plane(): other = lax.ppermute(part, 'seq', pairs)  13.4 us
    ppermute x1, waiting for transfers between devices, reduce_in_plane(): terms = [keep, lax.ppermute(send, 'seq', steps[0][0])]  13.2 us
    pallas_call x1, Pallas kernels, per_device(): pl.pallas_call(functools.partial(backward_kernel, n_seq, first_bits), gri...  12.6 us
    pallas_call x1, Pallas kernels, per_device(): pl.pallas_call(functools.partial(forward_kernel, n_seq, capacity), grid=(...  8.3 us
    all_to_all x2, starting transfers between devices, exchange(): got = lax.all_to_all(sent, 'seq', split_axis=0, concat_axis=0, tiled=True)  7.61 us
  transfers between devices with their start and end apart: 22, of which 13 were waited for; matrix products, arithmetic and copies ran while one was open for 3% of the time, Pallas kernels for 8%

profile of v4, /device:TPU:0, one launch (start us, length us, event | category | flops | bytes accessed | tf_op | source)
XLA Modules:
  0.0 150.3 jit_solution(2271186560604631529)
XLA Ops:
  0.6 3.9 %pack.1 = (s32[1,512]{1,0:T(1,128)}, bf16[1024,512]{1,0:T(8,128)(2,1)}, bf16[144,512]{1,0:T(8,128)(2,1)}, bf16[144,512]{1,0:T(8,128)(2,1)}, bf16[144,512]{1,0:T(...) custom-call(s32[1]{0:T(128)} %bitcast.me_ref, ...), custom_call_target="tpu_custom_call" | custom-call | flops 1073741824 | bytes 4194304 | tf_op jit(solution)/shard_map/pack/pallas_call | solution.py:408
  5.0 2.6 %collective-permute-start.1 = (bf16[144,512]{1,0:T(8,128)(2,1)}, bf16[144,512]{1,0:T(8,128)(2,1)S(1)}, u32[]{:S(2)}, u32[]{:S(2)}) collective-permute-start(bf16[144,512]{1,0:T(8,128)(2,1)} %get-tuple-element.47), channel_id=1, source_target_pairs={{0,8},{4,12},{8,0},{12,4},{16,24},{20,28},{24,16},{28,20},{1,9},{5... | collective-permute-start | bytes 442376 | tf_op jit(solution)/shard_map/ppermute | solution.py:322
  7.7 1.8 %collective-permute-start.3 = (bf16[144,512]{1,0:T(8,128)(2,1)}, bf16[144,512]{1,0:T(8,128)(2,1)S(1)}, u32[]{:S(2)}, u32[]{:S(2)}) collective-permute-start(bf16[144,512]{1,0:T(8,128)(2,1)} %get-tuple-element.49), channel_id=1, source_target_pairs={{0,16},{4,20},{8,24},{12,28},{16,0},{20,4},{24,8},{28,12},{1,17},{... | collective-permute-start | bytes 442376 | tf_op jit(solution)/shard_map/ppermute | solution.py:322
  9.4 2.6 %collective-permute-start.5 = (bf16[144,512]{1,0:T(8,128)(2,1)}, bf16[144,512]{1,0:T(8,128)(2,1)S(1)}, u32[]{:S(2)}, u32[]{:S(2)}) collective-permute-start(bf16[144,512]{1,0:T(8,128)(2,1)} %get-tuple-element.51), channel_id=1, source_target_pairs={{0,24},{4,28},{8,16},{12,20},{16,8},{20,12},{24,0},{28,4},{1,25},{... | collective-permute-start | bytes 442376 | tf_op jit(solution)/shard_map/ppermute | solution.py:322
  12.5 1.7 %collective-permute-start.6 = (bf16[144,512]{1,0:T(8,128)(2,1)}, bf16[144,512]{1,0:T(8,128)(2,1)S(1)}, u32[]{:S(2)}, u32[]{:S(2)}) collective-permute-start(bf16[144,512]{1,0:T(8,128)(2,1)} %get-tuple-element.52), channel_id=1, source_target_pairs={{0,28},{4,24},{8,20},{12,16},{16,12},{20,8},{24,4},{28,0},{1,29},{... | collective-permute-start | bytes 442376 | tf_op jit(solution)/shard_map/ppermute | solution.py:322
  14.2 1.0 collective-permute-done.2.refs_3_
  15.2 7.6 %collective-permute-done.4.refs_5_ = bf16[144,512]{1,0:T(8,128)(2,1)S(1)} collective-permute-done((bf16[144,512]{1,0:T(8,128)(2,1)}, bf16[144,512]{1,0:T(8,128)(2,1)S(1)}, u32[]{:S(2)}, u32[]{:S(2)}) %collective-permute-start.4) | collective-permute-done | bytes 147488 | tf_op jit(solution)/shard_map/ppermute | solution.py:322
  22.8 4.0 %all-to-all-start = ((bf16[8,128,512]{2,1,0:T(8,128)(2,1)}), bf16[8,128,512]{2,1,0:T(8,128)(2,1)S(1)}, u32[]{:S(2)}, u32[]{:S(2)}) async-start(bf16[8,128,512]{2,1,0:T(8,128)(2,1)} %bitcast.30), calls=%async_computation | async-start | bytes 2097152 | tf_op jit(solution)/shard_map/all_to_all | solution.py:429
  26.9 1.4 copy-done.2
  28.3 0.9 copy-done.16
  29.2 8.3 %forward.1 = (s32[1,1024]{1,0:T(1,128)S(1)}, f32[512,512]{1,0:T(8,128)S(1)}, f32[512,128]{1,0:T(8,128)S(1)}, bf16[512,512]{1,0:T(8,128)(2,1)S(1)}, bf16[512,1536...) custom-call(bf16[512,1536]{1,0:T(8,128)(2,1)S(1)} %copy-done.2, f32[1,512]{1,0:T(1,128)S(1)} %bitcast.28, ...), custom_call_target="tpu_custom_call" | custom-call | flops 2952790016 | bytes 16777216 | tf_op jit(solution)/shard_map/forward/pallas_call | solution.py:436
  37.5 3.3 %copy-done = f32[8,512,512]{2,1,0:T(8,128)} copy-done((f32[8,512,512]{2,1,0:T(8,128)}, f32[8,512,512]{2,1,0:T(8,128)S(1)}, u32[]{:S(2)}) %copy-start) | copy-done | bytes 8388632
  40.8 1.1 copy-done.4
  42.0 0.8 copy-done.11
  42.8 0.8 copy-done.13
  43.6 3.4 %copy-done.1 = f32[8,512,512]{2,1,0:T(8,128)S(1)} copy-done((f32[8,512,512]{2,1,0:T(8,128)S(1)}, f32[8,512,512]{2,1,0:T(8,128)}, u32[]{:S(2)}) %copy-start.1) | copy-done | bytes 8388632
  47.0 1.4 copy-done.3
  48.4 1.4 copy-done.5
  49.8 1.0 copy-done.8
  50.8 1.0 copy-done.12
  51.9 1.0 copy-done.14
  52.9 12.6 %backward.1 = (f32[128,2176]{1,0:T(8,128)S(1)}, f32[128,2176]{1,0:T(8,128)}, f32[128,2176]{1,0:T(8,128)S(1)}, f32[128,2176]{1,0:T(8,128)S(1)}, bf16[512,512]{1,0:T(8,128)(2,1)S(1)}, /*index=5*/f32[512,512]{1,0:T(8,128)S(1)}) custom-call(s32[1]{0:T(128)} %bitcast.me_ref, s32[1,1024]{1,0:T(1,128)S(1)} %get-tuple-element.62.pos_ref, ...), custom_call_target="tpu_custom_call" | custom-call | flops 3758096384 | bytes 25165824 | tf_op jit(solution)/shard_map/backward/pallas_call | solution.py:474
  66.2 3.1 %collective-permute-done.8 = f32[128,2176]{1,0:T(8,128)S(1)} collective-permute-done((f32[128,2176]{1,0:T(8,128)S(1)}, f32[128,2176]{1,0:T(8,128)S(1)}, u32[]{:S(2)}, u32[]{:S(2)}) %collective-permute-start.8) | collective-permute-done | bytes 1114144 | tf_op jit(solution)/shard_map/ppermute | solution.py:357
  69.3 1.1 add.72
  70.4 1.2 collective-permute-start.9
  71.6 1.4 add.70
  73.0 13.2 %collective-permute-done.9 = f32[128,2176]{1,0:T(8,128)} collective-permute-done((f32[128,2176]{1,0:T(8,128)}, f32[128,2176]{1,0:T(8,128)}, u32[]{:S(2)}, u32[]{:S(2)}) %collective-permute-start.9) | collective-permute-done | bytes 1114144 | tf_op jit(solution)/shard_map/ppermute | solution.py:359
  86.3 2.2 %dynamic-slice_add_fusion = (f32[64,2176]{1,0:T(8,128)}, f32[64,2176]{1,0:T(8,128)S(1)}) fusion(f32[128,2176]{1,0:T(8,128)} %collective-permute-done.9, s32[]{:T(128)S(6)} %select_n.62, f32[128,2176]{1,0:T(8,128)S(1)} %add.70, s32[]{:T(128)S(6)} %select_n.61), kind=kLoop, calls=%fused_computation.1 | loop fusion | flops 278528 | bytes 3342344 | tf_op jit(solution)/shard_map/add | solution.py:348
  88.4 1.3 collective-permute-start.10
  89.7 2.1 %residual.1 = bf16[1024,512]{1,0:T(8,128)(2,1)} custom-call(s32[1]{0:T(128)} %bitcast.me_ref, s32[1,1024]{1,0:T(1,128)S(1)} %get-tuple-element.62.pos_ref, f32[1,512]{1,0:T(1,128)S(1)} %bitcast.29, f32[512,128]{1,0:T(8,128)S(1)} %get-tuple-element.63.inv_ref, f32[512,512]{1,0:T(8,128)S(1)} %get-tuple-element.64.refs_3_.xhat_ref, ...), custom_call_target="tpu_custom_call" | custom-call | flops 536870912 | bytes 4194304 | tf_op jit(solution)/shard_map/residual/pallas_call | solution.py:516
  91.8 6.5 %collective-permute-done.10 = f32[64,2176]{1,0:T(8,128)} collective-permute-done((f32[64,2176]{1,0:T(8,128)}, f32[64,2176]{1,0:T(8,128)}, u32[]{:S(2)}, u32[]{:S(2)}) %collective-permute-start.10) | collective-permute-done | bytes 557088 | tf_op jit(solution)/shard_map/ppermute | solution.py:361
  98.3 3.6 %all-to-all-start.1 = ((bf16[8,128,512]{2,1,0:T(8,128)(2,1)}), bf16[8,128,512]{2,1,0:T(8,128)(2,1)S(1)}, u32[]{:S(2)}, u32[]{:S(2)}) async-start(bf16[8,128,512]{2,1,0:T(8,128)(2,1)} %bitcast.6), calls=%async_computation.1 | async-start | bytes 2097152 | tf_op jit(solution)/shard_map/all_to_all | solution.py:429
  101.9 1.1 dynamic-slice_add_fusion.4
  103.0 3.7 %collective-permute-start.13 = (f32[16,2176]{1,0:T(8,128)S(1)}, f32[16,2176]{1,0:T(8,128)S(1)}, u32[]{:S(2)}, u32[]{:S(2)}) collective-permute-start(f32[16,2176]{1,0:T(8,128)S(1)} %get-tuple-element.95), channel_id=1, source_target_pairs={{0,3},{1,2},{2,1},{3,0},{4,7},{5,6},{6,5},{7,4},{8,11},{9,10},{10,... | collective-permute-start | bytes 417800 | tf_op jit(solution)/shard_map/ppermute | solution.py:322
  107.4 4.0 %collective-permute-done.13 = f32[16,2176]{1,0:T(8,128)S(1)} collective-permute-done((f32[16,2176]{1,0:T(8,128)S(1)}, f32[16,2176]{1,0:T(8,128)S(1)}, u32[]{:S(2)}, u32[]{:S(2)}) %collective-permute-start.13) | collective-permute-done | bytes 139296 | tf_op jit(solution)/shard_map/ppermute | solution.py:322
  111.4 7.6 %collective-permute-done.12 = f32[16,2176]{1,0:T(8,128)S(1)} collective-permute-done((f32[16,2176]{1,0:T(8,128)S(1)}, f32[16,2176]{1,0:T(8,128)S(1)}, u32[]{:S(2)}, u32[]{:S(2)}) %collective-permute-start.12) | collective-permute-done | bytes 139296 | tf_op jit(solution)/shard_map/ppermute | solution.py:322
  119.0 1.0 add_convert_fusion
  120.0 2.5 %collective-permute-start.16 = (bf16[16,2176]{1,0:T(8,128)(2,1)S(1)}, bf16[16,2176]{1,0:T(8,128)(2,1)S(1)}, u32[]{:S(2)}, u32[]{:S(2)}) collective-permute-start(bf16[16,2176]{1,0:T(8,128)(2,1)S(1)} %add_convert_fusion), channel_id=1, source_target_pairs={{0,3},{1,2},{2,1},{3,0},{4,7},{5,6},{6,5},{7,4},{8,11},{9,10},{10,... | collective-permute-start | bytes 208904 | tf_op jit(solution)/shard_map/ppermute | solution.py:322
  122.5 1.9 %collective-permute-start.14 = (bf16[16,2176]{1,0:T(8,128)(2,1)S(1)}, bf16[16,2176]{1,0:T(8,128)(2,1)S(1)}, u32[]{:S(2)}, u32[]{:S(2)}) collective-permute-start(bf16[16,2176]{1,0:T(8,128)(2,1)S(1)} %add_convert_fusion), channel_id=1, source_target_pairs={{0,1},{1,0},{2,3},{3,2},{4,5},{5,4},{6,7},{7,6},{8,9},{9,8},{10,11... | collective-permute-start | bytes 208904 | tf_op jit(solution)/shard_map/ppermute | solution.py:322
  124.4 2.0 %collective-permute-done.16 = bf16[16,2176]{1,0:T(8,128)(2,1)S(1)} collective-permute-done((bf16[16,2176]{1,0:T(8,128)(2,1)S(1)}, bf16[16,2176]{1,0:T(8,128)(2,1)S(1)}, u32[]{:S(2)}, u32[]{:S(2)}) %collective-permute-start.16) | collective-permute-done | bytes 69664 | tf_op jit(solution)/shard_map/ppermute | solution.py:322
  126.4 2.1 %collective-permute-done.15 = bf16[16,2176]{1,0:T(8,128)(2,1)S(1)} collective-permute-done((bf16[16,2176]{1,0:T(8,128)(2,1)S(1)}, bf16[16,2176]{1,0:T(8,128)(2,1)S(1)}, u32[]{:S(2)}, u32[]{:S(2)}) %collective-permute-start.15) | collective-permute-done | bytes 69664 | tf_op jit(solution)/shard_map/ppermute | solution.py:322
  128.7 1.4 collective-permute-start.17
  130.1 5.2 %collective-permute-done.17 = bf16[64,2176]{1,0:T(8,128)(2,1)S(1)} collective-permute-done((bf16[64,2176]{1,0:T(8,128)(2,1)S(1)}, bf16[64,2176]{1,0:T(8,128)(2,1)S(1)}, u32[]{:S(2)}, u32[]{:S(2)}) %collective-permute-start.17) | collective-permute-done | bytes 278560 | tf_op jit(solution)/shard_map/ppermute | solution.py:383
  135.5 1.4 collective-permute-start.18
  136.9 8.2 %collective-permute-done.18 = bf16[128,2176]{1,0:T(8,128)(2,1)S(1)} collective-permute-done((bf16[128,2176]{1,0:T(8,128)(2,1)S(1)}, bf16[128,2176]{1,0:T(8,128)(2,1)S(1)}, u32[]{:S(2)}, u32[]{:S(2)}) %collective-permute-start.18) | collective-permute-done | bytes 557088 | tf_op jit(solution)/shard_map/ppermute | solution.py:383
  145.4 1.5 %unpack.1 = bf16[512,512]{1,0:T(8,128)(2,1)} custom-call(s32[1]{0:T(128)} %bitcast.me_ref, s32[1,512]{1,0:T(1,128)S(1)} %copy-done.17, bf16[1024,512]{1,0:T(8,128)(2,1)S(1)} %bitcast.27), custom_call_target="tpu_custom_call" | custom-call | flops 536870912 | bytes 2097152 | tf_op jit(solution)/shard_map/unpack/pallas_call | solution.py:535
  147.0 1.2 collective-permute-done.19.other_ref
  148.2 2.2 %split.1 = (f32[512,1536]{1,0:T(8,128)}, f32[512,512]{1,0:T(8,128)}, f32[1,512]{1,0:T(1,128)}) custom-call(s32[1]{0:T(128)S(6)} %and.19.side_ref, bf16[256,2176]{1,0:T(8,128)(2,1)S(1)} %maximum_select_fusion.own_ref, bf16[256,2176]{1,0:T(8,128)(2,1)S(1)} %collective-permute-done.19.other_ref), custom_call_target="tpu_custom_call" | custom-call | bytes 8388608 | tf_op jit(solution)/shard_map/split/pallas_call | solution.py:547
  (56 shorter events, 3.2 us)
Async XLA Ops:
  4.5 22.4 %copy-start.15 = (f32[512]{0:T(512)S(1)}, f32[512]{0:T(512)}, u32[]{:S(2)}) copy-start(f32[512]{0:T(512)} %param.11) | copy-start | bytes 6148
  4.5 4.9 %collective-permute-start = (bf16[144,512]{1,0:T(8,128)(2,1)}, bf16[144,512]{1,0:T(8,128)(2,1)S(1)}, u32[]{:S(2)}, u32[]{:S(2)}) collective-permute-start(bf16[144,512]{1,0:T(8,128)(2,1)} %get-tuple-element.46), channel_id=1, source_target_pairs={{0,4},{4,0},{8,12},{12,8},{16,20},{20,16},{24,28},{28,24},{1,5},{5... | collective-permute-start | bytes 442376 | tf_op jit(solution)/shard_map/ppermute | solution.py:322
  5.0 7.5 %collective-permute-start.1 = (bf16[144,512]{1,0:T(8,128)(2,1)}, bf16[144,512]{1,0:T(8,128)(2,1)S(1)}, u32[]{:S(2)}, u32[]{:S(2)}) collective-permute-start(bf16[144,512]{1,0:T(8,128)(2,1)} %get-tuple-element.47), channel_id=1, source_target_pairs={{0,8},{4,12},{8,0},{12,4},{16,24},{20,28},{24,16},{28,20},{1,9},{5... | collective-permute-start | bytes 442376 | tf_op jit(solution)/shard_map/ppermute | solution.py:322
  7.6 7.6 %collective-permute-start.2 = (bf16[144,512]{1,0:T(8,128)(2,1)}, bf16[144,512]{1,0:T(8,128)(2,1)S(1)}, u32[]{:S(2)}, u32[]{:S(2)}) collective-permute-start(bf16[144,512]{1,0:T(8,128)(2,1)} %get-tuple-element.48), channel_id=1, source_target_pairs={{0,12},{4,8},{8,4},{12,0},{16,28},{20,24},{24,20},{28,16},{1,13},{... | collective-permute-start | bytes 442376 | tf_op jit(solution)/shard_map/ppermute | solution.py:322
  7.7 7.6 %collective-permute-start.3 = (bf16[144,512]{1,0:T(8,128)(2,1)}, bf16[144,512]{1,0:T(8,128)(2,1)S(1)}, u32[]{:S(2)}, u32[]{:S(2)}) collective-permute-start(bf16[144,512]{1,0:T(8,128)(2,1)} %get-tuple-element.49), channel_id=1, source_target_pairs={{0,16},{4,20},{8,24},{12,28},{16,0},{20,4},{24,8},{28,12},{1,17},{... | collective-permute-start | bytes 442376 | tf_op jit(solution)/shard_map/ppermute | solution.py:322
  9.4 13.4 %collective-permute-start.4 = (bf16[144,512]{1,0:T(8,128)(2,1)}, bf16[144,512]{1,0:T(8,128)(2,1)S(1)}, u32[]{:S(2)}, u32[]{:S(2)}) collective-permute-start(bf16[144,512]{1,0:T(8,128)(2,1)} %get-tuple-element.50), channel_id=1, source_target_pairs={{0,20},{4,16},{8,28},{12,24},{16,4},{20,0},{24,12},{28,8},{1,21},{... | collective-permute-start | bytes 442376 | tf_op jit(solution)/shard_map/ppermute | solution.py:322
  9.4 13.4 %collective-permute-start.5 = (bf16[144,512]{1,0:T(8,128)(2,1)}, bf16[144,512]{1,0:T(8,128)(2,1)S(1)}, u32[]{:S(2)}, u32[]{:S(2)}) collective-permute-start(bf16[144,512]{1,0:T(8,128)(2,1)} %get-tuple-element.51), channel_id=1, source_target_pairs={{0,24},{4,28},{8,16},{12,20},{16,8},{20,12},{24,0},{28,4},{1,25},{... | collective-permute-start | bytes 442376 | tf_op jit(solution)/shard_map/ppermute | solution.py:322
  12.5 10.3 %collective-permute-start.6 = (bf16[144,512]{1,0:T(8,128)(2,1)}, bf16[144,512]{1,0:T(8,128)(2,1)S(1)}, u32[]{:S(2)}, u32[]{:S(2)}) collective-permute-start(bf16[144,512]{1,0:T(8,128)(2,1)} %get-tuple-element.52), channel_id=1, source_target_pairs={{0,28},{4,24},{8,20},{12,16},{16,12},{20,8},{24,4},{28,0},{1,29},{... | collective-permute-start | bytes 442376 | tf_op jit(solution)/shard_map/ppermute | solution.py:322
  22.8 20.7 %all-to-all-start = ((bf16[8,128,512]{2,1,0:T(8,128)(2,1)}), bf16[8,128,512]{2,1,0:T(8,128)(2,1)S(1)}, u32[]{:S(2)}, u32[]{:S(2)}) async-start(bf16[8,128,512]{2,1,0:T(8,128)(2,1)} %bitcast.30), calls=%async_computation | async-start | bytes 2097152 | tf_op jit(solution)/shard_map/all_to_all | solution.py:429
  26.9 1.4 copy-start.2
  28.3 0.9 copy-start.16
  37.5 3.3 %copy-start = (f32[8,512,512]{2,1,0:T(8,128)}, f32[8,512,512]{2,1,0:T(8,128)S(1)}, u32[]{:S(2)}) copy-start(f32[8,512,512]{2,1,0:T(8,128)S(1)} %get-tuple-element.65.probs_ref) | copy-start | bytes 25165828
  40.8 1.1 copy-start.4
  42.0 0.8 copy-start.11
  42.7 0.8 copy-start.13
  43.6 3.4 %copy-start.1 = (f32[8,512,512]{2,1,0:T(8,128)S(1)}, f32[8,512,512]{2,1,0:T(8,128)}, u32[]{:S(2)}) copy-start(f32[8,512,512]{2,1,0:T(8,128)} %copy-done) | copy-start | bytes 25165828
  47.0 1.4 copy-start.3
  48.4 1.4 copy-start.5
  49.8 1.0 copy-start.8
  50.8 1.0 copy-start.12
  51.9 1.0 copy-start.14
  65.5 4.9 %copy-start.6 = (f32[512,512]{1,0:T(8,128)}, f32[512,512]{1,0:T(8,128)S(1)}, u32[]{:S(2)}) copy-start(f32[512,512]{1,0:T(8,128)S(1)} %get-tuple-element.71.d_normed_ref) | copy-start | bytes 3145732
  65.5 4.9 %copy-start.9 = (bf16[512,512]{1,0:T(8,128)(2,1)}, bf16[512,512]{1,0:T(8,128)(2,1)S(1)}, u32[]{:S(2)}) copy-start(bf16[512,512]{1,0:T(8,128)(2,1)S(1)} %get-tuple-element.70.serial_grad_ref) | copy-start | bytes 1572868
  65.5 3.8 %collective-permute-start.8 = (f32[128,2176]{1,0:T(8,128)S(1)}, f32[128,2176]{1,0:T(8,128)S(1)}, u32[]{:S(2)}, u32[]{:S(2)}) collective-permute-start(f32[128,2176]{1,0:T(8,128)S(1)} %get-tuple-element.75), channel_id=1, source_target_pairs={{0,4},{4,0},{8,12},{12,8},{16,20},{20,16},{24,28},{28,24},{1,5},{5... | collective-permute-start | bytes 3342344 | tf_op jit(solution)/shard_map/ppermute | solution.py:357
  66.1 5.5 %collective-permute-start.7 = (f32[128,2176]{1,0:T(8,128)}, f32[128,2176]{1,0:T(8,128)}, u32[]{:S(2)}, u32[]{:S(2)}) collective-permute-start(f32[128,2176]{1,0:T(8,128)} %get-tuple-element.73), channel_id=1, source_target_pairs={{0,4},{4,0},{8,12},{12,8},{16,20},{20,16},{24,28},{28,24},{1,5},{5... | collective-permute-start | bytes 3342344 | tf_op jit(solution)/shard_map/ppermute | solution.py:358
  70.4 15.8 %collective-permute-start.9 = (f32[128,2176]{1,0:T(8,128)}, f32[128,2176]{1,0:T(8,128)}, u32[]{:S(2)}, u32[]{:S(2)}) collective-permute-start(f32[128,2176]{1,0:T(8,128)} %add.72), channel_id=1, source_target_pairs={{0,8},{4,20},{8,0},{12,28},{16,24},{20,4},{24,16},{28,12},{1,9},{5... | collective-permute-start | bytes 3342344 | tf_op jit(solution)/shard_map/ppermute | solution.py:359
  73.0 16.7 %copy-start.7 = (f32[512,512]{1,0:T(8,128)S(1)}, f32[512,512]{1,0:T(8,128)}, u32[]{:S(2)}) copy-start(f32[512,512]{1,0:T(8,128)} %copy-done.6) | copy-start | bytes 3145732
  73.0 16.7 %copy-start.10 = (bf16[512,512]{1,0:T(8,128)(2,1)S(1)}, bf16[512,512]{1,0:T(8,128)(2,1)}, u32[]{:S(2)}) copy-start(bf16[512,512]{1,0:T(8,128)(2,1)} %copy-done.9) | copy-start | bytes 1572868
  88.4 9.8 %collective-permute-start.10 = (f32[64,2176]{1,0:T(8,128)}, f32[64,2176]{1,0:T(8,128)}, u32[]{:S(2)}, u32[]{:S(2)}) collective-permute-start(f32[64,2176]{1,0:T(8,128)} %get-tuple-element.92), channel_id=1, source_target_pairs={{0,16},{4,12},{8,24},{12,4},{16,0},{20,28},{24,8},{28,20},{1,17},{... | collective-permute-start | bytes 1671176 | tf_op jit(solution)/shard_map/ppermute | solution.py:361
  98.3 21.7 %all-to-all-start.1 = ((bf16[8,128,512]{2,1,0:T(8,128)(2,1)}), bf16[8,128,512]{2,1,0:T(8,128)(2,1)S(1)}, u32[]{:S(2)}, u32[]{:S(2)}) async-start(bf16[8,128,512]{2,1,0:T(8,128)(2,1)} %bitcast.6), calls=%async_computation.1 | async-start | bytes 2097152 | tf_op jit(solution)/shard_map/all_to_all | solution.py:429
  103.0 8.5 %collective-permute-start.13 = (f32[16,2176]{1,0:T(8,128)S(1)}, f32[16,2176]{1,0:T(8,128)S(1)}, u32[]{:S(2)}, u32[]{:S(2)}) collective-permute-start(f32[16,2176]{1,0:T(8,128)S(1)} %get-tuple-element.95), channel_id=1, source_target_pairs={{0,3},{1,2},{2,1},{3,0},{4,7},{5,6},{6,5},{7,4},{8,11},{9,10},{10,... | collective-permute-start | bytes 417800 | tf_op jit(solution)/shard_map/ppermute | solution.py:322
  106.7 12.3 %collective-permute-start.12 = (f32[16,2176]{1,0:T(8,128)S(1)}, f32[16,2176]{1,0:T(8,128)S(1)}, u32[]{:S(2)}, u32[]{:S(2)}) collective-permute-start(f32[16,2176]{1,0:T(8,128)S(1)} %get-tuple-element.96), channel_id=1, source_target_pairs={{0,2},{1,3},{2,0},{3,1},{4,6},{5,7},{6,4},{7,5},{8,10},{9,11},{10,... | collective-permute-start | bytes 417800 | tf_op jit(solution)/shard_map/ppermute | solution.py:322
  106.7 12.3 %collective-permute-start.11 = (f32[16,2176]{1,0:T(8,128)S(1)}, f32[16,2176]{1,0:T(8,128)S(1)}, u32[]{:S(2)}, u32[]{:S(2)}) collective-permute-start(f32[16,2176]{1,0:T(8,128)S(1)} %get-tuple-element.94), channel_id=1, source_target_pairs={{0,1},{1,0},{2,3},{3,2},{4,5},{5,4},{6,7},{7,6},{8,9},{9,8},{10,11... | collective-permute-start | bytes 417800 | tf_op jit(solution)/shard_map/ppermute | solution.py:322
  120.0 6.5 %collective-permute-start.16 = (bf16[16,2176]{1,0:T(8,128)(2,1)S(1)}, bf16[16,2176]{1,0:T(8,128)(2,1)S(1)}, u32[]{:S(2)}, u32[]{:S(2)}) collective-permute-start(bf16[16,2176]{1,0:T(8,128)(2,1)S(1)} %add_convert_fusion), channel_id=1, source_target_pairs={{0,3},{1,2},{2,1},{3,0},{4,7},{5,6},{6,5},{7,4},{8,11},{9,10},{10,... | collective-permute-start | bytes 208904 | tf_op jit(solution)/shard_map/ppermute | solution.py:322
  122.5 6.1 %collective-permute-start.15 = (bf16[16,2176]{1,0:T(8,128)(2,1)S(1)}, bf16[16,2176]{1,0:T(8,128)(2,1)S(1)}, u32[]{:S(2)}, u32[]{:S(2)}) collective-permute-start(bf16[16,2176]{1,0:T(8,128)(2,1)S(1)} %add_convert_fusion), channel_id=1, source_target_pairs={{0,2},{1,3},{2,0},{3,1},{4,6},{5,7},{6,4},{7,5},{8,10},{9,11},{10,... | collective-permute-start | bytes 208904 | tf_op jit(solution)/shard_map/ppermute | solution.py:322
  122.5 6.1 %collective-permute-start.14 = (bf16[16,2176]{1,0:T(8,128)(2,1)S(1)}, bf16[16,2176]{1,0:T(8,128)(2,1)S(1)}, u32[]{:S(2)}, u32[]{:S(2)}) collective-permute-start(bf16[16,2176]{1,0:T(8,128)(2,1)S(1)} %add_convert_fusion), channel_id=1, source_target_pairs={{0,1},{1,0},{2,3},{3,2},{4,5},{5,4},{6,7},{7,6},{8,9},{9,8},{10,11... | collective-permute-start | bytes 208904 | tf_op jit(solution)/shard_map/ppermute | solution.py:322
  128.7 6.6 %collective-permute-start.17 = (bf16[64,2176]{1,0:T(8,128)(2,1)S(1)}, bf16[64,2176]{1,0:T(8,128)(2,1)S(1)}, u32[]{:S(2)}, u32[]{:S(2)}) collective-permute-start(bf16[64,2176]{1,0:T(8,128)(2,1)S(1)} %pad_maximum_fusion.1), channel_id=1, source_target_pairs={{0,16},{4,12},{8,24},{12,4},{16,0},{20,28},{24,8},{28,20},{1,17},{... | collective-permute-start | bytes 835592 | tf_op jit(solution)/shard_map/ppermute | solution.py:383
  135.5 9.6 %collective-permute-start.18 = (bf16[128,2176]{1,0:T(8,128)(2,1)S(1)}, bf16[128,2176]{1,0:T(8,128)(2,1)S(1)}, u32[]{:S(2)}, u32[]{:S(2)}) collective-permute-start(bf16[128,2176]{1,0:T(8,128)(2,1)S(1)} %broadcast_select_fusion), channel_id=1, source_target_pairs={{0,8},{4,20},{8,0},{12,28},{16,24},{20,4},{24,16},{28,12},{1,9},{5... | collective-permute-start | bytes 1671176 | tf_op jit(solution)/shard_map/ppermute | solution.py:383
  136.9 8.5 %copy-start.17 = (s32[1,512]{1,0:T(1,128)S(1)}, s32[1,512]{1,0:T(1,128)}, u32[]{:S(2)}) copy-start(s32[1,512]{1,0:T(1,128)} %get-tuple-element.44.slot_ref) | copy-start | bytes 6148
  145.3 2.8 %collective-permute-start.19 = (bf16[256,2176]{1,0:T(8,128)(2,1)S(1)}, bf16[256,2176]{1,0:T(8,128)(2,1)S(1)}, u32[]{:S(2)}, u32[]{:S(2)}) collective-permute-start(bf16[256,2176]{1,0:T(8,128)(2,1)S(1)} %maximum_select_fusion.own_ref), channel_id=1, source_target_pairs={{0,4},{4,0},{8,12},{12,8},{16,20},{20,16},{24,28},{28,24},{1,5},{5... | collective-permute-start | bytes 3342344 | tf_op jit(solution)/shard_map/ppermute | solution.py:534

commit v5 on v4

--- a/solution.py
+++ b/solution.py
@@ -41,15 +41,13 @@
     return pl.ds(pl.multiple_of(lax.bitwise_xor(me, distance) * capacity, capacity), capacity)
 
 
-def pack_kernel(n_seq, capacity, me_ref, dest_hbm, feats_hbm, grads_hbm, slot_out, grads_out, *refs):
-    outs, (dest_ref, feats_ref, grads_ref, sems) = refs[:n_seq], refs[n_seq:]
+def pack_kernel(n_seq, capacity, me_ref, dest_hbm, feats_hbm, slot_out, *refs):
+    outs, (dest_ref, feats_ref, sems) = refs[:n_seq], refs[n_seq:]
     rows, width = feats_ref.shape
     slots = n_seq * capacity
     loads = [
         pltpu.make_async_copy(source, target, sems.at[i])
-        for i, (source, target) in enumerate(
-            ((dest_hbm, dest_ref), (feats_hbm, feats_ref), (grads_hbm, grads_ref))
-        )
+        for i, (source, target) in enumerate(((dest_hbm, dest_ref), (feats_hbm, feats_ref)))
     ]
     for load in loads:
         load.start()
@@ -84,7 +82,10 @@
     for d in range(n_seq):
         outs[d][:capacity, :] = feats[d * capacity : (d + 1) * capacity]
         outs[d][capacity:, :] = position[d * EXTRA : (d + 1) * EXTRA]
-    loads[2].wait()
+
+
+def pack_grads_kernel(n_seq, capacity, me_ref, slot_ref, grads_ref, grads_out):
+    select = hot(iota((n_seq * capacity, grads_ref.shape[0]), 0) == slot_ref[...])
     grads = mm(select, grads_ref[...]).astype(BF16)
     for d in range(n_seq):
         grads_out[by_receiver(me_ref[0], d, capacity), :] = grads[d * capacity : (d + 1) * capacity]
@@ -154,7 +155,7 @@
             save.wait()
 
 
-def backward_kernel(n_seq, first_bits, me_ref, pos_ref, w_proj_ref, probs_ref, *refs):
+def backward_kernel(n_seq, chip_bits, me_ref, pos_ref, w_proj_ref, probs_ref, *refs):
     (recv_hbm, qkv_hbm, w_hbm, xhat_hbm, normed_hbm, attn_hbm), refs = refs[:6], refs[6:]
     outs, serial_grad_hbm, d_normed_hbm, refs = refs[:4], refs[4], refs[5], refs[6:]
     recv_ref, qkv_ref, w_ref, xhat_ref, normed_ref, attn_ref, refs = *refs[:6], refs[6:]
@@ -242,24 +243,29 @@
         saves[5].start()
         gain_row = jnp.sum(d_normed * xhat_ref[...], axis=0, keepdims=True)
         gain_column[...] = jnp.transpose(jnp.broadcast_to(gain_row, (LANES, width)))
-        quarter = width // 4
+        eighth = width // 8
         odd = lax.bitwise_and(me, 1)
-        even_bit, odd_bit = first_bits
-        even_side = lax.bitwise_and(lax.shift_right_logical(me, even_bit), 1)
-        odd_side = lax.bitwise_and(lax.shift_right_logical(me, odd_bit), 1)
-        mine = jnp.where(odd == 1, odd_side, even_side)
-        other = jnp.where(odd == 1, even_side, odd_side)
+
+        def sides(even_bit, odd_bit):
+            even_side = lax.bitwise_and(lax.shift_right_logical(me, even_bit), 1)
+            odd_side = lax.bitwise_and(lax.shift_right_logical(me, odd_bit), 1)
+            mine = jnp.where(odd == 1, odd_side, even_side)
+            return mine, even_side + odd_side - mine
+
+        (mine, other), (mine_next, other_next) = (sides(*bits) for bits in chip_bits)
         starts = (
-            (1 - odd) * 2 + 1 - other,
-            (1 - odd) * 2 + other,
-            odd * 2 + 1 - mine,
-            odd * 2 + mine,
+            ((1 - odd) * 2 + 1 - other, other_next),
+            ((1 - odd) * 2 + other, other_next),
+            (odd * 2 + 1 - mine, mine_next),
+            (odd * 2 + mine, mine_next),
         )
-        for out, start, save in zip(sums, starts, saves):
-            part = pl.ds(pl.multiple_of(start * quarter, quarter), quarter)
-            out[:, : 3 * width] = mm(normed_t[part, :], d_qkv[...])
-            out[:, 3 * width : 4 * width] = mm(attn_ref[part, :], serial_grad[...])
-            out[:, 4 * width :] = gain_column[part, :]
+        for out, (start, side), save in zip(sums, starts, saves):
+            for j, half in enumerate((1 - side, side)):
+                part = pl.ds(pl.multiple_of((start * 2 + half) * eighth, eighth), eighth)
+                lines = slice(j * eighth, (j + 1) * eighth)
+                out[lines, : 3 * width] = mm(normed_t[part, :], d_qkv[...])
+                out[lines, 3 * width : 4 * width] = mm(attn_ref[part, :], serial_grad[...])
+                out[lines, 4 * width :] = gain_column[part, :]
             save.start()
         for save in saves:
             save.wait()
@@ -352,12 +358,18 @@
     return [(i, i ^ 1) for i in range(lax.axis_size("seq"))]
 
 
-def reduce_in_plane(quarters, steps):
+def first_step(quarters, steps):
     pass_on, pass_keep, own_on, own_keep = quarters
     send = own_on + lax.ppermute(pass_on, "seq", core_pairs())
     keep = own_keep + lax.ppermute(pass_keep, "seq", core_pairs())
-    terms = [keep, lax.ppermute(send, "seq", steps[0][0])]
-    for pairs, side in steps[1:]:
+    return [keep, lax.ppermute(send, "seq", steps[0][0])]
+
+
+def next_steps(terms, steps):
+    half = terms[0].shape[0] // 2
+    got = lax.ppermute(terms[0][:half] + terms[1][:half], "seq", steps[1][0])
+    terms = [terms[0][half:] + terms[1][half:], got]
+    for pairs, side in steps[2:]:
         got = lax.ppermute(piece(terms, 1 - side, 2), "seq", pairs)
         terms = [piece(terms, side, 2), got]
     return terms
@@ -405,31 +417,41 @@
     in_hbm = pl.BlockSpec(memory_space=pl.ANY)
     stay_hbm = pl.BlockSpec(memory_space=pltpu.HBM)
 
-    slot, grads_sent, *feats_sent = pl.pallas_call(
+    slot, *feats_sent = pl.pallas_call(
         functools.partial(pack_kernel, n_seq, capacity),
-        out_shape=[shape_of((1, rows), jnp.int32), shape_of((slots, width), BF16)]
-        + [shape_of((block, width), BF16)] * n_seq,
-        in_specs=[in_smem] + [stay_hbm] * 3,
-        out_specs=[in_vmem] * (2 + n_seq),
+        out_shape=[shape_of((1, rows), jnp.int32)] + [shape_of((block, width), BF16)] * n_seq,
+        in_specs=[in_smem] + [stay_hbm] * 2,
+        out_specs=[in_vmem] * (1 + n_seq),
         scratch_shapes=[
             pltpu.VMEM((1, rows), jnp.int32),
             pltpu.VMEM((rows, width), BF16),
-            pltpu.VMEM((rows, width), BF16),
-            pltpu.SemaphoreType.DMA((3,)),
+            pltpu.SemaphoreType.DMA((2,)),
         ],
         compiler_params=params(60),
         cost_estimate=pl.CostEstimate(
-            flops=4 * slots * rows * width, bytes_accessed=4 * MIB, transcendentals=0
+            flops=2 * slots * rows * width, bytes_accessed=2 * MIB, transcendentals=0
         ),
         name="pack",
-    )(me, dest, feats, grads)
+    )(me, dest, feats)
+    feats_got = by_distance(feats_sent, "seq")
+    feats_got[1], slot = lax.optimization_barrier((feats_got[1], slot))
+    grads_sent = pl.pallas_call(
+        functools.partial(pack_grads_kernel, n_seq, capacity),
+        out_shape=shape_of((slots, width), BF16),
+        in_specs=[in_smem] + [in_vmem] * 2,
+        out_specs=in_vmem,
+        compiler_params=params(20),
+        cost_estimate=pl.CostEstimate(
+            flops=2 * slots * rows * width, bytes_accessed=2 * MIB, transcendentals=0
+        ),
+        name="pack_grads",
+    )(me, slot, grads)
 
     def exchange(sent):
         sent = sent.reshape(n_seq, capacity, width)
         got = lax.all_to_all(sent, "seq", split_axis=0, concat_axis=0, tiled=True)
         return got.reshape(slots, width)
 
-    feats_got = by_distance(feats_sent, "seq")
     feats_got, grads_sent = lax.optimization_barrier((feats_got, grads_sent))
     grads_got = exchange(grads_sent)
 
@@ -461,7 +483,7 @@
             pltpu.VMEM((3 * width, rows), BF16),
             pltpu.SemaphoreType.DMA((5,)),
         ],
-        compiler_params=params(24),
+        compiler_params=params(60),
         cost_estimate=pl.CostEstimate(
             flops=6 * rows * width * width + 8 * HEADS * rows * rows * pair,
             bytes_accessed=16 * MIB,
@@ -470,9 +492,9 @@
         name="forward",
     )(w_qkv, gain_row, *feats_got)
 
-    first_bits = tuple(order[0] for order in chip_orders(n_seq))
+    chip_bits = tuple(zip(*chip_orders(n_seq)))[:2]
     *quarters, serial_grad, d_normed = pl.pallas_call(
-        functools.partial(backward_kernel, n_seq, first_bits),
+        functools.partial(backward_kernel, n_seq, chip_bits),
         grid=(pairs,),
         out_shape=[shape_of(sum_shape, F32)] * 4
         + [shape_of((rows, width), BF16), shape_of((rows, width), F32)],
@@ -504,7 +526,7 @@
             pltpu.VMEM((width, LANES), F32),
             pltpu.SemaphoreType.DMA((12,)),
         ],
-        compiler_params=params(32),
+        compiler_params=params(60),
         cost_estimate=pl.CostEstimate(
             flops=12 * rows * width * width + 8 * HEADS * rows * rows * pair,
             bytes_accessed=24 * MIB,
@@ -513,6 +535,9 @@
         name="backward",
     )(me, pos, w_proj, probs, grads_got, qkv, w_qkv, xhat, normed, attn_t)
 
+    steps = chip_steps()
+    terms = first_step(quarters, steps)
+    d_normed, terms = lax.optimization_barrier((d_normed, terms))
     back = pl.pallas_call(
         functools.partial(residual_kernel, n_seq),
         out_shape=shape_of((slots, width), BF16),
@@ -524,11 +549,8 @@
         ),
         name="residual",
     )(me, pos, gain_row, inv, xhat, serial_grad, d_normed)
-
-    steps = chip_steps()
-    terms = reduce_in_plane(quarters, steps)
-    back, terms = lax.optimization_barrier((back, terms))
     returned = exchange(back)
+    terms = next_steps(terms, steps)
     part, returned = lax.optimization_barrier((reduce_over_planes(terms), returned))
     own = share_in_plane(share_over_planes(part), steps)
     other = lax.ppermute(own, "seq", core_pairs())

time: 151 us -> 140 us (0.927)
  local copies, waits for them, and re-layouts: 17.9 us -> 2.37 us
  Pallas kernels: 30.6 us -> 39 us
  starting transfers between devices: 31.8 us -> 28.8 us
  other arithmetic: 7.13 us -> 4.91 us
  waiting for transfers between devices: 62.1 us -> 63.7 us
    unnamed x44, local copies, waits for them, and re-layouts: 17.9 us -> 2.35 us
    pallas_call x1 -> x2, Pallas kernels: 12.6 us -> 19.2 us  [the longest x1 17.5 us: per_device(): pl.pallas_call(functools.partial(backward_kernel, n_seq, chip_bits), grid...]
    all_to_all x2, waiting for transfers between devices: 0.01 us -> 4.34 us  [exchange(): got = lax.all_to_all(sent, 'seq', split_axis=0, concat_axis=0, tiled=True)]
    ppermute x13, waiting for transfers between devices: 24.7 us -> 20.8 us  [by_distance(): lax.ppermute(blocks[k], axis, [(i, i ^ k) for i in range(count)])]
    ppermute x2, waiting for transfers between devices: 13.4 us -> 16.8 us  [share_in_plane(): other = lax.ppermute(part, 'seq', pairs)]
    pallas_call x1, Pallas kernels: 8.3 us -> 11 us  [per_device(): pl.pallas_call(functools.partial(forward_kernel, n_seq, capacity), grid=(...]
    ppermute x4, waiting for transfers between devices: 22.8 us -> 20.6 us  [the longest x1 14.9 us: first_step(): return [keep, lax.ppermute(send, 'seq', steps[0][0])]]
    add x2 -> x1, other arithmetic: 3.29 us -> 1.09 us  [piece(): functools.reduce(jnp.add, [lax.dynamic_slice_in_dim(t, index * size, size...]
  transfers between devices with their start and end apart: 22 -> 22, of which waited for: 13 -> 14; matrix products, arithmetic and copies ran while one was open for 3% -> 3% of each run, Pallas kernels for 8% -> 12%
where the time goes in v5:
time: 140 us
  waiting for transfers between devices  63.7 us (46%)
  Pallas kernels  39 us (28%)
  starting transfers between devices  28.8 us (21%)
  other arithmetic  4.91 us (4%)
  local copies, waits for them, and re-layouts  2.37 us (2%)
    ppermute x13, waiting for transfers between devices, by_distance(): lax.ppermute(blocks[k], axis, [(i, i ^ k) for i in range(count)])  20.8 us
    ppermute x13, starting transfers between devices, by_distance(): lax.ppermute(blocks[k], axis, [(i, i ^ k) for i in range(count)])  18.3 us
    pallas_call x1, Pallas kernels, per_device(): pl.pallas_call(functools.partial(backward_kernel, n_seq, chip_bits), grid...  17.5 us
    ppermute x2, waiting for transfers between devices, share_in_plane(): other = lax.ppermute(part, 'seq', pairs)  16.8 us
    ppermute x1, waiting for transfers between devices, first_step(): return [keep, lax.ppermute(send, 'seq', steps[0][0])]  14.9 us
    pallas_call x1, Pallas kernels, per_device(): pl.pallas_call(functools.partial(forward_kernel, n_seq, capacity), grid=(...  11 us
    all_to_all x2, starting transfers between devices, exchange(): got = lax.all_to_all(sent, 'seq', split_axis=0, concat_axis=0, tiled=True)  7.61 us
    all_to_all x2, waiting for transfers between devices, exchange(): got = lax.all_to_all(sent, 'seq', split_axis=0, concat_axis=0, tiled=True)  4.34 us
  transfers between devices with their start and end apart: 22, of which 14 were waited for; matrix products, arithmetic and copies ran while one was open for 3% of the time, Pallas kernels for 12%

profile of v5, /device:TPU:0, one launch (start us, length us, event | category | flops | bytes accessed | tf_op | source)
XLA Modules:
  0.0 139.7 jit_solution(8789095302325959361)
XLA Ops:
  0.6 3.0 %pack.1 = (s32[1,512]{1,0:T(1,128)}, bf16[144,512]{1,0:T(8,128)(2,1)}, bf16[144,512]{1,0:T(8,128)(2,1)}, bf16[144,512]{1,0:T(8,128)(2,1)}, bf16[144,512]{1,0:T(8...) custom-call(s32[1]{0:T(128)} %bitcast.me_ref, ...), custom_call_target="tpu_custom_call" | custom-call | flops 536870912 | bytes 2097152 | tf_op jit(solution)/shard_map/pack/pallas_call | solution.py:420
  3.7 0.5 collective-permute-start
  4.2 2.6 %collective-permute-start.1 = (bf16[144,512]{1,0:T(8,128)(2,1)}, bf16[144,512]{1,0:T(8,128)(2,1)S(1)}, u32[]{:S(2)}, u32[]{:S(2)}) collective-permute-start(bf16[144,512]{1,0:T(8,128)(2,1)} %get-tuple-element.50), channel_id=1, source_target_pairs={{0,8},{4,12},{8,0},{12,4},{16,24},{20,28},{24,16},{28,20},{1,9},{5... | collective-permute-start | bytes 442376 | tf_op jit(solution)/shard_map/ppermute | solution.py:328
  6.9 1.8 %collective-permute-start.3 = (bf16[144,512]{1,0:T(8,128)(2,1)}, bf16[144,512]{1,0:T(8,128)(2,1)S(1)}, u32[]{:S(2)}, u32[]{:S(2)}) collective-permute-start(bf16[144,512]{1,0:T(8,128)(2,1)} %get-tuple-element.52), channel_id=1, source_target_pairs={{0,16},{4,20},{8,24},{12,28},{16,0},{20,4},{24,8},{28,12},{1,17},{... | collective-permute-start | bytes 442376 | tf_op jit(solution)/shard_map/ppermute | solution.py:328
  8.6 2.6 %collective-permute-start.5 = (bf16[144,512]{1,0:T(8,128)(2,1)}, bf16[144,512]{1,0:T(8,128)(2,1)S(1)}, u32[]{:S(2)}, u32[]{:S(2)}) collective-permute-start(bf16[144,512]{1,0:T(8,128)(2,1)} %get-tuple-element.54), channel_id=1, source_target_pairs={{0,24},{4,28},{8,16},{12,20},{16,8},{20,12},{24,0},{28,4},{1,25},{... | collective-permute-start | bytes 442376 | tf_op jit(solution)/shard_map/ppermute | solution.py:328
  11.2 0.5 collective-permute-done.1.refs_2_
  11.7 1.7 %collective-permute-start.6 = (bf16[144,512]{1,0:T(8,128)(2,1)}, bf16[144,512]{1,0:T(8,128)(2,1)S(1)}, u32[]{:S(2)}, u32[]{:S(2)}) collective-permute-start(bf16[144,512]{1,0:T(8,128)(2,1)} %get-tuple-element.55), channel_id=1, source_target_pairs={{0,28},{4,24},{8,20},{12,16},{16,12},{20,8},{24,4},{28,0},{1,29},{... | collective-permute-start | bytes 442376 | tf_op jit(solution)/shard_map/ppermute | solution.py:328
  13.4 0.7 copy-done.7
  14.1 1.7 %pack_grads.1 = bf16[1024,512]{1,0:T(8,128)(2,1)} custom-call(s32[1]{0:T(128)} %bitcast.me_ref, s32[1,512]{1,0:T(1,128)S(1)} %copy-done.7, bf16[512,512]{1,0:T(8,128)(2,1)S(1)} %bitcast.29), custom_call_target="tpu_custom_call" | custom-call | flops 536870912 | bytes 2097152 | tf_op jit(solution)/shard_map/pack_grads/pallas_call | solution.py:438
  15.8 6.2 %collective-permute-done.4.refs_5_ = bf16[144,512]{1,0:T(8,128)(2,1)S(1)} collective-permute-done((bf16[144,512]{1,0:T(8,128)(2,1)}, bf16[144,512]{1,0:T(8,128)(2,1)S(1)}, u32[]{:S(2)}, u32[]{:S(2)}) %collective-permute-start.4) | collective-permute-done | bytes 147488 | tf_op jit(solution)/shard_map/ppermute | solution.py:328
  22.1 4.0 %all-to-all-start = ((bf16[8,128,512]{2,1,0:T(8,128)(2,1)}), bf16[8,128,512]{2,1,0:T(8,128)(2,1)S(1)}, u32[]{:S(2)}, u32[]{:S(2)}) async-start(bf16[8,128,512]{2,1,0:T(8,128)(2,1)} %bitcast.4), calls=%async_computation | async-start | bytes 2097152 | tf_op jit(solution)/shard_map/all_to_all | solution.py:452
  26.2 11.0 %forward.1 = (s32[1,1024]{1,0:T(1,128)}, f32[512,512]{1,0:T(8,128)}, f32[512,128]{1,0:T(8,128)}, bf16[512,512]{1,0:T(8,128)(2,1)}, bf16[512,1536]{1,0:T(8,128)(2...) custom-call(bf16[512,1536]{1,0:T(8,128)(2,1)} %refs_2_.1, f32[1,512]{1,0:T(1,128)} %bitcast.27, ...), custom_call_target="tpu_custom_call" | custom-call | flops 2952790016 | bytes 16777216 | tf_op jit(solution)/shard_map/forward/pallas_call | solution.py:458
  37.2 4.3 %all-to-all-done = bf16[8,128,512]{2,1,0:T(8,128)(2,1)S(1)} async-done(((bf16[8,128,512]{2,1,0:T(8,128)(2,1)}), bf16[8,128,512]{2,1,0:T(8,128)(2,1)S(1)}, u32[]{:S(2)}, u32[]{:S(2)}) %all-to-all-start) | async-done | bytes 1048608 | tf_op jit(solution)/shard_map/all_to_all | solution.py:452
  41.5 1.0 copy-done.9
  42.5 17.5 %backward.1 = (f32[128,2176]{1,0:T(8,128)}, f32[128,2176]{1,0:T(8,128)}, f32[128,2176]{1,0:T(8,128)}, f32[128,2176]{1,0:T(8,128)}, bf16[512,512]{1,0:T(8,128)(2,1)}, /*index=5*/f32[512,512]{1,0:T(8,128)}) custom-call(s32[1]{0:T(128)} %bitcast.me_ref, s32[1,1024]{1,0:T(1,128)} %get-tuple-element.64.pos_ref, bf16[512,512]{1,0:T(8,128)(2,1)} %w_proj_ref.1, ...), custom_call_target="tpu_custom_call" | custom-call | flops 3758096384 | bytes 25165824 | tf_op jit(solution)/shard_map/backward/pallas_call | solution.py:496
  60.1 0.5 collective-permute-start.7
  60.6 2.5 %collective-permute-done.8 = f32[128,2176]{1,0:T(8,128)S(1)} collective-permute-done((f32[128,2176]{1,0:T(8,128)}, f32[128,2176]{1,0:T(8,128)S(1)}, u32[]{:S(2)}, u32[]{:S(2)}) %collective-permute-start.8) | collective-permute-done | bytes 1114144 | tf_op jit(solution)/shard_map/ppermute | solution.py:363
  63.1 1.5 %add.63 = f32[128,2176]{1,0:T(8,128)S(1)} add(f32[128,2176]{1,0:T(8,128)} %get-tuple-element.74, f32[128,2176]{1,0:T(8,128)S(1)} %collective-permute-done.8) | non-fusion elementwise | flops 278528 | bytes 3342336 | tf_op jit(solution)/shard_map/add | solution.py:363
  64.5 0.6 collective-permute-start.9
  65.2 14.9 %collective-permute-done.9 = f32[128,2176]{1,0:T(8,128)S(1)} collective-permute-done((f32[128,2176]{1,0:T(8,128)S(1)}, f32[128,2176]{1,0:T(8,128)S(1)}, u32[]{:S(2)}, u32[]{:S(2)}) %collective-permute-start.9) | collective-permute-done | bytes 1114144 | tf_op jit(solution)/shard_map/ppermute | solution.py:365
  80.1 0.9 slice_add_fusion.1
  81.0 0.5 collective-permute-start.10
  81.6 0.2 copy-done.1
  81.8 0.1 copy-done.2
  82.0 2.1 %residual.1 = bf16[1024,512]{1,0:T(8,128)(2,1)} custom-call(s32[1]{0:T(128)} %bitcast.me_ref, s32[1,1024]{1,0:T(1,128)S(1)} %copy-done.4, f32[1,512]{1,0:T(1,128)S(1)} %bitcast.28, f32[512,128]{1,0:T(8,128)S(1)} %copy-done.3, f32[512,512]{1,0:T(8,128)S(1)} %copy-done, bf16[512,512]{1,0:T(8,128)(2,1)S(1)} %copy-done.2, f32[512,512]{1,0:T(8,128)S(1)} %copy-done.1), custom_call_target="tpu_custom_call" | custom-call | flops 536870912 | bytes 4194304 | tf_op jit(solution)/shard_map/residual/pallas_call | solution.py:541
  84.1 3.6 %all-to-all-start.1 = ((bf16[8,128,512]{2,1,0:T(8,128)(2,1)}), bf16[8,128,512]{2,1,0:T(8,128)(2,1)S(1)}, u32[]{:S(2)}, u32[]{:S(2)}) async-start(bf16[8,128,512]{2,1,0:T(8,128)(2,1)} %bitcast.6), calls=%async_computation.1 | async-start | bytes 2097152 | tf_op jit(solution)/shard_map/all_to_all | solution.py:452
  87.7 3.2 %collective-permute-done.10 = f32[64,2176]{1,0:T(8,128)} collective-permute-done((f32[64,2176]{1,0:T(8,128)}, f32[64,2176]{1,0:T(8,128)}, u32[]{:S(2)}, u32[]{:S(2)}) %collective-permute-start.10) | collective-permute-done | bytes 557088 | tf_op jit(solution)/shard_map/ppermute | solution.py:370
  90.9 1.1 dynamic-slice_add_fusion.2
  92.0 1.6 %collective-permute-start.11 = (f32[16,2176]{1,0:T(8,128)S(1)}, f32[16,2176]{1,0:T(8,128)S(1)}, u32[]{:S(2)}, u32[]{:S(2)}) collective-permute-start(f32[16,2176]{1,0:T(8,128)S(1)} %get-tuple-element.96), channel_id=1, source_target_pairs={{0,1},{1,0},{2,3},{3,2},{4,5},{5,4},{6,7},{7,6},{8,9},{9,8},{10,11... | collective-permute-start | bytes 417800 | tf_op jit(solution)/shard_map/ppermute | solution.py:328
  93.6 2.6 %collective-permute-start.12 = (f32[16,2176]{1,0:T(8,128)S(1)}, f32[16,2176]{1,0:T(8,128)S(1)}, u32[]{:S(2)}, u32[]{:S(2)}) collective-permute-start(f32[16,2176]{1,0:T(8,128)S(1)} %get-tuple-element.98), channel_id=1, source_target_pairs={{0,2},{1,3},{2,0},{3,1},{4,6},{5,7},{6,4},{7,5},{8,10},{9,11},{10,... | collective-permute-start | bytes 417800 | tf_op jit(solution)/shard_map/ppermute | solution.py:328
  96.2 0.2 collective-permute-start.13
  96.4 1.8 %collective-permute-done.11 = f32[16,2176]{1,0:T(8,128)S(1)} collective-permute-done((f32[16,2176]{1,0:T(8,128)S(1)}, f32[16,2176]{1,0:T(8,128)S(1)}, u32[]{:S(2)}, u32[]{:S(2)}) %collective-permute-start.11) | collective-permute-done | bytes 139296 | tf_op jit(solution)/shard_map/ppermute | solution.py:328
  98.3 7.4 %collective-permute-done.12 = f32[16,2176]{1,0:T(8,128)S(1)} collective-permute-done((f32[16,2176]{1,0:T(8,128)S(1)}, f32[16,2176]{1,0:T(8,128)S(1)}, u32[]{:S(2)}, u32[]{:S(2)}) %collective-permute-start.12) | collective-permute-done | bytes 139296 | tf_op jit(solution)/shard_map/ppermute | solution.py:328
  105.7 1.0 add_convert_fusion
  106.7 2.1 %collective-permute-start.14 = (bf16[16,2176]{1,0:T(8,128)(2,1)S(1)}, bf16[16,2176]{1,0:T(8,128)(2,1)S(1)}, u32[]{:S(2)}, u32[]{:S(2)}) collective-permute-start(bf16[16,2176]{1,0:T(8,128)(2,1)S(1)} %add_convert_fusion), channel_id=1, source_target_pairs={{0,1},{1,0},{2,3},{3,2},{4,5},{5,4},{6,7},{7,6},{8,9},{9,8},{10,11... | collective-permute-start | bytes 208904 | tf_op jit(solution)/shard_map/ppermute | solution.py:328
  108.8 1.1 collective-permute-start.15
  109.9 1.4 collective-permute-start.16
  111.3 0.1 collective-permute-done.14
  111.5 3.3 %collective-permute-done.15 = bf16[16,2176]{1,0:T(8,128)(2,1)S(1)} collective-permute-done((bf16[16,2176]{1,0:T(8,128)(2,1)S(1)}, bf16[16,2176]{1,0:T(8,128)(2,1)S(1)}, u32[]{:S(2)}, u32[]{:S(2)}) %collective-permute-start.15) | collective-permute-done | bytes 69664 | tf_op jit(solution)/shard_map/ppermute | solution.py:328
  114.8 1.4 collective-permute-done.16
  116.3 0.6 collective-permute-start.17
  117.0 7.7 %collective-permute-done.17 = bf16[64,2176]{1,0:T(8,128)(2,1)S(1)} collective-permute-done((bf16[64,2176]{1,0:T(8,128)(2,1)S(1)}, bf16[64,2176]{1,0:T(8,128)(2,1)S(1)}, u32[]{:S(2)}, u32[]{:S(2)}) %collective-permute-start.17) | collective-permute-done | bytes 278560 | tf_op jit(solution)/shard_map/ppermute | solution.py:395
  124.8 0.5 collective-permute-start.18
  125.3 9.1 %collective-permute-done.18 = bf16[128,2176]{1,0:T(8,128)(2,1)S(1)} collective-permute-done((bf16[128,2176]{1,0:T(8,128)(2,1)S(1)}, bf16[128,2176]{1,0:T(8,128)(2,1)S(1)}, u32[]{:S(2)}, u32[]{:S(2)}) %collective-permute-start.18) | collective-permute-done | bytes 557088 | tf_op jit(solution)/shard_map/ppermute | solution.py:395
  134.4 0.2 maximum_select_fusion.own_ref
  134.8 1.5 %unpack.1 = bf16[512,512]{1,0:T(8,128)(2,1)} custom-call(s32[1]{0:T(128)} %bitcast.me_ref, s32[1,512]{1,0:T(1,128)S(1)} %copy-done.8, bf16[1024,512]{1,0:T(8,128)(2,1)S(1)} %bitcast.26), custom_call_target="tpu_custom_call" | custom-call | flops 536870912 | bytes 2097152 | tf_op jit(solution)/shard_map/unpack/pallas_call | solution.py:557
  136.3 1.2 collective-permute-done.19.other_ref
  137.5 2.2 %split.1 = (f32[512,1536]{1,0:T(8,128)}, f32[512,512]{1,0:T(8,128)}, f32[1,512]{1,0:T(1,128)}) custom-call(s32[1]{0:T(128)S(6)} %and.16.side_ref, bf16[256,2176]{1,0:T(8,128)(2,1)S(1)} %maximum_select_fusion.own_ref, bf16[256,2176]{1,0:T(8,128)(2,1)S(1)} %collective-permute-done.19.other_ref), custom_call_target="tpu_custom_call" | custom-call | bytes 8388608 | tf_op jit(solution)/shard_map/split/pallas_call | solution.py:569
  (57 shorter events, 0.8 us)
Async XLA Ops:
  0.6 12.8 %copy-start.6 = (bf16[1,512,512]{2,1,0:T(8,128)(2,1)S(1)}, bf16[1,512,512]{2,1,0:T(8,128)(2,1)}, u32[]{:S(2)}) copy-start(bf16[1,512,512]{2,1,0:T(8,128)(2,1)} %param.7) | copy-start | bytes 1572868
  3.7 4.9 %collective-permute-start = (bf16[144,512]{1,0:T(8,128)(2,1)}, bf16[144,512]{1,0:T(8,128)(2,1)S(1)}, u32[]{:S(2)}, u32[]{:S(2)}) collective-permute-start(bf16[144,512]{1,0:T(8,128)(2,1)} %get-tuple-element.45), channel_id=1, source_target_pairs={{0,4},{4,0},{8,12},{12,8},{16,20},{20,16},{24,28},{28,24},{1,5},{5... | collective-permute-start | bytes 442376 | tf_op jit(solution)/shard_map/ppermute | solution.py:328
  4.2 7.5 %collective-permute-start.1 = (bf16[144,512]{1,0:T(8,128)(2,1)}, bf16[144,512]{1,0:T(8,128)(2,1)S(1)}, u32[]{:S(2)}, u32[]{:S(2)}) collective-permute-start(bf16[144,512]{1,0:T(8,128)(2,1)} %get-tuple-element.50), channel_id=1, source_target_pairs={{0,8},{4,12},{8,0},{12,4},{16,24},{20,28},{24,16},{28,20},{1,9},{5... | collective-permute-start | bytes 442376 | tf_op jit(solution)/shard_map/ppermute | solution.py:328
  6.8 9.0 %collective-permute-start.2 = (bf16[144,512]{1,0:T(8,128)(2,1)}, bf16[144,512]{1,0:T(8,128)(2,1)S(1)}, u32[]{:S(2)}, u32[]{:S(2)}) collective-permute-start(bf16[144,512]{1,0:T(8,128)(2,1)} %get-tuple-element.51), channel_id=1, source_target_pairs={{0,12},{4,8},{8,4},{12,0},{16,28},{20,24},{24,20},{28,16},{1,13},{... | collective-permute-start | bytes 442376 | tf_op jit(solution)/shard_map/ppermute | solution.py:328
  6.9 8.9 %collective-permute-start.3 = (bf16[144,512]{1,0:T(8,128)(2,1)}, bf16[144,512]{1,0:T(8,128)(2,1)S(1)}, u32[]{:S(2)}, u32[]{:S(2)}) collective-permute-start(bf16[144,512]{1,0:T(8,128)(2,1)} %get-tuple-element.52), channel_id=1, source_target_pairs={{0,16},{4,20},{8,24},{12,28},{16,0},{20,4},{24,8},{28,12},{1,17},{... | collective-permute-start | bytes 442376 | tf_op jit(solution)/shard_map/ppermute | solution.py:328
  8.6 13.4 %collective-permute-start.4 = (bf16[144,512]{1,0:T(8,128)(2,1)}, bf16[144,512]{1,0:T(8,128)(2,1)S(1)}, u32[]{:S(2)}, u32[]{:S(2)}) collective-permute-start(bf16[144,512]{1,0:T(8,128)(2,1)} %get-tuple-element.53), channel_id=1, source_target_pairs={{0,20},{4,16},{8,28},{12,24},{16,4},{20,0},{24,12},{28,8},{1,21},{... | collective-permute-start | bytes 442376 | tf_op jit(solution)/shard_map/ppermute | solution.py:328
  8.6 13.4 %copy-start.11 = (bf16[144,512]{1,0:T(8,128)(2,1)}, bf16[144,512]{1,0:T(8,128)(2,1)S(1)}, u32[]{:S(2)}) copy-start(bf16[144,512]{1,0:T(8,128)(2,1)S(1)} %collective-permute-done.refs_1_) | copy-start | bytes 442372
  8.6 13.4 %collective-permute-start.5 = (bf16[144,512]{1,0:T(8,128)(2,1)}, bf16[144,512]{1,0:T(8,128)(2,1)S(1)}, u32[]{:S(2)}, u32[]{:S(2)}) collective-permute-start(bf16[144,512]{1,0:T(8,128)(2,1)} %get-tuple-element.54), channel_id=1, source_target_pairs={{0,24},{4,28},{8,16},{12,20},{16,8},{20,12},{24,0},{28,4},{1,25},{... | collective-permute-start | bytes 442376 | tf_op jit(solution)/shard_map/ppermute | solution.py:328
  11.7 10.4 %copy-start.12 = (bf16[144,512]{1,0:T(8,128)(2,1)}, bf16[144,512]{1,0:T(8,128)(2,1)S(1)}, u32[]{:S(2)}) copy-start(bf16[144,512]{1,0:T(8,128)(2,1)S(1)} %collective-permute-done.1.refs_2_) | copy-start | bytes 442372
  11.7 10.3 %collective-permute-start.6 = (bf16[144,512]{1,0:T(8,128)(2,1)}, bf16[144,512]{1,0:T(8,128)(2,1)S(1)}, u32[]{:S(2)}, u32[]{:S(2)}) collective-permute-start(bf16[144,512]{1,0:T(8,128)(2,1)} %get-tuple-element.55), channel_id=1, source_target_pairs={{0,28},{4,24},{8,20},{12,16},{16,12},{20,8},{24,4},{28,0},{1,29},{... | collective-permute-start | bytes 442376 | tf_op jit(solution)/shard_map/ppermute | solution.py:328
  13.4 0.7 copy-start.7
  15.8 10.3 %copy-start.13 = (bf16[144,512]{1,0:T(8,128)(2,1)}, bf16[144,512]{1,0:T(8,128)(2,1)S(1)}, u32[]{:S(2)}) copy-start(bf16[144,512]{1,0:T(8,128)(2,1)S(1)} %collective-permute-done.2.refs_3_) | copy-start | bytes 442372
  15.8 10.3 %copy-start.14 = (bf16[144,512]{1,0:T(8,128)(2,1)}, bf16[144,512]{1,0:T(8,128)(2,1)S(1)}, u32[]{:S(2)}) copy-start(bf16[144,512]{1,0:T(8,128)(2,1)S(1)} %collective-permute-done.3.refs_4_) | copy-start | bytes 442372
  22.0 4.1 %copy-start.15 = (bf16[144,512]{1,0:T(8,128)(2,1)}, bf16[144,512]{1,0:T(8,128)(2,1)S(1)}, u32[]{:S(2)}) copy-start(bf16[144,512]{1,0:T(8,128)(2,1)S(1)} %collective-permute-done.4.refs_5_) | copy-start | bytes 442372
  22.0 4.1 %copy-start.16 = (bf16[144,512]{1,0:T(8,128)(2,1)}, bf16[144,512]{1,0:T(8,128)(2,1)S(1)}, u32[]{:S(2)}) copy-start(bf16[144,512]{1,0:T(8,128)(2,1)S(1)} %collective-permute-done.5.refs_6_) | copy-start | bytes 442372
  22.0 4.1 %copy-start.17 = (bf16[144,512]{1,0:T(8,128)(2,1)}, bf16[144,512]{1,0:T(8,128)(2,1)S(1)}, u32[]{:S(2)}) copy-start(bf16[144,512]{1,0:T(8,128)(2,1)S(1)} %collective-permute-done.6.refs_7_) | copy-start | bytes 442372
  22.1 19.5 %all-to-all-start = ((bf16[8,128,512]{2,1,0:T(8,128)(2,1)}), bf16[8,128,512]{2,1,0:T(8,128)(2,1)S(1)}, u32[]{:S(2)}, u32[]{:S(2)}) async-start(bf16[8,128,512]{2,1,0:T(8,128)(2,1)} %bitcast.4), calls=%async_computation | async-start | bytes 2097152 | tf_op jit(solution)/shard_map/all_to_all | solution.py:452
  41.5 1.0 copy-start.9
  60.0 3.0 %collective-permute-start.8 = (f32[128,2176]{1,0:T(8,128)}, f32[128,2176]{1,0:T(8,128)S(1)}, u32[]{:S(2)}, u32[]{:S(2)}) collective-permute-start(f32[128,2176]{1,0:T(8,128)} %get-tuple-element.75), channel_id=1, source_target_pairs={{0,4},{4,0},{8,12},{12,8},{16,20},{20,16},{24,28},{28,24},{1,5},{5... | collective-permute-start | bytes 3342344 | tf_op jit(solution)/shard_map/ppermute | solution.py:363
  60.1 5.0 %collective-permute-start.7 = (f32[128,2176]{1,0:T(8,128)}, f32[128,2176]{1,0:T(8,128)S(1)}, u32[]{:S(2)}, u32[]{:S(2)}) collective-permute-start(f32[128,2176]{1,0:T(8,128)} %get-tuple-element.73), channel_id=1, source_target_pairs={{0,4},{4,0},{8,12},{12,8},{16,20},{20,16},{24,28},{28,24},{1,5},{5... | collective-permute-start | bytes 3342344 | tf_op jit(solution)/shard_map/ppermute | solution.py:364
  63.1 2.0 %copy-start.10 = (f32[128,2176]{1,0:T(8,128)S(1)}, f32[128,2176]{1,0:T(8,128)}, u32[]{:S(2)}) copy-start(f32[128,2176]{1,0:T(8,128)} %get-tuple-element.72) | copy-start | bytes 3342340
  64.5 15.6 %collective-permute-start.9 = (f32[128,2176]{1,0:T(8,128)S(1)}, f32[128,2176]{1,0:T(8,128)S(1)}, u32[]{:S(2)}, u32[]{:S(2)}) collective-permute-start(f32[128,2176]{1,0:T(8,128)S(1)} %add.63), channel_id=1, source_target_pairs={{0,8},{4,20},{8,0},{12,28},{16,24},{20,4},{24,16},{28,12},{1,9},{5... | collective-permute-start | bytes 3342344 | tf_op jit(solution)/shard_map/ppermute | solution.py:365
  80.1 1.5 %copy-start = (f32[512,512]{1,0:T(8,128)S(1)}, f32[512,512]{1,0:T(8,128)}, u32[]{:S(2)}) copy-start(f32[512,512]{1,0:T(8,128)} %get-tuple-element.68.refs_3_.xhat_ref) | copy-start | bytes 3145732
  80.1 1.7 %copy-start.1 = (f32[512,512]{1,0:T(8,128)S(1)}, f32[512,512]{1,0:T(8,128)}, u32[]{:S(2)}) copy-start(f32[512,512]{1,0:T(8,128)} %get-tuple-element.80.d_normed_ref) | copy-start | bytes 3145732
  80.1 1.9 %copy-start.2 = (bf16[512,512]{1,0:T(8,128)(2,1)S(1)}, bf16[512,512]{1,0:T(8,128)(2,1)}, u32[]{:S(2)}) copy-start(bf16[512,512]{1,0:T(8,128)(2,1)} %get-tuple-element.79.serial_grad_ref) | copy-start | bytes 1572868
  80.1 1.9 %copy-start.3 = (f32[512,128]{1,0:T(8,128)S(1)}, f32[512,128]{1,0:T(8,128)}, u32[]{:S(2)}) copy-start(f32[512,128]{1,0:T(8,128)} %get-tuple-element.78.inv_ref) | copy-start | bytes 786436
  80.1 1.9 %copy-start.4 = (s32[1,1024]{1,0:T(1,128)S(1)}, s32[1,1024]{1,0:T(1,128)}, u32[]{:S(2)}) copy-start(s32[1,1024]{1,0:T(1,128)} %get-tuple-element.64.pos_ref) | copy-start | bytes 12292
  80.1 1.9 %copy-start.5 = (f32[512]{0:T(512)S(1)}, f32[512]{0:T(512)}, u32[]{:S(2)}) copy-start(f32[512]{0:T(512)} %param.11) | copy-start | bytes 6148
  81.0 9.8 %collective-permute-start.10 = (f32[64,2176]{1,0:T(8,128)}, f32[64,2176]{1,0:T(8,128)}, u32[]{:S(2)}, u32[]{:S(2)}) collective-permute-start(f32[64,2176]{1,0:T(8,128)} %get-tuple-element.95), channel_id=1, source_target_pairs={{0,16},{4,12},{8,24},{12,4},{16,0},{20,28},{24,8},{28,20},{1,17},{... | collective-permute-start | bytes 1671176 | tf_op jit(solution)/shard_map/ppermute | solution.py:370
  84.1 22.6 %all-to-all-start.1 = ((bf16[8,128,512]{2,1,0:T(8,128)(2,1)}), bf16[8,128,512]{2,1,0:T(8,128)(2,1)S(1)}, u32[]{:S(2)}, u32[]{:S(2)}) async-start(bf16[8,128,512]{2,1,0:T(8,128)(2,1)} %bitcast.6), calls=%async_computation.1 | async-start | bytes 2097152 | tf_op jit(solution)/shard_map/all_to_all | solution.py:452
  92.0 6.3 %collective-permute-start.11 = (f32[16,2176]{1,0:T(8,128)S(1)}, f32[16,2176]{1,0:T(8,128)S(1)}, u32[]{:S(2)}, u32[]{:S(2)}) collective-permute-start(f32[16,2176]{1,0:T(8,128)S(1)} %get-tuple-element.96), channel_id=1, source_target_pairs={{0,1},{1,0},{2,3},{3,2},{4,5},{5,4},{6,7},{7,6},{8,9},{9,8},{10,11... | collective-permute-start | bytes 417800 | tf_op jit(solution)/shard_map/ppermute | solution.py:328
  93.6 12.1 %collective-permute-start.12 = (f32[16,2176]{1,0:T(8,128)S(1)}, f32[16,2176]{1,0:T(8,128)S(1)}, u32[]{:S(2)}, u32[]{:S(2)}) collective-permute-start(f32[16,2176]{1,0:T(8,128)S(1)} %get-tuple-element.98), channel_id=1, source_target_pairs={{0,2},{1,3},{2,0},{3,1},{4,6},{5,7},{6,4},{7,5},{8,10},{9,11},{10,... | collective-permute-start | bytes 417800 | tf_op jit(solution)/shard_map/ppermute | solution.py:328
  96.2 9.5 %collective-permute-start.13 = (f32[16,2176]{1,0:T(8,128)S(1)}, f32[16,2176]{1,0:T(8,128)S(1)}, u32[]{:S(2)}, u32[]{:S(2)}) collective-permute-start(f32[16,2176]{1,0:T(8,128)S(1)} %get-tuple-element.97), channel_id=1, source_target_pairs={{0,3},{1,2},{2,1},{3,0},{4,7},{5,6},{6,5},{7,4},{8,11},{9,10},{10,... | collective-permute-start | bytes 417800 | tf_op jit(solution)/shard_map/ppermute | solution.py:328
  106.7 4.8 %collective-permute-start.14 = (bf16[16,2176]{1,0:T(8,128)(2,1)S(1)}, bf16[16,2176]{1,0:T(8,128)(2,1)S(1)}, u32[]{:S(2)}, u32[]{:S(2)}) collective-permute-start(bf16[16,2176]{1,0:T(8,128)(2,1)S(1)} %add_convert_fusion), channel_id=1, source_target_pairs={{0,1},{1,0},{2,3},{3,2},{4,5},{5,4},{6,7},{7,6},{8,9},{9,8},{10,11... | collective-permute-start | bytes 208904 | tf_op jit(solution)/shard_map/ppermute | solution.py:328
  108.8 6.0 %collective-permute-start.15 = (bf16[16,2176]{1,0:T(8,128)(2,1)S(1)}, bf16[16,2176]{1,0:T(8,128)(2,1)S(1)}, u32[]{:S(2)}, u32[]{:S(2)}) collective-permute-start(bf16[16,2176]{1,0:T(8,128)(2,1)S(1)} %add_convert_fusion), channel_id=1, source_target_pairs={{0,2},{1,3},{2,0},{3,1},{4,6},{5,7},{6,4},{7,5},{8,10},{9,11},{10,... | collective-permute-start | bytes 208904 | tf_op jit(solution)/shard_map/ppermute | solution.py:328
  109.9 6.2 %collective-permute-start.16 = (bf16[16,2176]{1,0:T(8,128)(2,1)S(1)}, bf16[16,2176]{1,0:T(8,128)(2,1)S(1)}, u32[]{:S(2)}, u32[]{:S(2)}) collective-permute-start(bf16[16,2176]{1,0:T(8,128)(2,1)S(1)} %add_convert_fusion), channel_id=1, source_target_pairs={{0,3},{1,2},{2,1},{3,0},{4,7},{5,6},{6,5},{7,4},{8,11},{9,10},{10,... | collective-permute-start | bytes 208904 | tf_op jit(solution)/shard_map/ppermute | solution.py:328
  116.3 8.3 %collective-permute-start.17 = (bf16[64,2176]{1,0:T(8,128)(2,1)S(1)}, bf16[64,2176]{1,0:T(8,128)(2,1)S(1)}, u32[]{:S(2)}, u32[]{:S(2)}) collective-permute-start(bf16[64,2176]{1,0:T(8,128)(2,1)S(1)} %pad_maximum_fusion.1), channel_id=1, source_target_pairs={{0,16},{4,12},{8,24},{12,4},{16,0},{20,28},{24,8},{28,20},{1,17},{... | collective-permute-start | bytes 835592 | tf_op jit(solution)/shard_map/ppermute | solution.py:395
  124.8 9.6 %collective-permute-start.18 = (bf16[128,2176]{1,0:T(8,128)(2,1)S(1)}, bf16[128,2176]{1,0:T(8,128)(2,1)S(1)}, u32[]{:S(2)}, u32[]{:S(2)}) collective-permute-start(bf16[128,2176]{1,0:T(8,128)(2,1)S(1)} %broadcast_select_fusion), channel_id=1, source_target_pairs={{0,8},{4,20},{8,0},{12,28},{16,24},{20,4},{24,16},{28,12},{1,9},{5... | collective-permute-start | bytes 1671176 | tf_op jit(solution)/shard_map/ppermute | solution.py:395
  125.3 9.4 %copy-start.8 = (s32[1,512]{1,0:T(1,128)S(1)}, s32[1,512]{1,0:T(1,128)}, u32[]{:S(2)}) copy-start(s32[1,512]{1,0:T(1,128)} %get-tuple-element.47.slot_ref) | copy-start | bytes 6148
  134.7 2.8 %collective-permute-start.19 = (bf16[256,2176]{1,0:T(8,128)(2,1)S(1)}, bf16[256,2176]{1,0:T(8,128)(2,1)S(1)}, u32[]{:S(2)}, u32[]{:S(2)}) collective-permute-start(bf16[256,2176]{1,0:T(8,128)(2,1)S(1)} %maximum_select_fusion.own_ref), channel_id=1, source_target_pairs={{0,4},{4,0},{8,12},{12,8},{16,20},{20,16},{24,28},{28,24},{1,5},{5... | collective-permute-start | bytes 3342344 | tf_op jit(solution)/shard_map/ppermute | solution.py:556

commit v6 on v5

--- a/solution.py
+++ b/solution.py
@@ -93,8 +93,8 @@
 
 def forward_kernel(n_seq, capacity, w_hbm, gain_ref, *refs):
     recv, refs = refs[:n_seq], refs[n_seq:]
-    pos_out, xhat_hbm, inv_hbm, normed_hbm, qkv_hbm, attn_out, probs_out = refs[:7]
-    w_ref, xhat_ref, inv_ref, normed_ref, qkv_ref, trans, sems = refs[7:]
+    pos_out, xhat_hbm, inv_hbm, normed_hbm, qkv_hbm, trans_hbm, attn_out, stats_out = refs[:8]
+    w_ref, xhat_ref, inv_ref, normed_ref, qkv_ref, trans, sems = refs[8:]
     width = w_ref.shape[0]
     rows = xhat_ref.shape[0]
     head = width // HEADS
@@ -104,7 +104,13 @@
     saves = [
         pltpu.make_async_copy(source, target, sems.at[1 + i])
         for i, (source, target) in enumerate(
-            ((xhat_ref, xhat_hbm), (inv_ref, inv_hbm), (normed_ref, normed_hbm), (qkv_ref, qkv_hbm))
+            (
+                (xhat_ref, xhat_hbm),
+                (inv_ref, inv_hbm),
+                (normed_ref, normed_hbm),
+                (qkv_ref, qkv_hbm),
+                (trans.at[pl.ds(0, 2 * width)], trans_hbm),
+            )
         )
     ]
 
@@ -131,9 +137,9 @@
         w_copy.wait()
         qkv = mm(normed, w_ref[...])
         qkv_ref[...] = qkv.astype(BF16)
+        trans[...] = jnp.transpose(qkv).astype(BF16)
         for save in saves:
             save.start()
-        trans[...] = jnp.transpose(qkv).astype(BF16)
 
     lo = pl.multiple_of(step * pair, pair)
     keys = qkv_ref[:, pl.ds(pl.multiple_of(width + step * pair, pair), pair)]
@@ -143,9 +149,12 @@
         part = query_t[j * head : (j + 1) * head]
         part = jnp.concatenate([part, zero] if j == 0 else [zero, part], axis=0)
         scores = mm(keys, part)
-        expo = jnp.exp(scores - jnp.max(scores, axis=0, keepdims=True))
-        probs = expo * (1.0 / jnp.sum(expo, axis=0, keepdims=True))
-        probs_out[j] = probs
+        top = jnp.max(scores, axis=0, keepdims=True)
+        expo = jnp.exp(scores - top)
+        share = 1.0 / jnp.sum(expo, axis=0, keepdims=True)
+        probs = expo * share
+        stats_out[pl.ds(2 * step + j, 1), :] = top
+        stats_out[pl.ds(HEADS + 2 * step + j, 1), :] = share
         values_t = trans[pl.ds(pl.multiple_of(2 * width + step * pair + j * head, head), head), :]
         attn_out[j * head : (j + 1) * head, :] = mm(values_t, probs.astype(BF16)).astype(BF16)
 
@@ -155,12 +164,12 @@
             save.wait()
 
 
-def backward_kernel(n_seq, chip_bits, me_ref, pos_ref, w_proj_ref, probs_ref, *refs):
-    (recv_hbm, qkv_hbm, w_hbm, xhat_hbm, normed_hbm, attn_hbm), refs = refs[:6], refs[6:]
+def backward_kernel(n_seq, chip_bits, me_ref, pos_ref, w_proj_ref, stats_ref, *refs):
+    (recv_hbm, qkv_hbm, trans_hbm, w_hbm, xhat_hbm, normed_hbm, attn_hbm), refs = refs[:7], refs[7:]
     outs, serial_grad_hbm, d_normed_hbm, refs = refs[:4], refs[4], refs[5], refs[6:]
-    recv_ref, qkv_ref, w_ref, xhat_ref, normed_ref, attn_ref, refs = *refs[:6], refs[6:]
+    recv_ref, qkv_ref, trans_ref, w_ref, xhat_ref, normed_ref, attn_ref, refs = *refs[:7], refs[7:]
     sums, refs = refs[:4], refs[4:]
-    serial_grad, d_normed_ref, d_attn, d_attn_t, keys_t, d_qkv, normed_t, gain_column, sems = refs
+    serial_grad, d_normed_ref, d_attn, d_attn_t, d_qkv, normed_t, gain_column, sems = refs
     width = w_proj_ref.shape[0]
     rows = xhat_ref.shape[0]
     capacity = recv_ref.shape[0] // n_seq
@@ -174,6 +183,7 @@
             (
                 (recv_hbm, recv_ref),
                 (qkv_hbm, qkv_ref),
+                (trans_hbm, trans_ref),
                 (normed_hbm, normed_ref),
                 (w_hbm, w_ref),
                 (xhat_hbm, xhat_ref),
@@ -182,7 +192,7 @@
         )
     ]
     saves = [
-        pltpu.make_async_copy(source, target, sems.at[6 + i])
+        pltpu.make_async_copy(source, target, sems.at[7 + i])
         for i, (source, target) in enumerate(
             [*zip(sums, outs), (serial_grad, serial_grad_hbm), (d_normed_ref, d_normed_hbm)]
         )
@@ -204,23 +214,29 @@
         d_attn[...] = d_att
         d_attn_t[...] = jnp.transpose(d_att.astype(F32)).astype(BF16)
         loads[1].wait()
-        keys_t[...] = jnp.transpose(qkv_ref[:, width : 2 * width].astype(F32)).astype(BF16)
+        loads[2].wait()
 
     lo = pl.multiple_of(step * pair, pair)
     queries = qkv_ref[:, pl.ds(lo, pair)]
     values = qkv_ref[:, pl.ds(pl.multiple_of(2 * width + step * pair, pair), pair)]
     d_att_t = d_attn_t[pl.ds(lo, pair), :] * BF16(0.125)
     d_att = d_attn[:, pl.ds(lo, pair)]
+    keys = qkv_ref[:, pl.ds(pl.multiple_of(width + step * pair, pair), pair)]
+    query_t = trans_ref[pl.ds(lo, pair), :] * BF16(0.125)
     zero = jnp.zeros((head, rows), BF16)
     d_q, d_k, d_v = [], [], []
     for j in range(2):
-        part = d_att_t[j * head : (j + 1) * head]
-        part = jnp.concatenate([part, zero] if j == 0 else [zero, part], axis=0)
-        probs = probs_ref[j]
-        d_probs = mm(values, part)
+        def alone(both):
+            part = both[j * head : (j + 1) * head]
+            return jnp.concatenate([part, zero] if j == 0 else [zero, part], axis=0)
+
+        top = stats_ref[pl.ds(2 * step + j, 1), :]
+        share = stats_ref[pl.ds(HEADS + 2 * step + j, 1), :]
+        probs = jnp.exp(mm(keys, alone(query_t)) - top) * share
+        d_probs = mm(values, alone(d_att_t))
         total = jnp.sum(d_probs * probs, axis=0, keepdims=True)
         d_scores = (probs * (d_probs - total)).astype(BF16)
-        k_t = keys_t[pl.ds(pl.multiple_of(step * pair + j * head, head), head), :]
+        k_t = trans_ref[pl.ds(pl.multiple_of(width + step * pair + j * head, head), head), :]
         d_q.append(mm(k_t, d_scores))
         d_k.append(mm(d_scores, queries))
         d_v.append(mm(probs.astype(BF16), d_att))
@@ -235,7 +251,7 @@
 
     @pl.when(step == pl.num_programs(0) - 1)
     def _():
-        for load in loads[2:]:
+        for load in loads[3:]:
             load.wait()
         normed_t[...] = jnp.transpose(normed_ref[...].astype(F32)).astype(BF16)
         d_normed = mm(d_qkv[...], w_ref[...], NT)
@@ -455,7 +471,7 @@
     feats_got, grads_sent = lax.optimization_barrier((feats_got, grads_sent))
     grads_got = exchange(grads_sent)
 
-    pos, xhat, inv, normed, qkv, attn_t, probs = pl.pallas_call(
+    pos, xhat, inv, normed, qkv, trans, attn_t, stats = pl.pallas_call(
         functools.partial(forward_kernel, n_seq, capacity),
         grid=(pairs,),
         out_shape=(
@@ -464,16 +480,14 @@
             shape_of((rows, LANES), F32),
             shape_of((rows, width), BF16),
             shape_of((rows, 3 * width), BF16),
+            shape_of((2 * width, rows), BF16),
             shape_of((width, rows), BF16),
-            shape_of((HEADS, rows, rows), F32),
+            shape_of((2 * HEADS, rows), F32),
         ),
         in_specs=[in_hbm, whole((1, width))] + [whole((block, width))] * n_seq,
         out_specs=[whole((1, slots))]
-        + [in_hbm] * 4
-        + [
-            pl.BlockSpec((pair, rows), lambda i: (i, 0)),
-            pl.BlockSpec((2, rows, rows), lambda i: (i, 0, 0)),
-        ],
+        + [in_hbm] * 5
+        + [pl.BlockSpec((pair, rows), lambda i: (i, 0)), whole((2 * HEADS, rows))],
         scratch_shapes=[
             pltpu.VMEM((width, 3 * width), BF16),
             pltpu.VMEM((rows, width), F32),
@@ -481,7 +495,7 @@
             pltpu.VMEM((rows, width), BF16),
             pltpu.VMEM((rows, 3 * width), BF16),
             pltpu.VMEM((3 * width, rows), BF16),
-            pltpu.SemaphoreType.DMA((5,)),
+            pltpu.SemaphoreType.DMA((6,)),
         ],
         compiler_params=params(60),
         cost_estimate=pl.CostEstimate(
@@ -502,13 +516,14 @@
             in_smem,
             whole((1, slots)),
             whole((width, width)),
-            pl.BlockSpec((2, rows, rows), lambda i: (i, 0, 0)),
+            whole((2 * HEADS, rows)),
         ]
-        + [in_hbm] * 6,
+        + [in_hbm] * 7,
         out_specs=[in_hbm] * 6,
         scratch_shapes=[
             pltpu.VMEM((slots, width), BF16),
             pltpu.VMEM((rows, 3 * width), BF16),
+            pltpu.VMEM((2 * width, rows), BF16),
             pltpu.VMEM((width, 3 * width), BF16),
             pltpu.VMEM((rows, width), F32),
             pltpu.VMEM((rows, width), BF16),
@@ -520,20 +535,19 @@
             pltpu.VMEM((rows, width), F32),
             pltpu.VMEM((rows, width), BF16),
             pltpu.VMEM((width, rows), BF16),
-            pltpu.VMEM((width, rows), BF16),
             pltpu.VMEM((rows, 3 * width), BF16),
             pltpu.VMEM((width, rows), BF16),
             pltpu.VMEM((width, LANES), F32),
-            pltpu.SemaphoreType.DMA((12,)),
+            pltpu.SemaphoreType.DMA((13,)),
         ],
         compiler_params=params(60),
         cost_estimate=pl.CostEstimate(
-            flops=12 * rows * width * width + 8 * HEADS * rows * rows * pair,
-            bytes_accessed=24 * MIB,
-            transcendentals=0,
+            flops=12 * rows * width * width + 10 * HEADS * rows * rows * pair,
+            bytes_accessed=16 * MIB,
+            transcendentals=HEADS * rows * rows,
         ),
         name="backward",
-    )(me, pos, w_proj, probs, grads_got, qkv, w_qkv, xhat, normed, attn_t)
+    )(me, pos, w_proj, stats, grads_got, qkv, trans, w_qkv, xhat, normed, attn_t)
 
     steps = chip_steps()
     terms = first_step(quarters, steps)

time: 140 us -> 140 us (level)
  Pallas kernels: 39 us -> 37.5 us
  waiting for transfers between devices: 63.7 us -> 65.2 us
    all_to_all x2, waiting for transfers between devices: 4.34 us -> 5.8 us  [exchange(): got = lax.all_to_all(sent, 'seq', split_axis=0, concat_axis=0, tiled=True)]
    pallas_call x1, Pallas kernels: 11 us -> 9.56 us  [per_device(): pl.pallas_call(functools.partial(forward_kernel, n_seq, capacity), grid=(...]
  transfers between devices with their start and end apart: 22 -> 22, of which waited for: 14 -> 14; matrix products, arithmetic and copies ran while one was open for 3% -> 3% of each run, Pallas kernels for 12% -> 11%
where the time goes in v6:
time: 140 us
  waiting for transfers between devices  65.2 us (47%)
  Pallas kernels  37.5 us (27%)
  starting transfers between devices  28.7 us (20%)
  other arithmetic  4.91 us (4%)
  local copies, waits for them, and re-layouts  2.35 us (2%)
    ppermute x13, waiting for transfers between devices, by_distance(): lax.ppermute(blocks[k], axis, [(i, i ^ k) for i in range(count)])  20.8 us
    ppermute x13, starting transfers between devices, by_distance(): lax.ppermute(blocks[k], axis, [(i, i ^ k) for i in range(count)])  18.3 us
    pallas_call x1, Pallas kernels, per_device(): pl.pallas_call(functools.partial(backward_kernel, n_seq, chip_bits), grid...  17.4 us
    ppermute x2, waiting for transfers between devices, share_in_plane(): other = lax.ppermute(part, 'seq', pairs)  16.9 us
    ppermute x1, waiting for transfers between devices, first_step(): return [keep, lax.ppermute(send, 'seq', steps[0][0])]  14.9 us
    pallas_call x1, Pallas kernels, per_device(): pl.pallas_call(functools.partial(forward_kernel, n_seq, capacity), grid=(...  9.56 us
    all_to_all x2, starting transfers between devices, exchange(): got = lax.all_to_all(sent, 'seq', split_axis=0, concat_axis=0, tiled=True)  7.61 us
    all_to_all x2, waiting for transfers between devices, exchange(): got = lax.all_to_all(sent, 'seq', split_axis=0, concat_axis=0, tiled=True)  5.8 us
  transfers between devices with their start and end apart: 22, of which 14 were waited for; matrix products, arithmetic and copies ran while one was open for 3% of the time, Pallas kernels for 11%

profile of v6, /device:TPU:0, one launch (start us, length us, event | category | flops | bytes accessed | tf_op | source)
XLA Modules:
  0.0 139.5 jit_solution(5582151135733597731)
XLA Ops:
  0.6 3.0 %pack.1 = (s32[1,512]{1,0:T(1,128)}, bf16[144,512]{1,0:T(8,128)(2,1)}, bf16[144,512]{1,0:T(8,128)(2,1)}, bf16[144,512]{1,0:T(8,128)(2,1)}, bf16[144,512]{1,0:T(8...) custom-call(s32[1]{0:T(128)} %bitcast.me_ref, ...), custom_call_target="tpu_custom_call" | custom-call | flops 536870912 | bytes 2097152 | tf_op jit(solution)/shard_map/pack/pallas_call | solution.py:436
  3.7 0.5 collective-permute-start
  4.2 2.6 %collective-permute-start.1 = (bf16[144,512]{1,0:T(8,128)(2,1)}, bf16[144,512]{1,0:T(8,128)(2,1)S(1)}, u32[]{:S(2)}, u32[]{:S(2)}) collective-permute-start(bf16[144,512]{1,0:T(8,128)(2,1)} %get-tuple-element.51), channel_id=1, source_target_pairs={{0,8},{4,12},{8,0},{12,4},{16,24},{20,28},{24,16},{28,20},{1,9},{5... | collective-permute-start | bytes 442376 | tf_op jit(solution)/shard_map/ppermute | solution.py:344
  6.8 1.8 %collective-permute-start.3 = (bf16[144,512]{1,0:T(8,128)(2,1)}, bf16[144,512]{1,0:T(8,128)(2,1)S(1)}, u32[]{:S(2)}, u32[]{:S(2)}) collective-permute-start(bf16[144,512]{1,0:T(8,128)(2,1)} %get-tuple-element.53), channel_id=1, source_target_pairs={{0,16},{4,20},{8,24},{12,28},{16,0},{20,4},{24,8},{28,12},{1,17},{... | collective-permute-start | bytes 442376 | tf_op jit(solution)/shard_map/ppermute | solution.py:344
  8.6 2.6 %collective-permute-start.5 = (bf16[144,512]{1,0:T(8,128)(2,1)}, bf16[144,512]{1,0:T(8,128)(2,1)S(1)}, u32[]{:S(2)}, u32[]{:S(2)}) collective-permute-start(bf16[144,512]{1,0:T(8,128)(2,1)} %get-tuple-element.55), channel_id=1, source_target_pairs={{0,24},{4,28},{8,16},{12,20},{16,8},{20,12},{24,0},{28,4},{1,25},{... | collective-permute-start | bytes 442376 | tf_op jit(solution)/shard_map/ppermute | solution.py:344
  11.2 0.5 collective-permute-done.1.refs_2_
  11.7 1.7 %collective-permute-start.6 = (bf16[144,512]{1,0:T(8,128)(2,1)}, bf16[144,512]{1,0:T(8,128)(2,1)S(1)}, u32[]{:S(2)}, u32[]{:S(2)}) collective-permute-start(bf16[144,512]{1,0:T(8,128)(2,1)} %get-tuple-element.56), channel_id=1, source_target_pairs={{0,28},{4,24},{8,20},{12,16},{16,12},{20,8},{24,4},{28,0},{1,29},{... | collective-permute-start | bytes 442376 | tf_op jit(solution)/shard_map/ppermute | solution.py:344
  13.4 0.7 copy-done.7
  14.1 1.7 %pack_grads.1 = bf16[1024,512]{1,0:T(8,128)(2,1)} custom-call(s32[1]{0:T(128)} %bitcast.me_ref, s32[1,512]{1,0:T(1,128)S(1)} %copy-done.7, bf16[512,512]{1,0:T(8,128)(2,1)S(1)} %bitcast.29), custom_call_target="tpu_custom_call" | custom-call | flops 536870912 | bytes 2097152 | tf_op jit(solution)/shard_map/pack_grads/pallas_call | solution.py:454
  15.8 6.2 %collective-permute-done.4.refs_5_ = bf16[144,512]{1,0:T(8,128)(2,1)S(1)} collective-permute-done((bf16[144,512]{1,0:T(8,128)(2,1)}, bf16[144,512]{1,0:T(8,128)(2,1)S(1)}, u32[]{:S(2)}, u32[]{:S(2)}) %collective-permute-start.4) | collective-permute-done | bytes 147488 | tf_op jit(solution)/shard_map/ppermute | solution.py:344
  22.0 4.0 %all-to-all-start = ((bf16[8,128,512]{2,1,0:T(8,128)(2,1)}), bf16[8,128,512]{2,1,0:T(8,128)(2,1)S(1)}, u32[]{:S(2)}, u32[]{:S(2)}) async-start(bf16[8,128,512]{2,1,0:T(8,128)(2,1)} %bitcast.4), calls=%async_computation | async-start | bytes 2097152 | tf_op jit(solution)/shard_map/all_to_all | solution.py:468
  26.1 9.6 %forward.1 = (s32[1,1024]{1,0:T(1,128)}, f32[512,512]{1,0:T(8,128)}, f32[512,128]{1,0:T(8,128)}, bf16[512,512]{1,0:T(8,128)(2,1)}, bf16[512,1536]{1,0:T(8,128)(2...) custom-call(bf16[512,1536]{1,0:T(8,128)(2,1)} %refs_3_.1, f32[1,512]{1,0:T(1,128)} %bitcast.27, ...), custom_call_target="tpu_custom_call" | custom-call | flops 2952790016 | bytes 16777216 | tf_op jit(solution)/shard_map/forward/pallas_call | solution.py:474
  35.7 5.8 %all-to-all-done = bf16[8,128,512]{2,1,0:T(8,128)(2,1)S(1)} async-done(((bf16[8,128,512]{2,1,0:T(8,128)(2,1)}), bf16[8,128,512]{2,1,0:T(8,128)(2,1)S(1)}, u32[]{:S(2)}, u32[]{:S(2)}) %all-to-all-start) | async-done | bytes 1048608 | tf_op jit(solution)/shard_map/all_to_all | solution.py:468
  41.5 1.0 copy-done.10
  42.5 17.4 %backward.1 = (f32[128,2176]{1,0:T(8,128)}, f32[128,2176]{1,0:T(8,128)}, f32[128,2176]{1,0:T(8,128)}, f32[128,2176]{1,0:T(8,128)}, bf16[512,512]{1,0:T(8,128)(2,1)}, /*index=5*/f32[512,512]{1,0:T(8,128)}) custom-call(s32[1]{0:T(128)} %bitcast.me_ref, s32[1,1024]{1,0:T(1,128)} %get-tuple-element.65.pos_ref, bf16[512,512]{1,0:T(8,128)(2,1)} %w_proj_ref.1, ...), custom_call_target="tpu_custom_call" | custom-call | flops 4294967296 | bytes 16777216 | tf_op jit(solution)/shard_map/backward/pallas_call | solution.py:510
  60.0 0.5 collective-permute-start.7
  60.5 2.5 %collective-permute-done.8 = f32[128,2176]{1,0:T(8,128)S(1)} collective-permute-done((f32[128,2176]{1,0:T(8,128)}, f32[128,2176]{1,0:T(8,128)S(1)}, u32[]{:S(2)}, u32[]{:S(2)}) %collective-permute-start.8) | collective-permute-done | bytes 1114144 | tf_op jit(solution)/shard_map/ppermute | solution.py:379
  63.0 1.5 %add.63 = f32[128,2176]{1,0:T(8,128)S(1)} add(f32[128,2176]{1,0:T(8,128)} %get-tuple-element.76, f32[128,2176]{1,0:T(8,128)S(1)} %collective-permute-done.8) | non-fusion elementwise | flops 278528 | bytes 3342336 | tf_op jit(solution)/shard_map/add | solution.py:379
  64.4 0.6 collective-permute-start.9
  65.1 14.9 %collective-permute-done.9 = f32[128,2176]{1,0:T(8,128)S(1)} collective-permute-done((f32[128,2176]{1,0:T(8,128)S(1)}, f32[128,2176]{1,0:T(8,128)S(1)}, u32[]{:S(2)}, u32[]{:S(2)}) %collective-permute-start.9) | collective-permute-done | bytes 1114144 | tf_op jit(solution)/shard_map/ppermute | solution.py:381
  80.0 0.9 slice_add_fusion.1
  80.9 0.6 collective-permute-start.10
  81.5 0.2 copy-done.1
  81.7 0.1 copy-done.2
  81.9 2.1 %residual.1 = bf16[1024,512]{1,0:T(8,128)(2,1)} custom-call(s32[1]{0:T(128)} %bitcast.me_ref, s32[1,1024]{1,0:T(1,128)S(1)} %copy-done.4, f32[1,512]{1,0:T(1,128)S(1)} %bitcast.28, f32[512,128]{1,0:T(8,128)S(1)} %copy-done.3, f32[512,512]{1,0:T(8,128)S(1)} %copy-done, bf16[512,512]{1,0:T(8,128)(2,1)S(1)} %copy-done.2, f32[512,512]{1,0:T(8,128)S(1)} %copy-done.1), custom_call_target="tpu_custom_call" | custom-call | flops 536870912 | bytes 4194304 | tf_op jit(solution)/shard_map/residual/pallas_call | solution.py:555
  84.0 3.6 %all-to-all-start.1 = ((bf16[8,128,512]{2,1,0:T(8,128)(2,1)}), bf16[8,128,512]{2,1,0:T(8,128)(2,1)S(1)}, u32[]{:S(2)}, u32[]{:S(2)}) async-start(bf16[8,128,512]{2,1,0:T(8,128)(2,1)} %bitcast.6), calls=%async_computation.1 | async-start | bytes 2097152 | tf_op jit(solution)/shard_map/all_to_all | solution.py:468
  87.6 3.2 %collective-permute-done.10 = f32[64,2176]{1,0:T(8,128)} collective-permute-done((f32[64,2176]{1,0:T(8,128)}, f32[64,2176]{1,0:T(8,128)}, u32[]{:S(2)}, u32[]{:S(2)}) %collective-permute-start.10) | collective-permute-done | bytes 557088 | tf_op jit(solution)/shard_map/ppermute | solution.py:386
  90.8 1.1 dynamic-slice_add_fusion.2
  91.9 1.6 %collective-permute-start.11 = (f32[16,2176]{1,0:T(8,128)S(1)}, f32[16,2176]{1,0:T(8,128)S(1)}, u32[]{:S(2)}, u32[]{:S(2)}) collective-permute-start(f32[16,2176]{1,0:T(8,128)S(1)} %get-tuple-element.98), channel_id=1, source_target_pairs={{0,1},{1,0},{2,3},{3,2},{4,5},{5,4},{6,7},{7,6},{8,9},{9,8},{10,11... | collective-permute-start | bytes 417800 | tf_op jit(solution)/shard_map/ppermute | solution.py:344
  93.5 2.6 %collective-permute-start.12 = (f32[16,2176]{1,0:T(8,128)S(1)}, f32[16,2176]{1,0:T(8,128)S(1)}, u32[]{:S(2)}, u32[]{:S(2)}) collective-permute-start(f32[16,2176]{1,0:T(8,128)S(1)} %get-tuple-element.100), channel_id=1, source_target_pairs={{0,2},{1,3},{2,0},{3,1},{4,6},{5,7},{6,4},{7,5},{8,10},{9,11},{10,... | collective-permute-start | bytes 417800 | tf_op jit(solution)/shard_map/ppermute | solution.py:344
  96.1 0.2 collective-permute-start.13
  96.3 1.8 %collective-permute-done.11 = f32[16,2176]{1,0:T(8,128)S(1)} collective-permute-done((f32[16,2176]{1,0:T(8,128)S(1)}, f32[16,2176]{1,0:T(8,128)S(1)}, u32[]{:S(2)}, u32[]{:S(2)}) %collective-permute-start.11) | collective-permute-done | bytes 139296 | tf_op jit(solution)/shard_map/ppermute | solution.py:344
  98.2 7.4 %collective-permute-done.12 = f32[16,2176]{1,0:T(8,128)S(1)} collective-permute-done((f32[16,2176]{1,0:T(8,128)S(1)}, f32[16,2176]{1,0:T(8,128)S(1)}, u32[]{:S(2)}, u32[]{:S(2)}) %collective-permute-start.12) | collective-permute-done | bytes 139296 | tf_op jit(solution)/shard_map/ppermute | solution.py:344
  105.6 1.0 add_convert_fusion
  106.6 2.1 %collective-permute-start.14 = (bf16[16,2176]{1,0:T(8,128)(2,1)S(1)}, bf16[16,2176]{1,0:T(8,128)(2,1)S(1)}, u32[]{:S(2)}, u32[]{:S(2)}) collective-permute-start(bf16[16,2176]{1,0:T(8,128)(2,1)S(1)} %add_convert_fusion), channel_id=1, source_target_pairs={{0,1},{1,0},{2,3},{3,2},{4,5},{5,4},{6,7},{7,6},{8,9},{9,8},{10,11... | collective-permute-start | bytes 208904 | tf_op jit(solution)/shard_map/ppermute | solution.py:344
  108.7 1.1 collective-permute-start.15
  109.8 1.4 collective-permute-start.16
  111.2 0.2 collective-permute-done.14
  111.4 3.3 %collective-permute-done.15 = bf16[16,2176]{1,0:T(8,128)(2,1)S(1)} collective-permute-done((bf16[16,2176]{1,0:T(8,128)(2,1)S(1)}, bf16[16,2176]{1,0:T(8,128)(2,1)S(1)}, u32[]{:S(2)}, u32[]{:S(2)}) %collective-permute-start.15) | collective-permute-done | bytes 69664 | tf_op jit(solution)/shard_map/ppermute | solution.py:344
  114.7 1.4 collective-permute-done.16
  116.2 0.6 collective-permute-start.17
  116.9 7.7 %collective-permute-done.17 = bf16[64,2176]{1,0:T(8,128)(2,1)S(1)} collective-permute-done((bf16[64,2176]{1,0:T(8,128)(2,1)S(1)}, bf16[64,2176]{1,0:T(8,128)(2,1)S(1)}, u32[]{:S(2)}, u32[]{:S(2)}) %collective-permute-start.17) | collective-permute-done | bytes 278560 | tf_op jit(solution)/shard_map/ppermute | solution.py:411
  124.7 0.4 collective-permute-start.18
  125.2 9.2 %collective-permute-done.18 = bf16[128,2176]{1,0:T(8,128)(2,1)S(1)} collective-permute-done((bf16[128,2176]{1,0:T(8,128)(2,1)S(1)}, bf16[128,2176]{1,0:T(8,128)(2,1)S(1)}, u32[]{:S(2)}, u32[]{:S(2)}) %collective-permute-start.18) | collective-permute-done | bytes 557088 | tf_op jit(solution)/shard_map/ppermute | solution.py:411
  134.3 0.2 maximum_select_fusion.own_ref
  134.6 1.5 %unpack.1 = bf16[512,512]{1,0:T(8,128)(2,1)} custom-call(s32[1]{0:T(128)} %bitcast.me_ref, s32[1,512]{1,0:T(1,128)S(1)} %copy-done.8, bf16[1024,512]{1,0:T(8,128)(2,1)S(1)} %bitcast.26), custom_call_target="tpu_custom_call" | custom-call | flops 536870912 | bytes 2097152 | tf_op jit(solution)/shard_map/unpack/pallas_call | solution.py:571
  136.2 1.2 collective-permute-done.19.other_ref
  137.4 2.2 %split.1 = (f32[512,1536]{1,0:T(8,128)}, f32[512,512]{1,0:T(8,128)}, f32[1,512]{1,0:T(1,128)}) custom-call(s32[1]{0:T(128)S(6)} %and.16.side_ref, bf16[256,2176]{1,0:T(8,128)(2,1)S(1)} %maximum_select_fusion.own_ref, bf16[256,2176]{1,0:T(8,128)(2,1)S(1)} %collective-permute-done.19.other_ref), custom_call_target="tpu_custom_call" | custom-call | bytes 8388608 | tf_op jit(solution)/shard_map/split/pallas_call | solution.py:583
  (57 shorter events, 0.8 us)
Async XLA Ops:
  0.6 12.8 %copy-start.6 = (bf16[1,512,512]{2,1,0:T(8,128)(2,1)S(1)}, bf16[1,512,512]{2,1,0:T(8,128)(2,1)}, u32[]{:S(2)}) copy-start(bf16[1,512,512]{2,1,0:T(8,128)(2,1)} %param.7) | copy-start | bytes 1572868
  3.7 4.9 %collective-permute-start = (bf16[144,512]{1,0:T(8,128)(2,1)}, bf16[144,512]{1,0:T(8,128)(2,1)S(1)}, u32[]{:S(2)}, u32[]{:S(2)}) collective-permute-start(bf16[144,512]{1,0:T(8,128)(2,1)} %get-tuple-element.46), channel_id=1, source_target_pairs={{0,4},{4,0},{8,12},{12,8},{16,20},{20,16},{24,28},{28,24},{1,5},{5... | collective-permute-start | bytes 442376 | tf_op jit(solution)/shard_map/ppermute | solution.py:344
  4.2 7.5 %collective-permute-start.1 = (bf16[144,512]{1,0:T(8,128)(2,1)}, bf16[144,512]{1,0:T(8,128)(2,1)S(1)}, u32[]{:S(2)}, u32[]{:S(2)}) collective-permute-start(bf16[144,512]{1,0:T(8,128)(2,1)} %get-tuple-element.51), channel_id=1, source_target_pairs={{0,8},{4,12},{8,0},{12,4},{16,24},{20,28},{24,16},{28,20},{1,9},{5... | collective-permute-start | bytes 442376 | tf_op jit(solution)/shard_map/ppermute | solution.py:344
  6.8 9.0 %collective-permute-start.2 = (bf16[144,512]{1,0:T(8,128)(2,1)}, bf16[144,512]{1,0:T(8,128)(2,1)S(1)}, u32[]{:S(2)}, u32[]{:S(2)}) collective-permute-start(bf16[144,512]{1,0:T(8,128)(2,1)} %get-tuple-element.52), channel_id=1, source_target_pairs={{0,12},{4,8},{8,4},{12,0},{16,28},{20,24},{24,20},{28,16},{1,13},{... | collective-permute-start | bytes 442376 | tf_op jit(solution)/shard_map/ppermute | solution.py:344
  6.8 9.0 %collective-permute-start.3 = (bf16[144,512]{1,0:T(8,128)(2,1)}, bf16[144,512]{1,0:T(8,128)(2,1)S(1)}, u32[]{:S(2)}, u32[]{:S(2)}) collective-permute-start(bf16[144,512]{1,0:T(8,128)(2,1)} %get-tuple-element.53), channel_id=1, source_target_pairs={{0,16},{4,20},{8,24},{12,28},{16,0},{20,4},{24,8},{28,12},{1,17},{... | collective-permute-start | bytes 442376 | tf_op jit(solution)/shard_map/ppermute | solution.py:344
  8.6 13.4 %collective-permute-start.4 = (bf16[144,512]{1,0:T(8,128)(2,1)}, bf16[144,512]{1,0:T(8,128)(2,1)S(1)}, u32[]{:S(2)}, u32[]{:S(2)}) collective-permute-start(bf16[144,512]{1,0:T(8,128)(2,1)} %get-tuple-element.54), channel_id=1, source_target_pairs={{0,20},{4,16},{8,28},{12,24},{16,4},{20,0},{24,12},{28,8},{1,21},{... | collective-permute-start | bytes 442376 | tf_op jit(solution)/shard_map/ppermute | solution.py:344
  8.6 13.4 %copy-start.11 = (bf16[144,512]{1,0:T(8,128)(2,1)}, bf16[144,512]{1,0:T(8,128)(2,1)S(1)}, u32[]{:S(2)}) copy-start(bf16[144,512]{1,0:T(8,128)(2,1)S(1)} %collective-permute-done.refs_1_) | copy-start | bytes 442372
  8.6 13.4 %collective-permute-start.5 = (bf16[144,512]{1,0:T(8,128)(2,1)}, bf16[144,512]{1,0:T(8,128)(2,1)S(1)}, u32[]{:S(2)}, u32[]{:S(2)}) collective-permute-start(bf16[144,512]{1,0:T(8,128)(2,1)} %get-tuple-element.55), channel_id=1, source_target_pairs={{0,24},{4,28},{8,16},{12,20},{16,8},{20,12},{24,0},{28,4},{1,25},{... | collective-permute-start | bytes 442376 | tf_op jit(solution)/shard_map/ppermute | solution.py:344
  11.7 10.4 %copy-start.12 = (bf16[144,512]{1,0:T(8,128)(2,1)}, bf16[144,512]{1,0:T(8,128)(2,1)S(1)}, u32[]{:S(2)}) copy-start(bf16[144,512]{1,0:T(8,128)(2,1)S(1)} %collective-permute-done.1.refs_2_) | copy-start | bytes 442372
  11.7 10.3 %collective-permute-start.6 = (bf16[144,512]{1,0:T(8,128)(2,1)}, bf16[144,512]{1,0:T(8,128)(2,1)S(1)}, u32[]{:S(2)}, u32[]{:S(2)}) collective-permute-start(bf16[144,512]{1,0:T(8,128)(2,1)} %get-tuple-element.56), channel_id=1, source_target_pairs={{0,28},{4,24},{8,20},{12,16},{16,12},{20,8},{24,4},{28,0},{1,29},{... | collective-permute-start | bytes 442376 | tf_op jit(solution)/shard_map/ppermute | solution.py:344
  13.4 0.7 copy-start.7
  15.8 10.3 %copy-start.13 = (bf16[144,512]{1,0:T(8,128)(2,1)}, bf16[144,512]{1,0:T(8,128)(2,1)S(1)}, u32[]{:S(2)}) copy-start(bf16[144,512]{1,0:T(8,128)(2,1)S(1)} %collective-permute-done.2.refs_3_) | copy-start | bytes 442372
  15.8 10.3 %copy-start.14 = (bf16[144,512]{1,0:T(8,128)(2,1)}, bf16[144,512]{1,0:T(8,128)(2,1)S(1)}, u32[]{:S(2)}) copy-start(bf16[144,512]{1,0:T(8,128)(2,1)S(1)} %collective-permute-done.3.refs_4_) | copy-start | bytes 442372
  22.0 4.1 %copy-start.15 = (bf16[144,512]{1,0:T(8,128)(2,1)}, bf16[144,512]{1,0:T(8,128)(2,1)S(1)}, u32[]{:S(2)}) copy-start(bf16[144,512]{1,0:T(8,128)(2,1)S(1)} %collective-permute-done.4.refs_5_) | copy-start | bytes 442372
  22.0 4.1 %copy-start.16 = (bf16[144,512]{1,0:T(8,128)(2,1)}, bf16[144,512]{1,0:T(8,128)(2,1)S(1)}, u32[]{:S(2)}) copy-start(bf16[144,512]{1,0:T(8,128)(2,1)S(1)} %collective-permute-done.5.refs_6_) | copy-start | bytes 442372
  22.0 4.1 %copy-start.17 = (bf16[144,512]{1,0:T(8,128)(2,1)}, bf16[144,512]{1,0:T(8,128)(2,1)S(1)}, u32[]{:S(2)}) copy-start(bf16[144,512]{1,0:T(8,128)(2,1)S(1)} %collective-permute-done.6.refs_7_) | copy-start | bytes 442372
  22.0 19.5 %all-to-all-start = ((bf16[8,128,512]{2,1,0:T(8,128)(2,1)}), bf16[8,128,512]{2,1,0:T(8,128)(2,1)S(1)}, u32[]{:S(2)}, u32[]{:S(2)}) async-start(bf16[8,128,512]{2,1,0:T(8,128)(2,1)} %bitcast.4), calls=%async_computation | async-start | bytes 2097152 | tf_op jit(solution)/shard_map/all_to_all | solution.py:468
  41.5 1.0 copy-start.10
  59.9 3.0 %collective-permute-start.8 = (f32[128,2176]{1,0:T(8,128)}, f32[128,2176]{1,0:T(8,128)S(1)}, u32[]{:S(2)}, u32[]{:S(2)}) collective-permute-start(f32[128,2176]{1,0:T(8,128)} %get-tuple-element.77), channel_id=1, source_target_pairs={{0,4},{4,0},{8,12},{12,8},{16,20},{20,16},{24,28},{28,24},{1,5},{5... | collective-permute-start | bytes 3342344 | tf_op jit(solution)/shard_map/ppermute | solution.py:379
  60.0 5.0 %collective-permute-start.7 = (f32[128,2176]{1,0:T(8,128)}, f32[128,2176]{1,0:T(8,128)S(1)}, u32[]{:S(2)}, u32[]{:S(2)}) collective-permute-start(f32[128,2176]{1,0:T(8,128)} %get-tuple-element.75), channel_id=1, source_target_pairs={{0,4},{4,0},{8,12},{12,8},{16,20},{20,16},{24,28},{28,24},{1,5},{5... | collective-permute-start | bytes 3342344 | tf_op jit(solution)/shard_map/ppermute | solution.py:380
  63.0 2.0 %copy-start.9 = (f32[128,2176]{1,0:T(8,128)S(1)}, f32[128,2176]{1,0:T(8,128)}, u32[]{:S(2)}) copy-start(f32[128,2176]{1,0:T(8,128)} %get-tuple-element.74) | copy-start | bytes 3342340
  64.4 15.6 %collective-permute-start.9 = (f32[128,2176]{1,0:T(8,128)S(1)}, f32[128,2176]{1,0:T(8,128)S(1)}, u32[]{:S(2)}, u32[]{:S(2)}) collective-permute-start(f32[128,2176]{1,0:T(8,128)S(1)} %add.63), channel_id=1, source_target_pairs={{0,8},{4,20},{8,0},{12,28},{16,24},{20,4},{24,16},{28,12},{1,9},{5... | collective-permute-start | bytes 3342344 | tf_op jit(solution)/shard_map/ppermute | solution.py:381
  80.0 1.5 %copy-start = (f32[512,512]{1,0:T(8,128)S(1)}, f32[512,512]{1,0:T(8,128)}, u32[]{:S(2)}) copy-start(f32[512,512]{1,0:T(8,128)} %get-tuple-element.70.refs_4_.xhat_ref) | copy-start | bytes 3145732
  80.0 1.7 %copy-start.1 = (f32[512,512]{1,0:T(8,128)S(1)}, f32[512,512]{1,0:T(8,128)}, u32[]{:S(2)}) copy-start(f32[512,512]{1,0:T(8,128)} %get-tuple-element.82.d_normed_ref) | copy-start | bytes 3145732
  80.0 1.9 %copy-start.2 = (bf16[512,512]{1,0:T(8,128)(2,1)S(1)}, bf16[512,512]{1,0:T(8,128)(2,1)}, u32[]{:S(2)}) copy-start(bf16[512,512]{1,0:T(8,128)(2,1)} %get-tuple-element.81.serial_grad_ref) | copy-start | bytes 1572868
  80.0 1.9 %copy-start.3 = (f32[512,128]{1,0:T(8,128)S(1)}, f32[512,128]{1,0:T(8,128)}, u32[]{:S(2)}) copy-start(f32[512,128]{1,0:T(8,128)} %get-tuple-element.80.inv_ref) | copy-start | bytes 786436
  80.0 1.9 %copy-start.4 = (s32[1,1024]{1,0:T(1,128)S(1)}, s32[1,1024]{1,0:T(1,128)}, u32[]{:S(2)}) copy-start(s32[1,1024]{1,0:T(1,128)} %get-tuple-element.65.pos_ref) | copy-start | bytes 12292
  80.0 1.9 %copy-start.5 = (f32[512]{0:T(512)S(1)}, f32[512]{0:T(512)}, u32[]{:S(2)}) copy-start(f32[512]{0:T(512)} %param.11) | copy-start | bytes 6148
  80.9 9.8 %collective-permute-start.10 = (f32[64,2176]{1,0:T(8,128)}, f32[64,2176]{1,0:T(8,128)}, u32[]{:S(2)}, u32[]{:S(2)}) collective-permute-start(f32[64,2176]{1,0:T(8,128)} %get-tuple-element.97), channel_id=1, source_target_pairs={{0,16},{4,12},{8,24},{12,4},{16,0},{20,28},{24,8},{28,20},{1,17},{... | collective-permute-start | bytes 1671176 | tf_op jit(solution)/shard_map/ppermute | solution.py:386
  84.0 22.6 %all-to-all-start.1 = ((bf16[8,128,512]{2,1,0:T(8,128)(2,1)}), bf16[8,128,512]{2,1,0:T(8,128)(2,1)S(1)}, u32[]{:S(2)}, u32[]{:S(2)}) async-start(bf16[8,128,512]{2,1,0:T(8,128)(2,1)} %bitcast.6), calls=%async_computation.1 | async-start | bytes 2097152 | tf_op jit(solution)/shard_map/all_to_all | solution.py:468
  91.9 6.3 %collective-permute-start.11 = (f32[16,2176]{1,0:T(8,128)S(1)}, f32[16,2176]{1,0:T(8,128)S(1)}, u32[]{:S(2)}, u32[]{:S(2)}) collective-permute-start(f32[16,2176]{1,0:T(8,128)S(1)} %get-tuple-element.98), channel_id=1, source_target_pairs={{0,1},{1,0},{2,3},{3,2},{4,5},{5,4},{6,7},{7,6},{8,9},{9,8},{10,11... | collective-permute-start | bytes 417800 | tf_op jit(solution)/shard_map/ppermute | solution.py:344
  93.5 12.1 %collective-permute-start.12 = (f32[16,2176]{1,0:T(8,128)S(1)}, f32[16,2176]{1,0:T(8,128)S(1)}, u32[]{:S(2)}, u32[]{:S(2)}) collective-permute-start(f32[16,2176]{1,0:T(8,128)S(1)} %get-tuple-element.100), channel_id=1, source_target_pairs={{0,2},{1,3},{2,0},{3,1},{4,6},{5,7},{6,4},{7,5},{8,10},{9,11},{10,... | collective-permute-start | bytes 417800 | tf_op jit(solution)/shard_map/ppermute | solution.py:344
  96.1 9.5 %collective-permute-start.13 = (f32[16,2176]{1,0:T(8,128)S(1)}, f32[16,2176]{1,0:T(8,128)S(1)}, u32[]{:S(2)}, u32[]{:S(2)}) collective-permute-start(f32[16,2176]{1,0:T(8,128)S(1)} %get-tuple-element.99), channel_id=1, source_target_pairs={{0,3},{1,2},{2,1},{3,0},{4,7},{5,6},{6,5},{7,4},{8,11},{9,10},{10,... | collective-permute-start | bytes 417800 | tf_op jit(solution)/shard_map/ppermute | solution.py:344
  106.6 4.8 %collective-permute-start.14 = (bf16[16,2176]{1,0:T(8,128)(2,1)S(1)}, bf16[16,2176]{1,0:T(8,128)(2,1)S(1)}, u32[]{:S(2)}, u32[]{:S(2)}) collective-permute-start(bf16[16,2176]{1,0:T(8,128)(2,1)S(1)} %add_convert_fusion), channel_id=1, source_target_pairs={{0,1},{1,0},{2,3},{3,2},{4,5},{5,4},{6,7},{7,6},{8,9},{9,8},{10,11... | collective-permute-start | bytes 208904 | tf_op jit(solution)/shard_map/ppermute | solution.py:344
  108.7 6.0 %collective-permute-start.15 = (bf16[16,2176]{1,0:T(8,128)(2,1)S(1)}, bf16[16,2176]{1,0:T(8,128)(2,1)S(1)}, u32[]{:S(2)}, u32[]{:S(2)}) collective-permute-start(bf16[16,2176]{1,0:T(8,128)(2,1)S(1)} %add_convert_fusion), channel_id=1, source_target_pairs={{0,2},{1,3},{2,0},{3,1},{4,6},{5,7},{6,4},{7,5},{8,10},{9,11},{10,... | collective-permute-start | bytes 208904 | tf_op jit(solution)/shard_map/ppermute | solution.py:344
  109.8 6.2 %collective-permute-start.16 = (bf16[16,2176]{1,0:T(8,128)(2,1)S(1)}, bf16[16,2176]{1,0:T(8,128)(2,1)S(1)}, u32[]{:S(2)}, u32[]{:S(2)}) collective-permute-start(bf16[16,2176]{1,0:T(8,128)(2,1)S(1)} %add_convert_fusion), channel_id=1, source_target_pairs={{0,3},{1,2},{2,1},{3,0},{4,7},{5,6},{6,5},{7,4},{8,11},{9,10},{10,... | collective-permute-start | bytes 208904 | tf_op jit(solution)/shard_map/ppermute | solution.py:344
  116.2 8.3 %collective-permute-start.17 = (bf16[64,2176]{1,0:T(8,128)(2,1)S(1)}, bf16[64,2176]{1,0:T(8,128)(2,1)S(1)}, u32[]{:S(2)}, u32[]{:S(2)}) collective-permute-start(bf16[64,2176]{1,0:T(8,128)(2,1)S(1)} %pad_maximum_fusion.1), channel_id=1, source_target_pairs={{0,16},{4,12},{8,24},{12,4},{16,0},{20,28},{24,8},{28,20},{1,17},{... | collective-permute-start | bytes 835592 | tf_op jit(solution)/shard_map/ppermute | solution.py:411
  124.7 9.6 %collective-permute-start.18 = (bf16[128,2176]{1,0:T(8,128)(2,1)S(1)}, bf16[128,2176]{1,0:T(8,128)(2,1)S(1)}, u32[]{:S(2)}, u32[]{:S(2)}) collective-permute-start(bf16[128,2176]{1,0:T(8,128)(2,1)S(1)} %broadcast_select_fusion), channel_id=1, source_target_pairs={{0,8},{4,20},{8,0},{12,28},{16,24},{20,4},{24,16},{28,12},{1,9},{5... | collective-permute-start | bytes 1671176 | tf_op jit(solution)/shard_map/ppermute | solution.py:411
  125.2 9.5 %copy-start.8 = (s32[1,512]{1,0:T(1,128)S(1)}, s32[1,512]{1,0:T(1,128)}, u32[]{:S(2)}) copy-start(s32[1,512]{1,0:T(1,128)} %get-tuple-element.48.slot_ref) | copy-start | bytes 6148
  134.6 2.8 %collective-permute-start.19 = (bf16[256,2176]{1,0:T(8,128)(2,1)S(1)}, bf16[256,2176]{1,0:T(8,128)(2,1)S(1)}, u32[]{:S(2)}, u32[]{:S(2)}) collective-permute-start(bf16[256,2176]{1,0:T(8,128)(2,1)S(1)} %maximum_select_fusion.own_ref), channel_id=1, source_target_pairs={{0,4},{4,0},{8,12},{12,8},{16,20},{20,16},{24,28},{28,24},{1,5},{5... | collective-permute-start | bytes 3342344 | tf_op jit(solution)/shard_map/ppermute | solution.py:570

commit v7 on v6

--- a/solution.py
+++ b/solution.py
@@ -11,6 +11,9 @@
 PATCH = 512
 EXTRA = 16
 LANES = 128
+BOUND = 1
+EXPONENT = 2
+HEADROOM = 10.0
 MIB = 1024 * 1024
 F32 = jnp.float32
 BF16 = jnp.bfloat16
@@ -276,12 +279,23 @@
             (odd * 2 + mine, mine_next),
         )
         for out, (start, side), save in zip(sums, starts, saves):
+            bound = jnp.full((1, 1), 0.0, F32)
             for j, half in enumerate((1 - side, side)):
                 part = pl.ds(pl.multiple_of((start * 2 + half) * eighth, eighth), eighth)
                 lines = slice(j * eighth, (j + 1) * eighth)
-                out[lines, : 3 * width] = mm(normed_t[part, :], d_qkv[...])
-                out[lines, 3 * width : 4 * width] = mm(attn_ref[part, :], serial_grad[...])
-                out[lines, 4 * width :] = gain_column[part, :]
+                blocks = (
+                    mm(normed_t[part, :], d_qkv[...]),
+                    mm(attn_ref[part, :], serial_grad[...]),
+                    gain_column[part, :],
+                )
+                column = 0
+                for block in blocks:
+                    out[lines, column : column + block.shape[1]] = block
+                    column += block.shape[1]
+                    largest = jnp.max(jnp.abs(block), axis=0, keepdims=True)
+                    bound = jnp.maximum(bound, jnp.max(largest, axis=1, keepdims=True))
+            lane = iota((2 * eighth, LANES), 1)
+            out[:, 4 * width :] = jnp.where(lane == BOUND, bound, out[:, 4 * width :])
             save.start()
         for save in saves:
             save.wait()
@@ -365,9 +379,31 @@
     return steps
 
 
+def encode(total, bound):
+    exponent = jnp.clip(jnp.ceil(jnp.log2(bound)), -100.0, 100.0)
+    lane = lax.broadcasted_iota(jnp.int32, total.shape, 1) - (total.shape[1] - LANES)
+    scaled = total * jnp.exp2(HEADROOM - exponent)
+    return jnp.where(lane == EXPONENT, exponent, scaled).astype(jnp.float16)
+
+
+def decode(message):
+    exponent = message[0, message.shape[1] - LANES + EXPONENT].astype(F32)
+    return message, jnp.exp2(exponent - HEADROOM)
+
+
+def bound_of(terms):
+    return sum(array[0, array.shape[1] - LANES + BOUND].astype(F32) * factor for array, factor in terms)
+
+
 def piece(terms, index, count):
-    size = terms[0].shape[0] // count
-    return functools.reduce(jnp.add, [lax.dynamic_slice_in_dim(t, index * size, size) for t in terms])
+    size = terms[0][0].shape[0] // count
+
+    def cut(array):
+        if isinstance(index, int):
+            return array[index * size : (index + 1) * size]
+        return lax.dynamic_slice_in_dim(array, index * size, size)
+
+    return functools.reduce(jnp.add, [cut(array).astype(F32) * factor for array, factor in terms])
 
 
 def core_pairs():
@@ -376,25 +412,28 @@
 
 def first_step(quarters, steps):
     pass_on, pass_keep, own_on, own_keep = quarters
-    send = own_on + lax.ppermute(pass_on, "seq", core_pairs())
+    got = lax.ppermute(pass_on, "seq", core_pairs())
+    send = encode(own_on + got, bound_of([(own_on, 1.0), (got, 1.0)]))
     keep = own_keep + lax.ppermute(pass_keep, "seq", core_pairs())
-    return [keep, lax.ppermute(send, "seq", steps[0][0])]
+    return [(keep, 1.0), decode(lax.ppermute(send, "seq", steps[0][0]))]
 
 
 def next_steps(terms, steps):
-    half = terms[0].shape[0] // 2
-    got = lax.ppermute(terms[0][:half] + terms[1][:half], "seq", steps[1][0])
-    terms = [terms[0][half:] + terms[1][half:], got]
-    for pairs, side in steps[2:]:
-        got = lax.ppermute(piece(terms, 1 - side, 2), "seq", pairs)
-        terms = [piece(terms, side, 2), got]
+    for i, (pairs, side) in enumerate(steps[1:]):
+        on, stay = (0, 1) if i == 0 else (1 - side, side)
+        send = encode(piece(terms, on, 2), bound_of(terms))
+        keep = piece(terms, stay, 2)
+        terms = [(keep, 1.0), decode(lax.ppermute(send, "seq", pairs))]
     return terms
 
 
 def reduce_over_planes(terms):
     n_dp, plane = lax.axis_size("dp"), lax.axis_index("dp")
-    pieces = [piece(terms, lax.bitwise_xor(plane, k), n_dp) for k in range(n_dp)]
-    return functools.reduce(jnp.add, by_distance(pieces, "dp")).astype(BF16)
+    bound = bound_of(terms)
+    own = piece(terms, plane, n_dp)
+    sent = [encode(piece(terms, lax.bitwise_xor(plane, k), n_dp), bound) for k in range(1, n_dp)]
+    got = [decode(message) for message in by_distance([None] + sent, "dp")[1:]]
+    return piece([(own, 1.0)] + got, 0, 1).astype(BF16)
 
 
 def share_over_planes(part):
@@ -468,7 +507,6 @@
         got = lax.all_to_all(sent, "seq", split_axis=0, concat_axis=0, tiled=True)
         return got.reshape(slots, width)
 
-    feats_got, grads_sent = lax.optimization_barrier((feats_got, grads_sent))
     grads_got = exchange(grads_sent)
 
     pos, xhat, inv, normed, qkv, trans, attn_t, stats = pl.pallas_call(

time: 140 us -> 152 us (1.086)
  local copies, waits for them, and re-layouts: 2.35 us -> 11.2 us
  waiting for transfers between devices: 65.2 us -> 57.1 us
  between operations: 0.89 us -> 8.58 us
  starting transfers between devices: 28.7 us -> 30.4 us
  other arithmetic: 4.91 us -> 6.51 us
    ppermute x13, waiting for transfers between devices: 20.8 us -> 31.5 us  [by_distance(): lax.ppermute(blocks[k], axis, [(i, i ^ k) for i in range(count)])]
    ppermute x3, waiting for transfers between devices: 20.6 us -> 10.1 us  [the longest x1 8.9 us: first_step(): return [(keep, 1.0), decode(lax.ppermute(send, 'seq', steps[0][0]))]]
    slice x0 -> x10, local copies, waits for them, and re-layouts: none -> 8.63 us  [the longest x5 4.37 us: decode(): exponent = message[0, message.shape[1] - LANES + EXPONENT].astype(F32)]
    all_to_all x2, waiting for transfers between devices: 5.8 us -> 0.01 us  [exchange(): got = lax.all_to_all(sent, 'seq', split_axis=0, concat_axis=0, tiled=True)]
    convert_element_type x1 -> x4, other arithmetic: 0.97 us -> 5.99 us  [the longest x3 5.03 us: encode(): return jnp.where(lane == EXPONENT, exponent, scaled).astype(jnp.float16)]
    add x3 -> x0, other arithmetic: 3.47 us -> none  [the longest x1 1.46 us: first_step(): send = own_on + lax.ppermute(pass_on, 'seq', core_pairs())]
    ppermute x2, waiting for transfers between devices: 16.9 us -> 14.3 us  [share_in_plane(): other = lax.ppermute(part, 'seq', pairs)]
    ppermute x2, starting transfers between devices: 1.03 us -> 3.58 us  [share_in_plane(): other = lax.ppermute(part, 'seq', pairs)]
  transfers between devices with their start and end apart: 22 -> 22, of which waited for: 14 -> 14; matrix products, arithmetic and copies ran while one was open for 3% -> 6% of each run, Pallas kernels for 11% -> 9%
where the time goes in v7:
time: 152 us; the launch traced here: 151 us
  waiting for transfers between devices  57.1 us (38%)
  Pallas kernels  37.7 us (25%)
  starting transfers between devices  30.4 us (20%)
  local copies, waits for them, and re-layouts  11.2 us (7%)
  between operations  8.58 us (6%)
  other arithmetic  6.51 us (4%)
    ppermute x13, waiting for transfers between devices, by_distance(): lax.ppermute(blocks[k], axis, [(i, i ^ k) for i in range(count)])  31.5 us
    pallas_call x1, Pallas kernels, per_device(): pl.pallas_call(functools.partial(backward_kernel, n_seq, chip_bits), grid...  17.6 us
    ppermute x13, starting transfers between devices, by_distance(): lax.ppermute(blocks[k], axis, [(i, i ^ k) for i in range(count)])  16.1 us
    ppermute x2, waiting for transfers between devices, share_in_plane(): other = lax.ppermute(part, 'seq', pairs)  14.3 us
    pallas_call x1, Pallas kernels, per_device(): pl.pallas_call(functools.partial(forward_kernel, n_seq, capacity), grid=(...  9.52 us
    all_to_all x2, starting transfers between devices, exchange(): got = lax.all_to_all(sent, 'seq', split_axis=0, concat_axis=0, tiled=True)  8.97 us
    ppermute x1, waiting for transfers between devices, first_step(): return [(keep, 1.0), decode(lax.ppermute(send, 'seq', steps[0][0]))]  8.9 us
    convert_element_type x3, other arithmetic, encode(): return jnp.where(lane == EXPONENT, exponent, scaled).astype(jnp.float16)  5.03 us
  transfers between devices with their start and end apart: 22, of which 14 were waited for; matrix products, arithmetic and copies ran while one was open for 6% of the time, Pallas kernels for 9%

profile of v7, /device:TPU:0, one launch (start us, length us, event | category | flops | bytes accessed | tf_op | source)
XLA Modules:
  0.0 151.5 jit_solution(9081292726891528268)
XLA Ops:
  0.6 3.0 %pack.1 = (s32[1,512]{1,0:T(1,128)}, bf16[144,512]{1,0:T(8,128)(2,1)}, bf16[144,512]{1,0:T(8,128)(2,1)}, bf16[144,512]{1,0:T(8,128)(2,1)}, bf16[144,512]{1,0:T(8...) custom-call(s32[1]{0:T(128)} %bitcast.me_ref, ...), custom_call_target="tpu_custom_call" | custom-call | flops 536870912 | bytes 2097152 | tf_op jit(solution)/shard_map/pack/pallas_call | solution.py:475
  4.2 1.2 collective-permute-done.refs_1_
  5.4 0.7 copy-done.7
  6.1 1.7 %pack_grads.1 = bf16[1024,512]{1,0:T(8,128)(2,1)} custom-call(s32[1]{0:T(128)} %bitcast.me_ref, s32[1,512]{1,0:T(1,128)S(1)} %copy-done.7, bf16[512,512]{1,0:T(8,128)(2,1)S(1)} %bitcast.41), custom_call_target="tpu_custom_call" | custom-call | flops 536870912 | bytes 2097152 | tf_op jit(solution)/shard_map/pack_grads/pallas_call | solution.py:493
  7.9 5.2 %all-to-all-start = ((bf16[8,128,512]{2,1,0:T(8,128)(2,1)}), bf16[8,128,512]{2,1,0:T(8,128)(2,1)S(1)}, u32[]{:S(2)}, u32[]{:S(2)}) async-start(bf16[8,128,512]{2,1,0:T(8,128)(2,1)} %bitcast.4), calls=%async_computation | async-start | bytes 2097152 | tf_op jit(solution)/shard_map/all_to_all | solution.py:507
  13.1 2.0 %collective-permute-start.1 = (bf16[144,512]{1,0:T(8,128)(2,1)S(1)}, bf16[144,512]{1,0:T(8,128)(2,1)S(1)}, u32[]{:S(2)}, u32[]{:S(2)}) collective-permute-start(bf16[144,512]{1,0:T(8,128)(2,1)S(1)} %copy-done.23), channel_id=1, source_target_pairs={{0,8},{4,12},{8,0},{12,4},{16,24},{20,28},{24,16},{28,20},{1,9},{5... | collective-permute-start | bytes 442376 | tf_op jit(solution)/shard_map/ppermute | solution.py:358
  15.1 1.5 %collective-permute-start.3 = (bf16[144,512]{1,0:T(8,128)(2,1)S(1)}, bf16[144,512]{1,0:T(8,128)(2,1)S(1)}, u32[]{:S(2)}, u32[]{:S(2)}) collective-permute-start(bf16[144,512]{1,0:T(8,128)(2,1)S(1)} %copy-done.18), channel_id=1, source_target_pairs={{0,16},{4,20},{8,24},{12,28},{16,0},{20,4},{24,8},{28,12},{1,17},{... | collective-permute-start | bytes 442376 | tf_op jit(solution)/shard_map/ppermute | solution.py:358
  17.0 2.6 %collective-permute-start.5 = (bf16[144,512]{1,0:T(8,128)(2,1)S(1)}, bf16[144,512]{1,0:T(8,128)(2,1)S(1)}, u32[]{:S(2)}, u32[]{:S(2)}) collective-permute-start(bf16[144,512]{1,0:T(8,128)(2,1)S(1)} %copy-done.14), channel_id=1, source_target_pairs={{0,24},{4,28},{8,16},{12,20},{16,8},{20,12},{24,0},{28,4},{1,25},{... | collective-permute-start | bytes 442376 | tf_op jit(solution)/shard_map/ppermute | solution.py:358
  19.5 11.8 %collective-permute-done.1.refs_2_ = bf16[144,512]{1,0:T(8,128)(2,1)S(1)} collective-permute-done((bf16[144,512]{1,0:T(8,128)(2,1)S(1)}, bf16[144,512]{1,0:T(8,128)(2,1)S(1)}, u32[]{:S(2)}, u32[]{:S(2)}) %collective-permute-start.1) | collective-permute-done | bytes 147488 | tf_op jit(solution)/shard_map/ppermute | solution.py:358
  31.5 2.0 %collective-permute-done.2.refs_3_ = bf16[144,512]{1,0:T(8,128)(2,1)S(1)} collective-permute-done((bf16[144,512]{1,0:T(8,128)(2,1)S(1)}, bf16[144,512]{1,0:T(8,128)(2,1)S(1)}, u32[]{:S(2)}, u32[]{:S(2)}) %collective-permute-start.2) | collective-permute-done | bytes 147488 | tf_op jit(solution)/shard_map/ppermute | solution.py:358
  33.5 5.0 %collective-permute-done.5.refs_6_ = bf16[144,512]{1,0:T(8,128)(2,1)S(1)} collective-permute-done((bf16[144,512]{1,0:T(8,128)(2,1)S(1)}, bf16[144,512]{1,0:T(8,128)(2,1)S(1)}, u32[]{:S(2)}, u32[]{:S(2)}) %collective-permute-start.5) | collective-permute-done | bytes 147488 | tf_op jit(solution)/shard_map/ppermute | solution.py:358
  38.5 2.2 %collective-permute-done.6.refs_7_ = bf16[144,512]{1,0:T(8,128)(2,1)S(1)} collective-permute-done((bf16[144,512]{1,0:T(8,128)(2,1)S(1)}, bf16[144,512]{1,0:T(8,128)(2,1)S(1)}, u32[]{:S(2)}, u32[]{:S(2)}) %collective-permute-start.6) | collective-permute-done | bytes 147488 | tf_op jit(solution)/shard_map/ppermute | solution.py:358
  40.8 0.6 copy-done.24
  41.4 9.5 %forward.1 = (s32[1,1024]{1,0:T(1,128)}, f32[512,512]{1,0:T(8,128)}, f32[512,128]{1,0:T(8,128)}, bf16[512,512]{1,0:T(8,128)(2,1)}, bf16[512,1536]{1,0:T(8,128)(2...) custom-call(bf16[512,1536]{1,0:T(8,128)(2,1)} %refs_3_.1, f32[1,512]{1,0:T(1,128)} %bitcast.39, ...), custom_call_target="tpu_custom_call" | custom-call | flops 2952790016 | bytes 16777216 | tf_op jit(solution)/shard_map/forward/pallas_call | solution.py:512
  50.9 1.0 copy-done.11
  51.9 17.6 %backward.1 = (f32[128,2176]{1,0:T(8,128)}, f32[128,2176]{1,0:T(8,128)}, f32[128,2176]{1,0:T(8,128)}, f32[128,2176]{1,0:T(8,128)}, bf16[512,512]{1,0:T(8,128)(2,1)}, /*index=5*/f32[512,512]{1,0:T(8,128)}) custom-call(s32[1]{0:T(128)} %bitcast.me_ref, s32[1,1024]{1,0:T(1,128)} %get-tuple-element.50.pos_ref, bf16[512,512]{1,0:T(8,128)(2,1)} %w_proj_ref.1, ...), custom_call_target="tpu_custom_call" | custom-call | flops 4294967296 | bytes 16777216 | tf_op jit(solution)/shard_map/backward/pallas_call | solution.py:548
  69.9 1.3 slice.45
  71.4 1.2 collective-permute-done.8
  74.6 1.5 select_convert_fusion
  76.1 0.6 collective-permute-start.9
  76.9 8.9 %collective-permute-done.9 = f16[128,2176]{1,0:T(8,128)(2,1)} collective-permute-done((f16[128,2176]{1,0:T(8,128)(2,1)S(1)}, f16[128,2176]{1,0:T(8,128)(2,1)}, u32[]{:S(2)}, u32[]{:S(2)}) %collective-permute-start.9) | collective-permute-done | bytes 557088 | tf_op jit(solution)/shard_map/ppermute | solution.py:418
  85.8 1.3 slice.61
  87.8 1.3 slice.51
  89.7 0.6 slice.50
  91.1 2.5 %select_convert_fusion.1 = (f16[64,2176]{1,0:T(8,128)(2,1)}, f32[64,2176]{1,0:T(8,128)S(1)}) fusion(f32[128,2176]{1,0:T(8,128)} %copy-done.9, f32[]{:T(128)S(6)} %exp2.78, f16[128,2176]{1,0:T(8,128)(2,1)} %collective-permute-done.9, f32[]{:T(128)S(6)} %min.13, f32[]{:T(128)} %bitcast.7, f32[]{:T(128)} %constant.56.clone.1, pred[2176]{0:T(1024)(128)(4,1)S(1)} %add_compare_fusion), kind=kLoop, calls=%fused_computation.2 | loop fusion | flops 1531904 | bytes 2508944 | tf_op jit(solution)/shard_map/convert_element_type | solution.py:386
  94.1 2.0 %residual.1 = bf16[1024,512]{1,0:T(8,128)(2,1)} custom-call(s32[1]{0:T(128)} %bitcast.me_ref, s32[1,1024]{1,0:T(1,128)S(1)} %copy-done.4, f32[1,512]{1,0:T(1,128)S(1)} %bitcast.40, f32[512,128]{1,0:T(8,128)S(1)} %copy-done.3, f32[512,512]{1,0:T(8,128)S(1)} %copy-done, bf16[512,512]{1,0:T(8,128)(2,1)S(1)} %copy-done.2, f32[512,512]{1,0:T(8,128)S(1)} %copy-done.1), custom_call_target="tpu_custom_call" | custom-call | flops 536870912 | bytes 4194304 | tf_op jit(solution)/shard_map/residual/pallas_call | solution.py:593
  96.1 3.7 %all-to-all-start.1 = ((bf16[8,128,512]{2,1,0:T(8,128)(2,1)}), bf16[8,128,512]{2,1,0:T(8,128)(2,1)S(1)}, u32[]{:S(2)}, u32[]{:S(2)}) async-start(bf16[8,128,512]{2,1,0:T(8,128)(2,1)} %bitcast.16), calls=%async_computation.1 | async-start | bytes 2097152 | tf_op jit(solution)/shard_map/all_to_all | solution.py:507
  99.9 0.6 slice.63
  100.5 1.4 fusion
  103.9 1.1 select_convert_fusion.4
  104.9 1.6 %collective-permute-start.11 = (f16[16,2176]{1,0:T(8,128)(2,1)S(1)}, f16[16,2176]{1,0:T(8,128)(2,1)S(1)}, u32[]{:S(2)}, u32[]{:S(2)}) collective-permute-start(f16[16,2176]{1,0:T(8,128)(2,1)S(1)} %get-tuple-element.84), channel_id=1, source_target_pairs={{0,1},{1,0},{2,3},{3,2},{4,5},{5,4},{6,7},{7,6},{8,9},{9,8},{10,11... | collective-permute-start | bytes 208904 | tf_op jit(solution)/shard_map/ppermute | solution.py:358
  106.6 2.6 %collective-permute-start.12 = (f16[16,2176]{1,0:T(8,128)(2,1)S(1)}, f16[16,2176]{1,0:T(8,128)(2,1)S(1)}, u32[]{:S(2)}, u32[]{:S(2)}) collective-permute-start(f16[16,2176]{1,0:T(8,128)(2,1)S(1)} %get-tuple-element.86), channel_id=1, source_target_pairs={{0,2},{1,3},{2,0},{3,1},{4,6},{5,7},{6,4},{7,5},{8,10},{9,11},{10,... | collective-permute-start | bytes 208904 | tf_op jit(solution)/shard_map/ppermute | solution.py:358
  109.4 0.6 slice.65
  110.7 3.8 %collective-permute-done.12 = f16[16,2176]{1,0:T(8,128)(2,1)S(1)} collective-permute-done((f16[16,2176]{1,0:T(8,128)(2,1)S(1)}, f16[16,2176]{1,0:T(8,128)(2,1)S(1)}, u32[]{:S(2)}, u32[]{:S(2)}) %collective-permute-start.12) | collective-permute-done | bytes 69664 | tf_op jit(solution)/shard_map/ppermute | solution.py:358
  114.4 0.6 slice.66
  115.7 0.6 slice.67
  117.0 1.0 add_convert_fusion
  118.0 1.0 collective-permute-start.14
  119.0 2.9 %collective-permute-start.15 = (bf16[16,2176]{1,0:T(8,128)(2,1)S(1)}, bf16[16,2176]{1,0:T(8,128)(2,1)S(1)}, u32[]{:S(2)}, u32[]{:S(2)}) collective-permute-start(bf16[16,2176]{1,0:T(8,128)(2,1)S(1)} %add_convert_fusion), channel_id=1, source_target_pairs={{0,2},{1,3},{2,0},{3,1},{4,6},{5,7},{6,4},{7,5},{8,10},{9,11},{10,... | collective-permute-start | bytes 208904 | tf_op jit(solution)/shard_map/ppermute | solution.py:358
  122.6 3.6 %collective-permute-done.15 = bf16[16,2176]{1,0:T(8,128)(2,1)S(1)} collective-permute-done((bf16[16,2176]{1,0:T(8,128)(2,1)S(1)}, bf16[16,2176]{1,0:T(8,128)(2,1)S(1)}, u32[]{:S(2)}, u32[]{:S(2)}) %collective-permute-start.15) | collective-permute-done | bytes 69664 | tf_op jit(solution)/shard_map/ppermute | solution.py:358
  126.1 1.9 %collective-permute-done.16 = bf16[16,2176]{1,0:T(8,128)(2,1)S(1)} collective-permute-done((bf16[16,2176]{1,0:T(8,128)(2,1)S(1)}, bf16[16,2176]{1,0:T(8,128)(2,1)S(1)}, u32[]{:S(2)}, u32[]{:S(2)}) %collective-permute-start.16) | collective-permute-done | bytes 69664 | tf_op jit(solution)/shard_map/ppermute | solution.py:358
  128.2 1.8 %collective-permute-start.17 = (bf16[64,2176]{1,0:T(8,128)(2,1)S(1)}, bf16[64,2176]{1,0:T(8,128)(2,1)S(1)}, u32[]{:S(2)}, u32[]{:S(2)}) collective-permute-start(bf16[64,2176]{1,0:T(8,128)(2,1)S(1)} %pad_maximum_fusion.1), channel_id=1, source_target_pairs={{0,16},{4,12},{8,24},{12,4},{16,0},{20,28},{24,8},{28,20},{1,17},{... | collective-permute-start | bytes 835592 | tf_op jit(solution)/shard_map/ppermute | solution.py:450
  129.9 6.6 %collective-permute-done.17 = bf16[64,2176]{1,0:T(8,128)(2,1)S(1)} collective-permute-done((bf16[64,2176]{1,0:T(8,128)(2,1)S(1)}, bf16[64,2176]{1,0:T(8,128)(2,1)S(1)}, u32[]{:S(2)}, u32[]{:S(2)}) %collective-permute-start.17) | collective-permute-done | bytes 278560 | tf_op jit(solution)/shard_map/ppermute | solution.py:450
  136.7 1.8 %collective-permute-start.18 = (bf16[128,2176]{1,0:T(8,128)(2,1)S(1)}, bf16[128,2176]{1,0:T(8,128)(2,1)S(1)}, u32[]{:S(2)}, u32[]{:S(2)}) collective-permute-start(bf16[128,2176]{1,0:T(8,128)(2,1)S(1)} %broadcast_select_fusion), channel_id=1, source_target_pairs={{0,8},{4,20},{8,0},{12,28},{16,24},{20,4},{24,16},{28,12},{1,9},{5... | collective-permute-start | bytes 1671176 | tf_op jit(solution)/shard_map/ppermute | solution.py:450
  138.5 7.8 %collective-permute-done.18 = bf16[128,2176]{1,0:T(8,128)(2,1)S(1)} collective-permute-done((bf16[128,2176]{1,0:T(8,128)(2,1)S(1)}, bf16[128,2176]{1,0:T(8,128)(2,1)S(1)}, u32[]{:S(2)}, u32[]{:S(2)}) %collective-permute-start.18) | collective-permute-done | bytes 557088 | tf_op jit(solution)/shard_map/ppermute | solution.py:450
  146.6 1.5 %unpack.1 = bf16[512,512]{1,0:T(8,128)(2,1)} custom-call(s32[1]{0:T(128)} %bitcast.me_ref, s32[1,512]{1,0:T(1,128)S(1)} %copy-done.8, bf16[1024,512]{1,0:T(8,128)(2,1)S(1)} %bitcast.38), custom_call_target="tpu_custom_call" | custom-call | flops 536870912 | bytes 2097152 | tf_op jit(solution)/shard_map/unpack/pallas_call | solution.py:609
  148.1 1.2 collective-permute-done.19.other_ref
  149.3 2.2 %split.1 = (f32[512,1536]{1,0:T(8,128)}, f32[512,512]{1,0:T(8,128)}, f32[1,512]{1,0:T(1,128)}) custom-call(s32[1]{0:T(128)S(6)} %and.16.side_ref, bf16[256,2176]{1,0:T(8,128)(2,1)S(1)} %maximum_select_fusion.own_ref, bf16[256,2176]{1,0:T(8,128)(2,1)S(1)} %collective-permute-done.19.other_ref), custom_call_target="tpu_custom_call" | custom-call | bytes 8388608 | tf_op jit(solution)/shard_map/split/pallas_call | solution.py:621
  (82 shorter events, 4.5 us)
Async XLA Ops:
  0.6 4.8 %copy-start.6 = (bf16[1,512,512]{2,1,0:T(8,128)(2,1)S(1)}, bf16[1,512,512]{2,1,0:T(8,128)(2,1)}, u32[]{:S(2)}) copy-start(bf16[1,512,512]{2,1,0:T(8,128)(2,1)} %param.7) | copy-start | bytes 1572868
  3.7 1.7 %collective-permute-start = (bf16[144,512]{1,0:T(8,128)(2,1)}, bf16[144,512]{1,0:T(8,128)(2,1)S(1)}, u32[]{:S(2)}, u32[]{:S(2)}) collective-permute-start(bf16[144,512]{1,0:T(8,128)(2,1)} %get-tuple-element.39), channel_id=1, source_target_pairs={{0,4},{4,0},{8,12},{12,8},{16,20},{20,16},{24,28},{28,24},{1,5},{5... | collective-permute-start | bytes 442376 | tf_op jit(solution)/shard_map/ppermute | solution.py:358
  5.4 2.4 %copy-start.12 = (bf16[144,512]{1,0:T(8,128)(2,1)}, bf16[144,512]{1,0:T(8,128)(2,1)S(1)}, u32[]{:S(2)}) copy-start(bf16[144,512]{1,0:T(8,128)(2,1)S(1)} %collective-permute-done.refs_1_) | copy-start | bytes 442372
  5.4 0.7 copy-start.7
  7.8 5.3 %copy-start.23 = (bf16[144,512]{1,0:T(8,128)(2,1)S(1)}, bf16[144,512]{1,0:T(8,128)(2,1)}, u32[]{:S(2)}) copy-start(bf16[144,512]{1,0:T(8,128)(2,1)} %get-tuple-element.44) | copy-start | bytes 442372
  7.8 7.3 %copy-start.20 = (bf16[144,512]{1,0:T(8,128)(2,1)S(1)}, bf16[144,512]{1,0:T(8,128)(2,1)}, u32[]{:S(2)}) copy-start(bf16[144,512]{1,0:T(8,128)(2,1)} %get-tuple-element.45) | copy-start | bytes 442372
  7.8 7.3 %copy-start.18 = (bf16[144,512]{1,0:T(8,128)(2,1)S(1)}, bf16[144,512]{1,0:T(8,128)(2,1)}, u32[]{:S(2)}) copy-start(bf16[144,512]{1,0:T(8,128)(2,1)} %get-tuple-element.46) | copy-start | bytes 442372
  7.8 8.8 %copy-start.16 = (bf16[144,512]{1,0:T(8,128)(2,1)S(1)}, bf16[144,512]{1,0:T(8,128)(2,1)}, u32[]{:S(2)}) copy-start(bf16[144,512]{1,0:T(8,128)(2,1)} %get-tuple-element.47) | copy-start | bytes 442372
  7.8 9.1 %copy-start.14 = (bf16[144,512]{1,0:T(8,128)(2,1)S(1)}, bf16[144,512]{1,0:T(8,128)(2,1)}, u32[]{:S(2)}) copy-start(bf16[144,512]{1,0:T(8,128)(2,1)} %get-tuple-element.48) | copy-start | bytes 442372
  7.9 23.4 %copy-start.13 = (bf16[144,512]{1,0:T(8,128)(2,1)S(1)}, bf16[144,512]{1,0:T(8,128)(2,1)}, u32[]{:S(2)}) copy-start(bf16[144,512]{1,0:T(8,128)(2,1)} %get-tuple-element.49) | copy-start | bytes 442372
  7.9 43.0 %all-to-all-start = ((bf16[8,128,512]{2,1,0:T(8,128)(2,1)}), bf16[8,128,512]{2,1,0:T(8,128)(2,1)S(1)}, u32[]{:S(2)}, u32[]{:S(2)}) async-start(bf16[8,128,512]{2,1,0:T(8,128)(2,1)} %bitcast.4), calls=%async_computation | async-start | bytes 2097152 | tf_op jit(solution)/shard_map/all_to_all | solution.py:507
  13.1 18.2 %collective-permute-start.1 = (bf16[144,512]{1,0:T(8,128)(2,1)S(1)}, bf16[144,512]{1,0:T(8,128)(2,1)S(1)}, u32[]{:S(2)}, u32[]{:S(2)}) collective-permute-start(bf16[144,512]{1,0:T(8,128)(2,1)S(1)} %copy-done.23), channel_id=1, source_target_pairs={{0,8},{4,12},{8,0},{12,4},{16,24},{20,28},{24,16},{28,20},{1,9},{5... | collective-permute-start | bytes 442376 | tf_op jit(solution)/shard_map/ppermute | solution.py:358
  15.1 18.4 %collective-permute-start.2 = (bf16[144,512]{1,0:T(8,128)(2,1)S(1)}, bf16[144,512]{1,0:T(8,128)(2,1)S(1)}, u32[]{:S(2)}, u32[]{:S(2)}) collective-permute-start(bf16[144,512]{1,0:T(8,128)(2,1)S(1)} %copy-done.20), channel_id=1, source_target_pairs={{0,12},{4,8},{8,4},{12,0},{16,28},{20,24},{24,20},{28,16},{1,13},{... | collective-permute-start | bytes 442376 | tf_op jit(solution)/shard_map/ppermute | solution.py:358
  15.1 18.4 %collective-permute-start.3 = (bf16[144,512]{1,0:T(8,128)(2,1)S(1)}, bf16[144,512]{1,0:T(8,128)(2,1)S(1)}, u32[]{:S(2)}, u32[]{:S(2)}) collective-permute-start(bf16[144,512]{1,0:T(8,128)(2,1)S(1)} %copy-done.18), channel_id=1, source_target_pairs={{0,16},{4,20},{8,24},{12,28},{16,0},{20,4},{24,8},{28,12},{1,17},{... | collective-permute-start | bytes 442376 | tf_op jit(solution)/shard_map/ppermute | solution.py:358
  16.7 16.8 %collective-permute-start.4 = (bf16[144,512]{1,0:T(8,128)(2,1)S(1)}, bf16[144,512]{1,0:T(8,128)(2,1)S(1)}, u32[]{:S(2)}, u32[]{:S(2)}) collective-permute-start(bf16[144,512]{1,0:T(8,128)(2,1)S(1)} %copy-done.16), channel_id=1, source_target_pairs={{0,20},{4,16},{8,28},{12,24},{16,4},{20,0},{24,12},{28,8},{1,21},{... | collective-permute-start | bytes 442376 | tf_op jit(solution)/shard_map/ppermute | solution.py:358
  17.0 21.6 %collective-permute-start.5 = (bf16[144,512]{1,0:T(8,128)(2,1)S(1)}, bf16[144,512]{1,0:T(8,128)(2,1)S(1)}, u32[]{:S(2)}, u32[]{:S(2)}) collective-permute-start(bf16[144,512]{1,0:T(8,128)(2,1)S(1)} %copy-done.14), channel_id=1, source_target_pairs={{0,24},{4,28},{8,16},{12,20},{16,8},{20,12},{24,0},{28,4},{1,25},{... | collective-permute-start | bytes 442376 | tf_op jit(solution)/shard_map/ppermute | solution.py:358
  31.3 9.4 %copy-start.15 = (bf16[144,512]{1,0:T(8,128)(2,1)}, bf16[144,512]{1,0:T(8,128)(2,1)S(1)}, u32[]{:S(2)}) copy-start(bf16[144,512]{1,0:T(8,128)(2,1)S(1)} %collective-permute-done.1.refs_2_) | copy-start | bytes 442372
  31.3 9.4 %collective-permute-start.6 = (bf16[144,512]{1,0:T(8,128)(2,1)S(1)}, bf16[144,512]{1,0:T(8,128)(2,1)S(1)}, u32[]{:S(2)}, u32[]{:S(2)}) collective-permute-start(bf16[144,512]{1,0:T(8,128)(2,1)S(1)} %copy-done.13), channel_id=1, source_target_pairs={{0,28},{4,24},{8,20},{12,16},{16,12},{20,8},{24,4},{28,0},{1,29},{... | collective-permute-start | bytes 442376 | tf_op jit(solution)/shard_map/ppermute | solution.py:358
  33.5 7.2 %copy-start.17 = (bf16[144,512]{1,0:T(8,128)(2,1)}, bf16[144,512]{1,0:T(8,128)(2,1)S(1)}, u32[]{:S(2)}) copy-start(bf16[144,512]{1,0:T(8,128)(2,1)S(1)} %collective-permute-done.2.refs_3_) | copy-start | bytes 442372
  33.5 7.2 %copy-start.19 = (bf16[144,512]{1,0:T(8,128)(2,1)}, bf16[144,512]{1,0:T(8,128)(2,1)S(1)}, u32[]{:S(2)}) copy-start(bf16[144,512]{1,0:T(8,128)(2,1)S(1)} %collective-permute-done.3.refs_4_) | copy-start | bytes 442372
  33.5 7.2 %copy-start.21 = (bf16[144,512]{1,0:T(8,128)(2,1)}, bf16[144,512]{1,0:T(8,128)(2,1)S(1)}, u32[]{:S(2)}) copy-start(bf16[144,512]{1,0:T(8,128)(2,1)S(1)} %collective-permute-done.4.refs_5_) | copy-start | bytes 442372
  38.5 2.2 %copy-start.22 = (bf16[144,512]{1,0:T(8,128)(2,1)}, bf16[144,512]{1,0:T(8,128)(2,1)S(1)}, u32[]{:S(2)}) copy-start(bf16[144,512]{1,0:T(8,128)(2,1)S(1)} %collective-permute-done.5.refs_6_) | copy-start | bytes 442372
  40.7 0.7 copy-start.24
  50.9 1.0 copy-start.11
  69.6 3.0 %collective-permute-start.8 = (f32[128,2176]{1,0:T(8,128)}, f32[128,2176]{1,0:T(8,128)S(1)}, u32[]{:S(2)}, u32[]{:S(2)}) collective-permute-start(f32[128,2176]{1,0:T(8,128)} %get-tuple-element.61), channel_id=1, source_target_pairs={{0,4},{4,0},{8,12},{12,8},{16,20},{20,16},{24,28},{28,24},{1,5},{5... | collective-permute-start | bytes 3342344 | tf_op jit(solution)/shard_map/ppermute | solution.py:415
  71.2 5.5 %collective-permute-start.7 = (f32[128,2176]{1,0:T(8,128)}, f32[128,2176]{1,0:T(8,128)S(1)}, u32[]{:S(2)}, u32[]{:S(2)}) collective-permute-start(f32[128,2176]{1,0:T(8,128)} %get-tuple-element.59), channel_id=1, source_target_pairs={{0,4},{4,0},{8,12},{12,8},{16,20},{20,16},{24,28},{28,24},{1,5},{5... | collective-permute-start | bytes 3342344 | tf_op jit(solution)/shard_map/ppermute | solution.py:417
  74.6 2.2 %copy-start.10 = (f32[128,2176]{1,0:T(8,128)S(1)}, f32[128,2176]{1,0:T(8,128)}, u32[]{:S(2)}) copy-start(f32[128,2176]{1,0:T(8,128)} %get-tuple-element.58) | copy-start | bytes 3342340
  76.1 9.7 %collective-permute-start.9 = (f16[128,2176]{1,0:T(8,128)(2,1)S(1)}, f16[128,2176]{1,0:T(8,128)(2,1)}, u32[]{:S(2)}, u32[]{:S(2)}) collective-permute-start(f16[128,2176]{1,0:T(8,128)(2,1)S(1)} %select_convert_fusion), channel_id=1, source_target_pairs={{0,8},{4,20},{8,0},{12,28},{16,24},{20,4},{24,16},{28,12},{1,9},{5... | collective-permute-start | bytes 1671176 | tf_op jit(solution)/shard_map/ppermute | solution.py:418
  76.7 17.3 %copy-start.2 = (bf16[512,512]{1,0:T(8,128)(2,1)S(1)}, bf16[512,512]{1,0:T(8,128)(2,1)}, u32[]{:S(2)}) copy-start(bf16[512,512]{1,0:T(8,128)(2,1)} %get-tuple-element.67.serial_grad_ref) | copy-start | bytes 1572868
  76.9 14.1 %copy-start.9 = (f32[128,2176]{1,0:T(8,128)}, f32[128,2176]{1,0:T(8,128)S(1)}, u32[]{:S(2)}) copy-start(f32[128,2176]{1,0:T(8,128)S(1)} %add.88) | copy-start | bytes 3342340
  91.0 3.1 %copy-start = (f32[512,512]{1,0:T(8,128)S(1)}, f32[512,512]{1,0:T(8,128)}, u32[]{:S(2)}) copy-start(f32[512,512]{1,0:T(8,128)} %get-tuple-element.54.refs_4_.xhat_ref) | copy-start | bytes 3145732
  91.0 3.1 %copy-start.1 = (f32[512,512]{1,0:T(8,128)S(1)}, f32[512,512]{1,0:T(8,128)}, u32[]{:S(2)}) copy-start(f32[512,512]{1,0:T(8,128)} %get-tuple-element.68.d_normed_ref) | copy-start | bytes 3145732
  91.0 3.0 %copy-start.3 = (f32[512,128]{1,0:T(8,128)S(1)}, f32[512,128]{1,0:T(8,128)}, u32[]{:S(2)}) copy-start(f32[512,128]{1,0:T(8,128)} %get-tuple-element.66.inv_ref) | copy-start | bytes 786436
  91.0 3.0 %copy-start.4 = (s32[1,1024]{1,0:T(1,128)S(1)}, s32[1,1024]{1,0:T(1,128)}, u32[]{:S(2)}) copy-start(s32[1,1024]{1,0:T(1,128)} %get-tuple-element.50.pos_ref) | copy-start | bytes 12292
  91.0 3.0 %copy-start.5 = (f32[512]{0:T(512)S(1)}, f32[512]{0:T(512)}, u32[]{:S(2)}) copy-start(f32[512]{0:T(512)} %param.11) | copy-start | bytes 6148
  93.5 7.0 %collective-permute-start.10 = (f16[64,2176]{1,0:T(8,128)(2,1)}, f16[64,2176]{1,0:T(8,128)(2,1)}, u32[]{:S(2)}, u32[]{:S(2)}) collective-permute-start(f16[64,2176]{1,0:T(8,128)(2,1)} %get-tuple-element.82), channel_id=1, source_target_pairs={{0,16},{4,12},{8,24},{12,4},{16,0},{20,28},{24,8},{28,20},{1,17},{... | collective-permute-start | bytes 835592 | tf_op jit(solution)/shard_map/ppermute | solution.py:426
  96.1 21.8 %all-to-all-start.1 = ((bf16[8,128,512]{2,1,0:T(8,128)(2,1)}), bf16[8,128,512]{2,1,0:T(8,128)(2,1)S(1)}, u32[]{:S(2)}, u32[]{:S(2)}) async-start(bf16[8,128,512]{2,1,0:T(8,128)(2,1)} %bitcast.16), calls=%async_computation.1 | async-start | bytes 2097152 | tf_op jit(solution)/shard_map/all_to_all | solution.py:507
  104.9 4.5 %collective-permute-start.11 = (f16[16,2176]{1,0:T(8,128)(2,1)S(1)}, f16[16,2176]{1,0:T(8,128)(2,1)S(1)}, u32[]{:S(2)}, u32[]{:S(2)}) collective-permute-start(f16[16,2176]{1,0:T(8,128)(2,1)S(1)} %get-tuple-element.84), channel_id=1, source_target_pairs={{0,1},{1,0},{2,3},{3,2},{4,5},{5,4},{6,7},{7,6},{8,9},{9,8},{10,11... | collective-permute-start | bytes 208904 | tf_op jit(solution)/shard_map/ppermute | solution.py:358
  106.6 7.8 %collective-permute-start.12 = (f16[16,2176]{1,0:T(8,128)(2,1)S(1)}, f16[16,2176]{1,0:T(8,128)(2,1)S(1)}, u32[]{:S(2)}, u32[]{:S(2)}) collective-permute-start(f16[16,2176]{1,0:T(8,128)(2,1)S(1)} %get-tuple-element.86), channel_id=1, source_target_pairs={{0,2},{1,3},{2,0},{3,1},{4,6},{5,7},{6,4},{7,5},{8,10},{9,11},{10,... | collective-permute-start | bytes 208904 | tf_op jit(solution)/shard_map/ppermute | solution.py:358
  109.2 6.5 %collective-permute-start.13 = (f16[16,2176]{1,0:T(8,128)(2,1)S(1)}, f16[16,2176]{1,0:T(8,128)(2,1)S(1)}, u32[]{:S(2)}, u32[]{:S(2)}) collective-permute-start(f16[16,2176]{1,0:T(8,128)(2,1)S(1)} %get-tuple-element.85), channel_id=1, source_target_pairs={{0,3},{1,2},{2,1},{3,0},{4,7},{5,6},{6,5},{7,4},{8,11},{9,10},{10,... | collective-permute-start | bytes 208904 | tf_op jit(solution)/shard_map/ppermute | solution.py:358
  118.0 4.6 %collective-permute-start.14 = (bf16[16,2176]{1,0:T(8,128)(2,1)S(1)}, bf16[16,2176]{1,0:T(8,128)(2,1)S(1)}, u32[]{:S(2)}, u32[]{:S(2)}) collective-permute-start(bf16[16,2176]{1,0:T(8,128)(2,1)S(1)} %add_convert_fusion), channel_id=1, source_target_pairs={{0,1},{1,0},{2,3},{3,2},{4,5},{5,4},{6,7},{7,6},{8,9},{9,8},{10,11... | collective-permute-start | bytes 208904 | tf_op jit(solution)/shard_map/ppermute | solution.py:358
  119.0 7.2 %collective-permute-start.15 = (bf16[16,2176]{1,0:T(8,128)(2,1)S(1)}, bf16[16,2176]{1,0:T(8,128)(2,1)S(1)}, u32[]{:S(2)}, u32[]{:S(2)}) collective-permute-start(bf16[16,2176]{1,0:T(8,128)(2,1)S(1)} %add_convert_fusion), channel_id=1, source_target_pairs={{0,2},{1,3},{2,0},{3,1},{4,6},{5,7},{6,4},{7,5},{8,10},{9,11},{10,... | collective-permute-start | bytes 208904 | tf_op jit(solution)/shard_map/ppermute | solution.py:358
  121.9 6.1 %collective-permute-start.16 = (bf16[16,2176]{1,0:T(8,128)(2,1)S(1)}, bf16[16,2176]{1,0:T(8,128)(2,1)S(1)}, u32[]{:S(2)}, u32[]{:S(2)}) collective-permute-start(bf16[16,2176]{1,0:T(8,128)(2,1)S(1)} %add_convert_fusion), channel_id=1, source_target_pairs={{0,3},{1,2},{2,1},{3,0},{4,7},{5,6},{6,5},{7,4},{8,11},{9,10},{10,... | collective-permute-start | bytes 208904 | tf_op jit(solution)/shard_map/ppermute | solution.py:358
  128.2 8.3 %collective-permute-start.17 = (bf16[64,2176]{1,0:T(8,128)(2,1)S(1)}, bf16[64,2176]{1,0:T(8,128)(2,1)S(1)}, u32[]{:S(2)}, u32[]{:S(2)}) collective-permute-start(bf16[64,2176]{1,0:T(8,128)(2,1)S(1)} %pad_maximum_fusion.1), channel_id=1, source_target_pairs={{0,16},{4,12},{8,24},{12,4},{16,0},{20,28},{24,8},{28,20},{1,17},{... | collective-permute-start | bytes 835592 | tf_op jit(solution)/shard_map/ppermute | solution.py:450
  136.7 9.6 %collective-permute-start.18 = (bf16[128,2176]{1,0:T(8,128)(2,1)S(1)}, bf16[128,2176]{1,0:T(8,128)(2,1)S(1)}, u32[]{:S(2)}, u32[]{:S(2)}) collective-permute-start(bf16[128,2176]{1,0:T(8,128)(2,1)S(1)} %broadcast_select_fusion), channel_id=1, source_target_pairs={{0,8},{4,20},{8,0},{12,28},{16,24},{20,4},{24,16},{28,12},{1,9},{5... | collective-permute-start | bytes 1671176 | tf_op jit(solution)/shard_map/ppermute | solution.py:450
  138.5 8.1 %copy-start.8 = (s32[1,512]{1,0:T(1,128)S(1)}, s32[1,512]{1,0:T(1,128)}, u32[]{:S(2)}) copy-start(s32[1,512]{1,0:T(1,128)} %get-tuple-element.41.slot_ref) | copy-start | bytes 6148
  146.5 2.8 %collective-permute-start.19 = (bf16[256,2176]{1,0:T(8,128)(2,1)S(1)}, bf16[256,2176]{1,0:T(8,128)(2,1)S(1)}, u32[]{:S(2)}, u32[]{:S(2)}) collective-permute-start(bf16[256,2176]{1,0:T(8,128)(2,1)S(1)} %maximum_select_fusion.own_ref), channel_id=1, source_target_pairs={{0,4},{4,0},{8,12},{12,8},{16,20},{20,16},{24,28},{28,24},{1,5},{5... | collective-permute-start | bytes 3342344 | tf_op jit(solution)/shard_map/ppermute | solution.py:608

commit v8 on v6

--- a/solution.py
+++ b/solution.py
@@ -11,6 +11,8 @@
 PATCH = 512
 EXTRA = 16
 LANES = 128
+CODE_MAX = 32000.0
+DIGIT = 60000.0
 MIB = 1024 * 1024
 F32 = jnp.float32
 BF16 = jnp.bfloat16
@@ -326,6 +328,67 @@
     pl.when(jnp.logical_not(own))(lambda: write(other_ref))
 
 
+def exponent_of(largest):
+    return jnp.clip(jnp.ceil(jnp.log(jnp.maximum(largest, 1e-30)) * 1.4426950408889634), -100.0, 120.0)
+
+
+def encode(out_ref, total):
+    width = total.shape[1] - LANES
+    body, gain = total[:, :width], total[:, width : width + 1]
+    exponent = exponent_of(jnp.max(jnp.abs(body), axis=1, keepdims=True))
+    codes = jnp.round(body * (jnp.exp2(-exponent) * CODE_MAX))
+    out_ref[:, :width] = codes.astype(jnp.int32).astype(jnp.int16)
+    gain_exponent = exponent_of(jnp.abs(gain))
+    scaled = gain * (jnp.exp2(-gain_exponent) * CODE_MAX)
+    high = jnp.round(scaled)
+    low = jnp.round((scaled - high) * DIGIT)
+    lane = iota((total.shape[0], LANES), 1)
+    tail = jnp.where(lane == 0, high, jnp.where(lane == 1, low, jnp.where(lane == 2, gain_exponent, exponent)))
+    out_ref[:, width:] = tail.astype(jnp.int32).astype(jnp.int16)
+
+
+def decode(codes):
+    values = codes.astype(jnp.int32).astype(F32)
+    width = values.shape[1] - LANES
+    tail = values[:, width:]
+    body = values[:, :width] * (jnp.exp2(tail[:, 3:4]) * (1.0 / CODE_MAX))
+    gain = (tail[:, 0:1] + tail[:, 1:2] * (1.0 / DIGIT)) * (jnp.exp2(tail[:, 2:3]) * (1.0 / CODE_MAX))
+    return jnp.concatenate([body, jnp.broadcast_to(gain, tail.shape)], axis=1)
+
+
+def total_of(terms, part):
+    half = terms[0].shape[0] // 2
+    rows = {"all": slice(None), "first": slice(0, half), "second": slice(half, 2 * half)}[part]
+    values = [ref[rows, :] for ref in terms]
+    return functools.reduce(jnp.add, [decode(v) if v.dtype == jnp.int16 else v for v in values])
+
+
+def message_kernel(part, *refs):
+    encode(refs[-1], total_of(refs[:-1], part))
+
+
+def sum_kernel(parts, *refs):
+    refs[-1][...] = functools.reduce(jnp.add, [total_of([ref], p) for ref, p in zip(refs, parts)])
+
+
+def pieces_kernel(parts, n_dp, plane_ref, *refs):
+    terms, own, messages, total = refs[: len(parts)], refs[len(parts)], refs[len(parts) + 1 : -1], refs[-1]
+    total[...] = functools.reduce(jnp.add, [total_of([ref], p) for ref, p in zip(terms, parts)])
+    size = own.shape[0]
+
+    def rows_of(distance):
+        start = lax.bitwise_xor(plane_ref[0], distance) * size
+        return total[pl.ds(pl.multiple_of(start, size), size), :]
+
+    for k in range(1, n_dp):
+        encode(messages[k - 1], rows_of(k))
+    own[...] = rows_of(0)
+
+
+def finish_kernel(*refs):
+    refs[-1][...] = total_of(refs[:-1], "all").astype(BF16)
+
+
 def whole(shape):
     return pl.BlockSpec(shape, lambda *_: (0,) * len(shape), pipeline_mode=pl.Buffered(1))
 
@@ -374,27 +437,72 @@
     return [(i, i ^ 1) for i in range(lax.axis_size("seq"))]
 
 
+def small_kernel(kernel, outs, operands, scalars=0, scratch=(), name="sum"):
+    in_smem = pl.BlockSpec(memory_space=pltpu.SMEM)
+    in_vmem = pl.BlockSpec(memory_space=pltpu.VMEM)
+    touched = sum(x.size * x.dtype.itemsize for x in (*operands, *outs))
+    return pl.pallas_call(
+        kernel,
+        out_shape=outs,
+        in_specs=[in_smem] * scalars + [in_vmem] * (len(operands) - scalars),
+        out_specs=[in_vmem] * len(outs),
+        scratch_shapes=list(scratch),
+        compiler_params=params(16),
+        cost_estimate=pl.CostEstimate(flops=2 * touched, bytes_accessed=touched, transcendentals=0),
+        name=name,
+    )(*operands)
+
+
+def message(terms, part, name):
+    rows, width = terms[0].shape
+    rows = rows if part == "all" else rows // 2
+    return small_kernel(
+        functools.partial(message_kernel, part), [shape_of((rows, width), jnp.int16)], terms, name=name
+    )[0]
+
+
 def first_step(quarters, steps):
     pass_on, pass_keep, own_on, own_keep = quarters
-    send = own_on + lax.ppermute(pass_on, "seq", core_pairs())
-    keep = own_keep + lax.ppermute(pass_keep, "seq", core_pairs())
-    return [keep, lax.ppermute(send, "seq", steps[0][0])]
-
-
-def next_steps(terms, steps):
-    half = terms[0].shape[0] // 2
-    got = lax.ppermute(terms[0][:half] + terms[1][:half], "seq", steps[1][0])
-    terms = [terms[0][half:] + terms[1][half:], got]
-    for pairs, side in steps[2:]:
-        got = lax.ppermute(piece(terms, 1 - side, 2), "seq", pairs)
-        terms = [piece(terms, side, 2), got]
-    return terms
-
-
-def reduce_over_planes(terms):
+    got_on = lax.ppermute(pass_on, "seq", core_pairs())
+    got_keep = lax.ppermute(pass_keep, "seq", core_pairs())
+    sent = message([own_on, got_on], "all", "code_first")
+    return [own_keep, got_keep, lax.ppermute(sent, "seq", steps[0][0])]
+
+
+def second_step(terms, steps):
+    sent = message(terms, "first", "code_second")
+    return terms, lax.ppermute(sent, "seq", steps[1][0])
+
+
+def halves_of_plain(part, steps):
+    for pairs, side in steps:
+        got = lax.ppermute(piece([part], 1 - side, 2), "seq", pairs)
+        part = piece([part], side, 2) + got
+    return part
+
+
+def reduce_over_planes(terms, got, steps):
     n_dp, plane = lax.axis_size("dp"), lax.axis_index("dp")
-    pieces = [piece(terms, lax.bitwise_xor(plane, k), n_dp) for k in range(n_dp)]
-    return functools.reduce(jnp.add, by_distance(pieces, "dp")).astype(BF16)
+    rows, width = got.shape
+    parts = ["second"] * len(terms) + ["all"]
+    if len(steps) > 2 or rows // n_dp % 16:
+        part = small_kernel(
+            functools.partial(sum_kernel, parts), [shape_of((rows, width), F32)], [*terms, got]
+        )[0]
+        part = halves_of_plain(part, steps[2:])
+        pieces = [piece([part], lax.bitwise_xor(plane, k), n_dp) for k in range(n_dp)]
+        return functools.reduce(jnp.add, by_distance(pieces, "dp")).astype(BF16)
+    size = rows // n_dp
+    own, *sent = small_kernel(
+        functools.partial(pieces_kernel, parts, n_dp),
+        [shape_of((size, width), F32)] + [shape_of((size, width), jnp.int16)] * (n_dp - 1),
+        [jnp.reshape(plane.astype(jnp.int32), (1,)), *terms, got],
+        scalars=1,
+        scratch=[pltpu.VMEM((rows, width), F32)],
+        name="code_planes",
+    )
+    arrived = by_distance([own] + sent, "dp")
+    return small_kernel(finish_kernel, [shape_of((size, width), BF16)], arrived, name="finish")[0]
 
 
 def share_over_planes(part):
@@ -564,8 +672,8 @@
         name="residual",
     )(me, pos, gain_row, inv, xhat, serial_grad, d_normed)
     returned = exchange(back)
-    terms = next_steps(terms, steps)
-    part, returned = lax.optimization_barrier((reduce_over_planes(terms), returned))
+    terms, got = second_step(terms, steps)
+    part, returned = lax.optimization_barrier((reduce_over_planes(terms, got, steps), returned))
     own = share_in_plane(share_over_planes(part), steps)
     other = lax.ppermute(own, "seq", core_pairs())
     grad_local = pl.pallas_call(

time: 140 us -> 141 us (level)
  other arithmetic: 4.91 us -> 0.35 us
  starting transfers between devices: 28.7 us -> 32.1 us
  Pallas kernels: 37.5 us -> 40 us
  waiting for transfers between devices: 65.2 us -> 63.5 us
    ppermute x4, waiting for transfers between devices: 20.6 us -> 26.5 us  [the longest x1 15.1 us: second_step(): return (terms, lax.ppermute(sent, 'seq', steps[1][0]))]
    add x4 -> x0, other arithmetic: 3.58 us -> none  [the longest x1 1.46 us: first_step(): send = own_on + lax.ppermute(pass_on, 'seq', core_pairs())]
    ppermute x13, waiting for transfers between devices: 20.8 us -> 17.3 us  [by_distance(): lax.ppermute(blocks[k], axis, [(i, i ^ k) for i in range(count)])]
    ppermute x2, waiting for transfers between devices: 16.9 us -> 13.9 us  [share_in_plane(): other = lax.ppermute(part, 'seq', pairs)]
    unnamed x44 -> x46, local copies, waits for them, and re-layouts: 2.34 us -> 3.17 us
  transfers between devices with their start and end apart: 22 -> 22, of which waited for: 14 -> 12; matrix products, arithmetic and copies ran while one was open for 3% -> 0% of each run, Pallas kernels for 11% -> 11%
where the time goes in v8:
time: 141 us; the launch traced here: 140 us
  waiting for transfers between devices  63.5 us (45%)
  Pallas kernels  40 us (28%)
  starting transfers between devices  32.1 us (23%)
  local copies, waits for them, and re-layouts  3.18 us (2%)
    ppermute x13, starting transfers between devices, by_distance(): lax.ppermute(blocks[k], axis, [(i, i ^ k) for i in range(count)])  18.1 us
    pallas_call x1, Pallas kernels, per_device(): pl.pallas_call(functools.partial(backward_kernel, n_seq, chip_bits), grid...  17.5 us
    ppermute x13, waiting for transfers between devices, by_distance(): lax.ppermute(blocks[k], axis, [(i, i ^ k) for i in range(count)])  17.3 us
    ppermute x1, waiting for transfers between devices, second_step(): return (terms, lax.ppermute(sent, 'seq', steps[1][0]))  15.1 us
    ppermute x2, waiting for transfers between devices, share_in_plane(): other = lax.ppermute(part, 'seq', pairs)  13.9 us
    pallas_call x1, Pallas kernels, per_device(): pl.pallas_call(functools.partial(forward_kernel, n_seq, capacity), grid=(...  9.56 us
    ppermute x1, waiting for transfers between devices, first_step(): return [own_keep, got_keep, lax.ppermute(sent, 'seq', steps[0][0])]  9 us
    all_to_all x2, starting transfers between devices, exchange(): got = lax.all_to_all(sent, 'seq', split_axis=0, concat_axis=0, tiled=True)  8.65 us
  transfers between devices with their start and end apart: 22, of which 12 were waited for; matrix products, arithmetic and copies ran while one was open for 0% of the time, Pallas kernels for 11%

profile of v8, /device:TPU:0, one launch (start us, length us, event | category | flops | bytes accessed | tf_op | source)
XLA Modules:
  0.0 140.0 jit_solution(16473850347891194130)
XLA Ops:
  0.6 3.0 %pack.1 = (s32[1,512]{1,0:T(1,128)}, bf16[144,512]{1,0:T(8,128)(2,1)}, bf16[144,512]{1,0:T(8,128)(2,1)}, bf16[144,512]{1,0:T(8,128)(2,1)}, bf16[144,512]{1,0:T(8...) custom-call(s32[1]{0:T(128)} %bitcast.me_ref, ...), custom_call_target="tpu_custom_call" | custom-call | flops 536870912 | bytes 2097152 | tf_op jit(solution)/shard_map/pack/pallas_call | solution.py:544
  3.7 0.5 collective-permute-start
  4.2 2.6 %collective-permute-start.1 = (bf16[144,512]{1,0:T(8,128)(2,1)}, bf16[144,512]{1,0:T(8,128)(2,1)S(1)}, u32[]{:S(2)}, u32[]{:S(2)}) collective-permute-start(bf16[144,512]{1,0:T(8,128)(2,1)} %get-tuple-element.56), channel_id=1, source_target_pairs={{0,8},{4,12},{8,0},{12,4},{16,24},{20,28},{24,16},{28,20},{1,9},{5... | collective-permute-start | bytes 442376 | tf_op jit(solution)/shard_map/ppermute | solution.py:407
  6.8 0.1 collective-permute-start.2
  6.8 1.8 %collective-permute-start.3 = (bf16[144,512]{1,0:T(8,128)(2,1)}, bf16[144,512]{1,0:T(8,128)(2,1)S(1)}, u32[]{:S(2)}, u32[]{:S(2)}) collective-permute-start(bf16[144,512]{1,0:T(8,128)(2,1)} %get-tuple-element.58), channel_id=1, source_target_pairs={{0,16},{4,20},{8,24},{12,28},{16,0},{20,4},{24,8},{28,12},{1,17},{... | collective-permute-start | bytes 442376 | tf_op jit(solution)/shard_map/ppermute | solution.py:407
  8.6 2.6 %collective-permute-start.5 = (bf16[144,512]{1,0:T(8,128)(2,1)}, bf16[144,512]{1,0:T(8,128)(2,1)S(1)}, u32[]{:S(2)}, u32[]{:S(2)}) collective-permute-start(bf16[144,512]{1,0:T(8,128)(2,1)} %get-tuple-element.60), channel_id=1, source_target_pairs={{0,24},{4,28},{8,16},{12,20},{16,8},{20,12},{24,0},{28,4},{1,25},{... | collective-permute-start | bytes 442376 | tf_op jit(solution)/shard_map/ppermute | solution.py:407
  11.2 0.5 collective-permute-done.1.refs_2_
  11.7 1.7 %collective-permute-start.6 = (bf16[144,512]{1,0:T(8,128)(2,1)}, bf16[144,512]{1,0:T(8,128)(2,1)S(1)}, u32[]{:S(2)}, u32[]{:S(2)}) collective-permute-start(bf16[144,512]{1,0:T(8,128)(2,1)} %get-tuple-element.61), channel_id=1, source_target_pairs={{0,28},{4,24},{8,20},{12,16},{16,12},{20,8},{24,4},{28,0},{1,29},{... | collective-permute-start | bytes 442376 | tf_op jit(solution)/shard_map/ppermute | solution.py:407
  13.4 0.7 copy-done.9
  14.1 1.7 %pack_grads.1 = bf16[1024,512]{1,0:T(8,128)(2,1)} custom-call(s32[1]{0:T(128)} %bitcast.me_ref, s32[1,512]{1,0:T(1,128)S(1)} %copy-done.9, bf16[512,512]{1,0:T(8,128)(2,1)S(1)} %bitcast.30), custom_call_target="tpu_custom_call" | custom-call | flops 536870912 | bytes 2097152 | tf_op jit(solution)/shard_map/pack_grads/pallas_call | solution.py:562
  15.8 6.2 %collective-permute-done.4.refs_5_ = bf16[144,512]{1,0:T(8,128)(2,1)S(1)} collective-permute-done((bf16[144,512]{1,0:T(8,128)(2,1)}, bf16[144,512]{1,0:T(8,128)(2,1)S(1)}, u32[]{:S(2)}, u32[]{:S(2)}) %collective-permute-start.4) | collective-permute-done | bytes 147488 | tf_op jit(solution)/shard_map/ppermute | solution.py:407
  22.0 4.0 %all-to-all-start = ((bf16[8,128,512]{2,1,0:T(8,128)(2,1)}), bf16[8,128,512]{2,1,0:T(8,128)(2,1)S(1)}, u32[]{:S(2)}, u32[]{:S(2)}) async-start(bf16[8,128,512]{2,1,0:T(8,128)(2,1)} %bitcast.5), calls=%async_computation | async-start | bytes 2097152 | tf_op jit(solution)/shard_map/all_to_all | solution.py:576
  26.1 9.6 %forward.1 = (s32[1,1024]{1,0:T(1,128)}, f32[512,512]{1,0:T(8,128)}, f32[512,128]{1,0:T(8,128)}, bf16[512,512]{1,0:T(8,128)(2,1)}, bf16[512,1536]{1,0:T(8,128)(2...) custom-call(bf16[512,1536]{1,0:T(8,128)(2,1)} %refs_3_.1, f32[1,512]{1,0:T(1,128)} %bitcast.28, ...), custom_call_target="tpu_custom_call" | custom-call | flops 2952790016 | bytes 16777216 | tf_op jit(solution)/shard_map/forward/pallas_call | solution.py:582
  35.7 5.8 %all-to-all-done = bf16[8,128,512]{2,1,0:T(8,128)(2,1)S(1)} async-done(((bf16[8,128,512]{2,1,0:T(8,128)(2,1)}), bf16[8,128,512]{2,1,0:T(8,128)(2,1)S(1)}, u32[]{:S(2)}, u32[]{:S(2)}) %all-to-all-start) | async-done | bytes 1048608 | tf_op jit(solution)/shard_map/all_to_all | solution.py:576
  41.5 1.0 copy-done.11
  42.5 17.5 %backward.1 = (f32[128,2176]{1,0:T(8,128)}, f32[128,2176]{1,0:T(8,128)}, f32[128,2176]{1,0:T(8,128)}, f32[128,2176]{1,0:T(8,128)}, bf16[512,512]{1,0:T(8,128)(2,1)}, /*index=5*/f32[512,512]{1,0:T(8,128)}) custom-call(s32[1]{0:T(128)} %bitcast.me_ref, s32[1,1024]{1,0:T(1,128)} %get-tuple-element.70.pos_ref, bf16[512,512]{1,0:T(8,128)(2,1)} %w_proj_ref.1, ...), custom_call_target="tpu_custom_call" | custom-call | flops 4294967296 | bytes 16777216 | tf_op jit(solution)/shard_map/backward/pallas_call | solution.py:618
  60.0 0.1 collective-permute-start.8
  60.1 0.5 collective-permute-start.7
  60.6 2.5 %collective-permute-done.8.refs_1_ = f32[128,2176]{1,0:T(8,128)S(1)} collective-permute-done((f32[128,2176]{1,0:T(8,128)}, f32[128,2176]{1,0:T(8,128)S(1)}, u32[]{:S(2)}, u32[]{:S(2)}) %collective-permute-start.8) | collective-permute-done | bytes 1114144 | tf_op jit(solution)/shard_map/ppermute | solution.py:466
  63.0 1.2 copy-done.1
  64.3 0.3 code_first.1
  64.6 0.6 collective-permute-start.9
  65.2 9.0 %collective-permute-done.9.refs_2_ = s16[128,2176]{1,0:T(8,128)(2,1)S(1)} collective-permute-done((s16[128,2176]{1,0:T(8,128)(2,1)S(1)}, s16[128,2176]{1,0:T(8,128)(2,1)S(1)}, u32[]{:S(2)}, u32[]{:S(2)}) %collective-permute-start.9) | collective-permute-done | bytes 557088 | tf_op jit(solution)/shard_map/ppermute | solution.py:469
  74.2 2.1 %residual.1 = bf16[1024,512]{1,0:T(8,128)(2,1)} custom-call(s32[1]{0:T(128)} %bitcast.me_ref, s32[1,1024]{1,0:T(1,128)S(1)} %copy-done.6, f32[1,512]{1,0:T(1,128)S(1)} %bitcast.29, f32[512,128]{1,0:T(8,128)S(1)} %copy-done.5, f32[512,512]{1,0:T(8,128)S(1)} %copy-done.2, bf16[512,512]{1,0:T(8,128)(2,1)S(1)} %copy-done.4, f32[512,512]{1,0:T(8,128)S(1)} %copy-done.3), custom_call_target="tpu_custom_call" | custom-call | flops 536870912 | bytes 4194304 | tf_op jit(solution)/shard_map/residual/pallas_call | solution.py:663
  76.3 4.6 %all-to-all-start.1 = ((bf16[8,128,512]{2,1,0:T(8,128)(2,1)}), bf16[8,128,512]{2,1,0:T(8,128)(2,1)}, u32[]{:S(2)}, u32[]{:S(2)}) async-start(bf16[8,128,512]{2,1,0:T(8,128)(2,1)} %bitcast.7), calls=%async_computation.1 | async-start | bytes 2097152 | tf_op jit(solution)/shard_map/all_to_all | solution.py:576
  80.9 0.3 code_second.1
  81.2 1.7 %collective-permute-start.10 = (s16[64,2176]{1,0:T(8,128)(2,1)S(1)}, s16[64,2176]{1,0:T(8,128)(2,1)S(1)}, u32[]{:S(2)}, u32[]{:S(2)}) collective-permute-start(s16[64,2176]{1,0:T(8,128)(2,1)S(1)} %code_second.1), channel_id=1, source_target_pairs={{0,16},{4,12},{8,24},{12,4},{16,0},{20,28},{24,8},{28,20},{1,17},{... | collective-permute-start | bytes 835592 | tf_op jit(solution)/shard_map/ppermute | solution.py:474
  83.0 15.1 %collective-permute-done.10.refs_3_ = s16[64,2176]{1,0:T(8,128)(2,1)S(1)} collective-permute-done((s16[64,2176]{1,0:T(8,128)(2,1)S(1)}, s16[64,2176]{1,0:T(8,128)(2,1)S(1)}, u32[]{:S(2)}, u32[]{:S(2)}) %collective-permute-start.10) | collective-permute-done | bytes 278560 | tf_op jit(solution)/shard_map/ppermute | solution.py:474
  98.1 0.5 code_planes.1
  98.6 1.6 %collective-permute-start.11 = (s16[16,2176]{1,0:T(8,128)(2,1)S(1)}, s16[16,2176]{1,0:T(8,128)(2,1)S(1)}, u32[]{:S(2)}, u32[]{:S(2)}) collective-permute-start(s16[16,2176]{1,0:T(8,128)(2,1)S(1)} %get-tuple-element.87), channel_id=1, source_target_pairs={{0,1},{1,0},{2,3},{3,2},{4,5},{5,4},{6,7},{7,6},{8,9},{9,8},{10,11... | collective-permute-start | bytes 208904 | tf_op jit(solution)/shard_map/ppermute | solution.py:407
  100.2 2.6 %collective-permute-start.12 = (s16[16,2176]{1,0:T(8,128)(2,1)S(1)}, s16[16,2176]{1,0:T(8,128)(2,1)S(1)}, u32[]{:S(2)}, u32[]{:S(2)}) collective-permute-start(s16[16,2176]{1,0:T(8,128)(2,1)S(1)} %get-tuple-element.88), channel_id=1, source_target_pairs={{0,2},{1,3},{2,0},{3,1},{4,6},{5,7},{6,4},{7,5},{8,10},{9,11},{10,... | collective-permute-start | bytes 208904 | tf_op jit(solution)/shard_map/ppermute | solution.py:407
  102.8 0.2 collective-permute-start.13
  103.0 5.0 %collective-permute-done.12.refs_2_ = s16[16,2176]{1,0:T(8,128)(2,1)S(1)} collective-permute-done((s16[16,2176]{1,0:T(8,128)(2,1)S(1)}, s16[16,2176]{1,0:T(8,128)(2,1)S(1)}, u32[]{:S(2)}, u32[]{:S(2)}) %collective-permute-start.12) | collective-permute-done | bytes 69664 | tf_op jit(solution)/shard_map/ppermute | solution.py:407
  108.0 1.0 collective-permute-done.13.refs_3_
  109.0 0.2 finish.1
  109.2 1.2 collective-permute-start.14
  110.3 1.7 %collective-permute-start.15 = (bf16[16,2176]{1,0:T(8,128)(2,1)S(1)}, bf16[16,2176]{1,0:T(8,128)(2,1)S(1)}, u32[]{:S(2)}, u32[]{:S(2)}) collective-permute-start(bf16[16,2176]{1,0:T(8,128)(2,1)S(1)} %finish.1), channel_id=1, source_target_pairs={{0,2},{1,3},{2,0},{3,1},{4,6},{5,7},{6,4},{7,5},{8,10},{9,11},{10,... | collective-permute-start | bytes 208904 | tf_op jit(solution)/shard_map/ppermute | solution.py:407
  112.0 1.6 %collective-permute-start.16 = (bf16[16,2176]{1,0:T(8,128)(2,1)S(1)}, bf16[16,2176]{1,0:T(8,128)(2,1)S(1)}, u32[]{:S(2)}, u32[]{:S(2)}) collective-permute-start(bf16[16,2176]{1,0:T(8,128)(2,1)S(1)} %finish.1), channel_id=1, source_target_pairs={{0,3},{1,2},{2,1},{3,0},{4,7},{5,6},{6,5},{7,4},{8,11},{9,10},{10,... | collective-permute-start | bytes 208904 | tf_op jit(solution)/shard_map/ppermute | solution.py:407
  113.6 3.1 %collective-permute-done.15 = bf16[16,2176]{1,0:T(8,128)(2,1)S(1)} collective-permute-done((bf16[16,2176]{1,0:T(8,128)(2,1)S(1)}, bf16[16,2176]{1,0:T(8,128)(2,1)S(1)}, u32[]{:S(2)}, u32[]{:S(2)}) %collective-permute-start.15) | collective-permute-done | bytes 69664 | tf_op jit(solution)/shard_map/ppermute | solution.py:407
  116.7 1.5 %collective-permute-done.16 = bf16[16,2176]{1,0:T(8,128)(2,1)S(1)} collective-permute-done((bf16[16,2176]{1,0:T(8,128)(2,1)S(1)}, bf16[16,2176]{1,0:T(8,128)(2,1)S(1)}, u32[]{:S(2)}, u32[]{:S(2)}) %collective-permute-start.16) | collective-permute-done | bytes 69664 | tf_op jit(solution)/shard_map/ppermute | solution.py:407
  118.4 1.8 %collective-permute-start.17 = (bf16[64,2176]{1,0:T(8,128)(2,1)S(1)}, bf16[64,2176]{1,0:T(8,128)(2,1)S(1)}, u32[]{:S(2)}, u32[]{:S(2)}) collective-permute-start(bf16[64,2176]{1,0:T(8,128)(2,1)S(1)} %pad_maximum_fusion.1), channel_id=1, source_target_pairs={{0,16},{4,12},{8,24},{12,4},{16,0},{20,28},{24,8},{28,20},{1,17},{... | collective-permute-start | bytes 835592 | tf_op jit(solution)/shard_map/ppermute | solution.py:519
  120.2 4.8 %collective-permute-done.17 = bf16[64,2176]{1,0:T(8,128)(2,1)S(1)} collective-permute-done((bf16[64,2176]{1,0:T(8,128)(2,1)S(1)}, bf16[64,2176]{1,0:T(8,128)(2,1)S(1)}, u32[]{:S(2)}, u32[]{:S(2)}) %collective-permute-start.17) | collective-permute-done | bytes 278560 | tf_op jit(solution)/shard_map/ppermute | solution.py:519
  125.2 0.5 collective-permute-start.18
  125.7 9.1 %collective-permute-done.18 = bf16[128,2176]{1,0:T(8,128)(2,1)S(1)} collective-permute-done((bf16[128,2176]{1,0:T(8,128)(2,1)S(1)}, bf16[128,2176]{1,0:T(8,128)(2,1)S(1)}, u32[]{:S(2)}, u32[]{:S(2)}) %collective-permute-start.18) | collective-permute-done | bytes 557088 | tf_op jit(solution)/shard_map/ppermute | solution.py:519
  134.8 0.2 maximum_select_fusion.own_ref
  135.0 0.1 collective-permute-start.19
  135.1 2.8 %unpack.1 = bf16[512,512]{1,0:T(8,128)(2,1)} custom-call(s32[1]{0:T(128)} %bitcast.me_ref, s32[1,512]{1,0:T(1,128)S(1)} %copy-done.10, bf16[1024,512]{1,0:T(8,128)(2,1)} %bitcast.8.recv_ref), custom_call_target="tpu_custom_call" | custom-call | flops 536870912 | bytes 2097152 | tf_op jit(solution)/shard_map/unpack/pallas_call | solution.py:679
  137.9 2.2 %split.1 = (f32[512,1536]{1,0:T(8,128)}, f32[512,512]{1,0:T(8,128)}, f32[1,512]{1,0:T(1,128)}) custom-call(s32[1]{0:T(128)S(6)} %and.16.side_ref, bf16[256,2176]{1,0:T(8,128)(2,1)S(1)} %maximum_select_fusion.own_ref, bf16[256,2176]{1,0:T(8,128)(2,1)S(1)} %collective-permute-done.19.other_ref), custom_call_target="tpu_custom_call" | custom-call | bytes 8388608 | tf_op jit(solution)/shard_map/split/pallas_call | solution.py:691
  (58 shorter events, 0.4 us)
Async XLA Ops:
  0.6 12.8 %copy-start.8 = (bf16[1,512,512]{2,1,0:T(8,128)(2,1)S(1)}, bf16[1,512,512]{2,1,0:T(8,128)(2,1)}, u32[]{:S(2)}) copy-start(bf16[1,512,512]{2,1,0:T(8,128)(2,1)} %param.7) | copy-start | bytes 1572868
  3.7 4.9 %collective-permute-start = (bf16[144,512]{1,0:T(8,128)(2,1)}, bf16[144,512]{1,0:T(8,128)(2,1)S(1)}, u32[]{:S(2)}, u32[]{:S(2)}) collective-permute-start(bf16[144,512]{1,0:T(8,128)(2,1)} %get-tuple-element.51), channel_id=1, source_target_pairs={{0,4},{4,0},{8,12},{12,8},{16,20},{20,16},{24,28},{28,24},{1,5},{5... | collective-permute-start | bytes 442376 | tf_op jit(solution)/shard_map/ppermute | solution.py:407
  4.2 7.5 %collective-permute-start.1 = (bf16[144,512]{1,0:T(8,128)(2,1)}, bf16[144,512]{1,0:T(8,128)(2,1)S(1)}, u32[]{:S(2)}, u32[]{:S(2)}) collective-permute-start(bf16[144,512]{1,0:T(8,128)(2,1)} %get-tuple-element.56), channel_id=1, source_target_pairs={{0,8},{4,12},{8,0},{12,4},{16,24},{20,28},{24,16},{28,20},{1,9},{5... | collective-permute-start | bytes 442376 | tf_op jit(solution)/shard_map/ppermute | solution.py:407
  6.8 9.0 %collective-permute-start.2 = (bf16[144,512]{1,0:T(8,128)(2,1)}, bf16[144,512]{1,0:T(8,128)(2,1)S(1)}, u32[]{:S(2)}, u32[]{:S(2)}) collective-permute-start(bf16[144,512]{1,0:T(8,128)(2,1)} %get-tuple-element.57), channel_id=1, source_target_pairs={{0,12},{4,8},{8,4},{12,0},{16,28},{20,24},{24,20},{28,16},{1,13},{... | collective-permute-start | bytes 442376 | tf_op jit(solution)/shard_map/ppermute | solution.py:407
  6.8 9.0 %collective-permute-start.3 = (bf16[144,512]{1,0:T(8,128)(2,1)}, bf16[144,512]{1,0:T(8,128)(2,1)S(1)}, u32[]{:S(2)}, u32[]{:S(2)}) collective-permute-start(bf16[144,512]{1,0:T(8,128)(2,1)} %get-tuple-element.58), channel_id=1, source_target_pairs={{0,16},{4,20},{8,24},{12,28},{16,0},{20,4},{24,8},{28,12},{1,17},{... | collective-permute-start | bytes 442376 | tf_op jit(solution)/shard_map/ppermute | solution.py:407
  8.6 13.4 %collective-permute-start.4 = (bf16[144,512]{1,0:T(8,128)(2,1)}, bf16[144,512]{1,0:T(8,128)(2,1)S(1)}, u32[]{:S(2)}, u32[]{:S(2)}) collective-permute-start(bf16[144,512]{1,0:T(8,128)(2,1)} %get-tuple-element.59), channel_id=1, source_target_pairs={{0,20},{4,16},{8,28},{12,24},{16,4},{20,0},{24,12},{28,8},{1,21},{... | collective-permute-start | bytes 442376 | tf_op jit(solution)/shard_map/ppermute | solution.py:407
  8.6 13.4 %copy-start.12 = (bf16[144,512]{1,0:T(8,128)(2,1)}, bf16[144,512]{1,0:T(8,128)(2,1)S(1)}, u32[]{:S(2)}) copy-start(bf16[144,512]{1,0:T(8,128)(2,1)S(1)} %collective-permute-done.refs_1_) | copy-start | bytes 442372
  8.6 13.4 %collective-permute-start.5 = (bf16[144,512]{1,0:T(8,128)(2,1)}, bf16[144,512]{1,0:T(8,128)(2,1)S(1)}, u32[]{:S(2)}, u32[]{:S(2)}) collective-permute-start(bf16[144,512]{1,0:T(8,128)(2,1)} %get-tuple-element.60), channel_id=1, source_target_pairs={{0,24},{4,28},{8,16},{12,20},{16,8},{20,12},{24,0},{28,4},{1,25},{... | collective-permute-start | bytes 442376 | tf_op jit(solution)/shard_map/ppermute | solution.py:407
  11.7 10.4 %copy-start.13 = (bf16[144,512]{1,0:T(8,128)(2,1)}, bf16[144,512]{1,0:T(8,128)(2,1)S(1)}, u32[]{:S(2)}) copy-start(bf16[144,512]{1,0:T(8,128)(2,1)S(1)} %collective-permute-done.1.refs_2_) | copy-start | bytes 442372
  11.7 10.3 %collective-permute-start.6 = (bf16[144,512]{1,0:T(8,128)(2,1)}, bf16[144,512]{1,0:T(8,128)(2,1)S(1)}, u32[]{:S(2)}, u32[]{:S(2)}) collective-permute-start(bf16[144,512]{1,0:T(8,128)(2,1)} %get-tuple-element.61), channel_id=1, source_target_pairs={{0,28},{4,24},{8,20},{12,16},{16,12},{20,8},{24,4},{28,0},{1,29},{... | collective-permute-start | bytes 442376 | tf_op jit(solution)/shard_map/ppermute | solution.py:407
  13.4 0.7 copy-start.9
  15.8 10.3 %copy-start.14 = (bf16[144,512]{1,0:T(8,128)(2,1)}, bf16[144,512]{1,0:T(8,128)(2,1)S(1)}, u32[]{:S(2)}) copy-start(bf16[144,512]{1,0:T(8,128)(2,1)S(1)} %collective-permute-done.2.refs_3_) | copy-start | bytes 442372
  15.8 10.3 %copy-start.15 = (bf16[144,512]{1,0:T(8,128)(2,1)}, bf16[144,512]{1,0:T(8,128)(2,1)S(1)}, u32[]{:S(2)}) copy-start(bf16[144,512]{1,0:T(8,128)(2,1)S(1)} %collective-permute-done.3.refs_4_) | copy-start | bytes 442372
  22.0 4.1 %copy-start.16 = (bf16[144,512]{1,0:T(8,128)(2,1)}, bf16[144,512]{1,0:T(8,128)(2,1)S(1)}, u32[]{:S(2)}) copy-start(bf16[144,512]{1,0:T(8,128)(2,1)S(1)} %collective-permute-done.4.refs_5_) | copy-start | bytes 442372
  22.0 4.1 %copy-start.17 = (bf16[144,512]{1,0:T(8,128)(2,1)}, bf16[144,512]{1,0:T(8,128)(2,1)S(1)}, u32[]{:S(2)}) copy-start(bf16[144,512]{1,0:T(8,128)(2,1)S(1)} %collective-permute-done.5.refs_6_) | copy-start | bytes 442372
  22.0 4.1 %copy-start.18 = (bf16[144,512]{1,0:T(8,128)(2,1)}, bf16[144,512]{1,0:T(8,128)(2,1)S(1)}, u32[]{:S(2)}) copy-start(bf16[144,512]{1,0:T(8,128)(2,1)S(1)} %collective-permute-done.6.refs_7_) | copy-start | bytes 442372
  22.0 19.5 %all-to-all-start = ((bf16[8,128,512]{2,1,0:T(8,128)(2,1)}), bf16[8,128,512]{2,1,0:T(8,128)(2,1)S(1)}, u32[]{:S(2)}, u32[]{:S(2)}) async-start(bf16[8,128,512]{2,1,0:T(8,128)(2,1)} %bitcast.5), calls=%async_computation | async-start | bytes 2097152 | tf_op jit(solution)/shard_map/all_to_all | solution.py:576
  41.5 1.0 copy-start.11
  42.5 31.7 %copy-start.5 = (f32[512,128]{1,0:T(8,128)S(1)}, f32[512,128]{1,0:T(8,128)}, u32[]{:S(2)}) copy-start(f32[512,128]{1,0:T(8,128)} %get-tuple-element.90.inv_ref) | copy-start | bytes 786436
  60.0 3.0 %collective-permute-start.8 = (f32[128,2176]{1,0:T(8,128)}, f32[128,2176]{1,0:T(8,128)S(1)}, u32[]{:S(2)}, u32[]{:S(2)}) collective-permute-start(f32[128,2176]{1,0:T(8,128)} %get-tuple-element.82), channel_id=1, source_target_pairs={{0,4},{4,0},{8,12},{12,8},{16,20},{20,16},{24,28},{28,24},{1,5},{5... | collective-permute-start | bytes 3342344 | tf_op jit(solution)/shard_map/ppermute | solution.py:466
  60.1 5.1 %collective-permute-start.7 = (f32[128,2176]{1,0:T(8,128)}, f32[128,2176]{1,0:T(8,128)S(1)}, u32[]{:S(2)}, u32[]{:S(2)}) collective-permute-start(f32[128,2176]{1,0:T(8,128)} %get-tuple-element.80), channel_id=1, source_target_pairs={{0,4},{4,0},{8,12},{12,8},{16,20},{20,16},{24,28},{28,24},{1,5},{5... | collective-permute-start | bytes 3342344 | tf_op jit(solution)/shard_map/ppermute | solution.py:467
  63.0 1.2 copy-start.1
  64.3 9.9 %copy-start.2 = (f32[512,512]{1,0:T(8,128)S(1)}, f32[512,512]{1,0:T(8,128)}, u32[]{:S(2)}) copy-start(f32[512,512]{1,0:T(8,128)} %get-tuple-element.75.refs_4_.xhat_ref) | copy-start | bytes 3145732
  64.3 9.9 %copy-start.3 = (f32[512,512]{1,0:T(8,128)S(1)}, f32[512,512]{1,0:T(8,128)}, u32[]{:S(2)}) copy-start(f32[512,512]{1,0:T(8,128)} %get-tuple-element.92.d_normed_ref) | copy-start | bytes 3145732
  64.3 9.9 %copy-start.4 = (bf16[512,512]{1,0:T(8,128)(2,1)S(1)}, bf16[512,512]{1,0:T(8,128)(2,1)}, u32[]{:S(2)}) copy-start(bf16[512,512]{1,0:T(8,128)(2,1)} %get-tuple-element.91.serial_grad_ref) | copy-start | bytes 1572868
  64.3 9.9 %copy-start.6 = (s32[1,1024]{1,0:T(1,128)S(1)}, s32[1,1024]{1,0:T(1,128)}, u32[]{:S(2)}) copy-start(s32[1,1024]{1,0:T(1,128)} %get-tuple-element.70.pos_ref) | copy-start | bytes 12292
  64.3 10.0 %copy-start.7 = (f32[512]{0:T(512)S(1)}, f32[512]{0:T(512)}, u32[]{:S(2)}) copy-start(f32[512]{0:T(512)} %param.11) | copy-start | bytes 6148
  64.6 9.6 %collective-permute-start.9 = (s16[128,2176]{1,0:T(8,128)(2,1)S(1)}, s16[128,2176]{1,0:T(8,128)(2,1)S(1)}, u32[]{:S(2)}, u32[]{:S(2)}) collective-permute-start(s16[128,2176]{1,0:T(8,128)(2,1)S(1)} %code_first.1), channel_id=1, source_target_pairs={{0,8},{4,20},{8,0},{12,28},{16,24},{20,4},{24,16},{28,12},{1,9},{5... | collective-permute-start | bytes 1671176 | tf_op jit(solution)/shard_map/ppermute | solution.py:469
  76.3 4.6 %copy-start = (f32[128,2176]{1,0:T(8,128)S(1)}, f32[128,2176]{1,0:T(8,128)}, u32[]{:S(2)}) copy-start(f32[128,2176]{1,0:T(8,128)} %get-tuple-element.83.refs_0_) | copy-start | bytes 3342340
  76.3 32.8 %all-to-all-start.1 = ((bf16[8,128,512]{2,1,0:T(8,128)(2,1)}), bf16[8,128,512]{2,1,0:T(8,128)(2,1)}, u32[]{:S(2)}, u32[]{:S(2)}) async-start(bf16[8,128,512]{2,1,0:T(8,128)(2,1)} %bitcast.7), calls=%async_computation.1 | async-start | bytes 2097152 | tf_op jit(solution)/shard_map/all_to_all | solution.py:576
  81.2 16.8 %collective-permute-start.10 = (s16[64,2176]{1,0:T(8,128)(2,1)S(1)}, s16[64,2176]{1,0:T(8,128)(2,1)S(1)}, u32[]{:S(2)}, u32[]{:S(2)}) collective-permute-start(s16[64,2176]{1,0:T(8,128)(2,1)S(1)} %code_second.1), channel_id=1, source_target_pairs={{0,16},{4,12},{8,24},{12,4},{16,0},{20,28},{24,8},{28,20},{1,17},{... | collective-permute-start | bytes 835592 | tf_op jit(solution)/shard_map/ppermute | solution.py:474
  98.6 4.5 %collective-permute-start.11 = (s16[16,2176]{1,0:T(8,128)(2,1)S(1)}, s16[16,2176]{1,0:T(8,128)(2,1)S(1)}, u32[]{:S(2)}, u32[]{:S(2)}) collective-permute-start(s16[16,2176]{1,0:T(8,128)(2,1)S(1)} %get-tuple-element.87), channel_id=1, source_target_pairs={{0,1},{1,0},{2,3},{3,2},{4,5},{5,4},{6,7},{7,6},{8,9},{9,8},{10,11... | collective-permute-start | bytes 208904 | tf_op jit(solution)/shard_map/ppermute | solution.py:407
  100.2 7.8 %collective-permute-start.12 = (s16[16,2176]{1,0:T(8,128)(2,1)S(1)}, s16[16,2176]{1,0:T(8,128)(2,1)S(1)}, u32[]{:S(2)}, u32[]{:S(2)}) collective-permute-start(s16[16,2176]{1,0:T(8,128)(2,1)S(1)} %get-tuple-element.88), channel_id=1, source_target_pairs={{0,2},{1,3},{2,0},{3,1},{4,6},{5,7},{6,4},{7,5},{8,10},{9,11},{10,... | collective-permute-start | bytes 208904 | tf_op jit(solution)/shard_map/ppermute | solution.py:407
  102.8 6.2 %collective-permute-start.13 = (s16[16,2176]{1,0:T(8,128)(2,1)S(1)}, s16[16,2176]{1,0:T(8,128)(2,1)S(1)}, u32[]{:S(2)}, u32[]{:S(2)}) collective-permute-start(s16[16,2176]{1,0:T(8,128)(2,1)S(1)} %get-tuple-element.89), channel_id=1, source_target_pairs={{0,3},{1,2},{2,1},{3,0},{4,7},{5,6},{6,5},{7,4},{8,11},{9,10},{10,... | collective-permute-start | bytes 208904 | tf_op jit(solution)/shard_map/ppermute | solution.py:407
  109.2 4.4 %collective-permute-start.14 = (bf16[16,2176]{1,0:T(8,128)(2,1)S(1)}, bf16[16,2176]{1,0:T(8,128)(2,1)S(1)}, u32[]{:S(2)}, u32[]{:S(2)}) collective-permute-start(bf16[16,2176]{1,0:T(8,128)(2,1)S(1)} %finish.1), channel_id=1, source_target_pairs={{0,1},{1,0},{2,3},{3,2},{4,5},{5,4},{6,7},{7,6},{8,9},{9,8},{10,11... | collective-permute-start | bytes 208904 | tf_op jit(solution)/shard_map/ppermute | solution.py:407
  110.3 6.4 %collective-permute-start.15 = (bf16[16,2176]{1,0:T(8,128)(2,1)S(1)}, bf16[16,2176]{1,0:T(8,128)(2,1)S(1)}, u32[]{:S(2)}, u32[]{:S(2)}) collective-permute-start(bf16[16,2176]{1,0:T(8,128)(2,1)S(1)} %finish.1), channel_id=1, source_target_pairs={{0,2},{1,3},{2,0},{3,1},{4,6},{5,7},{6,4},{7,5},{8,10},{9,11},{10,... | collective-permute-start | bytes 208904 | tf_op jit(solution)/shard_map/ppermute | solution.py:407
  112.0 6.2 %collective-permute-start.16 = (bf16[16,2176]{1,0:T(8,128)(2,1)S(1)}, bf16[16,2176]{1,0:T(8,128)(2,1)S(1)}, u32[]{:S(2)}, u32[]{:S(2)}) collective-permute-start(bf16[16,2176]{1,0:T(8,128)(2,1)S(1)} %finish.1), channel_id=1, source_target_pairs={{0,3},{1,2},{2,1},{3,0},{4,7},{5,6},{6,5},{7,4},{8,11},{9,10},{10,... | collective-permute-start | bytes 208904 | tf_op jit(solution)/shard_map/ppermute | solution.py:407
  118.4 6.6 %collective-permute-start.17 = (bf16[64,2176]{1,0:T(8,128)(2,1)S(1)}, bf16[64,2176]{1,0:T(8,128)(2,1)S(1)}, u32[]{:S(2)}, u32[]{:S(2)}) collective-permute-start(bf16[64,2176]{1,0:T(8,128)(2,1)S(1)} %pad_maximum_fusion.1), channel_id=1, source_target_pairs={{0,16},{4,12},{8,24},{12,4},{16,0},{20,28},{24,8},{28,20},{1,17},{... | collective-permute-start | bytes 835592 | tf_op jit(solution)/shard_map/ppermute | solution.py:519
  125.2 9.6 %collective-permute-start.18 = (bf16[128,2176]{1,0:T(8,128)(2,1)S(1)}, bf16[128,2176]{1,0:T(8,128)(2,1)S(1)}, u32[]{:S(2)}, u32[]{:S(2)}) collective-permute-start(bf16[128,2176]{1,0:T(8,128)(2,1)S(1)} %broadcast_select_fusion), channel_id=1, source_target_pairs={{0,8},{4,20},{8,0},{12,28},{16,24},{20,4},{24,16},{28,12},{1,9},{5... | collective-permute-start | bytes 1671176 | tf_op jit(solution)/shard_map/ppermute | solution.py:519
  125.7 9.4 %copy-start.10 = (s32[1,512]{1,0:T(1,128)S(1)}, s32[1,512]{1,0:T(1,128)}, u32[]{:S(2)}) copy-start(s32[1,512]{1,0:T(1,128)} %get-tuple-element.53.slot_ref) | copy-start | bytes 6148
  135.0 2.9 %collective-permute-start.19 = (bf16[256,2176]{1,0:T(8,128)(2,1)S(1)}, bf16[256,2176]{1,0:T(8,128)(2,1)S(1)}, u32[]{:S(2)}, u32[]{:S(2)}) collective-permute-start(bf16[256,2176]{1,0:T(8,128)(2,1)S(1)} %maximum_select_fusion.own_ref), channel_id=1, source_target_pairs={{0,4},{4,0},{8,12},{12,8},{16,20},{20,16},{24,28},{28,24},{1,5},{5... | collective-permute-start | bytes 3342344 | tf_op jit(solution)/shard_map/ppermute | solution.py:678

commit v9 on v8

--- a/solution.py
+++ b/solution.py
@@ -481,7 +481,7 @@
     return part
 
 
-def reduce_over_planes(terms, got, steps):
+def reduce_over_planes(terms, got, steps, later):
     n_dp, plane = lax.axis_size("dp"), lax.axis_index("dp")
     rows, width = got.shape
     parts = ["second"] * len(terms) + ["all"]
@@ -491,7 +491,9 @@
         )[0]
         part = halves_of_plain(part, steps[2:])
         pieces = [piece([part], lax.bitwise_xor(plane, k), n_dp) for k in range(n_dp)]
-        return functools.reduce(jnp.add, by_distance(pieces, "dp")).astype(BF16)
+        arrived = by_distance(pieces, "dp")
+        arrived[1], later = lax.optimization_barrier((arrived[1], later))
+        return functools.reduce(jnp.add, arrived).astype(BF16), later
     size = rows // n_dp
     own, *sent = small_kernel(
         functools.partial(pieces_kernel, parts, n_dp),
@@ -502,7 +504,8 @@
         name="code_planes",
     )
     arrived = by_distance([own] + sent, "dp")
-    return small_kernel(finish_kernel, [shape_of((size, width), BF16)], arrived, name="finish")[0]
+    arrived[1], later = lax.optimization_barrier((arrived[1], later))
+    return small_kernel(finish_kernel, [shape_of((size, width), BF16)], arrived, name="finish")[0], later
 
 
 def share_over_planes(part):
@@ -659,7 +662,6 @@
 
     steps = chip_steps()
     terms = first_step(quarters, steps)
-    d_normed, terms = lax.optimization_barrier((d_normed, terms))
     back = pl.pallas_call(
         functools.partial(residual_kernel, n_seq),
         out_shape=shape_of((slots, width), BF16),
@@ -671,10 +673,12 @@
         ),
         name="residual",
     )(me, pos, gain_row, inv, xhat, serial_grad, d_normed)
+    terms, got = second_step(terms, steps)
+    got, back = lax.optimization_barrier((got, back))
+    part, back = reduce_over_planes(terms, got, steps, back)
     returned = exchange(back)
-    terms, got = second_step(terms, steps)
-    part, returned = lax.optimization_barrier((reduce_over_planes(terms, got, steps), returned))
-    own = share_in_plane(share_over_planes(part), steps)
+    part, returned = lax.optimization_barrier((share_over_planes(part), returned))
+    own = share_in_plane(part, steps)
     other = lax.ppermute(own, "seq", core_pairs())
     grad_local = pl.pallas_call(
         functools.partial(unpack_kernel, n_seq),

time: 141 us -> 139 us (0.986)
  starting transfers between devices: 32.1 us -> 28.6 us
  local copies, waits for them, and re-layouts: 3.18 us -> 6.4 us
    all_to_all x2, waiting for transfers between devices: 5.8 us -> 21 us  [exchange(): got = lax.all_to_all(sent, 'seq', split_axis=0, concat_axis=0, tiled=True)]
    ppermute x1, waiting for transfers between devices: 15.1 us -> 0.81 us  [second_step(): return (terms, lax.ppermute(sent, 'seq', steps[1][0]))]
    ppermute x13, waiting for transfers between devices: 17.3 us -> 12.7 us  [by_distance(): lax.ppermute(blocks[k], axis, [(i, i ^ k) for i in range(count)])]
    unnamed x46 -> x38, local copies, waits for them, and re-layouts: 3.17 us -> 6.36 us
    pallas_call x4, Pallas kernels: 1.22 us -> 2.89 us  [small_kernel(): pl.pallas_call(kernel, out_shape=outs, in_specs=[in_smem] * scalars + [in...]
  transfers between devices with their start and end apart: 22 -> 22, of which waited for: 12 -> 13; matrix products, arithmetic and copies ran while one was open for 0% -> 0% of each run, Pallas kernels for 11% -> 11%
where the time goes in v9:
time: 139 us
  waiting for transfers between devices  62.1 us (45%)
  Pallas kernels  40.4 us (29%)
  starting transfers between devices  28.6 us (21%)
  local copies, waits for them, and re-layouts  6.4 us (5%)
    all_to_all x2, waiting for transfers between devices, exchange(): got = lax.all_to_all(sent, 'seq', split_axis=0, concat_axis=0, tiled=True)  21 us
    ppermute x13, starting transfers between devices, by_distance(): lax.ppermute(blocks[k], axis, [(i, i ^ k) for i in range(count)])  18.1 us
    pallas_call x1, Pallas kernels, per_device(): pl.pallas_call(functools.partial(backward_kernel, n_seq, chip_bits), grid...  17.4 us
    ppermute x2, waiting for transfers between devices, share_in_plane(): other = lax.ppermute(part, 'seq', pairs)  15 us
    ppermute x13, waiting for transfers between devices, by_distance(): lax.ppermute(blocks[k], axis, [(i, i ^ k) for i in range(count)])  12.7 us
    pallas_call x1, Pallas kernels, per_device(): pl.pallas_call(functools.partial(forward_kernel, n_seq, capacity), grid=(...  9.57 us
    ppermute x1, waiting for transfers between devices, first_step(): return [own_keep, got_keep, lax.ppermute(sent, 'seq', steps[0][0])]  9 us
    all_to_all x2, starting transfers between devices, exchange(): got = lax.all_to_all(sent, 'seq', split_axis=0, concat_axis=0, tiled=True)  7.61 us
  transfers between devices with their start and end apart: 22, of which 13 were waited for; matrix products, arithmetic and copies ran while one was open for 0% of the time, Pallas kernels for 11%

profile of v9, /device:TPU:0, one launch (start us, length us, event | category | flops | bytes accessed | tf_op | source)
XLA Modules:
  0.0 138.8 jit_solution(13825763450217345378)
XLA Ops:
  0.6 3.0 %pack.1 = (s32[1,512]{1,0:T(1,128)}, bf16[144,512]{1,0:T(8,128)(2,1)}, bf16[144,512]{1,0:T(8,128)(2,1)}, bf16[144,512]{1,0:T(8,128)(2,1)}, bf16[144,512]{1,0:T(8...) custom-call(s32[1]{0:T(128)} %bitcast.me_ref, ...), custom_call_target="tpu_custom_call" | custom-call | flops 536870912 | bytes 2097152 | tf_op jit(solution)/shard_map/pack/pallas_call | solution.py:547
  3.7 0.5 collective-permute-start
  4.2 2.6 %collective-permute-start.1 = (bf16[144,512]{1,0:T(8,128)(2,1)}, bf16[144,512]{1,0:T(8,128)(2,1)S(1)}, u32[]{:S(2)}, u32[]{:S(2)}) collective-permute-start(bf16[144,512]{1,0:T(8,128)(2,1)} %get-tuple-element.56), channel_id=1, source_target_pairs={{0,8},{4,12},{8,0},{12,4},{16,24},{20,28},{24,16},{28,20},{1,9},{5... | collective-permute-start | bytes 442376 | tf_op jit(solution)/shard_map/ppermute | solution.py:407
  6.8 1.8 %collective-permute-start.3 = (bf16[144,512]{1,0:T(8,128)(2,1)}, bf16[144,512]{1,0:T(8,128)(2,1)S(1)}, u32[]{:S(2)}, u32[]{:S(2)}) collective-permute-start(bf16[144,512]{1,0:T(8,128)(2,1)} %get-tuple-element.58), channel_id=1, source_target_pairs={{0,16},{4,20},{8,24},{12,28},{16,0},{20,4},{24,8},{28,12},{1,17},{... | collective-permute-start | bytes 442376 | tf_op jit(solution)/shard_map/ppermute | solution.py:407
  8.6 2.6 %collective-permute-start.5 = (bf16[144,512]{1,0:T(8,128)(2,1)}, bf16[144,512]{1,0:T(8,128)(2,1)S(1)}, u32[]{:S(2)}, u32[]{:S(2)}) collective-permute-start(bf16[144,512]{1,0:T(8,128)(2,1)} %get-tuple-element.60), channel_id=1, source_target_pairs={{0,24},{4,28},{8,16},{12,20},{16,8},{20,12},{24,0},{28,4},{1,25},{... | collective-permute-start | bytes 442376 | tf_op jit(solution)/shard_map/ppermute | solution.py:407
  11.2 0.5 collective-permute-done.1.refs_2_
  11.7 1.7 %collective-permute-start.6 = (bf16[144,512]{1,0:T(8,128)(2,1)}, bf16[144,512]{1,0:T(8,128)(2,1)S(1)}, u32[]{:S(2)}, u32[]{:S(2)}) collective-permute-start(bf16[144,512]{1,0:T(8,128)(2,1)} %get-tuple-element.61), channel_id=1, source_target_pairs={{0,28},{4,24},{8,20},{12,16},{16,12},{20,8},{24,4},{28,0},{1,29},{... | collective-permute-start | bytes 442376 | tf_op jit(solution)/shard_map/ppermute | solution.py:407
  13.4 0.7 copy-done.9
  14.1 1.7 %pack_grads.1 = bf16[1024,512]{1,0:T(8,128)(2,1)} custom-call(s32[1]{0:T(128)} %bitcast.me_ref, s32[1,512]{1,0:T(1,128)S(1)} %copy-done.9, bf16[512,512]{1,0:T(8,128)(2,1)S(1)} %bitcast.27), custom_call_target="tpu_custom_call" | custom-call | flops 536870912 | bytes 2097152 | tf_op jit(solution)/shard_map/pack_grads/pallas_call | solution.py:565
  15.8 6.2 %collective-permute-done.4.refs_5_ = bf16[144,512]{1,0:T(8,128)(2,1)S(1)} collective-permute-done((bf16[144,512]{1,0:T(8,128)(2,1)}, bf16[144,512]{1,0:T(8,128)(2,1)S(1)}, u32[]{:S(2)}, u32[]{:S(2)}) %collective-permute-start.4) | collective-permute-done | bytes 147488 | tf_op jit(solution)/shard_map/ppermute | solution.py:407
  22.1 4.0 %all-to-all-start = ((bf16[8,128,512]{2,1,0:T(8,128)(2,1)}), bf16[8,128,512]{2,1,0:T(8,128)(2,1)S(1)}, u32[]{:S(2)}, u32[]{:S(2)}) async-start(bf16[8,128,512]{2,1,0:T(8,128)(2,1)} %bitcast.5), calls=%async_computation | async-start | bytes 2097152 | tf_op jit(solution)/shard_map/all_to_all | solution.py:579
  26.2 9.6 %forward.1 = (s32[1,1024]{1,0:T(1,128)}, f32[512,512]{1,0:T(8,128)}, f32[512,128]{1,0:T(8,128)}, bf16[512,512]{1,0:T(8,128)(2,1)}, bf16[512,1536]{1,0:T(8,128)(2...) custom-call(bf16[512,1536]{1,0:T(8,128)(2,1)} %refs_3_.1, f32[1,512]{1,0:T(1,128)} %bitcast.25, ...), custom_call_target="tpu_custom_call" | custom-call | flops 2952790016 | bytes 16777216 | tf_op jit(solution)/shard_map/forward/pallas_call | solution.py:585
  35.7 5.8 %all-to-all-done = bf16[8,128,512]{2,1,0:T(8,128)(2,1)S(1)} async-done(((bf16[8,128,512]{2,1,0:T(8,128)(2,1)}), bf16[8,128,512]{2,1,0:T(8,128)(2,1)S(1)}, u32[]{:S(2)}, u32[]{:S(2)}) %all-to-all-start) | async-done | bytes 1048608 | tf_op jit(solution)/shard_map/all_to_all | solution.py:579
  41.5 1.0 copy-done.11
  42.5 17.4 %backward.1 = (f32[128,2176]{1,0:T(8,128)}, f32[128,2176]{1,0:T(8,128)}, f32[128,2176]{1,0:T(8,128)}, f32[128,2176]{1,0:T(8,128)}, bf16[512,512]{1,0:T(8,128)(2,1)}, /*index=5*/f32[512,512]{1,0:T(8,128)}) custom-call(s32[1]{0:T(128)} %bitcast.me_ref, s32[1,1024]{1,0:T(1,128)} %get-tuple-element.70.pos_ref, bf16[512,512]{1,0:T(8,128)(2,1)} %w_proj_ref.1, ...), custom_call_target="tpu_custom_call" | custom-call | flops 4294967296 | bytes 16777216 | tf_op jit(solution)/shard_map/backward/pallas_call | solution.py:621
  60.0 0.5 collective-permute-start.7
  60.5 2.5 %collective-permute-done.8.refs_1_ = f32[128,2176]{1,0:T(8,128)S(1)} collective-permute-done((f32[128,2176]{1,0:T(8,128)}, f32[128,2176]{1,0:T(8,128)S(1)}, u32[]{:S(2)}, u32[]{:S(2)}) %collective-permute-start.8) | collective-permute-done | bytes 1114144 | tf_op jit(solution)/shard_map/ppermute | solution.py:466
  63.0 1.2 copy-done.1
  64.2 0.3 code_first.1
  64.5 0.6 collective-permute-start.9
  65.1 9.0 %collective-permute-done.9.refs_2_ = s16[128,2176]{1,0:T(8,128)(2,1)S(1)} collective-permute-done((s16[128,2176]{1,0:T(8,128)(2,1)S(1)}, s16[128,2176]{1,0:T(8,128)(2,1)S(1)}, u32[]{:S(2)}, u32[]{:S(2)}) %collective-permute-start.9) | collective-permute-done | bytes 557088 | tf_op jit(solution)/shard_map/ppermute | solution.py:469
  74.1 1.0 code_second.1
  75.1 0.6 collective-permute-start.10
  75.7 1.2 copy-done.2
  76.9 1.2 copy-done.3
  78.1 0.9 copy-done.5
  79.1 2.1 %residual.1 = bf16[1024,512]{1,0:T(8,128)(2,1)} custom-call(s32[1]{0:T(128)} %bitcast.me_ref, s32[1,1024]{1,0:T(1,128)S(1)} %copy-done.6, f32[1,512]{1,0:T(1,128)S(1)} %bitcast.26, f32[512,128]{1,0:T(8,128)S(1)} %copy-done.5, f32[512,512]{1,0:T(8,128)S(1)} %copy-done.2, bf16[512,512]{1,0:T(8,128)(2,1)S(1)} %copy-done.4, f32[512,512]{1,0:T(8,128)S(1)} %copy-done.3), custom_call_target="tpu_custom_call" | custom-call | flops 536870912 | bytes 4194304 | tf_op jit(solution)/shard_map/residual/pallas_call | solution.py:665
  81.2 0.8 collective-permute-done.10.refs_3_
  82.0 1.5 %code_planes.1 = (f32[16,2176]{1,0:T(8,128)S(1)}, s16[16,2176]{1,0:T(8,128)(2,1)S(1)}, s16[16,2176]{1,0:T(8,128)(2,1)S(1)}, s16[16,2176]{1,0:T(8,128)(2,1)S(1)}) custom-call(s32[1]{0:T(128)} %bitcast.2.plane_ref, f32[128,2176]{1,0:T(8,128)S(1)} %copy-done, f32[128,2176]{1,0:T(8,128)S(1)} %collective-permute-done.7.refs_1_, ...), custom_call_target="tpu_custom_call" | custom-call | flops 6823944 | bytes 3411972 | tf_op jit(solution)/shard_map/code_planes/pallas_call | solution.py:444
  83.4 1.6 %collective-permute-start.11 = (s16[16,2176]{1,0:T(8,128)(2,1)S(1)}, s16[16,2176]{1,0:T(8,128)(2,1)S(1)}, u32[]{:S(2)}, u32[]{:S(2)}) collective-permute-start(s16[16,2176]{1,0:T(8,128)(2,1)S(1)} %get-tuple-element.87), channel_id=1, source_target_pairs={{0,1},{1,0},{2,3},{3,2},{4,5},{5,4},{6,7},{7,6},{8,9},{9,8},{10,11... | collective-permute-start | bytes 208904 | tf_op jit(solution)/shard_map/ppermute | solution.py:407
  85.1 2.6 %collective-permute-start.12 = (s16[16,2176]{1,0:T(8,128)(2,1)S(1)}, s16[16,2176]{1,0:T(8,128)(2,1)S(1)}, u32[]{:S(2)}, u32[]{:S(2)}) collective-permute-start(s16[16,2176]{1,0:T(8,128)(2,1)S(1)} %get-tuple-element.90), channel_id=1, source_target_pairs={{0,2},{1,3},{2,0},{3,1},{4,6},{5,7},{6,4},{7,5},{8,10},{9,11},{10,... | collective-permute-start | bytes 208904 | tf_op jit(solution)/shard_map/ppermute | solution.py:407
  87.7 0.2 collective-permute-start.13
  87.9 0.3 collective-permute-done.11.refs_1_
  88.2 3.6 %collective-permute-done.12.refs_2_ = s16[16,2176]{1,0:T(8,128)(2,1)S(1)} collective-permute-done((s16[16,2176]{1,0:T(8,128)(2,1)S(1)}, s16[16,2176]{1,0:T(8,128)(2,1)S(1)}, u32[]{:S(2)}, u32[]{:S(2)}) %collective-permute-start.12) | collective-permute-done | bytes 69664 | tf_op jit(solution)/shard_map/ppermute | solution.py:407
  91.8 2.1 %collective-permute-done.13.refs_3_ = s16[16,2176]{1,0:T(8,128)(2,1)S(1)} collective-permute-done((s16[16,2176]{1,0:T(8,128)(2,1)S(1)}, s16[16,2176]{1,0:T(8,128)(2,1)S(1)}, u32[]{:S(2)}, u32[]{:S(2)}) %collective-permute-start.13) | collective-permute-done | bytes 69664 | tf_op jit(solution)/shard_map/ppermute | solution.py:407
  94.1 0.8 collective-permute-start.16
  94.9 1.1 collective-permute-start.14
  96.0 2.4 %collective-permute-start.15 = (bf16[16,2176]{1,0:T(8,128)(2,1)S(1)}, bf16[16,2176]{1,0:T(8,128)(2,1)S(1)}, u32[]{:S(2)}, u32[]{:S(2)}) collective-permute-start(bf16[16,2176]{1,0:T(8,128)(2,1)S(1)} %finish.1), channel_id=1, source_target_pairs={{0,2},{1,3},{2,0},{3,1},{4,6},{5,7},{6,4},{7,5},{8,10},{9,11},{10,... | collective-permute-start | bytes 208904 | tf_op jit(solution)/shard_map/ppermute | solution.py:407
  98.5 3.6 %all-to-all-start.1 = ((bf16[8,128,512]{2,1,0:T(8,128)(2,1)}), bf16[8,128,512]{2,1,0:T(8,128)(2,1)S(1)}, u32[]{:S(2)}, u32[]{:S(2)}) async-start(bf16[8,128,512]{2,1,0:T(8,128)(2,1)} %bitcast.15), calls=%async_computation.1 | async-start | bytes 2097152 | tf_op jit(solution)/shard_map/all_to_all | solution.py:579
  102.2 15.2 %all-to-all-done.1 = bf16[8,128,512]{2,1,0:T(8,128)(2,1)S(1)} async-done(((bf16[8,128,512]{2,1,0:T(8,128)(2,1)}), bf16[8,128,512]{2,1,0:T(8,128)(2,1)S(1)}, u32[]{:S(2)}, u32[]{:S(2)}) %all-to-all-start.1) | async-done | bytes 1048608 | tf_op jit(solution)/shard_map/all_to_all | solution.py:579
  117.4 0.5 collective-permute-start.17
  117.9 6.0 %collective-permute-done.17 = bf16[64,2176]{1,0:T(8,128)(2,1)S(1)} collective-permute-done((bf16[64,2176]{1,0:T(8,128)(2,1)S(1)}, bf16[64,2176]{1,0:T(8,128)(2,1)S(1)}, u32[]{:S(2)}, u32[]{:S(2)}) %collective-permute-start.17) | collective-permute-done | bytes 278560 | tf_op jit(solution)/shard_map/ppermute | solution.py:522
  124.0 0.6 collective-permute-start.18
  124.6 9.0 %collective-permute-done.18 = bf16[128,2176]{1,0:T(8,128)(2,1)S(1)} collective-permute-done((bf16[128,2176]{1,0:T(8,128)(2,1)S(1)}, bf16[128,2176]{1,0:T(8,128)(2,1)S(1)}, u32[]{:S(2)}, u32[]{:S(2)}) %collective-permute-start.18) | collective-permute-done | bytes 557088 | tf_op jit(solution)/shard_map/ppermute | solution.py:522
  133.6 0.2 maximum_select_fusion.own_ref
  133.9 1.5 %unpack.1 = bf16[512,512]{1,0:T(8,128)(2,1)} custom-call(s32[1]{0:T(128)} %bitcast.me_ref, s32[1,512]{1,0:T(1,128)S(1)} %copy-done.10, bf16[1024,512]{1,0:T(8,128)(2,1)S(1)} %bitcast.23), custom_call_target="tpu_custom_call" | custom-call | flops 536870912 | bytes 2097152 | tf_op jit(solution)/shard_map/unpack/pallas_call | solution.py:683
  135.5 1.2 collective-permute-done.19.other_ref
  136.7 2.2 %split.1 = (f32[512,1536]{1,0:T(8,128)}, f32[512,512]{1,0:T(8,128)}, f32[1,512]{1,0:T(1,128)}) custom-call(s32[1]{0:T(128)S(6)} %and.16.side_ref, bf16[256,2176]{1,0:T(8,128)(2,1)S(1)} %maximum_select_fusion.own_ref, bf16[256,2176]{1,0:T(8,128)(2,1)S(1)} %collective-permute-done.19.other_ref), custom_call_target="tpu_custom_call" | custom-call | bytes 8388608 | tf_op jit(solution)/shard_map/split/pallas_call | solution.py:695
  (50 shorter events, 0.7 us)
Async XLA Ops:
  0.6 12.8 %copy-start.8 = (bf16[1,512,512]{2,1,0:T(8,128)(2,1)S(1)}, bf16[1,512,512]{2,1,0:T(8,128)(2,1)}, u32[]{:S(2)}) copy-start(bf16[1,512,512]{2,1,0:T(8,128)(2,1)} %param.7) | copy-start | bytes 1572868
  3.7 4.9 %collective-permute-start = (bf16[144,512]{1,0:T(8,128)(2,1)}, bf16[144,512]{1,0:T(8,128)(2,1)S(1)}, u32[]{:S(2)}, u32[]{:S(2)}) collective-permute-start(bf16[144,512]{1,0:T(8,128)(2,1)} %get-tuple-element.51), channel_id=1, source_target_pairs={{0,4},{4,0},{8,12},{12,8},{16,20},{20,16},{24,28},{28,24},{1,5},{5... | collective-permute-start | bytes 442376 | tf_op jit(solution)/shard_map/ppermute | solution.py:407
  4.2 7.5 %collective-permute-start.1 = (bf16[144,512]{1,0:T(8,128)(2,1)}, bf16[144,512]{1,0:T(8,128)(2,1)S(1)}, u32[]{:S(2)}, u32[]{:S(2)}) collective-permute-start(bf16[144,512]{1,0:T(8,128)(2,1)} %get-tuple-element.56), channel_id=1, source_target_pairs={{0,8},{4,12},{8,0},{12,4},{16,24},{20,28},{24,16},{28,20},{1,9},{5... | collective-permute-start | bytes 442376 | tf_op jit(solution)/shard_map/ppermute | solution.py:407
  6.8 9.0 %collective-permute-start.2 = (bf16[144,512]{1,0:T(8,128)(2,1)}, bf16[144,512]{1,0:T(8,128)(2,1)S(1)}, u32[]{:S(2)}, u32[]{:S(2)}) collective-permute-start(bf16[144,512]{1,0:T(8,128)(2,1)} %get-tuple-element.57), channel_id=1, source_target_pairs={{0,12},{4,8},{8,4},{12,0},{16,28},{20,24},{24,20},{28,16},{1,13},{... | collective-permute-start | bytes 442376 | tf_op jit(solution)/shard_map/ppermute | solution.py:407
  6.8 9.0 %collective-permute-start.3 = (bf16[144,512]{1,0:T(8,128)(2,1)}, bf16[144,512]{1,0:T(8,128)(2,1)S(1)}, u32[]{:S(2)}, u32[]{:S(2)}) collective-permute-start(bf16[144,512]{1,0:T(8,128)(2,1)} %get-tuple-element.58), channel_id=1, source_target_pairs={{0,16},{4,20},{8,24},{12,28},{16,0},{20,4},{24,8},{28,12},{1,17},{... | collective-permute-start | bytes 442376 | tf_op jit(solution)/shard_map/ppermute | solution.py:407
  8.6 13.4 %collective-permute-start.4 = (bf16[144,512]{1,0:T(8,128)(2,1)}, bf16[144,512]{1,0:T(8,128)(2,1)S(1)}, u32[]{:S(2)}, u32[]{:S(2)}) collective-permute-start(bf16[144,512]{1,0:T(8,128)(2,1)} %get-tuple-element.59), channel_id=1, source_target_pairs={{0,20},{4,16},{8,28},{12,24},{16,4},{20,0},{24,12},{28,8},{1,21},{... | collective-permute-start | bytes 442376 | tf_op jit(solution)/shard_map/ppermute | solution.py:407
  8.6 13.4 %copy-start.12 = (bf16[144,512]{1,0:T(8,128)(2,1)}, bf16[144,512]{1,0:T(8,128)(2,1)S(1)}, u32[]{:S(2)}) copy-start(bf16[144,512]{1,0:T(8,128)(2,1)S(1)} %collective-permute-done.refs_1_) | copy-start | bytes 442372
  8.6 13.4 %collective-permute-start.5 = (bf16[144,512]{1,0:T(8,128)(2,1)}, bf16[144,512]{1,0:T(8,128)(2,1)S(1)}, u32[]{:S(2)}, u32[]{:S(2)}) collective-permute-start(bf16[144,512]{1,0:T(8,128)(2,1)} %get-tuple-element.60), channel_id=1, source_target_pairs={{0,24},{4,28},{8,16},{12,20},{16,8},{20,12},{24,0},{28,4},{1,25},{... | collective-permute-start | bytes 442376 | tf_op jit(solution)/shard_map/ppermute | solution.py:407
  11.7 10.4 %copy-start.13 = (bf16[144,512]{1,0:T(8,128)(2,1)}, bf16[144,512]{1,0:T(8,128)(2,1)S(1)}, u32[]{:S(2)}) copy-start(bf16[144,512]{1,0:T(8,128)(2,1)S(1)} %collective-permute-done.1.refs_2_) | copy-start | bytes 442372
  11.7 10.3 %collective-permute-start.6 = (bf16[144,512]{1,0:T(8,128)(2,1)}, bf16[144,512]{1,0:T(8,128)(2,1)S(1)}, u32[]{:S(2)}, u32[]{:S(2)}) collective-permute-start(bf16[144,512]{1,0:T(8,128)(2,1)} %get-tuple-element.61), channel_id=1, source_target_pairs={{0,28},{4,24},{8,20},{12,16},{16,12},{20,8},{24,4},{28,0},{1,29},{... | collective-permute-start | bytes 442376 | tf_op jit(solution)/shard_map/ppermute | solution.py:407
  13.4 0.7 copy-start.9
  15.8 10.3 %copy-start.14 = (bf16[144,512]{1,0:T(8,128)(2,1)}, bf16[144,512]{1,0:T(8,128)(2,1)S(1)}, u32[]{:S(2)}) copy-start(bf16[144,512]{1,0:T(8,128)(2,1)S(1)} %collective-permute-done.2.refs_3_) | copy-start | bytes 442372
  15.8 10.3 %copy-start.15 = (bf16[144,512]{1,0:T(8,128)(2,1)}, bf16[144,512]{1,0:T(8,128)(2,1)S(1)}, u32[]{:S(2)}) copy-start(bf16[144,512]{1,0:T(8,128)(2,1)S(1)} %collective-permute-done.3.refs_4_) | copy-start | bytes 442372
  22.0 4.1 %copy-start.16 = (bf16[144,512]{1,0:T(8,128)(2,1)}, bf16[144,512]{1,0:T(8,128)(2,1)S(1)}, u32[]{:S(2)}) copy-start(bf16[144,512]{1,0:T(8,128)(2,1)S(1)} %collective-permute-done.4.refs_5_) | copy-start | bytes 442372
  22.0 4.1 %copy-start.17 = (bf16[144,512]{1,0:T(8,128)(2,1)}, bf16[144,512]{1,0:T(8,128)(2,1)S(1)}, u32[]{:S(2)}) copy-start(bf16[144,512]{1,0:T(8,128)(2,1)S(1)} %collective-permute-done.5.refs_6_) | copy-start | bytes 442372
  22.0 4.1 %copy-start.18 = (bf16[144,512]{1,0:T(8,128)(2,1)}, bf16[144,512]{1,0:T(8,128)(2,1)S(1)}, u32[]{:S(2)}) copy-start(bf16[144,512]{1,0:T(8,128)(2,1)S(1)} %collective-permute-done.6.refs_7_) | copy-start | bytes 442372
  22.1 19.5 %all-to-all-start = ((bf16[8,128,512]{2,1,0:T(8,128)(2,1)}), bf16[8,128,512]{2,1,0:T(8,128)(2,1)S(1)}, u32[]{:S(2)}, u32[]{:S(2)}) async-start(bf16[8,128,512]{2,1,0:T(8,128)(2,1)} %bitcast.5), calls=%async_computation | async-start | bytes 2097152 | tf_op jit(solution)/shard_map/all_to_all | solution.py:579
  41.5 1.0 copy-start.11
  59.9 3.0 %collective-permute-start.8 = (f32[128,2176]{1,0:T(8,128)}, f32[128,2176]{1,0:T(8,128)S(1)}, u32[]{:S(2)}, u32[]{:S(2)}) collective-permute-start(f32[128,2176]{1,0:T(8,128)} %get-tuple-element.81), channel_id=1, source_target_pairs={{0,4},{4,0},{8,12},{12,8},{16,20},{20,16},{24,28},{28,24},{1,5},{5... | collective-permute-start | bytes 3342344 | tf_op jit(solution)/shard_map/ppermute | solution.py:466
  60.0 5.1 %collective-permute-start.7 = (f32[128,2176]{1,0:T(8,128)}, f32[128,2176]{1,0:T(8,128)S(1)}, u32[]{:S(2)}, u32[]{:S(2)}) collective-permute-start(f32[128,2176]{1,0:T(8,128)} %get-tuple-element.79), channel_id=1, source_target_pairs={{0,4},{4,0},{8,12},{12,8},{16,20},{20,16},{24,28},{28,24},{1,5},{5... | collective-permute-start | bytes 3342344 | tf_op jit(solution)/shard_map/ppermute | solution.py:467
  63.0 1.2 copy-start.1
  64.2 9.9 %copy-start = (f32[128,2176]{1,0:T(8,128)S(1)}, f32[128,2176]{1,0:T(8,128)}, u32[]{:S(2)}) copy-start(f32[128,2176]{1,0:T(8,128)} %get-tuple-element.78.refs_0_) | copy-start | bytes 3342340
  64.5 9.6 %collective-permute-start.9 = (s16[128,2176]{1,0:T(8,128)(2,1)S(1)}, s16[128,2176]{1,0:T(8,128)(2,1)S(1)}, u32[]{:S(2)}, u32[]{:S(2)}) collective-permute-start(s16[128,2176]{1,0:T(8,128)(2,1)S(1)} %code_first.1), channel_id=1, source_target_pairs={{0,8},{4,20},{8,0},{12,28},{16,24},{20,4},{24,16},{28,12},{1,9},{5... | collective-permute-start | bytes 1671176 | tf_op jit(solution)/shard_map/ppermute | solution.py:469
  74.1 1.6 %copy-start.4 = (bf16[512,512]{1,0:T(8,128)(2,1)S(1)}, bf16[512,512]{1,0:T(8,128)(2,1)}, u32[]{:S(2)}) copy-start(bf16[512,512]{1,0:T(8,128)(2,1)} %get-tuple-element.83.serial_grad_ref) | copy-start | bytes 1572868
  74.1 1.6 %copy-start.6 = (s32[1,1024]{1,0:T(1,128)S(1)}, s32[1,1024]{1,0:T(1,128)}, u32[]{:S(2)}) copy-start(s32[1,1024]{1,0:T(1,128)} %get-tuple-element.70.pos_ref) | copy-start | bytes 12292
  74.1 1.6 %copy-start.7 = (f32[512]{0:T(512)S(1)}, f32[512]{0:T(512)}, u32[]{:S(2)}) copy-start(f32[512]{0:T(512)} %param.11) | copy-start | bytes 6148
  75.1 6.9 %collective-permute-start.10 = (s16[64,2176]{1,0:T(8,128)(2,1)}, s16[64,2176]{1,0:T(8,128)(2,1)}, u32[]{:S(2)}, u32[]{:S(2)}) collective-permute-start(s16[64,2176]{1,0:T(8,128)(2,1)} %code_second.1), channel_id=1, source_target_pairs={{0,16},{4,12},{8,24},{12,4},{16,0},{20,28},{24,8},{28,20},{1,17},{... | collective-permute-start | bytes 835592 | tf_op jit(solution)/shard_map/ppermute | solution.py:474
  75.7 1.2 copy-start.2
  76.9 1.2 copy-start.3
  78.1 0.9 copy-start.5
  83.4 4.7 %collective-permute-start.11 = (s16[16,2176]{1,0:T(8,128)(2,1)S(1)}, s16[16,2176]{1,0:T(8,128)(2,1)S(1)}, u32[]{:S(2)}, u32[]{:S(2)}) collective-permute-start(s16[16,2176]{1,0:T(8,128)(2,1)S(1)} %get-tuple-element.87), channel_id=1, source_target_pairs={{0,1},{1,0},{2,3},{3,2},{4,5},{5,4},{6,7},{7,6},{8,9},{9,8},{10,11... | collective-permute-start | bytes 208904 | tf_op jit(solution)/shard_map/ppermute | solution.py:407
  85.1 6.7 %collective-permute-start.12 = (s16[16,2176]{1,0:T(8,128)(2,1)S(1)}, s16[16,2176]{1,0:T(8,128)(2,1)S(1)}, u32[]{:S(2)}, u32[]{:S(2)}) collective-permute-start(s16[16,2176]{1,0:T(8,128)(2,1)S(1)} %get-tuple-element.90), channel_id=1, source_target_pairs={{0,2},{1,3},{2,0},{3,1},{4,6},{5,7},{6,4},{7,5},{8,10},{9,11},{10,... | collective-permute-start | bytes 208904 | tf_op jit(solution)/shard_map/ppermute | solution.py:407
  87.7 6.2 %collective-permute-start.13 = (s16[16,2176]{1,0:T(8,128)(2,1)S(1)}, s16[16,2176]{1,0:T(8,128)(2,1)S(1)}, u32[]{:S(2)}, u32[]{:S(2)}) collective-permute-start(s16[16,2176]{1,0:T(8,128)(2,1)S(1)} %get-tuple-element.91), channel_id=1, source_target_pairs={{0,3},{1,2},{2,1},{3,0},{4,7},{5,6},{6,5},{7,4},{8,11},{9,10},{10,... | collective-permute-start | bytes 208904 | tf_op jit(solution)/shard_map/ppermute | solution.py:407
  94.1 8.0 %collective-permute-start.16 = (bf16[16,2176]{1,0:T(8,128)(2,1)S(1)}, bf16[16,2176]{1,0:T(8,128)(2,1)S(1)}, u32[]{:S(2)}, u32[]{:S(2)}) collective-permute-start(bf16[16,2176]{1,0:T(8,128)(2,1)S(1)} %finish.1), channel_id=1, source_target_pairs={{0,3},{1,2},{2,1},{3,0},{4,7},{5,6},{6,5},{7,4},{8,11},{9,10},{10,... | collective-permute-start | bytes 208904 | tf_op jit(solution)/shard_map/ppermute | solution.py:407
  94.9 7.2 %collective-permute-start.14 = (bf16[16,2176]{1,0:T(8,128)(2,1)S(1)}, bf16[16,2176]{1,0:T(8,128)(2,1)S(1)}, u32[]{:S(2)}, u32[]{:S(2)}) collective-permute-start(bf16[16,2176]{1,0:T(8,128)(2,1)S(1)} %finish.1), channel_id=1, source_target_pairs={{0,1},{1,0},{2,3},{3,2},{4,5},{5,4},{6,7},{7,6},{8,9},{9,8},{10,11... | collective-permute-start | bytes 208904 | tf_op jit(solution)/shard_map/ppermute | solution.py:407
  96.0 6.0 %collective-permute-start.15 = (bf16[16,2176]{1,0:T(8,128)(2,1)S(1)}, bf16[16,2176]{1,0:T(8,128)(2,1)S(1)}, u32[]{:S(2)}, u32[]{:S(2)}) collective-permute-start(bf16[16,2176]{1,0:T(8,128)(2,1)S(1)} %finish.1), channel_id=1, source_target_pairs={{0,2},{1,3},{2,0},{3,1},{4,6},{5,7},{6,4},{7,5},{8,10},{9,11},{10,... | collective-permute-start | bytes 208904 | tf_op jit(solution)/shard_map/ppermute | solution.py:407
  98.5 18.9 %all-to-all-start.1 = ((bf16[8,128,512]{2,1,0:T(8,128)(2,1)}), bf16[8,128,512]{2,1,0:T(8,128)(2,1)S(1)}, u32[]{:S(2)}, u32[]{:S(2)}) async-start(bf16[8,128,512]{2,1,0:T(8,128)(2,1)} %bitcast.15), calls=%async_computation.1 | async-start | bytes 2097152 | tf_op jit(solution)/shard_map/all_to_all | solution.py:579
  117.4 6.5 %collective-permute-start.17 = (bf16[64,2176]{1,0:T(8,128)(2,1)S(1)}, bf16[64,2176]{1,0:T(8,128)(2,1)S(1)}, u32[]{:S(2)}, u32[]{:S(2)}) collective-permute-start(bf16[64,2176]{1,0:T(8,128)(2,1)S(1)} %pad_maximum_fusion.1), channel_id=1, source_target_pairs={{0,16},{4,12},{8,24},{12,4},{16,0},{20,28},{24,8},{28,20},{1,17},{... | collective-permute-start | bytes 835592 | tf_op jit(solution)/shard_map/ppermute | solution.py:522
  124.0 9.6 %collective-permute-start.18 = (bf16[128,2176]{1,0:T(8,128)(2,1)S(1)}, bf16[128,2176]{1,0:T(8,128)(2,1)S(1)}, u32[]{:S(2)}, u32[]{:S(2)}) collective-permute-start(bf16[128,2176]{1,0:T(8,128)(2,1)S(1)} %maximum_select_fusion.1), channel_id=1, source_target_pairs={{0,8},{4,20},{8,0},{12,28},{16,24},{20,4},{24,16},{28,12},{1,9},{5... | collective-permute-start | bytes 1671176 | tf_op jit(solution)/shard_map/ppermute | solution.py:522
  124.6 9.3 %copy-start.10 = (s32[1,512]{1,0:T(1,128)S(1)}, s32[1,512]{1,0:T(1,128)}, u32[]{:S(2)}) copy-start(s32[1,512]{1,0:T(1,128)} %get-tuple-element.53.slot_ref) | copy-start | bytes 6148
  133.9 2.8 %collective-permute-start.19 = (bf16[256,2176]{1,0:T(8,128)(2,1)S(1)}, bf16[256,2176]{1,0:T(8,128)(2,1)S(1)}, u32[]{:S(2)}, u32[]{:S(2)}) collective-permute-start(bf16[256,2176]{1,0:T(8,128)(2,1)S(1)} %maximum_select_fusion.own_ref), channel_id=1, source_target_pairs={{0,4},{4,0},{8,12},{12,8},{16,20},{20,16},{24,28},{28,24},{1,5},{5... | collective-permute-start | bytes 3342344 | tf_op jit(solution)/shard_map/ppermute | solution.py:682

commit v10 on v8

--- a/solution.py
+++ b/solution.py
@@ -659,7 +659,6 @@
 
     steps = chip_steps()
     terms = first_step(quarters, steps)
-    d_normed, terms = lax.optimization_barrier((d_normed, terms))
     back = pl.pallas_call(
         functools.partial(residual_kernel, n_seq),
         out_shape=shape_of((slots, width), BF16),
@@ -671,8 +670,9 @@
         ),
         name="residual",
     )(me, pos, gain_row, inv, xhat, serial_grad, d_normed)
+    terms, got = second_step(terms, steps)
+    got, back = lax.optimization_barrier((got, back))
     returned = exchange(back)
-    terms, got = second_step(terms, steps)
     part, returned = lax.optimization_barrier((reduce_over_planes(terms, got, steps), returned))
     own = share_in_plane(share_over_planes(part), steps)
     other = lax.ppermute(own, "seq", core_pairs())

time: 141 us -> 134 us (0.950)
  waiting for transfers between devices: 63.5 us -> 59.6 us
  starting transfers between devices: 32.1 us -> 29.1 us
    ppermute x1, waiting for transfers between devices: 15.1 us -> 3.1 us  [second_step(): return (terms, lax.ppermute(sent, 'seq', steps[1][0]))]
    all_to_all x2, waiting for transfers between devices: 5.8 us -> 9.9 us  [exchange(): got = lax.all_to_all(sent, 'seq', split_axis=0, concat_axis=0, tiled=True)]
    ppermute x2, waiting for transfers between devices: 13.9 us -> 16.6 us  [share_in_plane(): other = lax.ppermute(part, 'seq', pairs)]
    ppermute x2, starting transfers between devices: 2.32 us -> 0.67 us  [share_in_plane(): other = lax.ppermute(part, 'seq', pairs)]
  transfers between devices with their start and end apart: 22 -> 22, of which waited for: 12 -> 13; matrix products, arithmetic and copies ran while one was open for 0% -> 0% of each run, Pallas kernels for 11% -> 13%
where the time goes in v10:
time: 134 us
  waiting for transfers between devices  59.6 us (44%)
  Pallas kernels  40 us (30%)
  starting transfers between devices  29.1 us (22%)
  local copies, waits for them, and re-layouts  3.97 us (3%)
    ppermute x13, waiting for transfers between devices, by_distance(): lax.ppermute(blocks[k], axis, [(i, i ^ k) for i in range(count)])  18.5 us
    ppermute x13, starting transfers between devices, by_distance(): lax.ppermute(blocks[k], axis, [(i, i ^ k) for i in range(count)])  18.1 us
    pallas_call x1, Pallas kernels, per_device(): pl.pallas_call(functools.partial(backward_kernel, n_seq, chip_bits), grid...  17.4 us
    ppermute x2, waiting for transfers between devices, share_in_plane(): other = lax.ppermute(part, 'seq', pairs)  16.6 us
    all_to_all x2, waiting for transfers between devices, exchange(): got = lax.all_to_all(sent, 'seq', split_axis=0, concat_axis=0, tiled=True)  9.9 us
    pallas_call x1, Pallas kernels, per_device(): pl.pallas_call(functools.partial(forward_kernel, n_seq, capacity), grid=(...  9.56 us
    ppermute x1, waiting for transfers between devices, first_step(): return [own_keep, got_keep, lax.ppermute(sent, 'seq', steps[0][0])]  9.03 us
    all_to_all x2, starting transfers between devices, exchange(): got = lax.all_to_all(sent, 'seq', split_axis=0, concat_axis=0, tiled=True)  8.52 us
  transfers between devices with their start and end apart: 22, of which 13 were waited for; matrix products, arithmetic and copies ran while one was open for 0% of the time, Pallas kernels for 13%

profile of v10, /device:TPU:0, one launch (start us, length us, event | category | flops | bytes accessed | tf_op | source)
XLA Modules:
  0.0 133.9 jit_solution(13002157184506958195)
XLA Ops:
  0.6 3.0 %pack.1 = (s32[1,512]{1,0:T(1,128)}, bf16[144,512]{1,0:T(8,128)(2,1)}, bf16[144,512]{1,0:T(8,128)(2,1)}, bf16[144,512]{1,0:T(8,128)(2,1)}, bf16[144,512]{1,0:T(8...) custom-call(s32[1]{0:T(128)} %bitcast.me_ref, ...), custom_call_target="tpu_custom_call" | custom-call | flops 536870912 | bytes 2097152 | tf_op jit(solution)/shard_map/pack/pallas_call | solution.py:544
  3.7 0.5 collective-permute-start
  4.2 2.6 %collective-permute-start.1 = (bf16[144,512]{1,0:T(8,128)(2,1)}, bf16[144,512]{1,0:T(8,128)(2,1)S(1)}, u32[]{:S(2)}, u32[]{:S(2)}) collective-permute-start(bf16[144,512]{1,0:T(8,128)(2,1)} %get-tuple-element.54), channel_id=1, source_target_pairs={{0,8},{4,12},{8,0},{12,4},{16,24},{20,28},{24,16},{28,20},{1,9},{5... | collective-permute-start | bytes 442376 | tf_op jit(solution)/shard_map/ppermute | solution.py:407
  6.8 1.8 %collective-permute-start.3 = (bf16[144,512]{1,0:T(8,128)(2,1)}, bf16[144,512]{1,0:T(8,128)(2,1)S(1)}, u32[]{:S(2)}, u32[]{:S(2)}) collective-permute-start(bf16[144,512]{1,0:T(8,128)(2,1)} %get-tuple-element.56), channel_id=1, source_target_pairs={{0,16},{4,20},{8,24},{12,28},{16,0},{20,4},{24,8},{28,12},{1,17},{... | collective-permute-start | bytes 442376 | tf_op jit(solution)/shard_map/ppermute | solution.py:407
  8.6 2.6 %collective-permute-start.5 = (bf16[144,512]{1,0:T(8,128)(2,1)}, bf16[144,512]{1,0:T(8,128)(2,1)S(1)}, u32[]{:S(2)}, u32[]{:S(2)}) collective-permute-start(bf16[144,512]{1,0:T(8,128)(2,1)} %get-tuple-element.58), channel_id=1, source_target_pairs={{0,24},{4,28},{8,16},{12,20},{16,8},{20,12},{24,0},{28,4},{1,25},{... | collective-permute-start | bytes 442376 | tf_op jit(solution)/shard_map/ppermute | solution.py:407
  11.2 0.5 collective-permute-done.1.refs_2_
  11.7 1.7 %collective-permute-start.6 = (bf16[144,512]{1,0:T(8,128)(2,1)}, bf16[144,512]{1,0:T(8,128)(2,1)S(1)}, u32[]{:S(2)}, u32[]{:S(2)}) collective-permute-start(bf16[144,512]{1,0:T(8,128)(2,1)} %get-tuple-element.59), channel_id=1, source_target_pairs={{0,28},{4,24},{8,20},{12,16},{16,12},{20,8},{24,4},{28,0},{1,29},{... | collective-permute-start | bytes 442376 | tf_op jit(solution)/shard_map/ppermute | solution.py:407
  13.4 0.7 copy-done.9
  14.1 1.7 %pack_grads.1 = bf16[1024,512]{1,0:T(8,128)(2,1)} custom-call(s32[1]{0:T(128)} %bitcast.me_ref, s32[1,512]{1,0:T(1,128)S(1)} %copy-done.9, bf16[512,512]{1,0:T(8,128)(2,1)S(1)} %bitcast.30), custom_call_target="tpu_custom_call" | custom-call | flops 536870912 | bytes 2097152 | tf_op jit(solution)/shard_map/pack_grads/pallas_call | solution.py:562
  15.8 6.2 %collective-permute-done.4.refs_5_ = bf16[144,512]{1,0:T(8,128)(2,1)S(1)} collective-permute-done((bf16[144,512]{1,0:T(8,128)(2,1)}, bf16[144,512]{1,0:T(8,128)(2,1)S(1)}, u32[]{:S(2)}, u32[]{:S(2)}) %collective-permute-start.4) | collective-permute-done | bytes 147488 | tf_op jit(solution)/shard_map/ppermute | solution.py:407
  22.0 4.0 %all-to-all-start = ((bf16[8,128,512]{2,1,0:T(8,128)(2,1)}), bf16[8,128,512]{2,1,0:T(8,128)(2,1)S(1)}, u32[]{:S(2)}, u32[]{:S(2)}) async-start(bf16[8,128,512]{2,1,0:T(8,128)(2,1)} %bitcast.5), calls=%async_computation | async-start | bytes 2097152 | tf_op jit(solution)/shard_map/all_to_all | solution.py:576
  26.1 9.6 %forward.1 = (s32[1,1024]{1,0:T(1,128)}, f32[512,512]{1,0:T(8,128)}, f32[512,128]{1,0:T(8,128)}, bf16[512,512]{1,0:T(8,128)(2,1)}, bf16[512,1536]{1,0:T(8,128)(2...) custom-call(bf16[512,1536]{1,0:T(8,128)(2,1)} %refs_3_.1, f32[1,512]{1,0:T(1,128)} %bitcast.28, ...), custom_call_target="tpu_custom_call" | custom-call | flops 2952790016 | bytes 16777216 | tf_op jit(solution)/shard_map/forward/pallas_call | solution.py:582
  35.7 5.8 %all-to-all-done = bf16[8,128,512]{2,1,0:T(8,128)(2,1)S(1)} async-done(((bf16[8,128,512]{2,1,0:T(8,128)(2,1)}), bf16[8,128,512]{2,1,0:T(8,128)(2,1)S(1)}, u32[]{:S(2)}, u32[]{:S(2)}) %all-to-all-start) | async-done | bytes 1048608 | tf_op jit(solution)/shard_map/all_to_all | solution.py:576
  41.5 1.0 copy-done.11
  42.5 17.4 %backward.1 = (f32[128,2176]{1,0:T(8,128)}, f32[128,2176]{1,0:T(8,128)}, f32[128,2176]{1,0:T(8,128)}, f32[128,2176]{1,0:T(8,128)}, bf16[512,512]{1,0:T(8,128)(2,1)}, /*index=5*/f32[512,512]{1,0:T(8,128)}) custom-call(s32[1]{0:T(128)} %bitcast.me_ref, s32[1,1024]{1,0:T(1,128)} %get-tuple-element.68.pos_ref, bf16[512,512]{1,0:T(8,128)(2,1)} %w_proj_ref.1, ...), custom_call_target="tpu_custom_call" | custom-call | flops 4294967296 | bytes 16777216 | tf_op jit(solution)/shard_map/backward/pallas_call | solution.py:618
  60.0 0.5 collective-permute-start.7
  60.5 2.5 %collective-permute-done.8.refs_1_ = f32[128,2176]{1,0:T(8,128)S(1)} collective-permute-done((f32[128,2176]{1,0:T(8,128)}, f32[128,2176]{1,0:T(8,128)S(1)}, u32[]{:S(2)}, u32[]{:S(2)}) %collective-permute-start.8) | collective-permute-done | bytes 1114144 | tf_op jit(solution)/shard_map/ppermute | solution.py:466
  63.0 1.2 copy-done.1
  64.2 0.3 code_first.1
  64.5 0.6 collective-permute-start.9
  65.1 9.0 %collective-permute-done.9.refs_2_ = s16[128,2176]{1,0:T(8,128)(2,1)S(1)} collective-permute-done((s16[128,2176]{1,0:T(8,128)(2,1)S(1)}, s16[128,2176]{1,0:T(8,128)(2,1)S(1)}, u32[]{:S(2)}, u32[]{:S(2)}) %collective-permute-start.9) | collective-permute-done | bytes 557088 | tf_op jit(solution)/shard_map/ppermute | solution.py:469
  74.2 0.3 code_second.1
  74.4 0.6 collective-permute-start.10
  75.1 0.3 copy-done.2
  75.3 0.3 copy-done.3
  75.7 0.1 copy-done.4
  75.9 2.1 %residual.1 = bf16[1024,512]{1,0:T(8,128)(2,1)} custom-call(s32[1]{0:T(128)} %bitcast.me_ref, s32[1,1024]{1,0:T(1,128)S(1)} %copy-done.6, f32[1,512]{1,0:T(1,128)S(1)} %bitcast.29, f32[512,128]{1,0:T(8,128)S(1)} %copy-done.5, f32[512,512]{1,0:T(8,128)S(1)} %copy-done.2, bf16[512,512]{1,0:T(8,128)(2,1)S(1)} %copy-done.4, f32[512,512]{1,0:T(8,128)S(1)} %copy-done.3), custom_call_target="tpu_custom_call" | custom-call | flops 536870912 | bytes 4194304 | tf_op jit(solution)/shard_map/residual/pallas_call | solution.py:662
  77.9 3.1 %collective-permute-done.10.refs_3_ = s16[64,2176]{1,0:T(8,128)(2,1)S(1)} collective-permute-done((s16[64,2176]{1,0:T(8,128)(2,1)S(1)}, s16[64,2176]{1,0:T(8,128)(2,1)S(1)}, u32[]{:S(2)}, u32[]{:S(2)}) %collective-permute-start.10) | collective-permute-done | bytes 278560 | tf_op jit(solution)/shard_map/ppermute | solution.py:474
  81.0 4.5 %all-to-all-start.1 = ((bf16[8,128,512]{2,1,0:T(8,128)(2,1)}), bf16[8,128,512]{2,1,0:T(8,128)(2,1)}, u32[]{:S(2)}, u32[]{:S(2)}) async-start(bf16[8,128,512]{2,1,0:T(8,128)(2,1)} %bitcast.7), calls=%async_computation.1 | async-start | bytes 2097152 | tf_op jit(solution)/shard_map/all_to_all | solution.py:576
  85.5 0.5 code_planes.1
  86.0 1.6 %collective-permute-start.11 = (s16[16,2176]{1,0:T(8,128)(2,1)S(1)}, s16[16,2176]{1,0:T(8,128)(2,1)S(1)}, u32[]{:S(2)}, u32[]{:S(2)}) collective-permute-start(s16[16,2176]{1,0:T(8,128)(2,1)S(1)} %get-tuple-element.85), channel_id=1, source_target_pairs={{0,1},{1,0},{2,3},{3,2},{4,5},{5,4},{6,7},{7,6},{8,9},{9,8},{10,11... | collective-permute-start | bytes 208904 | tf_op jit(solution)/shard_map/ppermute | solution.py:407
  87.7 2.6 %collective-permute-start.12 = (s16[16,2176]{1,0:T(8,128)(2,1)S(1)}, s16[16,2176]{1,0:T(8,128)(2,1)S(1)}, u32[]{:S(2)}, u32[]{:S(2)}) collective-permute-start(s16[16,2176]{1,0:T(8,128)(2,1)S(1)} %get-tuple-element.86), channel_id=1, source_target_pairs={{0,2},{1,3},{2,0},{3,1},{4,6},{5,7},{6,4},{7,5},{8,10},{9,11},{10,... | collective-permute-start | bytes 208904 | tf_op jit(solution)/shard_map/ppermute | solution.py:407
  90.2 0.2 collective-permute-start.13
  90.5 5.0 %collective-permute-done.12.refs_2_ = s16[16,2176]{1,0:T(8,128)(2,1)S(1)} collective-permute-done((s16[16,2176]{1,0:T(8,128)(2,1)S(1)}, s16[16,2176]{1,0:T(8,128)(2,1)S(1)}, u32[]{:S(2)}, u32[]{:S(2)}) %collective-permute-start.12) | collective-permute-done | bytes 69664 | tf_op jit(solution)/shard_map/ppermute | solution.py:407
  95.5 1.0 collective-permute-done.13.refs_3_
  96.5 0.2 finish.1
  96.6 4.1 %all-to-all-done.1 = bf16[8,128,512]{2,1,0:T(8,128)(2,1)} async-done(((bf16[8,128,512]{2,1,0:T(8,128)(2,1)}), bf16[8,128,512]{2,1,0:T(8,128)(2,1)}, u32[]{:S(2)}, u32[]{:S(2)}) %all-to-all-start.1) | async-done | bytes 1048608 | tf_op jit(solution)/shard_map/all_to_all | solution.py:576
  100.7 1.6 %collective-permute-start.14 = (bf16[16,2176]{1,0:T(8,128)(2,1)S(1)}, bf16[16,2176]{1,0:T(8,128)(2,1)S(1)}, u32[]{:S(2)}, u32[]{:S(2)}) collective-permute-start(bf16[16,2176]{1,0:T(8,128)(2,1)S(1)} %finish.1), channel_id=1, source_target_pairs={{0,1},{1,0},{2,3},{3,2},{4,5},{5,4},{6,7},{7,6},{8,9},{9,8},{10,11... | collective-permute-start | bytes 208904 | tf_op jit(solution)/shard_map/ppermute | solution.py:407
  102.3 2.6 %collective-permute-start.15 = (bf16[16,2176]{1,0:T(8,128)(2,1)S(1)}, bf16[16,2176]{1,0:T(8,128)(2,1)S(1)}, u32[]{:S(2)}, u32[]{:S(2)}) collective-permute-start(bf16[16,2176]{1,0:T(8,128)(2,1)S(1)} %finish.1), channel_id=1, source_target_pairs={{0,2},{1,3},{2,0},{3,1},{4,6},{5,7},{6,4},{7,5},{8,10},{9,11},{10,... | collective-permute-start | bytes 208904 | tf_op jit(solution)/shard_map/ppermute | solution.py:407
  104.9 0.2 collective-permute-start.16
  105.1 3.1 %collective-permute-done.15 = bf16[16,2176]{1,0:T(8,128)(2,1)S(1)} collective-permute-done((bf16[16,2176]{1,0:T(8,128)(2,1)S(1)}, bf16[16,2176]{1,0:T(8,128)(2,1)S(1)}, u32[]{:S(2)}, u32[]{:S(2)}) %collective-permute-start.15) | collective-permute-done | bytes 69664 | tf_op jit(solution)/shard_map/ppermute | solution.py:407
  108.3 2.7 %collective-permute-done.16 = bf16[16,2176]{1,0:T(8,128)(2,1)S(1)} collective-permute-done((bf16[16,2176]{1,0:T(8,128)(2,1)S(1)}, bf16[16,2176]{1,0:T(8,128)(2,1)S(1)}, u32[]{:S(2)}, u32[]{:S(2)}) %collective-permute-start.16) | collective-permute-done | bytes 69664 | tf_op jit(solution)/shard_map/ppermute | solution.py:407
  111.2 0.6 collective-permute-start.17
  111.8 7.1 %collective-permute-done.17 = bf16[64,2176]{1,0:T(8,128)(2,1)S(1)} collective-permute-done((bf16[64,2176]{1,0:T(8,128)(2,1)S(1)}, bf16[64,2176]{1,0:T(8,128)(2,1)S(1)}, u32[]{:S(2)}, u32[]{:S(2)}) %collective-permute-start.17) | collective-permute-done | bytes 278560 | tf_op jit(solution)/shard_map/ppermute | solution.py:519
  119.2 9.5 %collective-permute-done.18 = bf16[128,2176]{1,0:T(8,128)(2,1)S(1)} collective-permute-done((bf16[128,2176]{1,0:T(8,128)(2,1)S(1)}, bf16[128,2176]{1,0:T(8,128)(2,1)S(1)}, u32[]{:S(2)}, u32[]{:S(2)}) %collective-permute-start.18) | collective-permute-done | bytes 557088 | tf_op jit(solution)/shard_map/ppermute | solution.py:519
  128.7 0.2 maximum_select_fusion.own_ref
  129.0 2.8 %unpack.1 = bf16[512,512]{1,0:T(8,128)(2,1)} custom-call(s32[1]{0:T(128)} %bitcast.me_ref, s32[1,512]{1,0:T(1,128)S(1)} %copy-done.10, bf16[1024,512]{1,0:T(8,128)(2,1)} %bitcast.8.recv_ref), custom_call_target="tpu_custom_call" | custom-call | flops 536870912 | bytes 2097152 | tf_op jit(solution)/shard_map/unpack/pallas_call | solution.py:679
  131.8 2.2 %split.1 = (f32[512,1536]{1,0:T(8,128)}, f32[512,512]{1,0:T(8,128)}, f32[1,512]{1,0:T(1,128)}) custom-call(s32[1]{0:T(128)S(6)} %and.16.side_ref, bf16[256,2176]{1,0:T(8,128)(2,1)S(1)} %maximum_select_fusion.own_ref, bf16[256,2176]{1,0:T(8,128)(2,1)S(1)} %collective-permute-done.19.other_ref), custom_call_target="tpu_custom_call" | custom-call | bytes 8388608 | tf_op jit(solution)/shard_map/split/pallas_call | solution.py:691
  (58 shorter events, 0.8 us)
Async XLA Ops:
  0.6 12.8 %copy-start.8 = (bf16[1,512,512]{2,1,0:T(8,128)(2,1)S(1)}, bf16[1,512,512]{2,1,0:T(8,128)(2,1)}, u32[]{:S(2)}) copy-start(bf16[1,512,512]{2,1,0:T(8,128)(2,1)} %param.7) | copy-start | bytes 1572868
  3.7 4.9 %collective-permute-start = (bf16[144,512]{1,0:T(8,128)(2,1)}, bf16[144,512]{1,0:T(8,128)(2,1)S(1)}, u32[]{:S(2)}, u32[]{:S(2)}) collective-permute-start(bf16[144,512]{1,0:T(8,128)(2,1)} %get-tuple-element.49), channel_id=1, source_target_pairs={{0,4},{4,0},{8,12},{12,8},{16,20},{20,16},{24,28},{28,24},{1,5},{5... | collective-permute-start | bytes 442376 | tf_op jit(solution)/shard_map/ppermute | solution.py:407
  4.2 7.5 %collective-permute-start.1 = (bf16[144,512]{1,0:T(8,128)(2,1)}, bf16[144,512]{1,0:T(8,128)(2,1)S(1)}, u32[]{:S(2)}, u32[]{:S(2)}) collective-permute-start(bf16[144,512]{1,0:T(8,128)(2,1)} %get-tuple-element.54), channel_id=1, source_target_pairs={{0,8},{4,12},{8,0},{12,4},{16,24},{20,28},{24,16},{28,20},{1,9},{5... | collective-permute-start | bytes 442376 | tf_op jit(solution)/shard_map/ppermute | solution.py:407
  6.8 9.0 %collective-permute-start.2 = (bf16[144,512]{1,0:T(8,128)(2,1)}, bf16[144,512]{1,0:T(8,128)(2,1)S(1)}, u32[]{:S(2)}, u32[]{:S(2)}) collective-permute-start(bf16[144,512]{1,0:T(8,128)(2,1)} %get-tuple-element.55), channel_id=1, source_target_pairs={{0,12},{4,8},{8,4},{12,0},{16,28},{20,24},{24,20},{28,16},{1,13},{... | collective-permute-start | bytes 442376 | tf_op jit(solution)/shard_map/ppermute | solution.py:407
  6.8 9.0 %collective-permute-start.3 = (bf16[144,512]{1,0:T(8,128)(2,1)}, bf16[144,512]{1,0:T(8,128)(2,1)S(1)}, u32[]{:S(2)}, u32[]{:S(2)}) collective-permute-start(bf16[144,512]{1,0:T(8,128)(2,1)} %get-tuple-element.56), channel_id=1, source_target_pairs={{0,16},{4,20},{8,24},{12,28},{16,0},{20,4},{24,8},{28,12},{1,17},{... | collective-permute-start | bytes 442376 | tf_op jit(solution)/shard_map/ppermute | solution.py:407
  8.6 13.4 %collective-permute-start.4 = (bf16[144,512]{1,0:T(8,128)(2,1)}, bf16[144,512]{1,0:T(8,128)(2,1)S(1)}, u32[]{:S(2)}, u32[]{:S(2)}) collective-permute-start(bf16[144,512]{1,0:T(8,128)(2,1)} %get-tuple-element.57), channel_id=1, source_target_pairs={{0,20},{4,16},{8,28},{12,24},{16,4},{20,0},{24,12},{28,8},{1,21},{... | collective-permute-start | bytes 442376 | tf_op jit(solution)/shard_map/ppermute | solution.py:407
  8.6 13.4 %copy-start.12 = (bf16[144,512]{1,0:T(8,128)(2,1)}, bf16[144,512]{1,0:T(8,128)(2,1)S(1)}, u32[]{:S(2)}) copy-start(bf16[144,512]{1,0:T(8,128)(2,1)S(1)} %collective-permute-done.refs_1_) | copy-start | bytes 442372
  8.6 13.4 %collective-permute-start.5 = (bf16[144,512]{1,0:T(8,128)(2,1)}, bf16[144,512]{1,0:T(8,128)(2,1)S(1)}, u32[]{:S(2)}, u32[]{:S(2)}) collective-permute-start(bf16[144,512]{1,0:T(8,128)(2,1)} %get-tuple-element.58), channel_id=1, source_target_pairs={{0,24},{4,28},{8,16},{12,20},{16,8},{20,12},{24,0},{28,4},{1,25},{... | collective-permute-start | bytes 442376 | tf_op jit(solution)/shard_map/ppermute | solution.py:407
  11.7 10.4 %copy-start.13 = (bf16[144,512]{1,0:T(8,128)(2,1)}, bf16[144,512]{1,0:T(8,128)(2,1)S(1)}, u32[]{:S(2)}) copy-start(bf16[144,512]{1,0:T(8,128)(2,1)S(1)} %collective-permute-done.1.refs_2_) | copy-start | bytes 442372
  11.7 10.3 %collective-permute-start.6 = (bf16[144,512]{1,0:T(8,128)(2,1)}, bf16[144,512]{1,0:T(8,128)(2,1)S(1)}, u32[]{:S(2)}, u32[]{:S(2)}) collective-permute-start(bf16[144,512]{1,0:T(8,128)(2,1)} %get-tuple-element.59), channel_id=1, source_target_pairs={{0,28},{4,24},{8,20},{12,16},{16,12},{20,8},{24,4},{28,0},{1,29},{... | collective-permute-start | bytes 442376 | tf_op jit(solution)/shard_map/ppermute | solution.py:407
  13.4 0.7 copy-start.9
  15.8 10.3 %copy-start.14 = (bf16[144,512]{1,0:T(8,128)(2,1)}, bf16[144,512]{1,0:T(8,128)(2,1)S(1)}, u32[]{:S(2)}) copy-start(bf16[144,512]{1,0:T(8,128)(2,1)S(1)} %collective-permute-done.2.refs_3_) | copy-start | bytes 442372
  15.8 10.3 %copy-start.15 = (bf16[144,512]{1,0:T(8,128)(2,1)}, bf16[144,512]{1,0:T(8,128)(2,1)S(1)}, u32[]{:S(2)}) copy-start(bf16[144,512]{1,0:T(8,128)(2,1)S(1)} %collective-permute-done.3.refs_4_) | copy-start | bytes 442372
  22.0 4.1 %copy-start.16 = (bf16[144,512]{1,0:T(8,128)(2,1)}, bf16[144,512]{1,0:T(8,128)(2,1)S(1)}, u32[]{:S(2)}) copy-start(bf16[144,512]{1,0:T(8,128)(2,1)S(1)} %collective-permute-done.4.refs_5_) | copy-start | bytes 442372
  22.0 4.1 %copy-start.17 = (bf16[144,512]{1,0:T(8,128)(2,1)}, bf16[144,512]{1,0:T(8,128)(2,1)S(1)}, u32[]{:S(2)}) copy-start(bf16[144,512]{1,0:T(8,128)(2,1)S(1)} %collective-permute-done.5.refs_6_) | copy-start | bytes 442372
  22.0 4.1 %copy-start.18 = (bf16[144,512]{1,0:T(8,128)(2,1)}, bf16[144,512]{1,0:T(8,128)(2,1)S(1)}, u32[]{:S(2)}) copy-start(bf16[144,512]{1,0:T(8,128)(2,1)S(1)} %collective-permute-done.6.refs_7_) | copy-start | bytes 442372
  22.0 19.5 %all-to-all-start = ((bf16[8,128,512]{2,1,0:T(8,128)(2,1)}), bf16[8,128,512]{2,1,0:T(8,128)(2,1)S(1)}, u32[]{:S(2)}, u32[]{:S(2)}) async-start(bf16[8,128,512]{2,1,0:T(8,128)(2,1)} %bitcast.5), calls=%async_computation | async-start | bytes 2097152 | tf_op jit(solution)/shard_map/all_to_all | solution.py:576
  41.5 1.0 copy-start.11
  59.9 3.0 %collective-permute-start.8 = (f32[128,2176]{1,0:T(8,128)}, f32[128,2176]{1,0:T(8,128)S(1)}, u32[]{:S(2)}, u32[]{:S(2)}) collective-permute-start(f32[128,2176]{1,0:T(8,128)} %get-tuple-element.79), channel_id=1, source_target_pairs={{0,4},{4,0},{8,12},{12,8},{16,20},{20,16},{24,28},{28,24},{1,5},{5... | collective-permute-start | bytes 3342344 | tf_op jit(solution)/shard_map/ppermute | solution.py:466
  60.0 5.1 %collective-permute-start.7 = (f32[128,2176]{1,0:T(8,128)}, f32[128,2176]{1,0:T(8,128)S(1)}, u32[]{:S(2)}, u32[]{:S(2)}) collective-permute-start(f32[128,2176]{1,0:T(8,128)} %get-tuple-element.77), channel_id=1, source_target_pairs={{0,4},{4,0},{8,12},{12,8},{16,20},{20,16},{24,28},{28,24},{1,5},{5... | collective-permute-start | bytes 3342344 | tf_op jit(solution)/shard_map/ppermute | solution.py:467
  63.0 1.2 copy-start.1
  64.2 9.9 %copy-start = (f32[128,2176]{1,0:T(8,128)S(1)}, f32[128,2176]{1,0:T(8,128)}, u32[]{:S(2)}) copy-start(f32[128,2176]{1,0:T(8,128)} %get-tuple-element.76.refs_0_) | copy-start | bytes 3342340
  64.5 9.6 %collective-permute-start.9 = (s16[128,2176]{1,0:T(8,128)(2,1)S(1)}, s16[128,2176]{1,0:T(8,128)(2,1)S(1)}, u32[]{:S(2)}, u32[]{:S(2)}) collective-permute-start(s16[128,2176]{1,0:T(8,128)(2,1)S(1)} %code_first.1), channel_id=1, source_target_pairs={{0,8},{4,20},{8,0},{12,28},{16,24},{20,4},{24,16},{28,12},{1,9},{5... | collective-permute-start | bytes 1671176 | tf_op jit(solution)/shard_map/ppermute | solution.py:469
  74.1 1.2 copy-start.2
  74.1 1.5 %copy-start.3 = (f32[512,512]{1,0:T(8,128)S(1)}, f32[512,512]{1,0:T(8,128)}, u32[]{:S(2)}) copy-start(f32[512,512]{1,0:T(8,128)} %get-tuple-element.82.d_normed_ref) | copy-start | bytes 3145732
  74.1 1.7 %copy-start.4 = (bf16[512,512]{1,0:T(8,128)(2,1)S(1)}, bf16[512,512]{1,0:T(8,128)(2,1)}, u32[]{:S(2)}) copy-start(bf16[512,512]{1,0:T(8,128)(2,1)} %get-tuple-element.81.serial_grad_ref) | copy-start | bytes 1572868
  74.1 1.7 %copy-start.5 = (f32[512,128]{1,0:T(8,128)S(1)}, f32[512,128]{1,0:T(8,128)}, u32[]{:S(2)}) copy-start(f32[512,128]{1,0:T(8,128)} %get-tuple-element.80.inv_ref) | copy-start | bytes 786436
  74.1 1.7 %copy-start.6 = (s32[1,1024]{1,0:T(1,128)S(1)}, s32[1,1024]{1,0:T(1,128)}, u32[]{:S(2)}) copy-start(s32[1,1024]{1,0:T(1,128)} %get-tuple-element.68.pos_ref) | copy-start | bytes 12292
  74.1 1.7 %copy-start.7 = (f32[512]{0:T(512)S(1)}, f32[512]{0:T(512)}, u32[]{:S(2)}) copy-start(f32[512]{0:T(512)} %param.11) | copy-start | bytes 6148
  74.4 6.6 %collective-permute-start.10 = (s16[64,2176]{1,0:T(8,128)(2,1)S(1)}, s16[64,2176]{1,0:T(8,128)(2,1)S(1)}, u32[]{:S(2)}, u32[]{:S(2)}) collective-permute-start(s16[64,2176]{1,0:T(8,128)(2,1)S(1)} %code_second.1), channel_id=1, source_target_pairs={{0,16},{4,12},{8,24},{12,4},{16,0},{20,28},{24,8},{28,20},{1,17},{... | collective-permute-start | bytes 835592 | tf_op jit(solution)/shard_map/ppermute | solution.py:474
  81.0 19.7 %all-to-all-start.1 = ((bf16[8,128,512]{2,1,0:T(8,128)(2,1)}), bf16[8,128,512]{2,1,0:T(8,128)(2,1)}, u32[]{:S(2)}, u32[]{:S(2)}) async-start(bf16[8,128,512]{2,1,0:T(8,128)(2,1)} %bitcast.7), calls=%async_computation.1 | async-start | bytes 2097152 | tf_op jit(solution)/shard_map/all_to_all | solution.py:576
  86.0 4.5 %collective-permute-start.11 = (s16[16,2176]{1,0:T(8,128)(2,1)S(1)}, s16[16,2176]{1,0:T(8,128)(2,1)S(1)}, u32[]{:S(2)}, u32[]{:S(2)}) collective-permute-start(s16[16,2176]{1,0:T(8,128)(2,1)S(1)} %get-tuple-element.85), channel_id=1, source_target_pairs={{0,1},{1,0},{2,3},{3,2},{4,5},{5,4},{6,7},{7,6},{8,9},{9,8},{10,11... | collective-permute-start | bytes 208904 | tf_op jit(solution)/shard_map/ppermute | solution.py:407
  87.7 7.8 %collective-permute-start.12 = (s16[16,2176]{1,0:T(8,128)(2,1)S(1)}, s16[16,2176]{1,0:T(8,128)(2,1)S(1)}, u32[]{:S(2)}, u32[]{:S(2)}) collective-permute-start(s16[16,2176]{1,0:T(8,128)(2,1)S(1)} %get-tuple-element.86), channel_id=1, source_target_pairs={{0,2},{1,3},{2,0},{3,1},{4,6},{5,7},{6,4},{7,5},{8,10},{9,11},{10,... | collective-permute-start | bytes 208904 | tf_op jit(solution)/shard_map/ppermute | solution.py:407
  90.2 6.2 %collective-permute-start.13 = (s16[16,2176]{1,0:T(8,128)(2,1)S(1)}, s16[16,2176]{1,0:T(8,128)(2,1)S(1)}, u32[]{:S(2)}, u32[]{:S(2)}) collective-permute-start(s16[16,2176]{1,0:T(8,128)(2,1)S(1)} %get-tuple-element.87), channel_id=1, source_target_pairs={{0,3},{1,2},{2,1},{3,0},{4,7},{5,6},{6,5},{7,4},{8,11},{9,10},{10,... | collective-permute-start | bytes 208904 | tf_op jit(solution)/shard_map/ppermute | solution.py:407
  100.7 4.4 %collective-permute-start.14 = (bf16[16,2176]{1,0:T(8,128)(2,1)S(1)}, bf16[16,2176]{1,0:T(8,128)(2,1)S(1)}, u32[]{:S(2)}, u32[]{:S(2)}) collective-permute-start(bf16[16,2176]{1,0:T(8,128)(2,1)S(1)} %finish.1), channel_id=1, source_target_pairs={{0,1},{1,0},{2,3},{3,2},{4,5},{5,4},{6,7},{7,6},{8,9},{9,8},{10,11... | collective-permute-start | bytes 208904 | tf_op jit(solution)/shard_map/ppermute | solution.py:407
  102.3 6.0 %collective-permute-start.15 = (bf16[16,2176]{1,0:T(8,128)(2,1)S(1)}, bf16[16,2176]{1,0:T(8,128)(2,1)S(1)}, u32[]{:S(2)}, u32[]{:S(2)}) collective-permute-start(bf16[16,2176]{1,0:T(8,128)(2,1)S(1)} %finish.1), channel_id=1, source_target_pairs={{0,2},{1,3},{2,0},{3,1},{4,6},{5,7},{6,4},{7,5},{8,10},{9,11},{10,... | collective-permute-start | bytes 208904 | tf_op jit(solution)/shard_map/ppermute | solution.py:407
  104.9 6.1 %collective-permute-start.16 = (bf16[16,2176]{1,0:T(8,128)(2,1)S(1)}, bf16[16,2176]{1,0:T(8,128)(2,1)S(1)}, u32[]{:S(2)}, u32[]{:S(2)}) collective-permute-start(bf16[16,2176]{1,0:T(8,128)(2,1)S(1)} %finish.1), channel_id=1, source_target_pairs={{0,3},{1,2},{2,1},{3,0},{4,7},{5,6},{6,5},{7,4},{8,11},{9,10},{10,... | collective-permute-start | bytes 208904 | tf_op jit(solution)/shard_map/ppermute | solution.py:407
  111.2 7.7 %collective-permute-start.17 = (bf16[64,2176]{1,0:T(8,128)(2,1)S(1)}, bf16[64,2176]{1,0:T(8,128)(2,1)S(1)}, u32[]{:S(2)}, u32[]{:S(2)}) collective-permute-start(bf16[64,2176]{1,0:T(8,128)(2,1)S(1)} %pad_maximum_fusion.1), channel_id=1, source_target_pairs={{0,16},{4,12},{8,24},{12,4},{16,0},{20,28},{24,8},{28,20},{1,17},{... | collective-permute-start | bytes 835592 | tf_op jit(solution)/shard_map/ppermute | solution.py:519
  119.1 9.6 %collective-permute-start.18 = (bf16[128,2176]{1,0:T(8,128)(2,1)S(1)}, bf16[128,2176]{1,0:T(8,128)(2,1)S(1)}, u32[]{:S(2)}, u32[]{:S(2)}) collective-permute-start(bf16[128,2176]{1,0:T(8,128)(2,1)S(1)} %broadcast_select_fusion), channel_id=1, source_target_pairs={{0,8},{4,20},{8,0},{12,28},{16,24},{20,4},{24,16},{28,12},{1,9},{5... | collective-permute-start | bytes 1671176 | tf_op jit(solution)/shard_map/ppermute | solution.py:519
  119.2 9.8 %copy-start.10 = (s32[1,512]{1,0:T(1,128)S(1)}, s32[1,512]{1,0:T(1,128)}, u32[]{:S(2)}) copy-start(s32[1,512]{1,0:T(1,128)} %get-tuple-element.51.slot_ref) | copy-start | bytes 6148
  128.9 2.9 %collective-permute-start.19 = (bf16[256,2176]{1,0:T(8,128)(2,1)S(1)}, bf16[256,2176]{1,0:T(8,128)(2,1)S(1)}, u32[]{:S(2)}, u32[]{:S(2)}) collective-permute-start(bf16[256,2176]{1,0:T(8,128)(2,1)S(1)} %maximum_select_fusion.own_ref), channel_id=1, source_target_pairs={{0,4},{4,0},{8,12},{12,8},{16,20},{20,16},{24,28},{28,24},{1,5},{5... | collective-permute-start | bytes 3342344 | tf_op jit(solution)/shard_map/ppermute | solution.py:678

commit v11 on v10

--- a/solution.py
+++ b/solution.py
@@ -101,7 +101,6 @@
     rows = xhat_ref.shape[0]
     head = width // HEADS
     pair = 2 * head
-    step = pl.program_id(0)
     w_copy = pltpu.make_async_copy(w_hbm, w_ref, sems.at[0])
     saves = [
         pltpu.make_async_copy(source, target, sems.at[1 + i])
@@ -116,54 +115,51 @@
         )
     ]
 
-    @pl.when(step == 0)
-    def _():
-        w_copy.start()
-        tile = recv[0][capacity:, :].astype(F32)
-        for s in range(1, n_seq):
-            tile = tile + recv[s][capacity:, :].astype(F32)
-        high = jnp.concatenate([tile[0:1], tile[1:2]], axis=1)
-        low = jnp.concatenate([tile[2:3], tile[3:4]], axis=1)
-        pos = (high * 256.0 + low).astype(jnp.int32) - 1
-        pos_out[...] = pos
-        place = hot(iota((rows, n_seq * capacity), 0) == pos)
-        values = jnp.concatenate([recv[s][:capacity, :] for s in range(n_seq)], axis=0)
-        feats = mm(place, values)
-        centered = feats - jnp.mean(feats, axis=1, keepdims=True)
-        inv = lax.rsqrt(jnp.mean(centered * centered, axis=1, keepdims=True) + 1e-05)
-        xhat = centered * inv
-        xhat_ref[...] = xhat
-        inv_ref[...] = jnp.broadcast_to(inv, inv_ref.shape)
-        normed = (xhat * gain_ref[...]).astype(BF16)
-        normed_ref[...] = normed
-        w_copy.wait()
-        qkv = mm(normed, w_ref[...])
-        qkv_ref[...] = qkv.astype(BF16)
-        trans[...] = jnp.transpose(qkv).astype(BF16)
-        for save in saves:
-            save.start()
-
-    lo = pl.multiple_of(step * pair, pair)
-    keys = qkv_ref[:, pl.ds(pl.multiple_of(width + step * pair, pair), pair)]
-    query_t = trans[pl.ds(lo, pair), :] * BF16(0.125)
-    zero = jnp.zeros((head, rows), BF16)
-    for j in range(2):
-        part = query_t[j * head : (j + 1) * head]
-        part = jnp.concatenate([part, zero] if j == 0 else [zero, part], axis=0)
-        scores = mm(keys, part)
-        top = jnp.max(scores, axis=0, keepdims=True)
-        expo = jnp.exp(scores - top)
-        share = 1.0 / jnp.sum(expo, axis=0, keepdims=True)
-        probs = expo * share
-        stats_out[pl.ds(2 * step + j, 1), :] = top
-        stats_out[pl.ds(HEADS + 2 * step + j, 1), :] = share
-        values_t = trans[pl.ds(pl.multiple_of(2 * width + step * pair + j * head, head), head), :]
-        attn_out[j * head : (j + 1) * head, :] = mm(values_t, probs.astype(BF16)).astype(BF16)
-
-    @pl.when(step == pl.num_programs(0) - 1)
-    def _():
-        for save in saves:
-            save.wait()
+    w_copy.start()
+    tile = recv[0][capacity:, :].astype(F32)
+    for s in range(1, n_seq):
+        tile = tile + recv[s][capacity:, :].astype(F32)
+    high = jnp.concatenate([tile[0:1], tile[1:2]], axis=1)
+    low = jnp.concatenate([tile[2:3], tile[3:4]], axis=1)
+    pos = (high * 256.0 + low).astype(jnp.int32) - 1
+    pos_out[...] = pos
+    place = hot(iota((rows, n_seq * capacity), 0) == pos)
+    values = jnp.concatenate([recv[s][:capacity, :] for s in range(n_seq)], axis=0)
+    feats = mm(place, values)
+    centered = feats - jnp.mean(feats, axis=1, keepdims=True)
+    inv = lax.rsqrt(jnp.mean(centered * centered, axis=1, keepdims=True) + 1e-05)
+    xhat = centered * inv
+    xhat_ref[...] = xhat
+    inv_ref[...] = jnp.broadcast_to(inv, inv_ref.shape)
+    normed = (xhat * gain_ref[...]).astype(BF16)
+    normed_ref[...] = normed
+    w_copy.wait()
+    qkv = mm(normed, w_ref[...])
+    qkv_ref[...] = qkv.astype(BF16)
+    trans[...] = jnp.transpose(qkv).astype(BF16)
+    for save in saves:
+        save.start()
+
+    for step in range(HEADS // 2):
+        lo = step * pair
+        keys = qkv_ref[:, pl.ds(width + lo, pair)]
+        query_t = trans[pl.ds(lo, pair), :] * BF16(0.125)
+        zero = jnp.zeros((head, rows), BF16)
+        for j in range(2):
+            part = query_t[j * head : (j + 1) * head]
+            part = jnp.concatenate([part, zero] if j == 0 else [zero, part], axis=0)
+            scores = mm(keys, part)
+            top = jnp.max(scores, axis=0, keepdims=True)
+            expo = jnp.exp(scores - top)
+            share = 1.0 / jnp.sum(expo, axis=0, keepdims=True)
+            probs = expo * share
+            stats_out[pl.ds(2 * step + j, 1), :] = top
+            stats_out[pl.ds(HEADS + 2 * step + j, 1), :] = share
+            values_t = trans[pl.ds(2 * width + lo + j * head, head), :]
+            attn_out[pl.ds(lo + j * head, head), :] = mm(values_t, probs.astype(BF16)).astype(BF16)
+
+    for save in saves:
+        save.wait()
 
 
 def backward_kernel(n_seq, chip_bits, me_ref, pos_ref, w_proj_ref, stats_ref, *refs):
@@ -177,7 +173,6 @@
     capacity = recv_ref.shape[0] // n_seq
     head = width // HEADS
     pair = 2 * head
-    step = pl.program_id(0)
     me = me_ref[0]
     loads = [
         pltpu.make_async_copy(source, target, sems.at[i])
@@ -200,93 +195,91 @@
         )
     ]
 
-    @pl.when(step == 0)
-    def _():
-        for load in loads:
-            load.start()
-        place = hot(iota((rows, n_seq * capacity), 0) == pos_ref[...])
-        loads[0].wait()
-        values = jnp.concatenate(
-            [recv_ref[by_receiver(me, d, capacity), :] for d in range(n_seq)], axis=0
-        )
-        grads = mm(place, values).astype(BF16)
-        serial_grad[...] = grads
-        saves[4].start()
-        d_att = mm(grads, w_proj_ref[...], NT).astype(BF16)
-        d_attn[...] = d_att
-        d_attn_t[...] = jnp.transpose(d_att.astype(F32)).astype(BF16)
-        loads[1].wait()
-        loads[2].wait()
-
-    lo = pl.multiple_of(step * pair, pair)
-    queries = qkv_ref[:, pl.ds(lo, pair)]
-    values = qkv_ref[:, pl.ds(pl.multiple_of(2 * width + step * pair, pair), pair)]
-    d_att_t = d_attn_t[pl.ds(lo, pair), :] * BF16(0.125)
-    d_att = d_attn[:, pl.ds(lo, pair)]
-    keys = qkv_ref[:, pl.ds(pl.multiple_of(width + step * pair, pair), pair)]
-    query_t = trans_ref[pl.ds(lo, pair), :] * BF16(0.125)
+    for load in loads:
+        load.start()
+    place = hot(iota((rows, n_seq * capacity), 0) == pos_ref[...])
+    loads[0].wait()
+    values = jnp.concatenate(
+        [recv_ref[by_receiver(me, d, capacity), :] for d in range(n_seq)], axis=0
+    )
+    grads = mm(place, values).astype(BF16)
+    serial_grad[...] = grads
+    saves[4].start()
+    d_att = mm(grads, w_proj_ref[...], NT).astype(BF16)
+    d_attn[...] = d_att
+    d_attn_t[...] = jnp.transpose(d_att.astype(F32)).astype(BF16)
+    loads[1].wait()
+    loads[2].wait()
+
     zero = jnp.zeros((head, rows), BF16)
-    d_q, d_k, d_v = [], [], []
-    for j in range(2):
-        def alone(both):
-            part = both[j * head : (j + 1) * head]
-            return jnp.concatenate([part, zero] if j == 0 else [zero, part], axis=0)
-
-        top = stats_ref[pl.ds(2 * step + j, 1), :]
-        share = stats_ref[pl.ds(HEADS + 2 * step + j, 1), :]
-        probs = jnp.exp(mm(keys, alone(query_t)) - top) * share
-        d_probs = mm(values, alone(d_att_t))
-        total = jnp.sum(d_probs * probs, axis=0, keepdims=True)
-        d_scores = (probs * (d_probs - total)).astype(BF16)
-        k_t = trans_ref[pl.ds(pl.multiple_of(width + step * pair + j * head, head), head), :]
-        d_q.append(mm(k_t, d_scores))
-        d_k.append(mm(d_scores, queries))
-        d_v.append(mm(probs.astype(BF16), d_att))
     first = iota((rows, pair), 1) < head
-    d_qkv[:, pl.ds(lo, pair)] = jnp.transpose(jnp.concatenate(d_q, axis=0)).astype(BF16)
-    d_qkv[:, pl.ds(pl.multiple_of(width + step * pair, pair), pair)] = jnp.where(
-        first, d_k[0], d_k[1]
-    ).astype(BF16)
-    d_qkv[:, pl.ds(pl.multiple_of(2 * width + step * pair, pair), pair)] = jnp.where(
-        first, d_v[0], d_v[1]
-    ).astype(BF16)
-
-    @pl.when(step == pl.num_programs(0) - 1)
-    def _():
-        for load in loads[3:]:
-            load.wait()
-        normed_t[...] = jnp.transpose(normed_ref[...].astype(F32)).astype(BF16)
-        d_normed = mm(d_qkv[...], w_ref[...], NT)
-        d_normed_ref[...] = d_normed
-        saves[5].start()
-        gain_row = jnp.sum(d_normed * xhat_ref[...], axis=0, keepdims=True)
-        gain_column[...] = jnp.transpose(jnp.broadcast_to(gain_row, (LANES, width)))
-        eighth = width // 8
-        odd = lax.bitwise_and(me, 1)
-
-        def sides(even_bit, odd_bit):
-            even_side = lax.bitwise_and(lax.shift_right_logical(me, even_bit), 1)
-            odd_side = lax.bitwise_and(lax.shift_right_logical(me, odd_bit), 1)
-            mine = jnp.where(odd == 1, odd_side, even_side)
-            return mine, even_side + odd_side - mine
-
-        (mine, other), (mine_next, other_next) = (sides(*bits) for bits in chip_bits)
-        starts = (
-            ((1 - odd) * 2 + 1 - other, other_next),
-            ((1 - odd) * 2 + other, other_next),
-            (odd * 2 + 1 - mine, mine_next),
-            (odd * 2 + mine, mine_next),
-        )
-        for out, (start, side), save in zip(sums, starts, saves):
-            for j, half in enumerate((1 - side, side)):
-                part = pl.ds(pl.multiple_of((start * 2 + half) * eighth, eighth), eighth)
-                lines = slice(j * eighth, (j + 1) * eighth)
-                out[lines, : 3 * width] = mm(normed_t[part, :], d_qkv[...])
-                out[lines, 3 * width : 4 * width] = mm(attn_ref[part, :], serial_grad[...])
-                out[lines, 4 * width :] = gain_column[part, :]
-            save.start()
-        for save in saves:
-            save.wait()
+
+    def alone(both, j):
+        part = both[j * head : (j + 1) * head]
+        return jnp.concatenate([part, zero] if j == 0 else [zero, part], axis=0)
+
+    for step in range(HEADS // 2):
+        lo = step * pair
+        queries = qkv_ref[:, pl.ds(lo, pair)]
+        values = qkv_ref[:, pl.ds(2 * width + lo, pair)]
+        d_att_t = d_attn_t[pl.ds(lo, pair), :] * BF16(0.125)
+        d_att = d_attn[:, pl.ds(lo, pair)]
+        keys = qkv_ref[:, pl.ds(width + lo, pair)]
+        query_t = trans_ref[pl.ds(lo, pair), :] * BF16(0.125)
+        d_q, d_k, d_v = [], [], []
+        for j in range(2):
+            top = stats_ref[pl.ds(2 * step + j, 1), :]
+            share = stats_ref[pl.ds(HEADS + 2 * step + j, 1), :]
+            probs = jnp.exp(mm(keys, alone(query_t, j)) - top) * share
+            d_probs = mm(values, alone(d_att_t, j))
+            total = jnp.sum(d_probs * probs, axis=0, keepdims=True)
+            d_scores = (probs * (d_probs - total)).astype(BF16)
+            k_t = trans_ref[pl.ds(width + lo + j * head, head), :]
+            d_q.append(mm(k_t, d_scores))
+            d_k.append(mm(d_scores, queries))
+            d_v.append(mm(probs.astype(BF16), d_att))
+        d_qkv[:, pl.ds(lo, pair)] = jnp.transpose(jnp.concatenate(d_q, axis=0)).astype(BF16)
+        d_qkv[:, pl.ds(width + lo, pair)] = jnp.where(
+            first, d_k[0], d_k[1]
+        ).astype(BF16)
+        d_qkv[:, pl.ds(2 * width + lo, pair)] = jnp.where(
+            first, d_v[0], d_v[1]
+        ).astype(BF16)
+
+    for load in loads[3:]:
+        load.wait()
+    normed_t[...] = jnp.transpose(normed_ref[...].astype(F32)).astype(BF16)
+    d_normed = mm(d_qkv[...], w_ref[...], NT)
+    d_normed_ref[...] = d_normed
+    saves[5].start()
+    gain_row = jnp.sum(d_normed * xhat_ref[...], axis=0, keepdims=True)
+    gain_column[...] = jnp.transpose(jnp.broadcast_to(gain_row, (LANES, width)))
+    eighth = width // 8
+    odd = lax.bitwise_and(me, 1)
+
+    def sides(even_bit, odd_bit):
+        even_side = lax.bitwise_and(lax.shift_right_logical(me, even_bit), 1)
+        odd_side = lax.bitwise_and(lax.shift_right_logical(me, odd_bit), 1)
+        mine = jnp.where(odd == 1, odd_side, even_side)
+        return mine, even_side + odd_side - mine
+
+    (mine, other), (mine_next, other_next) = (sides(*bits) for bits in chip_bits)
+    starts = (
+        ((1 - odd) * 2 + 1 - other, other_next),
+        ((1 - odd) * 2 + other, other_next),
+        (odd * 2 + 1 - mine, mine_next),
+        (odd * 2 + mine, mine_next),
+    )
+    for out, (start, side), save in zip(sums, starts, saves):
+        for j, half in enumerate((1 - side, side)):
+            part = pl.ds(pl.multiple_of((start * 2 + half) * eighth, eighth), eighth)
+            lines = slice(j * eighth, (j + 1) * eighth)
+            out[lines, : 3 * width] = mm(normed_t[part, :], d_qkv[...])
+            out[lines, 3 * width : 4 * width] = mm(attn_ref[part, :], serial_grad[...])
+            out[lines, 4 * width :] = gain_column[part, :]
+        save.start()
+    for save in saves:
+        save.wait()
 
 
 def residual_kernel(
@@ -315,17 +308,12 @@
     out_ref[...] = mm(column_hot(slot_ref[...], values.shape[0]), values).astype(BF16)
 
 
-def split_kernel(side_ref, own_ref, other_ref, qkv_out, proj_out, gain_out):
+def split_kernel(side_ref, sums_ref, *refs):
+    qkv_out, proj_out, gain_out = refs[-3:]
     width = proj_out.shape[1]
-
-    def write(ref):
-        qkv_out[...] = ref[:, : 3 * width].astype(F32)
-        proj_out[...] = ref[:, 3 * width : 4 * width].astype(F32)
-        gain_out[...] = jnp.transpose(ref[:, 4 * width :].astype(F32))[0:1]
-
-    own = pl.program_id(0) == side_ref[0]
-    pl.when(own)(lambda: write(own_ref))
-    pl.when(jnp.logical_not(own))(lambda: write(other_ref))
+    qkv_out[...] = sums_ref[:, : 3 * width].astype(F32)
+    proj_out[...] = sums_ref[:, 3 * width : 4 * width].astype(F32)
+    gain_out[...] = jnp.transpose(sums_ref[:, 4 * width :].astype(F32))[0:1]
 
 
 def exponent_of(largest):
@@ -523,6 +511,33 @@
     return part
 
 
+def write_half(side, sums, outs=()):
+    half, width = sums.shape[0], (sums.shape[1] - LANES) // 4
+    return pl.pallas_call(
+        split_kernel,
+        grid_spec=pltpu.PrefetchScalarGridSpec(
+            num_scalar_prefetch=1,
+            grid=(2,),
+            in_specs=[pl.BlockSpec((half // 2, sums.shape[1]), lambda i, s: (i, 0))]
+            + [pl.BlockSpec(memory_space=pl.ANY)] * len(outs),
+            out_specs=[
+                pl.BlockSpec((half // 2, 3 * width), lambda i, s: (2 * s[0] + i, 0)),
+                pl.BlockSpec((half // 2, width), lambda i, s: (2 * s[0] + i, 0)),
+                pl.BlockSpec((1, half // 2), lambda i, s: (0, 2 * s[0] + i)),
+            ],
+        ),
+        out_shape=(
+            shape_of((2 * half, 3 * width), F32),
+            shape_of((2 * half, width), F32),
+            shape_of((1, 2 * half), F32),
+        ),
+        input_output_aliases={2 + i: i for i in range(len(outs))},
+        compiler_params=params(20),
+        cost_estimate=pl.CostEstimate(flops=0, bytes_accessed=4 * MIB, transcendentals=0),
+        name="split",
+    )(side, sums, *outs)
+
+
 def per_device(points, cotangent, dest, w_qkv, w_proj, gain):
     feats = points[0]
     grads = cotangent[0]
@@ -581,7 +596,7 @@
 
     pos, xhat, inv, normed, qkv, trans, attn_t, stats = pl.pallas_call(
         functools.partial(forward_kernel, n_seq, capacity),
-        grid=(pairs,),
+        grid=(1,),
         out_shape=(
             shape_of((1, slots), jnp.int32),
             shape_of((rows, width), F32),
@@ -595,7 +610,7 @@
         in_specs=[in_hbm, whole((1, width))] + [whole((block, width))] * n_seq,
         out_specs=[whole((1, slots))]
         + [in_hbm] * 5
-        + [pl.BlockSpec((pair, rows), lambda i: (i, 0)), whole((2 * HEADS, rows))],
+        + [whole((width, rows)), whole((2 * HEADS, rows))],
         scratch_shapes=[
             pltpu.VMEM((width, 3 * width), BF16),
             pltpu.VMEM((rows, width), F32),
@@ -617,7 +632,7 @@
     chip_bits = tuple(zip(*chip_orders(n_seq)))[:2]
     *quarters, serial_grad, d_normed = pl.pallas_call(
         functools.partial(backward_kernel, n_seq, chip_bits),
-        grid=(pairs,),
+        grid=(1,),
         out_shape=[shape_of(sum_shape, F32)] * 4
         + [shape_of((rows, width), BF16), shape_of((rows, width), F32)],
         in_specs=[
@@ -675,7 +690,6 @@
     returned = exchange(back)
     part, returned = lax.optimization_barrier((reduce_over_planes(terms, got, steps), returned))
     own = share_in_plane(share_over_planes(part), steps)
-    other = lax.ppermute(own, "seq", core_pairs())
     grad_local = pl.pallas_call(
         functools.partial(unpack_kernel, n_seq),
         out_shape=shape_of((rows, width), BF16),
@@ -687,25 +701,11 @@
         ),
         name="unpack",
     )(me, slot, returned)
-    half = width // 2
-    grad_qkv, grad_proj, gain_grad = pl.pallas_call(
-        split_kernel,
-        grid=(2,),
-        out_shape=(
-            shape_of((width, 3 * width), F32),
-            shape_of((width, width), F32),
-            shape_of((1, width), F32),
-        ),
-        in_specs=[in_smem] + [whole(own.shape)] * 2,
-        out_specs=[
-            pl.BlockSpec((half, 3 * width), lambda i: (i, 0)),
-            pl.BlockSpec((half, width), lambda i: (i, 0)),
-            pl.BlockSpec((1, half), lambda i: (0, i)),
-        ],
-        compiler_params=params(20),
-        cost_estimate=pl.CostEstimate(flops=0, bytes_accessed=8 * MIB, transcendentals=0),
-        name="split",
-    )(lax.bitwise_and(me, 1), own, other)
+    own, grad_local = lax.optimization_barrier((own, grad_local))
+    other = lax.ppermute(own, "seq", core_pairs())
+    side = lax.bitwise_and(me, 1)
+    outs = write_half(side, own)
+    grad_qkv, grad_proj, gain_grad = write_half(1 - side, other, outs)
     return (grad_local[None], grad_qkv, grad_proj, gain_grad[0])
 
 

time: 134 us -> 133 us (level)
  waiting for transfers between devices: 59.6 us -> 57.6 us
    ppermute x2, waiting for transfers between devices: 16.6 us -> 13.4 us  [share_in_plane(): other = lax.ppermute(part, 'seq', pairs)]
    ppermute x1, waiting for transfers between devices: 0.01 us -> 1.34 us  [per_device(): other = lax.ppermute(own, 'seq', core_pairs())]
    pallas_call x1 -> x2, Pallas kernels: 2.16 us -> 2.73 us  [write_half(): pl.pallas_call(split_kernel, grid_spec=pltpu.PrefetchScalarGridSpec(num_s...]
  transfers between devices with their start and end apart: 22 -> 22, of which waited for: 13 -> 15; matrix products, arithmetic and copies ran while one was open for 0% -> 0% of each run, Pallas kernels for 13% -> 14%
where the time goes in v11:
time: 133 us
  waiting for transfers between devices  57.6 us (43%)
  Pallas kernels  40.7 us (31%)
  starting transfers between devices  28.9 us (22%)
  local copies, waits for them, and re-layouts  4.41 us (3%)
    ppermute x13, waiting for transfers between devices, by_distance(): lax.ppermute(blocks[k], axis, [(i, i ^ k) for i in range(count)])  18.5 us
    ppermute x13, starting transfers between devices, by_distance(): lax.ppermute(blocks[k], axis, [(i, i ^ k) for i in range(count)])  18.1 us
    pallas_call x1, Pallas kernels, per_device(): pl.pallas_call(functools.partial(backward_kernel, n_seq, chip_bits), grid...  17.2 us
    ppermute x2, waiting for transfers between devices, share_in_plane(): other = lax.ppermute(part, 'seq', pairs)  13.4 us
    pallas_call x1, Pallas kernels, per_device(): pl.pallas_call(functools.partial(forward_kernel, n_seq, capacity), grid=(...  9.87 us
    all_to_all x2, waiting for transfers between devices, exchange(): got = lax.all_to_all(sent, 'seq', split_axis=0, concat_axis=0, tiled=True)  9.84 us
    ppermute x1, waiting for transfers between devices, first_step(): return [own_keep, got_keep, lax.ppermute(sent, 'seq', steps[0][0])]  9.02 us
    all_to_all x2, starting transfers between devices, exchange(): got = lax.all_to_all(sent, 'seq', split_axis=0, concat_axis=0, tiled=True)  8.3 us
  transfers between devices with their start and end apart: 22, of which 15 were waited for; matrix products, arithmetic and copies ran while one was open for 0% of the time, Pallas kernels for 14%

profile of v11, /device:TPU:0, one launch (start us, length us, event | category | flops | bytes accessed | tf_op | source)
XLA Modules:
  0.0 132.9 jit_solution(4724306925125543723)
XLA Ops:
  0.6 3.0 %pack.1 = (s32[1,512]{1,0:T(1,128)}, bf16[144,512]{1,0:T(8,128)(2,1)}, bf16[144,512]{1,0:T(8,128)(2,1)}, bf16[144,512]{1,0:T(8,128)(2,1)}, bf16[144,512]{1,0:T(8...) custom-call(s32[1]{0:T(128)} %bitcast.1.me_ref, ...), custom_call_target="tpu_custom_call" | custom-call | flops 536870912 | bytes 2097152 | tf_op jit(solution)/shard_map/pack/pallas_call | solution.py:559
  3.7 0.5 collective-permute-start
  4.2 2.6 %collective-permute-start.1 = (bf16[144,512]{1,0:T(8,128)(2,1)}, bf16[144,512]{1,0:T(8,128)(2,1)S(1)}, u32[]{:S(2)}, u32[]{:S(2)}) collective-permute-start(bf16[144,512]{1,0:T(8,128)(2,1)} %get-tuple-element.58), channel_id=1, source_target_pairs={{0,8},{4,12},{8,0},{12,4},{16,24},{20,28},{24,16},{28,20},{1,9},{5... | collective-permute-start | bytes 442376 | tf_op jit(solution)/shard_map/ppermute | solution.py:395
  6.8 1.8 %collective-permute-start.3 = (bf16[144,512]{1,0:T(8,128)(2,1)}, bf16[144,512]{1,0:T(8,128)(2,1)S(1)}, u32[]{:S(2)}, u32[]{:S(2)}) collective-permute-start(bf16[144,512]{1,0:T(8,128)(2,1)} %get-tuple-element.60), channel_id=1, source_target_pairs={{0,16},{4,20},{8,24},{12,28},{16,0},{20,4},{24,8},{28,12},{1,17},{... | collective-permute-start | bytes 442376 | tf_op jit(solution)/shard_map/ppermute | solution.py:395
  8.6 2.6 %collective-permute-start.5 = (bf16[144,512]{1,0:T(8,128)(2,1)}, bf16[144,512]{1,0:T(8,128)(2,1)S(1)}, u32[]{:S(2)}, u32[]{:S(2)}) collective-permute-start(bf16[144,512]{1,0:T(8,128)(2,1)} %get-tuple-element.62), channel_id=1, source_target_pairs={{0,24},{4,28},{8,16},{12,20},{16,8},{20,12},{24,0},{28,4},{1,25},{... | collective-permute-start | bytes 442376 | tf_op jit(solution)/shard_map/ppermute | solution.py:395
  11.2 0.5 collective-permute-done.1.refs_2_
  11.7 1.7 %collective-permute-start.6 = (bf16[144,512]{1,0:T(8,128)(2,1)}, bf16[144,512]{1,0:T(8,128)(2,1)S(1)}, u32[]{:S(2)}, u32[]{:S(2)}) collective-permute-start(bf16[144,512]{1,0:T(8,128)(2,1)} %get-tuple-element.63), channel_id=1, source_target_pairs={{0,28},{4,24},{8,20},{12,16},{16,12},{20,8},{24,4},{28,0},{1,29},{... | collective-permute-start | bytes 442376 | tf_op jit(solution)/shard_map/ppermute | solution.py:395
  13.4 0.7 copy-done.9
  14.1 1.7 %pack_grads.1 = bf16[1024,512]{1,0:T(8,128)(2,1)} custom-call(s32[1]{0:T(128)} %bitcast.1.me_ref, s32[1,512]{1,0:T(1,128)S(1)} %copy-done.9, bf16[512,512]{1,0:T(8,128)(2,1)S(1)} %bitcast.30), custom_call_target="tpu_custom_call" | custom-call | flops 536870912 | bytes 2097152 | tf_op jit(solution)/shard_map/pack_grads/pallas_call | solution.py:577
  15.8 6.2 %collective-permute-done.4.refs_5_ = bf16[144,512]{1,0:T(8,128)(2,1)S(1)} collective-permute-done((bf16[144,512]{1,0:T(8,128)(2,1)}, bf16[144,512]{1,0:T(8,128)(2,1)S(1)}, u32[]{:S(2)}, u32[]{:S(2)}) %collective-permute-start.4) | collective-permute-done | bytes 147488 | tf_op jit(solution)/shard_map/ppermute | solution.py:395
  22.0 4.0 %all-to-all-start = ((bf16[8,128,512]{2,1,0:T(8,128)(2,1)}), bf16[8,128,512]{2,1,0:T(8,128)(2,1)S(1)}, u32[]{:S(2)}, u32[]{:S(2)}) async-start(bf16[8,128,512]{2,1,0:T(8,128)(2,1)} %bitcast.5), calls=%async_computation | async-start | bytes 2097152 | tf_op jit(solution)/shard_map/all_to_all | solution.py:591
  26.1 9.9 %forward.1 = (s32[1,1024]{1,0:T(1,128)}, f32[512,512]{1,0:T(8,128)}, f32[512,128]{1,0:T(8,128)}, bf16[512,512]{1,0:T(8,128)(2,1)}, bf16[512,1536]{1,0:T(8,128)(2...) custom-call(bf16[512,1536]{1,0:T(8,128)(2,1)} %refs_3_.1, f32[1,512]{1,0:T(1,128)} %bitcast.28, ...), custom_call_target="tpu_custom_call" | custom-call | flops 2952790016 | bytes 16777216 | tf_op jit(solution)/shard_map/forward/pallas_call | solution.py:597
  36.0 5.5 %all-to-all-done = bf16[8,128,512]{2,1,0:T(8,128)(2,1)S(1)} async-done(((bf16[8,128,512]{2,1,0:T(8,128)(2,1)}), bf16[8,128,512]{2,1,0:T(8,128)(2,1)S(1)}, u32[]{:S(2)}, u32[]{:S(2)}) %all-to-all-start) | async-done | bytes 1048608 | tf_op jit(solution)/shard_map/all_to_all | solution.py:591
  41.5 1.0 copy-done.11
  42.5 17.2 %backward.1 = (f32[128,2176]{1,0:T(8,128)}, f32[128,2176]{1,0:T(8,128)}, f32[128,2176]{1,0:T(8,128)}, f32[128,2176]{1,0:T(8,128)}, bf16[512,512]{1,0:T(8,128)(2,1)}, /*index=5*/f32[512,512]{1,0:T(8,128)}) custom-call(s32[1]{0:T(128)} %bitcast.1.me_ref, s32[1,1024]{1,0:T(1,128)} %get-tuple-element.73.pos_ref, bf16[512,512]{1,0:T(8,128)(2,1)} %w_proj_ref.1, ...), custom_call_target="tpu_custom_call" | custom-call | flops 4294967296 | bytes 16777216 | tf_op jit(solution)/shard_map/backward/pallas_call | solution.py:633
  59.8 0.5 collective-permute-start.7
  60.3 2.5 %collective-permute-done.8.refs_1_ = f32[128,2176]{1,0:T(8,128)S(1)} collective-permute-done((f32[128,2176]{1,0:T(8,128)}, f32[128,2176]{1,0:T(8,128)S(1)}, u32[]{:S(2)}, u32[]{:S(2)}) %collective-permute-start.8) | collective-permute-done | bytes 1114144 | tf_op jit(solution)/shard_map/ppermute | solution.py:454
  62.8 1.2 copy-done.1
  64.0 0.3 code_first.1
  64.3 0.6 collective-permute-start.9
  64.9 9.0 %collective-permute-done.9.refs_2_ = s16[128,2176]{1,0:T(8,128)(2,1)S(1)} collective-permute-done((s16[128,2176]{1,0:T(8,128)(2,1)S(1)}, s16[128,2176]{1,0:T(8,128)(2,1)S(1)}, u32[]{:S(2)}, u32[]{:S(2)}) %collective-permute-start.9) | collective-permute-done | bytes 557088 | tf_op jit(solution)/shard_map/ppermute | solution.py:457
  74.0 0.3 code_second.1
  74.3 0.6 collective-permute-start.10
  74.9 0.3 copy-done.2
  75.2 0.3 copy-done.3
  75.7 2.1 %residual.1 = bf16[1024,512]{1,0:T(8,128)(2,1)} custom-call(s32[1]{0:T(128)} %bitcast.1.me_ref, s32[1,1024]{1,0:T(1,128)S(1)} %copy-done.6, f32[1,512]{1,0:T(1,128)S(1)} %bitcast.29, f32[512,128]{1,0:T(8,128)S(1)} %copy-done.5, f32[512,512]{1,0:T(8,128)S(1)} %copy-done.2, bf16[512,512]{1,0:T(8,128)(2,1)S(1)} %copy-done.4, f32[512,512]{1,0:T(8,128)S(1)} %copy-done.3), custom_call_target="tpu_custom_call" | custom-call | flops 536870912 | bytes 4194304 | tf_op jit(solution)/shard_map/residual/pallas_call | solution.py:677
  77.8 3.1 %collective-permute-done.10.refs_3_ = s16[64,2176]{1,0:T(8,128)(2,1)S(1)} collective-permute-done((s16[64,2176]{1,0:T(8,128)(2,1)S(1)}, s16[64,2176]{1,0:T(8,128)(2,1)S(1)}, u32[]{:S(2)}, u32[]{:S(2)}) %collective-permute-start.10) | collective-permute-done | bytes 278560 | tf_op jit(solution)/shard_map/ppermute | solution.py:462
  80.9 4.2 %all-to-all-start.1 = ((bf16[8,128,512]{2,1,0:T(8,128)(2,1)}), bf16[8,128,512]{2,1,0:T(8,128)(2,1)}, u32[]{:S(2)}, u32[]{:S(2)}) async-start(bf16[8,128,512]{2,1,0:T(8,128)(2,1)} %bitcast.7), calls=%async_computation.1 | async-start | bytes 2097152 | tf_op jit(solution)/shard_map/all_to_all | solution.py:591
  85.1 0.5 code_planes.1
  85.6 1.7 %collective-permute-start.11 = (s16[16,2176]{1,0:T(8,128)(2,1)S(1)}, s16[16,2176]{1,0:T(8,128)(2,1)S(1)}, u32[]{:S(2)}, u32[]{:S(2)}) collective-permute-start(s16[16,2176]{1,0:T(8,128)(2,1)S(1)} %get-tuple-element.90), channel_id=1, source_target_pairs={{0,1},{1,0},{2,3},{3,2},{4,5},{5,4},{6,7},{7,6},{8,9},{9,8},{10,11... | collective-permute-start | bytes 208904 | tf_op jit(solution)/shard_map/ppermute | solution.py:395
  87.3 2.6 %collective-permute-start.12 = (s16[16,2176]{1,0:T(8,128)(2,1)S(1)}, s16[16,2176]{1,0:T(8,128)(2,1)S(1)}, u32[]{:S(2)}, u32[]{:S(2)}) collective-permute-start(s16[16,2176]{1,0:T(8,128)(2,1)S(1)} %get-tuple-element.91), channel_id=1, source_target_pairs={{0,2},{1,3},{2,0},{3,1},{4,6},{5,7},{6,4},{7,5},{8,10},{9,11},{10,... | collective-permute-start | bytes 208904 | tf_op jit(solution)/shard_map/ppermute | solution.py:395
  89.9 0.2 collective-permute-start.13
  90.2 5.1 %collective-permute-done.12.refs_2_ = s16[16,2176]{1,0:T(8,128)(2,1)S(1)} collective-permute-done((s16[16,2176]{1,0:T(8,128)(2,1)S(1)}, s16[16,2176]{1,0:T(8,128)(2,1)S(1)}, u32[]{:S(2)}, u32[]{:S(2)}) %collective-permute-start.12) | collective-permute-done | bytes 69664 | tf_op jit(solution)/shard_map/ppermute | solution.py:395
  95.2 0.8 collective-permute-done.13.refs_3_
  96.2 4.4 %all-to-all-done.1 = bf16[8,128,512]{2,1,0:T(8,128)(2,1)} async-done(((bf16[8,128,512]{2,1,0:T(8,128)(2,1)}), bf16[8,128,512]{2,1,0:T(8,128)(2,1)}, u32[]{:S(2)}, u32[]{:S(2)}) %all-to-all-start.1) | async-done | bytes 1048608 | tf_op jit(solution)/shard_map/all_to_all | solution.py:591
  100.5 1.6 %collective-permute-start.14 = (bf16[16,2176]{1,0:T(8,128)(2,1)S(1)}, bf16[16,2176]{1,0:T(8,128)(2,1)S(1)}, u32[]{:S(2)}, u32[]{:S(2)}) collective-permute-start(bf16[16,2176]{1,0:T(8,128)(2,1)S(1)} %finish.1), channel_id=1, source_target_pairs={{0,1},{1,0},{2,3},{3,2},{4,5},{5,4},{6,7},{7,6},{8,9},{9,8},{10,11... | collective-permute-start | bytes 208904 | tf_op jit(solution)/shard_map/ppermute | solution.py:395
  102.1 2.6 %collective-permute-start.15 = (bf16[16,2176]{1,0:T(8,128)(2,1)S(1)}, bf16[16,2176]{1,0:T(8,128)(2,1)S(1)}, u32[]{:S(2)}, u32[]{:S(2)}) collective-permute-start(bf16[16,2176]{1,0:T(8,128)(2,1)S(1)} %finish.1), channel_id=1, source_target_pairs={{0,2},{1,3},{2,0},{3,1},{4,6},{5,7},{6,4},{7,5},{8,10},{9,11},{10,... | collective-permute-start | bytes 208904 | tf_op jit(solution)/shard_map/ppermute | solution.py:395
  104.7 0.2 collective-permute-start.16
  104.9 3.1 %collective-permute-done.15 = bf16[16,2176]{1,0:T(8,128)(2,1)S(1)} collective-permute-done((bf16[16,2176]{1,0:T(8,128)(2,1)S(1)}, bf16[16,2176]{1,0:T(8,128)(2,1)S(1)}, u32[]{:S(2)}, u32[]{:S(2)}) %collective-permute-start.15) | collective-permute-done | bytes 69664 | tf_op jit(solution)/shard_map/ppermute | solution.py:395
  108.1 2.7 %collective-permute-done.16 = bf16[16,2176]{1,0:T(8,128)(2,1)S(1)} collective-permute-done((bf16[16,2176]{1,0:T(8,128)(2,1)S(1)}, bf16[16,2176]{1,0:T(8,128)(2,1)S(1)}, u32[]{:S(2)}, u32[]{:S(2)}) %collective-permute-start.16) | collective-permute-done | bytes 69664 | tf_op jit(solution)/shard_map/ppermute | solution.py:395
  111.0 0.6 collective-permute-start.17
  111.6 7.1 %collective-permute-done.17 = bf16[64,2176]{1,0:T(8,128)(2,1)S(1)} collective-permute-done((bf16[64,2176]{1,0:T(8,128)(2,1)S(1)}, bf16[64,2176]{1,0:T(8,128)(2,1)S(1)}, u32[]{:S(2)}, u32[]{:S(2)}) %collective-permute-start.17) | collective-permute-done | bytes 278560 | tf_op jit(solution)/shard_map/ppermute | solution.py:507
  119.0 0.4 copy-done.10
  119.4 2.8 %unpack.1 = bf16[512,512]{1,0:T(8,128)(2,1)} custom-call(s32[1]{0:T(128)} %bitcast.1.me_ref, s32[1,512]{1,0:T(1,128)S(1)} %copy-done.10, bf16[1024,512]{1,0:T(8,128)(2,1)} %bitcast.8.recv_ref), custom_call_target="tpu_custom_call" | custom-call | flops 536870912 | bytes 2097152 | tf_op jit(solution)/shard_map/unpack/pallas_call | solution.py:693
  122.2 6.3 %collective-permute-done.18 = bf16[128,2176]{1,0:T(8,128)(2,1)S(1)} collective-permute-done((bf16[128,2176]{1,0:T(8,128)(2,1)S(1)}, bf16[128,2176]{1,0:T(8,128)(2,1)S(1)}, u32[]{:S(2)}, u32[]{:S(2)}) %collective-permute-start.18) | collective-permute-done | bytes 557088 | tf_op jit(solution)/shard_map/ppermute | solution.py:507
  128.8 1.4 %split.2 = (f32[512,1536]{1,0:T(8,128)}, f32[512,512]{1,0:T(8,128)}, f32[1,512]{1,0:T(1,128)}) custom-call(s32[1]{0:T(128)S(6)} %and.19.side_ref, bf16[256,2176]{1,0:T(8,128)(2,1)S(1)} %maximum_select_fusion.sums_ref), custom_call_target="tpu_custom_call" | custom-call | bytes 4194304 | tf_op jit(solution)/shard_map/split/pallas_call | solution.py:516
  130.2 1.3 %collective-permute-done.19.sums_ref = bf16[256,2176]{1,0:T(8,128)(2,1)S(1)} collective-permute-done((bf16[256,2176]{1,0:T(8,128)(2,1)S(1)}, bf16[256,2176]{1,0:T(8,128)(2,1)S(1)}, u32[]{:S(2)}, u32[]{:S(2)}) %collective-permute-start.19) | collective-permute-done | bytes 1114144 | tf_op jit(solution)/shard_map/ppermute | solution.py:705
  131.6 1.3 %split.3 = (f32[512,1536]{1,0:T(8,128)}, f32[512,512]{1,0:T(8,128)}, f32[1,512]{1,0:T(1,128)}) custom-call(s32[1]{0:T(128)S(6)} %sub.3.side_ref, bf16[256,2176]{1,0:T(8,128)(2,1)S(1)} %collective-permute-done.19.sums_ref, f32[512,1536]{1,0:T(8,128)} %get-tuple-element.98.refs_0_, ...), custom_call_target="tpu_custom_call", output_to_operand_aliasing={{0}: (2, {}), {1}: (3, {}), {2}: (4, {})} | custom-call | bytes 4194304 | tf_op jit(solution)/shard_map/split/pallas_call | solution.py:516
  (59 shorter events, 1.3 us)
Async XLA Ops:
  0.6 12.8 %copy-start.8 = (bf16[1,512,512]{2,1,0:T(8,128)(2,1)S(1)}, bf16[1,512,512]{2,1,0:T(8,128)(2,1)}, u32[]{:S(2)}) copy-start(bf16[1,512,512]{2,1,0:T(8,128)(2,1)} %param.7) | copy-start | bytes 1572868
  3.7 4.9 %collective-permute-start = (bf16[144,512]{1,0:T(8,128)(2,1)}, bf16[144,512]{1,0:T(8,128)(2,1)S(1)}, u32[]{:S(2)}, u32[]{:S(2)}) collective-permute-start(bf16[144,512]{1,0:T(8,128)(2,1)} %get-tuple-element.55), channel_id=1, source_target_pairs={{0,4},{4,0},{8,12},{12,8},{16,20},{20,16},{24,28},{28,24},{1,5},{5... | collective-permute-start | bytes 442376 | tf_op jit(solution)/shard_map/ppermute | solution.py:395
  4.2 7.5 %collective-permute-start.1 = (bf16[144,512]{1,0:T(8,128)(2,1)}, bf16[144,512]{1,0:T(8,128)(2,1)S(1)}, u32[]{:S(2)}, u32[]{:S(2)}) collective-permute-start(bf16[144,512]{1,0:T(8,128)(2,1)} %get-tuple-element.58), channel_id=1, source_target_pairs={{0,8},{4,12},{8,0},{12,4},{16,24},{20,28},{24,16},{28,20},{1,9},{5... | collective-permute-start | bytes 442376 | tf_op jit(solution)/shard_map/ppermute | solution.py:395
  6.8 9.0 %collective-permute-start.2 = (bf16[144,512]{1,0:T(8,128)(2,1)}, bf16[144,512]{1,0:T(8,128)(2,1)S(1)}, u32[]{:S(2)}, u32[]{:S(2)}) collective-permute-start(bf16[144,512]{1,0:T(8,128)(2,1)} %get-tuple-element.59), channel_id=1, source_target_pairs={{0,12},{4,8},{8,4},{12,0},{16,28},{20,24},{24,20},{28,16},{1,13},{... | collective-permute-start | bytes 442376 | tf_op jit(solution)/shard_map/ppermute | solution.py:395
  6.8 9.0 %collective-permute-start.3 = (bf16[144,512]{1,0:T(8,128)(2,1)}, bf16[144,512]{1,0:T(8,128)(2,1)S(1)}, u32[]{:S(2)}, u32[]{:S(2)}) collective-permute-start(bf16[144,512]{1,0:T(8,128)(2,1)} %get-tuple-element.60), channel_id=1, source_target_pairs={{0,16},{4,20},{8,24},{12,28},{16,0},{20,4},{24,8},{28,12},{1,17},{... | collective-permute-start | bytes 442376 | tf_op jit(solution)/shard_map/ppermute | solution.py:395
  8.6 13.4 %collective-permute-start.4 = (bf16[144,512]{1,0:T(8,128)(2,1)}, bf16[144,512]{1,0:T(8,128)(2,1)S(1)}, u32[]{:S(2)}, u32[]{:S(2)}) collective-permute-start(bf16[144,512]{1,0:T(8,128)(2,1)} %get-tuple-element.61), channel_id=1, source_target_pairs={{0,20},{4,16},{8,28},{12,24},{16,4},{20,0},{24,12},{28,8},{1,21},{... | collective-permute-start | bytes 442376 | tf_op jit(solution)/shard_map/ppermute | solution.py:395
  8.6 13.4 %copy-start.12 = (bf16[144,512]{1,0:T(8,128)(2,1)}, bf16[144,512]{1,0:T(8,128)(2,1)S(1)}, u32[]{:S(2)}) copy-start(bf16[144,512]{1,0:T(8,128)(2,1)S(1)} %collective-permute-done.refs_1_) | copy-start | bytes 442372
  8.6 13.4 %collective-permute-start.5 = (bf16[144,512]{1,0:T(8,128)(2,1)}, bf16[144,512]{1,0:T(8,128)(2,1)S(1)}, u32[]{:S(2)}, u32[]{:S(2)}) collective-permute-start(bf16[144,512]{1,0:T(8,128)(2,1)} %get-tuple-element.62), channel_id=1, source_target_pairs={{0,24},{4,28},{8,16},{12,20},{16,8},{20,12},{24,0},{28,4},{1,25},{... | collective-permute-start | bytes 442376 | tf_op jit(solution)/shard_map/ppermute | solution.py:395
  11.7 10.4 %copy-start.13 = (bf16[144,512]{1,0:T(8,128)(2,1)}, bf16[144,512]{1,0:T(8,128)(2,1)S(1)}, u32[]{:S(2)}) copy-start(bf16[144,512]{1,0:T(8,128)(2,1)S(1)} %collective-permute-done.1.refs_2_) | copy-start | bytes 442372
  11.7 10.3 %collective-permute-start.6 = (bf16[144,512]{1,0:T(8,128)(2,1)}, bf16[144,512]{1,0:T(8,128)(2,1)S(1)}, u32[]{:S(2)}, u32[]{:S(2)}) collective-permute-start(bf16[144,512]{1,0:T(8,128)(2,1)} %get-tuple-element.63), channel_id=1, source_target_pairs={{0,28},{4,24},{8,20},{12,16},{16,12},{20,8},{24,4},{28,0},{1,29},{... | collective-permute-start | bytes 442376 | tf_op jit(solution)/shard_map/ppermute | solution.py:395
  13.4 0.7 copy-start.9
  15.8 10.3 %copy-start.14 = (bf16[144,512]{1,0:T(8,128)(2,1)}, bf16[144,512]{1,0:T(8,128)(2,1)S(1)}, u32[]{:S(2)}) copy-start(bf16[144,512]{1,0:T(8,128)(2,1)S(1)} %collective-permute-done.2.refs_3_) | copy-start | bytes 442372
  15.8 10.3 %copy-start.15 = (bf16[144,512]{1,0:T(8,128)(2,1)}, bf16[144,512]{1,0:T(8,128)(2,1)S(1)}, u32[]{:S(2)}) copy-start(bf16[144,512]{1,0:T(8,128)(2,1)S(1)} %collective-permute-done.3.refs_4_) | copy-start | bytes 442372
  22.0 4.1 %copy-start.16 = (bf16[144,512]{1,0:T(8,128)(2,1)}, bf16[144,512]{1,0:T(8,128)(2,1)S(1)}, u32[]{:S(2)}) copy-start(bf16[144,512]{1,0:T(8,128)(2,1)S(1)} %collective-permute-done.4.refs_5_) | copy-start | bytes 442372
  22.0 4.1 %copy-start.17 = (bf16[144,512]{1,0:T(8,128)(2,1)}, bf16[144,512]{1,0:T(8,128)(2,1)S(1)}, u32[]{:S(2)}) copy-start(bf16[144,512]{1,0:T(8,128)(2,1)S(1)} %collective-permute-done.5.refs_6_) | copy-start | bytes 442372
  22.0 4.1 %copy-start.18 = (bf16[144,512]{1,0:T(8,128)(2,1)}, bf16[144,512]{1,0:T(8,128)(2,1)S(1)}, u32[]{:S(2)}) copy-start(bf16[144,512]{1,0:T(8,128)(2,1)S(1)} %collective-permute-done.6.refs_7_) | copy-start | bytes 442372
  22.0 19.5 %all-to-all-start = ((bf16[8,128,512]{2,1,0:T(8,128)(2,1)}), bf16[8,128,512]{2,1,0:T(8,128)(2,1)S(1)}, u32[]{:S(2)}, u32[]{:S(2)}) async-start(bf16[8,128,512]{2,1,0:T(8,128)(2,1)} %bitcast.5), calls=%async_computation | async-start | bytes 2097152 | tf_op jit(solution)/shard_map/all_to_all | solution.py:591
  41.5 1.0 copy-start.11
  59.7 3.0 %collective-permute-start.8 = (f32[128,2176]{1,0:T(8,128)}, f32[128,2176]{1,0:T(8,128)S(1)}, u32[]{:S(2)}, u32[]{:S(2)}) collective-permute-start(f32[128,2176]{1,0:T(8,128)} %get-tuple-element.84), channel_id=1, source_target_pairs={{0,4},{4,0},{8,12},{12,8},{16,20},{20,16},{24,28},{28,24},{1,5},{5... | collective-permute-start | bytes 3342344 | tf_op jit(solution)/shard_map/ppermute | solution.py:454
  59.8 5.1 %collective-permute-start.7 = (f32[128,2176]{1,0:T(8,128)}, f32[128,2176]{1,0:T(8,128)S(1)}, u32[]{:S(2)}, u32[]{:S(2)}) collective-permute-start(f32[128,2176]{1,0:T(8,128)} %get-tuple-element.82), channel_id=1, source_target_pairs={{0,4},{4,0},{8,12},{12,8},{16,20},{20,16},{24,28},{28,24},{1,5},{5... | collective-permute-start | bytes 3342344 | tf_op jit(solution)/shard_map/ppermute | solution.py:455
  62.8 1.2 copy-start.1
  64.0 9.9 %copy-start = (f32[128,2176]{1,0:T(8,128)S(1)}, f32[128,2176]{1,0:T(8,128)}, u32[]{:S(2)}) copy-start(f32[128,2176]{1,0:T(8,128)} %get-tuple-element.81.refs_0_) | copy-start | bytes 3342340
  64.3 9.6 %collective-permute-start.9 = (s16[128,2176]{1,0:T(8,128)(2,1)S(1)}, s16[128,2176]{1,0:T(8,128)(2,1)S(1)}, u32[]{:S(2)}, u32[]{:S(2)}) collective-permute-start(s16[128,2176]{1,0:T(8,128)(2,1)S(1)} %code_first.1), channel_id=1, source_target_pairs={{0,8},{4,20},{8,0},{12,28},{16,24},{20,4},{24,16},{28,12},{1,9},{5... | collective-permute-start | bytes 1671176 | tf_op jit(solution)/shard_map/ppermute | solution.py:457
  73.9 1.2 copy-start.2
  73.9 1.5 %copy-start.3 = (f32[512,512]{1,0:T(8,128)S(1)}, f32[512,512]{1,0:T(8,128)}, u32[]{:S(2)}) copy-start(f32[512,512]{1,0:T(8,128)} %get-tuple-element.87.d_normed_ref) | copy-start | bytes 3145732
  73.9 1.7 %copy-start.4 = (bf16[512,512]{1,0:T(8,128)(2,1)S(1)}, bf16[512,512]{1,0:T(8,128)(2,1)}, u32[]{:S(2)}) copy-start(bf16[512,512]{1,0:T(8,128)(2,1)} %get-tuple-element.86.serial_grad_ref) | copy-start | bytes 1572868
  73.9 1.7 %copy-start.5 = (f32[512,128]{1,0:T(8,128)S(1)}, f32[512,128]{1,0:T(8,128)}, u32[]{:S(2)}) copy-start(f32[512,128]{1,0:T(8,128)} %get-tuple-element.85.inv_ref) | copy-start | bytes 786436
  74.0 1.7 %copy-start.6 = (s32[1,1024]{1,0:T(1,128)S(1)}, s32[1,1024]{1,0:T(1,128)}, u32[]{:S(2)}) copy-start(s32[1,1024]{1,0:T(1,128)} %get-tuple-element.73.pos_ref) | copy-start | bytes 12292
  74.0 1.7 %copy-start.7 = (f32[512]{0:T(512)S(1)}, f32[512]{0:T(512)}, u32[]{:S(2)}) copy-start(f32[512]{0:T(512)} %param.11) | copy-start | bytes 6148
  74.3 6.6 %collective-permute-start.10 = (s16[64,2176]{1,0:T(8,128)(2,1)S(1)}, s16[64,2176]{1,0:T(8,128)(2,1)S(1)}, u32[]{:S(2)}, u32[]{:S(2)}) collective-permute-start(s16[64,2176]{1,0:T(8,128)(2,1)S(1)} %code_second.1), channel_id=1, source_target_pairs={{0,16},{4,12},{8,24},{12,4},{16,0},{20,28},{24,8},{28,20},{1,17},{... | collective-permute-start | bytes 835592 | tf_op jit(solution)/shard_map/ppermute | solution.py:462
  80.9 19.7 %all-to-all-start.1 = ((bf16[8,128,512]{2,1,0:T(8,128)(2,1)}), bf16[8,128,512]{2,1,0:T(8,128)(2,1)}, u32[]{:S(2)}, u32[]{:S(2)}) async-start(bf16[8,128,512]{2,1,0:T(8,128)(2,1)} %bitcast.7), calls=%async_computation.1 | async-start | bytes 2097152 | tf_op jit(solution)/shard_map/all_to_all | solution.py:591
  85.6 4.5 %collective-permute-start.11 = (s16[16,2176]{1,0:T(8,128)(2,1)S(1)}, s16[16,2176]{1,0:T(8,128)(2,1)S(1)}, u32[]{:S(2)}, u32[]{:S(2)}) collective-permute-start(s16[16,2176]{1,0:T(8,128)(2,1)S(1)} %get-tuple-element.90), channel_id=1, source_target_pairs={{0,1},{1,0},{2,3},{3,2},{4,5},{5,4},{6,7},{7,6},{8,9},{9,8},{10,11... | collective-permute-start | bytes 208904 | tf_op jit(solution)/shard_map/ppermute | solution.py:395
  87.3 7.9 %collective-permute-start.12 = (s16[16,2176]{1,0:T(8,128)(2,1)S(1)}, s16[16,2176]{1,0:T(8,128)(2,1)S(1)}, u32[]{:S(2)}, u32[]{:S(2)}) collective-permute-start(s16[16,2176]{1,0:T(8,128)(2,1)S(1)} %get-tuple-element.91), channel_id=1, source_target_pairs={{0,2},{1,3},{2,0},{3,1},{4,6},{5,7},{6,4},{7,5},{8,10},{9,11},{10,... | collective-permute-start | bytes 208904 | tf_op jit(solution)/shard_map/ppermute | solution.py:395
  89.9 6.2 %collective-permute-start.13 = (s16[16,2176]{1,0:T(8,128)(2,1)S(1)}, s16[16,2176]{1,0:T(8,128)(2,1)S(1)}, u32[]{:S(2)}, u32[]{:S(2)}) collective-permute-start(s16[16,2176]{1,0:T(8,128)(2,1)S(1)} %get-tuple-element.92), channel_id=1, source_target_pairs={{0,3},{1,2},{2,1},{3,0},{4,7},{5,6},{6,5},{7,4},{8,11},{9,10},{10,... | collective-permute-start | bytes 208904 | tf_op jit(solution)/shard_map/ppermute | solution.py:395
  100.5 4.4 %collective-permute-start.14 = (bf16[16,2176]{1,0:T(8,128)(2,1)S(1)}, bf16[16,2176]{1,0:T(8,128)(2,1)S(1)}, u32[]{:S(2)}, u32[]{:S(2)}) collective-permute-start(bf16[16,2176]{1,0:T(8,128)(2,1)S(1)} %finish.1), channel_id=1, source_target_pairs={{0,1},{1,0},{2,3},{3,2},{4,5},{5,4},{6,7},{7,6},{8,9},{9,8},{10,11... | collective-permute-start | bytes 208904 | tf_op jit(solution)/shard_map/ppermute | solution.py:395
  102.1 6.0 %collective-permute-start.15 = (bf16[16,2176]{1,0:T(8,128)(2,1)S(1)}, bf16[16,2176]{1,0:T(8,128)(2,1)S(1)}, u32[]{:S(2)}, u32[]{:S(2)}) collective-permute-start(bf16[16,2176]{1,0:T(8,128)(2,1)S(1)} %finish.1), channel_id=1, source_target_pairs={{0,2},{1,3},{2,0},{3,1},{4,6},{5,7},{6,4},{7,5},{8,10},{9,11},{10,... | collective-permute-start | bytes 208904 | tf_op jit(solution)/shard_map/ppermute | solution.py:395
  104.7 6.1 %collective-permute-start.16 = (bf16[16,2176]{1,0:T(8,128)(2,1)S(1)}, bf16[16,2176]{1,0:T(8,128)(2,1)S(1)}, u32[]{:S(2)}, u32[]{:S(2)}) collective-permute-start(bf16[16,2176]{1,0:T(8,128)(2,1)S(1)} %finish.1), channel_id=1, source_target_pairs={{0,3},{1,2},{2,1},{3,0},{4,7},{5,6},{6,5},{7,4},{8,11},{9,10},{10,... | collective-permute-start | bytes 208904 | tf_op jit(solution)/shard_map/ppermute | solution.py:395
  111.0 7.7 %collective-permute-start.17 = (bf16[64,2176]{1,0:T(8,128)(2,1)S(1)}, bf16[64,2176]{1,0:T(8,128)(2,1)S(1)}, u32[]{:S(2)}, u32[]{:S(2)}) collective-permute-start(bf16[64,2176]{1,0:T(8,128)(2,1)S(1)} %pad_maximum_fusion.1), channel_id=1, source_target_pairs={{0,16},{4,12},{8,24},{12,4},{16,0},{20,28},{24,8},{28,20},{1,17},{... | collective-permute-start | bytes 835592 | tf_op jit(solution)/shard_map/ppermute | solution.py:507
  118.8 0.7 copy-start.10
  118.9 9.6 %collective-permute-start.18 = (bf16[128,2176]{1,0:T(8,128)(2,1)S(1)}, bf16[128,2176]{1,0:T(8,128)(2,1)S(1)}, u32[]{:S(2)}, u32[]{:S(2)}) collective-permute-start(bf16[128,2176]{1,0:T(8,128)(2,1)S(1)} %broadcast_select_fusion), channel_id=1, source_target_pairs={{0,8},{4,20},{8,0},{12,28},{16,24},{20,4},{24,16},{28,12},{1,9},{5... | collective-permute-start | bytes 1671176 | tf_op jit(solution)/shard_map/ppermute | solution.py:507
  128.7 2.8 %collective-permute-start.19 = (bf16[256,2176]{1,0:T(8,128)(2,1)S(1)}, bf16[256,2176]{1,0:T(8,128)(2,1)S(1)}, u32[]{:S(2)}, u32[]{:S(2)}) collective-permute-start(bf16[256,2176]{1,0:T(8,128)(2,1)S(1)} %maximum_select_fusion.sums_ref), channel_id=1, source_target_pairs={{0,4},{4,0},{8,12},{12,8},{16,20},{20,16},{24,28},{28,24},{1,5},{5... | collective-permute-start | bytes 3342344 | tf_op jit(solution)/shard_map/ppermute | solution.py:705

commit v12 on v11

--- a/solution.py
+++ b/solution.py
@@ -131,8 +131,9 @@
     xhat = centered * inv
     xhat_ref[...] = xhat
     inv_ref[...] = jnp.broadcast_to(inv, inv_ref.shape)
-    normed = (xhat * gain_ref[...]).astype(BF16)
-    normed_ref[...] = normed
+    scaled = xhat * gain_ref[...]
+    normed = scaled.astype(BF16)
+    normed_ref[...] = jnp.transpose(scaled).astype(BF16)
     w_copy.wait()
     qkv = mm(normed, w_ref[...])
     qkv_ref[...] = qkv.astype(BF16)
@@ -167,7 +168,7 @@
     outs, serial_grad_hbm, d_normed_hbm, refs = refs[:4], refs[4], refs[5], refs[6:]
     recv_ref, qkv_ref, trans_ref, w_ref, xhat_ref, normed_ref, attn_ref, refs = *refs[:7], refs[7:]
     sums, refs = refs[:4], refs[4:]
-    serial_grad, d_normed_ref, d_attn, d_attn_t, d_qkv, normed_t, gain_column, sems = refs
+    serial_grad, d_normed_ref, d_attn, d_attn_t, d_qkv, gain_column, sems = refs
     width = w_proj_ref.shape[0]
     rows = xhat_ref.shape[0]
     capacity = recv_ref.shape[0] // n_seq
@@ -205,9 +206,8 @@
     grads = mm(place, values).astype(BF16)
     serial_grad[...] = grads
     saves[4].start()
-    d_att = mm(grads, w_proj_ref[...], NT).astype(BF16)
-    d_attn[...] = d_att
-    d_attn_t[...] = jnp.transpose(d_att.astype(F32)).astype(BF16)
+    d_attn[...] = mm(grads, w_proj_ref[...], NT).astype(BF16)
+    d_attn_t[...] = mm(w_proj_ref[...], grads, NT).astype(BF16)
     loads[1].wait()
     loads[2].wait()
 
@@ -248,7 +248,6 @@
 
     for load in loads[3:]:
         load.wait()
-    normed_t[...] = jnp.transpose(normed_ref[...].astype(F32)).astype(BF16)
     d_normed = mm(d_qkv[...], w_ref[...], NT)
     d_normed_ref[...] = d_normed
     saves[5].start()
@@ -270,14 +269,22 @@
         (odd * 2 + 1 - mine, mine_next),
         (odd * 2 + mine, mine_next),
     )
-    for out, (start, side), save in zip(sums, starts, saves):
-        for j, half in enumerate((1 - side, side)):
-            part = pl.ds(pl.multiple_of((start * 2 + half) * eighth, eighth), eighth)
-            lines = slice(j * eighth, (j + 1) * eighth)
-            out[lines, : 3 * width] = mm(normed_t[part, :], d_qkv[...])
-            out[lines, 3 * width : 4 * width] = mm(attn_ref[part, :], serial_grad[...])
-            out[lines, 4 * width :] = gain_column[part, :]
-        save.start()
+    order = [
+        pl.ds(pl.multiple_of((start * 2 + half) * eighth, eighth), eighth)
+        for start, side in starts
+        for half in (1 - side, side)
+    ]
+    for i in (0, 2):
+        parts = order[2 * i : 2 * i + 4]
+        of_qkv = mm(jnp.concatenate([normed_ref[part, :] for part in parts], axis=0), d_qkv[...])
+        of_proj = mm(jnp.concatenate([attn_ref[part, :] for part in parts], axis=0), serial_grad[...])
+        of_gain = jnp.concatenate([gain_column[part, :] for part in parts], axis=0)
+        for j in range(2):
+            lines = slice(2 * j * eighth, 2 * (j + 1) * eighth)
+            sums[i + j][:, : 3 * width] = of_qkv[lines]
+            sums[i + j][:, 3 * width : 4 * width] = of_proj[lines]
+            sums[i + j][:, 4 * width :] = of_gain[lines]
+            saves[i + j].start()
     for save in saves:
         save.wait()
 
@@ -659,7 +666,6 @@
             pltpu.VMEM((rows, width), BF16),
             pltpu.VMEM((width, rows), BF16),
             pltpu.VMEM((rows, 3 * width), BF16),
-            pltpu.VMEM((width, rows), BF16),
             pltpu.VMEM((width, LANES), F32),
             pltpu.SemaphoreType.DMA((13,)),
         ],

time: 133 us -> 132 us (level)
  Pallas kernels: 40.7 us -> 39 us
    pallas_call x1, Pallas kernels: 17.2 us -> 15.6 us  [per_device(): pl.pallas_call(functools.partial(backward_kernel, n_seq, chip_bits), grid...]
where the time goes in v12:
time: 132 us; the launch traced here: 131 us
  waiting for transfers between devices  57.6 us (44%)
  Pallas kernels  39 us (30%)
  starting transfers between devices  29 us (22%)
  local copies, waits for them, and re-layouts  4.39 us (3%)
    ppermute x13, waiting for transfers between devices, by_distance(): lax.ppermute(blocks[k], axis, [(i, i ^ k) for i in range(count)])  18.5 us
    ppermute x13, starting transfers between devices, by_distance(): lax.ppermute(blocks[k], axis, [(i, i ^ k) for i in range(count)])  18.1 us
    pallas_call x1, Pallas kernels, per_device(): pl.pallas_call(functools.partial(backward_kernel, n_seq, chip_bits), grid...  15.6 us
    ppermute x2, waiting for transfers between devices, share_in_plane(): other = lax.ppermute(part, 'seq', pairs)  13.4 us
    pallas_call x1, Pallas kernels, per_device(): pl.pallas_call(functools.partial(forward_kernel, n_seq, capacity), grid=(...  9.88 us
    all_to_all x2, waiting for transfers between devices, exchange(): got = lax.all_to_all(sent, 'seq', split_axis=0, concat_axis=0, tiled=True)  9.8 us
    ppermute x1, waiting for transfers between devices, first_step(): return [own_keep, got_keep, lax.ppermute(sent, 'seq', steps[0][0])]  8.99 us
    all_to_all x2, starting transfers between devices, exchange(): got = lax.all_to_all(sent, 'seq', split_axis=0, concat_axis=0, tiled=True)  8.3 us
  transfers between devices with their start and end apart: 22, of which 15 were waited for; matrix products, arithmetic and copies ran while one was open for 0% of the time, Pallas kernels for 14%

profile of v12, /device:TPU:0, one launch (start us, length us, event | category | flops | bytes accessed | tf_op | source)
XLA Modules:
  0.0 131.3 jit_solution(5512431737717710106)
XLA Ops:
  0.6 3.0 %pack.1 = (s32[1,512]{1,0:T(1,128)}, bf16[144,512]{1,0:T(8,128)(2,1)}, bf16[144,512]{1,0:T(8,128)(2,1)}, bf16[144,512]{1,0:T(8,128)(2,1)}, bf16[144,512]{1,0:T(8...) custom-call(s32[1]{0:T(128)} %bitcast.1.me_ref, ...), custom_call_target="tpu_custom_call" | custom-call | flops 536870912 | bytes 2097152 | tf_op jit(solution)/shard_map/pack/pallas_call | solution.py:566
  3.7 0.5 collective-permute-start
  4.2 2.6 %collective-permute-start.1 = (bf16[144,512]{1,0:T(8,128)(2,1)}, bf16[144,512]{1,0:T(8,128)(2,1)S(1)}, u32[]{:S(2)}, u32[]{:S(2)}) collective-permute-start(bf16[144,512]{1,0:T(8,128)(2,1)} %get-tuple-element.58), channel_id=1, source_target_pairs={{0,8},{4,12},{8,0},{12,4},{16,24},{20,28},{24,16},{28,20},{1,9},{5... | collective-permute-start | bytes 442376 | tf_op jit(solution)/shard_map/ppermute | solution.py:402
  6.8 1.8 %collective-permute-start.3 = (bf16[144,512]{1,0:T(8,128)(2,1)}, bf16[144,512]{1,0:T(8,128)(2,1)S(1)}, u32[]{:S(2)}, u32[]{:S(2)}) collective-permute-start(bf16[144,512]{1,0:T(8,128)(2,1)} %get-tuple-element.60), channel_id=1, source_target_pairs={{0,16},{4,20},{8,24},{12,28},{16,0},{20,4},{24,8},{28,12},{1,17},{... | collective-permute-start | bytes 442376 | tf_op jit(solution)/shard_map/ppermute | solution.py:402
  8.6 2.6 %collective-permute-start.5 = (bf16[144,512]{1,0:T(8,128)(2,1)}, bf16[144,512]{1,0:T(8,128)(2,1)S(1)}, u32[]{:S(2)}, u32[]{:S(2)}) collective-permute-start(bf16[144,512]{1,0:T(8,128)(2,1)} %get-tuple-element.62), channel_id=1, source_target_pairs={{0,24},{4,28},{8,16},{12,20},{16,8},{20,12},{24,0},{28,4},{1,25},{... | collective-permute-start | bytes 442376 | tf_op jit(solution)/shard_map/ppermute | solution.py:402
  11.2 0.5 collective-permute-done.1.refs_2_
  11.7 1.7 %collective-permute-start.6 = (bf16[144,512]{1,0:T(8,128)(2,1)}, bf16[144,512]{1,0:T(8,128)(2,1)S(1)}, u32[]{:S(2)}, u32[]{:S(2)}) collective-permute-start(bf16[144,512]{1,0:T(8,128)(2,1)} %get-tuple-element.63), channel_id=1, source_target_pairs={{0,28},{4,24},{8,20},{12,16},{16,12},{20,8},{24,4},{28,0},{1,29},{... | collective-permute-start | bytes 442376 | tf_op jit(solution)/shard_map/ppermute | solution.py:402
  13.4 0.7 copy-done.9
  14.1 1.7 %pack_grads.1 = bf16[1024,512]{1,0:T(8,128)(2,1)} custom-call(s32[1]{0:T(128)} %bitcast.1.me_ref, s32[1,512]{1,0:T(1,128)S(1)} %copy-done.9, bf16[512,512]{1,0:T(8,128)(2,1)S(1)} %bitcast.30), custom_call_target="tpu_custom_call" | custom-call | flops 536870912 | bytes 2097152 | tf_op jit(solution)/shard_map/pack_grads/pallas_call | solution.py:584
  15.8 6.2 %collective-permute-done.4.refs_5_ = bf16[144,512]{1,0:T(8,128)(2,1)S(1)} collective-permute-done((bf16[144,512]{1,0:T(8,128)(2,1)}, bf16[144,512]{1,0:T(8,128)(2,1)S(1)}, u32[]{:S(2)}, u32[]{:S(2)}) %collective-permute-start.4) | collective-permute-done | bytes 147488 | tf_op jit(solution)/shard_map/ppermute | solution.py:402
  22.0 4.0 %all-to-all-start = ((bf16[8,128,512]{2,1,0:T(8,128)(2,1)}), bf16[8,128,512]{2,1,0:T(8,128)(2,1)S(1)}, u32[]{:S(2)}, u32[]{:S(2)}) async-start(bf16[8,128,512]{2,1,0:T(8,128)(2,1)} %bitcast.5), calls=%async_computation | async-start | bytes 2097152 | tf_op jit(solution)/shard_map/all_to_all | solution.py:598
  26.1 9.9 %forward.1 = (s32[1,1024]{1,0:T(1,128)}, f32[512,512]{1,0:T(8,128)}, f32[512,128]{1,0:T(8,128)}, bf16[512,512]{1,0:T(8,128)(2,1)}, bf16[512,1536]{1,0:T(8,128)(2...) custom-call(bf16[512,1536]{1,0:T(8,128)(2,1)} %refs_3_.1, f32[1,512]{1,0:T(1,128)} %bitcast.28, ...), custom_call_target="tpu_custom_call" | custom-call | flops 2952790016 | bytes 16777216 | tf_op jit(solution)/shard_map/forward/pallas_call | solution.py:604
  36.0 5.5 %all-to-all-done = bf16[8,128,512]{2,1,0:T(8,128)(2,1)S(1)} async-done(((bf16[8,128,512]{2,1,0:T(8,128)(2,1)}), bf16[8,128,512]{2,1,0:T(8,128)(2,1)S(1)}, u32[]{:S(2)}, u32[]{:S(2)}) %all-to-all-start) | async-done | bytes 1048608 | tf_op jit(solution)/shard_map/all_to_all | solution.py:598
  41.5 1.0 copy-done.11
  42.5 15.6 %backward.1 = (f32[128,2176]{1,0:T(8,128)}, f32[128,2176]{1,0:T(8,128)}, f32[128,2176]{1,0:T(8,128)}, f32[128,2176]{1,0:T(8,128)}, bf16[512,512]{1,0:T(8,128)(2,1)}, /*index=5*/f32[512,512]{1,0:T(8,128)}) custom-call(s32[1]{0:T(128)} %bitcast.1.me_ref, s32[1,1024]{1,0:T(1,128)} %get-tuple-element.73.pos_ref, bf16[512,512]{1,0:T(8,128)(2,1)} %w_proj_ref.1, ...), custom_call_target="tpu_custom_call" | custom-call | flops 4294967296 | bytes 16777216 | tf_op jit(solution)/shard_map/backward/pallas_call | solution.py:640
  58.1 0.5 collective-permute-start.7
  58.6 2.5 %collective-permute-done.8.refs_1_ = f32[128,2176]{1,0:T(8,128)S(1)} collective-permute-done((f32[128,2176]{1,0:T(8,128)}, f32[128,2176]{1,0:T(8,128)S(1)}, u32[]{:S(2)}, u32[]{:S(2)}) %collective-permute-start.8) | collective-permute-done | bytes 1114144 | tf_op jit(solution)/shard_map/ppermute | solution.py:461
  61.1 1.2 copy-done.1
  62.3 0.3 code_first.1
  62.7 0.6 collective-permute-start.9
  63.3 9.0 %collective-permute-done.9.refs_2_ = s16[128,2176]{1,0:T(8,128)(2,1)S(1)} collective-permute-done((s16[128,2176]{1,0:T(8,128)(2,1)S(1)}, s16[128,2176]{1,0:T(8,128)(2,1)S(1)}, u32[]{:S(2)}, u32[]{:S(2)}) %collective-permute-start.9) | collective-permute-done | bytes 557088 | tf_op jit(solution)/shard_map/ppermute | solution.py:464
  72.3 0.3 code_second.1
  72.6 0.6 collective-permute-start.10
  73.2 0.3 copy-done.2
  73.5 0.3 copy-done.3
  74.0 2.1 %residual.1 = bf16[1024,512]{1,0:T(8,128)(2,1)} custom-call(s32[1]{0:T(128)} %bitcast.1.me_ref, s32[1,1024]{1,0:T(1,128)S(1)} %copy-done.6, f32[1,512]{1,0:T(1,128)S(1)} %bitcast.29, f32[512,128]{1,0:T(8,128)S(1)} %copy-done.5, f32[512,512]{1,0:T(8,128)S(1)} %copy-done.2, bf16[512,512]{1,0:T(8,128)(2,1)S(1)} %copy-done.4, f32[512,512]{1,0:T(8,128)S(1)} %copy-done.3), custom_call_target="tpu_custom_call" | custom-call | flops 536870912 | bytes 4194304 | tf_op jit(solution)/shard_map/residual/pallas_call | solution.py:683
  76.1 3.1 %collective-permute-done.10.refs_3_ = s16[64,2176]{1,0:T(8,128)(2,1)S(1)} collective-permute-done((s16[64,2176]{1,0:T(8,128)(2,1)S(1)}, s16[64,2176]{1,0:T(8,128)(2,1)S(1)}, u32[]{:S(2)}, u32[]{:S(2)}) %collective-permute-start.10) | collective-permute-done | bytes 278560 | tf_op jit(solution)/shard_map/ppermute | solution.py:469
  79.2 4.2 %all-to-all-start.1 = ((bf16[8,128,512]{2,1,0:T(8,128)(2,1)}), bf16[8,128,512]{2,1,0:T(8,128)(2,1)}, u32[]{:S(2)}, u32[]{:S(2)}) async-start(bf16[8,128,512]{2,1,0:T(8,128)(2,1)} %bitcast.7), calls=%async_computation.1 | async-start | bytes 2097152 | tf_op jit(solution)/shard_map/all_to_all | solution.py:598
  83.5 0.5 code_planes.1
  84.0 1.7 %collective-permute-start.11 = (s16[16,2176]{1,0:T(8,128)(2,1)S(1)}, s16[16,2176]{1,0:T(8,128)(2,1)S(1)}, u32[]{:S(2)}, u32[]{:S(2)}) collective-permute-start(s16[16,2176]{1,0:T(8,128)(2,1)S(1)} %get-tuple-element.90), channel_id=1, source_target_pairs={{0,1},{1,0},{2,3},{3,2},{4,5},{5,4},{6,7},{7,6},{8,9},{9,8},{10,11... | collective-permute-start | bytes 208904 | tf_op jit(solution)/shard_map/ppermute | solution.py:402
  85.6 2.6 %collective-permute-start.12 = (s16[16,2176]{1,0:T(8,128)(2,1)S(1)}, s16[16,2176]{1,0:T(8,128)(2,1)S(1)}, u32[]{:S(2)}, u32[]{:S(2)}) collective-permute-start(s16[16,2176]{1,0:T(8,128)(2,1)S(1)} %get-tuple-element.91), channel_id=1, source_target_pairs={{0,2},{1,3},{2,0},{3,1},{4,6},{5,7},{6,4},{7,5},{8,10},{9,11},{10,... | collective-permute-start | bytes 208904 | tf_op jit(solution)/shard_map/ppermute | solution.py:402
  88.5 5.1 %collective-permute-done.12.refs_2_ = s16[16,2176]{1,0:T(8,128)(2,1)S(1)} collective-permute-done((s16[16,2176]{1,0:T(8,128)(2,1)S(1)}, s16[16,2176]{1,0:T(8,128)(2,1)S(1)}, u32[]{:S(2)}, u32[]{:S(2)}) %collective-permute-start.12) | collective-permute-done | bytes 69664 | tf_op jit(solution)/shard_map/ppermute | solution.py:402
  93.5 0.8 collective-permute-done.13.refs_3_
  94.5 4.3 %all-to-all-done.1 = bf16[8,128,512]{2,1,0:T(8,128)(2,1)} async-done(((bf16[8,128,512]{2,1,0:T(8,128)(2,1)}), bf16[8,128,512]{2,1,0:T(8,128)(2,1)}, u32[]{:S(2)}, u32[]{:S(2)}) %all-to-all-start.1) | async-done | bytes 1048608 | tf_op jit(solution)/shard_map/all_to_all | solution.py:598
  98.9 1.6 %collective-permute-start.14 = (bf16[16,2176]{1,0:T(8,128)(2,1)S(1)}, bf16[16,2176]{1,0:T(8,128)(2,1)S(1)}, u32[]{:S(2)}, u32[]{:S(2)}) collective-permute-start(bf16[16,2176]{1,0:T(8,128)(2,1)S(1)} %finish.1), channel_id=1, source_target_pairs={{0,1},{1,0},{2,3},{3,2},{4,5},{5,4},{6,7},{7,6},{8,9},{9,8},{10,11... | collective-permute-start | bytes 208904 | tf_op jit(solution)/shard_map/ppermute | solution.py:402
  100.5 2.6 %collective-permute-start.15 = (bf16[16,2176]{1,0:T(8,128)(2,1)S(1)}, bf16[16,2176]{1,0:T(8,128)(2,1)S(1)}, u32[]{:S(2)}, u32[]{:S(2)}) collective-permute-start(bf16[16,2176]{1,0:T(8,128)(2,1)S(1)} %finish.1), channel_id=1, source_target_pairs={{0,2},{1,3},{2,0},{3,1},{4,6},{5,7},{6,4},{7,5},{8,10},{9,11},{10,... | collective-permute-start | bytes 208904 | tf_op jit(solution)/shard_map/ppermute | solution.py:402
  103.1 0.2 collective-permute-start.16
  103.3 3.1 %collective-permute-done.15 = bf16[16,2176]{1,0:T(8,128)(2,1)S(1)} collective-permute-done((bf16[16,2176]{1,0:T(8,128)(2,1)S(1)}, bf16[16,2176]{1,0:T(8,128)(2,1)S(1)}, u32[]{:S(2)}, u32[]{:S(2)}) %collective-permute-start.15) | collective-permute-done | bytes 69664 | tf_op jit(solution)/shard_map/ppermute | solution.py:402
  106.4 2.8 %collective-permute-done.16 = bf16[16,2176]{1,0:T(8,128)(2,1)S(1)} collective-permute-done((bf16[16,2176]{1,0:T(8,128)(2,1)S(1)}, bf16[16,2176]{1,0:T(8,128)(2,1)S(1)}, u32[]{:S(2)}, u32[]{:S(2)}) %collective-permute-start.16) | collective-permute-done | bytes 69664 | tf_op jit(solution)/shard_map/ppermute | solution.py:402
  109.4 0.6 collective-permute-start.17
  110.0 7.1 %collective-permute-done.17 = bf16[64,2176]{1,0:T(8,128)(2,1)S(1)} collective-permute-done((bf16[64,2176]{1,0:T(8,128)(2,1)S(1)}, bf16[64,2176]{1,0:T(8,128)(2,1)S(1)}, u32[]{:S(2)}, u32[]{:S(2)}) %collective-permute-start.17) | collective-permute-done | bytes 278560 | tf_op jit(solution)/shard_map/ppermute | solution.py:514
  117.4 0.4 copy-done.10
  117.8 2.8 %unpack.1 = bf16[512,512]{1,0:T(8,128)(2,1)} custom-call(s32[1]{0:T(128)} %bitcast.1.me_ref, s32[1,512]{1,0:T(1,128)S(1)} %copy-done.10, bf16[1024,512]{1,0:T(8,128)(2,1)} %bitcast.8.recv_ref), custom_call_target="tpu_custom_call" | custom-call | flops 536870912 | bytes 2097152 | tf_op jit(solution)/shard_map/unpack/pallas_call | solution.py:699
  120.6 6.3 %collective-permute-done.18 = bf16[128,2176]{1,0:T(8,128)(2,1)S(1)} collective-permute-done((bf16[128,2176]{1,0:T(8,128)(2,1)S(1)}, bf16[128,2176]{1,0:T(8,128)(2,1)S(1)}, u32[]{:S(2)}, u32[]{:S(2)}) %collective-permute-start.18) | collective-permute-done | bytes 557088 | tf_op jit(solution)/shard_map/ppermute | solution.py:514
  126.9 0.2 maximum_select_fusion.sums_ref
  127.2 1.4 %split.2 = (f32[512,1536]{1,0:T(8,128)}, f32[512,512]{1,0:T(8,128)}, f32[1,512]{1,0:T(1,128)}) custom-call(s32[1]{0:T(128)S(6)} %and.19.side_ref, bf16[256,2176]{1,0:T(8,128)(2,1)S(1)} %maximum_select_fusion.sums_ref), custom_call_target="tpu_custom_call" | custom-call | bytes 4194304 | tf_op jit(solution)/shard_map/split/pallas_call | solution.py:523
  128.6 1.3 %collective-permute-done.19.sums_ref = bf16[256,2176]{1,0:T(8,128)(2,1)S(1)} collective-permute-done((bf16[256,2176]{1,0:T(8,128)(2,1)S(1)}, bf16[256,2176]{1,0:T(8,128)(2,1)S(1)}, u32[]{:S(2)}, u32[]{:S(2)}) %collective-permute-start.19) | collective-permute-done | bytes 1114144 | tf_op jit(solution)/shard_map/ppermute | solution.py:711
  129.9 1.3 %split.3 = (f32[512,1536]{1,0:T(8,128)}, f32[512,512]{1,0:T(8,128)}, f32[1,512]{1,0:T(1,128)}) custom-call(s32[1]{0:T(128)S(6)} %sub.3.side_ref, bf16[256,2176]{1,0:T(8,128)(2,1)S(1)} %collective-permute-done.19.sums_ref, f32[512,1536]{1,0:T(8,128)} %get-tuple-element.98.refs_0_, ...), custom_call_target="tpu_custom_call", output_to_operand_aliasing={{0}: (2, {}), {1}: (3, {}), {2}: (4, {})} | custom-call | bytes 4194304 | tf_op jit(solution)/shard_map/split/pallas_call | solution.py:523
  (59 shorter events, 1.3 us)
Async XLA Ops:
  0.6 12.8 %copy-start.8 = (bf16[1,512,512]{2,1,0:T(8,128)(2,1)S(1)}, bf16[1,512,512]{2,1,0:T(8,128)(2,1)}, u32[]{:S(2)}) copy-start(bf16[1,512,512]{2,1,0:T(8,128)(2,1)} %param.7) | copy-start | bytes 1572868
  3.7 4.9 %collective-permute-start = (bf16[144,512]{1,0:T(8,128)(2,1)}, bf16[144,512]{1,0:T(8,128)(2,1)S(1)}, u32[]{:S(2)}, u32[]{:S(2)}) collective-permute-start(bf16[144,512]{1,0:T(8,128)(2,1)} %get-tuple-element.55), channel_id=1, source_target_pairs={{0,4},{4,0},{8,12},{12,8},{16,20},{20,16},{24,28},{28,24},{1,5},{5... | collective-permute-start | bytes 442376 | tf_op jit(solution)/shard_map/ppermute | solution.py:402
  4.2 7.5 %collective-permute-start.1 = (bf16[144,512]{1,0:T(8,128)(2,1)}, bf16[144,512]{1,0:T(8,128)(2,1)S(1)}, u32[]{:S(2)}, u32[]{:S(2)}) collective-permute-start(bf16[144,512]{1,0:T(8,128)(2,1)} %get-tuple-element.58), channel_id=1, source_target_pairs={{0,8},{4,12},{8,0},{12,4},{16,24},{20,28},{24,16},{28,20},{1,9},{5... | collective-permute-start | bytes 442376 | tf_op jit(solution)/shard_map/ppermute | solution.py:402
  6.8 9.0 %collective-permute-start.2 = (bf16[144,512]{1,0:T(8,128)(2,1)}, bf16[144,512]{1,0:T(8,128)(2,1)S(1)}, u32[]{:S(2)}, u32[]{:S(2)}) collective-permute-start(bf16[144,512]{1,0:T(8,128)(2,1)} %get-tuple-element.59), channel_id=1, source_target_pairs={{0,12},{4,8},{8,4},{12,0},{16,28},{20,24},{24,20},{28,16},{1,13},{... | collective-permute-start | bytes 442376 | tf_op jit(solution)/shard_map/ppermute | solution.py:402
  6.8 9.0 %collective-permute-start.3 = (bf16[144,512]{1,0:T(8,128)(2,1)}, bf16[144,512]{1,0:T(8,128)(2,1)S(1)}, u32[]{:S(2)}, u32[]{:S(2)}) collective-permute-start(bf16[144,512]{1,0:T(8,128)(2,1)} %get-tuple-element.60), channel_id=1, source_target_pairs={{0,16},{4,20},{8,24},{12,28},{16,0},{20,4},{24,8},{28,12},{1,17},{... | collective-permute-start | bytes 442376 | tf_op jit(solution)/shard_map/ppermute | solution.py:402
  8.6 13.4 %collective-permute-start.4 = (bf16[144,512]{1,0:T(8,128)(2,1)}, bf16[144,512]{1,0:T(8,128)(2,1)S(1)}, u32[]{:S(2)}, u32[]{:S(2)}) collective-permute-start(bf16[144,512]{1,0:T(8,128)(2,1)} %get-tuple-element.61), channel_id=1, source_target_pairs={{0,20},{4,16},{8,28},{12,24},{16,4},{20,0},{24,12},{28,8},{1,21},{... | collective-permute-start | bytes 442376 | tf_op jit(solution)/shard_map/ppermute | solution.py:402
  8.6 13.4 %copy-start.12 = (bf16[144,512]{1,0:T(8,128)(2,1)}, bf16[144,512]{1,0:T(8,128)(2,1)S(1)}, u32[]{:S(2)}) copy-start(bf16[144,512]{1,0:T(8,128)(2,1)S(1)} %collective-permute-done.refs_1_) | copy-start | bytes 442372
  8.6 13.4 %collective-permute-start.5 = (bf16[144,512]{1,0:T(8,128)(2,1)}, bf16[144,512]{1,0:T(8,128)(2,1)S(1)}, u32[]{:S(2)}, u32[]{:S(2)}) collective-permute-start(bf16[144,512]{1,0:T(8,128)(2,1)} %get-tuple-element.62), channel_id=1, source_target_pairs={{0,24},{4,28},{8,16},{12,20},{16,8},{20,12},{24,0},{28,4},{1,25},{... | collective-permute-start | bytes 442376 | tf_op jit(solution)/shard_map/ppermute | solution.py:402
  11.7 10.4 %copy-start.13 = (bf16[144,512]{1,0:T(8,128)(2,1)}, bf16[144,512]{1,0:T(8,128)(2,1)S(1)}, u32[]{:S(2)}) copy-start(bf16[144,512]{1,0:T(8,128)(2,1)S(1)} %collective-permute-done.1.refs_2_) | copy-start | bytes 442372
  11.7 10.3 %collective-permute-start.6 = (bf16[144,512]{1,0:T(8,128)(2,1)}, bf16[144,512]{1,0:T(8,128)(2,1)S(1)}, u32[]{:S(2)}, u32[]{:S(2)}) collective-permute-start(bf16[144,512]{1,0:T(8,128)(2,1)} %get-tuple-element.63), channel_id=1, source_target_pairs={{0,28},{4,24},{8,20},{12,16},{16,12},{20,8},{24,4},{28,0},{1,29},{... | collective-permute-start | bytes 442376 | tf_op jit(solution)/shard_map/ppermute | solution.py:402
  13.4 0.7 copy-start.9
  15.8 10.3 %copy-start.14 = (bf16[144,512]{1,0:T(8,128)(2,1)}, bf16[144,512]{1,0:T(8,128)(2,1)S(1)}, u32[]{:S(2)}) copy-start(bf16[144,512]{1,0:T(8,128)(2,1)S(1)} %collective-permute-done.2.refs_3_) | copy-start | bytes 442372
  15.8 10.3 %copy-start.15 = (bf16[144,512]{1,0:T(8,128)(2,1)}, bf16[144,512]{1,0:T(8,128)(2,1)S(1)}, u32[]{:S(2)}) copy-start(bf16[144,512]{1,0:T(8,128)(2,1)S(1)} %collective-permute-done.3.refs_4_) | copy-start | bytes 442372
  22.0 4.1 %copy-start.16 = (bf16[144,512]{1,0:T(8,128)(2,1)}, bf16[144,512]{1,0:T(8,128)(2,1)S(1)}, u32[]{:S(2)}) copy-start(bf16[144,512]{1,0:T(8,128)(2,1)S(1)} %collective-permute-done.4.refs_5_) | copy-start | bytes 442372
  22.0 4.1 %copy-start.17 = (bf16[144,512]{1,0:T(8,128)(2,1)}, bf16[144,512]{1,0:T(8,128)(2,1)S(1)}, u32[]{:S(2)}) copy-start(bf16[144,512]{1,0:T(8,128)(2,1)S(1)} %collective-permute-done.5.refs_6_) | copy-start | bytes 442372
  22.0 4.1 %copy-start.18 = (bf16[144,512]{1,0:T(8,128)(2,1)}, bf16[144,512]{1,0:T(8,128)(2,1)S(1)}, u32[]{:S(2)}) copy-start(bf16[144,512]{1,0:T(8,128)(2,1)S(1)} %collective-permute-done.6.refs_7_) | copy-start | bytes 442372
  22.0 19.5 %all-to-all-start = ((bf16[8,128,512]{2,1,0:T(8,128)(2,1)}), bf16[8,128,512]{2,1,0:T(8,128)(2,1)S(1)}, u32[]{:S(2)}, u32[]{:S(2)}) async-start(bf16[8,128,512]{2,1,0:T(8,128)(2,1)} %bitcast.5), calls=%async_computation | async-start | bytes 2097152 | tf_op jit(solution)/shard_map/all_to_all | solution.py:598
  41.5 1.0 copy-start.11
  58.1 3.0 %collective-permute-start.8 = (f32[128,2176]{1,0:T(8,128)}, f32[128,2176]{1,0:T(8,128)S(1)}, u32[]{:S(2)}, u32[]{:S(2)}) collective-permute-start(f32[128,2176]{1,0:T(8,128)} %get-tuple-element.84), channel_id=1, source_target_pairs={{0,4},{4,0},{8,12},{12,8},{16,20},{20,16},{24,28},{28,24},{1,5},{5... | collective-permute-start | bytes 3342344 | tf_op jit(solution)/shard_map/ppermute | solution.py:461
  58.1 5.1 %collective-permute-start.7 = (f32[128,2176]{1,0:T(8,128)}, f32[128,2176]{1,0:T(8,128)S(1)}, u32[]{:S(2)}, u32[]{:S(2)}) collective-permute-start(f32[128,2176]{1,0:T(8,128)} %get-tuple-element.82), channel_id=1, source_target_pairs={{0,4},{4,0},{8,12},{12,8},{16,20},{20,16},{24,28},{28,24},{1,5},{5... | collective-permute-start | bytes 3342344 | tf_op jit(solution)/shard_map/ppermute | solution.py:462
  61.1 1.2 copy-start.1
  62.3 9.9 %copy-start = (f32[128,2176]{1,0:T(8,128)S(1)}, f32[128,2176]{1,0:T(8,128)}, u32[]{:S(2)}) copy-start(f32[128,2176]{1,0:T(8,128)} %get-tuple-element.81.refs_0_) | copy-start | bytes 3342340
  62.7 9.6 %collective-permute-start.9 = (s16[128,2176]{1,0:T(8,128)(2,1)S(1)}, s16[128,2176]{1,0:T(8,128)(2,1)S(1)}, u32[]{:S(2)}, u32[]{:S(2)}) collective-permute-start(s16[128,2176]{1,0:T(8,128)(2,1)S(1)} %code_first.1), channel_id=1, source_target_pairs={{0,8},{4,20},{8,0},{12,28},{16,24},{20,4},{24,16},{28,12},{1,9},{5... | collective-permute-start | bytes 1671176 | tf_op jit(solution)/shard_map/ppermute | solution.py:464
  72.3 1.2 copy-start.2
  72.3 1.5 %copy-start.3 = (f32[512,512]{1,0:T(8,128)S(1)}, f32[512,512]{1,0:T(8,128)}, u32[]{:S(2)}) copy-start(f32[512,512]{1,0:T(8,128)} %get-tuple-element.87.d_normed_ref) | copy-start | bytes 3145732
  72.3 1.7 %copy-start.4 = (bf16[512,512]{1,0:T(8,128)(2,1)S(1)}, bf16[512,512]{1,0:T(8,128)(2,1)}, u32[]{:S(2)}) copy-start(bf16[512,512]{1,0:T(8,128)(2,1)} %get-tuple-element.86.serial_grad_ref) | copy-start | bytes 1572868
  72.3 1.7 %copy-start.5 = (f32[512,128]{1,0:T(8,128)S(1)}, f32[512,128]{1,0:T(8,128)}, u32[]{:S(2)}) copy-start(f32[512,128]{1,0:T(8,128)} %get-tuple-element.85.inv_ref) | copy-start | bytes 786436
  72.3 1.7 %copy-start.6 = (s32[1,1024]{1,0:T(1,128)S(1)}, s32[1,1024]{1,0:T(1,128)}, u32[]{:S(2)}) copy-start(s32[1,1024]{1,0:T(1,128)} %get-tuple-element.73.pos_ref) | copy-start | bytes 12292
  72.3 1.7 %copy-start.7 = (f32[512]{0:T(512)S(1)}, f32[512]{0:T(512)}, u32[]{:S(2)}) copy-start(f32[512]{0:T(512)} %param.11) | copy-start | bytes 6148
  72.6 6.6 %collective-permute-start.10 = (s16[64,2176]{1,0:T(8,128)(2,1)S(1)}, s16[64,2176]{1,0:T(8,128)(2,1)S(1)}, u32[]{:S(2)}, u32[]{:S(2)}) collective-permute-start(s16[64,2176]{1,0:T(8,128)(2,1)S(1)} %code_second.1), channel_id=1, source_target_pairs={{0,16},{4,12},{8,24},{12,4},{16,0},{20,28},{24,8},{28,20},{1,17},{... | collective-permute-start | bytes 835592 | tf_op jit(solution)/shard_map/ppermute | solution.py:469
  79.2 19.7 %all-to-all-start.1 = ((bf16[8,128,512]{2,1,0:T(8,128)(2,1)}), bf16[8,128,512]{2,1,0:T(8,128)(2,1)}, u32[]{:S(2)}, u32[]{:S(2)}) async-start(bf16[8,128,512]{2,1,0:T(8,128)(2,1)} %bitcast.7), calls=%async_computation.1 | async-start | bytes 2097152 | tf_op jit(solution)/shard_map/all_to_all | solution.py:598
  84.0 4.5 %collective-permute-start.11 = (s16[16,2176]{1,0:T(8,128)(2,1)S(1)}, s16[16,2176]{1,0:T(8,128)(2,1)S(1)}, u32[]{:S(2)}, u32[]{:S(2)}) collective-permute-start(s16[16,2176]{1,0:T(8,128)(2,1)S(1)} %get-tuple-element.90), channel_id=1, source_target_pairs={{0,1},{1,0},{2,3},{3,2},{4,5},{5,4},{6,7},{7,6},{8,9},{9,8},{10,11... | collective-permute-start | bytes 208904 | tf_op jit(solution)/shard_map/ppermute | solution.py:402
  85.6 7.9 %collective-permute-start.12 = (s16[16,2176]{1,0:T(8,128)(2,1)S(1)}, s16[16,2176]{1,0:T(8,128)(2,1)S(1)}, u32[]{:S(2)}, u32[]{:S(2)}) collective-permute-start(s16[16,2176]{1,0:T(8,128)(2,1)S(1)} %get-tuple-element.91), channel_id=1, source_target_pairs={{0,2},{1,3},{2,0},{3,1},{4,6},{5,7},{6,4},{7,5},{8,10},{9,11},{10,... | collective-permute-start | bytes 208904 | tf_op jit(solution)/shard_map/ppermute | solution.py:402
  88.2 6.2 %collective-permute-start.13 = (s16[16,2176]{1,0:T(8,128)(2,1)S(1)}, s16[16,2176]{1,0:T(8,128)(2,1)S(1)}, u32[]{:S(2)}, u32[]{:S(2)}) collective-permute-start(s16[16,2176]{1,0:T(8,128)(2,1)S(1)} %get-tuple-element.92), channel_id=1, source_target_pairs={{0,3},{1,2},{2,1},{3,0},{4,7},{5,6},{6,5},{7,4},{8,11},{9,10},{10,... | collective-permute-start | bytes 208904 | tf_op jit(solution)/shard_map/ppermute | solution.py:402
  98.9 4.4 %collective-permute-start.14 = (bf16[16,2176]{1,0:T(8,128)(2,1)S(1)}, bf16[16,2176]{1,0:T(8,128)(2,1)S(1)}, u32[]{:S(2)}, u32[]{:S(2)}) collective-permute-start(bf16[16,2176]{1,0:T(8,128)(2,1)S(1)} %finish.1), channel_id=1, source_target_pairs={{0,1},{1,0},{2,3},{3,2},{4,5},{5,4},{6,7},{7,6},{8,9},{9,8},{10,11... | collective-permute-start | bytes 208904 | tf_op jit(solution)/shard_map/ppermute | solution.py:402
  100.5 6.0 %collective-permute-start.15 = (bf16[16,2176]{1,0:T(8,128)(2,1)S(1)}, bf16[16,2176]{1,0:T(8,128)(2,1)S(1)}, u32[]{:S(2)}, u32[]{:S(2)}) collective-permute-start(bf16[16,2176]{1,0:T(8,128)(2,1)S(1)} %finish.1), channel_id=1, source_target_pairs={{0,2},{1,3},{2,0},{3,1},{4,6},{5,7},{6,4},{7,5},{8,10},{9,11},{10,... | collective-permute-start | bytes 208904 | tf_op jit(solution)/shard_map/ppermute | solution.py:402
  103.1 6.1 %collective-permute-start.16 = (bf16[16,2176]{1,0:T(8,128)(2,1)S(1)}, bf16[16,2176]{1,0:T(8,128)(2,1)S(1)}, u32[]{:S(2)}, u32[]{:S(2)}) collective-permute-start(bf16[16,2176]{1,0:T(8,128)(2,1)S(1)} %finish.1), channel_id=1, source_target_pairs={{0,3},{1,2},{2,1},{3,0},{4,7},{5,6},{6,5},{7,4},{8,11},{9,10},{10,... | collective-permute-start | bytes 208904 | tf_op jit(solution)/shard_map/ppermute | solution.py:402
  109.4 7.7 %collective-permute-start.17 = (bf16[64,2176]{1,0:T(8,128)(2,1)S(1)}, bf16[64,2176]{1,0:T(8,128)(2,1)S(1)}, u32[]{:S(2)}, u32[]{:S(2)}) collective-permute-start(bf16[64,2176]{1,0:T(8,128)(2,1)S(1)} %pad_maximum_fusion.1), channel_id=1, source_target_pairs={{0,16},{4,12},{8,24},{12,4},{16,0},{20,28},{24,8},{28,20},{1,17},{... | collective-permute-start | bytes 835592 | tf_op jit(solution)/shard_map/ppermute | solution.py:514
  117.1 0.7 copy-start.10
  117.3 9.6 %collective-permute-start.18 = (bf16[128,2176]{1,0:T(8,128)(2,1)S(1)}, bf16[128,2176]{1,0:T(8,128)(2,1)S(1)}, u32[]{:S(2)}, u32[]{:S(2)}) collective-permute-start(bf16[128,2176]{1,0:T(8,128)(2,1)S(1)} %broadcast_select_fusion), channel_id=1, source_target_pairs={{0,8},{4,20},{8,0},{12,28},{16,24},{20,4},{24,16},{28,12},{1,9},{5... | collective-permute-start | bytes 1671176 | tf_op jit(solution)/shard_map/ppermute | solution.py:514
  127.1 2.8 %collective-permute-start.19 = (bf16[256,2176]{1,0:T(8,128)(2,1)S(1)}, bf16[256,2176]{1,0:T(8,128)(2,1)S(1)}, u32[]{:S(2)}, u32[]{:S(2)}) collective-permute-start(bf16[256,2176]{1,0:T(8,128)(2,1)S(1)} %maximum_select_fusion.sums_ref), channel_id=1, source_target_pairs={{0,4},{4,0},{8,12},{12,8},{16,20},{20,16},{24,28},{28,24},{1,5},{5... | collective-permute-start | bytes 3342344 | tf_op jit(solution)/shard_map/ppermute | solution.py:711

commit v13 on v12

--- a/solution.py
+++ b/solution.py
@@ -43,13 +43,17 @@
     return pl.ds(pl.multiple_of(lax.bitwise_xor(me, distance) * capacity, capacity), capacity)
 
 
-def pack_kernel(n_seq, capacity, me_ref, dest_hbm, feats_hbm, slot_out, *refs):
-    outs, (dest_ref, feats_ref, sems) = refs[:n_seq], refs[n_seq:]
+def pack_kernel(
+    n_seq, capacity, me_ref, dest_hbm, feats_hbm, grads_hbm, slot_out, same_out, cross_out, *refs
+):
+    outs, (dest_ref, feats_ref, grads_ref, sems) = refs[:n_seq], refs[n_seq:]
     rows, width = feats_ref.shape
     slots = n_seq * capacity
     loads = [
         pltpu.make_async_copy(source, target, sems.at[i])
-        for i, (source, target) in enumerate(((dest_hbm, dest_ref), (feats_hbm, feats_ref)))
+        for i, (source, target) in enumerate(
+            ((dest_hbm, dest_ref), (feats_hbm, feats_ref), (grads_hbm, grads_ref))
+        )
     ]
     for load in loads:
         load.start()
@@ -84,13 +88,19 @@
     for d in range(n_seq):
         outs[d][:capacity, :] = feats[d * capacity : (d + 1) * capacity]
         outs[d][capacity:, :] = position[d * EXTRA : (d + 1) * EXTRA]
-
-
-def pack_grads_kernel(n_seq, capacity, me_ref, slot_ref, grads_ref, grads_out):
-    select = hot(iota((n_seq * capacity, grads_ref.shape[0]), 0) == slot_ref[...])
+    loads[2].wait()
     grads = mm(select, grads_ref[...]).astype(BF16)
-    for d in range(n_seq):
-        grads_out[by_receiver(me_ref[0], d, capacity), :] = grads[d * capacity : (d + 1) * capacity]
+    for j in range(n_seq // 2):
+        lines = slice(j * capacity, (j + 1) * capacity)
+        same_out[lines, :] = grads[2 * j * capacity : (2 * j + 1) * capacity]
+        cross_out[lines, :] = grads[(2 * j + 1) * capacity : (2 * j + 2) * capacity]
+
+
+def pair_kernel(capacity, same_ref, cross_ref, *outs):
+    for j, out in enumerate(outs):
+        lines = slice(j * capacity, (j + 1) * capacity)
+        out[:capacity, :] = same_ref[lines, :]
+        out[capacity:, :] = cross_ref[lines, :]
 
 
 def forward_kernel(n_seq, capacity, w_hbm, gain_ref, *refs):
@@ -164,7 +174,8 @@
 
 
 def backward_kernel(n_seq, chip_bits, me_ref, pos_ref, w_proj_ref, stats_ref, *refs):
-    (recv_hbm, qkv_hbm, trans_hbm, w_hbm, xhat_hbm, normed_hbm, attn_hbm), refs = refs[:7], refs[7:]
+    (qkv_hbm, trans_hbm, w_hbm, xhat_hbm, normed_hbm, attn_hbm), refs = refs[:6], refs[6:]
+    recv_hbm, refs = refs[: n_seq // 2], refs[n_seq // 2 :]
     outs, serial_grad_hbm, d_normed_hbm, refs = refs[:4], refs[4], refs[5], refs[6:]
     recv_ref, qkv_ref, trans_ref, w_ref, xhat_ref, normed_ref, attn_ref, refs = *refs[:7], refs[7:]
     sums, refs = refs[:4], refs[4:]
@@ -175,11 +186,13 @@
     head = width // HEADS
     pair = 2 * head
     me = me_ref[0]
+    chips = n_seq // 2
+    recv_parts = [recv_ref.at[pl.ds(2 * j * capacity, 2 * capacity)] for j in range(chips)]
     loads = [
         pltpu.make_async_copy(source, target, sems.at[i])
         for i, (source, target) in enumerate(
             (
-                (recv_hbm, recv_ref),
+                *zip(recv_hbm, recv_parts),
                 (qkv_hbm, qkv_ref),
                 (trans_hbm, trans_ref),
                 (normed_hbm, normed_ref),
@@ -190,7 +203,7 @@
         )
     ]
     saves = [
-        pltpu.make_async_copy(source, target, sems.at[7 + i])
+        pltpu.make_async_copy(source, target, sems.at[6 + chips + i])
         for i, (source, target) in enumerate(
             [*zip(sums, outs), (serial_grad, serial_grad_hbm), (d_normed_ref, d_normed_hbm)]
         )
@@ -199,17 +212,15 @@
     for load in loads:
         load.start()
     place = hot(iota((rows, n_seq * capacity), 0) == pos_ref[...])
-    loads[0].wait()
-    values = jnp.concatenate(
-        [recv_ref[by_receiver(me, d, capacity), :] for d in range(n_seq)], axis=0
-    )
-    grads = mm(place, values).astype(BF16)
+    for load in loads[:chips]:
+        load.wait()
+    grads = mm(place, recv_ref[...]).astype(BF16)
     serial_grad[...] = grads
     saves[4].start()
     d_attn[...] = mm(grads, w_proj_ref[...], NT).astype(BF16)
     d_attn_t[...] = mm(w_proj_ref[...], grads, NT).astype(BF16)
-    loads[1].wait()
-    loads[2].wait()
+    for load in loads[chips : chips + 2]:
+        load.wait()
 
     zero = jnp.zeros((head, rows), BF16)
     first = iota((rows, pair), 1) < head
@@ -246,7 +257,7 @@
             first, d_v[0], d_v[1]
         ).astype(BF16)
 
-    for load in loads[3:]:
+    for load in loads[chips + 2 :]:
         load.wait()
     d_normed = mm(d_qkv[...], w_ref[...], NT)
     d_normed_ref[...] = d_normed
@@ -563,43 +574,42 @@
     in_hbm = pl.BlockSpec(memory_space=pl.ANY)
     stay_hbm = pl.BlockSpec(memory_space=pltpu.HBM)
 
-    slot, *feats_sent = pl.pallas_call(
+    slot, same, cross, *feats_sent = pl.pallas_call(
         functools.partial(pack_kernel, n_seq, capacity),
-        out_shape=[shape_of((1, rows), jnp.int32)] + [shape_of((block, width), BF16)] * n_seq,
-        in_specs=[in_smem] + [stay_hbm] * 2,
-        out_specs=[in_vmem] * (1 + n_seq),
+        out_shape=[shape_of((1, rows), jnp.int32)]
+        + [shape_of((slots // 2, width), BF16)] * 2
+        + [shape_of((block, width), BF16)] * n_seq,
+        in_specs=[in_smem] + [stay_hbm] * 3,
+        out_specs=[in_vmem] * (3 + n_seq),
         scratch_shapes=[
             pltpu.VMEM((1, rows), jnp.int32),
             pltpu.VMEM((rows, width), BF16),
-            pltpu.SemaphoreType.DMA((2,)),
+            pltpu.VMEM((rows, width), BF16),
+            pltpu.SemaphoreType.DMA((3,)),
         ],
         compiler_params=params(60),
         cost_estimate=pl.CostEstimate(
-            flops=2 * slots * rows * width, bytes_accessed=2 * MIB, transcendentals=0
+            flops=4 * slots * rows * width, bytes_accessed=4 * MIB, transcendentals=0
         ),
         name="pack",
-    )(me, dest, feats)
+    )(me, dest, feats, grads)
     feats_got = by_distance(feats_sent, "seq")
-    feats_got[1], slot = lax.optimization_barrier((feats_got[1], slot))
-    grads_sent = pl.pallas_call(
-        functools.partial(pack_grads_kernel, n_seq, capacity),
-        out_shape=shape_of((slots, width), BF16),
-        in_specs=[in_smem] + [in_vmem] * 2,
-        out_specs=in_vmem,
-        compiler_params=params(20),
-        cost_estimate=pl.CostEstimate(
-            flops=2 * slots * rows * width, bytes_accessed=2 * MIB, transcendentals=0
-        ),
-        name="pack_grads",
-    )(me, slot, grads)
+    messages = small_kernel(
+        functools.partial(pair_kernel, capacity),
+        [shape_of((2 * capacity, width), BF16)] * (n_seq // 2),
+        [same, lax.ppermute(cross, "seq", core_pairs())],
+        name="pair_up",
+    )
+    feats_got, messages = lax.optimization_barrier((feats_got, messages))
+    grads_got = [messages[0]] + [
+        lax.ppermute(messages[j], "seq", [(i, i ^ (2 * j)) for i in range(n_seq)])
+        for j in range(1, n_seq // 2)
+    ]
 
     def exchange(sent):
         sent = sent.reshape(n_seq, capacity, width)
         got = lax.all_to_all(sent, "seq", split_axis=0, concat_axis=0, tiled=True)
         return got.reshape(slots, width)
-
-    feats_got, grads_sent = lax.optimization_barrier((feats_got, grads_sent))
-    grads_got = exchange(grads_sent)
 
     pos, xhat, inv, normed, qkv, trans, attn_t, stats = pl.pallas_call(
         functools.partial(forward_kernel, n_seq, capacity),
@@ -648,7 +658,7 @@
             whole((width, width)),
             whole((2 * HEADS, rows)),
         ]
-        + [in_hbm] * 7,
+        + [in_hbm] * (6 + n_seq // 2),
         out_specs=[in_hbm] * 6,
         scratch_shapes=[
             pltpu.VMEM((slots, width), BF16),
@@ -667,7 +677,7 @@
             pltpu.VMEM((width, rows), BF16),
             pltpu.VMEM((rows, 3 * width), BF16),
             pltpu.VMEM((width, LANES), F32),
-            pltpu.SemaphoreType.DMA((13,)),
+            pltpu.SemaphoreType.DMA((12 + n_seq // 2,)),
         ],
         compiler_params=params(60),
         cost_estimate=pl.CostEstimate(
@@ -676,7 +686,7 @@
             transcendentals=HEADS * rows * rows,
         ),
         name="backward",
-    )(me, pos, w_proj, stats, grads_got, qkv, trans, w_qkv, xhat, normed, attn_t)
+    )(me, pos, w_proj, stats, qkv, trans, w_qkv, xhat, normed, attn_t, *grads_got)
 
     steps = chip_steps()
     terms = first_step(quarters, steps)

time: 132 us -> 126 us (0.955)
  waiting for transfers between devices: 57.6 us -> 51.6 us
  starting transfers between devices: 29 us -> 30.7 us
    all_to_all x2 -> x1, waiting for transfers between devices: 9.8 us -> 4.34 us  [exchange(): got = lax.all_to_all(sent, 'seq', split_axis=0, concat_axis=0, tiled=True)]
    ppermute x0 -> x4, starting transfers between devices: none -> 4.14 us  [the longest x3 3.62 us: per_device(): lax.ppermute(messages[j], 'seq', [(i, i ^ 2 * j) for i in range(n_seq)])]
    all_to_all x2 -> x1, starting transfers between devices: 8.3 us -> 4.26 us  [exchange(): got = lax.all_to_all(sent, 'seq', split_axis=0, concat_axis=0, tiled=True)]
    ppermute x2, waiting for transfers between devices: 13.4 us -> 11.5 us  [share_in_plane(): other = lax.ppermute(part, 'seq', pairs)]
    ppermute x0 -> x4, waiting for transfers between devices: none -> 1.88 us  [the longest x3 1.88 us: per_device(): lax.ppermute(messages[j], 'seq', [(i, i ^ 2 * j) for i in range(n_seq)])]
    pallas_call x1 -> x0, Pallas kernels: 1.7 us -> none  [per_device(): pl.pallas_call(functools.partial(pack_grads_kernel, n_seq, capacity), out...]
    ppermute x13, starting transfers between devices: 18.1 us -> 16.7 us  [by_distance(): lax.ppermute(blocks[k], axis, [(i, i ^ k) for i in range(count)])]
    unnamed x46 -> x50, local copies, waits for them, and re-layouts: 4.38 us -> 4.17 us
  transfers between devices with their start and end apart: 22 -> 25, of which waited for: 15 -> 16; matrix products, arithmetic and copies ran while one was open for 0% -> 0% of each run, Pallas kernels for 14% -> 14%
where the time goes in v13:
time: 126 us
  waiting for transfers between devices  51.6 us (41%)
  Pallas kernels  37.9 us (30%)
  starting transfers between devices  30.7 us (24%)
  local copies, waits for them, and re-layouts  4.19 us (3%)
    ppermute x13, waiting for transfers between devices, by_distance(): lax.ppermute(blocks[k], axis, [(i, i ^ k) for i in range(count)])  19 us
    ppermute x13, starting transfers between devices, by_distance(): lax.ppermute(blocks[k], axis, [(i, i ^ k) for i in range(count)])  16.7 us
    pallas_call x1, Pallas kernels, per_device(): pl.pallas_call(functools.partial(backward_kernel, n_seq, chip_bits), grid...  15.4 us
    ppermute x2, waiting for transfers between devices, share_in_plane(): other = lax.ppermute(part, 'seq', pairs)  11.5 us
    pallas_call x1, Pallas kernels, per_device(): pl.pallas_call(functools.partial(forward_kernel, n_seq, capacity), grid=(...  9.86 us
    ppermute x1, waiting for transfers between devices, first_step(): return [own_keep, got_keep, lax.ppermute(sent, 'seq', steps[0][0])]  7.99 us
    all_to_all x1, waiting for transfers between devices, exchange(): got = lax.all_to_all(sent, 'seq', split_axis=0, concat_axis=0, tiled=True)  4.34 us
    all_to_all x1, starting transfers between devices, exchange(): got = lax.all_to_all(sent, 'seq', split_axis=0, concat_axis=0, tiled=True)  4.26 us
  transfers between devices with their start and end apart: 25, of which 16 were waited for; matrix products, arithmetic and copies ran while one was open for 0% of the time, Pallas kernels for 14%

profile of v13, /device:TPU:0, one launch (start us, length us, event | category | flops | bytes accessed | tf_op | source)
XLA Modules:
  0.0 125.6 jit_solution(12407288015836318451)
XLA Ops:
  0.6 3.7 %pack.1 = (s32[1,512]{1,0:T(1,128)}, bf16[512,512]{1,0:T(8,128)(2,1)}, bf16[512,512]{1,0:T(8,128)(2,1)}, bf16[144,512]{1,0:T(8,128)(2,1)}, bf16[144,512]{1,0:T(8...) custom-call(s32[1]{0:T(128)} %bitcast.1.me_ref, ...), custom_call_target="tpu_custom_call" | custom-call | flops 1073741824 | bytes 4194304 | tf_op jit(solution)/shard_map/pack/pallas_call | solution.py:577
  4.4 0.5 collective-permute-start.7
  5.0 2.9 %collective-permute-start.1 = (bf16[144,512]{1,0:T(8,128)(2,1)}, bf16[144,512]{1,0:T(8,128)(2,1)S(1)}, u32[]{:S(2)}, u32[]{:S(2)}) collective-permute-start(bf16[144,512]{1,0:T(8,128)(2,1)} %get-tuple-element.63), channel_id=1, source_target_pairs={{0,8},{4,12},{8,0},{12,4},{16,24},{20,28},{24,16},{28,20},{1,9},{5... | collective-permute-start | bytes 442376 | tf_op jit(solution)/shard_map/ppermute | solution.py:413
  7.9 1.5 %collective-permute-start.3 = (bf16[144,512]{1,0:T(8,128)(2,1)}, bf16[144,512]{1,0:T(8,128)(2,1)S(1)}, u32[]{:S(2)}, u32[]{:S(2)}) collective-permute-start(bf16[144,512]{1,0:T(8,128)(2,1)} %get-tuple-element.65), channel_id=1, source_target_pairs={{0,16},{4,20},{8,24},{12,28},{16,0},{20,4},{24,8},{28,12},{1,17},{... | collective-permute-start | bytes 442376 | tf_op jit(solution)/shard_map/ppermute | solution.py:413
  9.4 0.3 collective-permute-start.4
  9.7 3.0 %collective-permute-done.1.refs_2_ = bf16[144,512]{1,0:T(8,128)(2,1)S(1)} collective-permute-done((bf16[144,512]{1,0:T(8,128)(2,1)}, bf16[144,512]{1,0:T(8,128)(2,1)S(1)}, u32[]{:S(2)}, u32[]{:S(2)}) %collective-permute-start.1) | collective-permute-done | bytes 147488 | tf_op jit(solution)/shard_map/ppermute | solution.py:413
  12.7 3.0 %collective-permute-start.5 = (bf16[144,512]{1,0:T(8,128)(2,1)}, bf16[144,512]{1,0:T(8,128)(2,1)S(1)}, u32[]{:S(2)}, u32[]{:S(2)}) collective-permute-start(bf16[144,512]{1,0:T(8,128)(2,1)} %get-tuple-element.67), channel_id=1, source_target_pairs={{0,24},{4,28},{8,16},{12,20},{16,8},{20,12},{24,0},{28,4},{1,25},{... | collective-permute-start | bytes 442376 | tf_op jit(solution)/shard_map/ppermute | solution.py:413
  15.8 1.0 copy-done.5
  16.9 0.7 copy-done.9
  17.7 5.6 %collective-permute-done.4.refs_5_ = bf16[144,512]{1,0:T(8,128)(2,1)S(1)} collective-permute-done((bf16[144,512]{1,0:T(8,128)(2,1)}, bf16[144,512]{1,0:T(8,128)(2,1)S(1)}, u32[]{:S(2)}, u32[]{:S(2)}) %collective-permute-start.4) | collective-permute-done | bytes 147488 | tf_op jit(solution)/shard_map/ppermute | solution.py:413
  23.3 3.0 %collective-permute-start.10 = (bf16[256,512]{1,0:T(8,128)(2,1)S(1)}, bf16[256,512]{1,0:T(8,128)(2,1)S(1)}, u32[]{:S(2)}, u32[]{:S(2)}) collective-permute-start(bf16[256,512]{1,0:T(8,128)(2,1)S(1)} %get-tuple-element.93), channel_id=1, source_target_pairs={{0,24},{4,28},{8,16},{12,20},{16,8},{20,12},{24,0},{28,4},{1,25},{... | collective-permute-start | bytes 786440 | tf_op jit(solution)/shard_map/ppermute | solution.py:605
  26.3 0.4 collective-permute-start.8
  27.0 9.9 %forward.1 = (s32[1,1024]{1,0:T(1,128)}, f32[512,512]{1,0:T(8,128)}, f32[512,128]{1,0:T(8,128)}, bf16[512,512]{1,0:T(8,128)(2,1)}, bf16[512,1536]{1,0:T(8,128)(2...) custom-call(bf16[512,1536]{1,0:T(8,128)(2,1)} %refs_2_.1, f32[1,512]{1,0:T(1,128)} %bitcast.26, ...), custom_call_target="tpu_custom_call" | custom-call | flops 2952790016 | bytes 16777216 | tf_op jit(solution)/shard_map/forward/pallas_call | solution.py:614
  36.8 1.9 %collective-permute-done.8.refs_7_ = bf16[256,512]{1,0:T(8,128)(2,1)S(1)} collective-permute-done((bf16[256,512]{1,0:T(8,128)(2,1)S(1)}, bf16[256,512]{1,0:T(8,128)(2,1)S(1)}, u32[]{:S(2)}, u32[]{:S(2)}) %collective-permute-start.8) | collective-permute-done | bytes 262176 | tf_op jit(solution)/shard_map/ppermute | solution.py:605
  38.7 0.7 copy-done.12
  39.6 15.4 %backward.1 = (f32[128,2176]{1,0:T(8,128)}, f32[128,2176]{1,0:T(8,128)}, f32[128,2176]{1,0:T(8,128)}, f32[128,2176]{1,0:T(8,128)}, bf16[512,512]{1,0:T(8,128)(2,1)}, /*index=5*/f32[512,512]{1,0:T(8,128)}) custom-call(s32[1]{0:T(128)} %bitcast.1.me_ref, s32[1,1024]{1,0:T(1,128)} %get-tuple-element.83.pos_ref, bf16[512,512]{1,0:T(8,128)(2,1)} %w_proj_ref.1, ...), custom_call_target="tpu_custom_call" | custom-call | flops 4294967296 | bytes 16777216 | tf_op jit(solution)/shard_map/backward/pallas_call | solution.py:650
  55.1 0.5 collective-permute-start.11
  55.6 2.5 %collective-permute-done.12.refs_1_ = f32[128,2176]{1,0:T(8,128)S(1)} collective-permute-done((f32[128,2176]{1,0:T(8,128)}, f32[128,2176]{1,0:T(8,128)S(1)}, u32[]{:S(2)}, u32[]{:S(2)}) %collective-permute-start.12) | collective-permute-done | bytes 1114144 | tf_op jit(solution)/shard_map/ppermute | solution.py:472
  58.0 1.2 copy-done.1
  59.3 0.3 code_first.1
  59.6 1.6 %collective-permute-start.13 = (s16[128,2176]{1,0:T(8,128)(2,1)S(1)}, s16[128,2176]{1,0:T(8,128)(2,1)S(1)}, u32[]{:S(2)}, u32[]{:S(2)}) collective-permute-start(s16[128,2176]{1,0:T(8,128)(2,1)S(1)} %code_first.1), channel_id=1, source_target_pairs={{0,8},{4,20},{8,0},{12,28},{16,24},{20,4},{24,16},{28,12},{1,9},{5... | collective-permute-start | bytes 1671176 | tf_op jit(solution)/shard_map/ppermute | solution.py:475
  61.2 8.0 %collective-permute-done.13.refs_2_ = s16[128,2176]{1,0:T(8,128)(2,1)S(1)} collective-permute-done((s16[128,2176]{1,0:T(8,128)(2,1)S(1)}, s16[128,2176]{1,0:T(8,128)(2,1)S(1)}, u32[]{:S(2)}, u32[]{:S(2)}) %collective-permute-start.13) | collective-permute-done | bytes 557088 | tf_op jit(solution)/shard_map/ppermute | solution.py:475
  69.2 0.3 code_second.1
  69.5 1.4 %collective-permute-start.14 = (s16[64,2176]{1,0:T(8,128)(2,1)S(1)}, s16[64,2176]{1,0:T(8,128)(2,1)S(1)}, u32[]{:S(2)}, u32[]{:S(2)}) collective-permute-start(s16[64,2176]{1,0:T(8,128)(2,1)S(1)} %code_second.1), channel_id=1, source_target_pairs={{0,16},{4,12},{8,24},{12,4},{16,0},{20,28},{24,8},{28,20},{1,17},{... | collective-permute-start | bytes 835592 | tf_op jit(solution)/shard_map/ppermute | solution.py:480
  70.9 2.1 %residual.1 = bf16[1024,512]{1,0:T(8,128)(2,1)} custom-call(s32[1]{0:T(128)} %bitcast.1.me_ref, s32[1,1024]{1,0:T(1,128)S(1)} %copy-done.7, f32[1,512]{1,0:T(1,128)S(1)} %bitcast.27, f32[512,128]{1,0:T(8,128)S(1)} %copy-done.6, f32[512,512]{1,0:T(8,128)S(1)} %copy-done.2, bf16[512,512]{1,0:T(8,128)(2,1)S(1)} %copy-done.4, f32[512,512]{1,0:T(8,128)S(1)} %copy-done.3), custom_call_target="tpu_custom_call" | custom-call | flops 536870912 | bytes 4194304 | tf_op jit(solution)/shard_map/residual/pallas_call | solution.py:693
  73.0 3.1 %collective-permute-done.14.refs_3_ = s16[64,2176]{1,0:T(8,128)(2,1)S(1)} collective-permute-done((s16[64,2176]{1,0:T(8,128)(2,1)S(1)}, s16[64,2176]{1,0:T(8,128)(2,1)S(1)}, u32[]{:S(2)}, u32[]{:S(2)}) %collective-permute-start.14) | collective-permute-done | bytes 278560 | tf_op jit(solution)/shard_map/ppermute | solution.py:480
  76.1 4.3 %all-to-all-start = ((bf16[8,128,512]{2,1,0:T(8,128)(2,1)}), bf16[8,128,512]{2,1,0:T(8,128)(2,1)}, u32[]{:S(2)}, u32[]{:S(2)}) async-start(bf16[8,128,512]{2,1,0:T(8,128)(2,1)} %bitcast.5), calls=%async_computation | async-start | bytes 2097152 | tf_op jit(solution)/shard_map/all_to_all | solution.py:611
  80.4 0.5 code_planes.1
  80.9 1.7 %collective-permute-start.15 = (s16[16,2176]{1,0:T(8,128)(2,1)S(1)}, s16[16,2176]{1,0:T(8,128)(2,1)S(1)}, u32[]{:S(2)}, u32[]{:S(2)}) collective-permute-start(s16[16,2176]{1,0:T(8,128)(2,1)S(1)} %get-tuple-element.103), channel_id=1, source_target_pairs={{0,1},{1,0},{2,3},{3,2},{4,5},{5,4},{6,7},{7,6},{8,9},{9,8},{10,11... | collective-permute-start | bytes 208904 | tf_op jit(solution)/shard_map/ppermute | solution.py:413
  82.6 2.6 %collective-permute-start.16 = (s16[16,2176]{1,0:T(8,128)(2,1)S(1)}, s16[16,2176]{1,0:T(8,128)(2,1)S(1)}, u32[]{:S(2)}, u32[]{:S(2)}) collective-permute-start(s16[16,2176]{1,0:T(8,128)(2,1)S(1)} %get-tuple-element.104), channel_id=1, source_target_pairs={{0,2},{1,3},{2,0},{3,1},{4,6},{5,7},{6,4},{7,5},{8,10},{9,11},{10,... | collective-permute-start | bytes 208904 | tf_op jit(solution)/shard_map/ppermute | solution.py:413
  85.2 0.2 collective-permute-start.17
  85.4 5.1 %collective-permute-done.16.refs_2_ = s16[16,2176]{1,0:T(8,128)(2,1)S(1)} collective-permute-done((s16[16,2176]{1,0:T(8,128)(2,1)S(1)}, s16[16,2176]{1,0:T(8,128)(2,1)S(1)}, u32[]{:S(2)}, u32[]{:S(2)}) %collective-permute-start.16) | collective-permute-done | bytes 69664 | tf_op jit(solution)/shard_map/ppermute | solution.py:413
  90.5 0.8 collective-permute-done.17.refs_3_
  91.5 4.3 %all-to-all-done = bf16[8,128,512]{2,1,0:T(8,128)(2,1)} async-done(((bf16[8,128,512]{2,1,0:T(8,128)(2,1)}), bf16[8,128,512]{2,1,0:T(8,128)(2,1)}, u32[]{:S(2)}, u32[]{:S(2)}) %all-to-all-start) | async-done | bytes 1048608 | tf_op jit(solution)/shard_map/all_to_all | solution.py:611
  95.8 3.6 %collective-permute-start.20 = (bf16[16,2176]{1,0:T(8,128)(2,1)S(1)}, bf16[16,2176]{1,0:T(8,128)(2,1)S(1)}, u32[]{:S(2)}, u32[]{:S(2)}) collective-permute-start(bf16[16,2176]{1,0:T(8,128)(2,1)S(1)} %finish.1), channel_id=1, source_target_pairs={{0,3},{1,2},{2,1},{3,0},{4,7},{5,6},{6,5},{7,4},{8,11},{9,10},{10,... | collective-permute-start | bytes 208904 | tf_op jit(solution)/shard_map/ppermute | solution.py:413
  99.4 0.8 collective-permute-start.19
  100.2 2.1 %collective-permute-done.20 = bf16[16,2176]{1,0:T(8,128)(2,1)S(1)} collective-permute-done((bf16[16,2176]{1,0:T(8,128)(2,1)S(1)}, bf16[16,2176]{1,0:T(8,128)(2,1)S(1)}, u32[]{:S(2)}, u32[]{:S(2)}) %collective-permute-start.20) | collective-permute-done | bytes 69664 | tf_op jit(solution)/shard_map/ppermute | solution.py:413
  102.3 1.4 %collective-permute-done.18 = bf16[16,2176]{1,0:T(8,128)(2,1)S(1)} collective-permute-done((bf16[16,2176]{1,0:T(8,128)(2,1)S(1)}, bf16[16,2176]{1,0:T(8,128)(2,1)S(1)}, u32[]{:S(2)}, u32[]{:S(2)}) %collective-permute-start.18) | collective-permute-done | bytes 69664 | tf_op jit(solution)/shard_map/ppermute | solution.py:413
  103.7 0.9 collective-permute-done.19
  104.8 0.6 collective-permute-start.21
  105.5 6.0 %collective-permute-done.21 = bf16[64,2176]{1,0:T(8,128)(2,1)S(1)} collective-permute-done((bf16[64,2176]{1,0:T(8,128)(2,1)S(1)}, bf16[64,2176]{1,0:T(8,128)(2,1)S(1)}, u32[]{:S(2)}, u32[]{:S(2)}) %collective-permute-start.21) | collective-permute-done | bytes 278560 | tf_op jit(solution)/shard_map/ppermute | solution.py:525
  111.6 1.3 %collective-permute-start.22 = (bf16[128,2176]{1,0:T(8,128)(2,1)S(1)}, bf16[128,2176]{1,0:T(8,128)(2,1)S(1)}, u32[]{:S(2)}, u32[]{:S(2)}) collective-permute-start(bf16[128,2176]{1,0:T(8,128)(2,1)S(1)} %broadcast_select_fusion), channel_id=1, source_target_pairs={{0,8},{4,20},{8,0},{12,28},{16,24},{20,4},{24,16},{28,12},{1,9},{5... | collective-permute-start | bytes 1671176 | tf_op jit(solution)/shard_map/ppermute | solution.py:525
  113.0 2.8 %unpack.1 = bf16[512,512]{1,0:T(8,128)(2,1)} custom-call(s32[1]{0:T(128)} %bitcast.1.me_ref, s32[1,512]{1,0:T(1,128)S(1)} %copy-done.10, bf16[1024,512]{1,0:T(8,128)(2,1)} %bitcast.6.recv_ref), custom_call_target="tpu_custom_call" | custom-call | flops 536870912 | bytes 2097152 | tf_op jit(solution)/shard_map/unpack/pallas_call | solution.py:709
  115.7 5.5 %collective-permute-done.22 = bf16[128,2176]{1,0:T(8,128)(2,1)S(1)} collective-permute-done((bf16[128,2176]{1,0:T(8,128)(2,1)S(1)}, bf16[128,2176]{1,0:T(8,128)(2,1)S(1)}, u32[]{:S(2)}, u32[]{:S(2)}) %collective-permute-start.22) | collective-permute-done | bytes 557088 | tf_op jit(solution)/shard_map/ppermute | solution.py:525
  121.2 0.2 maximum_select_fusion.sums_ref
  121.6 1.4 %split.2 = (f32[512,1536]{1,0:T(8,128)}, f32[512,512]{1,0:T(8,128)}, f32[1,512]{1,0:T(1,128)}) custom-call(s32[1]{0:T(128)S(6)} %and.19.side_ref, bf16[256,2176]{1,0:T(8,128)(2,1)S(1)} %maximum_select_fusion.sums_ref), custom_call_target="tpu_custom_call" | custom-call | bytes 4194304 | tf_op jit(solution)/shard_map/split/pallas_call | solution.py:534
  122.9 1.3 %collective-permute-done.23.sums_ref = bf16[256,2176]{1,0:T(8,128)(2,1)S(1)} collective-permute-done((bf16[256,2176]{1,0:T(8,128)(2,1)S(1)}, bf16[256,2176]{1,0:T(8,128)(2,1)S(1)}, u32[]{:S(2)}, u32[]{:S(2)}) %collective-permute-start.23) | collective-permute-done | bytes 1114144 | tf_op jit(solution)/shard_map/ppermute | solution.py:721
  124.3 1.3 %split.3 = (f32[512,1536]{1,0:T(8,128)}, f32[512,512]{1,0:T(8,128)}, f32[1,512]{1,0:T(1,128)}) custom-call(s32[1]{0:T(128)S(6)} %sub.3.side_ref, bf16[256,2176]{1,0:T(8,128)(2,1)S(1)} %collective-permute-done.23.sums_ref, f32[512,1536]{1,0:T(8,128)} %get-tuple-element.112.refs_0_, ...), custom_call_target="tpu_custom_call", output_to_operand_aliasing={{0}: (2, {}), {1}: (3, {}), {2}: (4, {})} | custom-call | bytes 4194304 | tf_op jit(solution)/shard_map/split/pallas_call | solution.py:534
  (69 shorter events, 1.3 us)
Async XLA Ops:
  4.4 11.4 %collective-permute-start.7 = (bf16[512,512]{1,0:T(8,128)(2,1)}, bf16[512,512]{1,0:T(8,128)(2,1)S(1)}, u32[]{:S(2)}, u32[]{:S(2)}) collective-permute-start(bf16[512,512]{1,0:T(8,128)(2,1)} %get-tuple-element.70), channel_id=1, source_target_pairs={{0,4},{4,0},{8,12},{12,8},{16,20},{20,16},{24,28},{28,24},{1,5},{5... | collective-permute-start | bytes 1572872 | tf_op jit(solution)/shard_map/ppermute | solution.py:600
  4.9 4.5 %collective-permute-start = (bf16[144,512]{1,0:T(8,128)(2,1)}, bf16[144,512]{1,0:T(8,128)(2,1)S(1)}, u32[]{:S(2)}, u32[]{:S(2)}) collective-permute-start(bf16[144,512]{1,0:T(8,128)(2,1)} %get-tuple-element.62), channel_id=1, source_target_pairs={{0,4},{4,0},{8,12},{12,8},{16,20},{20,16},{24,28},{28,24},{1,5},{5... | collective-permute-start | bytes 442376 | tf_op jit(solution)/shard_map/ppermute | solution.py:413
  5.0 7.8 %collective-permute-start.1 = (bf16[144,512]{1,0:T(8,128)(2,1)}, bf16[144,512]{1,0:T(8,128)(2,1)S(1)}, u32[]{:S(2)}, u32[]{:S(2)}) collective-permute-start(bf16[144,512]{1,0:T(8,128)(2,1)} %get-tuple-element.63), channel_id=1, source_target_pairs={{0,8},{4,12},{8,0},{12,4},{16,24},{20,28},{24,16},{28,20},{1,9},{5... | collective-permute-start | bytes 442376 | tf_op jit(solution)/shard_map/ppermute | solution.py:413
  7.9 9.8 %collective-permute-start.2 = (bf16[144,512]{1,0:T(8,128)(2,1)}, bf16[144,512]{1,0:T(8,128)(2,1)S(1)}, u32[]{:S(2)}, u32[]{:S(2)}) collective-permute-start(bf16[144,512]{1,0:T(8,128)(2,1)} %get-tuple-element.64), channel_id=1, source_target_pairs={{0,12},{4,8},{8,4},{12,0},{16,28},{20,24},{24,20},{28,16},{1,13},{... | collective-permute-start | bytes 442376 | tf_op jit(solution)/shard_map/ppermute | solution.py:413
  7.9 9.8 %collective-permute-start.3 = (bf16[144,512]{1,0:T(8,128)(2,1)}, bf16[144,512]{1,0:T(8,128)(2,1)S(1)}, u32[]{:S(2)}, u32[]{:S(2)}) collective-permute-start(bf16[144,512]{1,0:T(8,128)(2,1)} %get-tuple-element.65), channel_id=1, source_target_pairs={{0,16},{4,20},{8,24},{12,28},{16,0},{20,4},{24,8},{28,12},{1,17},{... | collective-permute-start | bytes 442376 | tf_op jit(solution)/shard_map/ppermute | solution.py:413
  9.4 17.5 %copy-start.14 = (bf16[144,512]{1,0:T(8,128)(2,1)}, bf16[144,512]{1,0:T(8,128)(2,1)S(1)}, u32[]{:S(2)}) copy-start(bf16[144,512]{1,0:T(8,128)(2,1)S(1)} %collective-permute-done.refs_1_) | copy-start | bytes 442372
  9.4 13.8 %collective-permute-start.4 = (bf16[144,512]{1,0:T(8,128)(2,1)}, bf16[144,512]{1,0:T(8,128)(2,1)S(1)}, u32[]{:S(2)}, u32[]{:S(2)}) collective-permute-start(bf16[144,512]{1,0:T(8,128)(2,1)} %get-tuple-element.66), channel_id=1, source_target_pairs={{0,20},{4,16},{8,28},{12,24},{16,4},{20,0},{24,12},{28,8},{1,21},{... | collective-permute-start | bytes 442376 | tf_op jit(solution)/shard_map/ppermute | solution.py:413
  12.7 14.2 %copy-start.15 = (bf16[144,512]{1,0:T(8,128)(2,1)}, bf16[144,512]{1,0:T(8,128)(2,1)S(1)}, u32[]{:S(2)}) copy-start(bf16[144,512]{1,0:T(8,128)(2,1)S(1)} %collective-permute-done.1.refs_2_) | copy-start | bytes 442372
  12.7 10.5 %collective-permute-start.5 = (bf16[144,512]{1,0:T(8,128)(2,1)}, bf16[144,512]{1,0:T(8,128)(2,1)S(1)}, u32[]{:S(2)}, u32[]{:S(2)}) collective-permute-start(bf16[144,512]{1,0:T(8,128)(2,1)} %get-tuple-element.67), channel_id=1, source_target_pairs={{0,24},{4,28},{8,16},{12,20},{16,8},{20,12},{24,0},{28,4},{1,25},{... | collective-permute-start | bytes 442376 | tf_op jit(solution)/shard_map/ppermute | solution.py:413
  15.8 7.5 %collective-permute-start.6 = (bf16[144,512]{1,0:T(8,128)(2,1)}, bf16[144,512]{1,0:T(8,128)(2,1)S(1)}, u32[]{:S(2)}, u32[]{:S(2)}) collective-permute-start(bf16[144,512]{1,0:T(8,128)(2,1)} %get-tuple-element.68), channel_id=1, source_target_pairs={{0,28},{4,24},{8,20},{12,16},{16,12},{20,8},{24,4},{28,0},{1,29},{... | collective-permute-start | bytes 442376 | tf_op jit(solution)/shard_map/ppermute | solution.py:413
  15.8 1.0 copy-start.5
  16.9 0.8 copy-start.9
  17.6 9.3 %copy-start.16 = (bf16[144,512]{1,0:T(8,128)(2,1)}, bf16[144,512]{1,0:T(8,128)(2,1)S(1)}, u32[]{:S(2)}) copy-start(bf16[144,512]{1,0:T(8,128)(2,1)S(1)} %collective-permute-done.2.refs_3_) | copy-start | bytes 442372
  17.6 9.3 %copy-start.17 = (bf16[144,512]{1,0:T(8,128)(2,1)}, bf16[144,512]{1,0:T(8,128)(2,1)S(1)}, u32[]{:S(2)}) copy-start(bf16[144,512]{1,0:T(8,128)(2,1)S(1)} %collective-permute-done.3.refs_4_) | copy-start | bytes 442372
  23.3 3.7 %copy-start.18 = (bf16[144,512]{1,0:T(8,128)(2,1)}, bf16[144,512]{1,0:T(8,128)(2,1)S(1)}, u32[]{:S(2)}) copy-start(bf16[144,512]{1,0:T(8,128)(2,1)S(1)} %collective-permute-done.4.refs_5_) | copy-start | bytes 442372
  23.3 3.7 %copy-start.19 = (bf16[144,512]{1,0:T(8,128)(2,1)}, bf16[144,512]{1,0:T(8,128)(2,1)S(1)}, u32[]{:S(2)}) copy-start(bf16[144,512]{1,0:T(8,128)(2,1)S(1)} %collective-permute-done.5.refs_6_) | copy-start | bytes 442372
  23.3 3.7 %copy-start.20 = (bf16[144,512]{1,0:T(8,128)(2,1)}, bf16[144,512]{1,0:T(8,128)(2,1)S(1)}, u32[]{:S(2)}) copy-start(bf16[144,512]{1,0:T(8,128)(2,1)S(1)} %collective-permute-done.6.refs_7_) | copy-start | bytes 442372
  23.3 13.5 %collective-permute-start.10 = (bf16[256,512]{1,0:T(8,128)(2,1)S(1)}, bf16[256,512]{1,0:T(8,128)(2,1)S(1)}, u32[]{:S(2)}, u32[]{:S(2)}) collective-permute-start(bf16[256,512]{1,0:T(8,128)(2,1)S(1)} %get-tuple-element.93), channel_id=1, source_target_pairs={{0,24},{4,28},{8,16},{12,20},{16,8},{20,12},{24,0},{28,4},{1,25},{... | collective-permute-start | bytes 786440 | tf_op jit(solution)/shard_map/ppermute | solution.py:605
  26.3 12.4 %collective-permute-start.8 = (bf16[256,512]{1,0:T(8,128)(2,1)S(1)}, bf16[256,512]{1,0:T(8,128)(2,1)S(1)}, u32[]{:S(2)}, u32[]{:S(2)}) collective-permute-start(bf16[256,512]{1,0:T(8,128)(2,1)S(1)} %get-tuple-element.91), channel_id=1, source_target_pairs={{0,8},{4,12},{8,0},{12,4},{16,24},{20,28},{24,16},{28,20},{1,9},{5... | collective-permute-start | bytes 786440 | tf_op jit(solution)/shard_map/ppermute | solution.py:605
  26.7 12.0 %collective-permute-start.9 = (bf16[256,512]{1,0:T(8,128)(2,1)S(1)}, bf16[256,512]{1,0:T(8,128)(2,1)S(1)}, u32[]{:S(2)}, u32[]{:S(2)}) collective-permute-start(bf16[256,512]{1,0:T(8,128)(2,1)S(1)} %get-tuple-element.92), channel_id=1, source_target_pairs={{0,16},{4,20},{8,24},{12,28},{16,0},{20,4},{24,8},{28,12},{1,17},{... | collective-permute-start | bytes 786440 | tf_op jit(solution)/shard_map/ppermute | solution.py:605
  36.8 1.9 %copy-start.11 = (bf16[256,512]{1,0:T(8,128)(2,1)}, bf16[256,512]{1,0:T(8,128)(2,1)S(1)}, u32[]{:S(2)}) copy-start(bf16[256,512]{1,0:T(8,128)(2,1)S(1)} %collective-permute-done.10.refs_9_) | copy-start | bytes 786436
  38.7 0.7 copy-start.12
  38.7 0.8 copy-start.13
  55.0 3.0 %collective-permute-start.12 = (f32[128,2176]{1,0:T(8,128)}, f32[128,2176]{1,0:T(8,128)S(1)}, u32[]{:S(2)}, u32[]{:S(2)}) collective-permute-start(f32[128,2176]{1,0:T(8,128)} %get-tuple-element.97), channel_id=1, source_target_pairs={{0,4},{4,0},{8,12},{12,8},{16,20},{20,16},{24,28},{28,24},{1,5},{5... | collective-permute-start | bytes 3342344 | tf_op jit(solution)/shard_map/ppermute | solution.py:472
  55.1 6.1 %collective-permute-start.11 = (f32[128,2176]{1,0:T(8,128)}, f32[128,2176]{1,0:T(8,128)S(1)}, u32[]{:S(2)}, u32[]{:S(2)}) collective-permute-start(f32[128,2176]{1,0:T(8,128)} %get-tuple-element.95), channel_id=1, source_target_pairs={{0,4},{4,0},{8,12},{12,8},{16,20},{20,16},{24,28},{28,24},{1,5},{5... | collective-permute-start | bytes 3342344 | tf_op jit(solution)/shard_map/ppermute | solution.py:473
  58.0 1.2 copy-start.1
  59.3 9.9 %copy-start = (f32[128,2176]{1,0:T(8,128)S(1)}, f32[128,2176]{1,0:T(8,128)}, u32[]{:S(2)}) copy-start(f32[128,2176]{1,0:T(8,128)} %get-tuple-element.94.refs_0_) | copy-start | bytes 3342340
  59.6 9.6 %collective-permute-start.13 = (s16[128,2176]{1,0:T(8,128)(2,1)S(1)}, s16[128,2176]{1,0:T(8,128)(2,1)S(1)}, u32[]{:S(2)}, u32[]{:S(2)}) collective-permute-start(s16[128,2176]{1,0:T(8,128)(2,1)S(1)} %code_first.1), channel_id=1, source_target_pairs={{0,8},{4,20},{8,0},{12,28},{16,24},{20,4},{24,16},{28,12},{1,9},{5... | collective-permute-start | bytes 1671176 | tf_op jit(solution)/shard_map/ppermute | solution.py:475
  69.2 1.7 %copy-start.2 = (f32[512,512]{1,0:T(8,128)S(1)}, f32[512,512]{1,0:T(8,128)}, u32[]{:S(2)}) copy-start(f32[512,512]{1,0:T(8,128)} %get-tuple-element.87.refs_3_.xhat_ref) | copy-start | bytes 3145732
  69.2 1.7 %copy-start.3 = (f32[512,512]{1,0:T(8,128)S(1)}, f32[512,512]{1,0:T(8,128)}, u32[]{:S(2)}) copy-start(f32[512,512]{1,0:T(8,128)} %get-tuple-element.100.d_normed_ref) | copy-start | bytes 3145732
  69.2 1.7 %copy-start.4 = (bf16[512,512]{1,0:T(8,128)(2,1)S(1)}, bf16[512,512]{1,0:T(8,128)(2,1)}, u32[]{:S(2)}) copy-start(bf16[512,512]{1,0:T(8,128)(2,1)} %get-tuple-element.99.serial_grad_ref) | copy-start | bytes 1572868
  69.2 1.7 %copy-start.6 = (f32[512,128]{1,0:T(8,128)S(1)}, f32[512,128]{1,0:T(8,128)}, u32[]{:S(2)}) copy-start(f32[512,128]{1,0:T(8,128)} %get-tuple-element.98.inv_ref) | copy-start | bytes 786436
  69.2 1.7 %copy-start.7 = (s32[1,1024]{1,0:T(1,128)S(1)}, s32[1,1024]{1,0:T(1,128)}, u32[]{:S(2)}) copy-start(s32[1,1024]{1,0:T(1,128)} %get-tuple-element.83.pos_ref) | copy-start | bytes 12292
  69.2 1.7 %copy-start.8 = (f32[512]{0:T(512)S(1)}, f32[512]{0:T(512)}, u32[]{:S(2)}) copy-start(f32[512]{0:T(512)} %param.11) | copy-start | bytes 6148
  69.5 6.6 %collective-permute-start.14 = (s16[64,2176]{1,0:T(8,128)(2,1)S(1)}, s16[64,2176]{1,0:T(8,128)(2,1)S(1)}, u32[]{:S(2)}, u32[]{:S(2)}) collective-permute-start(s16[64,2176]{1,0:T(8,128)(2,1)S(1)} %code_second.1), channel_id=1, source_target_pairs={{0,16},{4,12},{8,24},{12,4},{16,0},{20,28},{24,8},{28,20},{1,17},{... | collective-permute-start | bytes 835592 | tf_op jit(solution)/shard_map/ppermute | solution.py:480
  76.1 19.7 %all-to-all-start = ((bf16[8,128,512]{2,1,0:T(8,128)(2,1)}), bf16[8,128,512]{2,1,0:T(8,128)(2,1)}, u32[]{:S(2)}, u32[]{:S(2)}) async-start(bf16[8,128,512]{2,1,0:T(8,128)(2,1)} %bitcast.5), calls=%async_computation | async-start | bytes 2097152 | tf_op jit(solution)/shard_map/all_to_all | solution.py:611
  80.9 4.5 %collective-permute-start.15 = (s16[16,2176]{1,0:T(8,128)(2,1)S(1)}, s16[16,2176]{1,0:T(8,128)(2,1)S(1)}, u32[]{:S(2)}, u32[]{:S(2)}) collective-permute-start(s16[16,2176]{1,0:T(8,128)(2,1)S(1)} %get-tuple-element.103), channel_id=1, source_target_pairs={{0,1},{1,0},{2,3},{3,2},{4,5},{5,4},{6,7},{7,6},{8,9},{9,8},{10,11... | collective-permute-start | bytes 208904 | tf_op jit(solution)/shard_map/ppermute | solution.py:413
  82.6 7.9 %collective-permute-start.16 = (s16[16,2176]{1,0:T(8,128)(2,1)S(1)}, s16[16,2176]{1,0:T(8,128)(2,1)S(1)}, u32[]{:S(2)}, u32[]{:S(2)}) collective-permute-start(s16[16,2176]{1,0:T(8,128)(2,1)S(1)} %get-tuple-element.104), channel_id=1, source_target_pairs={{0,2},{1,3},{2,0},{3,1},{4,6},{5,7},{6,4},{7,5},{8,10},{9,11},{10,... | collective-permute-start | bytes 208904 | tf_op jit(solution)/shard_map/ppermute | solution.py:413
  85.2 6.2 %collective-permute-start.17 = (s16[16,2176]{1,0:T(8,128)(2,1)S(1)}, s16[16,2176]{1,0:T(8,128)(2,1)S(1)}, u32[]{:S(2)}, u32[]{:S(2)}) collective-permute-start(s16[16,2176]{1,0:T(8,128)(2,1)S(1)} %get-tuple-element.105), channel_id=1, source_target_pairs={{0,3},{1,2},{2,1},{3,0},{4,7},{5,6},{6,5},{7,4},{8,11},{9,10},{10,... | collective-permute-start | bytes 208904 | tf_op jit(solution)/shard_map/ppermute | solution.py:413
  95.8 6.5 %collective-permute-start.20 = (bf16[16,2176]{1,0:T(8,128)(2,1)S(1)}, bf16[16,2176]{1,0:T(8,128)(2,1)S(1)}, u32[]{:S(2)}, u32[]{:S(2)}) collective-permute-start(bf16[16,2176]{1,0:T(8,128)(2,1)S(1)} %finish.1), channel_id=1, source_target_pairs={{0,3},{1,2},{2,1},{3,0},{4,7},{5,6},{6,5},{7,4},{8,11},{9,10},{10,... | collective-permute-start | bytes 208904 | tf_op jit(solution)/shard_map/ppermute | solution.py:413
  99.4 4.3 %collective-permute-start.18 = (bf16[16,2176]{1,0:T(8,128)(2,1)S(1)}, bf16[16,2176]{1,0:T(8,128)(2,1)S(1)}, u32[]{:S(2)}, u32[]{:S(2)}) collective-permute-start(bf16[16,2176]{1,0:T(8,128)(2,1)S(1)} %finish.1), channel_id=1, source_target_pairs={{0,1},{1,0},{2,3},{3,2},{4,5},{5,4},{6,7},{7,6},{8,9},{9,8},{10,11... | collective-permute-start | bytes 208904 | tf_op jit(solution)/shard_map/ppermute | solution.py:413
  99.4 5.2 %collective-permute-start.19 = (bf16[16,2176]{1,0:T(8,128)(2,1)S(1)}, bf16[16,2176]{1,0:T(8,128)(2,1)S(1)}, u32[]{:S(2)}, u32[]{:S(2)}) collective-permute-start(bf16[16,2176]{1,0:T(8,128)(2,1)S(1)} %finish.1), channel_id=1, source_target_pairs={{0,2},{1,3},{2,0},{3,1},{4,6},{5,7},{6,4},{7,5},{8,10},{9,11},{10,... | collective-permute-start | bytes 208904 | tf_op jit(solution)/shard_map/ppermute | solution.py:413
  104.8 6.6 %collective-permute-start.21 = (bf16[64,2176]{1,0:T(8,128)(2,1)S(1)}, bf16[64,2176]{1,0:T(8,128)(2,1)S(1)}, u32[]{:S(2)}, u32[]{:S(2)}) collective-permute-start(bf16[64,2176]{1,0:T(8,128)(2,1)S(1)} %pad_maximum_fusion.1), channel_id=1, source_target_pairs={{0,16},{4,12},{8,24},{12,4},{16,0},{20,28},{24,8},{28,20},{1,17},{... | collective-permute-start | bytes 835592 | tf_op jit(solution)/shard_map/ppermute | solution.py:525
  111.5 1.5 %copy-start.10 = (s32[1,512]{1,0:T(1,128)S(1)}, s32[1,512]{1,0:T(1,128)}, u32[]{:S(2)}) copy-start(s32[1,512]{1,0:T(1,128)} %get-tuple-element.108.slot_ref) | copy-start | bytes 6148
  111.6 9.6 %collective-permute-start.22 = (bf16[128,2176]{1,0:T(8,128)(2,1)S(1)}, bf16[128,2176]{1,0:T(8,128)(2,1)S(1)}, u32[]{:S(2)}, u32[]{:S(2)}) collective-permute-start(bf16[128,2176]{1,0:T(8,128)(2,1)S(1)} %broadcast_select_fusion), channel_id=1, source_target_pairs={{0,8},{4,20},{8,0},{12,28},{16,24},{20,4},{24,16},{28,12},{1,9},{5... | collective-permute-start | bytes 1671176 | tf_op jit(solution)/shard_map/ppermute | solution.py:525
  121.5 2.8 %collective-permute-start.23 = (bf16[256,2176]{1,0:T(8,128)(2,1)S(1)}, bf16[256,2176]{1,0:T(8,128)(2,1)S(1)}, u32[]{:S(2)}, u32[]{:S(2)}) collective-permute-start(bf16[256,2176]{1,0:T(8,128)(2,1)S(1)} %maximum_select_fusion.sums_ref), channel_id=1, source_target_pairs={{0,4},{4,0},{8,12},{12,8},{16,20},{20,16},{24,28},{28,24},{1,5},{5... | collective-permute-start | bytes 3342344 | tf_op jit(solution)/shard_map/ppermute | solution.py:721

commit v14 on v13

--- a/solution.py
+++ b/solution.py
@@ -37,10 +37,6 @@
     column = jnp.transpose(jnp.broadcast_to(row, (LANES, size)))
     lane = iota((size, LANES), 1)
     return jnp.concatenate([hot(column == lane + j * LANES) for j in range(count // LANES)], axis=1)
-
-
-def by_receiver(me, distance, capacity):
-    return pl.ds(pl.multiple_of(lax.bitwise_xor(me, distance) * capacity, capacity), capacity)
 
 
 def pack_kernel(
@@ -300,12 +296,9 @@
         save.wait()
 
 
-def residual_kernel(
-    n_seq, me_ref, pos_ref, gain_ref, inv_ref, xhat_ref, serial_grad_ref, d_normed_ref, back_out
-):
+def residual_kernel(pos_ref, gain_ref, inv_ref, xhat_ref, serial_grad_ref, d_normed_ref, *outs):
     xhat = xhat_ref[...]
     rows = xhat.shape[0]
-    capacity = pos_ref.shape[1] // n_seq
     scaled = d_normed_ref[...] * gain_ref[...]
     residual = inv_ref[:, 0:1] * (
         scaled
@@ -314,16 +307,24 @@
     )
     serial_dx = (serial_grad_ref[...].astype(F32) + residual).astype(BF16)
     returned = mm(column_hot(pos_ref[...], rows), serial_dx).astype(BF16)
-    for d in range(n_seq):
-        back_out[by_receiver(me_ref[0], d, capacity), :] = returned[d * capacity : (d + 1) * capacity]
-
-
-def unpack_kernel(n_seq, me_ref, slot_ref, recv_ref, out_ref):
-    capacity = recv_ref.shape[0] // n_seq
-    values = jnp.concatenate(
-        [recv_ref[by_receiver(me_ref[0], d, capacity), :] for d in range(n_seq)], axis=0
-    )
-    out_ref[...] = mm(column_hot(slot_ref[...], values.shape[0]), values).astype(BF16)
+    size = outs[0].shape[0]
+    for j, out in enumerate(outs):
+        out[...] = returned[j * size : (j + 1) * size]
+
+
+def cross_kernel(*refs):
+    size = refs[0].shape[0] // 2
+    for j, ref in enumerate(refs[:-1]):
+        refs[-1][j * size : (j + 1) * size, :] = ref[size:, :]
+
+
+def unpack_kernel(slot_ref, cross_ref, *refs):
+    size = refs[0].shape[0] // 2
+    blocks = []
+    for j, ref in enumerate(refs[:-1]):
+        blocks += [ref[:size, :], cross_ref[j * size : (j + 1) * size, :]]
+    values = jnp.concatenate(blocks, axis=0)
+    refs[-1][...] = mm(column_hot(slot_ref[...], values.shape[0]), values).astype(BF16)
 
 
 def split_kernel(side_ref, sums_ref, *refs):
@@ -414,6 +415,14 @@
     ]
 
 
+def by_chip(messages):
+    count = 2 * len(messages)
+    return [messages[0]] + [
+        lax.ppermute(messages[j], "seq", [(i, i ^ (2 * j)) for i in range(count)])
+        for j in range(1, len(messages))
+    ]
+
+
 def chip_orders(n_seq):
     bits = list(range(1, n_seq.bit_length() - 1))
     middle = len(bits) // 2
@@ -453,7 +462,7 @@
         in_specs=[in_smem] * scalars + [in_vmem] * (len(operands) - scalars),
         out_specs=[in_vmem] * len(outs),
         scratch_shapes=list(scratch),
-        compiler_params=params(16),
+        compiler_params=params(20),
         cost_estimate=pl.CostEstimate(flops=2 * touched, bytes_accessed=touched, transcendentals=0),
         name=name,
     )(*operands)
@@ -601,15 +610,7 @@
         name="pair_up",
     )
     feats_got, messages = lax.optimization_barrier((feats_got, messages))
-    grads_got = [messages[0]] + [
-        lax.ppermute(messages[j], "seq", [(i, i ^ (2 * j)) for i in range(n_seq)])
-        for j in range(1, n_seq // 2)
-    ]
-
-    def exchange(sent):
-        sent = sent.reshape(n_seq, capacity, width)
-        got = lax.all_to_all(sent, "seq", split_axis=0, concat_axis=0, tiled=True)
-        return got.reshape(slots, width)
+    grads_got = by_chip(messages)
 
     pos, xhat, inv, normed, qkv, trans, attn_t, stats = pl.pallas_call(
         functools.partial(forward_kernel, n_seq, capacity),
@@ -690,33 +691,26 @@
 
     steps = chip_steps()
     terms = first_step(quarters, steps)
-    back = pl.pallas_call(
-        functools.partial(residual_kernel, n_seq),
-        out_shape=shape_of((slots, width), BF16),
-        in_specs=[in_smem] + [in_vmem] * 6,
-        out_specs=in_vmem,
-        compiler_params=params(20),
-        cost_estimate=pl.CostEstimate(
-            flops=2 * slots * rows * width, bytes_accessed=4 * MIB, transcendentals=0
-        ),
+    back = small_kernel(
+        residual_kernel,
+        [shape_of((2 * capacity, width), BF16)] * (n_seq // 2),
+        [pos, gain_row, inv, xhat, serial_grad, d_normed],
         name="residual",
-    )(me, pos, gain_row, inv, xhat, serial_grad, d_normed)
+    )
     terms, got = second_step(terms, steps)
     got, back = lax.optimization_barrier((got, back))
-    returned = exchange(back)
+    returned = by_chip(back)
     part, returned = lax.optimization_barrier((reduce_over_planes(terms, got, steps), returned))
+    cross = small_kernel(
+        cross_kernel, [shape_of((slots // 2, width), BF16)], returned, name="for_core_pair"
+    )[0]
     own = share_in_plane(share_over_planes(part), steps)
-    grad_local = pl.pallas_call(
-        functools.partial(unpack_kernel, n_seq),
-        out_shape=shape_of((rows, width), BF16),
-        in_specs=[in_smem] + [in_vmem] * 2,
-        out_specs=in_vmem,
-        compiler_params=params(20),
-        cost_estimate=pl.CostEstimate(
-            flops=2 * slots * rows * width, bytes_accessed=2 * MIB, transcendentals=0
-        ),
+    grad_local = small_kernel(
+        unpack_kernel,
+        [shape_of((rows, width), BF16)],
+        [slot, lax.ppermute(cross, "seq", core_pairs()), *returned],
         name="unpack",
-    )(me, slot, returned)
+    )[0]
     own, grad_local = lax.optimization_barrier((own, grad_local))
     other = lax.ppermute(own, "seq", core_pairs())
     side = lax.bitwise_and(me, 1)

time: 126 us -> 127 us (level)
  waiting for transfers between devices: 51.6 us -> 46.8 us
  starting transfers between devices: 30.7 us -> 34.4 us
  local copies, waits for them, and re-layouts: 4.19 us -> 5.75 us
    pallas_call x5 -> x8, Pallas kernels: 1.29 us -> 6.8 us  [small_kernel(): pl.pallas_call(kernel, out_shape=outs, in_specs=[in_smem] * scalars + [in...]
    pallas_call x2 -> x0, Pallas kernels: 4.86 us -> none  [the longest x1 2.77 us: per_device(): pl.pallas_call(functools.partial(unpack_kernel, n_seq), out_shape=shape_o...]
    all_to_all x1 -> x0, waiting for transfers between devices: 4.34 us -> none  [exchange(): got = lax.all_to_all(sent, 'seq', split_axis=0, concat_axis=0, tiled=True)]
    all_to_all x1 -> x0, starting transfers between devices: 4.26 us -> none  [exchange(): got = lax.all_to_all(sent, 'seq', split_axis=0, concat_axis=0, tiled=True)]
    ppermute x3 -> x6, starting transfers between devices: 3.62 us -> 7.1 us  [by_chip(): lax.ppermute(messages[j], 'seq', [(i, i ^ 2 * j) for i in range(count)])]
    ppermute x13, starting transfers between devices: 16.7 us -> 20.1 us  [by_distance(): lax.ppermute(blocks[k], axis, [(i, i ^ k) for i in range(count)])]
    ppermute x1 -> x2, waiting for transfers between devices: 0.01 us -> 1.89 us  [per_device(): lax.ppermute(cross, 'seq', core_pairs())]
    ppermute x13, waiting for transfers between devices: 19 us -> 17.4 us  [by_distance(): lax.ppermute(blocks[k], axis, [(i, i ^ k) for i in range(count)])]
  transfers between devices with their start and end apart: 25 -> 28, of which waited for: 16 -> 16; matrix products, arithmetic and copies ran while one was open for 0% -> 0% of each run, Pallas kernels for 14% -> 14%
where the time goes in v14:
time: 127 us
  waiting for transfers between devices  46.8 us (37%)
  Pallas kernels  38.6 us (30%)
  starting transfers between devices  34.4 us (27%)
  local copies, waits for them, and re-layouts  5.75 us (5%)
    ppermute x13, starting transfers between devices, by_distance(): lax.ppermute(blocks[k], axis, [(i, i ^ k) for i in range(count)])  20.1 us
    ppermute x13, waiting for transfers between devices, by_distance(): lax.ppermute(blocks[k], axis, [(i, i ^ k) for i in range(count)])  17.4 us
    pallas_call x1, Pallas kernels, per_device(): pl.pallas_call(functools.partial(backward_kernel, n_seq, chip_bits), grid...  15.5 us
    ppermute x2, waiting for transfers between devices, share_in_plane(): other = lax.ppermute(part, 'seq', pairs)  10.6 us
    pallas_call x1, Pallas kernels, per_device(): pl.pallas_call(functools.partial(forward_kernel, n_seq, capacity), grid=(...  9.85 us
    ppermute x1, waiting for transfers between devices, first_step(): return [own_keep, got_keep, lax.ppermute(sent, 'seq', steps[0][0])]  7.99 us
    ppermute x6, starting transfers between devices, by_chip(): lax.ppermute(messages[j], 'seq', [(i, i ^ 2 * j) for i in range(count)])  7.1 us
    pallas_call x8, Pallas kernels, small_kernel(): pl.pallas_call(kernel, out_shape=outs, in_specs=[in_smem] * scalars + [in...  6.8 us
  transfers between devices with their start and end apart: 28, of which 16 were waited for; matrix products, arithmetic and copies ran while one was open for 0% of the time, Pallas kernels for 14%

profile of v14, /device:TPU:0, one launch (start us, length us, event | category | flops | bytes accessed | tf_op | source)
XLA Modules:
  0.0 126.8 jit_solution(17730765457803656355)
XLA Ops:
  0.6 3.7 %pack.1 = (s32[1,512]{1,0:T(1,128)}, bf16[512,512]{1,0:T(8,128)(2,1)}, bf16[512,512]{1,0:T(8,128)(2,1)}, bf16[144,512]{1,0:T(8,128)(2,1)}, bf16[144,512]{1,0:T(8...) custom-call(s32[1]{0:T(128)} %bitcast.1.me_ref, ...), custom_call_target="tpu_custom_call" | custom-call | flops 1073741824 | bytes 4194304 | tf_op jit(solution)/shard_map/pack/pallas_call | solution.py:586
  4.4 0.5 collective-permute-start.7
  5.0 2.9 %collective-permute-start.1 = (bf16[144,512]{1,0:T(8,128)(2,1)}, bf16[144,512]{1,0:T(8,128)(2,1)S(1)}, u32[]{:S(2)}, u32[]{:S(2)}) collective-permute-start(bf16[144,512]{1,0:T(8,128)(2,1)} %get-tuple-element.73), channel_id=1, source_target_pairs={{0,8},{4,12},{8,0},{12,4},{16,24},{20,28},{24,16},{28,20},{1,9},{5... | collective-permute-start | bytes 442376 | tf_op jit(solution)/shard_map/ppermute | solution.py:414
  7.9 1.5 %collective-permute-start.3 = (bf16[144,512]{1,0:T(8,128)(2,1)}, bf16[144,512]{1,0:T(8,128)(2,1)S(1)}, u32[]{:S(2)}, u32[]{:S(2)}) collective-permute-start(bf16[144,512]{1,0:T(8,128)(2,1)} %get-tuple-element.75), channel_id=1, source_target_pairs={{0,16},{4,20},{8,24},{12,28},{16,0},{20,4},{24,8},{28,12},{1,17},{... | collective-permute-start | bytes 442376 | tf_op jit(solution)/shard_map/ppermute | solution.py:414
  9.7 3.0 %collective-permute-done.1.refs_2_ = bf16[144,512]{1,0:T(8,128)(2,1)S(1)} collective-permute-done((bf16[144,512]{1,0:T(8,128)(2,1)}, bf16[144,512]{1,0:T(8,128)(2,1)S(1)}, u32[]{:S(2)}, u32[]{:S(2)}) %collective-permute-start.1) | collective-permute-done | bytes 147488 | tf_op jit(solution)/shard_map/ppermute | solution.py:414
  12.7 3.0 %collective-permute-start.5 = (bf16[144,512]{1,0:T(8,128)(2,1)}, bf16[144,512]{1,0:T(8,128)(2,1)S(1)}, u32[]{:S(2)}, u32[]{:S(2)}) collective-permute-start(bf16[144,512]{1,0:T(8,128)(2,1)} %get-tuple-element.77), channel_id=1, source_target_pairs={{0,24},{4,28},{8,16},{12,20},{16,8},{20,12},{24,0},{28,4},{1,25},{... | collective-permute-start | bytes 442376 | tf_op jit(solution)/shard_map/ppermute | solution.py:414
  15.8 1.0 copy-done.5
  16.9 0.7 copy-done.12
  17.6 5.7 %collective-permute-done.4.refs_5_ = bf16[144,512]{1,0:T(8,128)(2,1)S(1)} collective-permute-done((bf16[144,512]{1,0:T(8,128)(2,1)}, bf16[144,512]{1,0:T(8,128)(2,1)S(1)}, u32[]{:S(2)}, u32[]{:S(2)}) %collective-permute-start.4) | collective-permute-done | bytes 147488 | tf_op jit(solution)/shard_map/ppermute | solution.py:414
  23.3 3.0 %collective-permute-start.10 = (bf16[256,512]{1,0:T(8,128)(2,1)S(1)}, bf16[256,512]{1,0:T(8,128)(2,1)S(1)}, u32[]{:S(2)}, u32[]{:S(2)}) collective-permute-start(bf16[256,512]{1,0:T(8,128)(2,1)S(1)} %get-tuple-element.103), channel_id=1, source_target_pairs={{0,24},{4,28},{8,16},{12,20},{16,8},{20,12},{24,0},{28,4},{1,25},{... | collective-permute-start | bytes 786440 | tf_op jit(solution)/shard_map/ppermute | solution.py:421
  26.3 0.4 collective-permute-start.8
  27.0 9.8 %forward.1 = (s32[1,1024]{1,0:T(1,128)}, f32[512,512]{1,0:T(8,128)}, f32[512,128]{1,0:T(8,128)}, bf16[512,512]{1,0:T(8,128)(2,1)}, bf16[512,1536]{1,0:T(8,128)(2...) custom-call(bf16[512,1536]{1,0:T(8,128)(2,1)} %refs_2_.1, f32[1,512]{1,0:T(1,128)} %bitcast.24, ...), custom_call_target="tpu_custom_call" | custom-call | flops 2952790016 | bytes 16777216 | tf_op jit(solution)/shard_map/forward/pallas_call | solution.py:615
  36.8 1.9 %collective-permute-done.8.refs_7_ = bf16[256,512]{1,0:T(8,128)(2,1)S(1)} collective-permute-done((bf16[256,512]{1,0:T(8,128)(2,1)S(1)}, bf16[256,512]{1,0:T(8,128)(2,1)S(1)}, u32[]{:S(2)}, u32[]{:S(2)}) %collective-permute-start.8) | collective-permute-done | bytes 262176 | tf_op jit(solution)/shard_map/ppermute | solution.py:421
  38.7 0.7 copy-done.14
  39.5 15.5 %backward.1 = (f32[128,2176]{1,0:T(8,128)}, f32[128,2176]{1,0:T(8,128)}, f32[128,2176]{1,0:T(8,128)}, f32[128,2176]{1,0:T(8,128)}, bf16[512,512]{1,0:T(8,128)(2,1)}, /*index=5*/f32[512,512]{1,0:T(8,128)}) custom-call(s32[1]{0:T(128)} %bitcast.1.me_ref, s32[1,1024]{1,0:T(1,128)} %get-tuple-element.93.pos_ref, bf16[512,512]{1,0:T(8,128)(2,1)} %w_proj_ref.1, ...), custom_call_target="tpu_custom_call" | custom-call | flops 4294967296 | bytes 16777216 | tf_op jit(solution)/shard_map/backward/pallas_call | solution.py:651
  55.1 0.5 collective-permute-start.11
  55.6 2.5 %collective-permute-done.12.refs_1_ = f32[128,2176]{1,0:T(8,128)S(1)} collective-permute-done((f32[128,2176]{1,0:T(8,128)}, f32[128,2176]{1,0:T(8,128)S(1)}, u32[]{:S(2)}, u32[]{:S(2)}) %collective-permute-start.12) | collective-permute-done | bytes 1114144 | tf_op jit(solution)/shard_map/ppermute | solution.py:481
  58.0 1.2 copy-done.1
  59.6 1.6 %collective-permute-start.13 = (s16[128,2176]{1,0:T(8,128)(2,1)S(1)}, s16[128,2176]{1,0:T(8,128)(2,1)S(1)}, u32[]{:S(2)}, u32[]{:S(2)}) collective-permute-start(s16[128,2176]{1,0:T(8,128)(2,1)S(1)} %code_first.1), channel_id=1, source_target_pairs={{0,8},{4,20},{8,0},{12,28},{16,24},{20,4},{24,16},{28,12},{1,9},{5... | collective-permute-start | bytes 1671176 | tf_op jit(solution)/shard_map/ppermute | solution.py:484
  61.2 8.0 %collective-permute-done.13.refs_2_ = s16[128,2176]{1,0:T(8,128)(2,1)S(1)} collective-permute-done((s16[128,2176]{1,0:T(8,128)(2,1)S(1)}, s16[128,2176]{1,0:T(8,128)(2,1)S(1)}, u32[]{:S(2)}, u32[]{:S(2)}) %collective-permute-start.13) | collective-permute-done | bytes 557088 | tf_op jit(solution)/shard_map/ppermute | solution.py:484
  69.5 1.4 %collective-permute-start.14 = (s16[64,2176]{1,0:T(8,128)(2,1)S(1)}, s16[64,2176]{1,0:T(8,128)(2,1)S(1)}, u32[]{:S(2)}, u32[]{:S(2)}) collective-permute-start(s16[64,2176]{1,0:T(8,128)(2,1)S(1)} %code_second.1), channel_id=1, source_target_pairs={{0,16},{4,12},{8,24},{12,4},{16,0},{20,28},{24,8},{28,20},{1,17},{... | collective-permute-start | bytes 835592 | tf_op jit(solution)/shard_map/ppermute | solution.py:489
  70.9 1.9 %residual.1 = (bf16[256,512]{1,0:T(8,128)(2,1)S(1)}, bf16[256,512]{1,0:T(8,128)(2,1)}, bf16[256,512]{1,0:T(8,128)(2,1)}, bf16[256,512]{1,0:T(8,128)(2,1)}) custom-call(s32[1,1024]{1,0:T(1,128)S(1)} %copy-done.9, f32[1,512]{1,0:T(1,128)S(1)} %bitcast.25, f32[512,128]{1,0:T(8,128)S(1)} %copy-done.8, f32[512,512]{1,0:T(8,128)S(1)} %copy-done.2, ...), custom_call_target="tpu_custom_call" | custom-call | flops 7876608 | bytes 3938304 | tf_op jit(solution)/shard_map/residual/pallas_call | solution.py:459
  72.8 3.3 %collective-permute-done.14.refs_3_ = s16[64,2176]{1,0:T(8,128)(2,1)S(1)} collective-permute-done((s16[64,2176]{1,0:T(8,128)(2,1)S(1)}, s16[64,2176]{1,0:T(8,128)(2,1)S(1)}, u32[]{:S(2)}, u32[]{:S(2)}) %collective-permute-start.14) | collective-permute-done | bytes 278560 | tf_op jit(solution)/shard_map/ppermute | solution.py:489
  76.1 0.7 copy-done.6
  76.8 1.5 %collective-permute-start.18 = (bf16[256,512]{1,0:T(8,128)(2,1)}, bf16[256,512]{1,0:T(8,128)(2,1)S(1)}, u32[]{:S(2)}, u32[]{:S(2)}) collective-permute-start(bf16[256,512]{1,0:T(8,128)(2,1)} %get-tuple-element.121), channel_id=1, source_target_pairs={{0,8},{4,12},{8,0},{12,4},{16,24},{20,28},{24,16},{28,20},{1,9},{5... | collective-permute-start | bytes 786440 | tf_op jit(solution)/shard_map/ppermute | solution.py:421
  78.4 1.3 %collective-permute-start.19 = (bf16[256,512]{1,0:T(8,128)(2,1)}, bf16[256,512]{1,0:T(8,128)(2,1)}, u32[]{:S(2)}, u32[]{:S(2)}) collective-permute-start(bf16[256,512]{1,0:T(8,128)(2,1)} %get-tuple-element.122), channel_id=1, source_target_pairs={{0,16},{4,20},{8,24},{12,28},{16,0},{20,4},{24,8},{28,12},{1,17},{... | collective-permute-start | bytes 786440 | tf_op jit(solution)/shard_map/ppermute | solution.py:421
  79.7 0.6 collective-permute-start.20
  80.3 1.0 copy-done.7
  81.3 0.5 code_planes.1
  81.8 1.6 %collective-permute-start.15 = (s16[16,2176]{1,0:T(8,128)(2,1)S(1)}, s16[16,2176]{1,0:T(8,128)(2,1)S(1)}, u32[]{:S(2)}, u32[]{:S(2)}) collective-permute-start(s16[16,2176]{1,0:T(8,128)(2,1)S(1)} %get-tuple-element.117), channel_id=1, source_target_pairs={{0,1},{1,0},{2,3},{3,2},{4,5},{5,4},{6,7},{7,6},{8,9},{9,8},{10,11... | collective-permute-start | bytes 208904 | tf_op jit(solution)/shard_map/ppermute | solution.py:414
  83.4 2.6 %collective-permute-start.16 = (s16[16,2176]{1,0:T(8,128)(2,1)S(1)}, s16[16,2176]{1,0:T(8,128)(2,1)S(1)}, u32[]{:S(2)}, u32[]{:S(2)}) collective-permute-start(s16[16,2176]{1,0:T(8,128)(2,1)S(1)} %get-tuple-element.118), channel_id=1, source_target_pairs={{0,2},{1,3},{2,0},{3,1},{4,6},{5,7},{6,4},{7,5},{8,10},{9,11},{10,... | collective-permute-start | bytes 208904 | tf_op jit(solution)/shard_map/ppermute | solution.py:414
  86.2 3.5 %collective-permute-start.17 = (s16[16,2176]{1,0:T(8,128)(2,1)S(1)}, s16[16,2176]{1,0:T(8,128)(2,1)S(1)}, u32[]{:S(2)}, u32[]{:S(2)}) collective-permute-start(s16[16,2176]{1,0:T(8,128)(2,1)S(1)} %get-tuple-element.119), channel_id=1, source_target_pairs={{0,3},{1,2},{2,1},{3,0},{4,7},{5,6},{6,5},{7,4},{8,11},{9,10},{10,... | collective-permute-start | bytes 208904 | tf_op jit(solution)/shard_map/ppermute | solution.py:414
  89.9 2.6 %collective-permute-done.17.refs_3_ = s16[16,2176]{1,0:T(8,128)(2,1)S(1)} collective-permute-done((s16[16,2176]{1,0:T(8,128)(2,1)S(1)}, s16[16,2176]{1,0:T(8,128)(2,1)S(1)}, u32[]{:S(2)}, u32[]{:S(2)}) %collective-permute-start.17) | collective-permute-done | bytes 69664 | tf_op jit(solution)/shard_map/ppermute | solution.py:414
  92.7 0.6 collective-permute-start.21
  93.3 3.5 %collective-permute-start.22 = (bf16[16,2176]{1,0:T(8,128)(2,1)S(1)}, bf16[16,2176]{1,0:T(8,128)(2,1)S(1)}, u32[]{:S(2)}, u32[]{:S(2)}) collective-permute-start(bf16[16,2176]{1,0:T(8,128)(2,1)S(1)} %finish.1), channel_id=1, source_target_pairs={{0,2},{1,3},{2,0},{3,1},{4,6},{5,7},{6,4},{7,5},{8,10},{9,11},{10,... | collective-permute-start | bytes 208904 | tf_op jit(solution)/shard_map/ppermute | solution.py:414
  97.2 0.7 collective-permute-done.21
  97.8 2.0 %collective-permute-done.22 = bf16[16,2176]{1,0:T(8,128)(2,1)S(1)} collective-permute-done((bf16[16,2176]{1,0:T(8,128)(2,1)S(1)}, bf16[16,2176]{1,0:T(8,128)(2,1)S(1)}, u32[]{:S(2)}, u32[]{:S(2)}) %collective-permute-start.22) | collective-permute-done | bytes 69664 | tf_op jit(solution)/shard_map/ppermute | solution.py:414
  99.8 3.1 %collective-permute-done.23 = bf16[16,2176]{1,0:T(8,128)(2,1)S(1)} collective-permute-done((bf16[16,2176]{1,0:T(8,128)(2,1)S(1)}, bf16[16,2176]{1,0:T(8,128)(2,1)S(1)}, u32[]{:S(2)}, u32[]{:S(2)}) %collective-permute-start.23) | collective-permute-done | bytes 69664 | tf_op jit(solution)/shard_map/ppermute | solution.py:414
  103.1 1.4 %collective-permute-start.24 = (bf16[64,2176]{1,0:T(8,128)(2,1)S(1)}, bf16[64,2176]{1,0:T(8,128)(2,1)S(1)}, u32[]{:S(2)}, u32[]{:S(2)}) collective-permute-start(bf16[64,2176]{1,0:T(8,128)(2,1)S(1)} %pad_maximum_fusion.1), channel_id=1, source_target_pairs={{0,16},{4,12},{8,24},{12,4},{16,0},{20,28},{24,8},{28,20},{1,17},{... | collective-permute-start | bytes 835592 | tf_op jit(solution)/shard_map/ppermute | solution.py:534
  104.5 8.2 %collective-permute-done.24 = bf16[64,2176]{1,0:T(8,128)(2,1)S(1)} collective-permute-done((bf16[64,2176]{1,0:T(8,128)(2,1)S(1)}, bf16[64,2176]{1,0:T(8,128)(2,1)S(1)}, u32[]{:S(2)}, u32[]{:S(2)}) %collective-permute-start.24) | collective-permute-done | bytes 278560 | tf_op jit(solution)/shard_map/ppermute | solution.py:534
  112.8 1.6 %collective-permute-start.25 = (bf16[128,2176]{1,0:T(8,128)(2,1)S(1)}, bf16[128,2176]{1,0:T(8,128)(2,1)S(1)}, u32[]{:S(2)}, u32[]{:S(2)}) collective-permute-start(bf16[128,2176]{1,0:T(8,128)(2,1)S(1)} %broadcast_select_fusion), channel_id=1, source_target_pairs={{0,8},{4,20},{8,0},{12,28},{16,24},{20,4},{24,16},{28,12},{1,9},{5... | collective-permute-start | bytes 1671176 | tf_op jit(solution)/shard_map/ppermute | solution.py:534
  114.4 1.1 for_core_pair.1
  115.6 1.9 %collective-permute-done.26.cross_ref = bf16[512,512]{1,0:T(8,128)(2,1)S(1)} collective-permute-done((bf16[512,512]{1,0:T(8,128)(2,1)S(1)}, bf16[512,512]{1,0:T(8,128)(2,1)S(1)}, u32[]{:S(2)}, u32[]{:S(2)}) %collective-permute-start.26) | collective-permute-done | bytes 524320 | tf_op jit(solution)/shard_map/ppermute | solution.py:711
  117.5 2.6 %unpack.1 = bf16[512,512]{1,0:T(8,128)(2,1)} custom-call(s32[1,512]{1,0:T(1,128)S(1)} %copy-done.11, bf16[512,512]{1,0:T(8,128)(2,1)S(1)} %collective-permute-done.26.cross_ref, bf16[256,512]{1,0:T(8,128)(2,1)S(1)} %get-tuple-element.126.refs_0_, bf16[256,512]{1,0:T(8,128)(2,1)S(1)} %collective-permute-done.18.refs_1_, ...), custom_call_target="tpu_custom_call" | custom-call | flops 4198400 | bytes 2099200 | tf_op jit(solution)/shard_map/unpack/pallas_call | solution.py:459
  120.0 2.4 %collective-permute-done.25 = bf16[128,2176]{1,0:T(8,128)(2,1)S(1)} collective-permute-done((bf16[128,2176]{1,0:T(8,128)(2,1)S(1)}, bf16[128,2176]{1,0:T(8,128)(2,1)S(1)}, u32[]{:S(2)}, u32[]{:S(2)}) %collective-permute-start.25) | collective-permute-done | bytes 557088 | tf_op jit(solution)/shard_map/ppermute | solution.py:534
  122.7 1.4 %split.2 = (f32[512,1536]{1,0:T(8,128)}, f32[512,512]{1,0:T(8,128)}, f32[1,512]{1,0:T(1,128)}) custom-call(s32[1]{0:T(128)S(6)} %and.19.side_ref, bf16[256,2176]{1,0:T(8,128)(2,1)S(1)} %maximum_select_fusion.sums_ref), custom_call_target="tpu_custom_call" | custom-call | bytes 4194304 | tf_op jit(solution)/shard_map/split/pallas_call | solution.py:543
  124.1 1.3 %collective-permute-done.27.sums_ref = bf16[256,2176]{1,0:T(8,128)(2,1)S(1)} collective-permute-done((bf16[256,2176]{1,0:T(8,128)(2,1)S(1)}, bf16[256,2176]{1,0:T(8,128)(2,1)S(1)}, u32[]{:S(2)}, u32[]{:S(2)}) %collective-permute-start.27) | collective-permute-done | bytes 1114144 | tf_op jit(solution)/shard_map/ppermute | solution.py:715
  125.5 1.3 %split.3 = (f32[512,1536]{1,0:T(8,128)}, f32[512,512]{1,0:T(8,128)}, f32[1,512]{1,0:T(1,128)}) custom-call(s32[1]{0:T(128)S(6)} %sub.3.side_ref, bf16[256,2176]{1,0:T(8,128)(2,1)S(1)} %collective-permute-done.27.sums_ref, f32[512,1536]{1,0:T(8,128)} %get-tuple-element.132.refs_0_, ...), custom_call_target="tpu_custom_call", output_to_operand_aliasing={{0}: (2, {}), {1}: (3, {}), {2}: (4, {})} | custom-call | bytes 4194304 | tf_op jit(solution)/shard_map/split/pallas_call | solution.py:543
  (80 shorter events, 3.1 us)
Async XLA Ops:
  4.4 11.4 %collective-permute-start.7 = (bf16[512,512]{1,0:T(8,128)(2,1)}, bf16[512,512]{1,0:T(8,128)(2,1)S(1)}, u32[]{:S(2)}, u32[]{:S(2)}) collective-permute-start(bf16[512,512]{1,0:T(8,128)(2,1)} %get-tuple-element.80), channel_id=1, source_target_pairs={{0,4},{4,0},{8,12},{12,8},{16,20},{20,16},{24,28},{28,24},{1,5},{5... | collective-permute-start | bytes 1572872 | tf_op jit(solution)/shard_map/ppermute | solution.py:609
  4.9 4.5 %collective-permute-start = (bf16[144,512]{1,0:T(8,128)(2,1)}, bf16[144,512]{1,0:T(8,128)(2,1)S(1)}, u32[]{:S(2)}, u32[]{:S(2)}) collective-permute-start(bf16[144,512]{1,0:T(8,128)(2,1)} %get-tuple-element.72), channel_id=1, source_target_pairs={{0,4},{4,0},{8,12},{12,8},{16,20},{20,16},{24,28},{28,24},{1,5},{5... | collective-permute-start | bytes 442376 | tf_op jit(solution)/shard_map/ppermute | solution.py:414
  5.0 7.8 %collective-permute-start.1 = (bf16[144,512]{1,0:T(8,128)(2,1)}, bf16[144,512]{1,0:T(8,128)(2,1)S(1)}, u32[]{:S(2)}, u32[]{:S(2)}) collective-permute-start(bf16[144,512]{1,0:T(8,128)(2,1)} %get-tuple-element.73), channel_id=1, source_target_pairs={{0,8},{4,12},{8,0},{12,4},{16,24},{20,28},{24,16},{28,20},{1,9},{5... | collective-permute-start | bytes 442376 | tf_op jit(solution)/shard_map/ppermute | solution.py:414
  7.9 9.7 %collective-permute-start.2 = (bf16[144,512]{1,0:T(8,128)(2,1)}, bf16[144,512]{1,0:T(8,128)(2,1)S(1)}, u32[]{:S(2)}, u32[]{:S(2)}) collective-permute-start(bf16[144,512]{1,0:T(8,128)(2,1)} %get-tuple-element.74), channel_id=1, source_target_pairs={{0,12},{4,8},{8,4},{12,0},{16,28},{20,24},{24,20},{28,16},{1,13},{... | collective-permute-start | bytes 442376 | tf_op jit(solution)/shard_map/ppermute | solution.py:414
  7.9 9.7 %collective-permute-start.3 = (bf16[144,512]{1,0:T(8,128)(2,1)}, bf16[144,512]{1,0:T(8,128)(2,1)S(1)}, u32[]{:S(2)}, u32[]{:S(2)}) collective-permute-start(bf16[144,512]{1,0:T(8,128)(2,1)} %get-tuple-element.75), channel_id=1, source_target_pairs={{0,16},{4,20},{8,24},{12,28},{16,0},{20,4},{24,8},{28,12},{1,17},{... | collective-permute-start | bytes 442376 | tf_op jit(solution)/shard_map/ppermute | solution.py:414
  9.4 17.5 %copy-start.16 = (bf16[144,512]{1,0:T(8,128)(2,1)}, bf16[144,512]{1,0:T(8,128)(2,1)S(1)}, u32[]{:S(2)}) copy-start(bf16[144,512]{1,0:T(8,128)(2,1)S(1)} %collective-permute-done.refs_1_) | copy-start | bytes 442372
  9.4 13.8 %collective-permute-start.4 = (bf16[144,512]{1,0:T(8,128)(2,1)}, bf16[144,512]{1,0:T(8,128)(2,1)S(1)}, u32[]{:S(2)}, u32[]{:S(2)}) collective-permute-start(bf16[144,512]{1,0:T(8,128)(2,1)} %get-tuple-element.76), channel_id=1, source_target_pairs={{0,20},{4,16},{8,28},{12,24},{16,4},{20,0},{24,12},{28,8},{1,21},{... | collective-permute-start | bytes 442376 | tf_op jit(solution)/shard_map/ppermute | solution.py:414
  12.7 14.2 %copy-start.17 = (bf16[144,512]{1,0:T(8,128)(2,1)}, bf16[144,512]{1,0:T(8,128)(2,1)S(1)}, u32[]{:S(2)}) copy-start(bf16[144,512]{1,0:T(8,128)(2,1)S(1)} %collective-permute-done.1.refs_2_) | copy-start | bytes 442372
  12.7 10.5 %collective-permute-start.5 = (bf16[144,512]{1,0:T(8,128)(2,1)}, bf16[144,512]{1,0:T(8,128)(2,1)S(1)}, u32[]{:S(2)}, u32[]{:S(2)}) collective-permute-start(bf16[144,512]{1,0:T(8,128)(2,1)} %get-tuple-element.77), channel_id=1, source_target_pairs={{0,24},{4,28},{8,16},{12,20},{16,8},{20,12},{24,0},{28,4},{1,25},{... | collective-permute-start | bytes 442376 | tf_op jit(solution)/shard_map/ppermute | solution.py:414
  15.8 7.5 %collective-permute-start.6 = (bf16[144,512]{1,0:T(8,128)(2,1)}, bf16[144,512]{1,0:T(8,128)(2,1)S(1)}, u32[]{:S(2)}, u32[]{:S(2)}) collective-permute-start(bf16[144,512]{1,0:T(8,128)(2,1)} %get-tuple-element.78), channel_id=1, source_target_pairs={{0,28},{4,24},{8,20},{12,16},{16,12},{20,8},{24,4},{28,0},{1,29},{... | collective-permute-start | bytes 442376 | tf_op jit(solution)/shard_map/ppermute | solution.py:414
  15.8 1.0 copy-start.5
  17.6 9.3 %copy-start.18 = (bf16[144,512]{1,0:T(8,128)(2,1)}, bf16[144,512]{1,0:T(8,128)(2,1)S(1)}, u32[]{:S(2)}) copy-start(bf16[144,512]{1,0:T(8,128)(2,1)S(1)} %collective-permute-done.2.refs_3_) | copy-start | bytes 442372
  17.6 9.3 %copy-start.19 = (bf16[144,512]{1,0:T(8,128)(2,1)}, bf16[144,512]{1,0:T(8,128)(2,1)S(1)}, u32[]{:S(2)}) copy-start(bf16[144,512]{1,0:T(8,128)(2,1)S(1)} %collective-permute-done.3.refs_4_) | copy-start | bytes 442372
  23.3 3.7 %copy-start.20 = (bf16[144,512]{1,0:T(8,128)(2,1)}, bf16[144,512]{1,0:T(8,128)(2,1)S(1)}, u32[]{:S(2)}) copy-start(bf16[144,512]{1,0:T(8,128)(2,1)S(1)} %collective-permute-done.4.refs_5_) | copy-start | bytes 442372
  23.3 3.7 %copy-start.21 = (bf16[144,512]{1,0:T(8,128)(2,1)}, bf16[144,512]{1,0:T(8,128)(2,1)S(1)}, u32[]{:S(2)}) copy-start(bf16[144,512]{1,0:T(8,128)(2,1)S(1)} %collective-permute-done.5.refs_6_) | copy-start | bytes 442372
  23.3 3.7 %copy-start.22 = (bf16[144,512]{1,0:T(8,128)(2,1)}, bf16[144,512]{1,0:T(8,128)(2,1)S(1)}, u32[]{:S(2)}) copy-start(bf16[144,512]{1,0:T(8,128)(2,1)S(1)} %collective-permute-done.6.refs_7_) | copy-start | bytes 442372
  23.3 13.5 %collective-permute-start.10 = (bf16[256,512]{1,0:T(8,128)(2,1)S(1)}, bf16[256,512]{1,0:T(8,128)(2,1)S(1)}, u32[]{:S(2)}, u32[]{:S(2)}) collective-permute-start(bf16[256,512]{1,0:T(8,128)(2,1)S(1)} %get-tuple-element.103), channel_id=1, source_target_pairs={{0,24},{4,28},{8,16},{12,20},{16,8},{20,12},{24,0},{28,4},{1,25},{... | collective-permute-start | bytes 786440 | tf_op jit(solution)/shard_map/ppermute | solution.py:421
  26.3 12.4 %collective-permute-start.8 = (bf16[256,512]{1,0:T(8,128)(2,1)S(1)}, bf16[256,512]{1,0:T(8,128)(2,1)S(1)}, u32[]{:S(2)}, u32[]{:S(2)}) collective-permute-start(bf16[256,512]{1,0:T(8,128)(2,1)S(1)} %get-tuple-element.101), channel_id=1, source_target_pairs={{0,8},{4,12},{8,0},{12,4},{16,24},{20,28},{24,16},{28,20},{1,9},{5... | collective-permute-start | bytes 786440 | tf_op jit(solution)/shard_map/ppermute | solution.py:421
  26.7 12.0 %collective-permute-start.9 = (bf16[256,512]{1,0:T(8,128)(2,1)S(1)}, bf16[256,512]{1,0:T(8,128)(2,1)S(1)}, u32[]{:S(2)}, u32[]{:S(2)}) collective-permute-start(bf16[256,512]{1,0:T(8,128)(2,1)S(1)} %get-tuple-element.102), channel_id=1, source_target_pairs={{0,16},{4,20},{8,24},{12,28},{16,0},{20,4},{24,8},{28,12},{1,17},{... | collective-permute-start | bytes 786440 | tf_op jit(solution)/shard_map/ppermute | solution.py:421
  36.8 1.9 %copy-start.13 = (bf16[256,512]{1,0:T(8,128)(2,1)}, bf16[256,512]{1,0:T(8,128)(2,1)S(1)}, u32[]{:S(2)}) copy-start(bf16[256,512]{1,0:T(8,128)(2,1)S(1)} %collective-permute-done.10.refs_9_) | copy-start | bytes 786436
  38.7 0.8 copy-start.15
  55.0 3.0 %collective-permute-start.12 = (f32[128,2176]{1,0:T(8,128)}, f32[128,2176]{1,0:T(8,128)S(1)}, u32[]{:S(2)}, u32[]{:S(2)}) collective-permute-start(f32[128,2176]{1,0:T(8,128)} %get-tuple-element.107), channel_id=1, source_target_pairs={{0,4},{4,0},{8,12},{12,8},{16,20},{20,16},{24,28},{28,24},{1,5},{5... | collective-permute-start | bytes 3342344 | tf_op jit(solution)/shard_map/ppermute | solution.py:481
  55.1 6.1 %collective-permute-start.11 = (f32[128,2176]{1,0:T(8,128)}, f32[128,2176]{1,0:T(8,128)S(1)}, u32[]{:S(2)}, u32[]{:S(2)}) collective-permute-start(f32[128,2176]{1,0:T(8,128)} %get-tuple-element.105), channel_id=1, source_target_pairs={{0,4},{4,0},{8,12},{12,8},{16,20},{20,16},{24,28},{28,24},{1,5},{5... | collective-permute-start | bytes 3342344 | tf_op jit(solution)/shard_map/ppermute | solution.py:482
  58.0 1.2 copy-start.1
  59.3 9.9 %copy-start = (f32[128,2176]{1,0:T(8,128)S(1)}, f32[128,2176]{1,0:T(8,128)}, u32[]{:S(2)}) copy-start(f32[128,2176]{1,0:T(8,128)} %get-tuple-element.104.refs_0_) | copy-start | bytes 3342340
  59.6 9.6 %collective-permute-start.13 = (s16[128,2176]{1,0:T(8,128)(2,1)S(1)}, s16[128,2176]{1,0:T(8,128)(2,1)S(1)}, u32[]{:S(2)}, u32[]{:S(2)}) collective-permute-start(s16[128,2176]{1,0:T(8,128)(2,1)S(1)} %code_first.1), channel_id=1, source_target_pairs={{0,8},{4,20},{8,0},{12,28},{16,24},{20,4},{24,16},{28,12},{1,9},{5... | collective-permute-start | bytes 1671176 | tf_op jit(solution)/shard_map/ppermute | solution.py:484
  69.2 1.7 %copy-start.2 = (f32[512,512]{1,0:T(8,128)S(1)}, f32[512,512]{1,0:T(8,128)}, u32[]{:S(2)}) copy-start(f32[512,512]{1,0:T(8,128)} %get-tuple-element.97.refs_3_.xhat_ref) | copy-start | bytes 3145732
  69.2 1.7 %copy-start.3 = (f32[512,512]{1,0:T(8,128)S(1)}, f32[512,512]{1,0:T(8,128)}, u32[]{:S(2)}) copy-start(f32[512,512]{1,0:T(8,128)} %get-tuple-element.110.d_normed_ref) | copy-start | bytes 3145732
  69.2 1.7 %copy-start.4 = (bf16[512,512]{1,0:T(8,128)(2,1)S(1)}, bf16[512,512]{1,0:T(8,128)(2,1)}, u32[]{:S(2)}) copy-start(bf16[512,512]{1,0:T(8,128)(2,1)} %get-tuple-element.109.serial_grad_ref) | copy-start | bytes 1572868
  69.2 1.7 %copy-start.8 = (f32[512,128]{1,0:T(8,128)S(1)}, f32[512,128]{1,0:T(8,128)}, u32[]{:S(2)}) copy-start(f32[512,128]{1,0:T(8,128)} %get-tuple-element.108.inv_ref) | copy-start | bytes 786436
  69.2 1.7 %copy-start.9 = (s32[1,1024]{1,0:T(1,128)S(1)}, s32[1,1024]{1,0:T(1,128)}, u32[]{:S(2)}) copy-start(s32[1,1024]{1,0:T(1,128)} %get-tuple-element.93.pos_ref) | copy-start | bytes 12292
  69.2 1.7 %copy-start.10 = (f32[512]{0:T(512)S(1)}, f32[512]{0:T(512)}, u32[]{:S(2)}) copy-start(f32[512]{0:T(512)} %param.11) | copy-start | bytes 6148
  69.5 6.6 %collective-permute-start.14 = (s16[64,2176]{1,0:T(8,128)(2,1)S(1)}, s16[64,2176]{1,0:T(8,128)(2,1)S(1)}, u32[]{:S(2)}, u32[]{:S(2)}) collective-permute-start(s16[64,2176]{1,0:T(8,128)(2,1)S(1)} %code_second.1), channel_id=1, source_target_pairs={{0,16},{4,12},{8,24},{12,4},{16,0},{20,28},{24,8},{28,20},{1,17},{... | collective-permute-start | bytes 835592 | tf_op jit(solution)/shard_map/ppermute | solution.py:489
  76.8 15.9 %collective-permute-start.18 = (bf16[256,512]{1,0:T(8,128)(2,1)}, bf16[256,512]{1,0:T(8,128)(2,1)S(1)}, u32[]{:S(2)}, u32[]{:S(2)}) collective-permute-start(bf16[256,512]{1,0:T(8,128)(2,1)} %get-tuple-element.121), channel_id=1, source_target_pairs={{0,8},{4,12},{8,0},{12,4},{16,24},{20,28},{24,16},{28,20},{1,9},{5... | collective-permute-start | bytes 786440 | tf_op jit(solution)/shard_map/ppermute | solution.py:421
  78.4 14.3 %collective-permute-start.19 = (bf16[256,512]{1,0:T(8,128)(2,1)}, bf16[256,512]{1,0:T(8,128)(2,1)}, u32[]{:S(2)}, u32[]{:S(2)}) collective-permute-start(bf16[256,512]{1,0:T(8,128)(2,1)} %get-tuple-element.122), channel_id=1, source_target_pairs={{0,16},{4,20},{8,24},{12,28},{16,0},{20,4},{24,8},{28,12},{1,17},{... | collective-permute-start | bytes 786440 | tf_op jit(solution)/shard_map/ppermute | solution.py:421
  79.7 13.0 %collective-permute-start.20 = (bf16[256,512]{1,0:T(8,128)(2,1)}, bf16[256,512]{1,0:T(8,128)(2,1)}, u32[]{:S(2)}, u32[]{:S(2)}) collective-permute-start(bf16[256,512]{1,0:T(8,128)(2,1)} %get-tuple-element.123), channel_id=1, source_target_pairs={{0,24},{4,28},{8,16},{12,20},{16,8},{20,12},{24,0},{28,4},{1,25},{... | collective-permute-start | bytes 786440 | tf_op jit(solution)/shard_map/ppermute | solution.py:421
  80.3 1.0 copy-start.7
  81.8 4.4 %collective-permute-start.15 = (s16[16,2176]{1,0:T(8,128)(2,1)S(1)}, s16[16,2176]{1,0:T(8,128)(2,1)S(1)}, u32[]{:S(2)}, u32[]{:S(2)}) collective-permute-start(s16[16,2176]{1,0:T(8,128)(2,1)S(1)} %get-tuple-element.117), channel_id=1, source_target_pairs={{0,1},{1,0},{2,3},{3,2},{4,5},{5,4},{6,7},{7,6},{8,9},{9,8},{10,11... | collective-permute-start | bytes 208904 | tf_op jit(solution)/shard_map/ppermute | solution.py:414
  83.4 6.5 %collective-permute-start.16 = (s16[16,2176]{1,0:T(8,128)(2,1)S(1)}, s16[16,2176]{1,0:T(8,128)(2,1)S(1)}, u32[]{:S(2)}, u32[]{:S(2)}) collective-permute-start(s16[16,2176]{1,0:T(8,128)(2,1)S(1)} %get-tuple-element.118), channel_id=1, source_target_pairs={{0,2},{1,3},{2,0},{3,1},{4,6},{5,7},{6,4},{7,5},{8,10},{9,11},{10,... | collective-permute-start | bytes 208904 | tf_op jit(solution)/shard_map/ppermute | solution.py:414
  86.2 6.3 %collective-permute-start.17 = (s16[16,2176]{1,0:T(8,128)(2,1)S(1)}, s16[16,2176]{1,0:T(8,128)(2,1)S(1)}, u32[]{:S(2)}, u32[]{:S(2)}) collective-permute-start(s16[16,2176]{1,0:T(8,128)(2,1)S(1)} %get-tuple-element.119), channel_id=1, source_target_pairs={{0,3},{1,2},{2,1},{3,0},{4,7},{5,6},{6,5},{7,4},{8,11},{9,10},{10,... | collective-permute-start | bytes 208904 | tf_op jit(solution)/shard_map/ppermute | solution.py:414
  92.7 5.1 %collective-permute-start.21 = (bf16[16,2176]{1,0:T(8,128)(2,1)S(1)}, bf16[16,2176]{1,0:T(8,128)(2,1)S(1)}, u32[]{:S(2)}, u32[]{:S(2)}) collective-permute-start(bf16[16,2176]{1,0:T(8,128)(2,1)S(1)} %finish.1), channel_id=1, source_target_pairs={{0,1},{1,0},{2,3},{3,2},{4,5},{5,4},{6,7},{7,6},{8,9},{9,8},{10,11... | collective-permute-start | bytes 208904 | tf_op jit(solution)/shard_map/ppermute | solution.py:414
  93.3 6.5 %collective-permute-start.22 = (bf16[16,2176]{1,0:T(8,128)(2,1)S(1)}, bf16[16,2176]{1,0:T(8,128)(2,1)S(1)}, u32[]{:S(2)}, u32[]{:S(2)}) collective-permute-start(bf16[16,2176]{1,0:T(8,128)(2,1)S(1)} %finish.1), channel_id=1, source_target_pairs={{0,2},{1,3},{2,0},{3,1},{4,6},{5,7},{6,4},{7,5},{8,10},{9,11},{10,... | collective-permute-start | bytes 208904 | tf_op jit(solution)/shard_map/ppermute | solution.py:414
  96.8 6.1 %collective-permute-start.23 = (bf16[16,2176]{1,0:T(8,128)(2,1)S(1)}, bf16[16,2176]{1,0:T(8,128)(2,1)S(1)}, u32[]{:S(2)}, u32[]{:S(2)}) collective-permute-start(bf16[16,2176]{1,0:T(8,128)(2,1)S(1)} %finish.1), channel_id=1, source_target_pairs={{0,3},{1,2},{2,1},{3,0},{4,7},{5,6},{6,5},{7,4},{8,11},{9,10},{10,... | collective-permute-start | bytes 208904 | tf_op jit(solution)/shard_map/ppermute | solution.py:414
  103.1 9.6 %collective-permute-start.24 = (bf16[64,2176]{1,0:T(8,128)(2,1)S(1)}, bf16[64,2176]{1,0:T(8,128)(2,1)S(1)}, u32[]{:S(2)}, u32[]{:S(2)}) collective-permute-start(bf16[64,2176]{1,0:T(8,128)(2,1)S(1)} %pad_maximum_fusion.1), channel_id=1, source_target_pairs={{0,16},{4,12},{8,24},{12,4},{16,0},{20,28},{24,8},{28,20},{1,17},{... | collective-permute-start | bytes 835592 | tf_op jit(solution)/shard_map/ppermute | solution.py:534
  112.8 4.6 %copy-start.11 = (s32[1,512]{1,0:T(1,128)S(1)}, s32[1,512]{1,0:T(1,128)}, u32[]{:S(2)}) copy-start(s32[1,512]{1,0:T(1,128)} %get-tuple-element.125.slot_ref) | copy-start | bytes 6148
  112.8 9.6 %collective-permute-start.25 = (bf16[128,2176]{1,0:T(8,128)(2,1)S(1)}, bf16[128,2176]{1,0:T(8,128)(2,1)S(1)}, u32[]{:S(2)}, u32[]{:S(2)}) collective-permute-start(bf16[128,2176]{1,0:T(8,128)(2,1)S(1)} %broadcast_select_fusion), channel_id=1, source_target_pairs={{0,8},{4,20},{8,0},{12,28},{16,24},{20,4},{24,16},{28,12},{1,9},{5... | collective-permute-start | bytes 1671176 | tf_op jit(solution)/shard_map/ppermute | solution.py:534
  115.5 2.0 %collective-permute-start.26 = (bf16[512,512]{1,0:T(8,128)(2,1)S(1)}, bf16[512,512]{1,0:T(8,128)(2,1)S(1)}, u32[]{:S(2)}, u32[]{:S(2)}) collective-permute-start(bf16[512,512]{1,0:T(8,128)(2,1)S(1)} %for_core_pair.1), channel_id=1, source_target_pairs={{0,4},{4,0},{8,12},{12,8},{16,20},{20,16},{24,28},{28,24},{1,5},{5... | collective-permute-start | bytes 1572872 | tf_op jit(solution)/shard_map/ppermute | solution.py:711
  122.7 2.8 %collective-permute-start.27 = (bf16[256,2176]{1,0:T(8,128)(2,1)S(1)}, bf16[256,2176]{1,0:T(8,128)(2,1)S(1)}, u32[]{:S(2)}, u32[]{:S(2)}) collective-permute-start(bf16[256,2176]{1,0:T(8,128)(2,1)S(1)} %maximum_select_fusion.sums_ref), channel_id=1, source_target_pairs={{0,4},{4,0},{8,12},{12,8},{16,20},{20,16},{24,28},{28,24},{1,5},{5... | collective-permute-start | bytes 3342344 | tf_op jit(solution)/shard_map/ppermute | solution.py:715
  (3 other events, 2.1 us)

commit v15 on v14

--- a/solution.py
+++ b/solution.py
@@ -198,10 +198,16 @@
             )
         )
     ]
+    body, tail = pl.ds(0, 4 * width), pl.ds(4 * width, LANES)
     saves = [
         pltpu.make_async_copy(source, target, sems.at[6 + chips + i])
         for i, (source, target) in enumerate(
-            [*zip(sums, outs), (serial_grad, serial_grad_hbm), (d_normed_ref, d_normed_hbm)]
+            [
+                *[(source.at[:, body], target.at[:, body]) for source, target in zip(sums, outs)],
+                (serial_grad, serial_grad_hbm),
+                (d_normed_ref, d_normed_hbm),
+                *[(source.at[:, tail], target.at[:, tail]) for source, target in zip(sums, outs)],
+            ]
         )
     ]
 
@@ -255,11 +261,6 @@
 
     for load in loads[chips + 2 :]:
         load.wait()
-    d_normed = mm(d_qkv[...], w_ref[...], NT)
-    d_normed_ref[...] = d_normed
-    saves[5].start()
-    gain_row = jnp.sum(d_normed * xhat_ref[...], axis=0, keepdims=True)
-    gain_column[...] = jnp.transpose(jnp.broadcast_to(gain_row, (LANES, width)))
     eighth = width // 8
     odd = lax.bitwise_and(me, 1)
 
@@ -285,18 +286,27 @@
         parts = order[2 * i : 2 * i + 4]
         of_qkv = mm(jnp.concatenate([normed_ref[part, :] for part in parts], axis=0), d_qkv[...])
         of_proj = mm(jnp.concatenate([attn_ref[part, :] for part in parts], axis=0), serial_grad[...])
-        of_gain = jnp.concatenate([gain_column[part, :] for part in parts], axis=0)
         for j in range(2):
             lines = slice(2 * j * eighth, 2 * (j + 1) * eighth)
             sums[i + j][:, : 3 * width] = of_qkv[lines]
             sums[i + j][:, 3 * width : 4 * width] = of_proj[lines]
-            sums[i + j][:, 4 * width :] = of_gain[lines]
             saves[i + j].start()
+    d_normed = mm(d_qkv[...], w_ref[...], NT)
+    d_normed_ref[...] = d_normed
+    saves[5].start()
+    gain_row = jnp.sum(d_normed * xhat_ref[...], axis=0, keepdims=True)
+    gain_column[...] = jnp.transpose(jnp.broadcast_to(gain_row, (LANES, width)))
+    for i in range(4):
+        parts = order[2 * i : 2 * i + 2]
+        sums[i][:, 4 * width :] = jnp.concatenate([gain_column[part, :] for part in parts], axis=0)
+        saves[6 + i].start()
     for save in saves:
         save.wait()
 
 
-def residual_kernel(pos_ref, gain_ref, inv_ref, xhat_ref, serial_grad_ref, d_normed_ref, *outs):
+def residual_kernel(
+    capacity, pos_ref, gain_ref, inv_ref, xhat_ref, serial_grad_ref, d_normed_ref, same_out, cross_out
+):
     xhat = xhat_ref[...]
     rows = xhat.shape[0]
     scaled = d_normed_ref[...] * gain_ref[...]
@@ -307,23 +317,14 @@
     )
     serial_dx = (serial_grad_ref[...].astype(F32) + residual).astype(BF16)
     returned = mm(column_hot(pos_ref[...], rows), serial_dx).astype(BF16)
-    size = outs[0].shape[0]
-    for j, out in enumerate(outs):
-        out[...] = returned[j * size : (j + 1) * size]
-
-
-def cross_kernel(*refs):
-    size = refs[0].shape[0] // 2
-    for j, ref in enumerate(refs[:-1]):
-        refs[-1][j * size : (j + 1) * size, :] = ref[size:, :]
-
-
-def unpack_kernel(slot_ref, cross_ref, *refs):
-    size = refs[0].shape[0] // 2
-    blocks = []
-    for j, ref in enumerate(refs[:-1]):
-        blocks += [ref[:size, :], cross_ref[j * size : (j + 1) * size, :]]
-    values = jnp.concatenate(blocks, axis=0)
+    for j in range(same_out.shape[0] // capacity):
+        lines = slice(j * capacity, (j + 1) * capacity)
+        same_out[lines, :] = returned[2 * j * capacity : (2 * j + 1) * capacity]
+        cross_out[lines, :] = returned[(2 * j + 1) * capacity : (2 * j + 2) * capacity]
+
+
+def unpack_kernel(slot_ref, *refs):
+    values = jnp.concatenate([ref[...] for ref in refs[:-1]], axis=0)
     refs[-1][...] = mm(column_hot(slot_ref[...], values.shape[0]), values).astype(BF16)
 
 
@@ -603,12 +604,15 @@
         name="pack",
     )(me, dest, feats, grads)
     feats_got = by_distance(feats_sent, "seq")
-    messages = small_kernel(
-        functools.partial(pair_kernel, capacity),
-        [shape_of((2 * capacity, width), BF16)] * (n_seq // 2),
-        [same, lax.ppermute(cross, "seq", core_pairs())],
-        name="pair_up",
-    )
+    def by_core(same, cross):
+        return small_kernel(
+            functools.partial(pair_kernel, capacity),
+            [shape_of((2 * capacity, width), BF16)] * (n_seq // 2),
+            [same, lax.ppermute(cross, "seq", core_pairs())],
+            name="pair_up",
+        )
+
+    messages = by_core(same, cross)
     feats_got, messages = lax.optimization_barrier((feats_got, messages))
     grads_got = by_chip(messages)
 
@@ -678,7 +682,7 @@
             pltpu.VMEM((width, rows), BF16),
             pltpu.VMEM((rows, 3 * width), BF16),
             pltpu.VMEM((width, LANES), F32),
-            pltpu.SemaphoreType.DMA((12 + n_seq // 2,)),
+            pltpu.SemaphoreType.DMA((16 + n_seq // 2,)),
         ],
         compiler_params=params(60),
         cost_estimate=pl.CostEstimate(
@@ -691,25 +695,20 @@
 
     steps = chip_steps()
     terms = first_step(quarters, steps)
-    back = small_kernel(
-        residual_kernel,
-        [shape_of((2 * capacity, width), BF16)] * (n_seq // 2),
+    same, cross = small_kernel(
+        functools.partial(residual_kernel, capacity),
+        [shape_of((slots // 2, width), BF16)] * 2,
         [pos, gain_row, inv, xhat, serial_grad, d_normed],
         name="residual",
     )
+    back = by_core(same, cross)
     terms, got = second_step(terms, steps)
     got, back = lax.optimization_barrier((got, back))
     returned = by_chip(back)
     part, returned = lax.optimization_barrier((reduce_over_planes(terms, got, steps), returned))
-    cross = small_kernel(
-        cross_kernel, [shape_of((slots // 2, width), BF16)], returned, name="for_core_pair"
-    )[0]
     own = share_in_plane(share_over_planes(part), steps)
     grad_local = small_kernel(
-        unpack_kernel,
-        [shape_of((rows, width), BF16)],
-        [slot, lax.ppermute(cross, "seq", core_pairs()), *returned],
-        name="unpack",
+        unpack_kernel, [shape_of((rows, width), BF16)], [slot, *returned], name="unpack"
     )[0]
     own, grad_local = lax.optimization_barrier((own, grad_local))
     other = lax.ppermute(own, "seq", core_pairs())

time: 127 us -> 125 us (0.984)
  local copies, waits for them, and re-layouts: 5.75 us -> 4.08 us
  Pallas kernels: 38.6 us -> 37.1 us
    ppermute x2, waiting for transfers between devices: 10.6 us -> 13.7 us  [share_in_plane(): other = lax.ppermute(part, 'seq', pairs)]
    ppermute x2, waiting for transfers between devices: 1.89 us -> 0.01 us  [by_core(): lax.ppermute(cross, 'seq', core_pairs())]
    unnamed x54 -> x50, local copies, waits for them, and re-layouts: 5.73 us -> 4.07 us
  transfers between devices with their start and end apart: 28 -> 28, of which waited for: 16 -> 15; matrix products, arithmetic and copies ran while one was open for 0% -> 0% of each run, Pallas kernels for 14% -> 14%
where the time goes in v15:
time: 125 us
  waiting for transfers between devices  48 us (38%)
  Pallas kernels  37.1 us (30%)
  starting transfers between devices  34.2 us (27%)
  local copies, waits for them, and re-layouts  4.08 us (3%)
    ppermute x13, starting transfers between devices, by_distance(): lax.ppermute(blocks[k], axis, [(i, i ^ k) for i in range(count)])  20.1 us
    ppermute x13, waiting for transfers between devices, by_distance(): lax.ppermute(blocks[k], axis, [(i, i ^ k) for i in range(count)])  17.5 us
    pallas_call x1, Pallas kernels, per_device(): pl.pallas_call(functools.partial(backward_kernel, n_seq, chip_bits), grid...  14.8 us
    ppermute x2, waiting for transfers between devices, share_in_plane(): other = lax.ppermute(part, 'seq', pairs)  13.7 us
    pallas_call x1, Pallas kernels, per_device(): pl.pallas_call(functools.partial(forward_kernel, n_seq, capacity), grid=(...  9.86 us
    ppermute x6, starting transfers between devices, by_chip(): lax.ppermute(messages[j], 'seq', [(i, i ^ 2 * j) for i in range(count)])  7.1 us
    ppermute x1, waiting for transfers between devices, first_step(): return [own_keep, got_keep, lax.ppermute(sent, 'seq', steps[0][0])]  6.75 us
    pallas_call x8, Pallas kernels, small_kernel(): pl.pallas_call(kernel, out_shape=outs, in_specs=[in_smem] * scalars + [in...  5.98 us
  transfers between devices with their start and end apart: 28, of which 15 were waited for; matrix products, arithmetic and copies ran while one was open for 0% of the time, Pallas kernels for 14%

profile of v15, /device:TPU:0, one launch (start us, length us, event | category | flops | bytes accessed | tf_op | source)
XLA Modules:
  0.0 124.6 jit_solution(17303209939248523852)
XLA Ops:
  0.6 3.7 %pack.1 = (s32[1,512]{1,0:T(1,128)}, bf16[512,512]{1,0:T(8,128)(2,1)}, bf16[512,512]{1,0:T(8,128)(2,1)}, bf16[144,512]{1,0:T(8,128)(2,1)}, bf16[144,512]{1,0:T(8...) custom-call(s32[1]{0:T(128)} %bitcast.1.me_ref, ...), custom_call_target="tpu_custom_call" | custom-call | flops 1073741824 | bytes 4194304 | tf_op jit(solution)/shard_map/pack/pallas_call | solution.py:587
  4.4 0.5 collective-permute-start.7
  5.0 2.9 %collective-permute-start.1 = (bf16[144,512]{1,0:T(8,128)(2,1)}, bf16[144,512]{1,0:T(8,128)(2,1)S(1)}, u32[]{:S(2)}, u32[]{:S(2)}) collective-permute-start(bf16[144,512]{1,0:T(8,128)(2,1)} %get-tuple-element.75), channel_id=1, source_target_pairs={{0,8},{4,12},{8,0},{12,4},{16,24},{20,28},{24,16},{28,20},{1,9},{5... | collective-permute-start | bytes 442376 | tf_op jit(solution)/shard_map/ppermute | solution.py:415
  7.9 1.5 %collective-permute-start.3 = (bf16[144,512]{1,0:T(8,128)(2,1)}, bf16[144,512]{1,0:T(8,128)(2,1)S(1)}, u32[]{:S(2)}, u32[]{:S(2)}) collective-permute-start(bf16[144,512]{1,0:T(8,128)(2,1)} %get-tuple-element.77), channel_id=1, source_target_pairs={{0,16},{4,20},{8,24},{12,28},{16,0},{20,4},{24,8},{28,12},{1,17},{... | collective-permute-start | bytes 442376 | tf_op jit(solution)/shard_map/ppermute | solution.py:415
  9.4 0.3 collective-permute-start.4
  9.7 3.0 %collective-permute-done.1.refs_2_ = bf16[144,512]{1,0:T(8,128)(2,1)S(1)} collective-permute-done((bf16[144,512]{1,0:T(8,128)(2,1)}, bf16[144,512]{1,0:T(8,128)(2,1)S(1)}, u32[]{:S(2)}, u32[]{:S(2)}) %collective-permute-start.1) | collective-permute-done | bytes 147488 | tf_op jit(solution)/shard_map/ppermute | solution.py:415
  12.7 3.0 %collective-permute-start.5 = (bf16[144,512]{1,0:T(8,128)(2,1)}, bf16[144,512]{1,0:T(8,128)(2,1)S(1)}, u32[]{:S(2)}, u32[]{:S(2)}) collective-permute-start(bf16[144,512]{1,0:T(8,128)(2,1)} %get-tuple-element.79), channel_id=1, source_target_pairs={{0,24},{4,28},{8,16},{12,20},{16,8},{20,12},{24,0},{28,4},{1,25},{... | collective-permute-start | bytes 442376 | tf_op jit(solution)/shard_map/ppermute | solution.py:415
  15.8 1.0 copy-done.5
  16.9 0.7 copy-done.10
  17.6 5.6 %collective-permute-done.4.refs_5_ = bf16[144,512]{1,0:T(8,128)(2,1)S(1)} collective-permute-done((bf16[144,512]{1,0:T(8,128)(2,1)}, bf16[144,512]{1,0:T(8,128)(2,1)S(1)}, u32[]{:S(2)}, u32[]{:S(2)}) %collective-permute-start.4) | collective-permute-done | bytes 147488 | tf_op jit(solution)/shard_map/ppermute | solution.py:415
  23.3 3.0 %collective-permute-start.10 = (bf16[256,512]{1,0:T(8,128)(2,1)S(1)}, bf16[256,512]{1,0:T(8,128)(2,1)S(1)}, u32[]{:S(2)}, u32[]{:S(2)}) collective-permute-start(bf16[256,512]{1,0:T(8,128)(2,1)S(1)} %get-tuple-element.105), channel_id=1, source_target_pairs={{0,24},{4,28},{8,16},{12,20},{16,8},{20,12},{24,0},{28,4},{1,25},{... | collective-permute-start | bytes 786440 | tf_op jit(solution)/shard_map/ppermute | solution.py:422
  26.3 0.4 collective-permute-start.8
  27.0 9.9 %forward.1 = (s32[1,1024]{1,0:T(1,128)}, f32[512,512]{1,0:T(8,128)}, f32[512,128]{1,0:T(8,128)}, bf16[512,512]{1,0:T(8,128)(2,1)}, bf16[512,1536]{1,0:T(8,128)(2...) custom-call(bf16[512,1536]{1,0:T(8,128)(2,1)} %refs_2_.1, f32[1,512]{1,0:T(1,128)} %bitcast.24, ...), custom_call_target="tpu_custom_call" | custom-call | flops 2952790016 | bytes 16777216 | tf_op jit(solution)/shard_map/forward/pallas_call | solution.py:619
  36.8 1.9 %collective-permute-done.8.refs_7_ = bf16[256,512]{1,0:T(8,128)(2,1)S(1)} collective-permute-done((bf16[256,512]{1,0:T(8,128)(2,1)S(1)}, bf16[256,512]{1,0:T(8,128)(2,1)S(1)}, u32[]{:S(2)}, u32[]{:S(2)}) %collective-permute-start.8) | collective-permute-done | bytes 262176 | tf_op jit(solution)/shard_map/ppermute | solution.py:422
  38.7 0.7 copy-done.12
  39.5 14.8 %backward.1 = (f32[128,2176]{1,0:T(8,128)}, f32[128,2176]{1,0:T(8,128)}, f32[128,2176]{1,0:T(8,128)}, f32[128,2176]{1,0:T(8,128)}, bf16[512,512]{1,0:T(8,128)(2,1)}, /*index=5*/f32[512,512]{1,0:T(8,128)}) custom-call(s32[1]{0:T(128)} %bitcast.1.me_ref, s32[1,1024]{1,0:T(1,128)} %get-tuple-element.95.pos_ref, bf16[512,512]{1,0:T(8,128)(2,1)} %w_proj_ref.1, ...), custom_call_target="tpu_custom_call" | custom-call | flops 4294967296 | bytes 16777216 | tf_op jit(solution)/shard_map/backward/pallas_call | solution.py:655
  54.4 0.5 collective-permute-start.11
  54.9 2.5 %collective-permute-done.12.refs_1_ = f32[128,2176]{1,0:T(8,128)S(1)} collective-permute-done((f32[128,2176]{1,0:T(8,128)}, f32[128,2176]{1,0:T(8,128)S(1)}, u32[]{:S(2)}, u32[]{:S(2)}) %collective-permute-start.12) | collective-permute-done | bytes 1114144 | tf_op jit(solution)/shard_map/ppermute | solution.py:482
  57.4 1.2 copy-done.1
  58.6 0.3 code_first.1
  59.0 1.6 %collective-permute-start.13 = (s16[128,2176]{1,0:T(8,128)(2,1)S(1)}, s16[128,2176]{1,0:T(8,128)(2,1)S(1)}, u32[]{:S(2)}, u32[]{:S(2)}) collective-permute-start(s16[128,2176]{1,0:T(8,128)(2,1)S(1)} %code_first.1), channel_id=1, source_target_pairs={{0,8},{4,20},{8,0},{12,28},{16,24},{20,4},{24,16},{28,12},{1,9},{5... | collective-permute-start | bytes 1671176 | tf_op jit(solution)/shard_map/ppermute | solution.py:485
  60.6 1.1 residual.1
  61.8 6.8 %collective-permute-done.13.refs_2_ = s16[128,2176]{1,0:T(8,128)(2,1)S(1)} collective-permute-done((s16[128,2176]{1,0:T(8,128)(2,1)S(1)}, s16[128,2176]{1,0:T(8,128)(2,1)S(1)}, u32[]{:S(2)}, u32[]{:S(2)}) %collective-permute-start.13) | collective-permute-done | bytes 557088 | tf_op jit(solution)/shard_map/ppermute | solution.py:485
  68.6 0.3 code_second.1
  68.8 1.4 %collective-permute-start.14 = (s16[64,2176]{1,0:T(8,128)(2,1)S(1)}, s16[64,2176]{1,0:T(8,128)(2,1)S(1)}, u32[]{:S(2)}, u32[]{:S(2)}) collective-permute-start(s16[64,2176]{1,0:T(8,128)(2,1)S(1)} %code_second.1), channel_id=1, source_target_pairs={{0,16},{4,12},{8,24},{12,4},{16,0},{20,28},{24,8},{28,20},{1,17},{... | collective-permute-start | bytes 835592 | tf_op jit(solution)/shard_map/ppermute | solution.py:490
  70.2 0.9 pair_up.3
  71.1 4.3 %collective-permute-done.14.refs_3_ = s16[64,2176]{1,0:T(8,128)(2,1)S(1)} collective-permute-done((s16[64,2176]{1,0:T(8,128)(2,1)S(1)}, s16[64,2176]{1,0:T(8,128)(2,1)S(1)}, u32[]{:S(2)}, u32[]{:S(2)}) %collective-permute-start.14) | collective-permute-done | bytes 278560 | tf_op jit(solution)/shard_map/ppermute | solution.py:490
  75.4 1.5 %collective-permute-start.19 = (bf16[256,512]{1,0:T(8,128)(2,1)}, bf16[256,512]{1,0:T(8,128)(2,1)}, u32[]{:S(2)}, u32[]{:S(2)}) collective-permute-start(bf16[256,512]{1,0:T(8,128)(2,1)} %get-tuple-element.125), channel_id=1, source_target_pairs={{0,8},{4,12},{8,0},{12,4},{16,24},{20,28},{24,16},{28,20},{1,9},{5... | collective-permute-start | bytes 786440 | tf_op jit(solution)/shard_map/ppermute | solution.py:422
  77.0 1.3 %collective-permute-start.20 = (bf16[256,512]{1,0:T(8,128)(2,1)}, bf16[256,512]{1,0:T(8,128)(2,1)}, u32[]{:S(2)}, u32[]{:S(2)}) collective-permute-start(bf16[256,512]{1,0:T(8,128)(2,1)} %get-tuple-element.126), channel_id=1, source_target_pairs={{0,16},{4,20},{8,24},{12,28},{16,0},{20,4},{24,8},{28,12},{1,17},{... | collective-permute-start | bytes 786440 | tf_op jit(solution)/shard_map/ppermute | solution.py:422
  78.3 0.6 collective-permute-start.21
  78.9 0.5 code_planes.1
  79.4 1.6 %collective-permute-start.16 = (s16[16,2176]{1,0:T(8,128)(2,1)S(1)}, s16[16,2176]{1,0:T(8,128)(2,1)S(1)}, u32[]{:S(2)}, u32[]{:S(2)}) collective-permute-start(s16[16,2176]{1,0:T(8,128)(2,1)S(1)} %get-tuple-element.121), channel_id=1, source_target_pairs={{0,1},{1,0},{2,3},{3,2},{4,5},{5,4},{6,7},{7,6},{8,9},{9,8},{10,11... | collective-permute-start | bytes 208904 | tf_op jit(solution)/shard_map/ppermute | solution.py:415
  81.1 2.6 %collective-permute-start.17 = (s16[16,2176]{1,0:T(8,128)(2,1)S(1)}, s16[16,2176]{1,0:T(8,128)(2,1)S(1)}, u32[]{:S(2)}, u32[]{:S(2)}) collective-permute-start(s16[16,2176]{1,0:T(8,128)(2,1)S(1)} %get-tuple-element.122), channel_id=1, source_target_pairs={{0,2},{1,3},{2,0},{3,1},{4,6},{5,7},{6,4},{7,5},{8,10},{9,11},{10,... | collective-permute-start | bytes 208904 | tf_op jit(solution)/shard_map/ppermute | solution.py:415
  83.9 3.5 %collective-permute-start.18 = (s16[16,2176]{1,0:T(8,128)(2,1)S(1)}, s16[16,2176]{1,0:T(8,128)(2,1)S(1)}, u32[]{:S(2)}, u32[]{:S(2)}) collective-permute-start(s16[16,2176]{1,0:T(8,128)(2,1)S(1)} %get-tuple-element.123), channel_id=1, source_target_pairs={{0,3},{1,2},{2,1},{3,0},{4,7},{5,6},{6,5},{7,4},{8,11},{9,10},{10,... | collective-permute-start | bytes 208904 | tf_op jit(solution)/shard_map/ppermute | solution.py:415
  87.6 2.6 %collective-permute-done.18.refs_3_ = s16[16,2176]{1,0:T(8,128)(2,1)S(1)} collective-permute-done((s16[16,2176]{1,0:T(8,128)(2,1)S(1)}, s16[16,2176]{1,0:T(8,128)(2,1)S(1)}, u32[]{:S(2)}, u32[]{:S(2)}) %collective-permute-start.18) | collective-permute-done | bytes 69664 | tf_op jit(solution)/shard_map/ppermute | solution.py:415
  90.4 0.6 collective-permute-start.22
  91.0 3.6 %collective-permute-start.23 = (bf16[16,2176]{1,0:T(8,128)(2,1)S(1)}, bf16[16,2176]{1,0:T(8,128)(2,1)S(1)}, u32[]{:S(2)}, u32[]{:S(2)}) collective-permute-start(bf16[16,2176]{1,0:T(8,128)(2,1)S(1)} %finish.1), channel_id=1, source_target_pairs={{0,2},{1,3},{2,0},{3,1},{4,6},{5,7},{6,4},{7,5},{8,10},{9,11},{10,... | collective-permute-start | bytes 208904 | tf_op jit(solution)/shard_map/ppermute | solution.py:415
  94.8 0.7 collective-permute-done.22
  95.5 2.1 %collective-permute-done.23 = bf16[16,2176]{1,0:T(8,128)(2,1)S(1)} collective-permute-done((bf16[16,2176]{1,0:T(8,128)(2,1)S(1)}, bf16[16,2176]{1,0:T(8,128)(2,1)S(1)}, u32[]{:S(2)}, u32[]{:S(2)}) %collective-permute-start.23) | collective-permute-done | bytes 69664 | tf_op jit(solution)/shard_map/ppermute | solution.py:415
  97.6 3.1 %collective-permute-done.24 = bf16[16,2176]{1,0:T(8,128)(2,1)S(1)} collective-permute-done((bf16[16,2176]{1,0:T(8,128)(2,1)S(1)}, bf16[16,2176]{1,0:T(8,128)(2,1)S(1)}, u32[]{:S(2)}, u32[]{:S(2)}) %collective-permute-start.24) | collective-permute-done | bytes 69664 | tf_op jit(solution)/shard_map/ppermute | solution.py:415
  100.9 1.2 collective-permute-start.25
  102.1 8.4 %collective-permute-done.25 = bf16[64,2176]{1,0:T(8,128)(2,1)S(1)} collective-permute-done((bf16[64,2176]{1,0:T(8,128)(2,1)S(1)}, bf16[64,2176]{1,0:T(8,128)(2,1)S(1)}, u32[]{:S(2)}, u32[]{:S(2)}) %collective-permute-start.25) | collective-permute-done | bytes 278560 | tf_op jit(solution)/shard_map/ppermute | solution.py:535
  110.7 1.6 %collective-permute-start.26 = (bf16[128,2176]{1,0:T(8,128)(2,1)S(1)}, bf16[128,2176]{1,0:T(8,128)(2,1)S(1)}, u32[]{:S(2)}, u32[]{:S(2)}) collective-permute-start(bf16[128,2176]{1,0:T(8,128)(2,1)S(1)} %broadcast_select_fusion), channel_id=1, source_target_pairs={{0,8},{4,20},{8,0},{12,28},{16,24},{20,4},{24,16},{28,12},{1,9},{5... | collective-permute-start | bytes 1671176 | tf_op jit(solution)/shard_map/ppermute | solution.py:535
  112.2 2.7 %unpack.1 = bf16[512,512]{1,0:T(8,128)(2,1)} custom-call(s32[1,512]{1,0:T(1,128)S(1)} %copy-done.9, bf16[256,512]{1,0:T(8,128)(2,1)S(1)} %get-tuple-element.130.refs_0_, bf16[256,512]{1,0:T(8,128)(2,1)} %collective-permute-done.19.refs_1_, bf16[256,512]{1,0:T(8,128)(2,1)} %collective-permute-done.20.refs_2_, bf16[256,512]{1,0:T(8,128)(2,1)} %collective-permute-done.21.refs_3_), custom_call_target="tpu_custom_call" | custom-call | flops 3149824 | bytes 1574912 | tf_op jit(solution)/shard_map/unpack/pallas_call | solution.py:460
  114.9 5.4 %collective-permute-done.26 = bf16[128,2176]{1,0:T(8,128)(2,1)S(1)} collective-permute-done((bf16[128,2176]{1,0:T(8,128)(2,1)S(1)}, bf16[128,2176]{1,0:T(8,128)(2,1)S(1)}, u32[]{:S(2)}, u32[]{:S(2)}) %collective-permute-start.26) | collective-permute-done | bytes 557088 | tf_op jit(solution)/shard_map/ppermute | solution.py:535
  120.6 1.4 %split.2 = (f32[512,1536]{1,0:T(8,128)}, f32[512,512]{1,0:T(8,128)}, f32[1,512]{1,0:T(1,128)}) custom-call(s32[1]{0:T(128)S(6)} %and.19.side_ref, bf16[256,2176]{1,0:T(8,128)(2,1)S(1)} %maximum_select_fusion.sums_ref), custom_call_target="tpu_custom_call" | custom-call | bytes 4194304 | tf_op jit(solution)/shard_map/split/pallas_call | solution.py:544
  122.0 1.3 %collective-permute-done.27.sums_ref = bf16[256,2176]{1,0:T(8,128)(2,1)S(1)} collective-permute-done((bf16[256,2176]{1,0:T(8,128)(2,1)S(1)}, bf16[256,2176]{1,0:T(8,128)(2,1)S(1)}, u32[]{:S(2)}, u32[]{:S(2)}) %collective-permute-start.27) | collective-permute-done | bytes 1114144 | tf_op jit(solution)/shard_map/ppermute | solution.py:714
  123.3 1.3 %split.3 = (f32[512,1536]{1,0:T(8,128)}, f32[512,512]{1,0:T(8,128)}, f32[1,512]{1,0:T(1,128)}) custom-call(s32[1]{0:T(128)S(6)} %sub.3.side_ref, bf16[256,2176]{1,0:T(8,128)(2,1)S(1)} %collective-permute-done.27.sums_ref, f32[512,1536]{1,0:T(8,128)} %get-tuple-element.136.refs_0_, ...), custom_call_target="tpu_custom_call", output_to_operand_aliasing={{0}: (2, {}), {1}: (3, {}), {2}: (4, {})} | custom-call | bytes 4194304 | tf_op jit(solution)/shard_map/split/pallas_call | solution.py:544
  (76 shorter events, 2.1 us)
Async XLA Ops:
  4.4 11.4 %collective-permute-start.7 = (bf16[512,512]{1,0:T(8,128)(2,1)}, bf16[512,512]{1,0:T(8,128)(2,1)S(1)}, u32[]{:S(2)}, u32[]{:S(2)}) collective-permute-start(bf16[512,512]{1,0:T(8,128)(2,1)} %get-tuple-element.82), channel_id=1, source_target_pairs={{0,4},{4,0},{8,12},{12,8},{16,20},{20,16},{24,28},{28,24},{1,5},{5... | collective-permute-start | bytes 1572872 | tf_op jit(solution)/shard_map/ppermute | solution.py:611
  4.9 4.5 %collective-permute-start = (bf16[144,512]{1,0:T(8,128)(2,1)}, bf16[144,512]{1,0:T(8,128)(2,1)S(1)}, u32[]{:S(2)}, u32[]{:S(2)}) collective-permute-start(bf16[144,512]{1,0:T(8,128)(2,1)} %get-tuple-element.74), channel_id=1, source_target_pairs={{0,4},{4,0},{8,12},{12,8},{16,20},{20,16},{24,28},{28,24},{1,5},{5... | collective-permute-start | bytes 442376 | tf_op jit(solution)/shard_map/ppermute | solution.py:415
  5.0 7.8 %collective-permute-start.1 = (bf16[144,512]{1,0:T(8,128)(2,1)}, bf16[144,512]{1,0:T(8,128)(2,1)S(1)}, u32[]{:S(2)}, u32[]{:S(2)}) collective-permute-start(bf16[144,512]{1,0:T(8,128)(2,1)} %get-tuple-element.75), channel_id=1, source_target_pairs={{0,8},{4,12},{8,0},{12,4},{16,24},{20,28},{24,16},{28,20},{1,9},{5... | collective-permute-start | bytes 442376 | tf_op jit(solution)/shard_map/ppermute | solution.py:415
  7.9 9.7 %collective-permute-start.2 = (bf16[144,512]{1,0:T(8,128)(2,1)}, bf16[144,512]{1,0:T(8,128)(2,1)S(1)}, u32[]{:S(2)}, u32[]{:S(2)}) collective-permute-start(bf16[144,512]{1,0:T(8,128)(2,1)} %get-tuple-element.76), channel_id=1, source_target_pairs={{0,12},{4,8},{8,4},{12,0},{16,28},{20,24},{24,20},{28,16},{1,13},{... | collective-permute-start | bytes 442376 | tf_op jit(solution)/shard_map/ppermute | solution.py:415
  7.9 9.7 %collective-permute-start.3 = (bf16[144,512]{1,0:T(8,128)(2,1)}, bf16[144,512]{1,0:T(8,128)(2,1)S(1)}, u32[]{:S(2)}, u32[]{:S(2)}) collective-permute-start(bf16[144,512]{1,0:T(8,128)(2,1)} %get-tuple-element.77), channel_id=1, source_target_pairs={{0,16},{4,20},{8,24},{12,28},{16,0},{20,4},{24,8},{28,12},{1,17},{... | collective-permute-start | bytes 442376 | tf_op jit(solution)/shard_map/ppermute | solution.py:415
  9.4 17.5 %copy-start.14 = (bf16[144,512]{1,0:T(8,128)(2,1)}, bf16[144,512]{1,0:T(8,128)(2,1)S(1)}, u32[]{:S(2)}) copy-start(bf16[144,512]{1,0:T(8,128)(2,1)S(1)} %collective-permute-done.refs_1_) | copy-start | bytes 442372
  9.4 13.8 %collective-permute-start.4 = (bf16[144,512]{1,0:T(8,128)(2,1)}, bf16[144,512]{1,0:T(8,128)(2,1)S(1)}, u32[]{:S(2)}, u32[]{:S(2)}) collective-permute-start(bf16[144,512]{1,0:T(8,128)(2,1)} %get-tuple-element.78), channel_id=1, source_target_pairs={{0,20},{4,16},{8,28},{12,24},{16,4},{20,0},{24,12},{28,8},{1,21},{... | collective-permute-start | bytes 442376 | tf_op jit(solution)/shard_map/ppermute | solution.py:415
  12.7 14.2 %copy-start.15 = (bf16[144,512]{1,0:T(8,128)(2,1)}, bf16[144,512]{1,0:T(8,128)(2,1)S(1)}, u32[]{:S(2)}) copy-start(bf16[144,512]{1,0:T(8,128)(2,1)S(1)} %collective-permute-done.1.refs_2_) | copy-start | bytes 442372
  12.7 10.5 %collective-permute-start.5 = (bf16[144,512]{1,0:T(8,128)(2,1)}, bf16[144,512]{1,0:T(8,128)(2,1)S(1)}, u32[]{:S(2)}, u32[]{:S(2)}) collective-permute-start(bf16[144,512]{1,0:T(8,128)(2,1)} %get-tuple-element.79), channel_id=1, source_target_pairs={{0,24},{4,28},{8,16},{12,20},{16,8},{20,12},{24,0},{28,4},{1,25},{... | collective-permute-start | bytes 442376 | tf_op jit(solution)/shard_map/ppermute | solution.py:415
  15.8 7.5 %collective-permute-start.6 = (bf16[144,512]{1,0:T(8,128)(2,1)}, bf16[144,512]{1,0:T(8,128)(2,1)S(1)}, u32[]{:S(2)}, u32[]{:S(2)}) collective-permute-start(bf16[144,512]{1,0:T(8,128)(2,1)} %get-tuple-element.80), channel_id=1, source_target_pairs={{0,28},{4,24},{8,20},{12,16},{16,12},{20,8},{24,4},{28,0},{1,29},{... | collective-permute-start | bytes 442376 | tf_op jit(solution)/shard_map/ppermute | solution.py:415
  15.8 1.0 copy-start.5
  17.6 9.3 %copy-start.16 = (bf16[144,512]{1,0:T(8,128)(2,1)}, bf16[144,512]{1,0:T(8,128)(2,1)S(1)}, u32[]{:S(2)}) copy-start(bf16[144,512]{1,0:T(8,128)(2,1)S(1)} %collective-permute-done.2.refs_3_) | copy-start | bytes 442372
  17.6 9.3 %copy-start.17 = (bf16[144,512]{1,0:T(8,128)(2,1)}, bf16[144,512]{1,0:T(8,128)(2,1)S(1)}, u32[]{:S(2)}) copy-start(bf16[144,512]{1,0:T(8,128)(2,1)S(1)} %collective-permute-done.3.refs_4_) | copy-start | bytes 442372
  23.3 3.7 %copy-start.18 = (bf16[144,512]{1,0:T(8,128)(2,1)}, bf16[144,512]{1,0:T(8,128)(2,1)S(1)}, u32[]{:S(2)}) copy-start(bf16[144,512]{1,0:T(8,128)(2,1)S(1)} %collective-permute-done.4.refs_5_) | copy-start | bytes 442372
  23.3 3.7 %copy-start.19 = (bf16[144,512]{1,0:T(8,128)(2,1)}, bf16[144,512]{1,0:T(8,128)(2,1)S(1)}, u32[]{:S(2)}) copy-start(bf16[144,512]{1,0:T(8,128)(2,1)S(1)} %collective-permute-done.5.refs_6_) | copy-start | bytes 442372
  23.3 3.7 %copy-start.20 = (bf16[144,512]{1,0:T(8,128)(2,1)}, bf16[144,512]{1,0:T(8,128)(2,1)S(1)}, u32[]{:S(2)}) copy-start(bf16[144,512]{1,0:T(8,128)(2,1)S(1)} %collective-permute-done.6.refs_7_) | copy-start | bytes 442372
  23.3 13.5 %collective-permute-start.10 = (bf16[256,512]{1,0:T(8,128)(2,1)S(1)}, bf16[256,512]{1,0:T(8,128)(2,1)S(1)}, u32[]{:S(2)}, u32[]{:S(2)}) collective-permute-start(bf16[256,512]{1,0:T(8,128)(2,1)S(1)} %get-tuple-element.105), channel_id=1, source_target_pairs={{0,24},{4,28},{8,16},{12,20},{16,8},{20,12},{24,0},{28,4},{1,25},{... | collective-permute-start | bytes 786440 | tf_op jit(solution)/shard_map/ppermute | solution.py:422
  26.3 12.4 %collective-permute-start.8 = (bf16[256,512]{1,0:T(8,128)(2,1)S(1)}, bf16[256,512]{1,0:T(8,128)(2,1)S(1)}, u32[]{:S(2)}, u32[]{:S(2)}) collective-permute-start(bf16[256,512]{1,0:T(8,128)(2,1)S(1)} %get-tuple-element.103), channel_id=1, source_target_pairs={{0,8},{4,12},{8,0},{12,4},{16,24},{20,28},{24,16},{28,20},{1,9},{5... | collective-permute-start | bytes 786440 | tf_op jit(solution)/shard_map/ppermute | solution.py:422
  26.7 12.0 %collective-permute-start.9 = (bf16[256,512]{1,0:T(8,128)(2,1)S(1)}, bf16[256,512]{1,0:T(8,128)(2,1)S(1)}, u32[]{:S(2)}, u32[]{:S(2)}) collective-permute-start(bf16[256,512]{1,0:T(8,128)(2,1)S(1)} %get-tuple-element.104), channel_id=1, source_target_pairs={{0,16},{4,20},{8,24},{12,28},{16,0},{20,4},{24,8},{28,12},{1,17},{... | collective-permute-start | bytes 786440 | tf_op jit(solution)/shard_map/ppermute | solution.py:422
  36.8 1.9 %copy-start.11 = (bf16[256,512]{1,0:T(8,128)(2,1)}, bf16[256,512]{1,0:T(8,128)(2,1)S(1)}, u32[]{:S(2)}) copy-start(bf16[256,512]{1,0:T(8,128)(2,1)S(1)} %collective-permute-done.10.refs_9_) | copy-start | bytes 786436
  38.7 0.7 copy-start.12
  38.7 0.8 copy-start.13
  39.5 21.0 %copy-start.6 = (f32[512,128]{1,0:T(8,128)S(1)}, f32[512,128]{1,0:T(8,128)}, u32[]{:S(2)}) copy-start(f32[512,128]{1,0:T(8,128)} %get-tuple-element.110.inv_ref) | copy-start | bytes 786436
  54.3 3.0 %collective-permute-start.12 = (f32[128,2176]{1,0:T(8,128)}, f32[128,2176]{1,0:T(8,128)S(1)}, u32[]{:S(2)}, u32[]{:S(2)}) collective-permute-start(f32[128,2176]{1,0:T(8,128)} %get-tuple-element.109), channel_id=1, source_target_pairs={{0,4},{4,0},{8,12},{12,8},{16,20},{20,16},{24,28},{28,24},{1,5},{5... | collective-permute-start | bytes 3342344 | tf_op jit(solution)/shard_map/ppermute | solution.py:482
  54.4 7.4 %collective-permute-start.11 = (f32[128,2176]{1,0:T(8,128)}, f32[128,2176]{1,0:T(8,128)S(1)}, u32[]{:S(2)}, u32[]{:S(2)}) collective-permute-start(f32[128,2176]{1,0:T(8,128)} %get-tuple-element.107), channel_id=1, source_target_pairs={{0,4},{4,0},{8,12},{12,8},{16,20},{20,16},{24,28},{28,24},{1,5},{5... | collective-permute-start | bytes 3342344 | tf_op jit(solution)/shard_map/ppermute | solution.py:483
  57.4 1.2 %copy-start.1 = (f32[128,2176]{1,0:T(8,128)S(1)}, f32[128,2176]{1,0:T(8,128)}, u32[]{:S(2)}) copy-start(f32[128,2176]{1,0:T(8,128)} %get-tuple-element.108.refs_0_) | copy-start | bytes 3342340
  58.6 1.9 %copy-start.2 = (f32[512,512]{1,0:T(8,128)S(1)}, f32[512,512]{1,0:T(8,128)}, u32[]{:S(2)}) copy-start(f32[512,512]{1,0:T(8,128)} %get-tuple-element.99.refs_3_.xhat_ref) | copy-start | bytes 3145732
  58.6 1.9 %copy-start.3 = (f32[512,512]{1,0:T(8,128)S(1)}, f32[512,512]{1,0:T(8,128)}, u32[]{:S(2)}) copy-start(f32[512,512]{1,0:T(8,128)} %get-tuple-element.112.d_normed_ref) | copy-start | bytes 3145732
  58.6 1.9 %copy-start.4 = (bf16[512,512]{1,0:T(8,128)(2,1)S(1)}, bf16[512,512]{1,0:T(8,128)(2,1)}, u32[]{:S(2)}) copy-start(bf16[512,512]{1,0:T(8,128)(2,1)} %get-tuple-element.111.serial_grad_ref) | copy-start | bytes 1572868
  58.6 1.9 %copy-start.7 = (s32[1,1024]{1,0:T(1,128)S(1)}, s32[1,1024]{1,0:T(1,128)}, u32[]{:S(2)}) copy-start(s32[1,1024]{1,0:T(1,128)} %get-tuple-element.95.pos_ref) | copy-start | bytes 12292
  58.6 1.9 %copy-start.8 = (f32[512]{0:T(512)S(1)}, f32[512]{0:T(512)}, u32[]{:S(2)}) copy-start(f32[512]{0:T(512)} %param.11) | copy-start | bytes 6148
  59.0 9.6 %collective-permute-start.13 = (s16[128,2176]{1,0:T(8,128)(2,1)S(1)}, s16[128,2176]{1,0:T(8,128)(2,1)S(1)}, u32[]{:S(2)}, u32[]{:S(2)}) collective-permute-start(s16[128,2176]{1,0:T(8,128)(2,1)S(1)} %code_first.1), channel_id=1, source_target_pairs={{0,8},{4,20},{8,0},{12,28},{16,24},{20,4},{24,16},{28,12},{1,9},{5... | collective-permute-start | bytes 1671176 | tf_op jit(solution)/shard_map/ppermute | solution.py:485
  60.6 8.0 %copy-start = (f32[128,2176]{1,0:T(8,128)S(1)}, f32[128,2176]{1,0:T(8,128)}, u32[]{:S(2)}) copy-start(f32[128,2176]{1,0:T(8,128)} %get-tuple-element.106.refs_0_) | copy-start | bytes 3342340
  61.7 8.5 %collective-permute-start.15 = (bf16[512,512]{1,0:T(8,128)(2,1)S(1)}, bf16[512,512]{1,0:T(8,128)(2,1)S(1)}, u32[]{:S(2)}, u32[]{:S(2)}) collective-permute-start(bf16[512,512]{1,0:T(8,128)(2,1)S(1)} %get-tuple-element.114), channel_id=1, source_target_pairs={{0,4},{4,0},{8,12},{12,8},{16,20},{20,16},{24,28},{28,24},{1,5},{5... | collective-permute-start | bytes 1572872 | tf_op jit(solution)/shard_map/ppermute | solution.py:611
  68.8 6.6 %collective-permute-start.14 = (s16[64,2176]{1,0:T(8,128)(2,1)S(1)}, s16[64,2176]{1,0:T(8,128)(2,1)S(1)}, u32[]{:S(2)}, u32[]{:S(2)}) collective-permute-start(s16[64,2176]{1,0:T(8,128)(2,1)S(1)} %code_second.1), channel_id=1, source_target_pairs={{0,16},{4,12},{8,24},{12,4},{16,0},{20,28},{24,8},{28,20},{1,17},{... | collective-permute-start | bytes 835592 | tf_op jit(solution)/shard_map/ppermute | solution.py:490
  75.4 14.9 %collective-permute-start.19 = (bf16[256,512]{1,0:T(8,128)(2,1)}, bf16[256,512]{1,0:T(8,128)(2,1)}, u32[]{:S(2)}, u32[]{:S(2)}) collective-permute-start(bf16[256,512]{1,0:T(8,128)(2,1)} %get-tuple-element.125), channel_id=1, source_target_pairs={{0,8},{4,12},{8,0},{12,4},{16,24},{20,28},{24,16},{28,20},{1,9},{5... | collective-permute-start | bytes 786440 | tf_op jit(solution)/shard_map/ppermute | solution.py:422
  77.0 13.4 %collective-permute-start.20 = (bf16[256,512]{1,0:T(8,128)(2,1)}, bf16[256,512]{1,0:T(8,128)(2,1)}, u32[]{:S(2)}, u32[]{:S(2)}) collective-permute-start(bf16[256,512]{1,0:T(8,128)(2,1)} %get-tuple-element.126), channel_id=1, source_target_pairs={{0,16},{4,20},{8,24},{12,28},{16,0},{20,4},{24,8},{28,12},{1,17},{... | collective-permute-start | bytes 786440 | tf_op jit(solution)/shard_map/ppermute | solution.py:422
  78.3 12.1 %collective-permute-start.21 = (bf16[256,512]{1,0:T(8,128)(2,1)}, bf16[256,512]{1,0:T(8,128)(2,1)}, u32[]{:S(2)}, u32[]{:S(2)}) collective-permute-start(bf16[256,512]{1,0:T(8,128)(2,1)} %get-tuple-element.127), channel_id=1, source_target_pairs={{0,24},{4,28},{8,16},{12,20},{16,8},{20,12},{24,0},{28,4},{1,25},{... | collective-permute-start | bytes 786440 | tf_op jit(solution)/shard_map/ppermute | solution.py:422
  79.4 4.4 %collective-permute-start.16 = (s16[16,2176]{1,0:T(8,128)(2,1)S(1)}, s16[16,2176]{1,0:T(8,128)(2,1)S(1)}, u32[]{:S(2)}, u32[]{:S(2)}) collective-permute-start(s16[16,2176]{1,0:T(8,128)(2,1)S(1)} %get-tuple-element.121), channel_id=1, source_target_pairs={{0,1},{1,0},{2,3},{3,2},{4,5},{5,4},{6,7},{7,6},{8,9},{9,8},{10,11... | collective-permute-start | bytes 208904 | tf_op jit(solution)/shard_map/ppermute | solution.py:415
  81.1 6.5 %collective-permute-start.17 = (s16[16,2176]{1,0:T(8,128)(2,1)S(1)}, s16[16,2176]{1,0:T(8,128)(2,1)S(1)}, u32[]{:S(2)}, u32[]{:S(2)}) collective-permute-start(s16[16,2176]{1,0:T(8,128)(2,1)S(1)} %get-tuple-element.122), channel_id=1, source_target_pairs={{0,2},{1,3},{2,0},{3,1},{4,6},{5,7},{6,4},{7,5},{8,10},{9,11},{10,... | collective-permute-start | bytes 208904 | tf_op jit(solution)/shard_map/ppermute | solution.py:415
  83.9 6.3 %collective-permute-start.18 = (s16[16,2176]{1,0:T(8,128)(2,1)S(1)}, s16[16,2176]{1,0:T(8,128)(2,1)S(1)}, u32[]{:S(2)}, u32[]{:S(2)}) collective-permute-start(s16[16,2176]{1,0:T(8,128)(2,1)S(1)} %get-tuple-element.123), channel_id=1, source_target_pairs={{0,3},{1,2},{2,1},{3,0},{4,7},{5,6},{6,5},{7,4},{8,11},{9,10},{10,... | collective-permute-start | bytes 208904 | tf_op jit(solution)/shard_map/ppermute | solution.py:415
  90.4 5.1 %collective-permute-start.22 = (bf16[16,2176]{1,0:T(8,128)(2,1)S(1)}, bf16[16,2176]{1,0:T(8,128)(2,1)S(1)}, u32[]{:S(2)}, u32[]{:S(2)}) collective-permute-start(bf16[16,2176]{1,0:T(8,128)(2,1)S(1)} %finish.1), channel_id=1, source_target_pairs={{0,1},{1,0},{2,3},{3,2},{4,5},{5,4},{6,7},{7,6},{8,9},{9,8},{10,11... | collective-permute-start | bytes 208904 | tf_op jit(solution)/shard_map/ppermute | solution.py:415
  91.0 6.7 %collective-permute-start.23 = (bf16[16,2176]{1,0:T(8,128)(2,1)S(1)}, bf16[16,2176]{1,0:T(8,128)(2,1)S(1)}, u32[]{:S(2)}, u32[]{:S(2)}) collective-permute-start(bf16[16,2176]{1,0:T(8,128)(2,1)S(1)} %finish.1), channel_id=1, source_target_pairs={{0,2},{1,3},{2,0},{3,1},{4,6},{5,7},{6,4},{7,5},{8,10},{9,11},{10,... | collective-permute-start | bytes 208904 | tf_op jit(solution)/shard_map/ppermute | solution.py:415
  94.6 6.1 %collective-permute-start.24 = (bf16[16,2176]{1,0:T(8,128)(2,1)S(1)}, bf16[16,2176]{1,0:T(8,128)(2,1)S(1)}, u32[]{:S(2)}, u32[]{:S(2)}) collective-permute-start(bf16[16,2176]{1,0:T(8,128)(2,1)S(1)} %finish.1), channel_id=1, source_target_pairs={{0,3},{1,2},{2,1},{3,0},{4,7},{5,6},{6,5},{7,4},{8,11},{9,10},{10,... | collective-permute-start | bytes 208904 | tf_op jit(solution)/shard_map/ppermute | solution.py:415
  100.9 9.6 %collective-permute-start.25 = (bf16[64,2176]{1,0:T(8,128)(2,1)S(1)}, bf16[64,2176]{1,0:T(8,128)(2,1)S(1)}, u32[]{:S(2)}, u32[]{:S(2)}) collective-permute-start(bf16[64,2176]{1,0:T(8,128)(2,1)S(1)} %pad_maximum_fusion.1), channel_id=1, source_target_pairs={{0,16},{4,12},{8,24},{12,4},{16,0},{20,28},{24,8},{28,20},{1,17},{... | collective-permute-start | bytes 835592 | tf_op jit(solution)/shard_map/ppermute | solution.py:535
  110.5 1.7 %copy-start.9 = (s32[1,512]{1,0:T(1,128)S(1)}, s32[1,512]{1,0:T(1,128)}, u32[]{:S(2)}) copy-start(s32[1,512]{1,0:T(1,128)} %get-tuple-element.129.slot_ref) | copy-start | bytes 6148
  110.7 9.6 %collective-permute-start.26 = (bf16[128,2176]{1,0:T(8,128)(2,1)S(1)}, bf16[128,2176]{1,0:T(8,128)(2,1)S(1)}, u32[]{:S(2)}, u32[]{:S(2)}) collective-permute-start(bf16[128,2176]{1,0:T(8,128)(2,1)S(1)} %broadcast_select_fusion), channel_id=1, source_target_pairs={{0,8},{4,20},{8,0},{12,28},{16,24},{20,4},{24,16},{28,12},{1,9},{5... | collective-permute-start | bytes 1671176 | tf_op jit(solution)/shard_map/ppermute | solution.py:535
  120.5 2.8 %collective-permute-start.27 = (bf16[256,2176]{1,0:T(8,128)(2,1)S(1)}, bf16[256,2176]{1,0:T(8,128)(2,1)S(1)}, u32[]{:S(2)}, u32[]{:S(2)}) collective-permute-start(bf16[256,2176]{1,0:T(8,128)(2,1)S(1)} %maximum_select_fusion.sums_ref), channel_id=1, source_target_pairs={{0,4},{4,0},{8,12},{12,8},{16,20},{20,16},{24,28},{28,24},{1,5},{5... | collective-permute-start | bytes 3342344 | tf_op jit(solution)/shard_map/ppermute | solution.py:714
  (1 other events, 0.7 us)

commit v16 on v15

--- a/solution.py
+++ b/solution.py
@@ -485,9 +485,10 @@
     return [own_keep, got_keep, lax.ppermute(sent, "seq", steps[0][0])]
 
 
-def second_step(terms, steps):
+def second_step(terms, steps, later):
     sent = message(terms, "first", "code_second")
-    return terms, lax.ppermute(sent, "seq", steps[1][0])
+    sent, later = lax.optimization_barrier((sent, later))
+    return terms, lax.ppermute(sent, "seq", steps[1][0]), later
 
 
 def halves_of_plain(part, steps):
@@ -701,10 +702,8 @@
         [pos, gain_row, inv, xhat, serial_grad, d_normed],
         name="residual",
     )
-    back = by_core(same, cross)
-    terms, got = second_step(terms, steps)
-    got, back = lax.optimization_barrier((got, back))
-    returned = by_chip(back)
+    terms, got, same = second_step(terms, steps, same)
+    returned = by_chip(by_core(same, cross))
     part, returned = lax.optimization_barrier((reduce_over_planes(terms, got, steps), returned))
     own = share_in_plane(share_over_planes(part), steps)
     grad_local = small_kernel(

time: 125 us -> 123 us (0.984)
  waiting for transfers between devices: 48 us -> 44.3 us
    ppermute x1, waiting for transfers between devices: 4.32 us -> 1.4 us  [second_step(): return (terms, lax.ppermute(sent, 'seq', steps[1][0]), later)]
    unnamed x50 -> x54, local copies, waits for them, and re-layouts: 4.07 us -> 4.76 us
  transfers between devices with their start and end apart: 28 -> 28, of which waited for: 15 -> 13; matrix products, arithmetic and copies ran while one was open for 0% -> 0% of each run, Pallas kernels for 14% -> 14%
where the time goes in v16:
time: 123 us; the launch traced here: 122 us
  waiting for transfers between devices  44.3 us (36%)
  Pallas kernels  37.1 us (30%)
  starting transfers between devices  34.9 us (28%)
  local copies, waits for them, and re-layouts  4.77 us (4%)
    ppermute x13, starting transfers between devices, by_distance(): lax.ppermute(blocks[k], axis, [(i, i ^ k) for i in range(count)])  20.4 us
    ppermute x13, waiting for transfers between devices, by_distance(): lax.ppermute(blocks[k], axis, [(i, i ^ k) for i in range(count)])  17.4 us
    pallas_call x1, Pallas kernels, per_device(): pl.pallas_call(functools.partial(backward_kernel, n_seq, chip_bits), grid...  14.8 us
    ppermute x2, waiting for transfers between devices, share_in_plane(): other = lax.ppermute(part, 'seq', pairs)  13.1 us
    pallas_call x1, Pallas kernels, per_device(): pl.pallas_call(functools.partial(forward_kernel, n_seq, capacity), grid=(...  9.87 us
    ppermute x6, starting transfers between devices, by_chip(): lax.ppermute(messages[j], 'seq', [(i, i ^ 2 * j) for i in range(count)])  7.1 us
    ppermute x1, waiting for transfers between devices, first_step(): return [own_keep, got_keep, lax.ppermute(sent, 'seq', steps[0][0])]  6.74 us
    pallas_call x8, Pallas kernels, small_kernel(): pl.pallas_call(kernel, out_shape=outs, in_specs=[in_smem] * scalars + [in...  5.98 us
  transfers between devices with their start and end apart: 28, of which 13 were waited for; matrix products, arithmetic and copies ran while one was open for 0% of the time, Pallas kernels for 14%

profile of v16, /device:TPU:0, one launch (start us, length us, event | category | flops | bytes accessed | tf_op | source)
XLA Modules:
  0.0 122.4 jit_solution(3628313052032368220)
XLA Ops:
  0.6 3.7 %pack.1 = (s32[1,512]{1,0:T(1,128)}, bf16[512,512]{1,0:T(8,128)(2,1)}, bf16[512,512]{1,0:T(8,128)(2,1)}, bf16[144,512]{1,0:T(8,128)(2,1)}, bf16[144,512]{1,0:T(8...) custom-call(s32[1]{0:T(128)} %bitcast.1.me_ref, ...), custom_call_target="tpu_custom_call" | custom-call | flops 1073741824 | bytes 4194304 | tf_op jit(solution)/shard_map/pack/pallas_call | solution.py:588
  4.4 0.5 collective-permute-start.7
  5.0 2.9 %collective-permute-start.1 = (bf16[144,512]{1,0:T(8,128)(2,1)}, bf16[144,512]{1,0:T(8,128)(2,1)S(1)}, u32[]{:S(2)}, u32[]{:S(2)}) collective-permute-start(bf16[144,512]{1,0:T(8,128)(2,1)} %get-tuple-element.72), channel_id=1, source_target_pairs={{0,8},{4,12},{8,0},{12,4},{16,24},{20,28},{24,16},{28,20},{1,9},{5... | collective-permute-start | bytes 442376 | tf_op jit(solution)/shard_map/ppermute | solution.py:415
  7.9 1.5 %collective-permute-start.3 = (bf16[144,512]{1,0:T(8,128)(2,1)}, bf16[144,512]{1,0:T(8,128)(2,1)S(1)}, u32[]{:S(2)}, u32[]{:S(2)}) collective-permute-start(bf16[144,512]{1,0:T(8,128)(2,1)} %get-tuple-element.74), channel_id=1, source_target_pairs={{0,16},{4,20},{8,24},{12,28},{16,0},{20,4},{24,8},{28,12},{1,17},{... | collective-permute-start | bytes 442376 | tf_op jit(solution)/shard_map/ppermute | solution.py:415
  9.4 0.3 collective-permute-start.4
  9.7 3.0 %collective-permute-done.1.refs_2_ = bf16[144,512]{1,0:T(8,128)(2,1)S(1)} collective-permute-done((bf16[144,512]{1,0:T(8,128)(2,1)}, bf16[144,512]{1,0:T(8,128)(2,1)S(1)}, u32[]{:S(2)}, u32[]{:S(2)}) %collective-permute-start.1) | collective-permute-done | bytes 147488 | tf_op jit(solution)/shard_map/ppermute | solution.py:415
  12.7 3.0 %collective-permute-start.5 = (bf16[144,512]{1,0:T(8,128)(2,1)}, bf16[144,512]{1,0:T(8,128)(2,1)S(1)}, u32[]{:S(2)}, u32[]{:S(2)}) collective-permute-start(bf16[144,512]{1,0:T(8,128)(2,1)} %get-tuple-element.76), channel_id=1, source_target_pairs={{0,24},{4,28},{8,16},{12,20},{16,8},{20,12},{24,0},{28,4},{1,25},{... | collective-permute-start | bytes 442376 | tf_op jit(solution)/shard_map/ppermute | solution.py:415
  15.8 1.0 copy-done.5
  16.9 0.7 copy-done.12
  17.6 5.6 %collective-permute-done.4.refs_5_ = bf16[144,512]{1,0:T(8,128)(2,1)S(1)} collective-permute-done((bf16[144,512]{1,0:T(8,128)(2,1)}, bf16[144,512]{1,0:T(8,128)(2,1)S(1)}, u32[]{:S(2)}, u32[]{:S(2)}) %collective-permute-start.4) | collective-permute-done | bytes 147488 | tf_op jit(solution)/shard_map/ppermute | solution.py:415
  23.3 3.0 %collective-permute-start.10 = (bf16[256,512]{1,0:T(8,128)(2,1)S(1)}, bf16[256,512]{1,0:T(8,128)(2,1)S(1)}, u32[]{:S(2)}, u32[]{:S(2)}) collective-permute-start(bf16[256,512]{1,0:T(8,128)(2,1)S(1)} %get-tuple-element.102), channel_id=1, source_target_pairs={{0,24},{4,28},{8,16},{12,20},{16,8},{20,12},{24,0},{28,4},{1,25},{... | collective-permute-start | bytes 786440 | tf_op jit(solution)/shard_map/ppermute | solution.py:422
  26.3 0.4 collective-permute-start.8
  27.0 9.9 %forward.1 = (s32[1,1024]{1,0:T(1,128)}, f32[512,512]{1,0:T(8,128)}, f32[512,128]{1,0:T(8,128)}, bf16[512,512]{1,0:T(8,128)(2,1)}, bf16[512,1536]{1,0:T(8,128)(2...) custom-call(bf16[512,1536]{1,0:T(8,128)(2,1)} %refs_2_.1, f32[1,512]{1,0:T(1,128)} %bitcast.24, ...), custom_call_target="tpu_custom_call" | custom-call | flops 2952790016 | bytes 16777216 | tf_op jit(solution)/shard_map/forward/pallas_call | solution.py:620
  36.9 1.9 %collective-permute-done.8.refs_7_ = bf16[256,512]{1,0:T(8,128)(2,1)S(1)} collective-permute-done((bf16[256,512]{1,0:T(8,128)(2,1)S(1)}, bf16[256,512]{1,0:T(8,128)(2,1)S(1)}, u32[]{:S(2)}, u32[]{:S(2)}) %collective-permute-start.8) | collective-permute-done | bytes 262176 | tf_op jit(solution)/shard_map/ppermute | solution.py:422
  38.7 0.7 copy-done.14
  39.5 14.8 %backward.1 = (f32[128,2176]{1,0:T(8,128)}, f32[128,2176]{1,0:T(8,128)}, f32[128,2176]{1,0:T(8,128)}, f32[128,2176]{1,0:T(8,128)}, bf16[512,512]{1,0:T(8,128)(2,1)}, /*index=5*/f32[512,512]{1,0:T(8,128)}) custom-call(s32[1]{0:T(128)} %bitcast.1.me_ref, s32[1,1024]{1,0:T(1,128)} %get-tuple-element.92.pos_ref, bf16[512,512]{1,0:T(8,128)(2,1)} %w_proj_ref.1, ...), custom_call_target="tpu_custom_call" | custom-call | flops 4294967296 | bytes 16777216 | tf_op jit(solution)/shard_map/backward/pallas_call | solution.py:656
  54.4 0.5 collective-permute-start.11
  54.9 2.5 %collective-permute-done.12.refs_1_ = f32[128,2176]{1,0:T(8,128)S(1)} collective-permute-done((f32[128,2176]{1,0:T(8,128)}, f32[128,2176]{1,0:T(8,128)S(1)}, u32[]{:S(2)}, u32[]{:S(2)}) %collective-permute-start.12) | collective-permute-done | bytes 1114144 | tf_op jit(solution)/shard_map/ppermute | solution.py:482
  57.3 1.2 %copy-done.1 = f32[128,2176]{1,0:T(8,128)S(1)} copy-done((f32[128,2176]{1,0:T(8,128)S(1)}, f32[128,2176]{1,0:T(8,128)}, u32[]{:S(2)}) %copy-start.1) | copy-done | bytes 1114136
  58.6 0.3 code_first.1
  58.9 1.6 %collective-permute-start.13 = (s16[128,2176]{1,0:T(8,128)(2,1)S(1)}, s16[128,2176]{1,0:T(8,128)(2,1)S(1)}, u32[]{:S(2)}, u32[]{:S(2)}) collective-permute-start(s16[128,2176]{1,0:T(8,128)(2,1)S(1)} %code_first.1), channel_id=1, source_target_pairs={{0,8},{4,20},{8,0},{12,28},{16,24},{20,4},{24,16},{28,12},{1,9},{5... | collective-permute-start | bytes 1671176 | tf_op jit(solution)/shard_map/ppermute | solution.py:485
  60.6 1.1 residual.1
  61.8 6.7 %collective-permute-done.13.refs_2_ = s16[128,2176]{1,0:T(8,128)(2,1)S(1)} collective-permute-done((s16[128,2176]{1,0:T(8,128)(2,1)S(1)}, s16[128,2176]{1,0:T(8,128)(2,1)S(1)}, u32[]{:S(2)}, u32[]{:S(2)}) %collective-permute-start.13) | collective-permute-done | bytes 557088 | tf_op jit(solution)/shard_map/ppermute | solution.py:485
  68.5 0.3 code_second.1
  68.8 1.4 %collective-permute-start.14 = (s16[64,2176]{1,0:T(8,128)(2,1)S(1)}, s16[64,2176]{1,0:T(8,128)(2,1)S(1)}, u32[]{:S(2)}, u32[]{:S(2)}) collective-permute-start(s16[64,2176]{1,0:T(8,128)(2,1)S(1)} %code_second.1), channel_id=1, source_target_pairs={{0,16},{4,12},{8,24},{12,4},{16,0},{20,28},{24,8},{28,20},{1,17},{... | collective-permute-start | bytes 835592 | tf_op jit(solution)/shard_map/ppermute | solution.py:491
  70.2 0.9 pair_up.3
  71.1 0.7 copy-done.7
  71.8 1.5 %collective-permute-start.19 = (bf16[256,512]{1,0:T(8,128)(2,1)}, bf16[256,512]{1,0:T(8,128)(2,1)}, u32[]{:S(2)}, u32[]{:S(2)}) collective-permute-start(bf16[256,512]{1,0:T(8,128)(2,1)} %get-tuple-element.119), channel_id=1, source_target_pairs={{0,8},{4,12},{8,0},{12,4},{16,24},{20,28},{24,16},{28,20},{1,9},{5... | collective-permute-start | bytes 786440 | tf_op jit(solution)/shard_map/ppermute | solution.py:422
  73.4 0.7 collective-permute-start.20
  74.1 1.2 %collective-permute-start.21 = (bf16[256,512]{1,0:T(8,128)(2,1)}, bf16[256,512]{1,0:T(8,128)(2,1)}, u32[]{:S(2)}, u32[]{:S(2)}) collective-permute-start(bf16[256,512]{1,0:T(8,128)(2,1)} %get-tuple-element.121), channel_id=1, source_target_pairs={{0,24},{4,28},{8,16},{12,20},{16,8},{20,12},{24,0},{28,4},{1,25},{... | collective-permute-start | bytes 786440 | tf_op jit(solution)/shard_map/ppermute | solution.py:422
  75.3 1.4 %collective-permute-done.14.refs_3_ = s16[64,2176]{1,0:T(8,128)(2,1)S(1)} collective-permute-done((s16[64,2176]{1,0:T(8,128)(2,1)S(1)}, s16[64,2176]{1,0:T(8,128)(2,1)S(1)}, u32[]{:S(2)}, u32[]{:S(2)}) %collective-permute-start.14) | collective-permute-done | bytes 278560 | tf_op jit(solution)/shard_map/ppermute | solution.py:491
  76.7 0.5 code_planes.1
  77.2 1.6 %collective-permute-start.15 = (s16[16,2176]{1,0:T(8,128)(2,1)S(1)}, s16[16,2176]{1,0:T(8,128)(2,1)S(1)}, u32[]{:S(2)}, u32[]{:S(2)}) collective-permute-start(s16[16,2176]{1,0:T(8,128)(2,1)S(1)} %get-tuple-element.113), channel_id=1, source_target_pairs={{0,1},{1,0},{2,3},{3,2},{4,5},{5,4},{6,7},{7,6},{8,9},{9,8},{10,11... | collective-permute-start | bytes 208904 | tf_op jit(solution)/shard_map/ppermute | solution.py:415
  78.8 2.6 %collective-permute-start.16 = (s16[16,2176]{1,0:T(8,128)(2,1)S(1)}, s16[16,2176]{1,0:T(8,128)(2,1)S(1)}, u32[]{:S(2)}, u32[]{:S(2)}) collective-permute-start(s16[16,2176]{1,0:T(8,128)(2,1)S(1)} %get-tuple-element.114), channel_id=1, source_target_pairs={{0,2},{1,3},{2,0},{3,1},{4,6},{5,7},{6,4},{7,5},{8,10},{9,11},{10,... | collective-permute-start | bytes 208904 | tf_op jit(solution)/shard_map/ppermute | solution.py:415
  81.6 3.6 %collective-permute-start.17 = (s16[16,2176]{1,0:T(8,128)(2,1)S(1)}, s16[16,2176]{1,0:T(8,128)(2,1)S(1)}, u32[]{:S(2)}, u32[]{:S(2)}) collective-permute-start(s16[16,2176]{1,0:T(8,128)(2,1)S(1)} %get-tuple-element.115), channel_id=1, source_target_pairs={{0,3},{1,2},{2,1},{3,0},{4,7},{5,6},{6,5},{7,4},{8,11},{9,10},{10,... | collective-permute-start | bytes 208904 | tf_op jit(solution)/shard_map/ppermute | solution.py:415
  85.2 2.5 %collective-permute-done.17.refs_3_ = s16[16,2176]{1,0:T(8,128)(2,1)S(1)} collective-permute-done((s16[16,2176]{1,0:T(8,128)(2,1)S(1)}, s16[16,2176]{1,0:T(8,128)(2,1)S(1)}, u32[]{:S(2)}, u32[]{:S(2)}) %collective-permute-start.17) | collective-permute-done | bytes 69664 | tf_op jit(solution)/shard_map/ppermute | solution.py:415
  87.9 0.5 collective-permute-start.22
  88.3 4.2 %collective-permute-start.23 = (bf16[16,2176]{1,0:T(8,128)(2,1)S(1)}, bf16[16,2176]{1,0:T(8,128)(2,1)S(1)}, u32[]{:S(2)}, u32[]{:S(2)}) collective-permute-start(bf16[16,2176]{1,0:T(8,128)(2,1)S(1)} %finish.1), channel_id=1, source_target_pairs={{0,2},{1,3},{2,0},{3,1},{4,6},{5,7},{6,4},{7,5},{8,10},{9,11},{10,... | collective-permute-start | bytes 208904 | tf_op jit(solution)/shard_map/ppermute | solution.py:415
  92.5 3.0 %collective-permute-done.23 = bf16[16,2176]{1,0:T(8,128)(2,1)S(1)} collective-permute-done((bf16[16,2176]{1,0:T(8,128)(2,1)S(1)}, bf16[16,2176]{1,0:T(8,128)(2,1)S(1)}, u32[]{:S(2)}, u32[]{:S(2)}) %collective-permute-start.23) | collective-permute-done | bytes 69664 | tf_op jit(solution)/shard_map/ppermute | solution.py:415
  95.5 3.1 %collective-permute-done.24 = bf16[16,2176]{1,0:T(8,128)(2,1)S(1)} collective-permute-done((bf16[16,2176]{1,0:T(8,128)(2,1)S(1)}, bf16[16,2176]{1,0:T(8,128)(2,1)S(1)}, u32[]{:S(2)}, u32[]{:S(2)}) %collective-permute-start.24) | collective-permute-done | bytes 69664 | tf_op jit(solution)/shard_map/ppermute | solution.py:415
  98.8 1.0 collective-permute-start.25
  99.8 8.2 %collective-permute-done.25 = bf16[64,2176]{1,0:T(8,128)(2,1)S(1)} collective-permute-done((bf16[64,2176]{1,0:T(8,128)(2,1)S(1)}, bf16[64,2176]{1,0:T(8,128)(2,1)S(1)}, u32[]{:S(2)}, u32[]{:S(2)}) %collective-permute-start.25) | collective-permute-done | bytes 278560 | tf_op jit(solution)/shard_map/ppermute | solution.py:536
  108.2 2.2 %collective-permute-start.26 = (bf16[128,2176]{1,0:T(8,128)(2,1)S(1)}, bf16[128,2176]{1,0:T(8,128)(2,1)S(1)}, u32[]{:S(2)}, u32[]{:S(2)}) collective-permute-start(bf16[128,2176]{1,0:T(8,128)(2,1)S(1)} %broadcast_select_fusion), channel_id=1, source_target_pairs={{0,8},{4,20},{8,0},{12,28},{16,24},{20,4},{24,16},{28,12},{1,9},{5... | collective-permute-start | bytes 1671176 | tf_op jit(solution)/shard_map/ppermute | solution.py:536
  110.5 2.7 %unpack.1 = bf16[512,512]{1,0:T(8,128)(2,1)} custom-call(s32[1,512]{1,0:T(1,128)S(1)} %copy-done.11, bf16[256,512]{1,0:T(8,128)(2,1)S(1)} %copy-done.8, bf16[256,512]{1,0:T(8,128)(2,1)} %collective-permute-done.19.refs_1_, bf16[256,512]{1,0:T(8,128)(2,1)} %collective-permute-done.20.refs_2_, bf16[256,512]{1,0:T(8,128)(2,1)} %collective-permute-done.21.refs_3_), custom_call_target="tpu_custom_call" | custom-call | flops 3149824 | bytes 1574912 | tf_op jit(solution)/shard_map/unpack/pallas_call | solution.py:460
  113.1 4.8 %collective-permute-done.26 = bf16[128,2176]{1,0:T(8,128)(2,1)S(1)} collective-permute-done((bf16[128,2176]{1,0:T(8,128)(2,1)S(1)}, bf16[128,2176]{1,0:T(8,128)(2,1)S(1)}, u32[]{:S(2)}, u32[]{:S(2)}) %collective-permute-start.26) | collective-permute-done | bytes 557088 | tf_op jit(solution)/shard_map/ppermute | solution.py:536
  118.3 1.4 %split.2 = (f32[512,1536]{1,0:T(8,128)}, f32[512,512]{1,0:T(8,128)}, f32[1,512]{1,0:T(1,128)}) custom-call(s32[1]{0:T(128)S(6)} %and.19.side_ref, bf16[256,2176]{1,0:T(8,128)(2,1)S(1)} %maximum_select_fusion.sums_ref), custom_call_target="tpu_custom_call" | custom-call | bytes 4194304 | tf_op jit(solution)/shard_map/split/pallas_call | solution.py:545
  119.7 1.3 %collective-permute-done.27.sums_ref = bf16[256,2176]{1,0:T(8,128)(2,1)S(1)} collective-permute-done((bf16[256,2176]{1,0:T(8,128)(2,1)S(1)}, bf16[256,2176]{1,0:T(8,128)(2,1)S(1)}, u32[]{:S(2)}, u32[]{:S(2)}) %collective-permute-start.27) | collective-permute-done | bytes 1114144 | tf_op jit(solution)/shard_map/ppermute | solution.py:713
  121.0 1.3 %split.3 = (f32[512,1536]{1,0:T(8,128)}, f32[512,512]{1,0:T(8,128)}, f32[1,512]{1,0:T(1,128)}) custom-call(s32[1]{0:T(128)S(6)} %sub.3.side_ref, bf16[256,2176]{1,0:T(8,128)(2,1)S(1)} %collective-permute-done.27.sums_ref, f32[512,1536]{1,0:T(8,128)} %get-tuple-element.130.refs_0_, ...), custom_call_target="tpu_custom_call", output_to_operand_aliasing={{0}: (2, {}), {1}: (3, {}), {2}: (4, {})} | custom-call | bytes 4194304 | tf_op jit(solution)/shard_map/split/pallas_call | solution.py:545
  (80 shorter events, 1.6 us)
Async XLA Ops:
  4.4 11.4 %collective-permute-start.7 = (bf16[512,512]{1,0:T(8,128)(2,1)}, bf16[512,512]{1,0:T(8,128)(2,1)S(1)}, u32[]{:S(2)}, u32[]{:S(2)}) collective-permute-start(bf16[512,512]{1,0:T(8,128)(2,1)} %get-tuple-element.79), channel_id=1, source_target_pairs={{0,4},{4,0},{8,12},{12,8},{16,20},{20,16},{24,28},{28,24},{1,5},{5... | collective-permute-start | bytes 1572872 | tf_op jit(solution)/shard_map/ppermute | solution.py:612
  4.9 4.5 %collective-permute-start = (bf16[144,512]{1,0:T(8,128)(2,1)}, bf16[144,512]{1,0:T(8,128)(2,1)S(1)}, u32[]{:S(2)}, u32[]{:S(2)}) collective-permute-start(bf16[144,512]{1,0:T(8,128)(2,1)} %get-tuple-element.71), channel_id=1, source_target_pairs={{0,4},{4,0},{8,12},{12,8},{16,20},{20,16},{24,28},{28,24},{1,5},{5... | collective-permute-start | bytes 442376 | tf_op jit(solution)/shard_map/ppermute | solution.py:415
  5.0 7.8 %collective-permute-start.1 = (bf16[144,512]{1,0:T(8,128)(2,1)}, bf16[144,512]{1,0:T(8,128)(2,1)S(1)}, u32[]{:S(2)}, u32[]{:S(2)}) collective-permute-start(bf16[144,512]{1,0:T(8,128)(2,1)} %get-tuple-element.72), channel_id=1, source_target_pairs={{0,8},{4,12},{8,0},{12,4},{16,24},{20,28},{24,16},{28,20},{1,9},{5... | collective-permute-start | bytes 442376 | tf_op jit(solution)/shard_map/ppermute | solution.py:415
  7.9 9.7 %collective-permute-start.2 = (bf16[144,512]{1,0:T(8,128)(2,1)}, bf16[144,512]{1,0:T(8,128)(2,1)S(1)}, u32[]{:S(2)}, u32[]{:S(2)}) collective-permute-start(bf16[144,512]{1,0:T(8,128)(2,1)} %get-tuple-element.73), channel_id=1, source_target_pairs={{0,12},{4,8},{8,4},{12,0},{16,28},{20,24},{24,20},{28,16},{1,13},{... | collective-permute-start | bytes 442376 | tf_op jit(solution)/shard_map/ppermute | solution.py:415
  7.9 9.7 %collective-permute-start.3 = (bf16[144,512]{1,0:T(8,128)(2,1)}, bf16[144,512]{1,0:T(8,128)(2,1)S(1)}, u32[]{:S(2)}, u32[]{:S(2)}) collective-permute-start(bf16[144,512]{1,0:T(8,128)(2,1)} %get-tuple-element.74), channel_id=1, source_target_pairs={{0,16},{4,20},{8,24},{12,28},{16,0},{20,4},{24,8},{28,12},{1,17},{... | collective-permute-start | bytes 442376 | tf_op jit(solution)/shard_map/ppermute | solution.py:415
  9.4 17.5 %copy-start.16 = (bf16[144,512]{1,0:T(8,128)(2,1)}, bf16[144,512]{1,0:T(8,128)(2,1)S(1)}, u32[]{:S(2)}) copy-start(bf16[144,512]{1,0:T(8,128)(2,1)S(1)} %collective-permute-done.refs_1_) | copy-start | bytes 442372
  9.4 13.8 %collective-permute-start.4 = (bf16[144,512]{1,0:T(8,128)(2,1)}, bf16[144,512]{1,0:T(8,128)(2,1)S(1)}, u32[]{:S(2)}, u32[]{:S(2)}) collective-permute-start(bf16[144,512]{1,0:T(8,128)(2,1)} %get-tuple-element.75), channel_id=1, source_target_pairs={{0,20},{4,16},{8,28},{12,24},{16,4},{20,0},{24,12},{28,8},{1,21},{... | collective-permute-start | bytes 442376 | tf_op jit(solution)/shard_map/ppermute | solution.py:415
  12.7 14.2 %copy-start.17 = (bf16[144,512]{1,0:T(8,128)(2,1)}, bf16[144,512]{1,0:T(8,128)(2,1)S(1)}, u32[]{:S(2)}) copy-start(bf16[144,512]{1,0:T(8,128)(2,1)S(1)} %collective-permute-done.1.refs_2_) | copy-start | bytes 442372
  12.7 10.5 %collective-permute-start.5 = (bf16[144,512]{1,0:T(8,128)(2,1)}, bf16[144,512]{1,0:T(8,128)(2,1)S(1)}, u32[]{:S(2)}, u32[]{:S(2)}) collective-permute-start(bf16[144,512]{1,0:T(8,128)(2,1)} %get-tuple-element.76), channel_id=1, source_target_pairs={{0,24},{4,28},{8,16},{12,20},{16,8},{20,12},{24,0},{28,4},{1,25},{... | collective-permute-start | bytes 442376 | tf_op jit(solution)/shard_map/ppermute | solution.py:415
  15.8 7.5 %collective-permute-start.6 = (bf16[144,512]{1,0:T(8,128)(2,1)}, bf16[144,512]{1,0:T(8,128)(2,1)S(1)}, u32[]{:S(2)}, u32[]{:S(2)}) collective-permute-start(bf16[144,512]{1,0:T(8,128)(2,1)} %get-tuple-element.77), channel_id=1, source_target_pairs={{0,28},{4,24},{8,20},{12,16},{16,12},{20,8},{24,4},{28,0},{1,29},{... | collective-permute-start | bytes 442376 | tf_op jit(solution)/shard_map/ppermute | solution.py:415
  15.8 1.0 copy-start.5
  17.6 9.3 %copy-start.18 = (bf16[144,512]{1,0:T(8,128)(2,1)}, bf16[144,512]{1,0:T(8,128)(2,1)S(1)}, u32[]{:S(2)}) copy-start(bf16[144,512]{1,0:T(8,128)(2,1)S(1)} %collective-permute-done.2.refs_3_) | copy-start | bytes 442372
  17.6 9.3 %copy-start.19 = (bf16[144,512]{1,0:T(8,128)(2,1)}, bf16[144,512]{1,0:T(8,128)(2,1)S(1)}, u32[]{:S(2)}) copy-start(bf16[144,512]{1,0:T(8,128)(2,1)S(1)} %collective-permute-done.3.refs_4_) | copy-start | bytes 442372
  23.3 3.7 %copy-start.20 = (bf16[144,512]{1,0:T(8,128)(2,1)}, bf16[144,512]{1,0:T(8,128)(2,1)S(1)}, u32[]{:S(2)}) copy-start(bf16[144,512]{1,0:T(8,128)(2,1)S(1)} %collective-permute-done.4.refs_5_) | copy-start | bytes 442372
  23.3 3.7 %copy-start.21 = (bf16[144,512]{1,0:T(8,128)(2,1)}, bf16[144,512]{1,0:T(8,128)(2,1)S(1)}, u32[]{:S(2)}) copy-start(bf16[144,512]{1,0:T(8,128)(2,1)S(1)} %collective-permute-done.5.refs_6_) | copy-start | bytes 442372
  23.3 3.7 %copy-start.22 = (bf16[144,512]{1,0:T(8,128)(2,1)}, bf16[144,512]{1,0:T(8,128)(2,1)S(1)}, u32[]{:S(2)}) copy-start(bf16[144,512]{1,0:T(8,128)(2,1)S(1)} %collective-permute-done.6.refs_7_) | copy-start | bytes 442372
  23.3 13.5 %collective-permute-start.10 = (bf16[256,512]{1,0:T(8,128)(2,1)S(1)}, bf16[256,512]{1,0:T(8,128)(2,1)S(1)}, u32[]{:S(2)}, u32[]{:S(2)}) collective-permute-start(bf16[256,512]{1,0:T(8,128)(2,1)S(1)} %get-tuple-element.102), channel_id=1, source_target_pairs={{0,24},{4,28},{8,16},{12,20},{16,8},{20,12},{24,0},{28,4},{1,25},{... | collective-permute-start | bytes 786440 | tf_op jit(solution)/shard_map/ppermute | solution.py:422
  26.3 12.4 %collective-permute-start.8 = (bf16[256,512]{1,0:T(8,128)(2,1)S(1)}, bf16[256,512]{1,0:T(8,128)(2,1)S(1)}, u32[]{:S(2)}, u32[]{:S(2)}) collective-permute-start(bf16[256,512]{1,0:T(8,128)(2,1)S(1)} %get-tuple-element.100), channel_id=1, source_target_pairs={{0,8},{4,12},{8,0},{12,4},{16,24},{20,28},{24,16},{28,20},{1,9},{5... | collective-permute-start | bytes 786440 | tf_op jit(solution)/shard_map/ppermute | solution.py:422
  26.7 12.0 %collective-permute-start.9 = (bf16[256,512]{1,0:T(8,128)(2,1)S(1)}, bf16[256,512]{1,0:T(8,128)(2,1)S(1)}, u32[]{:S(2)}, u32[]{:S(2)}) collective-permute-start(bf16[256,512]{1,0:T(8,128)(2,1)S(1)} %get-tuple-element.101), channel_id=1, source_target_pairs={{0,16},{4,20},{8,24},{12,28},{16,0},{20,4},{24,8},{28,12},{1,17},{... | collective-permute-start | bytes 786440 | tf_op jit(solution)/shard_map/ppermute | solution.py:422
  36.8 1.9 %copy-start.13 = (bf16[256,512]{1,0:T(8,128)(2,1)}, bf16[256,512]{1,0:T(8,128)(2,1)S(1)}, u32[]{:S(2)}) copy-start(bf16[256,512]{1,0:T(8,128)(2,1)S(1)} %collective-permute-done.10.refs_9_) | copy-start | bytes 786436
  38.7 0.8 copy-start.15
  39.5 21.0 %copy-start.6 = (f32[512,128]{1,0:T(8,128)S(1)}, f32[512,128]{1,0:T(8,128)}, u32[]{:S(2)}) copy-start(f32[512,128]{1,0:T(8,128)} %get-tuple-element.107.inv_ref) | copy-start | bytes 786436
  54.3 3.0 %collective-permute-start.12 = (f32[128,2176]{1,0:T(8,128)}, f32[128,2176]{1,0:T(8,128)S(1)}, u32[]{:S(2)}, u32[]{:S(2)}) collective-permute-start(f32[128,2176]{1,0:T(8,128)} %get-tuple-element.106), channel_id=1, source_target_pairs={{0,4},{4,0},{8,12},{12,8},{16,20},{20,16},{24,28},{28,24},{1,5},{5... | collective-permute-start | bytes 3342344 | tf_op jit(solution)/shard_map/ppermute | solution.py:482
  54.4 7.4 %collective-permute-start.11 = (f32[128,2176]{1,0:T(8,128)}, f32[128,2176]{1,0:T(8,128)S(1)}, u32[]{:S(2)}, u32[]{:S(2)}) collective-permute-start(f32[128,2176]{1,0:T(8,128)} %get-tuple-element.104), channel_id=1, source_target_pairs={{0,4},{4,0},{8,12},{12,8},{16,20},{20,16},{24,28},{28,24},{1,5},{5... | collective-permute-start | bytes 3342344 | tf_op jit(solution)/shard_map/ppermute | solution.py:483
  57.3 1.2 %copy-start.1 = (f32[128,2176]{1,0:T(8,128)S(1)}, f32[128,2176]{1,0:T(8,128)}, u32[]{:S(2)}) copy-start(f32[128,2176]{1,0:T(8,128)} %get-tuple-element.105.refs_0_) | copy-start | bytes 3342340
  58.6 1.9 %copy-start.2 = (f32[512,512]{1,0:T(8,128)S(1)}, f32[512,512]{1,0:T(8,128)}, u32[]{:S(2)}) copy-start(f32[512,512]{1,0:T(8,128)} %get-tuple-element.96.refs_3_.xhat_ref) | copy-start | bytes 3145732
  58.6 1.9 %copy-start.3 = (f32[512,512]{1,0:T(8,128)S(1)}, f32[512,512]{1,0:T(8,128)}, u32[]{:S(2)}) copy-start(f32[512,512]{1,0:T(8,128)} %get-tuple-element.109.d_normed_ref) | copy-start | bytes 3145732
  58.6 1.9 %copy-start.4 = (bf16[512,512]{1,0:T(8,128)(2,1)S(1)}, bf16[512,512]{1,0:T(8,128)(2,1)}, u32[]{:S(2)}) copy-start(bf16[512,512]{1,0:T(8,128)(2,1)} %get-tuple-element.108.serial_grad_ref) | copy-start | bytes 1572868
  58.6 1.9 %copy-start.9 = (s32[1,1024]{1,0:T(1,128)S(1)}, s32[1,1024]{1,0:T(1,128)}, u32[]{:S(2)}) copy-start(s32[1,1024]{1,0:T(1,128)} %get-tuple-element.92.pos_ref) | copy-start | bytes 12292
  58.6 1.9 %copy-start.10 = (f32[512]{0:T(512)S(1)}, f32[512]{0:T(512)}, u32[]{:S(2)}) copy-start(f32[512]{0:T(512)} %param.11) | copy-start | bytes 6148
  58.9 9.6 %collective-permute-start.13 = (s16[128,2176]{1,0:T(8,128)(2,1)S(1)}, s16[128,2176]{1,0:T(8,128)(2,1)S(1)}, u32[]{:S(2)}, u32[]{:S(2)}) collective-permute-start(s16[128,2176]{1,0:T(8,128)(2,1)S(1)} %code_first.1), channel_id=1, source_target_pairs={{0,8},{4,20},{8,0},{12,28},{16,24},{20,4},{24,16},{28,12},{1,9},{5... | collective-permute-start | bytes 1671176 | tf_op jit(solution)/shard_map/ppermute | solution.py:485
  60.6 8.0 %copy-start = (f32[128,2176]{1,0:T(8,128)S(1)}, f32[128,2176]{1,0:T(8,128)}, u32[]{:S(2)}) copy-start(f32[128,2176]{1,0:T(8,128)} %get-tuple-element.103.refs_0_) | copy-start | bytes 3342340
  61.7 8.5 %collective-permute-start.18 = (bf16[512,512]{1,0:T(8,128)(2,1)S(1)}, bf16[512,512]{1,0:T(8,128)(2,1)S(1)}, u32[]{:S(2)}, u32[]{:S(2)}) collective-permute-start(bf16[512,512]{1,0:T(8,128)(2,1)S(1)} %get-tuple-element.117), channel_id=1, source_target_pairs={{0,4},{4,0},{8,12},{12,8},{16,20},{20,16},{24,28},{28,24},{1,5},{5... | collective-permute-start | bytes 1572872 | tf_op jit(solution)/shard_map/ppermute | solution.py:612
  68.8 7.9 %collective-permute-start.14 = (s16[64,2176]{1,0:T(8,128)(2,1)S(1)}, s16[64,2176]{1,0:T(8,128)(2,1)S(1)}, u32[]{:S(2)}, u32[]{:S(2)}) collective-permute-start(s16[64,2176]{1,0:T(8,128)(2,1)S(1)} %code_second.1), channel_id=1, source_target_pairs={{0,16},{4,12},{8,24},{12,4},{16,0},{20,28},{24,8},{28,20},{1,17},{... | collective-permute-start | bytes 835592 | tf_op jit(solution)/shard_map/ppermute | solution.py:491
  71.8 16.0 %collective-permute-start.19 = (bf16[256,512]{1,0:T(8,128)(2,1)}, bf16[256,512]{1,0:T(8,128)(2,1)}, u32[]{:S(2)}, u32[]{:S(2)}) collective-permute-start(bf16[256,512]{1,0:T(8,128)(2,1)} %get-tuple-element.119), channel_id=1, source_target_pairs={{0,8},{4,12},{8,0},{12,4},{16,24},{20,28},{24,16},{28,20},{1,9},{5... | collective-permute-start | bytes 786440 | tf_op jit(solution)/shard_map/ppermute | solution.py:422
  73.4 14.5 %collective-permute-start.20 = (bf16[256,512]{1,0:T(8,128)(2,1)}, bf16[256,512]{1,0:T(8,128)(2,1)}, u32[]{:S(2)}, u32[]{:S(2)}) collective-permute-start(bf16[256,512]{1,0:T(8,128)(2,1)} %get-tuple-element.120), channel_id=1, source_target_pairs={{0,16},{4,20},{8,24},{12,28},{16,0},{20,4},{24,8},{28,12},{1,17},{... | collective-permute-start | bytes 786440 | tf_op jit(solution)/shard_map/ppermute | solution.py:422
  74.1 13.8 %collective-permute-start.21 = (bf16[256,512]{1,0:T(8,128)(2,1)}, bf16[256,512]{1,0:T(8,128)(2,1)}, u32[]{:S(2)}, u32[]{:S(2)}) collective-permute-start(bf16[256,512]{1,0:T(8,128)(2,1)} %get-tuple-element.121), channel_id=1, source_target_pairs={{0,24},{4,28},{8,16},{12,20},{16,8},{20,12},{24,0},{28,4},{1,25},{... | collective-permute-start | bytes 786440 | tf_op jit(solution)/shard_map/ppermute | solution.py:422
  77.2 4.4 %collective-permute-start.15 = (s16[16,2176]{1,0:T(8,128)(2,1)S(1)}, s16[16,2176]{1,0:T(8,128)(2,1)S(1)}, u32[]{:S(2)}, u32[]{:S(2)}) collective-permute-start(s16[16,2176]{1,0:T(8,128)(2,1)S(1)} %get-tuple-element.113), channel_id=1, source_target_pairs={{0,1},{1,0},{2,3},{3,2},{4,5},{5,4},{6,7},{7,6},{8,9},{9,8},{10,11... | collective-permute-start | bytes 208904 | tf_op jit(solution)/shard_map/ppermute | solution.py:415
  78.8 6.3 %collective-permute-start.16 = (s16[16,2176]{1,0:T(8,128)(2,1)S(1)}, s16[16,2176]{1,0:T(8,128)(2,1)S(1)}, u32[]{:S(2)}, u32[]{:S(2)}) collective-permute-start(s16[16,2176]{1,0:T(8,128)(2,1)S(1)} %get-tuple-element.114), channel_id=1, source_target_pairs={{0,2},{1,3},{2,0},{3,1},{4,6},{5,7},{6,4},{7,5},{8,10},{9,11},{10,... | collective-permute-start | bytes 208904 | tf_op jit(solution)/shard_map/ppermute | solution.py:415
  81.6 6.1 %collective-permute-start.17 = (s16[16,2176]{1,0:T(8,128)(2,1)S(1)}, s16[16,2176]{1,0:T(8,128)(2,1)S(1)}, u32[]{:S(2)}, u32[]{:S(2)}) collective-permute-start(s16[16,2176]{1,0:T(8,128)(2,1)S(1)} %get-tuple-element.115), channel_id=1, source_target_pairs={{0,3},{1,2},{2,1},{3,0},{4,7},{5,6},{6,5},{7,4},{8,11},{9,10},{10,... | collective-permute-start | bytes 208904 | tf_op jit(solution)/shard_map/ppermute | solution.py:415
  87.9 4.6 %collective-permute-start.22 = (bf16[16,2176]{1,0:T(8,128)(2,1)S(1)}, bf16[16,2176]{1,0:T(8,128)(2,1)S(1)}, u32[]{:S(2)}, u32[]{:S(2)}) collective-permute-start(bf16[16,2176]{1,0:T(8,128)(2,1)S(1)} %finish.1), channel_id=1, source_target_pairs={{0,1},{1,0},{2,3},{3,2},{4,5},{5,4},{6,7},{7,6},{8,9},{9,8},{10,11... | collective-permute-start | bytes 208904 | tf_op jit(solution)/shard_map/ppermute | solution.py:415
  88.3 7.2 %collective-permute-start.23 = (bf16[16,2176]{1,0:T(8,128)(2,1)S(1)}, bf16[16,2176]{1,0:T(8,128)(2,1)S(1)}, u32[]{:S(2)}, u32[]{:S(2)}) collective-permute-start(bf16[16,2176]{1,0:T(8,128)(2,1)S(1)} %finish.1), channel_id=1, source_target_pairs={{0,2},{1,3},{2,0},{3,1},{4,6},{5,7},{6,4},{7,5},{8,10},{9,11},{10,... | collective-permute-start | bytes 208904 | tf_op jit(solution)/shard_map/ppermute | solution.py:415
  92.5 6.1 %collective-permute-start.24 = (bf16[16,2176]{1,0:T(8,128)(2,1)S(1)}, bf16[16,2176]{1,0:T(8,128)(2,1)S(1)}, u32[]{:S(2)}, u32[]{:S(2)}) collective-permute-start(bf16[16,2176]{1,0:T(8,128)(2,1)S(1)} %finish.1), channel_id=1, source_target_pairs={{0,3},{1,2},{2,1},{3,0},{4,7},{5,6},{6,5},{7,4},{8,11},{9,10},{10,... | collective-permute-start | bytes 208904 | tf_op jit(solution)/shard_map/ppermute | solution.py:415
  98.8 9.2 %collective-permute-start.25 = (bf16[64,2176]{1,0:T(8,128)(2,1)S(1)}, bf16[64,2176]{1,0:T(8,128)(2,1)S(1)}, u32[]{:S(2)}, u32[]{:S(2)}) collective-permute-start(bf16[64,2176]{1,0:T(8,128)(2,1)S(1)} %pad_maximum_fusion.1), channel_id=1, source_target_pairs={{0,16},{4,12},{8,24},{12,4},{16,0},{20,28},{24,8},{28,20},{1,17},{... | collective-permute-start | bytes 835592 | tf_op jit(solution)/shard_map/ppermute | solution.py:536
  108.1 2.4 %copy-start.8 = (bf16[256,512]{1,0:T(8,128)(2,1)S(1)}, bf16[256,512]{1,0:T(8,128)(2,1)}, u32[]{:S(2)}) copy-start(bf16[256,512]{1,0:T(8,128)(2,1)} %copy-done.7) | copy-start | bytes 786436
  108.1 2.4 %copy-start.11 = (s32[1,512]{1,0:T(1,128)S(1)}, s32[1,512]{1,0:T(1,128)}, u32[]{:S(2)}) copy-start(s32[1,512]{1,0:T(1,128)} %get-tuple-element.123.slot_ref) | copy-start | bytes 6148
  108.2 9.8 %collective-permute-start.26 = (bf16[128,2176]{1,0:T(8,128)(2,1)S(1)}, bf16[128,2176]{1,0:T(8,128)(2,1)S(1)}, u32[]{:S(2)}, u32[]{:S(2)}) collective-permute-start(bf16[128,2176]{1,0:T(8,128)(2,1)S(1)} %broadcast_select_fusion), channel_id=1, source_target_pairs={{0,8},{4,20},{8,0},{12,28},{16,24},{20,4},{24,16},{28,12},{1,9},{5... | collective-permute-start | bytes 1671176 | tf_op jit(solution)/shard_map/ppermute | solution.py:536
  118.2 2.8 %collective-permute-start.27 = (bf16[256,2176]{1,0:T(8,128)(2,1)S(1)}, bf16[256,2176]{1,0:T(8,128)(2,1)S(1)}, u32[]{:S(2)}, u32[]{:S(2)}) collective-permute-start(bf16[256,2176]{1,0:T(8,128)(2,1)S(1)} %maximum_select_fusion.sums_ref), channel_id=1, source_target_pairs={{0,4},{4,0},{8,12},{12,8},{16,20},{20,16},{24,28},{28,24},{1,5},{5... | collective-permute-start | bytes 3342344 | tf_op jit(solution)/shard_map/ppermute | solution.py:713
  (3 other events, 2.1 us)

commit v17 on v16

--- a/solution.py
+++ b/solution.py
@@ -471,7 +471,19 @@
 
 def message(terms, part, name):
     rows, width = terms[0].shape
-    rows = rows if part == "all" else rows // 2
+    if part == "all":
+        spec = pl.BlockSpec((rows // 4, width), lambda i: (i, 0))
+        return pl.pallas_call(
+            functools.partial(message_kernel, part),
+            grid=(4,),
+            out_shape=shape_of((rows, width), jnp.int16),
+            in_specs=[spec] * len(terms),
+            out_specs=spec,
+            compiler_params=params(60),
+            cost_estimate=pl.CostEstimate(flops=2 * MIB, bytes_accessed=3 * MIB, transcendentals=0),
+            name=name,
+        )(*terms)
+    rows = rows // 2
     return small_kernel(
         functools.partial(message_kernel, part), [shape_of((rows, width), jnp.int16)], terms, name=name
     )[0]

time: 123 us -> 126 us (1.024)
  Pallas kernels: 37.1 us -> 40.5 us
  waiting for transfers between devices: 44.3 us -> 42.1 us
  local copies, waits for them, and re-layouts: 4.77 us -> 6.95 us
    pallas_call x0 -> x1, Pallas kernels: none -> 3.79 us  [message(): pl.pallas_call(functools.partial(message_kernel, part), grid=(4,), out_sh...]
    ppermute x1, waiting for transfers between devices: 6.74 us -> 4.57 us  [first_step(): return [own_keep, got_keep, lax.ppermute(sent, 'seq', steps[0][0])]]
    unnamed x54, local copies, waits for them, and re-layouts: 4.76 us -> 6.94 us
    pallas_call x8 -> x7, Pallas kernels: 5.98 us -> 5.64 us  [small_kernel(): pl.pallas_call(kernel, out_shape=outs, in_specs=[in_smem] * scalars + [in...]
  transfers between devices with their start and end apart: 28 -> 28, of which waited for: 13 -> 13; matrix products, arithmetic and copies ran while one was open for 0% -> 0% of each run, Pallas kernels for 14% -> 16%
where the time goes in v17:
time: 126 us
  waiting for transfers between devices  42.1 us (33%)
  Pallas kernels  40.5 us (32%)
  starting transfers between devices  34.8 us (28%)
  local copies, waits for them, and re-layouts  6.95 us (6%)
    ppermute x13, starting transfers between devices, by_distance(): lax.ppermute(blocks[k], axis, [(i, i ^ k) for i in range(count)])  20.3 us
    ppermute x13, waiting for transfers between devices, by_distance(): lax.ppermute(blocks[k], axis, [(i, i ^ k) for i in range(count)])  17.4 us
    pallas_call x1, Pallas kernels, per_device(): pl.pallas_call(functools.partial(backward_kernel, n_seq, chip_bits), grid...  14.7 us
    ppermute x2, waiting for transfers between devices, share_in_plane(): other = lax.ppermute(part, 'seq', pairs)  13.1 us
    pallas_call x1, Pallas kernels, per_device(): pl.pallas_call(functools.partial(forward_kernel, n_seq, capacity), grid=(...  9.87 us
    ppermute x6, starting transfers between devices, by_chip(): lax.ppermute(messages[j], 'seq', [(i, i ^ 2 * j) for i in range(count)])  7.1 us
    unnamed x54, local copies, waits for them, and re-layouts  6.94 us
    pallas_call x7, Pallas kernels, small_kernel(): pl.pallas_call(kernel, out_shape=outs, in_specs=[in_smem] * scalars + [in...  5.64 us
  transfers between devices with their start and end apart: 28, of which 13 were waited for; matrix products, arithmetic and copies ran while one was open for 0% of the time, Pallas kernels for 16%

profile of v17, /device:TPU:0, one launch (start us, length us, event | category | flops | bytes accessed | tf_op | source)
XLA Modules:
  0.0 125.7 jit_solution(15475997680411973019)
XLA Ops:
  0.6 3.7 %pack.1 = (s32[1,512]{1,0:T(1,128)}, bf16[512,512]{1,0:T(8,128)(2,1)}, bf16[512,512]{1,0:T(8,128)(2,1)}, bf16[144,512]{1,0:T(8,128)(2,1)}, bf16[144,512]{1,0:T(8...) custom-call(s32[1]{0:T(128)} %bitcast.1.me_ref, ...), custom_call_target="tpu_custom_call" | custom-call | flops 1073741824 | bytes 4194304 | tf_op jit(solution)/shard_map/pack/pallas_call | solution.py:600
  4.4 0.5 collective-permute-start.7
  5.0 2.9 %collective-permute-start.1 = (bf16[144,512]{1,0:T(8,128)(2,1)}, bf16[144,512]{1,0:T(8,128)(2,1)S(1)}, u32[]{:S(2)}, u32[]{:S(2)}) collective-permute-start(bf16[144,512]{1,0:T(8,128)(2,1)} %get-tuple-element.72), channel_id=1, source_target_pairs={{0,8},{4,12},{8,0},{12,4},{16,24},{20,28},{24,16},{28,20},{1,9},{5... | collective-permute-start | bytes 442376 | tf_op jit(solution)/shard_map/ppermute | solution.py:415
  7.9 1.5 %collective-permute-start.3 = (bf16[144,512]{1,0:T(8,128)(2,1)}, bf16[144,512]{1,0:T(8,128)(2,1)S(1)}, u32[]{:S(2)}, u32[]{:S(2)}) collective-permute-start(bf16[144,512]{1,0:T(8,128)(2,1)} %get-tuple-element.74), channel_id=1, source_target_pairs={{0,16},{4,20},{8,24},{12,28},{16,0},{20,4},{24,8},{28,12},{1,17},{... | collective-permute-start | bytes 442376 | tf_op jit(solution)/shard_map/ppermute | solution.py:415
  9.7 3.0 %collective-permute-done.1.refs_2_ = bf16[144,512]{1,0:T(8,128)(2,1)S(1)} collective-permute-done((bf16[144,512]{1,0:T(8,128)(2,1)}, bf16[144,512]{1,0:T(8,128)(2,1)S(1)}, u32[]{:S(2)}, u32[]{:S(2)}) %collective-permute-start.1) | collective-permute-done | bytes 147488 | tf_op jit(solution)/shard_map/ppermute | solution.py:415
  12.7 3.0 %collective-permute-start.5 = (bf16[144,512]{1,0:T(8,128)(2,1)}, bf16[144,512]{1,0:T(8,128)(2,1)S(1)}, u32[]{:S(2)}, u32[]{:S(2)}) collective-permute-start(bf16[144,512]{1,0:T(8,128)(2,1)} %get-tuple-element.76), channel_id=1, source_target_pairs={{0,24},{4,28},{8,16},{12,20},{16,8},{20,12},{24,0},{28,4},{1,25},{... | collective-permute-start | bytes 442376 | tf_op jit(solution)/shard_map/ppermute | solution.py:415
  15.8 1.0 copy-done.4
  16.9 0.7 copy-done.11
  17.6 5.6 %collective-permute-done.4.refs_5_ = bf16[144,512]{1,0:T(8,128)(2,1)S(1)} collective-permute-done((bf16[144,512]{1,0:T(8,128)(2,1)}, bf16[144,512]{1,0:T(8,128)(2,1)S(1)}, u32[]{:S(2)}, u32[]{:S(2)}) %collective-permute-start.4) | collective-permute-done | bytes 147488 | tf_op jit(solution)/shard_map/ppermute | solution.py:415
  23.3 3.0 %collective-permute-start.10 = (bf16[256,512]{1,0:T(8,128)(2,1)S(1)}, bf16[256,512]{1,0:T(8,128)(2,1)S(1)}, u32[]{:S(2)}, u32[]{:S(2)}) collective-permute-start(bf16[256,512]{1,0:T(8,128)(2,1)S(1)} %get-tuple-element.102), channel_id=1, source_target_pairs={{0,24},{4,28},{8,16},{12,20},{16,8},{20,12},{24,0},{28,4},{1,25},{... | collective-permute-start | bytes 786440 | tf_op jit(solution)/shard_map/ppermute | solution.py:422
  26.3 0.4 collective-permute-start.8
  27.0 9.9 %forward.1 = (s32[1,1024]{1,0:T(1,128)}, f32[512,512]{1,0:T(8,128)}, f32[512,128]{1,0:T(8,128)}, bf16[512,512]{1,0:T(8,128)(2,1)}, bf16[512,1536]{1,0:T(8,128)(2...) custom-call(bf16[512,1536]{1,0:T(8,128)(2,1)} %refs_2_.1, f32[1,512]{1,0:T(1,128)} %bitcast.24, ...), custom_call_target="tpu_custom_call" | custom-call | flops 2952790016 | bytes 16777216 | tf_op jit(solution)/shard_map/forward/pallas_call | solution.py:632
  36.9 1.9 %collective-permute-done.8.refs_7_ = bf16[256,512]{1,0:T(8,128)(2,1)S(1)} collective-permute-done((bf16[256,512]{1,0:T(8,128)(2,1)S(1)}, bf16[256,512]{1,0:T(8,128)(2,1)S(1)}, u32[]{:S(2)}, u32[]{:S(2)}) %collective-permute-start.8) | collective-permute-done | bytes 262176 | tf_op jit(solution)/shard_map/ppermute | solution.py:422
  38.7 0.7 copy-done.14
  39.5 14.7 %backward.1 = (f32[128,2176]{1,0:T(8,128)}, f32[128,2176]{1,0:T(8,128)}, f32[128,2176]{1,0:T(8,128)}, f32[128,2176]{1,0:T(8,128)}, bf16[512,512]{1,0:T(8,128)(2,1)}, /*index=5*/f32[512,512]{1,0:T(8,128)}) custom-call(s32[1]{0:T(128)} %bitcast.1.me_ref, s32[1,1024]{1,0:T(1,128)} %get-tuple-element.92.pos_ref, bf16[512,512]{1,0:T(8,128)(2,1)} %w_proj_ref.1, ...), custom_call_target="tpu_custom_call" | custom-call | flops 4294967296 | bytes 16777216 | tf_op jit(solution)/shard_map/backward/pallas_call | solution.py:668
  54.3 0.5 collective-permute-start.11
  54.8 2.5 %collective-permute-done.12.refs_1_ = f32[128,2176]{1,0:T(8,128)S(1)} collective-permute-done((f32[128,2176]{1,0:T(8,128)}, f32[128,2176]{1,0:T(8,128)S(1)}, u32[]{:S(2)}, u32[]{:S(2)}) %collective-permute-start.12) | collective-permute-done | bytes 1114144 | tf_op jit(solution)/shard_map/ppermute | solution.py:494
  57.3 1.0 copy-done.12
  58.3 3.8 %code_first.1 = s16[128,2176]{1,0:T(8,128)(2,1)} custom-call(f32[128,2176]{1,0:T(8,128)} %get-tuple-element.105.refs_0_, f32[128,2176]{1,0:T(8,128)} %copy-done.12), custom_call_target="tpu_custom_call" | custom-call | flops 2097152 | bytes 3145728 | tf_op jit(solution)/shard_map/code_first/pallas_call | solution.py:476
  62.1 1.5 %collective-permute-start.13 = (s16[128,2176]{1,0:T(8,128)(2,1)}, s16[128,2176]{1,0:T(8,128)(2,1)S(1)}, u32[]{:S(2)}, u32[]{:S(2)}) collective-permute-start(s16[128,2176]{1,0:T(8,128)(2,1)} %code_first.1), channel_id=1, source_target_pairs={{0,8},{4,20},{8,0},{12,28},{16,24},{20,4},{24,16},{28,12},{1,9},{5... | collective-permute-start | bytes 1671176 | tf_op jit(solution)/shard_map/ppermute | solution.py:497
  63.7 1.2 copy-done.1
  64.9 1.2 copy-done.2
  66.1 1.1 residual.1
  67.3 4.6 %collective-permute-done.13.refs_2_ = s16[128,2176]{1,0:T(8,128)(2,1)S(1)} collective-permute-done((s16[128,2176]{1,0:T(8,128)(2,1)}, s16[128,2176]{1,0:T(8,128)(2,1)S(1)}, u32[]{:S(2)}, u32[]{:S(2)}) %collective-permute-start.13) | collective-permute-done | bytes 557088 | tf_op jit(solution)/shard_map/ppermute | solution.py:497
  72.1 1.4 %collective-permute-start.14 = (s16[64,2176]{1,0:T(8,128)(2,1)S(1)}, s16[64,2176]{1,0:T(8,128)(2,1)S(1)}, u32[]{:S(2)}, u32[]{:S(2)}) collective-permute-start(s16[64,2176]{1,0:T(8,128)(2,1)S(1)} %code_second.1), channel_id=1, source_target_pairs={{0,16},{4,12},{8,24},{12,4},{16,0},{20,28},{24,8},{28,20},{1,17},{... | collective-permute-start | bytes 835592 | tf_op jit(solution)/shard_map/ppermute | solution.py:503
  73.5 0.9 pair_up.3
  74.4 0.7 copy-done.6
  75.1 1.5 %collective-permute-start.19 = (bf16[256,512]{1,0:T(8,128)(2,1)}, bf16[256,512]{1,0:T(8,128)(2,1)}, u32[]{:S(2)}, u32[]{:S(2)}) collective-permute-start(bf16[256,512]{1,0:T(8,128)(2,1)} %get-tuple-element.119), channel_id=1, source_target_pairs={{0,8},{4,12},{8,0},{12,4},{16,24},{20,28},{24,16},{28,20},{1,9},{5... | collective-permute-start | bytes 786440 | tf_op jit(solution)/shard_map/ppermute | solution.py:422
  76.7 0.7 collective-permute-start.20
  77.4 1.2 collective-permute-start.21
  78.6 1.4 %collective-permute-done.14.refs_3_ = s16[64,2176]{1,0:T(8,128)(2,1)S(1)} collective-permute-done((s16[64,2176]{1,0:T(8,128)(2,1)S(1)}, s16[64,2176]{1,0:T(8,128)(2,1)S(1)}, u32[]{:S(2)}, u32[]{:S(2)}) %collective-permute-start.14) | collective-permute-done | bytes 278560 | tf_op jit(solution)/shard_map/ppermute | solution.py:503
  80.0 0.5 code_planes.1
  80.5 1.6 %collective-permute-start.15 = (s16[16,2176]{1,0:T(8,128)(2,1)S(1)}, s16[16,2176]{1,0:T(8,128)(2,1)S(1)}, u32[]{:S(2)}, u32[]{:S(2)}) collective-permute-start(s16[16,2176]{1,0:T(8,128)(2,1)S(1)} %get-tuple-element.113), channel_id=1, source_target_pairs={{0,1},{1,0},{2,3},{3,2},{4,5},{5,4},{6,7},{7,6},{8,9},{9,8},{10,11... | collective-permute-start | bytes 208904 | tf_op jit(solution)/shard_map/ppermute | solution.py:415
  82.2 2.6 %collective-permute-start.16 = (s16[16,2176]{1,0:T(8,128)(2,1)S(1)}, s16[16,2176]{1,0:T(8,128)(2,1)S(1)}, u32[]{:S(2)}, u32[]{:S(2)}) collective-permute-start(s16[16,2176]{1,0:T(8,128)(2,1)S(1)} %get-tuple-element.114), channel_id=1, source_target_pairs={{0,2},{1,3},{2,0},{3,1},{4,6},{5,7},{6,4},{7,5},{8,10},{9,11},{10,... | collective-permute-start | bytes 208904 | tf_op jit(solution)/shard_map/ppermute | solution.py:415
  84.9 3.6 %collective-permute-start.17 = (s16[16,2176]{1,0:T(8,128)(2,1)S(1)}, s16[16,2176]{1,0:T(8,128)(2,1)S(1)}, u32[]{:S(2)}, u32[]{:S(2)}) collective-permute-start(s16[16,2176]{1,0:T(8,128)(2,1)S(1)} %get-tuple-element.115), channel_id=1, source_target_pairs={{0,3},{1,2},{2,1},{3,0},{4,7},{5,6},{6,5},{7,4},{8,11},{9,10},{10,... | collective-permute-start | bytes 208904 | tf_op jit(solution)/shard_map/ppermute | solution.py:415
  88.5 2.5 %collective-permute-done.17.refs_3_ = s16[16,2176]{1,0:T(8,128)(2,1)S(1)} collective-permute-done((s16[16,2176]{1,0:T(8,128)(2,1)S(1)}, s16[16,2176]{1,0:T(8,128)(2,1)S(1)}, u32[]{:S(2)}, u32[]{:S(2)}) %collective-permute-start.17) | collective-permute-done | bytes 69664 | tf_op jit(solution)/shard_map/ppermute | solution.py:415
  91.2 0.5 collective-permute-start.22
  91.7 4.2 %collective-permute-start.23 = (bf16[16,2176]{1,0:T(8,128)(2,1)S(1)}, bf16[16,2176]{1,0:T(8,128)(2,1)S(1)}, u32[]{:S(2)}, u32[]{:S(2)}) collective-permute-start(bf16[16,2176]{1,0:T(8,128)(2,1)S(1)} %finish.1), channel_id=1, source_target_pairs={{0,2},{1,3},{2,0},{3,1},{4,6},{5,7},{6,4},{7,5},{8,10},{9,11},{10,... | collective-permute-start | bytes 208904 | tf_op jit(solution)/shard_map/ppermute | solution.py:415
  95.8 3.0 %collective-permute-done.23 = bf16[16,2176]{1,0:T(8,128)(2,1)S(1)} collective-permute-done((bf16[16,2176]{1,0:T(8,128)(2,1)S(1)}, bf16[16,2176]{1,0:T(8,128)(2,1)S(1)}, u32[]{:S(2)}, u32[]{:S(2)}) %collective-permute-start.23) | collective-permute-done | bytes 69664 | tf_op jit(solution)/shard_map/ppermute | solution.py:415
  98.9 3.1 %collective-permute-done.24 = bf16[16,2176]{1,0:T(8,128)(2,1)S(1)} collective-permute-done((bf16[16,2176]{1,0:T(8,128)(2,1)S(1)}, bf16[16,2176]{1,0:T(8,128)(2,1)S(1)}, u32[]{:S(2)}, u32[]{:S(2)}) %collective-permute-start.24) | collective-permute-done | bytes 69664 | tf_op jit(solution)/shard_map/ppermute | solution.py:415
  102.1 1.0 collective-permute-start.25
  103.1 8.2 %collective-permute-done.25 = bf16[64,2176]{1,0:T(8,128)(2,1)S(1)} collective-permute-done((bf16[64,2176]{1,0:T(8,128)(2,1)S(1)}, bf16[64,2176]{1,0:T(8,128)(2,1)S(1)}, u32[]{:S(2)}, u32[]{:S(2)}) %collective-permute-start.25) | collective-permute-done | bytes 278560 | tf_op jit(solution)/shard_map/ppermute | solution.py:548
  111.5 2.2 %collective-permute-start.26 = (bf16[128,2176]{1,0:T(8,128)(2,1)S(1)}, bf16[128,2176]{1,0:T(8,128)(2,1)S(1)}, u32[]{:S(2)}, u32[]{:S(2)}) collective-permute-start(bf16[128,2176]{1,0:T(8,128)(2,1)S(1)} %broadcast_select_fusion), channel_id=1, source_target_pairs={{0,8},{4,20},{8,0},{12,28},{16,24},{20,4},{24,16},{28,12},{1,9},{5... | collective-permute-start | bytes 1671176 | tf_op jit(solution)/shard_map/ppermute | solution.py:548
  113.8 2.7 %unpack.1 = bf16[512,512]{1,0:T(8,128)(2,1)} custom-call(s32[1,512]{1,0:T(1,128)S(1)} %copy-done.10, bf16[256,512]{1,0:T(8,128)(2,1)S(1)} %copy-done.7, bf16[256,512]{1,0:T(8,128)(2,1)} %collective-permute-done.19.refs_1_, bf16[256,512]{1,0:T(8,128)(2,1)} %collective-permute-done.20.refs_2_, bf16[256,512]{1,0:T(8,128)(2,1)} %collective-permute-done.21.refs_3_), custom_call_target="tpu_custom_call" | custom-call | flops 3149824 | bytes 1574912 | tf_op jit(solution)/shard_map/unpack/pallas_call | solution.py:460
  116.4 4.8 %collective-permute-done.26 = bf16[128,2176]{1,0:T(8,128)(2,1)S(1)} collective-permute-done((bf16[128,2176]{1,0:T(8,128)(2,1)S(1)}, bf16[128,2176]{1,0:T(8,128)(2,1)S(1)}, u32[]{:S(2)}, u32[]{:S(2)}) %collective-permute-start.26) | collective-permute-done | bytes 557088 | tf_op jit(solution)/shard_map/ppermute | solution.py:548
  121.6 1.4 %split.2 = (f32[512,1536]{1,0:T(8,128)}, f32[512,512]{1,0:T(8,128)}, f32[1,512]{1,0:T(1,128)}) custom-call(s32[1]{0:T(128)S(6)} %and.19.side_ref, bf16[256,2176]{1,0:T(8,128)(2,1)S(1)} %maximum_select_fusion.sums_ref), custom_call_target="tpu_custom_call" | custom-call | bytes 4194304 | tf_op jit(solution)/shard_map/split/pallas_call | solution.py:557
  123.0 1.3 %collective-permute-done.27.sums_ref = bf16[256,2176]{1,0:T(8,128)(2,1)S(1)} collective-permute-done((bf16[256,2176]{1,0:T(8,128)(2,1)S(1)}, bf16[256,2176]{1,0:T(8,128)(2,1)S(1)}, u32[]{:S(2)}, u32[]{:S(2)}) %collective-permute-start.27) | collective-permute-done | bytes 1114144 | tf_op jit(solution)/shard_map/ppermute | solution.py:725
  124.3 1.3 %split.3 = (f32[512,1536]{1,0:T(8,128)}, f32[512,512]{1,0:T(8,128)}, f32[1,512]{1,0:T(1,128)}) custom-call(s32[1]{0:T(128)S(6)} %sub.3.side_ref, bf16[256,2176]{1,0:T(8,128)(2,1)S(1)} %collective-permute-done.27.sums_ref, f32[512,1536]{1,0:T(8,128)} %get-tuple-element.130.refs_0_, ...), custom_call_target="tpu_custom_call", output_to_operand_aliasing={{0}: (2, {}), {1}: (3, {}), {2}: (4, {})} | custom-call | bytes 4194304 | tf_op jit(solution)/shard_map/split/pallas_call | solution.py:557
  (80 shorter events, 2.2 us)
Async XLA Ops:
  4.4 11.4 %collective-permute-start.7 = (bf16[512,512]{1,0:T(8,128)(2,1)}, bf16[512,512]{1,0:T(8,128)(2,1)S(1)}, u32[]{:S(2)}, u32[]{:S(2)}) collective-permute-start(bf16[512,512]{1,0:T(8,128)(2,1)} %get-tuple-element.79), channel_id=1, source_target_pairs={{0,4},{4,0},{8,12},{12,8},{16,20},{20,16},{24,28},{28,24},{1,5},{5... | collective-permute-start | bytes 1572872 | tf_op jit(solution)/shard_map/ppermute | solution.py:624
  4.9 4.5 %collective-permute-start = (bf16[144,512]{1,0:T(8,128)(2,1)}, bf16[144,512]{1,0:T(8,128)(2,1)S(1)}, u32[]{:S(2)}, u32[]{:S(2)}) collective-permute-start(bf16[144,512]{1,0:T(8,128)(2,1)} %get-tuple-element.71), channel_id=1, source_target_pairs={{0,4},{4,0},{8,12},{12,8},{16,20},{20,16},{24,28},{28,24},{1,5},{5... | collective-permute-start | bytes 442376 | tf_op jit(solution)/shard_map/ppermute | solution.py:415
  5.0 7.8 %collective-permute-start.1 = (bf16[144,512]{1,0:T(8,128)(2,1)}, bf16[144,512]{1,0:T(8,128)(2,1)S(1)}, u32[]{:S(2)}, u32[]{:S(2)}) collective-permute-start(bf16[144,512]{1,0:T(8,128)(2,1)} %get-tuple-element.72), channel_id=1, source_target_pairs={{0,8},{4,12},{8,0},{12,4},{16,24},{20,28},{24,16},{28,20},{1,9},{5... | collective-permute-start | bytes 442376 | tf_op jit(solution)/shard_map/ppermute | solution.py:415
  7.9 9.7 %collective-permute-start.2 = (bf16[144,512]{1,0:T(8,128)(2,1)}, bf16[144,512]{1,0:T(8,128)(2,1)S(1)}, u32[]{:S(2)}, u32[]{:S(2)}) collective-permute-start(bf16[144,512]{1,0:T(8,128)(2,1)} %get-tuple-element.73), channel_id=1, source_target_pairs={{0,12},{4,8},{8,4},{12,0},{16,28},{20,24},{24,20},{28,16},{1,13},{... | collective-permute-start | bytes 442376 | tf_op jit(solution)/shard_map/ppermute | solution.py:415
  7.9 9.7 %collective-permute-start.3 = (bf16[144,512]{1,0:T(8,128)(2,1)}, bf16[144,512]{1,0:T(8,128)(2,1)S(1)}, u32[]{:S(2)}, u32[]{:S(2)}) collective-permute-start(bf16[144,512]{1,0:T(8,128)(2,1)} %get-tuple-element.74), channel_id=1, source_target_pairs={{0,16},{4,20},{8,24},{12,28},{16,0},{20,4},{24,8},{28,12},{1,17},{... | collective-permute-start | bytes 442376 | tf_op jit(solution)/shard_map/ppermute | solution.py:415
  9.4 17.5 %copy-start.16 = (bf16[144,512]{1,0:T(8,128)(2,1)}, bf16[144,512]{1,0:T(8,128)(2,1)S(1)}, u32[]{:S(2)}) copy-start(bf16[144,512]{1,0:T(8,128)(2,1)S(1)} %collective-permute-done.refs_1_) | copy-start | bytes 442372
  9.4 13.8 %collective-permute-start.4 = (bf16[144,512]{1,0:T(8,128)(2,1)}, bf16[144,512]{1,0:T(8,128)(2,1)S(1)}, u32[]{:S(2)}, u32[]{:S(2)}) collective-permute-start(bf16[144,512]{1,0:T(8,128)(2,1)} %get-tuple-element.75), channel_id=1, source_target_pairs={{0,20},{4,16},{8,28},{12,24},{16,4},{20,0},{24,12},{28,8},{1,21},{... | collective-permute-start | bytes 442376 | tf_op jit(solution)/shard_map/ppermute | solution.py:415
  12.7 14.2 %copy-start.17 = (bf16[144,512]{1,0:T(8,128)(2,1)}, bf16[144,512]{1,0:T(8,128)(2,1)S(1)}, u32[]{:S(2)}) copy-start(bf16[144,512]{1,0:T(8,128)(2,1)S(1)} %collective-permute-done.1.refs_2_) | copy-start | bytes 442372
  12.7 10.5 %collective-permute-start.5 = (bf16[144,512]{1,0:T(8,128)(2,1)}, bf16[144,512]{1,0:T(8,128)(2,1)S(1)}, u32[]{:S(2)}, u32[]{:S(2)}) collective-permute-start(bf16[144,512]{1,0:T(8,128)(2,1)} %get-tuple-element.76), channel_id=1, source_target_pairs={{0,24},{4,28},{8,16},{12,20},{16,8},{20,12},{24,0},{28,4},{1,25},{... | collective-permute-start | bytes 442376 | tf_op jit(solution)/shard_map/ppermute | solution.py:415
  15.8 7.5 %collective-permute-start.6 = (bf16[144,512]{1,0:T(8,128)(2,1)}, bf16[144,512]{1,0:T(8,128)(2,1)S(1)}, u32[]{:S(2)}, u32[]{:S(2)}) collective-permute-start(bf16[144,512]{1,0:T(8,128)(2,1)} %get-tuple-element.77), channel_id=1, source_target_pairs={{0,28},{4,24},{8,20},{12,16},{16,12},{20,8},{24,4},{28,0},{1,29},{... | collective-permute-start | bytes 442376 | tf_op jit(solution)/shard_map/ppermute | solution.py:415
  15.8 1.0 copy-start.4
  17.6 9.3 %copy-start.18 = (bf16[144,512]{1,0:T(8,128)(2,1)}, bf16[144,512]{1,0:T(8,128)(2,1)S(1)}, u32[]{:S(2)}) copy-start(bf16[144,512]{1,0:T(8,128)(2,1)S(1)} %collective-permute-done.2.refs_3_) | copy-start | bytes 442372
  17.6 9.3 %copy-start.19 = (bf16[144,512]{1,0:T(8,128)(2,1)}, bf16[144,512]{1,0:T(8,128)(2,1)S(1)}, u32[]{:S(2)}) copy-start(bf16[144,512]{1,0:T(8,128)(2,1)S(1)} %collective-permute-done.3.refs_4_) | copy-start | bytes 442372
  23.3 3.7 %copy-start.20 = (bf16[144,512]{1,0:T(8,128)(2,1)}, bf16[144,512]{1,0:T(8,128)(2,1)S(1)}, u32[]{:S(2)}) copy-start(bf16[144,512]{1,0:T(8,128)(2,1)S(1)} %collective-permute-done.4.refs_5_) | copy-start | bytes 442372
  23.3 3.7 %copy-start.21 = (bf16[144,512]{1,0:T(8,128)(2,1)}, bf16[144,512]{1,0:T(8,128)(2,1)S(1)}, u32[]{:S(2)}) copy-start(bf16[144,512]{1,0:T(8,128)(2,1)S(1)} %collective-permute-done.5.refs_6_) | copy-start | bytes 442372
  23.3 3.7 %copy-start.22 = (bf16[144,512]{1,0:T(8,128)(2,1)}, bf16[144,512]{1,0:T(8,128)(2,1)S(1)}, u32[]{:S(2)}) copy-start(bf16[144,512]{1,0:T(8,128)(2,1)S(1)} %collective-permute-done.6.refs_7_) | copy-start | bytes 442372
  23.3 13.5 %collective-permute-start.10 = (bf16[256,512]{1,0:T(8,128)(2,1)S(1)}, bf16[256,512]{1,0:T(8,128)(2,1)S(1)}, u32[]{:S(2)}, u32[]{:S(2)}) collective-permute-start(bf16[256,512]{1,0:T(8,128)(2,1)S(1)} %get-tuple-element.102), channel_id=1, source_target_pairs={{0,24},{4,28},{8,16},{12,20},{16,8},{20,12},{24,0},{28,4},{1,25},{... | collective-permute-start | bytes 786440 | tf_op jit(solution)/shard_map/ppermute | solution.py:422
  26.3 12.4 %collective-permute-start.8 = (bf16[256,512]{1,0:T(8,128)(2,1)S(1)}, bf16[256,512]{1,0:T(8,128)(2,1)S(1)}, u32[]{:S(2)}, u32[]{:S(2)}) collective-permute-start(bf16[256,512]{1,0:T(8,128)(2,1)S(1)} %get-tuple-element.100), channel_id=1, source_target_pairs={{0,8},{4,12},{8,0},{12,4},{16,24},{20,28},{24,16},{28,20},{1,9},{5... | collective-permute-start | bytes 786440 | tf_op jit(solution)/shard_map/ppermute | solution.py:422
  26.7 12.0 %collective-permute-start.9 = (bf16[256,512]{1,0:T(8,128)(2,1)S(1)}, bf16[256,512]{1,0:T(8,128)(2,1)S(1)}, u32[]{:S(2)}, u32[]{:S(2)}) collective-permute-start(bf16[256,512]{1,0:T(8,128)(2,1)S(1)} %get-tuple-element.101), channel_id=1, source_target_pairs={{0,16},{4,20},{8,24},{12,28},{16,0},{20,4},{24,8},{28,12},{1,17},{... | collective-permute-start | bytes 786440 | tf_op jit(solution)/shard_map/ppermute | solution.py:422
  36.8 1.9 %copy-start.13 = (bf16[256,512]{1,0:T(8,128)(2,1)}, bf16[256,512]{1,0:T(8,128)(2,1)S(1)}, u32[]{:S(2)}) copy-start(bf16[256,512]{1,0:T(8,128)(2,1)S(1)} %collective-permute-done.10.refs_9_) | copy-start | bytes 786436
  38.7 0.8 copy-start.15
  54.3 3.0 %collective-permute-start.12 = (f32[128,2176]{1,0:T(8,128)}, f32[128,2176]{1,0:T(8,128)S(1)}, u32[]{:S(2)}, u32[]{:S(2)}) collective-permute-start(f32[128,2176]{1,0:T(8,128)} %get-tuple-element.106), channel_id=1, source_target_pairs={{0,4},{4,0},{8,12},{12,8},{16,20},{20,16},{24,28},{28,24},{1,5},{5... | collective-permute-start | bytes 3342344 | tf_op jit(solution)/shard_map/ppermute | solution.py:494
  54.3 12.9 %collective-permute-start.11 = (f32[128,2176]{1,0:T(8,128)}, f32[128,2176]{1,0:T(8,128)S(1)}, u32[]{:S(2)}, u32[]{:S(2)}) collective-permute-start(f32[128,2176]{1,0:T(8,128)} %get-tuple-element.104), channel_id=1, source_target_pairs={{0,4},{4,0},{8,12},{12,8},{16,20},{20,16},{24,28},{28,24},{1,5},{5... | collective-permute-start | bytes 3342344 | tf_op jit(solution)/shard_map/ppermute | solution.py:495
  57.3 1.0 copy-start.12
  58.3 5.3 %copy-start.3 = (bf16[512,512]{1,0:T(8,128)(2,1)S(1)}, bf16[512,512]{1,0:T(8,128)(2,1)}, u32[]{:S(2)}) copy-start(bf16[512,512]{1,0:T(8,128)(2,1)} %get-tuple-element.108.serial_grad_ref) | copy-start | bytes 1572868
  58.3 5.3 %copy-start.5 = (f32[512,128]{1,0:T(8,128)S(1)}, f32[512,128]{1,0:T(8,128)}, u32[]{:S(2)}) copy-start(f32[512,128]{1,0:T(8,128)} %get-tuple-element.107.inv_ref) | copy-start | bytes 786436
  58.3 5.3 %copy-start.8 = (s32[1,1024]{1,0:T(1,128)S(1)}, s32[1,1024]{1,0:T(1,128)}, u32[]{:S(2)}) copy-start(s32[1,1024]{1,0:T(1,128)} %get-tuple-element.92.pos_ref) | copy-start | bytes 12292
  58.3 5.3 %copy-start.9 = (f32[512]{0:T(512)S(1)}, f32[512]{0:T(512)}, u32[]{:S(2)}) copy-start(f32[512]{0:T(512)} %param.11) | copy-start | bytes 6148
  62.1 9.7 %collective-permute-start.13 = (s16[128,2176]{1,0:T(8,128)(2,1)}, s16[128,2176]{1,0:T(8,128)(2,1)S(1)}, u32[]{:S(2)}, u32[]{:S(2)}) collective-permute-start(s16[128,2176]{1,0:T(8,128)(2,1)} %code_first.1), channel_id=1, source_target_pairs={{0,8},{4,20},{8,0},{12,28},{16,24},{20,4},{24,16},{28,12},{1,9},{5... | collective-permute-start | bytes 1671176 | tf_op jit(solution)/shard_map/ppermute | solution.py:497
  63.6 1.2 copy-start.1
  64.9 1.2 copy-start.2
  66.1 5.7 %copy-start = (f32[128,2176]{1,0:T(8,128)S(1)}, f32[128,2176]{1,0:T(8,128)}, u32[]{:S(2)}) copy-start(f32[128,2176]{1,0:T(8,128)} %get-tuple-element.103.refs_0_) | copy-start | bytes 3342340
  67.2 6.3 %collective-permute-start.18 = (bf16[512,512]{1,0:T(8,128)(2,1)S(1)}, bf16[512,512]{1,0:T(8,128)(2,1)S(1)}, u32[]{:S(2)}, u32[]{:S(2)}) collective-permute-start(bf16[512,512]{1,0:T(8,128)(2,1)S(1)} %get-tuple-element.117), channel_id=1, source_target_pairs={{0,4},{4,0},{8,12},{12,8},{16,20},{20,16},{24,28},{28,24},{1,5},{5... | collective-permute-start | bytes 1572872 | tf_op jit(solution)/shard_map/ppermute | solution.py:624
  72.1 7.9 %collective-permute-start.14 = (s16[64,2176]{1,0:T(8,128)(2,1)S(1)}, s16[64,2176]{1,0:T(8,128)(2,1)S(1)}, u32[]{:S(2)}, u32[]{:S(2)}) collective-permute-start(s16[64,2176]{1,0:T(8,128)(2,1)S(1)} %code_second.1), channel_id=1, source_target_pairs={{0,16},{4,12},{8,24},{12,4},{16,0},{20,28},{24,8},{28,20},{1,17},{... | collective-permute-start | bytes 835592 | tf_op jit(solution)/shard_map/ppermute | solution.py:503
  75.1 16.0 %collective-permute-start.19 = (bf16[256,512]{1,0:T(8,128)(2,1)}, bf16[256,512]{1,0:T(8,128)(2,1)}, u32[]{:S(2)}, u32[]{:S(2)}) collective-permute-start(bf16[256,512]{1,0:T(8,128)(2,1)} %get-tuple-element.119), channel_id=1, source_target_pairs={{0,8},{4,12},{8,0},{12,4},{16,24},{20,28},{24,16},{28,20},{1,9},{5... | collective-permute-start | bytes 786440 | tf_op jit(solution)/shard_map/ppermute | solution.py:422
  76.7 14.5 %collective-permute-start.20 = (bf16[256,512]{1,0:T(8,128)(2,1)}, bf16[256,512]{1,0:T(8,128)(2,1)}, u32[]{:S(2)}, u32[]{:S(2)}) collective-permute-start(bf16[256,512]{1,0:T(8,128)(2,1)} %get-tuple-element.120), channel_id=1, source_target_pairs={{0,16},{4,20},{8,24},{12,28},{16,0},{20,4},{24,8},{28,12},{1,17},{... | collective-permute-start | bytes 786440 | tf_op jit(solution)/shard_map/ppermute | solution.py:422
  77.4 13.8 %collective-permute-start.21 = (bf16[256,512]{1,0:T(8,128)(2,1)}, bf16[256,512]{1,0:T(8,128)(2,1)}, u32[]{:S(2)}, u32[]{:S(2)}) collective-permute-start(bf16[256,512]{1,0:T(8,128)(2,1)} %get-tuple-element.121), channel_id=1, source_target_pairs={{0,24},{4,28},{8,16},{12,20},{16,8},{20,12},{24,0},{28,4},{1,25},{... | collective-permute-start | bytes 786440 | tf_op jit(solution)/shard_map/ppermute | solution.py:422
  80.5 4.4 %collective-permute-start.15 = (s16[16,2176]{1,0:T(8,128)(2,1)S(1)}, s16[16,2176]{1,0:T(8,128)(2,1)S(1)}, u32[]{:S(2)}, u32[]{:S(2)}) collective-permute-start(s16[16,2176]{1,0:T(8,128)(2,1)S(1)} %get-tuple-element.113), channel_id=1, source_target_pairs={{0,1},{1,0},{2,3},{3,2},{4,5},{5,4},{6,7},{7,6},{8,9},{9,8},{10,11... | collective-permute-start | bytes 208904 | tf_op jit(solution)/shard_map/ppermute | solution.py:415
  82.2 6.3 %collective-permute-start.16 = (s16[16,2176]{1,0:T(8,128)(2,1)S(1)}, s16[16,2176]{1,0:T(8,128)(2,1)S(1)}, u32[]{:S(2)}, u32[]{:S(2)}) collective-permute-start(s16[16,2176]{1,0:T(8,128)(2,1)S(1)} %get-tuple-element.114), channel_id=1, source_target_pairs={{0,2},{1,3},{2,0},{3,1},{4,6},{5,7},{6,4},{7,5},{8,10},{9,11},{10,... | collective-permute-start | bytes 208904 | tf_op jit(solution)/shard_map/ppermute | solution.py:415
  84.9 6.1 %collective-permute-start.17 = (s16[16,2176]{1,0:T(8,128)(2,1)S(1)}, s16[16,2176]{1,0:T(8,128)(2,1)S(1)}, u32[]{:S(2)}, u32[]{:S(2)}) collective-permute-start(s16[16,2176]{1,0:T(8,128)(2,1)S(1)} %get-tuple-element.115), channel_id=1, source_target_pairs={{0,3},{1,2},{2,1},{3,0},{4,7},{5,6},{6,5},{7,4},{8,11},{9,10},{10,... | collective-permute-start | bytes 208904 | tf_op jit(solution)/shard_map/ppermute | solution.py:415
  91.2 4.6 %collective-permute-start.22 = (bf16[16,2176]{1,0:T(8,128)(2,1)S(1)}, bf16[16,2176]{1,0:T(8,128)(2,1)S(1)}, u32[]{:S(2)}, u32[]{:S(2)}) collective-permute-start(bf16[16,2176]{1,0:T(8,128)(2,1)S(1)} %finish.1), channel_id=1, source_target_pairs={{0,1},{1,0},{2,3},{3,2},{4,5},{5,4},{6,7},{7,6},{8,9},{9,8},{10,11... | collective-permute-start | bytes 208904 | tf_op jit(solution)/shard_map/ppermute | solution.py:415
  91.7 7.2 %collective-permute-start.23 = (bf16[16,2176]{1,0:T(8,128)(2,1)S(1)}, bf16[16,2176]{1,0:T(8,128)(2,1)S(1)}, u32[]{:S(2)}, u32[]{:S(2)}) collective-permute-start(bf16[16,2176]{1,0:T(8,128)(2,1)S(1)} %finish.1), channel_id=1, source_target_pairs={{0,2},{1,3},{2,0},{3,1},{4,6},{5,7},{6,4},{7,5},{8,10},{9,11},{10,... | collective-permute-start | bytes 208904 | tf_op jit(solution)/shard_map/ppermute | solution.py:415
  95.8 6.1 %collective-permute-start.24 = (bf16[16,2176]{1,0:T(8,128)(2,1)S(1)}, bf16[16,2176]{1,0:T(8,128)(2,1)S(1)}, u32[]{:S(2)}, u32[]{:S(2)}) collective-permute-start(bf16[16,2176]{1,0:T(8,128)(2,1)S(1)} %finish.1), channel_id=1, source_target_pairs={{0,3},{1,2},{2,1},{3,0},{4,7},{5,6},{6,5},{7,4},{8,11},{9,10},{10,... | collective-permute-start | bytes 208904 | tf_op jit(solution)/shard_map/ppermute | solution.py:415
  102.1 9.2 %collective-permute-start.25 = (bf16[64,2176]{1,0:T(8,128)(2,1)S(1)}, bf16[64,2176]{1,0:T(8,128)(2,1)S(1)}, u32[]{:S(2)}, u32[]{:S(2)}) collective-permute-start(bf16[64,2176]{1,0:T(8,128)(2,1)S(1)} %pad_maximum_fusion.1), channel_id=1, source_target_pairs={{0,16},{4,12},{8,24},{12,4},{16,0},{20,28},{24,8},{28,20},{1,17},{... | collective-permute-start | bytes 835592 | tf_op jit(solution)/shard_map/ppermute | solution.py:548
  111.4 2.4 %copy-start.7 = (bf16[256,512]{1,0:T(8,128)(2,1)S(1)}, bf16[256,512]{1,0:T(8,128)(2,1)}, u32[]{:S(2)}) copy-start(bf16[256,512]{1,0:T(8,128)(2,1)} %copy-done.6) | copy-start | bytes 786436
  111.4 2.4 %copy-start.10 = (s32[1,512]{1,0:T(1,128)S(1)}, s32[1,512]{1,0:T(1,128)}, u32[]{:S(2)}) copy-start(s32[1,512]{1,0:T(1,128)} %get-tuple-element.123.slot_ref) | copy-start | bytes 6148
  111.5 9.8 %collective-permute-start.26 = (bf16[128,2176]{1,0:T(8,128)(2,1)S(1)}, bf16[128,2176]{1,0:T(8,128)(2,1)S(1)}, u32[]{:S(2)}, u32[]{:S(2)}) collective-permute-start(bf16[128,2176]{1,0:T(8,128)(2,1)S(1)} %broadcast_select_fusion), channel_id=1, source_target_pairs={{0,8},{4,20},{8,0},{12,28},{16,24},{20,4},{24,16},{28,12},{1,9},{5... | collective-permute-start | bytes 1671176 | tf_op jit(solution)/shard_map/ppermute | solution.py:548
  121.5 2.8 %collective-permute-start.27 = (bf16[256,2176]{1,0:T(8,128)(2,1)S(1)}, bf16[256,2176]{1,0:T(8,128)(2,1)S(1)}, u32[]{:S(2)}, u32[]{:S(2)}) collective-permute-start(bf16[256,2176]{1,0:T(8,128)(2,1)S(1)} %maximum_select_fusion.sums_ref), channel_id=1, source_target_pairs={{0,4},{4,0},{8,12},{12,8},{16,20},{20,16},{24,28},{28,24},{1,5},{5... | collective-permute-start | bytes 3342344 | tf_op jit(solution)/shard_map/ppermute | solution.py:725
  (3 other events, 2.1 us)
